TPU v7x, 32 devices: a whole 2x2x4 slice. The times are simulated.
32 devices in a mesh: groups: 2 (over x), tensor: 4 (over y, core), dp: 4 (over z).
Axes of the slice: x: 2, y: 2, z: 4, core: 2. Of those that a mesh axis runs over, the one named last changes fastest.
Arguments:
- first_out: bfloat16 [4096, 1024], P(('groups', 'tensor', 'dp')), parts along dimension 0, may hold values from -6 to 6
- second_out: bfloat16 [4096, 1024], P(('groups', 'tensor', 'dp')), parts along dimension 0, may hold values from -6 to 6
- grad_first: bfloat16 [4096, 1024], P(('groups', 'tensor', 'dp')), parts along dimension 0, may hold values from -6 to 6
- grad_second: bfloat16 [4096, 1024], P(('groups', 'tensor', 'dp')), parts along dimension 0, may hold values from -6 to 6
- w_up: bfloat16 [1024, 8192], P('dp', 'tensor'), may hold values from -0.1875 to 0.1875
- w_down: bfloat16 [8192, 1024], P('tensor', 'dp'), may hold values from -0.0625 to 0.0625
- norm_gain: float32 [1024], replicated, may hold values from 0.25 to 1.75
- norm_bias: float32 [1024], replicated, may hold values from -3 to 3
Outputs:
- second_in: bfloat16 [4096, 1024], P(('groups', 'tensor', 'dp')), parts along dimension 0
- grad_first_in: float32 [4096, 1024], P(('groups', 'tensor', 'dp')), parts along dimension 0
- grad_up: float32 [2048, 8192], P(('groups', 'dp'), 'tensor'), parts along dimension 0
- grad_down: float32 [16384, 1024], P(('groups', 'tensor'), 'dp'), parts along dimension 0
- grad_norm: float32 [4, 1024], P('groups'), parts along dimension 0
There are 2 independent parts, one for each index of `groups`. A program takes and returns all parts, laid end to end along the dimension named above; an argument that names none is the same for every part. Nothing has to cross between parts.
All inputs are finite; a program needn't handle non-finite values.
Results may differ from a plain program's by a relative error of at most 0.017.
Values may be sent and summed in bfloat16 or wider, within the bound.
No kernel may reach another device: no remote copies, remote signals or barrier semaphores. Data moves between devices by JAX's collectives and lax.ppermute only.
A program may use at most 64 MiB of HBM per device.

v0:
```python
import jax
import jax.numpy as jnp
from jax import lax
from jax.sharding import PartitionSpec as P

epsilon = 1e-06


def normalize(row_data, norm_gain, norm_bias):
    values = row_data.astype(jnp.float32)
    row_mean = jnp.mean(values, axis=-1, keepdims=True)
    centred = values - row_mean
    inv_std = lax.rsqrt(jnp.mean(centred * centred, axis=-1, keepdims=True) + epsilon)
    standard = centred * inv_std
    normed = (standard * norm_gain + norm_bias).astype(jnp.bfloat16)
    return (standard, inv_std, normed)


def contract_tokens(left_rows, right_rows):
    return lax.dot_general(
        left_rows, right_rows, (((0,), (0,)), ((), ())), preferred_element_type=jnp.float32
    )


def body(first_out, second_out, grad_first, grad_second, w_up, w_down, norm_gain, norm_bias):
    own_rows = first_out.shape[0]
    up_full, down_full = (
        lax.all_gather(w_up, "dp", axis=0, tiled=True),
        lax.all_gather(w_down, "dp", axis=1, tiled=True),
    )
    first_all, grad_all = (
        lax.all_gather(first_out, "tensor", axis=0, tiled=True),
        lax.all_gather(grad_second, "tensor", axis=0, tiled=True),
    )
    standard_all, inv_std_all, normed = normalize(first_all, norm_gain, norm_bias)
    offset = lax.axis_index("tensor") * own_rows
    standard = lax.dynamic_slice_in_dim(standard_all, offset, own_rows, 0)
    inv_std = lax.dynamic_slice_in_dim(inv_std_all, offset, own_rows, 0)
    preact = jnp.dot(normed, up_full, preferred_element_type=jnp.float32)
    hidden = jax.nn.gelu(preact).astype(jnp.bfloat16)
    branch = lax.psum_scatter(
        jnp.dot(hidden, down_full, preferred_element_type=jnp.float32).astype(jnp.bfloat16),
        "tensor",
        scatter_dimension=0,
        tiled=True,
    ).astype(jnp.float32)
    second_in = (second_out.astype(jnp.float32) - branch).astype(jnp.bfloat16)
    tokens = own_rows * lax.axis_size("tensor") * lax.axis_size("dp")
    grad_scale = tokens ** (-0.5)
    grad_down_part = contract_tokens(hidden, grad_all)
    grad_down = (
        lax.psum_scatter(
            grad_down_part.astype(jnp.bfloat16), "dp", scatter_dimension=1, tiled=True
        ).astype(jnp.float32)
        * grad_scale
    )
    grad_hidden = lax.dot_general(
        grad_all, down_full, (((1,), (1,)), ((), ())), preferred_element_type=jnp.float32
    )
    grad_pre = jax.vjp(jax.nn.gelu, preact)[1](grad_hidden)[0].astype(jnp.bfloat16)
    grad_up_part = contract_tokens(normed, grad_pre)
    grad_up = (
        lax.psum_scatter(
            grad_up_part.astype(jnp.bfloat16), "dp", scatter_dimension=0, tiled=True
        ).astype(jnp.float32)
        * grad_scale
    )
    grad_normed = lax.psum_scatter(
        lax.dot_general(
            grad_pre, up_full, (((1,), (1,)), ((), ())), preferred_element_type=jnp.float32
        ).astype(jnp.bfloat16),
        "tensor",
        scatter_dimension=0,
        tiled=True,
    ).astype(jnp.float32)
    grad_std = grad_normed * norm_gain
    grad_rows = inv_std * (
        grad_std
        - jnp.mean(grad_std, axis=-1, keepdims=True)
        - standard * jnp.mean(grad_std * standard, axis=-1, keepdims=True)
    )
    grad_first_in = grad_first.astype(jnp.float32) + grad_rows
    local_stats = jnp.stack([jnp.sum(grad_normed * standard, axis=0), jnp.sum(grad_normed, axis=0)])
    grad_norm = lax.psum(local_stats, ("tensor", "dp")) * grad_scale
    return (second_in, grad_first_in, grad_up, grad_down, grad_norm)


def solution(mesh):
    in_specs = (
        P(("groups", "tensor", "dp"), None),
        P(("groups", "tensor", "dp"), None),
        P(("groups", "tensor", "dp"), None),
        P(("groups", "tensor", "dp"), None),
        P("dp", "tensor"),
        P("tensor", "dp"),
        P(),
        P(),
    )
    out_specs = (
        P(("groups", "tensor", "dp"), None),
        P(("groups", "tensor", "dp"), None),
        P(("groups", "dp"), "tensor"),
        P(("groups", "tensor"), "dp"),
        P("groups", None),
    )
    return jax.shard_map(body, mesh=mesh, in_specs=in_specs, out_specs=out_specs, check_vma=False)
```

profile of v0, /device:TPU:0, one launch (start us, length us, event | category | flops | bytes accessed | tf_op | source)
XLA Modules:
  0.0 443.0 jit_solution(17227224625132561028)
XLA Ops:
  7.2 0.7 all-gather.5.cloned.1.call-update
  7.9 0.7 all-gather.11.cloned.1.call-update
  8.7 0.7 all-gather.9.cloned.1.call-update
  9.4 0.5 all-gather.7.cloned.1.call-update
  10.0 19.0 %all-gather.5.cloned.1.call-done = bf16[512,1024]{1,0:T(8,128)(2,1)} async-done(((bf16[128,1024]{1,0:T(8,128)(2,1)}), bf16[512,1024]{1,0:T(8,128)(2,1)}) %all-gather.5.cloned.1.call-update) | async-done | bytes 1048592 | tf_op jit(solution)/shard_map/all_gather | solution.py:32
  29.0 1.4 convert_reduce_fusion
  30.5 1.6 fusion.9
  32.1 15.2 %all-gather.11.cloned.1.call-done = bf16[512,1024]{1,0:T(8,128)(2,1)} async-done(((bf16[128,1024]{1,0:T(8,128)(2,1)}), bf16[512,1024]{1,0:T(8,128)(2,1)}) %all-gather.11.cloned.1.call-update) | async-done | bytes 1048592 | tf_op jit(solution)/shard_map/all_gather | solution.py:33
  47.3 82.2 %all-gather.9.cloned.1.call-done = bf16[2048,1024]{1,0:T(8,128)(2,1)} async-done(((bf16[2048,256]{1,0:T(8,128)(2,1)}), bf16[2048,1024]{1,0:T(8,128)(2,1)}) %all-gather.9.cloned.1.call-update) | async-done | bytes 4194320 | tf_op jit(solution)/shard_map/all_gather | solution.py:29
  129.5 6.9 %fusion.21 = f32[512,2048]{1,0:T(8,128)} fusion(bf16[512,1024]{1,0:T(8,128)(2,1)} %all-gather.11.cloned.1.call-done, bf16[2048,1024]{1,0:T(8,128)(2,1)} %all-gather.9.cloned.1.call-done), kind=kOutput, calls=%fused_computation.41 | convolution fusion | flops 2147483648 | bytes 9437184 | tf_op jit(solution)/shard_map/dot_general | solution.py:57
  136.4 73.6 %all-gather.7.cloned.1.call-done = bf16[1024,2048]{1,0:T(8,128)(2,1)} async-done(((bf16[256,2048]{1,0:T(8,128)(2,1)}), bf16[1024,2048]{1,0:T(8,128)(2,1)}) %all-gather.7.cloned.1.call-update) | async-done | bytes 4194320 | tf_op jit(solution)/shard_map/all_gather | solution.py:28
  209.9 9.5 %fusion.6 = (bf16[512,2048]{1,0:T(8,128)(2,1)S(1)}, f32[512,2048]{1,0:T(8,128)}) fusion(f32[512,2048]{1,0:T(8,128)} %fusion.21, bf16[1024,2048]{1,0:T(8,128)(2,1)} %all-gather.7.cloned.1.call-done, f32[1024]{0:T(1024)S(1)} %copy-done.5, f32[1024]{0:T(1024)S(1)} %copy-done.2, f32[512]{0:T(512)S(1)} %add_rsqrt_fusion, f32[512]{0:T(512)S(1)} %broadcast_multiply_fusion.1, ...), kind=kOutput, calls=%fused_computation.8 | convolution fusion | flops 2171600896 | bytes 15740928 | tf_op jit(solution)/shard_map/dot_general | solution.py:39
  219.5 3.4 convolution_convert_fusion.2
  222.9 0.0 reduce-scatter.5.cloned.1.call-start
  222.9 7.1 %convolution_convert_fusion.3 = bf16[512,1024]{1,0:T(8,128)(2,1)} fusion(bf16[2048,1024]{1,0:T(8,128)(2,1)} %all-gather.9.cloned.1.call-done, f32[512,2048]{1,0:T(8,128)} %get-tuple-element.10), kind=kOutput, calls=%fused_computation.21 | convolution fusion | flops 2157445120 | bytes 9437184 | tf_op jit(solution)/shard_map/dot_general | solution.py:42
  230.1 0.2 reduce-scatter.9.cloned.1.call-start
  230.3 4.6 %convolution_convert_fusion.1 = bf16[1024,2048]{1,0:T(8,128)(2,1)} fusion(bf16[512,2048]{1,0:T(8,128)(2,1)S(1)} %get-tuple-element.9, f32[1024]{0:T(1024)S(1)} %copy-done.5, f32[1024]{0:T(1024)S(1)} %copy-done.2, bf16[512,1024]{1,0:T(8,128)(2,1)S(1)} %copy-done, f32[512]{0:T(512)S(1)} %add_rsqrt_fusion, f32[512]{0:T(512)S(1)} %broadcast_multiply_fusion.1), kind=kOutput, calls=%fused_computation.11 | convolution fusion | flops 2152726528 | bytes 7352320 | tf_op jit(solution)/shard_map/dot_general | solution.py:20
  234.9 0.0 reduce-scatter.11.cloned.1.call-start
  234.9 1.1 copy-done.4
  236.1 7.2 %convolution_convert_fusion = bf16[2048,1024]{1,0:T(8,128)(2,1)} fusion(bf16[512,1024]{1,0:T(8,128)(2,1)S(1)} %copy-done.4, f32[512,2048]{1,0:T(8,128)} %get-tuple-element.10), kind=kOutput, calls=%fused_computation.10 | convolution fusion | flops 2159017984 | bytes 9437184 | tf_op jit(solution)/shard_map/dot_general | solution.py:20
  243.3 0.1 dynamic-slice.3
  243.4 0.3 fusion.7
  243.7 2.8 reduce-scatter.7.cloned.1.call-done
  246.5 1.2 fusion.17
  247.6 33.4 %psum.7 = f32[2,1024]{1,0:T(2,128)S(1)} all-reduce(f32[2,1024]{1,0:T(2,128)S(1)} %pad_maximum_fusion), channel_id=1, replica_groups=mesh['groups'=2,'tensor'=4,'dp'=4] {'tensor','dp'}, use_global_device_ids=true, to_apply=%region_10.0 | all-reduce | flops 2048 | bytes 16384 | tf_op jit(solution)/shard_map/psum | solution.py:84
  281.1 0.6 broadcast_multiply_fusion
  281.7 1.7 subtract_convert_fusion
  283.4 2.0 fusion.15
  285.5 68.3 %reduce-scatter.9.cloned.1.call-done = bf16[256,2048]{1,0:T(8,128)(2,1)} async-done(((bf16[1024,2048]{1,0:T(8,128)(2,1)}), bf16[256,2048]{1,0:T(8,128)(2,1)}) %reduce-scatter.9.cloned.1.call-update) | async-done | bytes 1048592 | tf_op jit(solution)/shard_map/reduce_scatter | solution.py:63
  353.7 2.8 convert_multiply_fusion.1
  356.5 76.9 %reduce-scatter.11.cloned.1.call-done = bf16[2048,256]{1,0:T(8,128)(2,1)} async-done(((bf16[2048,1024]{1,0:T(8,128)(2,1)}), bf16[2048,256]{1,0:T(8,128)(2,1)}) %reduce-scatter.11.cloned.1.call-update) | async-done | bytes 1048592 | tf_op jit(solution)/shard_map/reduce_scatter | solution.py:52
  433.4 2.7 convert_multiply_fusion
  (25 shorter events, 0.3 us)
Async XLA Ops:
  7.2 21.9 %all-gather.5.cloned.1.call-start = ((), (), s32[]{:S(2)}) async-start(), calls=%async_computation.4 | async-start | bytes 1310720 | tf_op jit(solution)/shard_map/all_gather | solution.py:32
  7.9 39.4 %all-gather.11.cloned.1.call-start = ((), (), s32[]{:S(2)}) async-start(), calls=%async_computation.8 | async-start | bytes 1310720 | tf_op jit(solution)/shard_map/all_gather | solution.py:33
  8.7 120.8 %all-gather.9.cloned.1.call-start = ((), (), s32[]{:S(2)}) async-start(), calls=%async_computation.6 | async-start | bytes 5242880 | tf_op jit(solution)/shard_map/all_gather | solution.py:29
  9.4 200.5 %all-gather.7.cloned.1.call-start = ((), (), s32[]{:S(2)}) async-start(), calls=%async_computation.5 | async-start | bytes 5242880 | tf_op jit(solution)/shard_map/all_gather | solution.py:28
  10.0 236.5 %reduce-scatter.7.cloned.1.call-start = ((), (), s32[]{:S(2)}) async-start(), calls=%async_computation.9 | async-start | bytes 1310720 | tf_op jit(solution)/shard_map/reduce_scatter | solution.py:68
  32.1 177.8 %copy-start = (bf16[512,1024]{1,0:T(8,128)(2,1)S(1)}, bf16[512,1024]{1,0:T(8,128)(2,1)}, u32[]{:S(2)}) copy-start(bf16[512,1024]{1,0:T(8,128)(2,1)} %all-gather.5.cloned.1.call-done) | copy-start | bytes 3145732
  32.1 177.8 %copy-start.2 = (f32[1024]{0:T(1024)S(1)}, f32[1024]{0:T(1024)}, u32[]{:S(2)}) copy-start(f32[1024]{0:T(1024)} %param.14) | copy-start | bytes 12292
  32.1 177.8 %copy-start.5 = (f32[1024]{0:T(1024)S(1)}, f32[1024]{0:T(1024)}, u32[]{:S(2)}) copy-start(f32[1024]{0:T(1024)} %param.15) | copy-start | bytes 12292
  209.9 9.6 %copy-start.3 = (bf16[1024,2048]{1,0:T(8,128)(2,1)S(1)}, bf16[1024,2048]{1,0:T(8,128)(2,1)}, u32[]{:S(2)}) copy-start(bf16[1024,2048]{1,0:T(8,128)(2,1)} %all-gather.7.cloned.1.call-done) | copy-start | bytes 12582916
  222.9 58.8 %reduce-scatter.5.cloned.1.call-start = ((), (), s32[]{:S(2)}) async-start(), calls=%async_computation.7 | async-start | bytes 1310720 | tf_op jit(solution)/shard_map/reduce_scatter | solution.py:41
  230.1 123.7 %reduce-scatter.9.cloned.1.call-start = ((), (), s32[]{:S(2)}) async-start(), calls=%async_computation.10 | async-start | bytes 5242880 | tf_op jit(solution)/shard_map/reduce_scatter | solution.py:63
  234.9 1.2 copy-start.4
  234.9 198.5 %reduce-scatter.11.cloned.1.call-start = ((), (), s32[]{:S(2)}) async-start(), calls=%async_computation.11 | async-start | bytes 5242880 | tf_op jit(solution)/shard_map/reduce_scatter | solution.py:52
  243.3 38.4 %copy-start.1 = (bf16[128,1024]{1,0:T(8,128)(2,1)S(1)}, bf16[128,1024]{1,0:T(8,128)(2,1)}, u32[]{:S(2)}) copy-start(bf16[128,1024]{1,0:T(8,128)(2,1)} %param.9) | copy-start | bytes 786436
Sparse Core Ops, SparseCore 0:
  9.6 19.4 all-gather.4
  30.6 16.7 all-gather.10
  48.9 80.5 all-gather.8
  130.9 78.9 all-gather.6
  223.0 23.3 reduce-scatter.6
  249.6 25.0 reduce-scatter.4
  276.9 76.7 reduce-scatter.8
  356.1 77.2 reduce-scatter.10
where the time goes:
time: 443 us
  waiting for transfers between devices  340 us (77%)
  matrix products  38.7 us (9%)
  blocking collectives  33.4 us (8%)
  other arithmetic  14.5 us (3%)
  between operations  14.2 us (3%)
    all_gather x1, waiting for transfers between devices, body(): lax.all_gather(w_down, 'dp', axis=1, tiled=True)  82.2 us
    reduce_scatter x1, waiting for transfers between devices, body(): lax.psum_scatter(grad_down_part.astype(jnp.bfloat16), 'dp', scatter_dimen...  76.9 us
    all_gather x1, waiting for transfers between devices, body(): lax.all_gather(w_up, 'dp', axis=0, tiled=True)  73.6 us
    reduce_scatter x1, waiting for transfers between devices, body(): lax.psum_scatter(grad_up_part.astype(jnp.bfloat16), 'dp', scatter_dimensi...  68.3 us
    psum x1, blocking collectives, body(): grad_norm = lax.psum(local_stats, ('tensor', 'dp')) * grad_scale  33.4 us
    all_gather x1, waiting for transfers between devices, body(): lax.all_gather(first_out, 'tensor', axis=0, tiled=True)  19 us
    all_gather x1, waiting for transfers between devices, body(): lax.all_gather(grad_second, 'tensor', axis=0, tiled=True)  15.2 us
    dot_general x2, matrix products, contract_tokens(): lax.dot_general(left_rows, right_rows, (((0,), (0,)), ((), ())), preferre...  11.8 us
  transfers between devices with their start and end apart: 8, of which 7 were waited for; matrix products, arithmetic and copies ran while one was open for 8% of the time, Pallas kernels for 0%

commit v1 on v0

--- a/solution.py
+++ b/solution.py
@@ -22,16 +22,33 @@
     )
 
 
-def body(first_out, second_out, grad_first, grad_second, w_up, w_down, norm_gain, norm_bias):
+def contract_last(left_rows, right_rows):
+    return lax.dot_general(
+        left_rows, right_rows, (((1,), (1,)), ((), ())), preferred_element_type=jnp.float32
+    )
+
+
+def finish_rows(branch, grad_normed, second_out, grad_first, standard, inv_std, norm_gain):
+    second_in = (second_out.astype(jnp.float32) - branch).astype(jnp.bfloat16)
+    grad_std = grad_normed * norm_gain
+    grad_rows = inv_std * (
+        grad_std
+        - jnp.mean(grad_std, axis=-1, keepdims=True)
+        - standard * jnp.mean(grad_std * standard, axis=-1, keepdims=True)
+    )
+    grad_first_in = grad_first.astype(jnp.float32) + grad_rows
+    local_stats = jnp.stack([jnp.sum(grad_normed * standard, axis=0), jnp.sum(grad_normed, axis=0)])
+    return second_in, grad_first_in, local_stats
+
+
+def gather_weights_body(
+    first_out, second_out, grad_first, grad_second, w_up, w_down, norm_gain, norm_bias
+):
     own_rows = first_out.shape[0]
-    up_full, down_full = (
-        lax.all_gather(w_up, "dp", axis=0, tiled=True),
-        lax.all_gather(w_down, "dp", axis=1, tiled=True),
-    )
-    first_all, grad_all = (
-        lax.all_gather(first_out, "tensor", axis=0, tiled=True),
-        lax.all_gather(grad_second, "tensor", axis=0, tiled=True),
-    )
+    up_full = lax.all_gather(w_up, "dp", axis=0, tiled=True)
+    down_full = lax.all_gather(w_down, "dp", axis=1, tiled=True)
+    first_all = lax.all_gather(first_out, "tensor", axis=0, tiled=True)
+    grad_all = lax.all_gather(grad_second, "tensor", axis=0, tiled=True)
     standard_all, inv_std_all, normed = normalize(first_all, norm_gain, norm_bias)
     offset = lax.axis_index("tensor") * own_rows
     standard = lax.dynamic_slice_in_dim(standard_all, offset, own_rows, 0)
@@ -44,7 +61,6 @@
         scatter_dimension=0,
         tiled=True,
     ).astype(jnp.float32)
-    second_in = (second_out.astype(jnp.float32) - branch).astype(jnp.bfloat16)
     tokens = own_rows * lax.axis_size("tensor") * lax.axis_size("dp")
     grad_scale = tokens ** (-0.5)
     grad_down_part = contract_tokens(hidden, grad_all)
@@ -54,9 +70,7 @@
         ).astype(jnp.float32)
         * grad_scale
     )
-    grad_hidden = lax.dot_general(
-        grad_all, down_full, (((1,), (1,)), ((), ())), preferred_element_type=jnp.float32
-    )
+    grad_hidden = contract_last(grad_all, down_full)
     grad_pre = jax.vjp(jax.nn.gelu, preact)[1](grad_hidden)[0].astype(jnp.bfloat16)
     grad_up_part = contract_tokens(normed, grad_pre)
     grad_up = (
@@ -66,23 +80,115 @@
         * grad_scale
     )
     grad_normed = lax.psum_scatter(
-        lax.dot_general(
-            grad_pre, up_full, (((1,), (1,)), ((), ())), preferred_element_type=jnp.float32
-        ).astype(jnp.bfloat16),
+        contract_last(grad_pre, up_full).astype(jnp.bfloat16),
         "tensor",
         scatter_dimension=0,
         tiled=True,
     ).astype(jnp.float32)
-    grad_std = grad_normed * norm_gain
-    grad_rows = inv_std * (
-        grad_std
-        - jnp.mean(grad_std, axis=-1, keepdims=True)
-        - standard * jnp.mean(grad_std * standard, axis=-1, keepdims=True)
-    )
-    grad_first_in = grad_first.astype(jnp.float32) + grad_rows
-    local_stats = jnp.stack([jnp.sum(grad_normed * standard, axis=0), jnp.sum(grad_normed, axis=0)])
+    second_in, grad_first_in, local_stats = finish_rows(
+        branch, grad_normed, second_out, grad_first, standard, inv_std, norm_gain
+    )
     grad_norm = lax.psum(local_stats, ("tensor", "dp")) * grad_scale
     return (second_in, grad_first_in, grad_up, grad_down, grad_norm)
+
+
+def swap(values, axis, mask):
+    return lax.ppermute(values, axis, [(i, i ^ mask) for i in range(lax.axis_size(axis))])
+
+
+def bits_of(size):
+    return [1 << b for b in reversed(range(size.bit_length() - 1))]
+
+
+def gather_tokens_body(
+    first_out, second_out, grad_first, grad_second, w_up, w_down, norm_gain, norm_bias
+):
+    n_dp, n_tensor = lax.axis_size("dp"), lax.axis_size("tensor")
+    own_rows, depth = first_out.shape[0], w_up.shape[0]
+    units = w_up.shape[1] // n_dp
+    place = lax.axis_index("dp")
+    standard, inv_std, normed = normalize(first_out, norm_gain, norm_bias)
+
+    up = jnp.zeros((depth * n_dp, units), w_up.dtype)
+    down = jnp.zeros((units, depth * n_dp), w_down.dtype)
+    for k in range(n_dp):
+        other = place ^ k
+        block = lax.dynamic_slice_in_dim(w_up, other * units, units, 1)
+        block = swap(block, "dp", k) if k else block
+        up = lax.dynamic_update_slice_in_dim(up, block, other * depth, 0)
+    for k in range(n_dp):
+        other = place ^ k
+        block = lax.dynamic_slice_in_dim(w_down, other * units, units, 0)
+        block = swap(block, "dp", k) if k else block
+        down = lax.dynamic_update_slice_in_dim(down, block, other * depth, 1)
+
+    chunks = {0: jnp.stack([normed, grad_second])}
+    for bit in bits_of(n_dp):
+        chunks.update({k | bit: swap(chunk, "dp", bit) for k, chunk in chunks.items()})
+
+    sums = {}
+    up_total = down_total = 0.0
+    for k in sorted(chunks):
+        chunk = chunks[k]
+        for bit in bits_of(n_tensor):
+            chunk = jnp.concatenate([chunk, swap(chunk, "tensor", bit)], axis=1)
+        rows, grads = chunk[0], chunk[1]
+        preact = jnp.dot(rows, up, preferred_element_type=jnp.float32)
+        hidden = jax.nn.gelu(preact).astype(jnp.bfloat16)
+        grad_hidden = contract_last(grads, down)
+        grad_pre = jax.vjp(jax.nn.gelu, preact)[1](grad_hidden)[0].astype(jnp.bfloat16)
+        part = jnp.stack(
+            [
+                jnp.dot(hidden, down, preferred_element_type=jnp.float32).astype(jnp.bfloat16),
+                contract_last(grad_pre, up).astype(jnp.bfloat16),
+            ]
+        )
+        up_total = up_total + contract_tokens(rows, grad_pre)
+        down_total = down_total + contract_tokens(hidden, grads)
+        for bit in reversed(bits_of(n_tensor)):
+            half = part.shape[1] // 2
+            part = part[:, :half] + swap(part[:, half:], "tensor", bit)
+        sums[k] = part
+    for bit in reversed(bits_of(n_dp)):
+        for k in [k for k in sums if k & bit]:
+            got = swap(sums.pop(k), "dp", bit).astype(jnp.float32)
+            total = sums[k ^ bit].astype(jnp.float32) + got
+            sums[k ^ bit] = total if k == bit and bit == bits_of(n_dp)[0] else total.astype(jnp.bfloat16)
+    branch, grad_normed = sums[0][0], sums[0][1]
+    second_in, grad_first_in, stats = finish_rows(
+        branch, grad_normed, second_out, grad_first, standard, inv_std, norm_gain
+    )
+
+    grad_scale = (own_rows * n_tensor * n_dp) ** (-0.5)
+    up_total, down_total = up_total.astype(jnp.bfloat16), down_total.astype(jnp.bfloat16)
+    grad_up = jnp.zeros(w_up.shape, jnp.float32)
+    grad_down = jnp.zeros(w_down.shape, jnp.float32)
+    for k in range(n_dp):
+        other = place ^ k
+        block = lax.dynamic_slice_in_dim(up_total, other * depth, depth, 0)
+        block = swap(block, "dp", k) if k else block
+        block = block.astype(jnp.float32) * grad_scale
+        grad_up = lax.dynamic_update_slice_in_dim(grad_up, block, other * units, 1)
+    for k in range(n_dp):
+        other = place ^ k
+        block = lax.dynamic_slice_in_dim(down_total, other * depth, depth, 1)
+        block = swap(block, "dp", k) if k else block
+        block = block.astype(jnp.float32) * grad_scale
+        grad_down = lax.dynamic_update_slice_in_dim(grad_down, block, other * units, 0)
+
+    for axis in ("dp", "tensor"):
+        for bit in bits_of(lax.axis_size(axis)):
+            stats = stats + swap(stats, axis, bit)
+    return (second_in, grad_first_in, grad_up, grad_down, stats * grad_scale)
+
+
+def body(first_out, second_out, grad_first, grad_second, w_up, *rest):
+    n_dp, n_tensor = lax.axis_size("dp"), lax.axis_size("tensor")
+    powers = all(size & (size - 1) == 0 for size in (n_dp, n_tensor))
+    few_tokens = first_out.shape[0] * n_tensor < w_up.shape[1]
+    fits = w_up.shape[1] % n_dp == 0
+    pick = gather_tokens_body if powers and few_tokens and fits else gather_weights_body
+    return pick(first_out, second_out, grad_first, grad_second, w_up, *rest)
 
 
 def solution(mesh):

time: 443 us -> 239 us (0.54)
  waiting for transfers between devices: 340 us -> 149 us
  starting transfers between devices: 0.5 us -> 54 us
  blocking collectives: 33.4 us -> 0 us
  matrix products: 38.7 us -> 20.7 us
  between operations: 14.2 us -> 1.45 us
  other arithmetic: 14.5 us -> 5.24 us
  local copies, waits for them, and re-layouts: 1.25 us -> 8.84 us
    all_gather x4 -> x0, waiting for transfers between devices: 190 us -> none  [the longest x1 82.2 us: body(): lax.all_gather(w_down, 'dp', axis=1, tiled=True)]
    ppermute x0 -> x38, waiting for transfers between devices: none -> 149 us  [swap(): lax.ppermute(values, axis, [(i, i ^ mask) for i in range(lax.axis_size(ax...]
    reduce_scatter x4 -> x0, waiting for transfers between devices: 148 us -> none  [the longest x1 76.9 us: body(): lax.psum_scatter(grad_down_part.astype(jnp.bfloat16), 'dp', scatter_dimen...]
    ppermute x0 -> x38, starting transfers between devices: none -> 54 us  [swap(): lax.ppermute(values, axis, [(i, i ^ mask) for i in range(lax.axis_size(ax...]
    psum x1 -> x0, blocking collectives: 33.4 us -> none  [body(): grad_norm = lax.psum(local_stats, ('tensor', 'dp')) * grad_scale]
    dot_general x4 -> x16, matrix products: 26.9 us -> 14.3 us  [the longest x8 8.06 us: contract_last(): lax.dot_general(left_rows, right_rows, (((1,), (1,)), ((), ())), preferre...]
    mul x4 -> x1, other arithmetic: 6.41 us -> 0.61 us  [gather_tokens_body(): return (second_in, grad_first_in, grad_up, grad_down, stats * grad_scale)]
    dot_general x2 -> x8, matrix products: 11.8 us -> 6.35 us  [contract_tokens(): lax.dot_general(left_rows, right_rows, (((0,), (0,)), ((), ())), preferre...]
  transfers between devices with their start and end apart: 8 -> 38, of which waited for: 7 -> 18; matrix products, arithmetic and copies ran while one was open for 8% -> 13% of each run, Pallas kernels for 0% -> 0%
where the time goes in v1:
time: 239 us
  waiting for transfers between devices  149 us (62%)
  starting transfers between devices  54 us (23%)
  matrix products  20.7 us (9%)
  local copies, waits for them, and re-layouts  8.84 us (4%)
  other arithmetic  5.24 us (2%)
    ppermute x38, waiting for transfers between devices, swap(): lax.ppermute(values, axis, [(i, i ^ mask) for i in range(lax.axis_size(ax...  149 us
    ppermute x38, starting transfers between devices, swap(): lax.ppermute(values, axis, [(i, i ^ mask) for i in range(lax.axis_size(ax...  54 us
    dot_general x8, matrix products, contract_last(): lax.dot_general(left_rows, right_rows, (((1,), (1,)), ((), ())), preferre...  8.06 us
    dot_general x8, matrix products, contract_tokens(): lax.dot_general(left_rows, right_rows, (((0,), (0,)), ((), ())), preferre...  6.35 us
  transfers between devices with their start and end apart: 38, of which 18 were waited for; matrix products, arithmetic and copies ran while one was open for 13% of the time, Pallas kernels for 0%

profile of v1, /device:TPU:0, one launch (start us, length us, event | category | flops | bytes accessed | tf_op | source)
XLA Modules:
  0.0 238.8 jit_solution(2686490282351737355)
XLA Ops:
  0.8 2.2 constant_dynamic-slice_fusion.5
  3.0 3.1 %collective-permute-start.5 = (bf16[512,256]{1,0:T(8,128)(2,1)}, bf16[512,256]{1,0:T(8,128)(2,1)}, u32[]{:S(2)}, u32[]{:S(2)}) collective-permute-start(bf16[512,256]{1,0:T(8,128)(2,1)} %get-tuple-element.17), channel_id=1, source_target_pairs={{0,1},{1,0},{2,3},{3,2},{4,5},{5,4},{6,7},{7,6},{8,9},{9,8},{10,11... | collective-permute-start | bytes 786440 | tf_op jit(solution)/shard_map/ppermute | solution.py:96
  7.8 2.1 collective-permute-start.10
  11.4 2.6 %collective-permute-start.6 = (bf16[512,256]{1,0:T(8,128)(2,1)}, bf16[512,256]{1,0:T(8,128)(2,1)}, u32[]{:S(2)}, u32[]{:S(2)}) collective-permute-start(bf16[512,256]{1,0:T(8,128)(2,1)} %get-tuple-element.19), channel_id=1, source_target_pairs={{0,2},{1,3},{2,0},{3,1},{4,6},{5,7},{6,4},{7,5},{8,10},{9,11},{10,... | collective-permute-start | bytes 786440 | tf_op jit(solution)/shard_map/ppermute | solution.py:96
  14.0 12.9 %collective-permute-start.16 = (bf16[2,128,1024]{2,1,0:T(8,128)(2,1)S(1)}, bf16[2,128,1024]{2,1,0:T(8,128)(2,1)S(1)}, u32[]{:S(2)}, u32[]{:S(2)}) collective-permute-start(bf16[2,128,1024]{2,1,0:T(8,128)(2,1)S(1)} %pad_maximum_fusion.9), channel_id=1, source_target_pairs={{0,2},{1,3},{2,0},{3,1},{4,6},{5,7},{6,4},{7,5},{8,10},{9,11},{10,... | collective-permute-start | bytes 1572872 | tf_op jit(solution)/shard_map/ppermute | solution.py:96
  27.0 6.7 %collective-permute-done.2 = bf16[256,512]{1,0:T(8,128)(2,1)} collective-permute-done((bf16[256,512]{1,0:T(8,128)(2,1)}, bf16[256,512]{1,0:T(8,128)(2,1)}, u32[]{:S(2)}, u32[]{:S(2)}) %collective-permute-start.2) | collective-permute-done | bytes 262176 | tf_op jit(solution)/shard_map/ppermute | solution.py:96
  33.6 1.7 constant_dynamic-update-slice_fusion.11
  36.3 1.8 collective-permute-start.7
  38.1 1.7 constant_dynamic-update-slice_fusion.10
  39.8 30.4 %collective-permute-done.3 = bf16[256,512]{1,0:T(8,128)(2,1)S(1)} collective-permute-done((bf16[256,512]{1,0:T(8,128)(2,1)}, bf16[256,512]{1,0:T(8,128)(2,1)S(1)}, u32[]{:S(2)}, u32[]{:S(2)}) %collective-permute-start.3) | collective-permute-done | bytes 262176 | tf_op jit(solution)/shard_map/ppermute | solution.py:96
  70.2 9.6 %collective-permute-start.4 = (bf16[256,512]{1,0:T(8,128)(2,1)}, bf16[256,512]{1,0:T(8,128)(2,1)S(1)}, u32[]{:S(2)}, u32[]{:S(2)}) collective-permute-start(bf16[256,512]{1,0:T(8,128)(2,1)} %get-tuple-element.20), channel_id=1, source_target_pairs={{0,3},{1,2},{2,1},{3,0},{4,7},{5,6},{6,5},{7,4},{8,11},{9,10},{10,... | collective-permute-start | bytes 786440 | tf_op jit(solution)/shard_map/ppermute | solution.py:96
  79.8 1.6 collective-permute-start.11
  82.2 3.2 %collective-permute-done.4 = bf16[256,512]{1,0:T(8,128)(2,1)S(1)} collective-permute-done((bf16[256,512]{1,0:T(8,128)(2,1)}, bf16[256,512]{1,0:T(8,128)(2,1)S(1)}, u32[]{:S(2)}, u32[]{:S(2)}) %collective-permute-start.4) | collective-permute-done | bytes 262176 | tf_op jit(solution)/shard_map/ppermute | solution.py:96
  86.6 6.9 %collective-permute-done.11 = bf16[2,128,1024]{2,1,0:T(8,128)(2,1)S(1)} collective-permute-done((bf16[2,128,1024]{2,1,0:T(8,128)(2,1)S(1)}, bf16[2,128,1024]{2,1,0:T(8,128)(2,1)S(1)}, u32[]{:S(2)}, u32[]{:S(2)}) %collective-permute-start.11) | collective-permute-done | bytes 524320 | tf_op jit(solution)/shard_map/ppermute | solution.py:96
  93.7 6.6 %collective-permute-done.17 = bf16[2,128,1024]{2,1,0:T(8,128)(2,1)S(1)} collective-permute-done((bf16[2,128,1024]{2,1,0:T(8,128)(2,1)S(1)}, bf16[2,128,1024]{2,1,0:T(8,128)(2,1)S(1)}, u32[]{:S(2)}, u32[]{:S(2)}) %collective-permute-start.17) | collective-permute-done | bytes 524320 | tf_op jit(solution)/shard_map/ppermute | solution.py:96
  100.5 1.6 collective-permute-start.22
  106.3 8.5 %collective-permute-done.22 = bf16[2,128,1024]{2,1,0:T(8,128)(2,1)S(1)} collective-permute-done((bf16[2,128,1024]{2,1,0:T(8,128)(2,1)S(1)}, bf16[2,128,1024]{2,1,0:T(8,128)(2,1)S(1)}, u32[]{:S(2)}, u32[]{:S(2)}) %collective-permute-start.22) | collective-permute-done | bytes 524320 | tf_op jit(solution)/shard_map/ppermute | solution.py:96
  131.1 1.6 collective-permute-start.9
  137.2 1.6 collective-permute-start.14
  139.5 17.6 %collective-permute-done.25 = bf16[2,128,1024]{2,1,0:T(8,128)(2,1)S(1)} collective-permute-done((bf16[2,128,1024]{2,1,0:T(8,128)(2,1)S(1)}, bf16[2,128,1024]{2,1,0:T(8,128)(2,1)S(1)}, u32[]{:S(2)}, u32[]{:S(2)}) %collective-permute-start.25) | collective-permute-done | bytes 524320 | tf_op jit(solution)/shard_map/ppermute | solution.py:96
  158.2 10.1 %collective-permute-done.14 = bf16[2,128,1024]{2,1,0:T(8,128)(2,1)S(1)} collective-permute-done((bf16[2,128,1024]{2,1,0:T(8,128)(2,1)S(1)}, bf16[2,128,1024]{2,1,0:T(8,128)(2,1)S(1)}, u32[]{:S(2)}, u32[]{:S(2)}) %collective-permute-start.14) | collective-permute-done | bytes 524320 | tf_op jit(solution)/shard_map/ppermute | solution.py:96
  168.4 10.8 %collective-permute-done.20 = bf16[2,128,1024]{2,1,0:T(8,128)(2,1)S(1)} collective-permute-done((bf16[2,128,1024]{2,1,0:T(8,128)(2,1)S(1)}, bf16[2,128,1024]{2,1,0:T(8,128)(2,1)S(1)}, u32[]{:S(2)}, u32[]{:S(2)}) %collective-permute-start.20) | collective-permute-done | bytes 524320 | tf_op jit(solution)/shard_map/ppermute | solution.py:96
  179.2 2.5 %collective-permute-done.26 = bf16[2,128,1024]{2,1,0:T(8,128)(2,1)S(1)} collective-permute-done((bf16[2,128,1024]{2,1,0:T(8,128)(2,1)S(1)}, bf16[2,128,1024]{2,1,0:T(8,128)(2,1)S(1)}, u32[]{:S(2)}, u32[]{:S(2)}) %collective-permute-start.26) | collective-permute-done | bytes 524320 | tf_op jit(solution)/shard_map/ppermute | solution.py:96
  182.1 4.9 %collective-permute-start.29 = (bf16[256,512]{1,0:T(8,128)(2,1)S(1)}, bf16[256,512]{1,0:T(8,128)(2,1)S(1)}, u32[]{:S(2)}, u32[]{:S(2)}) collective-permute-start(bf16[256,512]{1,0:T(8,128)(2,1)S(1)} %get-tuple-element.12), channel_id=1, source_target_pairs={{0,2},{1,3},{2,0},{3,1},{4,6},{5,7},{6,4},{7,5},{8,10},{9,11},{10,... | collective-permute-start | bytes 786440 | tf_op jit(solution)/shard_map/ppermute | solution.py:96
  187.0 14.0 %collective-permute-done.28 = bf16[256,512]{1,0:T(8,128)(2,1)S(1)} collective-permute-done((bf16[256,512]{1,0:T(8,128)(2,1)S(1)}, bf16[256,512]{1,0:T(8,128)(2,1)S(1)}, u32[]{:S(2)}, u32[]{:S(2)}) %collective-permute-start.28) | collective-permute-done | bytes 262176 | tf_op jit(solution)/shard_map/ppermute | solution.py:96
  201.1 2.3 collective-permute-start.30
  203.5 7.7 %collective-permute-done.15 = bf16[2,128,1024]{2,1,0:T(8,128)(2,1)S(1)} collective-permute-done((bf16[2,128,1024]{2,1,0:T(8,128)(2,1)S(1)}, bf16[2,128,1024]{2,1,0:T(8,128)(2,1)S(1)}, u32[]{:S(2)}, u32[]{:S(2)}) %collective-permute-start.15) | collective-permute-done | bytes 524320 | tf_op jit(solution)/shard_map/ppermute | solution.py:96
  211.1 9.3 %collective-permute-done.27 = bf16[2,128,1024]{2,1,0:T(8,128)(2,1)S(1)} collective-permute-done((bf16[2,128,1024]{2,1,0:T(8,128)(2,1)S(1)}, bf16[2,128,1024]{2,1,0:T(8,128)(2,1)S(1)}, u32[]{:S(2)}, u32[]{:S(2)}) %collective-permute-start.27) | collective-permute-done | bytes 524320 | tf_op jit(solution)/shard_map/ppermute | solution.py:96
  221.2 4.8 %collective-permute-done.29 = bf16[256,512]{1,0:T(8,128)(2,1)S(1)} collective-permute-done((bf16[256,512]{1,0:T(8,128)(2,1)S(1)}, bf16[256,512]{1,0:T(8,128)(2,1)S(1)}, u32[]{:S(2)}, u32[]{:S(2)}) %collective-permute-start.29) | collective-permute-done | bytes 262176 | tf_op jit(solution)/shard_map/ppermute | solution.py:96
  226.1 3.4 %collective-permute-done.34 = f32[2,1024]{1,0:T(2,128)S(1)} collective-permute-done((f32[2,1024]{1,0:T(2,128)S(1)}, f32[2,1024]{1,0:T(2,128)S(1)}, u32[]{:S(2)}, u32[]{:S(2)}) %collective-permute-start.34) | collective-permute-done | bytes 8224 | tf_op jit(solution)/shard_map/ppermute | solution.py:96
  229.7 3.5 %collective-permute-done.35 = f32[2,1024]{1,0:T(2,128)S(1)} collective-permute-done((f32[2,1024]{1,0:T(2,128)S(1)}, f32[2,1024]{1,0:T(2,128)S(1)}, u32[]{:S(2)}, u32[]{:S(2)}) %collective-permute-start.35) | collective-permute-done | bytes 8224 | tf_op jit(solution)/shard_map/ppermute | solution.py:96
  234.9 2.1 collective-permute-done.36
  (157 shorter events, 38.0 us)
Async XLA Ops:
  7.1 26.5 %collective-permute-start.2 = (bf16[256,512]{1,0:T(8,128)(2,1)}, bf16[256,512]{1,0:T(8,128)(2,1)}, u32[]{:S(2)}, u32[]{:S(2)}) collective-permute-start(bf16[256,512]{1,0:T(8,128)(2,1)} %get-tuple-element.21), channel_id=1, source_target_pairs={{0,1},{1,0},{2,3},{3,2},{4,5},{5,4},{6,7},{7,6},{8,9},{9,8},{10,11... | collective-permute-start | bytes 786440 | tf_op jit(solution)/shard_map/ppermute | solution.py:96
  7.8 72.0 %collective-permute-start.10 = (bf16[2,128,1024]{2,1,0:T(8,128)(2,1)S(1)}, bf16[2,128,1024]{2,1,0:T(8,128)(2,1)S(1)}, u32[]{:S(2)}, u32[]{:S(2)}) collective-permute-start(bf16[2,128,1024]{2,1,0:T(8,128)(2,1)S(1)} %pad_maximum_fusion.9), channel_id=1, source_target_pairs={{0,1},{1,0},{2,3},{3,2},{4,5},{5,4},{6,7},{7,6},{8,9},{9,8},{10,11... | collective-permute-start | bytes 1572872 | tf_op jit(solution)/shard_map/ppermute | solution.py:96
  9.9 71.5 %collective-permute-start = (bf16[2,128,1024]{2,1,0:T(8,128)(2,1)S(1)}, bf16[2,128,1024]{2,1,0:T(8,128)(2,1)S(1)}, u32[]{:S(2)}, u32[]{:S(2)}) collective-permute-start(bf16[2,128,1024]{2,1,0:T(8,128)(2,1)S(1)} %pad_maximum_fusion.9), channel_id=1, source_target_pairs={{0,8},{4,12},{8,0},{12,4},{1,9},{5,13},{9,1},{13,5},{2,10},{6,14},... | collective-permute-start | bytes 1572872 | tf_op jit(solution)/shard_map/ppermute | solution.py:96
  11.4 24.9 %collective-permute-start.6 = (bf16[512,256]{1,0:T(8,128)(2,1)}, bf16[512,256]{1,0:T(8,128)(2,1)}, u32[]{:S(2)}, u32[]{:S(2)}) collective-permute-start(bf16[512,256]{1,0:T(8,128)(2,1)} %get-tuple-element.19), channel_id=1, source_target_pairs={{0,2},{1,3},{2,0},{3,1},{4,6},{5,7},{6,4},{7,5},{8,10},{9,11},{10,... | collective-permute-start | bytes 786440 | tf_op jit(solution)/shard_map/ppermute | solution.py:96
  14.0 67.5 %collective-permute-start.16 = (bf16[2,128,1024]{2,1,0:T(8,128)(2,1)S(1)}, bf16[2,128,1024]{2,1,0:T(8,128)(2,1)S(1)}, u32[]{:S(2)}, u32[]{:S(2)}) collective-permute-start(bf16[2,128,1024]{2,1,0:T(8,128)(2,1)S(1)} %pad_maximum_fusion.9), channel_id=1, source_target_pairs={{0,2},{1,3},{2,0},{3,1},{4,6},{5,7},{6,4},{7,5},{8,10},{9,11},{10,... | collective-permute-start | bytes 1572872 | tf_op jit(solution)/shard_map/ppermute | solution.py:96
  33.6 36.6 %collective-permute-start.3 = (bf16[256,512]{1,0:T(8,128)(2,1)}, bf16[256,512]{1,0:T(8,128)(2,1)S(1)}, u32[]{:S(2)}, u32[]{:S(2)}) collective-permute-start(bf16[256,512]{1,0:T(8,128)(2,1)} %get-tuple-element.23), channel_id=1, source_target_pairs={{0,2},{1,3},{2,0},{3,1},{4,6},{5,7},{6,4},{7,5},{8,10},{9,11},{10,... | collective-permute-start | bytes 786440 | tf_op jit(solution)/shard_map/ppermute | solution.py:96
  36.3 45.9 %collective-permute-start.7 = (bf16[512,256]{1,0:T(8,128)(2,1)}, bf16[512,256]{1,0:T(8,128)(2,1)S(1)}, u32[]{:S(2)}, u32[]{:S(2)}) collective-permute-start(bf16[512,256]{1,0:T(8,128)(2,1)} %get-tuple-element.16), channel_id=1, source_target_pairs={{0,3},{1,2},{2,1},{3,0},{4,7},{5,6},{6,5},{7,4},{8,11},{9,10},{10,... | collective-permute-start | bytes 786440 | tf_op jit(solution)/shard_map/ppermute | solution.py:96
  70.2 15.2 %collective-permute-start.4 = (bf16[256,512]{1,0:T(8,128)(2,1)}, bf16[256,512]{1,0:T(8,128)(2,1)S(1)}, u32[]{:S(2)}, u32[]{:S(2)}) collective-permute-start(bf16[256,512]{1,0:T(8,128)(2,1)} %get-tuple-element.20), channel_id=1, source_target_pairs={{0,3},{1,2},{2,1},{3,0},{4,7},{5,6},{6,5},{7,4},{8,11},{9,10},{10,... | collective-permute-start | bytes 786440 | tf_op jit(solution)/shard_map/ppermute | solution.py:96
  79.8 13.7 %collective-permute-start.11 = (bf16[2,128,1024]{2,1,0:T(8,128)(2,1)S(1)}, bf16[2,128,1024]{2,1,0:T(8,128)(2,1)S(1)}, u32[]{:S(2)}, u32[]{:S(2)}) collective-permute-start(bf16[2,128,1024]{2,1,0:T(8,128)(2,1)S(1)} %collective-permute-done.10), channel_id=1, source_target_pairs={{0,8},{4,12},{8,0},{12,4},{1,9},{5,13},{9,1},{13,5},{2,10},{6,14},... | collective-permute-start | bytes 1572872 | tf_op jit(solution)/shard_map/ppermute | solution.py:96
  81.5 20.7 %collective-permute-start.1 = (bf16[2,256,1024]{2,1,0:T(8,128)(2,1)S(1)}, bf16[2,256,1024]{2,1,0:T(8,128)(2,1)S(1)}, u32[]{:S(2)}, u32[]{:S(2)}) collective-permute-start(bf16[2,256,1024]{2,1,0:T(8,128)(2,1)S(1)} %pad_maximum_fusion.5), channel_id=1, source_target_pairs={{0,4},{4,0},{8,12},{12,8},{1,5},{5,1},{9,13},{13,9},{2,6},{6,2},{1... | collective-permute-start | bytes 3145736 | tf_op jit(solution)/shard_map/ppermute | solution.py:96
  81.6 18.7 %collective-permute-start.17 = (bf16[2,128,1024]{2,1,0:T(8,128)(2,1)S(1)}, bf16[2,128,1024]{2,1,0:T(8,128)(2,1)S(1)}, u32[]{:S(2)}, u32[]{:S(2)}) collective-permute-start(bf16[2,128,1024]{2,1,0:T(8,128)(2,1)S(1)} %collective-permute-done.16), channel_id=1, source_target_pairs={{0,8},{4,12},{8,0},{12,4},{1,9},{5,13},{9,1},{13,5},{2,10},{6,14},... | collective-permute-start | bytes 1572872 | tf_op jit(solution)/shard_map/ppermute | solution.py:96
  85.4 15.0 %collective-permute-start.21 = (bf16[2,128,1024]{2,1,0:T(8,128)(2,1)S(1)}, bf16[2,128,1024]{2,1,0:T(8,128)(2,1)S(1)}, u32[]{:S(2)}, u32[]{:S(2)}) collective-permute-start(bf16[2,128,1024]{2,1,0:T(8,128)(2,1)S(1)} %collective-permute-done.16), channel_id=1, source_target_pairs={{0,1},{1,0},{2,3},{3,2},{4,5},{5,4},{6,7},{7,6},{8,9},{9,8},{10,11... | collective-permute-start | bytes 1572872 | tf_op jit(solution)/shard_map/ppermute | solution.py:96
  93.6 23.0 %collective-permute-start.12 = (bf16[2,256,1024]{2,1,0:T(8,128)(2,1)S(1)}, bf16[2,256,1024]{2,1,0:T(8,128)(2,1)S(1)}, u32[]{:S(2)}, u32[]{:S(2)}) collective-permute-start(bf16[2,256,1024]{2,1,0:T(8,128)(2,1)S(1)} %pad_maximum_fusion.6), channel_id=1, source_target_pairs={{0,4},{4,0},{8,12},{12,8},{1,5},{5,1},{9,13},{13,9},{2,6},{6,2},{1... | collective-permute-start | bytes 3145736 | tf_op jit(solution)/shard_map/ppermute | solution.py:96
  100.4 19.1 %collective-permute-start.18 = (bf16[2,256,1024]{2,1,0:T(8,128)(2,1)S(1)}, bf16[2,256,1024]{2,1,0:T(8,128)(2,1)S(1)}, u32[]{:S(2)}, u32[]{:S(2)}) collective-permute-start(bf16[2,256,1024]{2,1,0:T(8,128)(2,1)S(1)} %pad_maximum_fusion.7), channel_id=1, source_target_pairs={{0,4},{4,0},{8,12},{12,8},{1,5},{5,1},{9,13},{13,9},{2,6},{6,2},{1... | collective-permute-start | bytes 3145736 | tf_op jit(solution)/shard_map/ppermute | solution.py:96
  100.5 14.3 %collective-permute-start.22 = (bf16[2,128,1024]{2,1,0:T(8,128)(2,1)S(1)}, bf16[2,128,1024]{2,1,0:T(8,128)(2,1)S(1)}, u32[]{:S(2)}, u32[]{:S(2)}) collective-permute-start(bf16[2,128,1024]{2,1,0:T(8,128)(2,1)S(1)} %collective-permute-done.21), channel_id=1, source_target_pairs={{0,8},{4,12},{8,0},{12,4},{1,9},{5,13},{9,1},{13,5},{2,10},{6,14},... | collective-permute-start | bytes 1572872 | tf_op jit(solution)/shard_map/ppermute | solution.py:96
  106.1 24.8 %collective-permute-start.8 = (bf16[2,256,1024]{2,1,0:T(8,128)(2,1)S(1)}, bf16[2,256,1024]{2,1,0:T(8,128)(2,1)S(1)}, u32[]{:S(2)}, u32[]{:S(2)}) collective-permute-start(bf16[2,256,1024]{2,1,0:T(8,128)(2,1)S(1)} %pad_maximum_fusion.4), channel_id=1, source_target_pairs={{0,4},{4,0},{8,12},{12,8},{1,5},{5,1},{9,13},{13,9},{2,6},{6,2},{1... | collective-permute-start | bytes 3145736 | tf_op jit(solution)/shard_map/ppermute | solution.py:96
  114.9 13.1 %collective-permute-start.23 = (bf16[2,256,1024]{2,1,0:T(8,128)(2,1)S(1)}, bf16[2,256,1024]{2,1,0:T(8,128)(2,1)S(1)}, u32[]{:S(2)}, u32[]{:S(2)}) collective-permute-start(bf16[2,256,1024]{2,1,0:T(8,128)(2,1)S(1)} %pad_maximum_fusion.8), channel_id=1, source_target_pairs={{0,4},{4,0},{8,12},{12,8},{1,5},{5,1},{9,13},{13,9},{2,6},{6,2},{1... | collective-permute-start | bytes 3145736 | tf_op jit(solution)/shard_map/ppermute | solution.py:96
  124.1 12.9 %collective-permute-start.13 = (bf16[2,256,1024]{2,1,0:T(8,128)(2,1)S(1)}, bf16[2,256,1024]{2,1,0:T(8,128)(2,1)S(1)}, u32[]{:S(2)}, u32[]{:S(2)}) collective-permute-start(bf16[2,256,1024]{2,1,0:T(8,128)(2,1)S(1)} %pad_maximum_fusion.3), channel_id=1, source_target_pairs={{0,4},{4,0},{8,12},{12,8},{1,5},{5,1},{9,13},{13,9},{2,6},{6,2},{1... | collective-permute-start | bytes 3145736 | tf_op jit(solution)/shard_map/ppermute | solution.py:96
  125.5 13.3 %collective-permute-start.19 = (bf16[2,256,1024]{2,1,0:T(8,128)(2,1)S(1)}, bf16[2,256,1024]{2,1,0:T(8,128)(2,1)S(1)}, u32[]{:S(2)}, u32[]{:S(2)}) collective-permute-start(bf16[2,256,1024]{2,1,0:T(8,128)(2,1)S(1)} %pad_maximum_fusion.2), channel_id=1, source_target_pairs={{0,4},{4,0},{8,12},{12,8},{1,5},{5,1},{9,13},{13,9},{2,6},{6,2},{1... | collective-permute-start | bytes 3145736 | tf_op jit(solution)/shard_map/ppermute | solution.py:96
  131.1 72.4 %collective-permute-start.9 = (bf16[2,128,1024]{2,1,0:T(8,128)(2,1)S(1)}, bf16[2,128,1024]{2,1,0:T(8,128)(2,1)S(1)}, u32[]{:S(2)}, u32[]{:S(2)}) collective-permute-start(bf16[2,128,1024]{2,1,0:T(8,128)(2,1)S(1)} %slice.109), channel_id=1, source_target_pairs={{0,8},{4,12},{8,0},{12,4},{1,9},{5,13},{9,1},{13,5},{2,10},{6,14},... | collective-permute-start | bytes 1572872 | tf_op jit(solution)/shard_map/ppermute | solution.py:96
  134.8 22.8 %collective-permute-start.31 = (bf16[512,256]{1,0:T(8,128)(2,1)S(1)}, bf16[512,256]{1,0:T(8,128)(2,1)S(1)}, u32[]{:S(2)}, u32[]{:S(2)}) collective-permute-start(bf16[512,256]{1,0:T(8,128)(2,1)S(1)} %get-tuple-element.10), channel_id=1, source_target_pairs={{0,1},{1,0},{2,3},{3,2},{4,5},{5,4},{6,7},{7,6},{8,9},{9,8},{10,11... | collective-permute-start | bytes 786440 | tf_op jit(solution)/shard_map/ppermute | solution.py:96
  136.4 20.7 %collective-permute-start.25 = (bf16[2,128,1024]{2,1,0:T(8,128)(2,1)S(1)}, bf16[2,128,1024]{2,1,0:T(8,128)(2,1)S(1)}, u32[]{:S(2)}, u32[]{:S(2)}) collective-permute-start(bf16[2,128,1024]{2,1,0:T(8,128)(2,1)S(1)} %slice.127), channel_id=1, source_target_pairs={{0,8},{4,12},{8,0},{12,4},{1,9},{5,13},{9,1},{13,5},{2,10},{6,14},... | collective-permute-start | bytes 1572872 | tf_op jit(solution)/shard_map/ppermute | solution.py:96
  137.2 31.2 %collective-permute-start.14 = (bf16[2,128,1024]{2,1,0:T(8,128)(2,1)S(1)}, bf16[2,128,1024]{2,1,0:T(8,128)(2,1)S(1)}, u32[]{:S(2)}, u32[]{:S(2)}) collective-permute-start(bf16[2,128,1024]{2,1,0:T(8,128)(2,1)S(1)} %slice.115), channel_id=1, source_target_pairs={{0,8},{4,12},{8,0},{12,4},{1,9},{5,13},{9,1},{13,5},{2,10},{6,14},... | collective-permute-start | bytes 1572872 | tf_op jit(solution)/shard_map/ppermute | solution.py:96
  138.9 40.2 %collective-permute-start.20 = (bf16[2,128,1024]{2,1,0:T(8,128)(2,1)S(1)}, bf16[2,128,1024]{2,1,0:T(8,128)(2,1)S(1)}, u32[]{:S(2)}, u32[]{:S(2)}) collective-permute-start(bf16[2,128,1024]{2,1,0:T(8,128)(2,1)S(1)} %slice.121), channel_id=1, source_target_pairs={{0,8},{4,12},{8,0},{12,4},{1,9},{5,13},{9,1},{13,5},{2,10},{6,14},... | collective-permute-start | bytes 1572872 | tf_op jit(solution)/shard_map/ppermute | solution.py:96
  157.2 24.5 %collective-permute-start.26 = (bf16[2,128,1024]{2,1,0:T(8,128)(2,1)S(1)}, bf16[2,128,1024]{2,1,0:T(8,128)(2,1)S(1)}, u32[]{:S(2)}, u32[]{:S(2)}) collective-permute-start(bf16[2,128,1024]{2,1,0:T(8,128)(2,1)S(1)} %slice_add_fusion), channel_id=1, source_target_pairs={{0,1},{1,0},{2,3},{3,2},{4,5},{5,4},{6,7},{7,6},{8,9},{9,8},{10,11... | collective-permute-start | bytes 1572872 | tf_op jit(solution)/shard_map/ppermute | solution.py:96
  157.6 24.4 %collective-permute-start.32 = (bf16[512,256]{1,0:T(8,128)(2,1)S(1)}, bf16[512,256]{1,0:T(8,128)(2,1)S(1)}, u32[]{:S(2)}, u32[]{:S(2)}) collective-permute-start(bf16[512,256]{1,0:T(8,128)(2,1)S(1)} %get-tuple-element.9), channel_id=1, source_target_pairs={{0,2},{1,3},{2,0},{3,1},{4,6},{5,7},{6,4},{7,5},{8,10},{9,11},{10,... | collective-permute-start | bytes 786440 | tf_op jit(solution)/shard_map/ppermute | solution.py:96
  168.3 13.8 %collective-permute-start.33 = (bf16[512,256]{1,0:T(8,128)(2,1)S(1)}, bf16[512,256]{1,0:T(8,128)(2,1)S(1)}, u32[]{:S(2)}, u32[]{:S(2)}) collective-permute-start(bf16[512,256]{1,0:T(8,128)(2,1)S(1)} %get-tuple-element.8), channel_id=1, source_target_pairs={{0,3},{1,2},{2,1},{3,0},{4,7},{5,6},{6,5},{7,4},{8,11},{9,10},{10,... | collective-permute-start | bytes 786440 | tf_op jit(solution)/shard_map/ppermute | solution.py:96
  179.2 21.9 %collective-permute-start.28 = (bf16[256,512]{1,0:T(8,128)(2,1)S(1)}, bf16[256,512]{1,0:T(8,128)(2,1)S(1)}, u32[]{:S(2)}, u32[]{:S(2)}) collective-permute-start(bf16[256,512]{1,0:T(8,128)(2,1)S(1)} %get-tuple-element.13), channel_id=1, source_target_pairs={{0,1},{1,0},{2,3},{3,2},{4,5},{5,4},{6,7},{7,6},{8,9},{9,8},{10,11... | collective-permute-start | bytes 786440 | tf_op jit(solution)/shard_map/ppermute | solution.py:96
  181.7 29.5 %collective-permute-start.15 = (bf16[2,128,1024]{2,1,0:T(8,128)(2,1)S(1)}, bf16[2,128,1024]{2,1,0:T(8,128)(2,1)S(1)}, u32[]{:S(2)}, u32[]{:S(2)}) collective-permute-start(bf16[2,128,1024]{2,1,0:T(8,128)(2,1)S(1)} %slice_add_fusion.2), channel_id=1, source_target_pairs={{0,1},{1,0},{2,3},{3,2},{4,5},{5,4},{6,7},{7,6},{8,9},{9,8},{10,11... | collective-permute-start | bytes 1572872 | tf_op jit(solution)/shard_map/ppermute | solution.py:96
  182.0 38.5 %collective-permute-start.27 = (bf16[2,128,1024]{2,1,0:T(8,128)(2,1)S(1)}, bf16[2,128,1024]{2,1,0:T(8,128)(2,1)S(1)}, u32[]{:S(2)}, u32[]{:S(2)}) collective-permute-start(bf16[2,128,1024]{2,1,0:T(8,128)(2,1)S(1)} %add_convert_fusion.2), channel_id=1, source_target_pairs={{0,2},{1,3},{2,0},{3,1},{4,6},{5,7},{6,4},{7,5},{8,10},{9,11},{10,... | collective-permute-start | bytes 1572872 | tf_op jit(solution)/shard_map/ppermute | solution.py:96
  182.1 43.9 %collective-permute-start.29 = (bf16[256,512]{1,0:T(8,128)(2,1)S(1)}, bf16[256,512]{1,0:T(8,128)(2,1)S(1)}, u32[]{:S(2)}, u32[]{:S(2)}) collective-permute-start(bf16[256,512]{1,0:T(8,128)(2,1)S(1)} %get-tuple-element.12), channel_id=1, source_target_pairs={{0,2},{1,3},{2,0},{3,1},{4,6},{5,7},{6,4},{7,5},{8,10},{9,11},{10,... | collective-permute-start | bytes 786440 | tf_op jit(solution)/shard_map/ppermute | solution.py:96
  201.1 28.6 %collective-permute-start.30 = (bf16[256,512]{1,0:T(8,128)(2,1)S(1)}, bf16[256,512]{1,0:T(8,128)(2,1)S(1)}, u32[]{:S(2)}, u32[]{:S(2)}) collective-permute-start(bf16[256,512]{1,0:T(8,128)(2,1)S(1)} %get-tuple-element.11), channel_id=1, source_target_pairs={{0,3},{1,2},{2,1},{3,0},{4,7},{5,6},{6,5},{7,4},{8,11},{9,10},{10,... | collective-permute-start | bytes 786440 | tf_op jit(solution)/shard_map/ppermute | solution.py:96
  (17 other events, 176.7 us)

commit v2 on v1

--- a/solution.py
+++ b/solution.py
@@ -1,6 +1,8 @@
 import jax
 import jax.numpy as jnp
 from jax import lax
+from jax.experimental import pallas as pl
+from jax.experimental.pallas import tpu as pltpu
 from jax.sharding import PartitionSpec as P
 
 epsilon = 1e-06
@@ -100,55 +102,184 @@
     return [1 << b for b in reversed(range(size.bit_length() - 1))]
 
 
+def pack_weights(w_up, w_down, mates):
+    n_dp = lax.axis_size("dp")
+    depth, units = w_up.shape[0], w_up.shape[1] // n_dp
+    up_rows, down_rows, strips = depth // mates, units // mates, units // depth
+    strip_rows = down_rows // strips
+
+    def kernel(up_ref, down_ref, *rest):
+        sends, sem = rest[:-1], rest[-1]
+        place, mate = lax.axis_index("dp"), lax.rem(lax.axis_index("groups"), mates)
+        copies = []
+
+        def copy(src, dst):
+            one = pltpu.make_async_copy(src, dst, sem.at[len(copies)])
+            one.start()
+            copies.append(one)
+
+        for k in range(1, n_dp):
+            first = pl.multiple_of((place ^ k) * units, units)
+            send = sends[k - 1]
+            copy(
+                up_ref.at[pl.ds(pl.multiple_of(mate * up_rows, up_rows), up_rows), pl.ds(first, units)],
+                send.at[pl.ds(0, up_rows), :],
+            )
+            for c in range(strips):
+                row = pl.multiple_of(first + mate * down_rows + c * strip_rows, strip_rows)
+                copy(
+                    down_ref.at[pl.ds(row, strip_rows), :],
+                    send.at[pl.ds(up_rows, strip_rows), pl.ds(c * depth, depth)],
+                )
+        for one in copies:
+            one.wait()
+
+    return pl.pallas_call(
+        kernel,
+        out_shape=[jax.ShapeDtypeStruct((2 * up_rows, units), w_up.dtype)] * (n_dp - 1),
+        in_specs=[pl.BlockSpec(memory_space=pl.ANY)] * 2,
+        out_specs=[pl.BlockSpec(memory_space=pl.ANY)] * (n_dp - 1),
+        scratch_shapes=[pltpu.SemaphoreType.DMA(((n_dp - 1) * (1 + strips),))],
+        name="pack_weights",
+    )(w_up, w_down)
+
+
+def unpack_weights(w_up, w_down, got, mates):
+    n_dp = lax.axis_size("dp")
+    depth, units = w_up.shape[0], w_up.shape[1] // n_dp
+    up_rows, down_rows, strips = depth // mates, units // mates, units // depth
+    strip_rows = down_rows // strips
+
+    def kernel(up_ref, down_ref, *rest):
+        pieces, (up_out, down_out, sem) = rest[:-3], rest[-3:]
+        place, mate = lax.axis_index("dp"), lax.rem(lax.axis_index("groups"), mates)
+        copies = []
+
+        def copy(src, dst):
+            one = pltpu.make_async_copy(src, dst, sem.at[len(copies)])
+            one.start()
+            copies.append(one)
+
+        copy(
+            up_ref.at[:, pl.ds(pl.multiple_of(place * units, units), units)],
+            up_out.at[pl.ds(pl.multiple_of(place * depth, depth), depth), :],
+        )
+        copy(
+            down_ref.at[pl.ds(pl.multiple_of(place * units, units), units), :],
+            down_out.at[:, pl.ds(pl.multiple_of(place * depth, depth), depth)],
+        )
+        for k in range(1, n_dp):
+            first = pl.multiple_of((place ^ k) * depth, depth)
+            for j in range(mates):
+                piece = pieces[j * (n_dp - 1) + k - 1]
+                part = mate ^ j
+                row = pl.multiple_of(first + part * up_rows, up_rows)
+                copy(piece.at[pl.ds(0, up_rows), :], up_out.at[pl.ds(row, up_rows), :])
+                for c in range(strips):
+                    row = pl.multiple_of(part * down_rows + c * strip_rows, strip_rows)
+                    copy(
+                        piece.at[pl.ds(up_rows, strip_rows), pl.ds(c * depth, depth)],
+                        down_out.at[pl.ds(row, strip_rows), pl.ds(first, depth)],
+                    )
+        for one in copies:
+            one.wait()
+
+    return pl.pallas_call(
+        kernel,
+        out_shape=[
+            jax.ShapeDtypeStruct((depth * n_dp, units), w_up.dtype),
+            jax.ShapeDtypeStruct((units, depth * n_dp), w_down.dtype),
+        ],
+        in_specs=[pl.BlockSpec(memory_space=pl.ANY)] * (2 + mates * (n_dp - 1)),
+        out_specs=[pl.BlockSpec(memory_space=pl.ANY)] * 2,
+        scratch_shapes=[pltpu.SemaphoreType.DMA((2 + mates * (n_dp - 1) * (1 + strips),))],
+        name="unpack_weights",
+    )(w_up, w_down, *[piece for pieces in got for piece in pieces])
+
+
+def weight_grads(place, chunks, hiddens, grad_pres, n_dp):
+    n_chunks, (_, rows, width), units = len(chunks), chunks[0].shape, hiddens[0].shape[1]
+    depth = width // n_dp
+    strips = units // depth
+
+    def kernel(place_ref, *refs):
+        toks, hids, pres = refs[:n_chunks], refs[n_chunks : 2 * n_chunks], refs[2 * n_chunks : -1]
+        out = refs[-1]
+        up = down = None
+        for tok, hid, pre in zip(toks, hids, pres, strict=True):
+            one = contract_tokens(tok[0], pre[...])
+            two = contract_tokens(hid[...], tok[1])
+            up, down = (one, two) if up is None else (up + one, down + two)
+        out[0, :depth, :] = up.astype(out.dtype)
+        for c in range(strips):
+            out[0, depth:, c * depth : (c + 1) * depth] = down[c * depth : (c + 1) * depth].astype(out.dtype)
+
+    return pl.pallas_call(
+        kernel,
+        out_shape=jax.ShapeDtypeStruct((n_dp, 2 * depth, units), jnp.bfloat16),
+        grid_spec=pltpu.PrefetchScalarGridSpec(
+            num_scalar_prefetch=1,
+            grid=(n_dp,),
+            in_specs=[pl.BlockSpec((2, rows, depth), lambda k, p: (0, 0, p[0] ^ k))] * n_chunks
+            + [pl.BlockSpec((rows, units), lambda k, p: (0, 0))] * (2 * n_chunks),
+            out_specs=pl.BlockSpec((1, 2 * depth, units), lambda k, p: (k, 0, 0)),
+        ),
+        compiler_params=pltpu.CompilerParams(vmem_limit_bytes=40 * 1024 * 1024),
+        cost_estimate=pl.CostEstimate(
+            flops=4 * n_chunks * rows * width * units,
+            bytes_accessed=4 * n_chunks * rows * (width + units) + 4 * width * units,
+            transcendentals=0,
+        ),
+        name="weight_grads",
+    )(place.reshape(1), *chunks, *hiddens, *grad_pres)
+
+
 def gather_tokens_body(
     first_out, second_out, grad_first, grad_second, w_up, w_down, norm_gain, norm_bias
 ):
-    n_dp, n_tensor = lax.axis_size("dp"), lax.axis_size("tensor")
+    n_dp, n_tensor, n_groups = (lax.axis_size(axis) for axis in ("dp", "tensor", "groups"))
     own_rows, depth = first_out.shape[0], w_up.shape[0]
     units = w_up.shape[1] // n_dp
+    mates = 2 if n_groups % 2 == 0 else 1
     place = lax.axis_index("dp")
     standard, inv_std, normed = normalize(first_out, norm_gain, norm_bias)
-
-    up = jnp.zeros((depth * n_dp, units), w_up.dtype)
-    down = jnp.zeros((units, depth * n_dp), w_down.dtype)
-    for k in range(n_dp):
-        other = place ^ k
-        block = lax.dynamic_slice_in_dim(w_up, other * units, units, 1)
-        block = swap(block, "dp", k) if k else block
-        up = lax.dynamic_update_slice_in_dim(up, block, other * depth, 0)
-    for k in range(n_dp):
-        other = place ^ k
-        block = lax.dynamic_slice_in_dim(w_down, other * units, units, 0)
-        block = swap(block, "dp", k) if k else block
-        down = lax.dynamic_update_slice_in_dim(down, block, other * depth, 1)
 
     chunks = {0: jnp.stack([normed, grad_second])}
     for bit in bits_of(n_dp):
         chunks.update({k | bit: swap(chunk, "dp", bit) for k, chunk in chunks.items()})
 
-    sums = {}
-    up_total = down_total = 0.0
+    sends = pack_weights(w_up, w_down, mates)
+    got = [[swap(sends[k - 1], "dp", k) for k in range(1, n_dp)]]
+    if mates == 2:
+        got.append([swap(piece, "groups", 1) for piece in got[0]])
+    up, down = unpack_weights(w_up, w_down, got, mates)
+
+    sums, hiddens, grad_pres = {}, {}, {}
     for k in sorted(chunks):
         chunk = chunks[k]
         for bit in bits_of(n_tensor):
             chunk = jnp.concatenate([chunk, swap(chunk, "tensor", bit)], axis=1)
-        rows, grads = chunk[0], chunk[1]
+        chunks[k] = chunk
+    for k in sorted(chunks, key=lambda k: (k & 1 == 0, -k)):
+        rows, grads = chunks[k][0], chunks[k][1]
         preact = jnp.dot(rows, up, preferred_element_type=jnp.float32)
-        hidden = jax.nn.gelu(preact).astype(jnp.bfloat16)
+        hiddens[k] = jax.nn.gelu(preact).astype(jnp.bfloat16)
         grad_hidden = contract_last(grads, down)
-        grad_pre = jax.vjp(jax.nn.gelu, preact)[1](grad_hidden)[0].astype(jnp.bfloat16)
+        grad_pres[k] = jax.vjp(jax.nn.gelu, preact)[1](grad_hidden)[0].astype(jnp.bfloat16)
         part = jnp.stack(
             [
-                jnp.dot(hidden, down, preferred_element_type=jnp.float32).astype(jnp.bfloat16),
-                contract_last(grad_pre, up).astype(jnp.bfloat16),
+                jnp.dot(hiddens[k], down, preferred_element_type=jnp.float32).astype(jnp.bfloat16),
+                contract_last(grad_pres[k], up).astype(jnp.bfloat16),
             ]
         )
-        up_total = up_total + contract_tokens(rows, grad_pre)
-        down_total = down_total + contract_tokens(hidden, grads)
         for bit in reversed(bits_of(n_tensor)):
             half = part.shape[1] // 2
             part = part[:, :half] + swap(part[:, half:], "tensor", bit)
         sums[k] = part
+    order = sorted(chunks)
+    blocks = weight_grads(
+        place, [chunks[k] for k in order], [hiddens[k] for k in order], [grad_pres[k] for k in order], n_dp
+    )
     for bit in reversed(bits_of(n_dp)):
         for k in [k for k in sums if k & bit]:
             got = swap(sums.pop(k), "dp", bit).astype(jnp.float32)
@@ -160,21 +291,17 @@
     )
 
     grad_scale = (own_rows * n_tensor * n_dp) ** (-0.5)
-    up_total, down_total = up_total.astype(jnp.bfloat16), down_total.astype(jnp.bfloat16)
     grad_up = jnp.zeros(w_up.shape, jnp.float32)
     grad_down = jnp.zeros(w_down.shape, jnp.float32)
     for k in range(n_dp):
         other = place ^ k
-        block = lax.dynamic_slice_in_dim(up_total, other * depth, depth, 0)
-        block = swap(block, "dp", k) if k else block
+        block = swap(blocks[k], "dp", k) if k else blocks[k]
         block = block.astype(jnp.float32) * grad_scale
-        grad_up = lax.dynamic_update_slice_in_dim(grad_up, block, other * units, 1)
-    for k in range(n_dp):
-        other = place ^ k
-        block = lax.dynamic_slice_in_dim(down_total, other * depth, depth, 1)
-        block = swap(block, "dp", k) if k else block
-        block = block.astype(jnp.float32) * grad_scale
-        grad_down = lax.dynamic_update_slice_in_dim(grad_down, block, other * units, 0)
+        grad_up = lax.dynamic_update_slice_in_dim(grad_up, block[:depth], other * units, 1)
+        strips = [block[depth:, c * depth : (c + 1) * depth] for c in range(units // depth)]
+        grad_down = lax.dynamic_update_slice_in_dim(
+            grad_down, jnp.concatenate(strips, axis=0), other * units, 0
+        )
 
     for axis in ("dp", "tensor"):
         for bit in bits_of(lax.axis_size(axis)):
@@ -186,7 +313,8 @@
     n_dp, n_tensor = lax.axis_size("dp"), lax.axis_size("tensor")
     powers = all(size & (size - 1) == 0 for size in (n_dp, n_tensor))
     few_tokens = first_out.shape[0] * n_tensor < w_up.shape[1]
-    fits = w_up.shape[1] % n_dp == 0
+    units, depth = w_up.shape[1] // n_dp, w_up.shape[0]
+    fits = w_up.shape[1] % n_dp == 0 and units % depth == 0 and depth % 128 == 0
     pick = gather_tokens_body if powers and few_tokens and fits else gather_weights_body
     return pick(first_out, second_out, grad_first, grad_second, w_up, *rest)
 

time: 239 us -> 317 us (1.33)
  Pallas kernels: 0 us -> 96.8 us
  starting transfers between devices: 54 us -> 32 us
  other arithmetic: 5.24 us -> 13.5 us
  matrix products: 20.7 us -> 14.7 us
  local copies, waits for them, and re-layouts: 8.84 us -> 3.7 us
  waiting for transfers between devices: 149 us -> 154 us
    pallas_call x0 -> x3, Pallas kernels: none -> 96.8 us  [the longest x1 64.8 us: unpack_weights(): pl.pallas_call(kernel, out_shape=[jax.ShapeDtypeStruct((depth * n_dp, uni...]
    ppermute x38 -> x35, starting transfers between devices: 54 us -> 32 us  [swap(): lax.ppermute(values, axis, [(i, i ^ mask) for i in range(lax.axis_size(ax...]
    dot_general x12 -> x4, matrix products: 9.77 us -> 3.03 us  [gather_tokens_body(): jnp.dot(hiddens[k], down, preferred_element_type=jnp.float32)]
    ppermute x38 -> x35, waiting for transfers between devices: 149 us -> 154 us  [swap(): lax.ppermute(values, axis, [(i, i ^ mask) for i in range(lax.axis_size(ax...]
    dynamic_update_slice x6 -> x4, local copies, waits for them, and re-layouts: 4.37 us -> 0.2 us  [gather_tokens_body(): lax.dynamic_update_slice_in_dim(grad_up, block[:depth], other * units, 1)]
    add x6, other arithmetic: 0.6 us -> 4.3 us  [gather_tokens_body(): part = part[:, :half] + swap(part[:, half:], 'tensor', bit)]
    dynamic_slice x4 -> x0, local copies, waits for them, and re-layouts: 3.29 us -> none  [the longest x1 2.19 us: gather_tokens_body(): block = lax.dynamic_slice_in_dim(w_down, other * units, units, 0)]
  transfers between devices with their start and end apart: 38 -> 35, of which waited for: 18 -> 15; matrix products, arithmetic and copies ran while one was open for 13% -> 9% of each run, Pallas kernels for 0% -> 23%
where the time goes in v2:
time: 317 us; the launch traced here: 316 us
  waiting for transfers between devices  154 us (49%)
  Pallas kernels  96.8 us (31%)
  starting transfers between devices  32 us (10%)
  matrix products  14.7 us (5%)
  other arithmetic  13.5 us (4%)
  local copies, waits for them, and re-layouts  3.7 us (1%)
    ppermute x35, waiting for transfers between devices, swap(): lax.ppermute(values, axis, [(i, i ^ mask) for i in range(lax.axis_size(ax...  154 us
    pallas_call x1, Pallas kernels, unpack_weights(): pl.pallas_call(kernel, out_shape=[jax.ShapeDtypeStruct((depth * n_dp, uni...  64.8 us
    ppermute x35, starting transfers between devices, swap(): lax.ppermute(values, axis, [(i, i ^ mask) for i in range(lax.axis_size(ax...  32 us
    pallas_call x1, Pallas kernels, pack_weights(): pl.pallas_call(kernel, out_shape=[jax.ShapeDtypeStruct((2 * up_rows, unit...  25 us
    dot_general x8, matrix products, contract_last(): lax.dot_general(left_rows, right_rows, (((1,), (1,)), ((), ())), preferre...  8.03 us
    pallas_call x1, Pallas kernels, weight_grads(): pl.pallas_call(kernel, out_shape=jax.ShapeDtypeStruct((n_dp, 2 * depth, u...  6.96 us
  transfers between devices with their start and end apart: 35, of which 15 were waited for; matrix products, arithmetic and copies ran while one was open for 9% of the time, Pallas kernels for 23%

profile of v2, /device:TPU:0, one launch (start us, length us, event | category | flops | bytes accessed | tf_op | source)
XLA Modules:
  0.0 316.4 jit_solution(13090175112491140279)
XLA Ops:
  0.7 25.0 %pack_weights.1 = (bf16[256,512]{1,0:T(8,128)(2,1)}, bf16[256,512]{1,0:T(8,128)(2,1)}, bf16[256,512]{1,0:T(8,128)(2,1)}) custom-call(bf16[256,2048]{1,0:T(8,128)(2,1)} %up_ref.3, bf16[2048,256]{1,0:T(8,128)(2,1)} %down_ref.3), custom_call_target="tpu_custom_call" | custom-call | tf_op jit(solution)/shard_map/pack_weights/pallas_call | solution.py:137
  25.7 3.1 collective-permute-start.2
  29.5 2.7 collective-permute-start.16
  32.7 1.8 collective-permute-start
  34.5 6.6 %collective-permute-done.2.rest_0_ = bf16[256,512]{1,0:T(8,128)(2,1)S(1)} collective-permute-done((bf16[256,512]{1,0:T(8,128)(2,1)}, bf16[256,512]{1,0:T(8,128)(2,1)S(1)}, u32[]{:S(2)}, u32[]{:S(2)}) %collective-permute-start.2) | collective-permute-done | bytes 262176 | tf_op jit(solution)/shard_map/ppermute | solution.py:98
  41.1 3.0 collective-permute-start.4
  44.1 29.4 %collective-permute-done.3.rest_1_ = bf16[256,512]{1,0:T(8,128)(2,1)S(1)} collective-permute-done((bf16[256,512]{1,0:T(8,128)(2,1)S(1)}, bf16[256,512]{1,0:T(8,128)(2,1)S(1)}, u32[]{:S(2)}, u32[]{:S(2)}) %collective-permute-start.3) | collective-permute-done | bytes 262176 | tf_op jit(solution)/shard_map/ppermute | solution.py:98
  73.5 1.5 collective-permute-start.5
  75.0 1.6 collective-permute-start.17
  76.5 6.1 %collective-permute-done.5.rest_3_ = bf16[256,512]{1,0:T(8,128)(2,1)S(1)} collective-permute-done((bf16[256,512]{1,0:T(8,128)(2,1)S(1)}, bf16[256,512]{1,0:T(8,128)(2,1)S(1)}, u32[]{:S(2)}, u32[]{:S(2)}) %collective-permute-start.5) | collective-permute-done | bytes 262176 | tf_op jit(solution)/shard_map/ppermute | solution.py:98
  82.7 1.5 collective-permute-start.6
  86.9 2.2 collective-permute-done.6.rest_4_
  89.7 2.2 collective-permute-done.7.rest_5_
  91.9 64.8 %unpack_weights.1 = (bf16[1024,512]{1,0:T(8,128)(2,1)}, bf16[512,1024]{1,0:T(8,128)(2,1)}) custom-call(bf16[256,2048]{1,0:T(8,128)(2,1)} %up_ref.3, bf16[2048,256]{1,0:T(8,128)(2,1)} %down_ref.3, bf16[256,512]{1,0:T(8,128)(2,1)} %copy-done.6, bf16[256,512]{1,0:T(8,128)(2,1)} %copy-done.7, bf16[256,512]{1,0:T(8,128)(2,1)} %collective-permute-done.4.rest_2_, ...), custom_call_target="tpu_custom_call" | custom-call | tf_op jit(solution)/shard_map/unpack_weights/pallas_call | solution.py:187
  158.9 10.2 %collective-permute-done.22 = bf16[2,128,1024]{2,1,0:T(8,128)(2,1)S(1)} collective-permute-done((bf16[2,128,1024]{2,1,0:T(8,128)(2,1)S(1)}, bf16[2,128,1024]{2,1,0:T(8,128)(2,1)S(1)}, u32[]{:S(2)}, u32[]{:S(2)}) %collective-permute-start.22) | collective-permute-done | bytes 524320 | tf_op jit(solution)/shard_map/ppermute | solution.py:98
  169.2 1.5 pad_maximum_fusion.refs_0_
  191.0 7.0 %weight_grads.1 = bf16[4,512,512]{2,1,0:T(8,128)(2,1)S(1)} custom-call(s32[1]{0:T(128)} %bitcast.20.place_ref, bf16[2,512,1024]{2,1,0:T(8,128)(2,1)S(1)} %pad_maximum_fusion.refs_0_, bf16[2,512,1024]{2,1,0:T(8,128)(2,1)S(1)} %constant_dynamic-update-slice_fusion.refs_1_, bf16[2,512,1024]{2,1,0:T(8,128)(2,1)S(1)} %constant_dynamic-update-slice_fusion.3.refs_2_, ...), custom_call_target="tpu_custom_call" | custom-call | flops 4294967296 | bytes 14680064 | tf_op jit(solution)/shard_map/weight_grads/pallas_call | solution.py:217
  199.0 2.8 collective-permute-start.29
  203.2 1.7 collective-permute-start.30
  204.9 1.3 fusion.41
  206.3 15.7 %collective-permute-done.28 = bf16[512,512]{1,0:T(8,128)(2,1)S(1)} collective-permute-done((bf16[512,512]{1,0:T(8,128)(2,1)S(1)}, bf16[512,512]{1,0:T(8,128)(2,1)S(1)}, u32[]{:S(2)}, u32[]{:S(2)}) %collective-permute-start.28) | collective-permute-done | bytes 524320 | tf_op jit(solution)/shard_map/ppermute | solution.py:98
  223.3 14.0 %collective-permute-done.29 = bf16[512,512]{1,0:T(8,128)(2,1)S(1)} collective-permute-done((bf16[512,512]{1,0:T(8,128)(2,1)S(1)}, bf16[512,512]{1,0:T(8,128)(2,1)S(1)}, u32[]{:S(2)}, u32[]{:S(2)}) %collective-permute-start.29) | collective-permute-done | bytes 524320 | tf_op jit(solution)/shard_map/ppermute | solution.py:98
  238.5 1.3 fusion.37
  241.1 19.7 %collective-permute-done.25 = bf16[2,128,1024]{2,1,0:T(8,128)(2,1)S(1)} collective-permute-done((bf16[2,128,1024]{2,1,0:T(8,128)(2,1)S(1)}, bf16[2,128,1024]{2,1,0:T(8,128)(2,1)S(1)}, u32[]{:S(2)}, u32[]{:S(2)}) %collective-permute-start.25) | collective-permute-done | bytes 524320 | tf_op jit(solution)/shard_map/ppermute | solution.py:98
  261.1 2.1 collective-permute-start.15
  263.2 18.2 %collective-permute-done.26 = bf16[2,128,1024]{2,1,0:T(8,128)(2,1)S(1)} collective-permute-done((bf16[2,128,1024]{2,1,0:T(8,128)(2,1)S(1)}, bf16[2,128,1024]{2,1,0:T(8,128)(2,1)S(1)}, u32[]{:S(2)}, u32[]{:S(2)}) %collective-permute-start.26) | collective-permute-done | bytes 524320 | tf_op jit(solution)/shard_map/ppermute | solution.py:98
  282.2 7.6 %collective-permute-done.15 = bf16[2,128,1024]{2,1,0:T(8,128)(2,1)S(1)} collective-permute-done((bf16[2,128,1024]{2,1,0:T(8,128)(2,1)S(1)}, bf16[2,128,1024]{2,1,0:T(8,128)(2,1)S(1)}, u32[]{:S(2)}, u32[]{:S(2)}) %collective-permute-start.15) | collective-permute-done | bytes 524320 | tf_op jit(solution)/shard_map/ppermute | solution.py:98
  289.8 10.9 %collective-permute-done.27 = bf16[2,128,1024]{2,1,0:T(8,128)(2,1)S(1)} collective-permute-done((bf16[2,128,1024]{2,1,0:T(8,128)(2,1)S(1)}, bf16[2,128,1024]{2,1,0:T(8,128)(2,1)S(1)}, u32[]{:S(2)}, u32[]{:S(2)}) %collective-permute-start.27) | collective-permute-done | bytes 524320 | tf_op jit(solution)/shard_map/ppermute | solution.py:98
  300.7 1.4 convert_add_fusion
  302.6 4.5 %collective-permute-done.31 = f32[2,1024]{1,0:T(2,128)S(1)} collective-permute-done((f32[2,1024]{1,0:T(2,128)S(1)}, f32[2,1024]{1,0:T(2,128)S(1)}, u32[]{:S(2)}, u32[]{:S(2)}) %collective-permute-start.31) | collective-permute-done | bytes 8224 | tf_op jit(solution)/shard_map/ppermute | solution.py:98
  307.2 3.6 %collective-permute-done.32 = f32[2,1024]{1,0:T(2,128)S(1)} collective-permute-done((f32[2,1024]{1,0:T(2,128)S(1)}, f32[2,1024]{1,0:T(2,128)S(1)}, u32[]{:S(2)}, u32[]{:S(2)}) %collective-permute-start.32) | collective-permute-done | bytes 8224 | tf_op jit(solution)/shard_map/ppermute | solution.py:98
  311.2 3.3 %collective-permute-done.33 = f32[2,1024]{1,0:T(2,128)S(1)} collective-permute-done((f32[2,1024]{1,0:T(2,128)S(1)}, f32[2,1024]{1,0:T(2,128)S(1)}, u32[]{:S(2)}, u32[]{:S(2)}) %collective-permute-start.33) | collective-permute-done | bytes 8224 | tf_op jit(solution)/shard_map/ppermute | solution.py:98
  (159 shorter events, 36.8 us)
Async XLA Ops:
  25.7 15.4 %collective-permute-start.2 = (bf16[256,512]{1,0:T(8,128)(2,1)}, bf16[256,512]{1,0:T(8,128)(2,1)S(1)}, u32[]{:S(2)}, u32[]{:S(2)}) collective-permute-start(bf16[256,512]{1,0:T(8,128)(2,1)} %get-tuple-element.10), channel_id=1, source_target_pairs={{0,1},{1,0},{2,3},{3,2},{4,5},{5,4},{6,7},{7,6},{8,9},{9,8},{10,11... | collective-permute-start | bytes 786440 | tf_op jit(solution)/shard_map/ppermute | solution.py:98
  29.5 45.4 %collective-permute-start.16 = (bf16[2,128,1024]{2,1,0:T(8,128)(2,1)S(1)}, bf16[2,128,1024]{2,1,0:T(8,128)(2,1)S(1)}, u32[]{:S(2)}, u32[]{:S(2)}) collective-permute-start(bf16[2,128,1024]{2,1,0:T(8,128)(2,1)S(1)} %pad_maximum_fusion.9), channel_id=1, source_target_pairs={{0,2},{1,3},{2,0},{3,1},{4,6},{5,7},{6,4},{7,5},{8,10},{9,11},{10,... | collective-permute-start | bytes 1572872 | tf_op jit(solution)/shard_map/ppermute | solution.py:98
  32.2 41.3 %collective-permute-start.3 = (bf16[256,512]{1,0:T(8,128)(2,1)S(1)}, bf16[256,512]{1,0:T(8,128)(2,1)S(1)}, u32[]{:S(2)}, u32[]{:S(2)}) collective-permute-start(bf16[256,512]{1,0:T(8,128)(2,1)S(1)} %copy-done.18), channel_id=1, source_target_pairs={{0,2},{1,3},{2,0},{3,1},{4,6},{5,7},{6,4},{7,5},{8,10},{9,11},{10,... | collective-permute-start | bytes 786440 | tf_op jit(solution)/shard_map/ppermute | solution.py:98
  32.5 51.6 %collective-permute-start.10 = (bf16[2,128,1024]{2,1,0:T(8,128)(2,1)S(1)}, bf16[2,128,1024]{2,1,0:T(8,128)(2,1)S(1)}, u32[]{:S(2)}, u32[]{:S(2)}) collective-permute-start(bf16[2,128,1024]{2,1,0:T(8,128)(2,1)S(1)} %pad_maximum_fusion.9), channel_id=1, source_target_pairs={{0,1},{1,0},{2,3},{3,2},{4,5},{5,4},{6,7},{7,6},{8,9},{9,8},{10,11... | collective-permute-start | bytes 1572872 | tf_op jit(solution)/shard_map/ppermute | solution.py:98
  32.7 52.0 %collective-permute-start = (bf16[2,128,1024]{2,1,0:T(8,128)(2,1)S(1)}, bf16[2,128,1024]{2,1,0:T(8,128)(2,1)S(1)}, u32[]{:S(2)}, u32[]{:S(2)}) collective-permute-start(bf16[2,128,1024]{2,1,0:T(8,128)(2,1)S(1)} %pad_maximum_fusion.9), channel_id=1, source_target_pairs={{0,8},{4,12},{8,0},{12,4},{1,9},{5,13},{9,1},{13,5},{2,10},{6,14},... | collective-permute-start | bytes 1572872 | tf_op jit(solution)/shard_map/ppermute | solution.py:98
  41.1 33.8 %collective-permute-start.4 = (bf16[256,512]{1,0:T(8,128)(2,1)S(1)}, bf16[256,512]{1,0:T(8,128)(2,1)}, u32[]{:S(2)}, u32[]{:S(2)}) collective-permute-start(bf16[256,512]{1,0:T(8,128)(2,1)S(1)} %copy-done.17), channel_id=1, source_target_pairs={{0,3},{1,2},{2,1},{3,0},{4,7},{5,6},{6,5},{7,4},{8,11},{9,10},{10,... | collective-permute-start | bytes 786440 | tf_op jit(solution)/shard_map/ppermute | solution.py:98
  73.5 9.2 %collective-permute-start.5 = (bf16[256,512]{1,0:T(8,128)(2,1)S(1)}, bf16[256,512]{1,0:T(8,128)(2,1)S(1)}, u32[]{:S(2)}, u32[]{:S(2)}) collective-permute-start(bf16[256,512]{1,0:T(8,128)(2,1)S(1)} %collective-permute-done.2.rest_0_), channel_id=1, source_target_pairs={{0,16},{16,0},{1,17},{17,1},{2,18},{18,2},{3,19},{19,3},{4,20},{20... | collective-permute-start | bytes 786440 | tf_op jit(solution)/shard_map/ppermute | solution.py:98
  74.9 81.9 %collective-permute-start.21 = (bf16[2,128,1024]{2,1,0:T(8,128)(2,1)S(1)}, bf16[2,128,1024]{2,1,0:T(8,128)(2,1)S(1)}, u32[]{:S(2)}, u32[]{:S(2)}) collective-permute-start(bf16[2,128,1024]{2,1,0:T(8,128)(2,1)S(1)} %collective-permute-done.16), channel_id=1, source_target_pairs={{0,1},{1,0},{2,3},{3,2},{4,5},{5,4},{6,7},{7,6},{8,9},{9,8},{10,11... | collective-permute-start | bytes 1572872 | tf_op jit(solution)/shard_map/ppermute | solution.py:98
  75.0 83.0 %collective-permute-start.17 = (bf16[2,128,1024]{2,1,0:T(8,128)(2,1)S(1)}, bf16[2,128,1024]{2,1,0:T(8,128)(2,1)S(1)}, u32[]{:S(2)}, u32[]{:S(2)}) collective-permute-start(bf16[2,128,1024]{2,1,0:T(8,128)(2,1)S(1)} %collective-permute-done.16), channel_id=1, source_target_pairs={{0,8},{4,12},{8,0},{12,4},{1,9},{5,13},{9,1},{13,5},{2,10},{6,14},... | collective-permute-start | bytes 1572872 | tf_op jit(solution)/shard_map/ppermute | solution.py:98
  82.7 6.4 %collective-permute-start.6 = (bf16[256,512]{1,0:T(8,128)(2,1)S(1)}, bf16[256,512]{1,0:T(8,128)(2,1)S(1)}, u32[]{:S(2)}, u32[]{:S(2)}) collective-permute-start(bf16[256,512]{1,0:T(8,128)(2,1)S(1)} %collective-permute-done.3.rest_1_), channel_id=1, source_target_pairs={{0,16},{16,0},{1,17},{17,1},{2,18},{18,2},{3,19},{19,3},{4,20},{20... | collective-permute-start | bytes 786440 | tf_op jit(solution)/shard_map/ppermute | solution.py:98
  84.1 7.8 %collective-permute-start.7 = (bf16[256,512]{1,0:T(8,128)(2,1)}, bf16[256,512]{1,0:T(8,128)(2,1)}, u32[]{:S(2)}, u32[]{:S(2)}) collective-permute-start(bf16[256,512]{1,0:T(8,128)(2,1)} %collective-permute-done.4.rest_2_), channel_id=1, source_target_pairs={{0,16},{16,0},{1,17},{17,1},{2,18},{18,2},{3,19},{19,3},{4,20},{20... | collective-permute-start | bytes 786440 | tf_op jit(solution)/shard_map/ppermute | solution.py:98
  84.7 73.4 %collective-permute-start.11 = (bf16[2,128,1024]{2,1,0:T(8,128)(2,1)S(1)}, bf16[2,128,1024]{2,1,0:T(8,128)(2,1)S(1)}, u32[]{:S(2)}, u32[]{:S(2)}) collective-permute-start(bf16[2,128,1024]{2,1,0:T(8,128)(2,1)S(1)} %collective-permute-done.10), channel_id=1, source_target_pairs={{0,8},{4,12},{8,0},{12,4},{1,9},{5,13},{9,1},{13,5},{2,10},{6,14},... | collective-permute-start | bytes 1572872 | tf_op jit(solution)/shard_map/ppermute | solution.py:98
  89.7 79.5 %collective-permute-start.1 = (bf16[2,256,1024]{2,1,0:T(8,128)(2,1)}, bf16[2,256,1024]{2,1,0:T(8,128)(2,1)}, u32[]{:S(2)}, u32[]{:S(2)}) collective-permute-start(bf16[2,256,1024]{2,1,0:T(8,128)(2,1)} %pad_maximum_fusion.5), channel_id=1, source_target_pairs={{0,4},{4,0},{8,12},{12,8},{1,5},{5,1},{9,13},{13,9},{2,6},{6,2},{1... | collective-permute-start | bytes 3145736 | tf_op jit(solution)/shard_map/ppermute | solution.py:98
  156.9 12.2 %collective-permute-start.22 = (bf16[2,128,1024]{2,1,0:T(8,128)(2,1)S(1)}, bf16[2,128,1024]{2,1,0:T(8,128)(2,1)S(1)}, u32[]{:S(2)}, u32[]{:S(2)}) collective-permute-start(bf16[2,128,1024]{2,1,0:T(8,128)(2,1)S(1)} %collective-permute-done.21), channel_id=1, source_target_pairs={{0,8},{4,12},{8,0},{12,4},{1,9},{5,13},{9,1},{13,5},{2,10},{6,14},... | collective-permute-start | bytes 1572872 | tf_op jit(solution)/shard_map/ppermute | solution.py:98
  158.0 17.3 %collective-permute-start.18 = (bf16[2,256,1024]{2,1,0:T(8,128)(2,1)S(1)}, bf16[2,256,1024]{2,1,0:T(8,128)(2,1)S(1)}, u32[]{:S(2)}, u32[]{:S(2)}) collective-permute-start(bf16[2,256,1024]{2,1,0:T(8,128)(2,1)S(1)} %pad_maximum_fusion.7), channel_id=1, source_target_pairs={{0,4},{4,0},{8,12},{12,8},{1,5},{5,1},{9,13},{13,9},{2,6},{6,2},{1... | collective-permute-start | bytes 3145736 | tf_op jit(solution)/shard_map/ppermute | solution.py:98
  158.2 21.1 %collective-permute-start.12 = (bf16[2,256,1024]{2,1,0:T(8,128)(2,1)S(1)}, bf16[2,256,1024]{2,1,0:T(8,128)(2,1)S(1)}, u32[]{:S(2)}, u32[]{:S(2)}) collective-permute-start(bf16[2,256,1024]{2,1,0:T(8,128)(2,1)S(1)} %pad_maximum_fusion.6), channel_id=1, source_target_pairs={{0,4},{4,0},{8,12},{12,8},{1,5},{5,1},{9,13},{13,9},{2,6},{6,2},{1... | collective-permute-start | bytes 3145736 | tf_op jit(solution)/shard_map/ppermute | solution.py:98
  169.1 15.5 %collective-permute-start.23 = (bf16[2,256,1024]{2,1,0:T(8,128)(2,1)S(1)}, bf16[2,256,1024]{2,1,0:T(8,128)(2,1)S(1)}, u32[]{:S(2)}, u32[]{:S(2)}) collective-permute-start(bf16[2,256,1024]{2,1,0:T(8,128)(2,1)S(1)} %pad_maximum_fusion.8), channel_id=1, source_target_pairs={{0,4},{4,0},{8,12},{12,8},{1,5},{5,1},{9,13},{13,9},{2,6},{6,2},{1... | collective-permute-start | bytes 3145736 | tf_op jit(solution)/shard_map/ppermute | solution.py:98
  174.8 14.2 %collective-permute-start.8 = (bf16[2,256,1024]{2,1,0:T(8,128)(2,1)S(1)}, bf16[2,256,1024]{2,1,0:T(8,128)(2,1)S(1)}, u32[]{:S(2)}, u32[]{:S(2)}) collective-permute-start(bf16[2,256,1024]{2,1,0:T(8,128)(2,1)S(1)} %pad_maximum_fusion.4), channel_id=1, source_target_pairs={{0,4},{4,0},{8,12},{12,8},{1,5},{5,1},{9,13},{13,9},{2,6},{6,2},{1... | collective-permute-start | bytes 3145736 | tf_op jit(solution)/shard_map/ppermute | solution.py:98
  179.1 19.9 %collective-permute-start.19 = (bf16[2,256,1024]{2,1,0:T(8,128)(2,1)S(1)}, bf16[2,256,1024]{2,1,0:T(8,128)(2,1)}, u32[]{:S(2)}, u32[]{:S(2)}) collective-permute-start(bf16[2,256,1024]{2,1,0:T(8,128)(2,1)S(1)} %pad_maximum_fusion.2), channel_id=1, source_target_pairs={{0,4},{4,0},{8,12},{12,8},{1,5},{5,1},{9,13},{13,9},{2,6},{6,2},{1... | collective-permute-start | bytes 3145736 | tf_op jit(solution)/shard_map/ppermute | solution.py:98
  184.2 19.0 %collective-permute-start.13 = (bf16[2,256,1024]{2,1,0:T(8,128)(2,1)}, bf16[2,256,1024]{2,1,0:T(8,128)(2,1)}, u32[]{:S(2)}, u32[]{:S(2)}) collective-permute-start(bf16[2,256,1024]{2,1,0:T(8,128)(2,1)} %pad_maximum_fusion.3), channel_id=1, source_target_pairs={{0,4},{4,0},{8,12},{12,8},{1,5},{5,1},{9,13},{13,9},{2,6},{6,2},{1... | collective-permute-start | bytes 3145736 | tf_op jit(solution)/shard_map/ppermute | solution.py:98
  188.8 49.6 %collective-permute-start.24 = (bf16[2,256,1024]{2,1,0:T(8,128)(2,1)S(1)}, bf16[2,256,1024]{2,1,0:T(8,128)(2,1)}, u32[]{:S(2)}, u32[]{:S(2)}) collective-permute-start(bf16[2,256,1024]{2,1,0:T(8,128)(2,1)S(1)} %pad_maximum_fusion.1), channel_id=1, source_target_pairs={{0,4},{4,0},{8,12},{12,8},{1,5},{5,1},{9,13},{13,9},{2,6},{6,2},{1... | collective-permute-start | bytes 3145736 | tf_op jit(solution)/shard_map/ppermute | solution.py:98
  190.0 92.2 %collective-permute-start.9 = (bf16[2,128,1024]{2,1,0:T(8,128)(2,1)}, bf16[2,128,1024]{2,1,0:T(8,128)(2,1)}, u32[]{:S(2)}, u32[]{:S(2)}) collective-permute-start(bf16[2,128,1024]{2,1,0:T(8,128)(2,1)} %slice.177), channel_id=1, source_target_pairs={{0,8},{4,12},{8,0},{12,4},{1,9},{5,13},{9,1},{13,5},{2,10},{6,14},... | collective-permute-start | bytes 1572872 | tf_op jit(solution)/shard_map/ppermute | solution.py:98
  198.1 24.0 %collective-permute-start.28 = (bf16[512,512]{1,0:T(8,128)(2,1)S(1)}, bf16[512,512]{1,0:T(8,128)(2,1)S(1)}, u32[]{:S(2)}, u32[]{:S(2)}) collective-permute-start(bf16[512,512]{1,0:T(8,128)(2,1)S(1)} %get-tuple-element.22), channel_id=1, source_target_pairs={{0,1},{1,0},{2,3},{3,2},{4,5},{5,4},{6,7},{7,6},{8,9},{9,8},{10,11... | collective-permute-start | bytes 1572872 | tf_op jit(solution)/shard_map/ppermute | solution.py:98
  199.0 38.2 %collective-permute-start.29 = (bf16[512,512]{1,0:T(8,128)(2,1)S(1)}, bf16[512,512]{1,0:T(8,128)(2,1)S(1)}, u32[]{:S(2)}, u32[]{:S(2)}) collective-permute-start(bf16[512,512]{1,0:T(8,128)(2,1)S(1)} %get-tuple-element.21), channel_id=1, source_target_pairs={{0,2},{1,3},{2,0},{3,1},{4,6},{5,7},{6,4},{7,5},{8,10},{9,11},{10,... | collective-permute-start | bytes 1572872 | tf_op jit(solution)/shard_map/ppermute | solution.py:98
  203.2 37.8 %collective-permute-start.30 = (bf16[512,512]{1,0:T(8,128)(2,1)S(1)}, bf16[512,512]{1,0:T(8,128)(2,1)S(1)}, u32[]{:S(2)}, u32[]{:S(2)}) collective-permute-start(bf16[512,512]{1,0:T(8,128)(2,1)S(1)} %get-tuple-element.20), channel_id=1, source_target_pairs={{0,3},{1,2},{2,1},{3,0},{4,7},{5,6},{6,5},{7,4},{8,11},{9,10},{10,... | collective-permute-start | bytes 1572872 | tf_op jit(solution)/shard_map/ppermute | solution.py:98
  222.1 41.2 %collective-permute-start.20 = (bf16[2,128,1024]{2,1,0:T(8,128)(2,1)S(1)}, bf16[2,128,1024]{2,1,0:T(8,128)(2,1)S(1)}, u32[]{:S(2)}, u32[]{:S(2)}) collective-permute-start(bf16[2,128,1024]{2,1,0:T(8,128)(2,1)S(1)} %slice.189), channel_id=1, source_target_pairs={{0,8},{4,12},{8,0},{12,4},{1,9},{5,13},{9,1},{13,5},{2,10},{6,14},... | collective-permute-start | bytes 1572872 | tf_op jit(solution)/shard_map/ppermute | solution.py:98
  237.3 23.8 %collective-permute-start.14 = (bf16[2,128,1024]{2,1,0:T(8,128)(2,1)S(1)}, bf16[2,128,1024]{2,1,0:T(8,128)(2,1)S(1)}, u32[]{:S(2)}, u32[]{:S(2)}) collective-permute-start(bf16[2,128,1024]{2,1,0:T(8,128)(2,1)S(1)} %slice.183), channel_id=1, source_target_pairs={{0,8},{4,12},{8,0},{12,4},{1,9},{5,13},{9,1},{13,5},{2,10},{6,14},... | collective-permute-start | bytes 1572872 | tf_op jit(solution)/shard_map/ppermute | solution.py:98
  239.9 21.0 %collective-permute-start.25 = (bf16[2,128,1024]{2,1,0:T(8,128)(2,1)S(1)}, bf16[2,128,1024]{2,1,0:T(8,128)(2,1)S(1)}, u32[]{:S(2)}, u32[]{:S(2)}) collective-permute-start(bf16[2,128,1024]{2,1,0:T(8,128)(2,1)S(1)} %slice.195), channel_id=1, source_target_pairs={{0,8},{4,12},{8,0},{12,4},{1,9},{5,13},{9,1},{13,5},{2,10},{6,14},... | collective-permute-start | bytes 1572872 | tf_op jit(solution)/shard_map/ppermute | solution.py:98
  260.9 20.5 %collective-permute-start.26 = (bf16[2,128,1024]{2,1,0:T(8,128)(2,1)S(1)}, bf16[2,128,1024]{2,1,0:T(8,128)(2,1)S(1)}, u32[]{:S(2)}, u32[]{:S(2)}) collective-permute-start(bf16[2,128,1024]{2,1,0:T(8,128)(2,1)S(1)} %slice_add_fusion), channel_id=1, source_target_pairs={{0,1},{1,0},{2,3},{3,2},{4,5},{5,4},{6,7},{7,6},{8,9},{9,8},{10,11... | collective-permute-start | bytes 1572872 | tf_op jit(solution)/shard_map/ppermute | solution.py:98
  261.1 28.7 %collective-permute-start.15 = (bf16[2,128,1024]{2,1,0:T(8,128)(2,1)S(1)}, bf16[2,128,1024]{2,1,0:T(8,128)(2,1)S(1)}, u32[]{:S(2)}, u32[]{:S(2)}) collective-permute-start(bf16[2,128,1024]{2,1,0:T(8,128)(2,1)S(1)} %slice_add_fusion.2), channel_id=1, source_target_pairs={{0,1},{1,0},{2,3},{3,2},{4,5},{5,4},{6,7},{7,6},{8,9},{9,8},{10,11... | collective-permute-start | bytes 1572872 | tf_op jit(solution)/shard_map/ppermute | solution.py:98
  281.7 19.0 %collective-permute-start.27 = (bf16[2,128,1024]{2,1,0:T(8,128)(2,1)S(1)}, bf16[2,128,1024]{2,1,0:T(8,128)(2,1)S(1)}, u32[]{:S(2)}, u32[]{:S(2)}) collective-permute-start(bf16[2,128,1024]{2,1,0:T(8,128)(2,1)S(1)} %add_convert_fusion), channel_id=1, source_target_pairs={{0,2},{1,3},{2,0},{3,1},{4,6},{5,7},{6,4},{7,5},{8,10},{9,11},{10,... | collective-permute-start | bytes 1572872 | tf_op jit(solution)/shard_map/ppermute | solution.py:98
  302.5 4.6 %collective-permute-start.31 = (f32[2,1024]{1,0:T(2,128)S(1)}, f32[2,1024]{1,0:T(2,128)S(1)}, u32[]{:S(2)}, u32[]{:S(2)}) collective-permute-start(f32[2,1024]{1,0:T(2,128)S(1)} %pad_maximum_fusion.10), channel_id=1, source_target_pairs={{0,2},{1,3},{2,0},{3,1},{4,6},{5,7},{6,4},{7,5},{8,10},{9,11},{10,... | collective-permute-start | bytes 24584 | tf_op jit(solution)/shard_map/ppermute | solution.py:98
  (22 other events, 274.3 us)

commit v3 on v2

--- a/solution.py
+++ b/solution.py
@@ -1,3 +1,5 @@
+import math
+
 import jax
 import jax.numpy as jnp
 from jax import lax
@@ -108,38 +110,23 @@
     up_rows, down_rows, strips = depth // mates, units // mates, units // depth
     strip_rows = down_rows // strips
 
-    def kernel(up_ref, down_ref, *rest):
-        sends, sem = rest[:-1], rest[-1]
+    def kernel(up_ref, down_ref, *sends):
         place, mate = lax.axis_index("dp"), lax.rem(lax.axis_index("groups"), mates)
-        copies = []
-
-        def copy(src, dst):
-            one = pltpu.make_async_copy(src, dst, sem.at[len(copies)])
-            one.start()
-            copies.append(one)
-
         for k in range(1, n_dp):
             first = pl.multiple_of((place ^ k) * units, units)
             send = sends[k - 1]
-            copy(
-                up_ref.at[pl.ds(pl.multiple_of(mate * up_rows, up_rows), up_rows), pl.ds(first, units)],
-                send.at[pl.ds(0, up_rows), :],
-            )
+            row = pl.multiple_of(mate * up_rows, up_rows)
+            send[:up_rows, :] = up_ref[pl.ds(row, up_rows), pl.ds(first, units)]
             for c in range(strips):
                 row = pl.multiple_of(first + mate * down_rows + c * strip_rows, strip_rows)
-                copy(
-                    down_ref.at[pl.ds(row, strip_rows), :],
-                    send.at[pl.ds(up_rows, strip_rows), pl.ds(c * depth, depth)],
-                )
-        for one in copies:
-            one.wait()
+                send[up_rows:, c * depth : (c + 1) * depth] = down_ref[pl.ds(row, strip_rows), :]
 
     return pl.pallas_call(
         kernel,
         out_shape=[jax.ShapeDtypeStruct((2 * up_rows, units), w_up.dtype)] * (n_dp - 1),
-        in_specs=[pl.BlockSpec(memory_space=pl.ANY)] * 2,
-        out_specs=[pl.BlockSpec(memory_space=pl.ANY)] * (n_dp - 1),
-        scratch_shapes=[pltpu.SemaphoreType.DMA(((n_dp - 1) * (1 + strips),))],
+        in_specs=[pl.BlockSpec(memory_space=pltpu.VMEM)] * 2,
+        out_specs=[pl.BlockSpec(memory_space=pltpu.VMEM)] * (n_dp - 1),
+        cost_estimate=pl.CostEstimate(flops=0, bytes_accessed=8 * w_up.size, transcendentals=0),
         name="pack_weights",
     )(w_up, w_down)
 
@@ -191,8 +178,9 @@
             jax.ShapeDtypeStruct((units, depth * n_dp), w_down.dtype),
         ],
         in_specs=[pl.BlockSpec(memory_space=pl.ANY)] * (2 + mates * (n_dp - 1)),
-        out_specs=[pl.BlockSpec(memory_space=pl.ANY)] * 2,
+        out_specs=[pl.BlockSpec(memory_space=pltpu.VMEM)] * 2,
         scratch_shapes=[pltpu.SemaphoreType.DMA((2 + mates * (n_dp - 1) * (1 + strips),))],
+        cost_estimate=pl.CostEstimate(flops=0, bytes_accessed=16 * w_up.size, transcendentals=0),
         name="unpack_weights",
     )(w_up, w_down, *[piece for pieces in got for piece in pieces])
 
@@ -234,6 +222,59 @@
     )(place.reshape(1), *chunks, *hiddens, *grad_pres)
 
 
+def middle(tokens, up, down):
+    (_, rows, width), units = tokens.shape, up.shape[1]
+    tile = rows // 2
+    slope = (2.0 / math.pi) ** 0.5
+
+    def kernel(tok_ref, up_ref, down_ref, hid_ref, pre_ref, part_ref):
+        x = jnp.dot(tok_ref[0], up_ref[...], preferred_element_type=jnp.float32)
+        gate = jnp.tanh(slope * (x + 0.044715 * (x * x * x)))
+        half = 0.5 + 0.5 * gate
+        hidden = (x * half).astype(jnp.bfloat16)
+        rise = half + (0.5 * slope) * x * (1.0 - gate * gate) * (1.0 + (3 * 0.044715) * (x * x))
+        grad_pre = (contract_last(tok_ref[1], down_ref[...]) * rise).astype(jnp.bfloat16)
+        hid_ref[...] = hidden
+        pre_ref[...] = grad_pre
+        branch = jnp.dot(hidden, down_ref[...], preferred_element_type=jnp.float32)
+        part_ref[0] = branch.astype(jnp.bfloat16)
+        part_ref[1] = contract_last(grad_pre, up_ref[...]).astype(jnp.bfloat16)
+
+    def both(i):
+        return (0, i, 0)
+
+    return pl.pallas_call(
+        kernel,
+        out_shape=[
+            jax.ShapeDtypeStruct((rows, units), jnp.bfloat16),
+            jax.ShapeDtypeStruct((rows, units), jnp.bfloat16),
+            jax.ShapeDtypeStruct((2, rows, width), jnp.bfloat16),
+        ],
+        grid=(rows // tile,),
+        in_specs=[
+            pl.BlockSpec((2, tile, width), both),
+            pl.BlockSpec((width, units), lambda i: (0, 0)),
+            pl.BlockSpec((units, width), lambda i: (0, 0)),
+        ],
+        out_specs=[
+            pl.BlockSpec((tile, units), lambda i: (i, 0)),
+            pl.BlockSpec((tile, units), lambda i: (i, 0)),
+            pl.BlockSpec((2, tile, width), both),
+        ],
+        compiler_params=pltpu.CompilerParams(vmem_limit_bytes=32 * 1024 * 1024),
+        cost_estimate=pl.CostEstimate(
+            flops=8 * rows * width * units,
+            bytes_accessed=8 * rows * width + 4 * rows * units + 4 * width * units,
+            transcendentals=rows * units,
+        ),
+        name="middle",
+    )(tokens, up, down)
+
+
+def after(values, *others):
+    return lax.optimization_barrier((values, *others))[0]
+
+
 def gather_tokens_body(
     first_out, second_out, grad_first, grad_second, w_up, w_down, norm_gain, norm_bias
 ):
@@ -247,8 +288,10 @@
     chunks = {0: jnp.stack([normed, grad_second])}
     for bit in bits_of(n_dp):
         chunks.update({k | bit: swap(chunk, "dp", bit) for k, chunk in chunks.items()})
+    top = bits_of(n_dp)[0]
 
     sends = pack_weights(w_up, w_down, mates)
+    sends = [after(send, chunks[top]) if k >= top else send for k, send in enumerate(sends, 1)]
     got = [[swap(sends[k - 1], "dp", k) for k in range(1, n_dp)]]
     if mates == 2:
         got.append([swap(piece, "groups", 1) for piece in got[0]])
@@ -260,31 +303,26 @@
         for bit in bits_of(n_tensor):
             chunk = jnp.concatenate([chunk, swap(chunk, "tensor", bit)], axis=1)
         chunks[k] = chunk
-    for k in sorted(chunks, key=lambda k: (k & 1 == 0, -k)):
-        rows, grads = chunks[k][0], chunks[k][1]
-        preact = jnp.dot(rows, up, preferred_element_type=jnp.float32)
-        hiddens[k] = jax.nn.gelu(preact).astype(jnp.bfloat16)
-        grad_hidden = contract_last(grads, down)
-        grad_pres[k] = jax.vjp(jax.nn.gelu, preact)[1](grad_hidden)[0].astype(jnp.bfloat16)
-        part = jnp.stack(
-            [
-                jnp.dot(hiddens[k], down, preferred_element_type=jnp.float32).astype(jnp.bfloat16),
-                contract_last(grad_pres[k], up).astype(jnp.bfloat16),
-            ]
-        )
+    order = sorted(chunks, reverse=True)
+    last = None
+    for k in order:
+        tokens = chunks[k] if last is None else after(chunks[k], last)
+        hiddens[k], grad_pres[k], part = middle(tokens, up, down)
+        last = hiddens[k]
         for bit in reversed(bits_of(n_tensor)):
             half = part.shape[1] // 2
             part = part[:, :half] + swap(part[:, half:], "tensor", bit)
         sums[k] = part
-    order = sorted(chunks)
     blocks = weight_grads(
         place, [chunks[k] for k in order], [hiddens[k] for k in order], [grad_pres[k] for k in order], n_dp
     )
+    came = {}
     for bit in reversed(bits_of(n_dp)):
-        for k in [k for k in sums if k & bit]:
-            got = swap(sums.pop(k), "dp", bit).astype(jnp.float32)
+        for k in [k for k in order if k & bit and k in sums]:
+            came[k] = swap(sums.pop(k), "dp", bit)
+            got = came[k].astype(jnp.float32)
             total = sums[k ^ bit].astype(jnp.float32) + got
-            sums[k ^ bit] = total if k == bit and bit == bits_of(n_dp)[0] else total.astype(jnp.bfloat16)
+            sums[k ^ bit] = total if k == top else total.astype(jnp.bfloat16)
     branch, grad_normed = sums[0][0], sums[0][1]
     second_in, grad_first_in, stats = finish_rows(
         branch, grad_normed, second_out, grad_first, standard, inv_std, norm_gain
@@ -295,7 +333,9 @@
     grad_down = jnp.zeros(w_down.shape, jnp.float32)
     for k in range(n_dp):
         other = place ^ k
-        block = swap(blocks[k], "dp", k) if k else blocks[k]
+        block = blocks[k]
+        if k:
+            block = swap(block if k == top else after(block, came[k & top or 1]), "dp", k)
         block = block.astype(jnp.float32) * grad_scale
         grad_up = lax.dynamic_update_slice_in_dim(grad_up, block[:depth], other * units, 1)
         strips = [block[depth:, c * depth : (c + 1) * depth] for c in range(units // depth)]

time: 317 us -> 231 us (0.73)
  Pallas kernels: 96.8 us -> 24.8 us
  waiting for transfers between devices: 154 us -> 129 us
  local copies, waits for them, and re-layouts: 3.7 us -> 21.7 us
  matrix products: 14.7 us -> 0 us
  other arithmetic: 13.5 us -> 18.2 us
  starting transfers between devices: 32 us -> 36.2 us
    pallas_call x1, Pallas kernels: 64.8 us -> 2.94 us  [unpack_weights(): pl.pallas_call(kernel, out_shape=[jax.ShapeDtypeStruct((depth * n_dp, uni...]
    ppermute x35, waiting for transfers between devices: 154 us -> 129 us  [swap(): lax.ppermute(values, axis, [(i, i ^ mask) for i in range(lax.axis_size(ax...]
    pallas_call x1, Pallas kernels: 25 us -> 2.47 us  [pack_weights(): pl.pallas_call(kernel, out_shape=[jax.ShapeDtypeStruct((2 * up_rows, unit...]
    dot_general x16 -> x0, matrix products: 14.7 us -> none  [the longest x8 8.03 us: contract_last(): lax.dot_general(left_rows, right_rows, (((1,), (1,)), ((), ())), preferre...]
    pallas_call x0 -> x4, Pallas kernels: none -> 12.4 us  [middle(): pl.pallas_call(kernel, out_shape=[jax.ShapeDtypeStruct((rows, units), jnp...]
    unnamed x44 -> x64, local copies, waits for them, and re-layouts: 1.71 us -> 10.7 us
    concatenate x5, other arithmetic: 2.74 us -> 8.25 us  [gather_tokens_body(): chunk = jnp.concatenate([chunk, swap(chunk, 'tensor', bit)], axis=1)]
    concatenate x3, local copies, waits for them, and re-layouts: 0.21 us -> 5.68 us  [gather_tokens_body(): chunk = jnp.concatenate([chunk, swap(chunk, 'tensor', bit)], axis=1)]
  transfers between devices with their start and end apart: 35 -> 35, of which waited for: 15 -> 14; matrix products, arithmetic and copies ran while one was open for 9% -> 12% of each run, Pallas kernels for 23% -> 9%
where the time goes in v3:
time: 231 us
  waiting for transfers between devices  129 us (56%)
  starting transfers between devices  36.2 us (16%)
  Pallas kernels  24.8 us (11%)
  local copies, waits for them, and re-layouts  21.7 us (9%)
  other arithmetic  18.2 us (8%)
    ppermute x35, waiting for transfers between devices, swap(): lax.ppermute(values, axis, [(i, i ^ mask) for i in range(lax.axis_size(ax...  129 us
    ppermute x35, starting transfers between devices, swap(): lax.ppermute(values, axis, [(i, i ^ mask) for i in range(lax.axis_size(ax...  36.2 us
    pallas_call x4, Pallas kernels, middle(): pl.pallas_call(kernel, out_shape=[jax.ShapeDtypeStruct((rows, units), jnp...  12.4 us
    unnamed x64, local copies, waits for them, and re-layouts  10.7 us
    concatenate x5, other arithmetic, gather_tokens_body(): chunk = jnp.concatenate([chunk, swap(chunk, 'tensor', bit)], axis=1)  8.25 us
    pallas_call x1, Pallas kernels, weight_grads(): pl.pallas_call(kernel, out_shape=jax.ShapeDtypeStruct((n_dp, 2 * depth, u...  6.91 us
    concatenate x3, local copies, waits for them, and re-layouts, gather_tokens_body(): chunk = jnp.concatenate([chunk, swap(chunk, 'tensor', bit)], axis=1)  5.68 us
  transfers between devices with their start and end apart: 35, of which 14 were waited for; matrix products, arithmetic and copies ran while one was open for 12% of the time, Pallas kernels for 9%

profile of v3, /device:TPU:0, one launch (start us, length us, event | category | flops | bytes accessed | tf_op | source)
XLA Modules:
  0.0 230.7 jit_solution(3248032407746746112)
XLA Ops:
  5.2 4.1 %collective-permute-start.5 = (bf16[2,128,1024]{2,1,0:T(8,128)(2,1)S(1)}, bf16[2,128,1024]{2,1,0:T(8,128)(2,1)}, u32[]{:S(2)}, u32[]{:S(2)}) collective-permute-start(bf16[2,128,1024]{2,1,0:T(8,128)(2,1)S(1)} %pad_maximum_fusion.5), channel_id=1, source_target_pairs={{0,2},{1,3},{2,0},{3,1},{4,6},{5,7},{6,4},{7,5},{8,10},{9,11},{10,... | collective-permute-start | bytes 1572872 | tf_op jit(solution)/shard_map/ppermute | solution.py:100
  9.3 1.6 collective-permute-start.2
  12.4 20.3 %collective-permute-done.5 = bf16[2,128,1024]{2,1,0:T(8,128)(2,1)} collective-permute-done((bf16[2,128,1024]{2,1,0:T(8,128)(2,1)S(1)}, bf16[2,128,1024]{2,1,0:T(8,128)(2,1)}, u32[]{:S(2)}, u32[]{:S(2)}) %collective-permute-start.5) | collective-permute-done | bytes 524320 | tf_op jit(solution)/shard_map/ppermute | solution.py:100
  33.1 2.5 %pack_weights.1 = (bf16[256,512]{1,0:T(8,128)(2,1)}, bf16[256,512]{1,0:T(8,128)(2,1)}, bf16[256,512]{1,0:T(8,128)(2,1)}) custom-call(bf16[256,2048]{1,0:T(8,128)(2,1)} %up_ref.3, bf16[2048,256]{1,0:T(8,128)(2,1)} %down_ref.3), custom_call_target="tpu_custom_call" | custom-call | bytes 4194304 | tf_op jit(solution)/shard_map/pack_weights/pallas_call | solution.py:124
  37.1 1.6 collective-permute-start.6
  38.7 12.8 %collective-permute-done.11.rest_0_ = bf16[256,512]{1,0:T(8,128)(2,1)S(1)} collective-permute-done((bf16[256,512]{1,0:T(8,128)(2,1)}, bf16[256,512]{1,0:T(8,128)(2,1)S(1)}, u32[]{:S(2)}, u32[]{:S(2)}) %collective-permute-start.11) | collective-permute-done | bytes 262176 | tf_op jit(solution)/shard_map/ppermute | solution.py:100
  54.3 3.3 %collective-permute-start.12 = (bf16[256,512]{1,0:T(8,128)(2,1)}, bf16[256,512]{1,0:T(8,128)(2,1)S(1)}, u32[]{:S(2)}, u32[]{:S(2)}) collective-permute-start(bf16[256,512]{1,0:T(8,128)(2,1)} %get-tuple-element.31), channel_id=1, source_target_pairs={{0,2},{1,3},{2,0},{3,1},{4,6},{5,7},{6,4},{7,5},{8,10},{9,11},{10,... | collective-permute-start | bytes 786440 | tf_op jit(solution)/shard_map/ppermute | solution.py:100
  61.0 4.0 %collective-permute-start.13 = (bf16[256,512]{1,0:T(8,128)(2,1)S(1)}, bf16[256,512]{1,0:T(8,128)(2,1)S(1)}, u32[]{:S(2)}, u32[]{:S(2)}) collective-permute-start(bf16[256,512]{1,0:T(8,128)(2,1)S(1)} %copy-done.28), channel_id=1, source_target_pairs={{0,3},{1,2},{2,1},{3,0},{4,7},{5,6},{6,5},{7,4},{8,11},{9,10},{10,... | collective-permute-start | bytes 786440 | tf_op jit(solution)/shard_map/ppermute | solution.py:100
  65.0 2.2 pad_maximum_fusion.3
  67.3 8.2 %collective-permute-done.12.rest_1_ = bf16[256,512]{1,0:T(8,128)(2,1)S(1)} collective-permute-done((bf16[256,512]{1,0:T(8,128)(2,1)}, bf16[256,512]{1,0:T(8,128)(2,1)S(1)}, u32[]{:S(2)}, u32[]{:S(2)}) %collective-permute-start.12) | collective-permute-done | bytes 262176 | tf_op jit(solution)/shard_map/ppermute | solution.py:100
  76.0 2.3 pad_maximum_fusion.2
  82.2 2.0 constant_dynamic-update-slice_fusion.2
  84.2 3.4 %collective-permute-done.16.rest_5_ = bf16[256,512]{1,0:T(8,128)(2,1)} collective-permute-done((bf16[256,512]{1,0:T(8,128)(2,1)S(1)}, bf16[256,512]{1,0:T(8,128)(2,1)}, u32[]{:S(2)}, u32[]{:S(2)}) %collective-permute-start.16) | collective-permute-done | bytes 262176 | tf_op jit(solution)/shard_map/ppermute | solution.py:100
  87.6 2.9 %unpack_weights.1 = (bf16[1024,512]{1,0:T(8,128)(2,1)}, bf16[512,1024]{1,0:T(8,128)(2,1)}) custom-call(bf16[256,2048]{1,0:T(8,128)(2,1)} %up_ref.3, bf16[2048,256]{1,0:T(8,128)(2,1)} %down_ref.3, bf16[256,512]{1,0:T(8,128)(2,1)} %copy-done.20, bf16[256,512]{1,0:T(8,128)(2,1)} %copy-done.22, bf16[256,512]{1,0:T(8,128)(2,1)} %copy-done.23, ...), custom_call_target="tpu_custom_call" | custom-call | bytes 8388608 | tf_op jit(solution)/shard_map/unpack_weights/pallas_call | solution.py:174
  91.7 2.3 constant_dynamic-update-slice_fusion.1
  97.7 2.1 constant_dynamic-update-slice_fusion.tok_ref.refs_2_
  99.8 2.1 constant_dynamic-update-slice_fusion.6.tok_ref.refs_0_
  101.9 3.3 %middle.4 = (bf16[512,512]{1,0:T(8,128)(2,1)S(1)}, bf16[512,512]{1,0:T(8,128)(2,1)S(1)}, bf16[2,512,1024]{2,1,0:T(8,128)(2,1)S(1)}) custom-call(bf16[2,512,1024]{2,1,0:T(8,128)(2,1)S(1)} %constant_dynamic-update-slice_fusion.6.tok_ref.refs_0_, bf16[1024,512]{1,0:T(8,128)(2,1)S(1)} %copy-done.10, bf16[512,1024]{1,0:T(8,128)(2,1)S(1)} %copy-done.11), custom_call_target="tpu_custom_call" | custom-call | flops 2147483648 | bytes 7340032 | tf_op jit(solution)/shard_map/middle/pallas_call | solution.py:246
  106.3 3.1 %middle.5 = (bf16[512,512]{1,0:T(8,128)(2,1)S(1)}, bf16[512,512]{1,0:T(8,128)(2,1)S(1)}, bf16[2,512,1024]{2,1,0:T(8,128)(2,1)S(1)}) custom-call(bf16[2,512,1024]{2,1,0:T(8,128)(2,1)S(1)} %constant_dynamic-update-slice_fusion.3.tok_ref.refs_1_, bf16[1024,512]{1,0:T(8,128)(2,1)S(1)} %copy-done.10, bf16[512,1024]{1,0:T(8,128)(2,1)S(1)} %copy-done.11), custom_call_target="tpu_custom_call" | custom-call | flops 2147483648 | bytes 7340032 | tf_op jit(solution)/shard_map/middle/pallas_call | solution.py:246
  110.9 3.1 %middle.6 = (bf16[512,512]{1,0:T(8,128)(2,1)S(1)}, bf16[512,512]{1,0:T(8,128)(2,1)S(1)}, bf16[2,512,1024]{2,1,0:T(8,128)(2,1)S(1)}) custom-call(bf16[2,512,1024]{2,1,0:T(8,128)(2,1)S(1)} %constant_dynamic-update-slice_fusion.tok_ref.refs_2_, bf16[1024,512]{1,0:T(8,128)(2,1)S(1)} %copy-done.10, bf16[512,1024]{1,0:T(8,128)(2,1)S(1)} %copy-done.11), custom_call_target="tpu_custom_call" | custom-call | flops 2147483648 | bytes 7340032 | tf_op jit(solution)/shard_map/middle/pallas_call | solution.py:246
  115.1 3.1 %middle.7 = (bf16[512,512]{1,0:T(8,128)(2,1)S(1)}, bf16[512,512]{1,0:T(8,128)(2,1)S(1)}, bf16[2,512,1024]{2,1,0:T(8,128)(2,1)S(1)}) custom-call(bf16[2,512,1024]{2,1,0:T(8,128)(2,1)S(1)} %pad_maximum_fusion.tok_ref.refs_3_, bf16[1024,512]{1,0:T(8,128)(2,1)S(1)} %copy-done.10, bf16[512,1024]{1,0:T(8,128)(2,1)S(1)} %copy-done.11), custom_call_target="tpu_custom_call" | custom-call | flops 2147483648 | bytes 7340032 | tf_op jit(solution)/shard_map/middle/pallas_call | solution.py:246
  120.2 6.9 %weight_grads.1 = bf16[4,512,512]{2,1,0:T(8,128)(2,1)S(1)} custom-call(s32[1]{0:T(128)} %bitcast.4.place_ref, bf16[2,512,1024]{2,1,0:T(8,128)(2,1)S(1)} %copy-done.9, bf16[2,512,1024]{2,1,0:T(8,128)(2,1)S(1)} %copy-done.4, bf16[2,512,1024]{2,1,0:T(8,128)(2,1)S(1)} %copy-done.7, bf16[2,512,1024]{2,1,0:T(8,128)(2,1)} %copy-done, ...), custom_call_target="tpu_custom_call" | custom-call | flops 4294967296 | bytes 14680064 | tf_op jit(solution)/shard_map/weight_grads/pallas_call | solution.py:205
  127.2 3.5 %collective-permute-start.29 = (bf16[512,512]{1,0:T(8,128)(2,1)S(1)}, bf16[512,512]{1,0:T(8,128)(2,1)S(1)}, u32[]{:S(2)}, u32[]{:S(2)}) collective-permute-start(bf16[512,512]{1,0:T(8,128)(2,1)S(1)} %get-tuple-element.59), channel_id=1, source_target_pairs={{0,2},{1,3},{2,0},{3,1},{4,6},{5,7},{6,4},{7,5},{8,10},{9,11},{10,... | collective-permute-start | bytes 1572872 | tf_op jit(solution)/shard_map/ppermute | solution.py:100
  133.4 1.6 collective-permute-start.23
  135.8 11.7 %collective-permute-done.25 = bf16[2,128,1024]{2,1,0:T(8,128)(2,1)S(1)} collective-permute-done((bf16[2,128,1024]{2,1,0:T(8,128)(2,1)S(1)}, bf16[2,128,1024]{2,1,0:T(8,128)(2,1)S(1)}, u32[]{:S(2)}, u32[]{:S(2)}) %collective-permute-start.25) | collective-permute-done | bytes 524320 | tf_op jit(solution)/shard_map/ppermute | solution.py:100
  149.9 20.1 %collective-permute-done.20 = bf16[2,128,1024]{2,1,0:T(8,128)(2,1)S(1)} collective-permute-done((bf16[2,128,1024]{2,1,0:T(8,128)(2,1)S(1)}, bf16[2,128,1024]{2,1,0:T(8,128)(2,1)S(1)}, u32[]{:S(2)}, u32[]{:S(2)}) %collective-permute-start.20) | collective-permute-done | bytes 524320 | tf_op jit(solution)/shard_map/ppermute | solution.py:100
  172.3 19.1 %collective-permute-done.21 = bf16[2,128,1024]{2,1,0:T(8,128)(2,1)S(1)} collective-permute-done((bf16[2,128,1024]{2,1,0:T(8,128)(2,1)S(1)}, bf16[2,128,1024]{2,1,0:T(8,128)(2,1)S(1)}, u32[]{:S(2)}, u32[]{:S(2)}) %collective-permute-start.21) | collective-permute-done | bytes 524320 | tf_op jit(solution)/shard_map/ppermute | solution.py:100
  191.5 6.2 %collective-permute-done.27 = bf16[2,128,1024]{2,1,0:T(8,128)(2,1)S(1)} collective-permute-done((bf16[2,128,1024]{2,1,0:T(8,128)(2,1)S(1)}, bf16[2,128,1024]{2,1,0:T(8,128)(2,1)S(1)}, u32[]{:S(2)}, u32[]{:S(2)}) %collective-permute-start.27) | collective-permute-done | bytes 524320 | tf_op jit(solution)/shard_map/ppermute | solution.py:100
  199.3 8.0 %collective-permute-done.28 = bf16[512,512]{1,0:T(8,128)(2,1)S(1)} collective-permute-done((bf16[512,512]{1,0:T(8,128)(2,1)S(1)}, bf16[512,512]{1,0:T(8,128)(2,1)S(1)}, u32[]{:S(2)}, u32[]{:S(2)}) %collective-permute-start.28) | collective-permute-done | bytes 524320 | tf_op jit(solution)/shard_map/ppermute | solution.py:100
  208.8 10.3 %collective-permute-done.31 = f32[2,1024]{1,0:T(2,128)S(1)} collective-permute-done((f32[2,1024]{1,0:T(2,128)S(1)}, f32[2,1024]{1,0:T(2,128)S(1)}, u32[]{:S(2)}, u32[]{:S(2)}) %collective-permute-start.31) | collective-permute-done | bytes 8224 | tf_op jit(solution)/shard_map/ppermute | solution.py:100
  219.3 3.6 %collective-permute-done.32 = f32[2,1024]{1,0:T(2,128)S(1)} collective-permute-done((f32[2,1024]{1,0:T(2,128)S(1)}, f32[2,1024]{1,0:T(2,128)S(1)}, u32[]{:S(2)}, u32[]{:S(2)}) %collective-permute-start.32) | collective-permute-done | bytes 8224 | tf_op jit(solution)/shard_map/ppermute | solution.py:100
  223.5 3.1 %collective-permute-done.33 = f32[2,1024]{1,0:T(2,128)S(1)} collective-permute-done((f32[2,1024]{1,0:T(2,128)S(1)}, f32[2,1024]{1,0:T(2,128)S(1)}, u32[]{:S(2)}, u32[]{:S(2)}) %collective-permute-start.33) | collective-permute-done | bytes 8224 | tf_op jit(solution)/shard_map/ppermute | solution.py:100
  (167 shorter events, 45.3 us)
Async XLA Ops:
  5.2 27.5 %collective-permute-start.5 = (bf16[2,128,1024]{2,1,0:T(8,128)(2,1)S(1)}, bf16[2,128,1024]{2,1,0:T(8,128)(2,1)}, u32[]{:S(2)}, u32[]{:S(2)}) collective-permute-start(bf16[2,128,1024]{2,1,0:T(8,128)(2,1)S(1)} %pad_maximum_fusion.5), channel_id=1, source_target_pairs={{0,2},{1,3},{2,0},{3,1},{4,6},{5,7},{6,4},{7,5},{8,10},{9,11},{10,... | collective-permute-start | bytes 1572872 | tf_op jit(solution)/shard_map/ppermute | solution.py:100
  9.3 43.5 %collective-permute-start.2 = (bf16[2,128,1024]{2,1,0:T(8,128)(2,1)S(1)}, bf16[2,128,1024]{2,1,0:T(8,128)(2,1)}, u32[]{:S(2)}, u32[]{:S(2)}) collective-permute-start(bf16[2,128,1024]{2,1,0:T(8,128)(2,1)S(1)} %pad_maximum_fusion.5), channel_id=1, source_target_pairs={{0,1},{1,0},{2,3},{3,2},{4,5},{5,4},{6,7},{7,6},{8,9},{9,8},{10,11... | collective-permute-start | bytes 1572872 | tf_op jit(solution)/shard_map/ppermute | solution.py:100
  10.8 43.4 %collective-permute-start = (bf16[2,128,1024]{2,1,0:T(8,128)(2,1)S(1)}, bf16[2,128,1024]{2,1,0:T(8,128)(2,1)S(1)}, u32[]{:S(2)}, u32[]{:S(2)}) collective-permute-start(bf16[2,128,1024]{2,1,0:T(8,128)(2,1)S(1)} %pad_maximum_fusion.5), channel_id=1, source_target_pairs={{0,8},{4,12},{8,0},{12,4},{1,9},{5,13},{9,1},{13,5},{2,10},{6,14},... | collective-permute-start | bytes 1572872 | tf_op jit(solution)/shard_map/ppermute | solution.py:100
  32.6 25.0 %collective-permute-start.8 = (bf16[2,128,1024]{2,1,0:T(8,128)(2,1)}, bf16[2,128,1024]{2,1,0:T(8,128)(2,1)S(1)}, u32[]{:S(2)}, u32[]{:S(2)}) collective-permute-start(bf16[2,128,1024]{2,1,0:T(8,128)(2,1)} %collective-permute-done.5), channel_id=1, source_target_pairs={{0,1},{1,0},{2,3},{3,2},{4,5},{5,4},{6,7},{7,6},{8,9},{9,8},{10,11... | collective-permute-start | bytes 1572872 | tf_op jit(solution)/shard_map/ppermute | solution.py:100
  35.6 15.9 %collective-permute-start.11 = (bf16[256,512]{1,0:T(8,128)(2,1)}, bf16[256,512]{1,0:T(8,128)(2,1)S(1)}, u32[]{:S(2)}, u32[]{:S(2)}) collective-permute-start(bf16[256,512]{1,0:T(8,128)(2,1)} %get-tuple-element.29), channel_id=1, source_target_pairs={{0,1},{1,0},{2,3},{3,2},{4,5},{5,4},{6,7},{7,6},{8,9},{9,8},{10,11... | collective-permute-start | bytes 786440 | tf_op jit(solution)/shard_map/ppermute | solution.py:100
  37.1 23.9 %collective-permute-start.6 = (bf16[2,128,1024]{2,1,0:T(8,128)(2,1)}, bf16[2,128,1024]{2,1,0:T(8,128)(2,1)}, u32[]{:S(2)}, u32[]{:S(2)}) collective-permute-start(bf16[2,128,1024]{2,1,0:T(8,128)(2,1)} %collective-permute-done.5), channel_id=1, source_target_pairs={{0,8},{4,12},{8,0},{12,4},{1,9},{5,13},{9,1},{13,5},{2,10},{6,14},... | collective-permute-start | bytes 1572872 | tf_op jit(solution)/shard_map/ppermute | solution.py:100
  51.5 7.7 %collective-permute-start.14 = (bf16[256,512]{1,0:T(8,128)(2,1)S(1)}, bf16[256,512]{1,0:T(8,128)(2,1)S(1)}, u32[]{:S(2)}, u32[]{:S(2)}) collective-permute-start(bf16[256,512]{1,0:T(8,128)(2,1)S(1)} %collective-permute-done.11.rest_0_), channel_id=1, source_target_pairs={{0,16},{16,0},{1,17},{17,1},{2,18},{18,2},{3,19},{19,3},{4,20},{20... | collective-permute-start | bytes 786440 | tf_op jit(solution)/shard_map/ppermute | solution.py:100
  52.8 23.2 %collective-permute-start.3 = (bf16[2,128,1024]{2,1,0:T(8,128)(2,1)}, bf16[2,128,1024]{2,1,0:T(8,128)(2,1)}, u32[]{:S(2)}, u32[]{:S(2)}) collective-permute-start(bf16[2,128,1024]{2,1,0:T(8,128)(2,1)} %collective-permute-done.2), channel_id=1, source_target_pairs={{0,8},{4,12},{8,0},{12,4},{1,9},{5,13},{9,1},{13,5},{2,10},{6,14},... | collective-permute-start | bytes 1572872 | tf_op jit(solution)/shard_map/ppermute | solution.py:100
  54.3 21.2 %collective-permute-start.12 = (bf16[256,512]{1,0:T(8,128)(2,1)}, bf16[256,512]{1,0:T(8,128)(2,1)S(1)}, u32[]{:S(2)}, u32[]{:S(2)}) collective-permute-start(bf16[256,512]{1,0:T(8,128)(2,1)} %get-tuple-element.31), channel_id=1, source_target_pairs={{0,2},{1,3},{2,0},{3,1},{4,6},{5,7},{6,4},{7,5},{8,10},{9,11},{10,... | collective-permute-start | bytes 786440 | tf_op jit(solution)/shard_map/ppermute | solution.py:100
  57.6 22.2 %collective-permute-start.9 = (bf16[2,128,1024]{2,1,0:T(8,128)(2,1)S(1)}, bf16[2,128,1024]{2,1,0:T(8,128)(2,1)S(1)}, u32[]{:S(2)}, u32[]{:S(2)}) collective-permute-start(bf16[2,128,1024]{2,1,0:T(8,128)(2,1)S(1)} %collective-permute-done.8), channel_id=1, source_target_pairs={{0,8},{4,12},{8,0},{12,4},{1,9},{5,13},{9,1},{13,5},{2,10},{6,14},... | collective-permute-start | bytes 1572872 | tf_op jit(solution)/shard_map/ppermute | solution.py:100
  59.9 34.1 %collective-permute-start.1 = (bf16[2,256,1024]{2,1,0:T(8,128)(2,1)}, bf16[2,256,1024]{2,1,0:T(8,128)(2,1)}, u32[]{:S(2)}, u32[]{:S(2)}) collective-permute-start(bf16[2,256,1024]{2,1,0:T(8,128)(2,1)} %pad_maximum_fusion.1), channel_id=1, source_target_pairs={{0,4},{4,0},{8,12},{12,8},{1,5},{5,1},{9,13},{13,9},{2,6},{6,2},{1... | collective-permute-start | bytes 3145736 | tf_op jit(solution)/shard_map/ppermute | solution.py:100
  61.0 17.3 %collective-permute-start.13 = (bf16[256,512]{1,0:T(8,128)(2,1)S(1)}, bf16[256,512]{1,0:T(8,128)(2,1)S(1)}, u32[]{:S(2)}, u32[]{:S(2)}) collective-permute-start(bf16[256,512]{1,0:T(8,128)(2,1)S(1)} %copy-done.28), channel_id=1, source_target_pairs={{0,3},{1,2},{2,1},{3,0},{4,7},{5,6},{6,5},{7,4},{8,11},{9,10},{10,... | collective-permute-start | bytes 786440 | tf_op jit(solution)/shard_map/ppermute | solution.py:100
  75.5 6.8 %collective-permute-start.15 = (bf16[256,512]{1,0:T(8,128)(2,1)S(1)}, bf16[256,512]{1,0:T(8,128)(2,1)S(1)}, u32[]{:S(2)}, u32[]{:S(2)}) collective-permute-start(bf16[256,512]{1,0:T(8,128)(2,1)S(1)} %collective-permute-done.12.rest_1_), channel_id=1, source_target_pairs={{0,16},{16,0},{1,17},{17,1},{2,18},{18,2},{3,19},{19,3},{4,20},{20... | collective-permute-start | bytes 786440 | tf_op jit(solution)/shard_map/ppermute | solution.py:100
  76.0 19.7 %collective-permute-start.7 = (bf16[2,256,1024]{2,1,0:T(8,128)(2,1)}, bf16[2,256,1024]{2,1,0:T(8,128)(2,1)}, u32[]{:S(2)}, u32[]{:S(2)}) collective-permute-start(bf16[2,256,1024]{2,1,0:T(8,128)(2,1)} %pad_maximum_fusion.3), channel_id=1, source_target_pairs={{0,4},{4,0},{8,12},{12,8},{1,5},{5,1},{9,13},{13,9},{2,6},{6,2},{1... | collective-permute-start | bytes 3145736 | tf_op jit(solution)/shard_map/ppermute | solution.py:100
  78.3 9.3 %collective-permute-start.16 = (bf16[256,512]{1,0:T(8,128)(2,1)S(1)}, bf16[256,512]{1,0:T(8,128)(2,1)}, u32[]{:S(2)}, u32[]{:S(2)}) collective-permute-start(bf16[256,512]{1,0:T(8,128)(2,1)S(1)} %collective-permute-done.13.rest_2_), channel_id=1, source_target_pairs={{0,16},{16,0},{1,17},{17,1},{2,18},{18,2},{3,19},{19,3},{4,20},{20... | collective-permute-start | bytes 786440 | tf_op jit(solution)/shard_map/ppermute | solution.py:100
  79.8 17.9 %collective-permute-start.4 = (bf16[2,256,1024]{2,1,0:T(8,128)(2,1)}, bf16[2,256,1024]{2,1,0:T(8,128)(2,1)}, u32[]{:S(2)}, u32[]{:S(2)}) collective-permute-start(bf16[2,256,1024]{2,1,0:T(8,128)(2,1)} %pad_maximum_fusion.2), channel_id=1, source_target_pairs={{0,4},{4,0},{8,12},{12,8},{1,5},{5,1},{9,13},{13,9},{2,6},{6,2},{1... | collective-permute-start | bytes 3145736 | tf_op jit(solution)/shard_map/ppermute | solution.py:100
  82.2 17.6 %collective-permute-start.10 = (bf16[2,256,1024]{2,1,0:T(8,128)(2,1)}, bf16[2,256,1024]{2,1,0:T(8,128)(2,1)}, u32[]{:S(2)}, u32[]{:S(2)}) collective-permute-start(bf16[2,256,1024]{2,1,0:T(8,128)(2,1)} %pad_maximum_fusion.4), channel_id=1, source_target_pairs={{0,4},{4,0},{8,12},{12,8},{1,5},{5,1},{9,13},{13,9},{2,6},{6,2},{1... | collective-permute-start | bytes 3145736 | tf_op jit(solution)/shard_map/ppermute | solution.py:100
  106.3 25.0 %collective-permute-start.24 = (bf16[2,256,1024]{2,1,0:T(8,128)(2,1)}, bf16[2,256,1024]{2,1,0:T(8,128)(2,1)}, u32[]{:S(2)}, u32[]{:S(2)}) collective-permute-start(bf16[2,256,1024]{2,1,0:T(8,128)(2,1)} %slice.118), channel_id=1, source_target_pairs={{0,4},{4,0},{8,12},{12,8},{1,5},{5,1},{9,13},{13,9},{2,6},{6,2},{1... | collective-permute-start | bytes 3145736 | tf_op jit(solution)/shard_map/ppermute | solution.py:100
  110.4 22.9 %collective-permute-start.22 = (bf16[2,256,1024]{2,1,0:T(8,128)(2,1)}, bf16[2,256,1024]{2,1,0:T(8,128)(2,1)S(1)}, u32[]{:S(2)}, u32[]{:S(2)}) collective-permute-start(bf16[2,256,1024]{2,1,0:T(8,128)(2,1)} %slice.114), channel_id=1, source_target_pairs={{0,4},{4,0},{8,12},{12,8},{1,5},{5,1},{9,13},{13,9},{2,6},{6,2},{1... | collective-permute-start | bytes 3145736 | tf_op jit(solution)/shard_map/ppermute | solution.py:100
  115.1 19.9 %collective-permute-start.19 = (bf16[2,256,1024]{2,1,0:T(8,128)(2,1)}, bf16[2,256,1024]{2,1,0:T(8,128)(2,1)S(1)}, u32[]{:S(2)}, u32[]{:S(2)}) collective-permute-start(bf16[2,256,1024]{2,1,0:T(8,128)(2,1)} %slice.110), channel_id=1, source_target_pairs={{0,4},{4,0},{8,12},{12,8},{1,5},{5,1},{9,13},{13,9},{2,6},{6,2},{1... | collective-permute-start | bytes 3145736 | tf_op jit(solution)/shard_map/ppermute | solution.py:100
  119.2 29.9 %collective-permute-start.17 = (bf16[2,256,1024]{2,1,0:T(8,128)(2,1)}, bf16[2,256,1024]{2,1,0:T(8,128)(2,1)S(1)}, u32[]{:S(2)}, u32[]{:S(2)}) collective-permute-start(bf16[2,256,1024]{2,1,0:T(8,128)(2,1)} %slice.106), channel_id=1, source_target_pairs={{0,4},{4,0},{8,12},{12,8},{1,5},{5,1},{9,13},{13,9},{2,6},{6,2},{1... | collective-permute-start | bytes 3145736 | tf_op jit(solution)/shard_map/ppermute | solution.py:100
  127.2 44.9 %collective-permute-start.29 = (bf16[512,512]{1,0:T(8,128)(2,1)S(1)}, bf16[512,512]{1,0:T(8,128)(2,1)S(1)}, u32[]{:S(2)}, u32[]{:S(2)}) collective-permute-start(bf16[512,512]{1,0:T(8,128)(2,1)S(1)} %get-tuple-element.59), channel_id=1, source_target_pairs={{0,2},{1,3},{2,0},{3,1},{4,6},{5,7},{6,4},{7,5},{8,10},{9,11},{10,... | collective-permute-start | bytes 1572872 | tf_op jit(solution)/shard_map/ppermute | solution.py:100
  132.7 14.8 %collective-permute-start.25 = (bf16[2,128,1024]{2,1,0:T(8,128)(2,1)S(1)}, bf16[2,128,1024]{2,1,0:T(8,128)(2,1)S(1)}, u32[]{:S(2)}, u32[]{:S(2)}) collective-permute-start(bf16[2,128,1024]{2,1,0:T(8,128)(2,1)S(1)} %slice.147), channel_id=1, source_target_pairs={{0,8},{4,12},{8,0},{12,4},{1,9},{5,13},{9,1},{13,5},{2,10},{6,14},... | collective-permute-start | bytes 1572872 | tf_op jit(solution)/shard_map/ppermute | solution.py:100
  133.4 38.1 %collective-permute-start.23 = (bf16[2,128,1024]{2,1,0:T(8,128)(2,1)S(1)}, bf16[2,128,1024]{2,1,0:T(8,128)(2,1)S(1)}, u32[]{:S(2)}, u32[]{:S(2)}) collective-permute-start(bf16[2,128,1024]{2,1,0:T(8,128)(2,1)S(1)} %slice.145), channel_id=1, source_target_pairs={{0,8},{4,12},{8,0},{12,4},{1,9},{5,13},{9,1},{13,5},{2,10},{6,14},... | collective-permute-start | bytes 1572872 | tf_op jit(solution)/shard_map/ppermute | solution.py:100
  135.2 34.7 %collective-permute-start.20 = (bf16[2,128,1024]{2,1,0:T(8,128)(2,1)S(1)}, bf16[2,128,1024]{2,1,0:T(8,128)(2,1)S(1)}, u32[]{:S(2)}, u32[]{:S(2)}) collective-permute-start(bf16[2,128,1024]{2,1,0:T(8,128)(2,1)S(1)} %slice.143), channel_id=1, source_target_pairs={{0,8},{4,12},{8,0},{12,4},{1,9},{5,13},{9,1},{13,5},{2,10},{6,14},... | collective-permute-start | bytes 1572872 | tf_op jit(solution)/shard_map/ppermute | solution.py:100
  147.6 24.0 %collective-permute-start.26 = (bf16[2,128,1024]{2,1,0:T(8,128)(2,1)S(1)}, bf16[2,128,1024]{2,1,0:T(8,128)(2,1)S(1)}, u32[]{:S(2)}, u32[]{:S(2)}) collective-permute-start(bf16[2,128,1024]{2,1,0:T(8,128)(2,1)S(1)} %slice_add_fusion.4), channel_id=1, source_target_pairs={{0,1},{1,0},{2,3},{3,2},{4,5},{5,4},{6,7},{7,6},{8,9},{9,8},{10,11... | collective-permute-start | bytes 1572872 | tf_op jit(solution)/shard_map/ppermute | solution.py:100
  149.3 48.4 %collective-permute-start.18 = (bf16[2,128,1024]{2,1,0:T(8,128)(2,1)S(1)}, bf16[2,128,1024]{2,1,0:T(8,128)(2,1)S(1)}, u32[]{:S(2)}, u32[]{:S(2)}) collective-permute-start(bf16[2,128,1024]{2,1,0:T(8,128)(2,1)S(1)} %slice.141), channel_id=1, source_target_pairs={{0,8},{4,12},{8,0},{12,4},{1,9},{5,13},{9,1},{13,5},{2,10},{6,14},... | collective-permute-start | bytes 1572872 | tf_op jit(solution)/shard_map/ppermute | solution.py:100
  170.0 21.5 %collective-permute-start.21 = (bf16[2,128,1024]{2,1,0:T(8,128)(2,1)S(1)}, bf16[2,128,1024]{2,1,0:T(8,128)(2,1)S(1)}, u32[]{:S(2)}, u32[]{:S(2)}) collective-permute-start(bf16[2,128,1024]{2,1,0:T(8,128)(2,1)S(1)} %slice_add_fusion.6), channel_id=1, source_target_pairs={{0,1},{1,0},{2,3},{3,2},{4,5},{5,4},{6,7},{7,6},{8,9},{9,8},{10,11... | collective-permute-start | bytes 1572872 | tf_op jit(solution)/shard_map/ppermute | solution.py:100
  171.8 25.8 %collective-permute-start.27 = (bf16[2,128,1024]{2,1,0:T(8,128)(2,1)S(1)}, bf16[2,128,1024]{2,1,0:T(8,128)(2,1)S(1)}, u32[]{:S(2)}, u32[]{:S(2)}) collective-permute-start(bf16[2,128,1024]{2,1,0:T(8,128)(2,1)S(1)} %add_convert_fusion), channel_id=1, source_target_pairs={{0,2},{1,3},{2,0},{3,1},{4,6},{5,7},{6,4},{7,5},{8,10},{9,11},{10,... | collective-permute-start | bytes 1572872 | tf_op jit(solution)/shard_map/ppermute | solution.py:100
  191.5 15.9 %collective-permute-start.28 = (bf16[512,512]{1,0:T(8,128)(2,1)S(1)}, bf16[512,512]{1,0:T(8,128)(2,1)S(1)}, u32[]{:S(2)}, u32[]{:S(2)}) collective-permute-start(bf16[512,512]{1,0:T(8,128)(2,1)S(1)} %get-tuple-element.51), channel_id=1, source_target_pairs={{0,1},{1,0},{2,3},{3,2},{4,5},{5,4},{6,7},{7,6},{8,9},{9,8},{10,11... | collective-permute-start | bytes 1572872 | tf_op jit(solution)/shard_map/ppermute | solution.py:100
  197.6 30.8 %collective-permute-start.30 = (bf16[512,512]{1,0:T(8,128)(2,1)S(1)}, bf16[512,512]{1,0:T(8,128)(2,1)S(1)}, u32[]{:S(2)}, u32[]{:S(2)}) collective-permute-start(bf16[512,512]{1,0:T(8,128)(2,1)S(1)} %get-tuple-element.52), channel_id=1, source_target_pairs={{0,3},{1,2},{2,1},{3,0},{4,7},{5,6},{6,5},{7,4},{8,11},{9,10},{10,... | collective-permute-start | bytes 1572872 | tf_op jit(solution)/shard_map/ppermute | solution.py:100
  198.4 20.8 %collective-permute-start.31 = (f32[2,1024]{1,0:T(2,128)S(1)}, f32[2,1024]{1,0:T(2,128)S(1)}, u32[]{:S(2)}, u32[]{:S(2)}) collective-permute-start(f32[2,1024]{1,0:T(2,128)S(1)} %pad_maximum_fusion.6), channel_id=1, source_target_pairs={{0,2},{1,3},{2,0},{3,1},{4,6},{5,7},{6,4},{7,5},{8,10},{9,11},{10,... | collective-permute-start | bytes 24584 | tf_op jit(solution)/shard_map/ppermute | solution.py:100
  (32 other events, 264.1 us)

commit v4 on v3

v4 whole, which is shorter than its diff:
```python
import math

import jax
import jax.numpy as jnp
from jax import lax
from jax.experimental import pallas as pl
from jax.experimental.pallas import tpu as pltpu
from jax.sharding import PartitionSpec as P

epsilon = 1e-06


def normalize(row_data, norm_gain, norm_bias):
    values = row_data.astype(jnp.float32)
    row_mean = jnp.mean(values, axis=-1, keepdims=True)
    centred = values - row_mean
    inv_std = lax.rsqrt(jnp.mean(centred * centred, axis=-1, keepdims=True) + epsilon)
    standard = centred * inv_std
    normed = (standard * norm_gain + norm_bias).astype(jnp.bfloat16)
    return (standard, inv_std, normed)


def contract_tokens(left_rows, right_rows):
    return lax.dot_general(
        left_rows, right_rows, (((0,), (0,)), ((), ())), preferred_element_type=jnp.float32
    )


def contract_last(left_rows, right_rows):
    return lax.dot_general(
        left_rows, right_rows, (((1,), (1,)), ((), ())), preferred_element_type=jnp.float32
    )


def finish_rows(branch, grad_normed, second_out, grad_first, first_out, norm_gain, norm_bias):
    standard, inv_std, _ = normalize(first_out, norm_gain, norm_bias)
    second_in = (second_out.astype(jnp.float32) - branch).astype(jnp.bfloat16)
    grad_std = grad_normed * norm_gain
    grad_rows = inv_std * (
        grad_std
        - jnp.mean(grad_std, axis=-1, keepdims=True)
        - standard * jnp.mean(grad_std * standard, axis=-1, keepdims=True)
    )
    return second_in, grad_first.astype(jnp.float32) + grad_rows


def gather_weights_body(
    first_out, second_out, grad_first, grad_second, w_up, w_down, norm_gain, norm_bias
):
    own_rows = first_out.shape[0]
    up_full = lax.all_gather(w_up, "dp", axis=0, tiled=True)
    down_full = lax.all_gather(w_down, "dp", axis=1, tiled=True)
    first_all = lax.all_gather(first_out, "tensor", axis=0, tiled=True)
    grad_all = lax.all_gather(grad_second, "tensor", axis=0, tiled=True)
    standard_all, _, normed = normalize(first_all, norm_gain, norm_bias)
    offset = lax.axis_index("tensor") * own_rows
    standard = lax.dynamic_slice_in_dim(standard_all, offset, own_rows, 0)
    preact = jnp.dot(normed, up_full, preferred_element_type=jnp.float32)
    hidden = jax.nn.gelu(preact).astype(jnp.bfloat16)
    branch = lax.psum_scatter(
        jnp.dot(hidden, down_full, preferred_element_type=jnp.float32).astype(jnp.bfloat16),
        "tensor",
        scatter_dimension=0,
        tiled=True,
    ).astype(jnp.float32)
    tokens = own_rows * lax.axis_size("tensor") * lax.axis_size("dp")
    grad_scale = tokens ** (-0.5)
    grad_down_part = contract_tokens(hidden, grad_all)
    grad_down = (
        lax.psum_scatter(
            grad_down_part.astype(jnp.bfloat16), "dp", scatter_dimension=1, tiled=True
        ).astype(jnp.float32)
        * grad_scale
    )
    grad_hidden = contract_last(grad_all, down_full)
    grad_pre = jax.vjp(jax.nn.gelu, preact)[1](grad_hidden)[0].astype(jnp.bfloat16)
    grad_up_part = contract_tokens(normed, grad_pre)
    grad_up = (
        lax.psum_scatter(
            grad_up_part.astype(jnp.bfloat16), "dp", scatter_dimension=0, tiled=True
        ).astype(jnp.float32)
        * grad_scale
    )
    grad_normed = lax.psum_scatter(
        contract_last(grad_pre, up_full).astype(jnp.bfloat16),
        "tensor",
        scatter_dimension=0,
        tiled=True,
    ).astype(jnp.float32)
    second_in, grad_first_in = finish_rows(
        branch, grad_normed, second_out, grad_first, first_out, norm_gain, norm_bias
    )
    local_stats = jnp.stack([jnp.sum(grad_normed * standard, axis=0), jnp.sum(grad_normed, axis=0)])
    grad_norm = lax.psum(local_stats, ("tensor", "dp")) * grad_scale
    return (second_in, grad_first_in, grad_up, grad_down, grad_norm)


def swap(values, axis, mask, scope):
    with jax.named_scope(scope):
        return lax.ppermute(values, axis, [(i, i ^ mask) for i in range(lax.axis_size(axis))])


def bits_of(size):
    return [1 << b for b in reversed(range(size.bit_length() - 1))]


def pack(first_out, grad_second, w_up, w_down, mates):
    n_dp = lax.axis_size("dp")
    depth, units = w_up.shape[0], w_up.shape[1] // n_dp
    up_rows, down_rows, strips = depth // mates, units // mates, units // depth
    strip_rows = down_rows // strips

    def kernel(first_ref, grad_ref, up_ref, down_ref, rows_ref, *sends):
        rows_ref[0] = first_ref[...]
        rows_ref[1] = grad_ref[...]
        place, mate = lax.axis_index("dp"), lax.rem(lax.axis_index("groups"), mates)
        for k in range(1, n_dp):
            first = pl.multiple_of((place ^ k) * units, units)
            send = sends[k - 1]
            row = pl.multiple_of(mate * up_rows, up_rows)
            send[:up_rows, :] = up_ref[pl.ds(row, up_rows), pl.ds(first, units)]
            for c in range(strips):
                row = pl.multiple_of(first + mate * down_rows + c * strip_rows, strip_rows)
                send[up_rows:, c * depth : (c + 1) * depth] = down_ref[pl.ds(row, strip_rows), :]

    return pl.pallas_call(
        kernel,
        out_shape=[jax.ShapeDtypeStruct((2, *first_out.shape), first_out.dtype)]
        + [jax.ShapeDtypeStruct((2 * up_rows, units), w_up.dtype)] * (n_dp - 1),
        in_specs=[pl.BlockSpec(memory_space=pltpu.VMEM)] * 4,
        out_specs=[pl.BlockSpec(memory_space=pltpu.VMEM)] * n_dp,
        cost_estimate=pl.CostEstimate(
            flops=0, bytes_accessed=8 * (w_up.size + first_out.size), transcendentals=0
        ),
        name="pack",
    )(first_out, grad_second, w_up, w_down)


def unpack_weights(w_up, w_down, got, mates):
    n_dp = lax.axis_size("dp")
    depth, units = w_up.shape[0], w_up.shape[1] // n_dp
    up_rows, down_rows, strips = depth // mates, units // mates, units // depth
    strip_rows = down_rows // strips

    def kernel(up_ref, down_ref, *rest):
        pieces, (up_out, down_out, sem) = rest[:-3], rest[-3:]
        place, mate = lax.axis_index("dp"), lax.rem(lax.axis_index("groups"), mates)
        copies = []

        def copy(src, dst):
            one = pltpu.make_async_copy(src, dst, sem.at[len(copies)])
            one.start()
            copies.append(one)

        copy(
            up_ref.at[:, pl.ds(pl.multiple_of(place * units, units), units)],
            up_out.at[pl.ds(pl.multiple_of(place * depth, depth), depth), :],
        )
        copy(
            down_ref.at[pl.ds(pl.multiple_of(place * units, units), units), :],
            down_out.at[:, pl.ds(pl.multiple_of(place * depth, depth), depth)],
        )
        for k in range(1, n_dp):
            first = pl.multiple_of((place ^ k) * depth, depth)
            for j in range(mates):
                piece = pieces[j * (n_dp - 1) + k - 1]
                part = mate ^ j
                row = pl.multiple_of(first + part * up_rows, up_rows)
                copy(piece.at[pl.ds(0, up_rows), :], up_out.at[pl.ds(row, up_rows), :])
                for c in range(strips):
                    row = pl.multiple_of(part * down_rows + c * strip_rows, strip_rows)
                    copy(
                        piece.at[pl.ds(up_rows, strip_rows), pl.ds(c * depth, depth)],
                        down_out.at[pl.ds(row, strip_rows), pl.ds(first, depth)],
                    )
        for one in copies:
            one.wait()

    return pl.pallas_call(
        kernel,
        out_shape=[
            jax.ShapeDtypeStruct((depth * n_dp, units), w_up.dtype),
            jax.ShapeDtypeStruct((units, depth * n_dp), w_down.dtype),
        ],
        in_specs=[pl.BlockSpec(memory_space=pl.ANY)] * (2 + mates * (n_dp - 1)),
        out_specs=[pl.BlockSpec(memory_space=pltpu.VMEM)] * 2,
        scratch_shapes=[pltpu.SemaphoreType.DMA((2 + mates * (n_dp - 1) * (1 + strips),))],
        cost_estimate=pl.CostEstimate(flops=0, bytes_accessed=16 * w_up.size, transcendentals=0),
        name="unpack_weights",
    )(w_up, w_down, *[piece for pieces in got for piece in pieces])


def weight_grads(place, first, count, normeds, grads, hiddens, grad_pres, n_dp):
    n_chunks, n_pieces = len(normeds), len(grads)
    (rows, width), units = normeds[0].shape, hiddens[0].shape[1]
    piece_rows, depth = grads[0].shape[1], width // n_dp
    strips = units // depth

    def kernel(place_ref, *refs):
        out = refs[-1]
        norm = jnp.concatenate([ref[...] for ref in refs[:n_chunks]], axis=0)
        refs = refs[n_chunks:]
        grad = jnp.concatenate([ref[0] for ref in refs[:n_pieces]], axis=0)
        refs = refs[n_pieces:]
        hid = jnp.concatenate([ref[...] for ref in refs[:n_chunks]], axis=0)
        pre = jnp.concatenate([ref[...] for ref in refs[n_chunks:-1]], axis=0)
        out[0, :depth, :] = contract_tokens(norm, pre).astype(out.dtype)
        down = contract_tokens(hid, grad).astype(out.dtype)
        for c in range(strips):
            out[0, depth:, c * depth : (c + 1) * depth] = down[c * depth : (c + 1) * depth]

    return pl.pallas_call(
        kernel,
        out_shape=jax.ShapeDtypeStruct((count, 2 * depth, units), jnp.bfloat16),
        grid_spec=pltpu.PrefetchScalarGridSpec(
            num_scalar_prefetch=1,
            grid=(count,),
            in_specs=[pl.BlockSpec((rows, depth), lambda k, p: (0, p[0] ^ (first + k)))] * n_chunks
            + [pl.BlockSpec((1, piece_rows, depth), lambda k, p: (1, 0, p[0] ^ (first + k)))] * n_pieces
            + [pl.BlockSpec((rows, units), lambda k, p: (0, 0))] * (2 * n_chunks),
            out_specs=pl.BlockSpec((1, 2 * depth, units), lambda k, p: (k, 0, 0)),
        ),
        compiler_params=pltpu.CompilerParams(vmem_limit_bytes=40 * 1024 * 1024),
        cost_estimate=pl.CostEstimate(
            flops=4 * n_chunks * rows * depth * count * units,
            bytes_accessed=4 * n_chunks * rows * (depth * count + units),
            transcendentals=0,
        ),
        name="weight_grads",
    )(place.reshape(1), *normeds, *grads, *hiddens, *grad_pres)


def middle(pieces, up, down, gain, bias):
    (_, piece_rows, width), units, n = pieces[0].shape, up.shape[1], len(pieces)
    rows = n * piece_rows
    slope = (2.0 / math.pi) ** 0.5

    def kernel(*refs):
        toks, (up_ref, down_ref, gain_ref, bias_ref) = refs[:n], refs[n : n + 4]
        norm_ref, hid_ref, pre_ref, stat_ref = refs[n + 4 : n + 8]
        parts = refs[n + 8 :]
        half_n = max(n // 2, 1)
        stat_ref[...] = jnp.zeros_like(stat_ref)
        for first in range(0, n, half_n):
            here = range(first, first + half_n)
            span = slice(first * piece_rows, (first + half_n) * piece_rows)
            values = jnp.concatenate([toks[j][0] for j in here], axis=0).astype(jnp.float32)
            centred = values - jnp.mean(values, axis=-1, keepdims=True)
            inv_std = lax.rsqrt(jnp.mean(centred * centred, axis=-1, keepdims=True) + epsilon)
            standard = centred * inv_std
            normed = (standard * gain_ref[...] + bias_ref[...]).astype(jnp.bfloat16)
            grads = jnp.concatenate([toks[j][1] for j in here], axis=0)
            x = jnp.dot(normed, up_ref[...], preferred_element_type=jnp.float32)
            gate = jnp.tanh(slope * (x + 0.044715 * (x * x * x)))
            half = 0.5 + 0.5 * gate
            hidden = (x * half).astype(jnp.bfloat16)
            rise = half + (0.5 * slope) * x * (1.0 - gate * gate) * (1.0 + (3 * 0.044715) * (x * x))
            grad_pre = (contract_last(grads, down_ref[...]) * rise).astype(jnp.bfloat16)
            norm_ref[span, :] = normed
            hid_ref[span, :] = hidden
            pre_ref[span, :] = grad_pre
            branch = jnp.dot(hidden, down_ref[...], preferred_element_type=jnp.float32)
            grad_normed = contract_last(grad_pre, up_ref[...])
            stat_ref[0:1, :] += jnp.sum(grad_normed * standard, axis=0, keepdims=True)
            stat_ref[1:2, :] += jnp.sum(grad_normed, axis=0, keepdims=True)
            for j in here:
                own = slice((j - first) * piece_rows, (j - first + 1) * piece_rows)
                parts[j][0] = branch[own].astype(jnp.bfloat16)
                parts[j][1] = grad_normed[own].astype(jnp.bfloat16)

    out = pl.pallas_call(
        kernel,
        out_shape=[
            jax.ShapeDtypeStruct((rows, width), jnp.bfloat16),
            jax.ShapeDtypeStruct((rows, units), jnp.bfloat16),
            jax.ShapeDtypeStruct((rows, units), jnp.bfloat16),
            jax.ShapeDtypeStruct((2, width), jnp.float32),
        ]
        + [jax.ShapeDtypeStruct((2, piece_rows, width), jnp.bfloat16)] * n,
        in_specs=[pl.BlockSpec(memory_space=pltpu.VMEM)] * (n + 4),
        out_specs=[pl.BlockSpec(memory_space=pltpu.VMEM)] * (n + 4),
        compiler_params=pltpu.CompilerParams(vmem_limit_bytes=32 * 1024 * 1024),
        cost_estimate=pl.CostEstimate(
            flops=8 * rows * width * units,
            bytes_accessed=10 * rows * width + 4 * width * units,
            transcendentals=rows * units,
        ),
        name="middle",
    )(*pieces, up, down, gain.reshape(1, width), bias.reshape(1, width))
    return out[0], out[1], out[2], out[3], dict(enumerate(out[4:]))


def after(values, *others):
    return lax.optimization_barrier((values, *others))[0]


def gather_tokens_body(
    first_out, second_out, grad_first, grad_second, w_up, w_down, norm_gain, norm_bias
):
    n_dp, n_tensor, n_groups = (lax.axis_size(axis) for axis in ("dp", "tensor", "groups"))
    own_rows, depth = first_out.shape[0], w_up.shape[0]
    units = w_up.shape[1] // n_dp
    mates = 2 if n_groups % 2 == 0 else 1
    place = lax.axis_index("dp")
    top = bits_of(n_dp)[0]

    own, *sends = pack(first_out, grad_second, w_up, w_down, mates)
    high, others = bits_of(n_tensor)[0], bits_of(n_tensor)[1:]
    tokens, chunks, got = {0: own}, {}, {}

    def tokens_dp(k, *first):
        tokens[k] = swap(after(tokens[k & (k - 1)], *first), "dp", k & -k, f"tokens_{k}")

    def tokens_tensor(k, *first):
        start = after(tokens[k], *first)
        chunks[k] = {0: tokens[k], high: swap(start, "tensor", high, f"tokens_{k}_{high}")}
        for bit in others:
            for j in list(chunks[k]):
                chunks[k][j | bit] = swap(chunks[k][j], "tensor", bit, f"tokens_{k}_{j | bit}")

    def weights_dp(k, *first):
        got[k] = swap(after(sends[k - 1], *first), "dp", k, f"weights_{k}")

    tokens_tensor(0)
    for bit in bits_of(n_dp):
        tokens_dp(bit)
    tokens_tensor(1, chunks[0][high])
    for bit in reversed(bits_of(n_dp)):
        weights_dp(bit, tokens[1], chunks[0][high])
    for k in range(2, n_dp):
        if k & (k - 1):
            tokens_dp(k, got[1], *chunks[0].values())
            weights_dp(k, tokens[top], got[1], chunks[1][high])
        tokens_tensor(k, chunks[k - 1][high], got[1 if k <= top else top])
    got = [got[k] for k in range(1, n_dp)]
    crossed = []
    if mates == 2:
        for k, piece in enumerate(got, 1):
            first = (*crossed[-1:], *chunks[k - 2].values()) if k > 1 else ()
            crossed.append(swap(after(piece, *first), "groups", 1, f"weights_{k}"))
    got = [got, crossed]
    up, down = unpack_weights(w_up, w_down, got[:mates], mates)

    order = sorted(chunks, reverse=True)
    normeds, hiddens, grad_pres, all_stats, ready = [], [], [], [], []
    for i, k in enumerate(order):
        pieces = [chunks[k][j] for j in range(n_tensor)]
        if i >= 1:
            pieces[0] = after(pieces[0], hiddens[-1], *(ready[i - 2] if i >= 2 else ()))
        normed, hidden, grad_pre, stats, parts = middle(pieces, up, down, norm_gain, norm_bias)
        normeds.append(normed)
        hiddens.append(hidden)
        grad_pres.append(grad_pre)
        all_stats.append(stats)
        for bit in reversed(others):
            for j in sorted((j for j in parts if j & bit), reverse=True):
                parts[j ^ bit] = parts[j ^ bit] + swap(parts.pop(j), "tensor", bit, f"sums_{k}_{j}")
        ready.append((parts[0], parts[high]))
    high_came = []
    for i, k in enumerate(order):
        part = after(ready[i][1], ready[i][0], *high_came[:i][-1:])
        high_came.append(swap(part, "tensor", high, f"sums_{k}_{high}"))
    grads = [chunks[k][j] for k in order for j in range(n_tensor)]
    grads[0] = after(grads[0], *ready[-2])
    far = weight_grads(place, top, n_dp - top, normeds, grads, hiddens, grad_pres, n_dp)
    grads[0] = after(grads[0], far)
    near = weight_grads(place, 0, top, normeds, grads, hiddens, grad_pres, n_dp)
    blocks = {k: near[k] if k < top else far[k - top] for k in range(n_dp)}
    blocks[top] = swap(blocks[top], "dp", top, f"grads_{top}")

    sums, came = {}, {}
    for i, k in enumerate(order):
        sums[k] = ready[i][0] + after(high_came[i], far, *sums.values())
        if i == 0 and k != top:
            sums[k] = after(sums[k], near)
            came[k] = swap(sums[k], "dp", k & -k, f"sums_{k}")
            sums[k] = came[k]
    for bit in bits_of(n_dp)[::-1]:
        inner = [k for k in order if k & bit and k in sums and k != bit]
        for k in inner:
            if k not in came:
                came[k] = swap(sums[k], "dp", bit, f"sums_{k}")
            del sums[k]
            sums[k ^ bit] = (sums[k ^ bit].astype(jnp.float32) + came[k]).astype(jnp.bfloat16)
    last = sums[top]
    came[top] = swap(last, "dp", top, f"sums_{top}")
    for bit in bits_of(n_dp)[:0:-1]:
        came[bit] = swap(after(sums[bit], last), "dp", bit, f"sums_{bit}")
    total = sums[0].astype(jnp.float32)
    for bit in bits_of(n_dp)[::-1]:
        total = total + came[bit].astype(jnp.float32)
    sums = {0: total}
    for k in range(1, n_dp):
        if k < top:
            blocks[k] = swap(after(blocks[k], last), "dp", k, f"grads_{k}")
        elif k > top:
            blocks[k] = swap(after(blocks[k], blocks[top], last), "dp", k, f"grads_{k}")
    blocks[top] = after(blocks[top], last)
    branch, grad_normed = sums[0][0], sums[0][1]
    second_in, grad_first_in = finish_rows(
        branch, grad_normed, second_out, grad_first, first_out, norm_gain, norm_bias
    )

    stats = after(sum(all_stats), blocks[top], came[1])
    for axis in ("tensor", "dp"):
        for bit in bits_of(lax.axis_size(axis)):
            stats = stats + swap(stats, axis, bit, "stats")
    blocks[n_dp - 1] = after(blocks[n_dp - 1], stats)

    grad_scale = (own_rows * n_tensor * n_dp) ** (-0.5)
    grad_up = jnp.zeros(w_up.shape, jnp.float32)
    grad_down = jnp.zeros(w_down.shape, jnp.float32)
    for k in range(n_dp):
        other = place ^ k
        block = blocks[k].astype(jnp.float32) * grad_scale
        grad_up = lax.dynamic_update_slice_in_dim(grad_up, block[:depth], other * units, 1)
        strips = [block[depth:, c * depth : (c + 1) * depth] for c in range(units // depth)]
        grad_down = lax.dynamic_update_slice_in_dim(
            grad_down, jnp.concatenate(strips, axis=0), other * units, 0
        )

    return (second_in, grad_first_in, grad_up, grad_down, stats * grad_scale)


def body(first_out, second_out, grad_first, grad_second, w_up, *rest):
    n_dp, n_tensor = lax.axis_size("dp"), lax.axis_size("tensor")
    powers = all(size > 1 and size & (size - 1) == 0 for size in (n_dp, n_tensor))
    few_tokens = first_out.shape[0] * n_tensor < w_up.shape[1]
    units, depth = w_up.shape[1] // n_dp, w_up.shape[0]
    fits = w_up.shape[1] % n_dp == 0 and units % depth == 0 and depth % 128 == 0
    pick = gather_tokens_body if powers and few_tokens and fits else gather_weights_body
    return pick(first_out, second_out, grad_first, grad_second, w_up, *rest)


def solution(mesh):
    in_specs = (
        P(("groups", "tensor", "dp"), None),
        P(("groups", "tensor", "dp"), None),
        P(("groups", "tensor", "dp"), None),
        P(("groups", "tensor", "dp"), None),
        P("dp", "tensor"),
        P("tensor", "dp"),
        P(),
        P(),
    )
    out_specs = (
        P(("groups", "tensor", "dp"), None),
        P(("groups", "tensor", "dp"), None),
        P(("groups", "dp"), "tensor"),
        P(("groups", "tensor"), "dp"),
        P("groups", None),
    )
    return jax.shard_map(body, mesh=mesh, in_specs=in_specs, out_specs=out_specs, check_vma=False)
```

time: 231 us -> 230 us (level)
  Pallas kernels: 24.8 us -> 31.7 us
  other arithmetic: 18.2 us -> 12.2 us
  local copies, waits for them, and re-layouts: 21.7 us -> 16.5 us
    concatenate x5 -> x0, other arithmetic: 8.25 us -> none  [gather_tokens_body(): chunk = jnp.concatenate([chunk, swap(chunk, 'tensor', bit)], axis=1)]
    pallas_call x6 -> x7, Pallas kernels: 21.8 us -> 28.7 us  [the longest x4 17.2 us: middle(): pl.pallas_call(kernel, out_shape=[jax.ShapeDtypeStruct((rows, width), jnp...]
    add x11 -> x16, other arithmetic: 3.43 us -> 9.91 us  [the longest x8 8.01 us: gather_tokens_body(): parts[j ^ bit] + swap(parts.pop(j), 'tensor', bit, f'sums_{k}_{j}')]
    concatenate x3 -> x0, local copies, waits for them, and re-layouts: 5.68 us -> none  [gather_tokens_body(): chunk = jnp.concatenate([chunk, swap(chunk, 'tensor', bit)], axis=1)]
    unnamed x64 -> x102, local copies, waits for them, and re-layouts: 10.7 us -> 15.7 us
    slice x8 -> x0, local copies, waits for them, and re-layouts: 4.44 us -> none  [gather_tokens_body(): part = part[:, :half] + swap(part[:, half:], 'tensor', bit)]
    ppermute x35 -> x43, waiting for transfers between devices: 129 us -> 131 us  [swap(): lax.ppermute(values, axis, [(i, i ^ mask) for i in range(lax.axis_size(ax...]
    ppermute x35 -> x43, starting transfers between devices: 36.2 us -> 36.9 us  [swap(): lax.ppermute(values, axis, [(i, i ^ mask) for i in range(lax.axis_size(ax...]
  transfers between devices with their start and end apart: 35 -> 43, of which waited for: 14 -> 20; matrix products, arithmetic and copies ran while one was open for 12% -> 6% of each run, Pallas kernels for 9% -> 13%
where the time goes in v4:
time: 230 us
  waiting for transfers between devices  131 us (57%)
  starting transfers between devices  36.9 us (16%)
  Pallas kernels  31.7 us (14%)
  local copies, waits for them, and re-layouts  16.5 us (7%)
  other arithmetic  12.2 us (5%)
    ppermute x43, waiting for transfers between devices, swap(): lax.ppermute(values, axis, [(i, i ^ mask) for i in range(lax.axis_size(ax...  131 us
    ppermute x43, starting transfers between devices, swap(): lax.ppermute(values, axis, [(i, i ^ mask) for i in range(lax.axis_size(ax...  36.9 us
    pallas_call x4, Pallas kernels, middle(): pl.pallas_call(kernel, out_shape=[jax.ShapeDtypeStruct((rows, width), jnp...  17.2 us
    unnamed x102, local copies, waits for them, and re-layouts  15.7 us
    pallas_call x2, Pallas kernels, weight_grads(): pl.pallas_call(kernel, out_shape=jax.ShapeDtypeStruct((count, 2 * depth,...  8.71 us
    add x8, other arithmetic, gather_tokens_body(): parts[j ^ bit] + swap(parts.pop(j), 'tensor', bit, f'sums_{k}_{j}')  8.01 us
  transfers between devices with their start and end apart: 43, of which 20 were waited for; matrix products, arithmetic and copies ran while one was open for 6% of the time, Pallas kernels for 13%

profile of v4, /device:TPU:0, one launch (start us, length us, event | category | flops | bytes accessed | tf_op | source)
XLA Modules:
  0.0 229.9 jit_solution(4112673502614351184)
XLA Ops:
  0.6 2.8 %pack.1 = (bf16[2,128,1024]{2,1,0:T(8,128)(2,1)}, bf16[256,512]{1,0:T(8,128)(2,1)}, bf16[256,512]{1,0:T(8,128)(2,1)}, bf16[256,512]{1,0:T(8,128)(2,1)}) custom-call(bf16[128,1024]{1,0:T(8,128)(2,1)} %first_ref.1, bf16[128,1024]{1,0:T(8,128)(2,1)} %grad_ref.1, bf16[256,2048]{1,0:T(8,128)(2,1)} %up_ref.3, bf16[2048,256]{1,0:T(8,128)(2,1)} %down_ref.3), custom_call_target="tpu_custom_call" | custom-call | bytes 5242880 | tf_op jit(solution)/shard_map/pack/pallas_call | solution.py:126
  3.5 3.0 %collective-permute-start.2 = (bf16[2,128,1024]{2,1,0:T(8,128)(2,1)}, bf16[2,128,1024]{2,1,0:T(8,128)(2,1)S(1)}, u32[]{:S(2)}, u32[]{:S(2)}) collective-permute-start(bf16[2,128,1024]{2,1,0:T(8,128)(2,1)} %get-tuple-element.100.refs_0_.refs_16_), channel_id=1, source_target_pairs={{0,8},{4,12},{8,0},{12,4},{1,9},{5,13},{9,1},{13,5},{2,10},{6,14},... | collective-permute-start | bytes 1572872 | tf_op jit(solution)/shard_map/tokens_0_2/ppermute | solution.py:100
  8.0 2.6 %collective-permute-start.1 = (bf16[2,128,1024]{2,1,0:T(8,128)(2,1)}, bf16[2,128,1024]{2,1,0:T(8,128)(2,1)S(1)}, u32[]{:S(2)}, u32[]{:S(2)}) collective-permute-start(bf16[2,128,1024]{2,1,0:T(8,128)(2,1)} %get-tuple-element.100.refs_0_.refs_16_), channel_id=1, source_target_pairs={{0,2},{1,3},{2,0},{3,1},{4,6},{5,7},{6,4},{7,5},{8,10},{9,11},{10,... | collective-permute-start | bytes 1572872 | tf_op jit(solution)/shard_map/tokens_2/ppermute | solution.py:100
  10.6 8.0 %collective-permute-done.2.refs_2_.refs_18_ = bf16[2,128,1024]{2,1,0:T(8,128)(2,1)S(1)} collective-permute-done((bf16[2,128,1024]{2,1,0:T(8,128)(2,1)}, bf16[2,128,1024]{2,1,0:T(8,128)(2,1)S(1)}, u32[]{:S(2)}, u32[]{:S(2)}) %collective-permute-start.2) | collective-permute-done | bytes 524320 | tf_op jit(solution)/shard_map/tokens_0_2/ppermute | solution.py:100
  18.6 11.3 %collective-permute-done.refs_0_.refs_12_ = bf16[2,128,1024]{2,1,0:T(8,128)(2,1)S(1)} collective-permute-done((bf16[2,128,1024]{2,1,0:T(8,128)(2,1)}, bf16[2,128,1024]{2,1,0:T(8,128)(2,1)S(1)}, u32[]{:S(2)}, u32[]{:S(2)}) %collective-permute-start) | collective-permute-done | bytes 524320 | tf_op jit(solution)/shard_map/tokens_1/ppermute | solution.py:100
  30.3 4.6 %collective-permute-done.1.refs_0_.refs_8_ = bf16[2,128,1024]{2,1,0:T(8,128)(2,1)S(1)} collective-permute-done((bf16[2,128,1024]{2,1,0:T(8,128)(2,1)}, bf16[2,128,1024]{2,1,0:T(8,128)(2,1)S(1)}, u32[]{:S(2)}, u32[]{:S(2)}) %collective-permute-start.1) | collective-permute-done | bytes 524320 | tf_op jit(solution)/shard_map/tokens_2/ppermute | solution.py:100
  34.9 3.9 %collective-permute-done.3.rest_0_ = bf16[256,512]{1,0:T(8,128)(2,1)S(1)} collective-permute-done((bf16[256,512]{1,0:T(8,128)(2,1)}, bf16[256,512]{1,0:T(8,128)(2,1)S(1)}, u32[]{:S(2)}, u32[]{:S(2)}) %collective-permute-start.3) | collective-permute-done | bytes 262176 | tf_op jit(solution)/shard_map/weights_1/ppermute | solution.py:100
  38.8 3.6 %collective-permute-done.8.refs_2_.refs_14_ = bf16[2,128,1024]{2,1,0:T(8,128)(2,1)S(1)} collective-permute-done((bf16[2,128,1024]{2,1,0:T(8,128)(2,1)S(1)}, bf16[2,128,1024]{2,1,0:T(8,128)(2,1)S(1)}, u32[]{:S(2)}, u32[]{:S(2)}) %collective-permute-start.8) | collective-permute-done | bytes 524320 | tf_op jit(solution)/shard_map/tokens_1_2/ppermute | solution.py:100
  43.9 10.7 %collective-permute-done.10.rest_1_ = bf16[256,512]{1,0:T(8,128)(2,1)S(1)} collective-permute-done((bf16[256,512]{1,0:T(8,128)(2,1)}, bf16[256,512]{1,0:T(8,128)(2,1)S(1)}, u32[]{:S(2)}, u32[]{:S(2)}) %collective-permute-start.10) | collective-permute-done | bytes 262176 | tf_op jit(solution)/shard_map/weights_2/ppermute | solution.py:100
  54.7 2.2 collective-permute-done.6.refs_0_.refs_4_
  56.9 1.6 collective-permute-start.11
  60.0 5.4 %collective-permute-done.14.rest_3_ = bf16[256,512]{1,0:T(8,128)(2,1)S(1)} collective-permute-done((bf16[256,512]{1,0:T(8,128)(2,1)S(1)}, bf16[256,512]{1,0:T(8,128)(2,1)S(1)}, u32[]{:S(2)}, u32[]{:S(2)}) %collective-permute-start.14) | collective-permute-done | bytes 262176 | tf_op jit(solution)/shard_map/weights_1/ppermute | solution.py:100
  66.8 3.8 %collective-permute-start.13 = (bf16[256,512]{1,0:T(8,128)(2,1)}, bf16[256,512]{1,0:T(8,128)(2,1)S(1)}, u32[]{:S(2)}, u32[]{:S(2)}) collective-permute-start(bf16[256,512]{1,0:T(8,128)(2,1)} %get-tuple-element.82), channel_id=1, source_target_pairs={{0,3},{1,2},{2,1},{3,0},{4,7},{5,6},{6,5},{7,4},{8,11},{9,10},{10,... | collective-permute-start | bytes 786440 | tf_op jit(solution)/shard_map/weights_3/ppermute | solution.py:100
  72.0 3.3 %collective-permute-done.13.rest_2_ = bf16[256,512]{1,0:T(8,128)(2,1)S(1)} collective-permute-done((bf16[256,512]{1,0:T(8,128)(2,1)}, bf16[256,512]{1,0:T(8,128)(2,1)S(1)}, u32[]{:S(2)}, u32[]{:S(2)}) %collective-permute-start.13) | collective-permute-done | bytes 262176 | tf_op jit(solution)/shard_map/weights_3/ppermute | solution.py:100
  77.3 5.3 %collective-permute-done.18.rest_5_ = bf16[256,512]{1,0:T(8,128)(2,1)} collective-permute-done((bf16[256,512]{1,0:T(8,128)(2,1)S(1)}, bf16[256,512]{1,0:T(8,128)(2,1)}, u32[]{:S(2)}, u32[]{:S(2)}) %collective-permute-start.18) | collective-permute-done | bytes 262176 | tf_op jit(solution)/shard_map/weights_3/ppermute | solution.py:100
  82.6 3.0 %unpack_weights.1 = (bf16[1024,512]{1,0:T(8,128)(2,1)}, bf16[512,1024]{1,0:T(8,128)(2,1)}) custom-call(bf16[256,2048]{1,0:T(8,128)(2,1)} %up_ref.3, bf16[2048,256]{1,0:T(8,128)(2,1)} %down_ref.3, bf16[256,512]{1,0:T(8,128)(2,1)} %copy-done.44, bf16[256,512]{1,0:T(8,128)(2,1)} %copy-done.45, bf16[256,512]{1,0:T(8,128)(2,1)} %copy-done.48, ...), custom_call_target="tpu_custom_call" | custom-call | bytes 8388608 | tf_op jit(solution)/shard_map/unpack_weights/pallas_call | solution.py:179
  88.1 4.8 %middle.4 = (bf16[512,1024]{1,0:T(8,128)(2,1)S(1)}, bf16[512,512]{1,0:T(8,128)(2,1)S(1)}, bf16[512,512]{1,0:T(8,128)(2,1)S(1)}, f32[2,1024]{1,0:T(2,128)S(1)}, b...) custom-call(bf16[2,128,1024]{2,1,0:T(8,128)(2,1)} %collective-permut, ...), custom_call_target="tpu_custom_call" | custom-call | flops 2147483648 | bytes 7340032 | tf_op jit(solution)/shard_map/middle/pallas_call | solution.py:271
  96.0 5.4 %middle.5 = (bf16[512,1024]{1,0:T(8,128)(2,1)S(1)}, bf16[512,512]{1,0:T(8,128)(2,1)S(1)}, bf16[512,512]{1,0:T(8,128)(2,1)S(1)}, f32[2,1024]{1,0:T(2,128)S(1)}, b...) custom-call(bf16[2,128,1024]{2,1,0:T(8,128)(2,1)S(1)} %collective-pe, ...), custom_call_target="tpu_custom_call" | custom-call | flops 2147483648 | bytes 7340032 | tf_op jit(solution)/shard_map/middle/pallas_call | solution.py:271
  106.0 3.9 %middle.6 = (bf16[512,1024]{1,0:T(8,128)(2,1)S(1)}, bf16[512,512]{1,0:T(8,128)(2,1)S(1)}, bf16[512,512]{1,0:T(8,128)(2,1)S(1)}, f32[2,1024]{1,0:T(2,128)S(1)}, b...) custom-call(bf16[2,128,1024]{2,1,0:T(8,128)(2,1)S(1)} %collective-pe, ...), custom_call_target="tpu_custom_call" | custom-call | flops 2147483648 | bytes 7340032 | tf_op jit(solution)/shard_map/middle/pallas_call | solution.py:271
  118.1 3.2 %middle.7 = (bf16[512,1024]{1,0:T(8,128)(2,1)S(1)}, bf16[512,512]{1,0:T(8,128)(2,1)S(1)}, bf16[512,512]{1,0:T(8,128)(2,1)S(1)}, f32[2,1024]{1,0:T(2,128)S(1)}, b...) custom-call(bf16[2,128,1024]{2,1,0:T(8,128)(2,1)S(1)} %copy-done.4, ...), custom_call_target="tpu_custom_call" | custom-call | flops 2147483648 | bytes 7340032 | tf_op jit(solution)/shard_map/middle/pallas_call | solution.py:271
  125.7 4.4 %weight_grads.2 = bf16[2,512,512]{2,1,0:T(8,128)(2,1)S(1)} custom-call(s32[1]{0:T(128)} %bitcast.2.place_ref, bf16[512,1024]{1,0:T(8,128)(2,1)} %copy-done, bf16[512,1024]{1,0:T(8,128)(2,1)} %copy-done.1, bf16[512,1024]{1,0:T(8,128)(2,1)} %copy-done.2, bf16[512,1024]{1,0:T(8,128)(2,1)} %copy-done.3, ...), custom_call_target="tpu_custom_call" | custom-call | flops 2147483648 | bytes 8388608 | tf_op jit(solution)/shard_map/weight_grads/pallas_call | solution.py:212
  130.1 4.4 %weight_grads.3 = bf16[2,512,512]{2,1,0:T(8,128)(2,1)S(1)} custom-call(s32[1]{0:T(128)} %bitcast.2.place_ref, bf16[512,1024]{1,0:T(8,128)(2,1)} %copy-done, bf16[512,1024]{1,0:T(8,128)(2,1)} %copy-done.1, bf16[512,1024]{1,0:T(8,128)(2,1)} %copy-done.2, bf16[512,1024]{1,0:T(8,128)(2,1)} %copy-done.3, ...), custom_call_target="tpu_custom_call" | custom-call | flops 2147483648 | bytes 8388608 | tf_op jit(solution)/shard_map/weight_grads/pallas_call | solution.py:212
  134.8 1.8 collective-permute-start.30
  136.9 6.7 %collective-permute-start.33 = (bf16[2,128,1024]{2,1,0:T(8,128)(2,1)S(1)}, bf16[2,128,1024]{2,1,0:T(8,128)(2,1)S(1)}, u32[]{:S(2)}, u32[]{:S(2)}) collective-permute-start(bf16[2,128,1024]{2,1,0:T(8,128)(2,1)S(1)} %add.104), channel_id=1, source_target_pairs={{0,1},{1,0},{2,3},{3,2},{4,5},{5,4},{6,7},{7,6},{8,9},{9,8},{10,11... | collective-permute-start | bytes 1572872 | tf_op jit(solution)/shard_map/sums_3/ppermute | solution.py:100
  144.1 4.5 %collective-permute-done.30 = bf16[2,128,1024]{2,1,0:T(8,128)(2,1)S(1)} collective-permute-done((bf16[2,128,1024]{2,1,0:T(8,128)(2,1)S(1)}, bf16[2,128,1024]{2,1,0:T(8,128)(2,1)S(1)}, u32[]{:S(2)}, u32[]{:S(2)}) %collective-permute-start.30) | collective-permute-done | bytes 524320 | tf_op jit(solution)/shard_map/sums_2_2/ppermute | solution.py:100
  148.6 15.8 %collective-permute-done.33 = bf16[2,128,1024]{2,1,0:T(8,128)(2,1)S(1)} collective-permute-done((bf16[2,128,1024]{2,1,0:T(8,128)(2,1)S(1)}, bf16[2,128,1024]{2,1,0:T(8,128)(2,1)S(1)}, u32[]{:S(2)}, u32[]{:S(2)}) %collective-permute-start.33) | collective-permute-done | bytes 524320 | tf_op jit(solution)/shard_map/sums_3/ppermute | solution.py:100
  165.4 3.3 %collective-permute-start.35 = (bf16[2,128,1024]{2,1,0:T(8,128)(2,1)S(1)}, bf16[2,128,1024]{2,1,0:T(8,128)(2,1)S(1)}, u32[]{:S(2)}, u32[]{:S(2)}) collective-permute-start(bf16[2,128,1024]{2,1,0:T(8,128)(2,1)S(1)} %add_convert_fusion), channel_id=1, source_target_pairs={{0,2},{1,3},{2,0},{3,1},{4,6},{5,7},{6,4},{7,5},{8,10},{9,11},{10,... | collective-permute-start | bytes 1572872 | tf_op jit(solution)/shard_map/sums_2/ppermute | solution.py:100
  170.9 19.3 %collective-permute-done.36 = bf16[512,512]{1,0:T(8,128)(2,1)S(1)} collective-permute-done((bf16[512,512]{1,0:T(8,128)(2,1)S(1)}, bf16[512,512]{1,0:T(8,128)(2,1)S(1)}, u32[]{:S(2)}, u32[]{:S(2)}) %collective-permute-start.36) | collective-permute-done | bytes 524320 | tf_op jit(solution)/shard_map/grads_1/ppermute | solution.py:100
  192.5 21.4 %collective-permute-done.34 = bf16[2,128,1024]{2,1,0:T(8,128)(2,1)S(1)} collective-permute-done((bf16[2,128,1024]{2,1,0:T(8,128)(2,1)S(1)}, bf16[2,128,1024]{2,1,0:T(8,128)(2,1)S(1)}, u32[]{:S(2)}, u32[]{:S(2)}) %collective-permute-start.34) | collective-permute-done | bytes 524320 | tf_op jit(solution)/shard_map/sums_1/ppermute | solution.py:100
  215.2 2.4 %collective-permute-done.39 = f32[2,1024]{1,0:T(2,128)S(1)} collective-permute-done((f32[2,1024]{1,0:T(2,128)S(1)}, f32[2,1024]{1,0:T(2,128)S(1)}, u32[]{:S(2)}, u32[]{:S(2)}) %collective-permute-start.39) | collective-permute-done | bytes 8224 | tf_op jit(solution)/shard_map/stats/ppermute | solution.py:100
  218.8 4.5 %collective-permute-done.41 = f32[2,1024]{1,0:T(2,128)S(1)} collective-permute-done((f32[2,1024]{1,0:T(2,128)S(1)}, f32[2,1024]{1,0:T(2,128)S(1)}, u32[]{:S(2)}, u32[]{:S(2)}) %collective-permute-start.41) | collective-permute-done | bytes 8224 | tf_op jit(solution)/shard_map/stats/ppermute | solution.py:100
  224.5 2.5 %collective-permute-done.42 = f32[2,1024]{1,0:T(2,128)S(1)} collective-permute-done((f32[2,1024]{1,0:T(2,128)S(1)}, f32[2,1024]{1,0:T(2,128)S(1)}, u32[]{:S(2)}, u32[]{:S(2)}) %collective-permute-start.42) | collective-permute-done | bytes 8224 | tf_op jit(solution)/shard_map/stats/ppermute | solution.py:100
  (208 shorter events, 45.1 us)
Async XLA Ops:
  3.5 15.1 %collective-permute-start.2 = (bf16[2,128,1024]{2,1,0:T(8,128)(2,1)}, bf16[2,128,1024]{2,1,0:T(8,128)(2,1)S(1)}, u32[]{:S(2)}, u32[]{:S(2)}) collective-permute-start(bf16[2,128,1024]{2,1,0:T(8,128)(2,1)} %get-tuple-element.100.refs_0_.refs_16_), channel_id=1, source_target_pairs={{0,8},{4,12},{8,0},{12,4},{1,9},{5,13},{9,1},{13,5},{2,10},{6,14},... | collective-permute-start | bytes 1572872 | tf_op jit(solution)/shard_map/tokens_0_2/ppermute | solution.py:100
  6.5 23.5 %collective-permute-start = (bf16[2,128,1024]{2,1,0:T(8,128)(2,1)}, bf16[2,128,1024]{2,1,0:T(8,128)(2,1)S(1)}, u32[]{:S(2)}, u32[]{:S(2)}) collective-permute-start(bf16[2,128,1024]{2,1,0:T(8,128)(2,1)} %get-tuple-element.100.refs_0_.refs_16_), channel_id=1, source_target_pairs={{0,1},{1,0},{2,3},{3,2},{4,5},{5,4},{6,7},{7,6},{8,9},{9,8},{10,11... | collective-permute-start | bytes 1572872 | tf_op jit(solution)/shard_map/tokens_1/ppermute | solution.py:100
  8.0 22.3 %collective-permute-start.4 = (bf16[2,128,1024]{2,1,0:T(8,128)(2,1)}, bf16[2,128,1024]{2,1,0:T(8,128)(2,1)S(1)}, u32[]{:S(2)}, u32[]{:S(2)}) collective-permute-start(bf16[2,128,1024]{2,1,0:T(8,128)(2,1)} %get-tuple-element.100.refs_0_.refs_16_), channel_id=1, source_target_pairs={{0,4},{4,0},{8,12},{12,8},{1,5},{5,1},{9,13},{13,9},{2,6},{6,2},{1... | collective-permute-start | bytes 1572872 | tf_op jit(solution)/shard_map/tokens_0_1/ppermute | solution.py:100
  8.0 26.8 %collective-permute-start.1 = (bf16[2,128,1024]{2,1,0:T(8,128)(2,1)}, bf16[2,128,1024]{2,1,0:T(8,128)(2,1)S(1)}, u32[]{:S(2)}, u32[]{:S(2)}) collective-permute-start(bf16[2,128,1024]{2,1,0:T(8,128)(2,1)} %get-tuple-element.100.refs_0_.refs_16_), channel_id=1, source_target_pairs={{0,2},{1,3},{2,0},{3,1},{4,6},{5,7},{6,4},{7,5},{8,10},{9,11},{10,... | collective-permute-start | bytes 1572872 | tf_op jit(solution)/shard_map/tokens_2/ppermute | solution.py:100
  18.6 20.2 %collective-permute-start.5 = (bf16[2,128,1024]{2,1,0:T(8,128)(2,1)S(1)}, bf16[2,128,1024]{2,1,0:T(8,128)(2,1)S(1)}, u32[]{:S(2)}, u32[]{:S(2)}) collective-permute-start(bf16[2,128,1024]{2,1,0:T(8,128)(2,1)S(1)} %collective-permute-done.2.refs_2_.refs_18_), channel_id=1, source_target_pairs={{0,4},{4,0},{8,12},{12,8},{1,5},{5,1},{9,13},{13,9},{2,6},{6,2},{1... | collective-permute-start | bytes 1572872 | tf_op jit(solution)/shard_map/tokens_0_3/ppermute | solution.py:100
  29.9 12.5 %collective-permute-start.8 = (bf16[2,128,1024]{2,1,0:T(8,128)(2,1)S(1)}, bf16[2,128,1024]{2,1,0:T(8,128)(2,1)S(1)}, u32[]{:S(2)}, u32[]{:S(2)}) collective-permute-start(bf16[2,128,1024]{2,1,0:T(8,128)(2,1)S(1)} %collective-permute-done.refs_0_.refs_12_), channel_id=1, source_target_pairs={{0,8},{4,12},{8,0},{12,4},{1,9},{5,13},{9,1},{13,5},{2,10},{6,14},... | collective-permute-start | bytes 1572872 | tf_op jit(solution)/shard_map/tokens_1_2/ppermute | solution.py:100
  38.8 18.1 %collective-permute-start.6 = (bf16[2,128,1024]{2,1,0:T(8,128)(2,1)S(1)}, bf16[2,128,1024]{2,1,0:T(8,128)(2,1)}, u32[]{:S(2)}, u32[]{:S(2)}) collective-permute-start(bf16[2,128,1024]{2,1,0:T(8,128)(2,1)S(1)} %collective-permute-done.1.refs_0_.refs_8_), channel_id=1, source_target_pairs={{0,1},{1,0},{2,3},{3,2},{4,5},{5,4},{6,7},{7,6},{8,9},{9,8},{10,11... | collective-permute-start | bytes 1572872 | tf_op jit(solution)/shard_map/tokens_3/ppermute | solution.py:100
  42.4 14.5 %collective-permute-start.9 = (bf16[2,128,1024]{2,1,0:T(8,128)(2,1)S(1)}, bf16[2,128,1024]{2,1,0:T(8,128)(2,1)}, u32[]{:S(2)}, u32[]{:S(2)}) collective-permute-start(bf16[2,128,1024]{2,1,0:T(8,128)(2,1)S(1)} %collective-permute-done.1.refs_0_.refs_8_), channel_id=1, source_target_pairs={{0,8},{4,12},{8,0},{12,4},{1,9},{5,13},{9,1},{13,5},{2,10},{6,14},... | collective-permute-start | bytes 1572872 | tf_op jit(solution)/shard_map/tokens_2_2/ppermute | solution.py:100
  43.1 11.6 %collective-permute-start.10 = (bf16[256,512]{1,0:T(8,128)(2,1)}, bf16[256,512]{1,0:T(8,128)(2,1)S(1)}, u32[]{:S(2)}, u32[]{:S(2)}) collective-permute-start(bf16[256,512]{1,0:T(8,128)(2,1)} %get-tuple-element.79), channel_id=1, source_target_pairs={{0,2},{1,3},{2,0},{3,1},{4,6},{5,7},{6,4},{7,5},{8,10},{9,11},{10,... | collective-permute-start | bytes 786440 | tf_op jit(solution)/shard_map/weights_2/ppermute | solution.py:100
  43.9 26.7 %collective-permute-start.16 = (bf16[2,128,1024]{2,1,0:T(8,128)(2,1)S(1)}, bf16[2,128,1024]{2,1,0:T(8,128)(2,1)S(1)}, u32[]{:S(2)}, u32[]{:S(2)}) collective-permute-start(bf16[2,128,1024]{2,1,0:T(8,128)(2,1)S(1)} %collective-permute-done.refs_0_.refs_12_), channel_id=1, source_target_pairs={{0,4},{4,0},{8,12},{12,8},{1,5},{5,1},{9,13},{13,9},{2,6},{6,2},{1... | collective-permute-start | bytes 1572872 | tf_op jit(solution)/shard_map/tokens_1_1/ppermute | solution.py:100
  56.9 14.6 %collective-permute-start.11 = (bf16[2,128,1024]{2,1,0:T(8,128)(2,1)}, bf16[2,128,1024]{2,1,0:T(8,128)(2,1)}, u32[]{:S(2)}, u32[]{:S(2)}) collective-permute-start(bf16[2,128,1024]{2,1,0:T(8,128)(2,1)} %collective-permute-done.6.refs_0_.refs_4_), channel_id=1, source_target_pairs={{0,8},{4,12},{8,0},{12,4},{1,9},{5,13},{9,1},{13,5},{2,10},{6,14},... | collective-permute-start | bytes 1572872 | tf_op jit(solution)/shard_map/tokens_3_2/ppermute | solution.py:100
  60.0 15.4 %collective-permute-start.17 = (bf16[2,128,1024]{2,1,0:T(8,128)(2,1)S(1)}, bf16[2,128,1024]{2,1,0:T(8,128)(2,1)S(1)}, u32[]{:S(2)}, u32[]{:S(2)}) collective-permute-start(bf16[2,128,1024]{2,1,0:T(8,128)(2,1)S(1)} %collective-permute-done.8.refs_2_.refs_14_), channel_id=1, source_target_pairs={{0,4},{4,0},{8,12},{12,8},{1,5},{5,1},{9,13},{13,9},{2,6},{6,2},{1... | collective-permute-start | bytes 1572872 | tf_op jit(solution)/shard_map/tokens_1_3/ppermute | solution.py:100
  71.5 14.1 %collective-permute-start.7 = (bf16[2,128,1024]{2,1,0:T(8,128)(2,1)}, bf16[2,128,1024]{2,1,0:T(8,128)(2,1)}, u32[]{:S(2)}, u32[]{:S(2)}) collective-permute-start(bf16[2,128,1024]{2,1,0:T(8,128)(2,1)} %collective-permute-done.6.refs_0_.refs_4_), channel_id=1, source_target_pairs={{0,4},{4,0},{8,12},{12,8},{1,5},{5,1},{9,13},{13,9},{2,6},{6,2},{1... | collective-permute-start | bytes 1572872 | tf_op jit(solution)/shard_map/tokens_3_1/ppermute | solution.py:100
  71.5 14.1 %collective-permute-start.12 = (bf16[2,128,1024]{2,1,0:T(8,128)(2,1)}, bf16[2,128,1024]{2,1,0:T(8,128)(2,1)}, u32[]{:S(2)}, u32[]{:S(2)}) collective-permute-start(bf16[2,128,1024]{2,1,0:T(8,128)(2,1)} %collective-permute-done.11.refs_2_.refs_6_), channel_id=1, source_target_pairs={{0,4},{4,0},{8,12},{12,8},{1,5},{5,1},{9,13},{13,9},{2,6},{6,2},{1... | collective-permute-start | bytes 1572872 | tf_op jit(solution)/shard_map/tokens_3_3/ppermute | solution.py:100
  76.7 19.3 %collective-permute-start.19 = (bf16[2,128,1024]{2,1,0:T(8,128)(2,1)S(1)}, bf16[2,128,1024]{2,1,0:T(8,128)(2,1)}, u32[]{:S(2)}, u32[]{:S(2)}) collective-permute-start(bf16[2,128,1024]{2,1,0:T(8,128)(2,1)S(1)} %collective-permute-done.1.refs_0_.refs_8_), channel_id=1, source_target_pairs={{0,4},{4,0},{8,12},{12,8},{1,5},{5,1},{9,13},{13,9},{2,6},{6,2},{1... | collective-permute-start | bytes 1572872 | tf_op jit(solution)/shard_map/tokens_2_1/ppermute | solution.py:100
  76.7 19.3 %collective-permute-start.20 = (bf16[2,128,1024]{2,1,0:T(8,128)(2,1)}, bf16[2,128,1024]{2,1,0:T(8,128)(2,1)}, u32[]{:S(2)}, u32[]{:S(2)}) collective-permute-start(bf16[2,128,1024]{2,1,0:T(8,128)(2,1)} %collective-permute-done.9.refs_2_.refs_10_), channel_id=1, source_target_pairs={{0,4},{4,0},{8,12},{12,8},{1,5},{5,1},{9,13},{13,9},{2,6},{6,2},{1... | collective-permute-start | bytes 1572872 | tf_op jit(solution)/shard_map/tokens_2_3/ppermute | solution.py:100
  95.5 9.5 %collective-permute-start.21 = (bf16[2,128,1024]{2,1,0:T(8,128)(2,1)S(1)}, bf16[2,128,1024]{2,1,0:T(8,128)(2,1)S(1)}, u32[]{:S(2)}, u32[]{:S(2)}) collective-permute-start(bf16[2,128,1024]{2,1,0:T(8,128)(2,1)S(1)} %get-tuple-element.91), channel_id=1, source_target_pairs={{0,4},{4,0},{8,12},{12,8},{1,5},{5,1},{9,13},{13,9},{2,6},{6,2},{1... | collective-permute-start | bytes 1572872 | tf_op jit(solution)/shard_map/sums_3_1/ppermute | solution.py:100
  103.1 11.4 %collective-permute-start.24 = (bf16[2,128,1024]{2,1,0:T(8,128)(2,1)}, bf16[2,128,1024]{2,1,0:T(8,128)(2,1)}, u32[]{:S(2)}, u32[]{:S(2)}) collective-permute-start(bf16[2,128,1024]{2,1,0:T(8,128)(2,1)} %get-tuple-element.99), channel_id=1, source_target_pairs={{0,4},{4,0},{8,12},{12,8},{1,5},{5,1},{9,13},{13,9},{2,6},{6,2},{1... | collective-permute-start | bytes 1572872 | tf_op jit(solution)/shard_map/sums_2_3/ppermute | solution.py:100
  103.2 13.0 %collective-permute-start.23 = (bf16[2,128,1024]{2,1,0:T(8,128)(2,1)}, bf16[2,128,1024]{2,1,0:T(8,128)(2,1)}, u32[]{:S(2)}, u32[]{:S(2)}) collective-permute-start(bf16[2,128,1024]{2,1,0:T(8,128)(2,1)} %get-tuple-element.97), channel_id=1, source_target_pairs={{0,4},{4,0},{8,12},{12,8},{1,5},{5,1},{9,13},{13,9},{2,6},{6,2},{1... | collective-permute-start | bytes 1572872 | tf_op jit(solution)/shard_map/sums_2_1/ppermute | solution.py:100
  114.1 10.3 %collective-permute-start.28 = (bf16[2,128,1024]{2,1,0:T(8,128)(2,1)}, bf16[2,128,1024]{2,1,0:T(8,128)(2,1)}, u32[]{:S(2)}, u32[]{:S(2)}) collective-permute-start(bf16[2,128,1024]{2,1,0:T(8,128)(2,1)} %get-tuple-element.108), channel_id=1, source_target_pairs={{0,4},{4,0},{8,12},{12,8},{1,5},{5,1},{9,13},{13,9},{2,6},{6,2},{1... | collective-permute-start | bytes 1572872 | tf_op jit(solution)/shard_map/sums_1_1/ppermute | solution.py:100
  117.7 17.1 %collective-permute-start.29 = (bf16[2,128,1024]{2,1,0:T(8,128)(2,1)S(1)}, bf16[2,128,1024]{2,1,0:T(8,128)(2,1)S(1)}, u32[]{:S(2)}, u32[]{:S(2)}) collective-permute-start(bf16[2,128,1024]{2,1,0:T(8,128)(2,1)S(1)} %copy-done.43), channel_id=1, source_target_pairs={{0,8},{4,12},{8,0},{12,4},{1,9},{5,13},{9,1},{13,5},{2,10},{6,14},... | collective-permute-start | bytes 1572872 | tf_op jit(solution)/shard_map/sums_3_2/ppermute | solution.py:100
  122.3 42.7 %collective-permute-start.26 = (bf16[2,128,1024]{2,1,0:T(8,128)(2,1)S(1)}, bf16[2,128,1024]{2,1,0:T(8,128)(2,1)S(1)}, u32[]{:S(2)}, u32[]{:S(2)}) collective-permute-start(bf16[2,128,1024]{2,1,0:T(8,128)(2,1)S(1)} %get-tuple-element.104), channel_id=1, source_target_pairs={{0,4},{4,0},{8,12},{12,8},{1,5},{5,1},{9,13},{13,9},{2,6},{6,2},{1... | collective-permute-start | bytes 1572872 | tf_op jit(solution)/shard_map/sums_0_3/ppermute | solution.py:100
  122.4 42.8 %collective-permute-start.25 = (bf16[2,128,1024]{2,1,0:T(8,128)(2,1)S(1)}, bf16[2,128,1024]{2,1,0:T(8,128)(2,1)S(1)}, u32[]{:S(2)}, u32[]{:S(2)}) collective-permute-start(bf16[2,128,1024]{2,1,0:T(8,128)(2,1)S(1)} %get-tuple-element.102), channel_id=1, source_target_pairs={{0,4},{4,0},{8,12},{12,8},{1,5},{5,1},{9,13},{13,9},{2,6},{6,2},{1... | collective-permute-start | bytes 1572872 | tf_op jit(solution)/shard_map/sums_0_1/ppermute | solution.py:100
  134.8 13.8 %collective-permute-start.30 = (bf16[2,128,1024]{2,1,0:T(8,128)(2,1)S(1)}, bf16[2,128,1024]{2,1,0:T(8,128)(2,1)S(1)}, u32[]{:S(2)}, u32[]{:S(2)}) collective-permute-start(bf16[2,128,1024]{2,1,0:T(8,128)(2,1)S(1)} %add.99), channel_id=1, source_target_pairs={{0,8},{4,12},{8,0},{12,4},{1,9},{5,13},{9,1},{13,5},{2,10},{6,14},... | collective-permute-start | bytes 1572872 | tf_op jit(solution)/shard_map/sums_2_2/ppermute | solution.py:100
  136.9 27.5 %collective-permute-start.33 = (bf16[2,128,1024]{2,1,0:T(8,128)(2,1)S(1)}, bf16[2,128,1024]{2,1,0:T(8,128)(2,1)S(1)}, u32[]{:S(2)}, u32[]{:S(2)}) collective-permute-start(bf16[2,128,1024]{2,1,0:T(8,128)(2,1)S(1)} %add.104), channel_id=1, source_target_pairs={{0,1},{1,0},{2,3},{3,2},{4,5},{5,4},{6,7},{7,6},{8,9},{9,8},{10,11... | collective-permute-start | bytes 1572872 | tf_op jit(solution)/shard_map/sums_3/ppermute | solution.py:100
  143.6 26.2 %collective-permute-start.37 = (bf16[512,512]{1,0:T(8,128)(2,1)S(1)}, bf16[512,512]{1,0:T(8,128)(2,1)S(1)}, u32[]{:S(2)}, u32[]{:S(2)}) collective-permute-start(bf16[512,512]{1,0:T(8,128)(2,1)S(1)} %get-tuple-element.156), channel_id=1, source_target_pairs={{0,2},{1,3},{2,0},{3,1},{4,6},{5,7},{6,4},{7,5},{8,10},{9,11},{10,... | collective-permute-start | bytes 1572872 | tf_op jit(solution)/shard_map/grads_2/ppermute | solution.py:100
  164.7 25.6 %collective-permute-start.36 = (bf16[512,512]{1,0:T(8,128)(2,1)S(1)}, bf16[512,512]{1,0:T(8,128)(2,1)S(1)}, u32[]{:S(2)}, u32[]{:S(2)}) collective-permute-start(bf16[512,512]{1,0:T(8,128)(2,1)S(1)} %slice_bitcast_fusion.2), channel_id=1, source_target_pairs={{0,1},{1,0},{2,3},{3,2},{4,5},{5,4},{6,7},{7,6},{8,9},{9,8},{10,11... | collective-permute-start | bytes 1572872 | tf_op jit(solution)/shard_map/grads_1/ppermute | solution.py:100
  165.4 49.5 %collective-permute-start.35 = (bf16[2,128,1024]{2,1,0:T(8,128)(2,1)S(1)}, bf16[2,128,1024]{2,1,0:T(8,128)(2,1)S(1)}, u32[]{:S(2)}, u32[]{:S(2)}) collective-permute-start(bf16[2,128,1024]{2,1,0:T(8,128)(2,1)S(1)} %add_convert_fusion), channel_id=1, source_target_pairs={{0,2},{1,3},{2,0},{3,1},{4,6},{5,7},{6,4},{7,5},{8,10},{9,11},{10,... | collective-permute-start | bytes 1572872 | tf_op jit(solution)/shard_map/sums_2/ppermute | solution.py:100
  169.8 20.6 %collective-permute-start.31 = (bf16[2,128,1024]{2,1,0:T(8,128)(2,1)S(1)}, bf16[2,128,1024]{2,1,0:T(8,128)(2,1)S(1)}, u32[]{:S(2)}, u32[]{:S(2)}) collective-permute-start(bf16[2,128,1024]{2,1,0:T(8,128)(2,1)S(1)} %add.102), channel_id=1, source_target_pairs={{0,8},{4,12},{8,0},{12,4},{1,9},{5,13},{9,1},{13,5},{2,10},{6,14},... | collective-permute-start | bytes 1572872 | tf_op jit(solution)/shard_map/sums_1_2/ppermute | solution.py:100
  170.6 57.1 %collective-permute-start.38 = (bf16[512,512]{1,0:T(8,128)(2,1)S(1)}, bf16[512,512]{1,0:T(8,128)(2,1)S(1)}, u32[]{:S(2)}, u32[]{:S(2)}) collective-permute-start(bf16[512,512]{1,0:T(8,128)(2,1)S(1)} %get-tuple-element.132), channel_id=1, source_target_pairs={{0,3},{1,2},{2,1},{3,0},{4,7},{5,6},{6,5},{7,4},{8,11},{9,10},{10,... | collective-permute-start | bytes 1572872 | tf_op jit(solution)/shard_map/grads_3/ppermute | solution.py:100
  190.7 23.3 %collective-permute-start.34 = (bf16[2,128,1024]{2,1,0:T(8,128)(2,1)S(1)}, bf16[2,128,1024]{2,1,0:T(8,128)(2,1)S(1)}, u32[]{:S(2)}, u32[]{:S(2)}) collective-permute-start(bf16[2,128,1024]{2,1,0:T(8,128)(2,1)S(1)} %add.106), channel_id=1, source_target_pairs={{0,1},{1,0},{2,3},{3,2},{4,5},{5,4},{6,7},{7,6},{8,9},{9,8},{10,11... | collective-permute-start | bytes 1572872 | tf_op jit(solution)/shard_map/sums_1/ppermute | solution.py:100
  190.7 24.1 %collective-permute-start.32 = (bf16[2,128,1024]{2,1,0:T(8,128)(2,1)S(1)}, bf16[2,128,1024]{2,1,0:T(8,128)(2,1)S(1)}, u32[]{:S(2)}, u32[]{:S(2)}) collective-permute-start(bf16[2,128,1024]{2,1,0:T(8,128)(2,1)S(1)} %add.101), channel_id=1, source_target_pairs={{0,8},{4,12},{8,0},{12,4},{1,9},{5,13},{9,1},{13,5},{2,10},{6,14},... | collective-permute-start | bytes 1572872 | tf_op jit(solution)/shard_map/sums_0_2/ppermute | solution.py:100
  (62 other events, 623.5 us)

commit v5 on v4

--- a/solution.py
+++ b/solution.py
@@ -104,15 +104,13 @@
     return [1 << b for b in reversed(range(size.bit_length() - 1))]
 
 
-def pack(first_out, grad_second, w_up, w_down, mates):
+def pack_weights(w_up, w_down, mates):
     n_dp = lax.axis_size("dp")
     depth, units = w_up.shape[0], w_up.shape[1] // n_dp
     up_rows, down_rows, strips = depth // mates, units // mates, units // depth
     strip_rows = down_rows // strips
 
-    def kernel(first_ref, grad_ref, up_ref, down_ref, rows_ref, *sends):
-        rows_ref[0] = first_ref[...]
-        rows_ref[1] = grad_ref[...]
+    def kernel(up_ref, down_ref, *sends):
         place, mate = lax.axis_index("dp"), lax.rem(lax.axis_index("groups"), mates)
         for k in range(1, n_dp):
             first = pl.multiple_of((place ^ k) * units, units)
@@ -125,15 +123,12 @@
 
     return pl.pallas_call(
         kernel,
-        out_shape=[jax.ShapeDtypeStruct((2, *first_out.shape), first_out.dtype)]
-        + [jax.ShapeDtypeStruct((2 * up_rows, units), w_up.dtype)] * (n_dp - 1),
-        in_specs=[pl.BlockSpec(memory_space=pltpu.VMEM)] * 4,
-        out_specs=[pl.BlockSpec(memory_space=pltpu.VMEM)] * n_dp,
-        cost_estimate=pl.CostEstimate(
-            flops=0, bytes_accessed=8 * (w_up.size + first_out.size), transcendentals=0
-        ),
-        name="pack",
-    )(first_out, grad_second, w_up, w_down)
+        out_shape=[jax.ShapeDtypeStruct((2 * up_rows, units), w_up.dtype)] * (n_dp - 1),
+        in_specs=[pl.BlockSpec(memory_space=pltpu.VMEM)] * 2,
+        out_specs=[pl.BlockSpec(memory_space=pltpu.VMEM)] * (n_dp - 1),
+        cost_estimate=pl.CostEstimate(flops=0, bytes_accessed=8 * w_up.size, transcendentals=0),
+        name="pack_weights",
+    )(w_up, w_down)
 
 
 def unpack_weights(w_up, w_down, got, mates):
@@ -190,104 +185,119 @@
     )(w_up, w_down, *[piece for pieces in got for piece in pieces])
 
 
-def weight_grads(place, first, count, normeds, grads, hiddens, grad_pres, n_dp):
-    n_chunks, n_pieces = len(normeds), len(grads)
-    (rows, width), units = normeds[0].shape, hiddens[0].shape[1]
-    piece_rows, depth = grads[0].shape[1], width // n_dp
-    strips = units // depth
-
-    def kernel(place_ref, *refs):
-        out = refs[-1]
-        norm = jnp.concatenate([ref[...] for ref in refs[:n_chunks]], axis=0)
-        refs = refs[n_chunks:]
-        grad = jnp.concatenate([ref[0] for ref in refs[:n_pieces]], axis=0)
-        refs = refs[n_pieces:]
-        hid = jnp.concatenate([ref[...] for ref in refs[:n_chunks]], axis=0)
-        pre = jnp.concatenate([ref[...] for ref in refs[n_chunks:-1]], axis=0)
-        out[0, :depth, :] = contract_tokens(norm, pre).astype(out.dtype)
-        down = contract_tokens(hid, grad).astype(out.dtype)
-        for c in range(strips):
-            out[0, depth:, c * depth : (c + 1) * depth] = down[c * depth : (c + 1) * depth]
-
-    return pl.pallas_call(
-        kernel,
-        out_shape=jax.ShapeDtypeStruct((count, 2 * depth, units), jnp.bfloat16),
-        grid_spec=pltpu.PrefetchScalarGridSpec(
-            num_scalar_prefetch=1,
-            grid=(count,),
-            in_specs=[pl.BlockSpec((rows, depth), lambda k, p: (0, p[0] ^ (first + k)))] * n_chunks
-            + [pl.BlockSpec((1, piece_rows, depth), lambda k, p: (1, 0, p[0] ^ (first + k)))] * n_pieces
-            + [pl.BlockSpec((rows, units), lambda k, p: (0, 0))] * (2 * n_chunks),
-            out_specs=pl.BlockSpec((1, 2 * depth, units), lambda k, p: (k, 0, 0)),
-        ),
-        compiler_params=pltpu.CompilerParams(vmem_limit_bytes=40 * 1024 * 1024),
-        cost_estimate=pl.CostEstimate(
-            flops=4 * n_chunks * rows * depth * count * units,
-            bytes_accessed=4 * n_chunks * rows * (depth * count + units),
-            transcendentals=0,
-        ),
-        name="weight_grads",
-    )(place.reshape(1), *normeds, *grads, *hiddens, *grad_pres)
-
-
-def middle(pieces, up, down, gain, bias):
-    (_, piece_rows, width), units, n = pieces[0].shape, up.shape[1], len(pieces)
-    rows = n * piece_rows
+def core(chunks, up, down, gain, bias, n_dp):
+    n_chunks, n = len(chunks), len(chunks[0])
+    (_, piece_rows, width), units = chunks[0][0].shape, up.shape[1]
+    depth = width // n_dp
+    strips, pair = units // depth, 2 * piece_rows
     slope = (2.0 / math.pi) ** 0.5
+    dtype = up.dtype
 
     def kernel(*refs):
-        toks, (up_ref, down_ref, gain_ref, bias_ref) = refs[:n], refs[n : n + 4]
-        norm_ref, hid_ref, pre_ref, stat_ref = refs[n + 4 : n + 8]
-        parts = refs[n + 8 :]
-        half_n = max(n // 2, 1)
+        toks, refs = refs[: n_chunks * n], refs[n_chunks * n :]
+        (up_hbm, down_hbm, gain_ref, bias_ref), refs = refs[:4], refs[4:]
+        outs, blocks, stat_ref = refs[: 2 * n_chunks], refs[2 * n_chunks : 2 * n_chunks + n_dp], refs[2 * n_chunks + n_dp]
+        tok, norm, hid, pre, part, block, up_ref, down_ref, in_sem, w_sem, out_sem, b_sem = refs[2 * n_chunks + n_dp + 1 :]
+        place = lax.axis_index("dp")
+        weights = [
+            pltpu.make_async_copy(up_hbm, up_ref, w_sem.at[0]),
+            pltpu.make_async_copy(down_hbm, down_ref, w_sem.at[1]),
+        ]
+        reads = [pltpu.make_async_copy(ref, tok.at[i], in_sem.at[i]) for i, ref in enumerate(toks)]
+        for one in weights[:1] + reads[:n] + weights[1:] + reads[n:]:
+            one.start()
         stat_ref[...] = jnp.zeros_like(stat_ref)
-        for first in range(0, n, half_n):
-            here = range(first, first + half_n)
-            span = slice(first * piece_rows, (first + half_n) * piece_rows)
-            values = jnp.concatenate([toks[j][0] for j in here], axis=0).astype(jnp.float32)
-            centred = values - jnp.mean(values, axis=-1, keepdims=True)
-            inv_std = lax.rsqrt(jnp.mean(centred * centred, axis=-1, keepdims=True) + epsilon)
-            standard = centred * inv_std
-            normed = (standard * gain_ref[...] + bias_ref[...]).astype(jnp.bfloat16)
-            grads = jnp.concatenate([toks[j][1] for j in here], axis=0)
-            x = jnp.dot(normed, up_ref[...], preferred_element_type=jnp.float32)
-            gate = jnp.tanh(slope * (x + 0.044715 * (x * x * x)))
-            half = 0.5 + 0.5 * gate
-            hidden = (x * half).astype(jnp.bfloat16)
-            rise = half + (0.5 * slope) * x * (1.0 - gate * gate) * (1.0 + (3 * 0.044715) * (x * x))
-            grad_pre = (contract_last(grads, down_ref[...]) * rise).astype(jnp.bfloat16)
-            norm_ref[span, :] = normed
-            hid_ref[span, :] = hidden
-            pre_ref[span, :] = grad_pre
-            branch = jnp.dot(hidden, down_ref[...], preferred_element_type=jnp.float32)
-            grad_normed = contract_last(grad_pre, up_ref[...])
-            stat_ref[0:1, :] += jnp.sum(grad_normed * standard, axis=0, keepdims=True)
-            stat_ref[1:2, :] += jnp.sum(grad_normed, axis=0, keepdims=True)
-            for j in here:
-                own = slice((j - first) * piece_rows, (j - first + 1) * piece_rows)
-                parts[j][0] = branch[own].astype(jnp.bfloat16)
-                parts[j][1] = grad_normed[own].astype(jnp.bfloat16)
-
+        writes = []
+        for i in range(n_chunks):
+            for one in reads[i * n : (i + 1) * n] + (weights if i == 0 else []):
+                one.wait()
+
+            @pl.loop(0, n // 2)
+            def _(t):
+                at = i * n + 2 * t
+                span = pl.ds(pl.multiple_of(at * piece_rows, pair), pair)
+                values = tok[pl.ds(at, 2), 0].reshape(pair, width).astype(jnp.float32)
+                centred = values - jnp.mean(values, axis=-1, keepdims=True)
+                inv_std = lax.rsqrt(jnp.mean(centred * centred, axis=-1, keepdims=True) + epsilon)
+                standard = centred * inv_std
+                normed = (standard * gain_ref[...] + bias_ref[...]).astype(dtype)
+                norm[span, :] = normed
+                x = jnp.dot(normed, up_ref[...], preferred_element_type=jnp.float32)
+                gate = jnp.tanh(slope * (x + 0.044715 * (x * x * x)))
+                half = 0.5 + 0.5 * gate
+                hidden = (x * half).astype(dtype)
+                hid[span, :] = hidden
+                rise = half + (0.5 * slope) * x * (1.0 - gate * gate) * (1.0 + (3 * 0.044715) * (x * x))
+                grads = tok[pl.ds(at, 2), 1].reshape(pair, width)
+                grad_pre = (contract_last(grads, down_ref[...]) * rise).astype(dtype)
+                pre[span, :] = grad_pre
+                branch = jnp.dot(hidden, down_ref[...], preferred_element_type=jnp.float32)
+                grad_normed = contract_last(grad_pre, up_ref[...])
+                stat_ref[0:1, :] += jnp.sum(grad_normed * standard, axis=0, keepdims=True)
+                stat_ref[1:2, :] += jnp.sum(grad_normed, axis=0, keepdims=True)
+                for odd in range(2):
+                    own = slice(odd * piece_rows, (odd + 1) * piece_rows)
+                    part[2 * i + odd, t, 0] = branch[own].astype(dtype)
+                    part[2 * i + odd, t, 1] = grad_normed[own].astype(dtype)
+
+            for odd in (1, 0):
+                at = 2 * i + odd
+                writes.append(pltpu.make_async_copy(part.at[at], outs[at], out_sem.at[at]))
+                writes[-1].start()
+        top = bits_of(n_dp)[0]
+        for k in sorted(range(n_dp), key=lambda k: (k < top, k)):
+            columns = pl.ds(pl.multiple_of((place ^ k) * depth, depth), depth)
+            block[k, :depth, :] = contract_tokens(norm[:, columns], pre[...]).astype(dtype)
+            grads = tok[:, 1, :, columns].reshape(n_chunks * n * piece_rows, depth)
+            down_block = contract_tokens(hid[...], grads).astype(dtype)
+            for c in range(strips):
+                block[k, depth:, c * depth : (c + 1) * depth] = down_block[c * depth : (c + 1) * depth]
+            writes.append(pltpu.make_async_copy(block.at[k], blocks[k], b_sem.at[k]))
+            writes[-1].start()
+        for one in writes:
+            one.wait()
+
+    rows = n_chunks * n * piece_rows
+    half = jax.ShapeDtypeStruct((n // 2, 2, piece_rows, width), dtype)
+    far = pl.BlockSpec(memory_space=pl.ANY)
+    near = pl.BlockSpec(memory_space=pltpu.VMEM)
     out = pl.pallas_call(
         kernel,
-        out_shape=[
-            jax.ShapeDtypeStruct((rows, width), jnp.bfloat16),
-            jax.ShapeDtypeStruct((rows, units), jnp.bfloat16),
-            jax.ShapeDtypeStruct((rows, units), jnp.bfloat16),
-            jax.ShapeDtypeStruct((2, width), jnp.float32),
-        ]
-        + [jax.ShapeDtypeStruct((2, piece_rows, width), jnp.bfloat16)] * n,
-        in_specs=[pl.BlockSpec(memory_space=pltpu.VMEM)] * (n + 4),
-        out_specs=[pl.BlockSpec(memory_space=pltpu.VMEM)] * (n + 4),
-        compiler_params=pltpu.CompilerParams(vmem_limit_bytes=32 * 1024 * 1024),
+        out_shape=[half] * (2 * n_chunks)
+        + [jax.ShapeDtypeStruct((2 * depth, units), dtype)] * n_dp
+        + [jax.ShapeDtypeStruct((2, width), jnp.float32)],
+        in_specs=[far] * (n_chunks * n + 2) + [near] * 2,
+        out_specs=[far] * (2 * n_chunks + n_dp) + [near],
+        scratch_shapes=[
+            pltpu.VMEM((n_chunks * n, 2, piece_rows, width), dtype),
+            pltpu.VMEM((rows, width), dtype),
+            pltpu.VMEM((rows, units), dtype),
+            pltpu.VMEM((rows, units), dtype),
+            pltpu.VMEM((2 * n_chunks, n // 2, 2, piece_rows, width), dtype),
+            pltpu.VMEM((n_dp, 2 * depth, units), dtype),
+            pltpu.VMEM((width, units), dtype),
+            pltpu.VMEM((units, width), dtype),
+            pltpu.SemaphoreType.DMA((n_chunks * n,)),
+            pltpu.SemaphoreType.DMA((2,)),
+            pltpu.SemaphoreType.DMA((2 * n_chunks,)),
+            pltpu.SemaphoreType.DMA((n_dp,)),
+        ],
+        compiler_params=pltpu.CompilerParams(vmem_limit_bytes=56 * 1024 * 1024),
         cost_estimate=pl.CostEstimate(
-            flops=8 * rows * width * units,
-            bytes_accessed=10 * rows * width + 4 * width * units,
+            flops=10 * rows * width * units,
+            bytes_accessed=8 * rows * width + 8 * width * units,
             transcendentals=rows * units,
         ),
-        name="middle",
-    )(*pieces, up, down, gain.reshape(1, width), bias.reshape(1, width))
-    return out[0], out[1], out[2], out[3], dict(enumerate(out[4:]))
+        name="core",
+    )(
+        *[piece for chunk in chunks for piece in chunk],
+        up,
+        down,
+        gain.reshape(1, width),
+        bias.reshape(1, width),
+    )
+    halves = [out[2 * i : 2 * i + 2] for i in range(n_chunks)]
+    return halves, list(out[2 * n_chunks : -1]), out[-1]
 
 
 def after(values, *others):
@@ -304,9 +314,9 @@
     place = lax.axis_index("dp")
     top = bits_of(n_dp)[0]
 
-    own, *sends = pack(first_out, grad_second, w_up, w_down, mates)
     high, others = bits_of(n_tensor)[0], bits_of(n_tensor)[1:]
-    tokens, chunks, got = {0: own}, {}, {}
+    own = jnp.stack([first_out, grad_second])
+    tokens, chunks, got, crossed = {0: own}, {}, {}, {}
 
     def tokens_dp(k, *first):
         tokens[k] = swap(after(tokens[k & (k - 1)], *first), "dp", k & -k, f"tokens_{k}")
@@ -321,66 +331,56 @@
     def weights_dp(k, *first):
         got[k] = swap(after(sends[k - 1], *first), "dp", k, f"weights_{k}")
 
+    def weights_groups(k, *first):
+        crossed[k] = swap(after(got[k], *first), "groups", 1, f"weights_{k}")
+
     tokens_tensor(0)
-    for bit in bits_of(n_dp):
+    for bit in bits_of(n_dp)[:0:-1]:
         tokens_dp(bit)
-    tokens_tensor(1, chunks[0][high])
+    sends = pack_weights(w_up, w_down, mates)
+    tokens_dp(top, sends[0])
+    stage = [tokens[1], chunks[0][high]]
+    tokens_tensor(1, *stage)
     for bit in reversed(bits_of(n_dp)):
-        weights_dp(bit, tokens[1], chunks[0][high])
+        weights_dp(bit, *stage)
+    stage = [tokens[top], chunks[1][high], *got.values(), *chunks[0].values()]
     for k in range(2, n_dp):
         if k & (k - 1):
-            tokens_dp(k, got[1], *chunks[0].values())
-            weights_dp(k, tokens[top], got[1], chunks[1][high])
-        tokens_tensor(k, chunks[k - 1][high], got[1 if k <= top else top])
-    got = [got[k] for k in range(1, n_dp)]
-    crossed = []
-    if mates == 2:
-        for k, piece in enumerate(got, 1):
-            first = (*crossed[-1:], *chunks[k - 2].values()) if k > 1 else ()
-            crossed.append(swap(after(piece, *first), "groups", 1, f"weights_{k}"))
-    got = [got, crossed]
-    up, down = unpack_weights(w_up, w_down, got[:mates], mates)
+            tokens_dp(k, *stage)
+            weights_dp(k, *stage)
+            stage = [tokens[k], got[k], chunks[k - 1][high]]
+        if mates == 2:
+            for other in (k - 1, k):
+                if other & (other - 1) == 0 and other not in crossed:
+                    weights_groups(other, *stage)
+        tokens_tensor(k, *stage)
+    for k in range(1, n_dp):
+        if mates == 2 and k not in crossed:
+            weights_groups(k, *stage, *chunks[1].values())
+    got = [[pieces[k] for k in range(1, n_dp)] for pieces in (got, crossed)[:mates]]
+    up, down = unpack_weights(w_up, w_down, got, mates)
 
     order = sorted(chunks, reverse=True)
-    normeds, hiddens, grad_pres, all_stats, ready = [], [], [], [], []
-    for i, k in enumerate(order):
-        pieces = [chunks[k][j] for j in range(n_tensor)]
-        if i >= 1:
-            pieces[0] = after(pieces[0], hiddens[-1], *(ready[i - 2] if i >= 2 else ()))
-        normed, hidden, grad_pre, stats, parts = middle(pieces, up, down, norm_gain, norm_bias)
-        normeds.append(normed)
-        hiddens.append(hidden)
-        grad_pres.append(grad_pre)
-        all_stats.append(stats)
-        for bit in reversed(others):
-            for j in sorted((j for j in parts if j & bit), reverse=True):
-                parts[j ^ bit] = parts[j ^ bit] + swap(parts.pop(j), "tensor", bit, f"sums_{k}_{j}")
-        ready.append((parts[0], parts[high]))
-    high_came = []
-    for i, k in enumerate(order):
-        part = after(ready[i][1], ready[i][0], *high_came[:i][-1:])
-        high_came.append(swap(part, "tensor", high, f"sums_{k}_{high}"))
-    grads = [chunks[k][j] for k in order for j in range(n_tensor)]
-    grads[0] = after(grads[0], *ready[-2])
-    far = weight_grads(place, top, n_dp - top, normeds, grads, hiddens, grad_pres, n_dp)
-    grads[0] = after(grads[0], far)
-    near = weight_grads(place, 0, top, normeds, grads, hiddens, grad_pres, n_dp)
-    blocks = {k: near[k] if k < top else far[k - top] for k in range(n_dp)}
+    halves, blocks, stats = core(
+        [[chunks[k][j] for j in range(n_tensor)] for k in order], up, down, norm_gain, norm_bias, n_dp
+    )
+    blocks = dict(enumerate(blocks))
     blocks[top] = swap(blocks[top], "dp", top, f"grads_{top}")
-
-    sums, came = {}, {}
-    for i, k in enumerate(order):
-        sums[k] = ready[i][0] + after(high_came[i], far, *sums.values())
-        if i == 0 and k != top:
-            sums[k] = after(sums[k], near)
-            came[k] = swap(sums[k], "dp", k & -k, f"sums_{k}")
-            sums[k] = came[k]
+    stats = jnp.sum(lax.all_gather(stats, ("tensor", "dp")), axis=0)
+
+    sums, behind = {}, ()
+    for k, (even, odd) in zip(order, halves, strict=True):
+        part = even + swap(odd, "tensor", 1, f"sums_{k}_1")
+        for bit in reversed(bits_of(n_tensor)[:-1]):
+            send = after(part[1::2], *behind)
+            came = swap(send, "tensor", bit, f"sums_{k}_{bit}")
+            part = part[0::2] + came
+            behind = (came,)
+        sums[k] = part[0]
+    came = {}
     for bit in bits_of(n_dp)[::-1]:
-        inner = [k for k in order if k & bit and k in sums and k != bit]
-        for k in inner:
-            if k not in came:
-                came[k] = swap(sums[k], "dp", bit, f"sums_{k}")
-            del sums[k]
+        for k in [k for k in order if k & bit and k in sums and k != bit]:
+            came[k] = swap(sums.pop(k), "dp", bit, f"sums_{k}")
             sums[k ^ bit] = (sums[k ^ bit].astype(jnp.float32) + came[k]).astype(jnp.bfloat16)
     last = sums[top]
     came[top] = swap(last, "dp", top, f"sums_{top}")
@@ -395,17 +395,12 @@
             blocks[k] = swap(after(blocks[k], last), "dp", k, f"grads_{k}")
         elif k > top:
             blocks[k] = swap(after(blocks[k], blocks[top], last), "dp", k, f"grads_{k}")
-    blocks[top] = after(blocks[top], last)
+    for k in range(1, n_dp):
+        blocks[k] = after(blocks[k], last if k == top else total)
     branch, grad_normed = sums[0][0], sums[0][1]
     second_in, grad_first_in = finish_rows(
         branch, grad_normed, second_out, grad_first, first_out, norm_gain, norm_bias
     )
-
-    stats = after(sum(all_stats), blocks[top], came[1])
-    for axis in ("tensor", "dp"):
-        for bit in bits_of(lax.axis_size(axis)):
-            stats = stats + swap(stats, axis, bit, "stats")
-    blocks[n_dp - 1] = after(blocks[n_dp - 1], stats)
 
     grad_scale = (own_rows * n_tensor * n_dp) ** (-0.5)
     grad_up = jnp.zeros(w_up.shape, jnp.float32)

time: 230 us -> 251 us (1.091)
  blocking collectives: 0 us -> 45.3 us
  local copies, waits for them, and re-layouts: 16.5 us -> 6.22 us
  starting transfers between devices: 36.9 us -> 28.1 us
  waiting for transfers between devices: 131 us -> 123 us
  other arithmetic: 12.2 us -> 17.5 us
    all_gather x0 -> x1, blocking collectives: none -> 45.3 us  [gather_tokens_body(): stats = jnp.sum(lax.all_gather(stats, ('tensor', 'dp')), axis=0)]
    unnamed x102 -> x54, local copies, waits for them, and re-layouts: 15.7 us -> 3.81 us
    ppermute x43 -> x35, starting transfers between devices: 36.9 us -> 28.1 us  [swap(): lax.ppermute(values, axis, [(i, i ^ mask) for i in range(lax.axis_size(ax...]
    ppermute x43 -> x35, waiting for transfers between devices: 131 us -> 123 us  [swap(): lax.ppermute(values, axis, [(i, i ^ mask) for i in range(lax.axis_size(ax...]
    pallas_call x7 -> x2, Pallas kernels: 28.7 us -> 26.7 us  [the longest x1 24.3 us: core(): pl.pallas_call(kernel, out_shape=[half] * (2 * n_chunks) + [jax.ShapeDtyp...]
    add x14 -> x4, other arithmetic: 8.42 us -> 7.22 us  [gather_tokens_body(): part = even + swap(odd, 'tensor', 1, f'sums_{k}_1')]
  transfers between devices with their start and end apart: 43 -> 35, of which waited for: 20 -> 16; matrix products, arithmetic and copies ran while one was open for 6% -> 7% of each run, Pallas kernels for 13% -> 2%
where the time goes in v5:
time: 251 us
  waiting for transfers between devices  123 us (49%)
  blocking collectives  45.3 us (18%)
  Pallas kernels  29.7 us (12%)
  starting transfers between devices  28.1 us (11%)
  other arithmetic  17.5 us (7%)
  local copies, waits for them, and re-layouts  6.22 us (2%)
    ppermute x35, waiting for transfers between devices, swap(): lax.ppermute(values, axis, [(i, i ^ mask) for i in range(lax.axis_size(ax...  123 us
    all_gather x1, blocking collectives, gather_tokens_body(): stats = jnp.sum(lax.all_gather(stats, ('tensor', 'dp')), axis=0)  45.3 us
    ppermute x35, starting transfers between devices, swap(): lax.ppermute(values, axis, [(i, i ^ mask) for i in range(lax.axis_size(ax...  28.1 us
    pallas_call x1, Pallas kernels, core(): pl.pallas_call(kernel, out_shape=[half] * (2 * n_chunks) + [jax.ShapeDtyp...  24.3 us
    add x4, other arithmetic, gather_tokens_body(): part = even + swap(odd, 'tensor', 1, f'sums_{k}_1')  7.22 us
  transfers between devices with their start and end apart: 35, of which 16 were waited for; matrix products, arithmetic and copies ran while one was open for 7% of the time, Pallas kernels for 2%

profile of v5, /device:TPU:0, one launch (start us, length us, event | category | flops | bytes accessed | tf_op | source)
XLA Modules:
  0.0 250.8 jit_solution(9931572311431674708)
XLA Ops:
  1.7 3.0 %collective-permute-start.2 = (bf16[2,128,1024]{2,1,0:T(8,128)(2,1)S(1)}, bf16[2,128,1024]{2,1,0:T(8,128)(2,1)S(1)}, u32[]{:S(2)}, u32[]{:S(2)}) collective-permute-start(bf16[2,128,1024]{2,1,0:T(8,128)(2,1)S(1)} %pad_maximum_fusion.refs_12_), channel_id=1, source_target_pairs={{0,8},{4,12},{8,0},{12,4},{1,9},{5,13},{9,1},{13,5},{2,10},{6,14},... | collective-permute-start | bytes 1572872 | tf_op jit(solution)/shard_map/tokens_0_2/ppermute | solution.py:100
  6.3 2.5 pack_weights.1
  8.8 2.6 %collective-permute-start = (bf16[2,128,1024]{2,1,0:T(8,128)(2,1)S(1)}, bf16[2,128,1024]{2,1,0:T(8,128)(2,1)}, u32[]{:S(2)}, u32[]{:S(2)}) collective-permute-start(bf16[2,128,1024]{2,1,0:T(8,128)(2,1)S(1)} %pad_maximum_fusion.refs_12_), channel_id=1, source_target_pairs={{0,2},{1,3},{2,0},{3,1},{4,6},{5,7},{6,4},{7,5},{8,10},{9,11},{10,... | collective-permute-start | bytes 1572872 | tf_op jit(solution)/shard_map/tokens_2/ppermute | solution.py:100
  11.4 5.3 %collective-permute-done.2.refs_14_ = bf16[2,128,1024]{2,1,0:T(8,128)(2,1)S(1)} collective-permute-done((bf16[2,128,1024]{2,1,0:T(8,128)(2,1)S(1)}, bf16[2,128,1024]{2,1,0:T(8,128)(2,1)S(1)}, u32[]{:S(2)}, u32[]{:S(2)}) %collective-permute-start.2) | collective-permute-done | bytes 524320 | tf_op jit(solution)/shard_map/tokens_0_2/ppermute | solution.py:100
  16.7 10.1 %collective-permute-done.1.refs_8_ = bf16[2,128,1024]{2,1,0:T(8,128)(2,1)S(1)} collective-permute-done((bf16[2,128,1024]{2,1,0:T(8,128)(2,1)S(1)}, bf16[2,128,1024]{2,1,0:T(8,128)(2,1)S(1)}, u32[]{:S(2)}, u32[]{:S(2)}) %collective-permute-start.1) | collective-permute-done | bytes 524320 | tf_op jit(solution)/shard_map/tokens_1/ppermute | solution.py:100
  27.2 7.1 %collective-permute-done.refs_4_ = bf16[2,128,1024]{2,1,0:T(8,128)(2,1)} collective-permute-done((bf16[2,128,1024]{2,1,0:T(8,128)(2,1)S(1)}, bf16[2,128,1024]{2,1,0:T(8,128)(2,1)}, u32[]{:S(2)}, u32[]{:S(2)}) %collective-permute-start) | collective-permute-done | bytes 524320 | tf_op jit(solution)/shard_map/tokens_2/ppermute | solution.py:100
  34.3 5.2 %collective-permute-done.4.rest_0_ = bf16[256,512]{1,0:T(8,128)(2,1)S(1)} collective-permute-done((bf16[256,512]{1,0:T(8,128)(2,1)}, bf16[256,512]{1,0:T(8,128)(2,1)S(1)}, u32[]{:S(2)}, u32[]{:S(2)}) %collective-permute-start.4) | collective-permute-done | bytes 262176 | tf_op jit(solution)/shard_map/weights_1/ppermute | solution.py:100
  39.5 8.0 %collective-permute-done.5.rest_1_ = bf16[256,512]{1,0:T(8,128)(2,1)S(1)} collective-permute-done((bf16[256,512]{1,0:T(8,128)(2,1)}, bf16[256,512]{1,0:T(8,128)(2,1)S(1)}, u32[]{:S(2)}, u32[]{:S(2)}) %collective-permute-start.5) | collective-permute-done | bytes 262176 | tf_op jit(solution)/shard_map/weights_2/ppermute | solution.py:100
  48.2 2.4 collective-permute-start.10
  51.1 16.6 %collective-permute-done.10.rest_2_ = bf16[256,512]{1,0:T(8,128)(2,1)S(1)} collective-permute-done((bf16[256,512]{1,0:T(8,128)(2,1)}, bf16[256,512]{1,0:T(8,128)(2,1)S(1)}, u32[]{:S(2)}, u32[]{:S(2)}) %collective-permute-start.10) | collective-permute-done | bytes 262176 | tf_op jit(solution)/shard_map/weights_3/ppermute | solution.py:100
  67.8 1.8 collective-permute-start.12
  71.6 7.2 %collective-permute-done.19.rest_4_ = bf16[256,512]{1,0:T(8,128)(2,1)S(1)} collective-permute-done((bf16[256,512]{1,0:T(8,128)(2,1)S(1)}, bf16[256,512]{1,0:T(8,128)(2,1)S(1)}, u32[]{:S(2)}, u32[]{:S(2)}) %collective-permute-start.19) | collective-permute-done | bytes 262176 | tf_op jit(solution)/shard_map/weights_2/ppermute | solution.py:100
  79.3 1.8 collective-permute-done.12.refs_2_
  83.7 6.1 %collective-permute-done.20.rest_5_ = bf16[256,512]{1,0:T(8,128)(2,1)S(1)} collective-permute-done((bf16[256,512]{1,0:T(8,128)(2,1)S(1)}, bf16[256,512]{1,0:T(8,128)(2,1)S(1)}, u32[]{:S(2)}, u32[]{:S(2)}) %collective-permute-start.20) | collective-permute-done | bytes 262176 | tf_op jit(solution)/shard_map/weights_3/ppermute | solution.py:100
  90.6 3.0 %unpack_weights.1 = (bf16[1024,512]{1,0:T(8,128)(2,1)}, bf16[512,1024]{1,0:T(8,128)(2,1)}) custom-call(bf16[256,2048]{1,0:T(8,128)(2,1)} %up_ref.3, bf16[2048,256]{1,0:T(8,128)(2,1)} %down_ref.3, bf16[256,512]{1,0:T(8,128)(2,1)} %copy-done.8, bf16[256,512]{1,0:T(8,128)(2,1)} %copy-done.9, bf16[256,512]{1,0:T(8,128)(2,1)} %copy-done.10, ...), custom_call_target="tpu_custom_call" | custom-call | bytes 8388608 | tf_op jit(solution)/shard_map/unpack_weights/pallas_call | solution.py:174
  93.7 24.3 %core.1 = (bf16[2,2,128,1024]{3,2,1,0:T(8,128)(2,1)}, bf16[2,2,128,1024]{3,2,1,0:T(8,128)(2,1)}, bf16[2,2,128,1024]{3,2,1,0:T(8,128)(2,1)}, bf16[2,2,128,1024]{3...) custom-call(bf16[2,128,1024]{2,1,0:T(8,128)(2,1)} %collective-permut, ...), custom_call_target="tpu_custom_call" | custom-call | flops 10737418240 | bytes 20971520 | tf_op jit(solution)/shard_map/core/pallas_call | solution.py:264
  118.6 2.2 collective-permute-done.24
  120.9 1.6 add.66
  123.3 1.7 collective-permute-start.25
  128.1 2.0 add.65
  130.9 6.7 %collective-permute-done.25 = bf16[1,2,128,1024]{3,2,1,0:T(8,128)(2,1)} collective-permute-done((bf16[1,2,128,1024]{3,2,1,0:T(8,128)(2,1)}, bf16[1,2,128,1024]{3,2,1,0:T(8,128)(2,1)}, u32[]{:S(2)}, u32[]{:S(2)}) %collective-permute-start.25) | collective-permute-done | bytes 524320 | tf_op jit(solution)/shard_map/sums_3_2/ppermute | solution.py:100
  137.6 1.7 collective-permute-start.26
  139.7 2.3 fusion.14
  141.9 45.3 %all-gather.1 = f32[16,2,1024]{2,1,0:T(2,128)S(1)} all-gather(f32[1,2,1024]{2,1,0:T(2,128)S(1)} %bitcast.38), channel_id=2, replica_groups=mesh['groups'=2,'tensor'=4,'dp'=4] {'tensor','dp'}, dimensions={0}, use_global_device_ids=true | all-gather | bytes 139264 | tf_op jit(solution)/shard_map/all_gather | solution.py:369
  187.3 2.0 add.64
  189.4 2.0 collective-permute-start.27
  192.0 1.6 add.63
  195.1 6.4 %collective-permute-done.27 = bf16[1,2,128,1024]{3,2,1,0:T(8,128)(2,1)S(1)} collective-permute-done((bf16[1,2,128,1024]{3,2,1,0:T(8,128)(2,1)S(1)}, bf16[1,2,128,1024]{3,2,1,0:T(8,128)(2,1)S(1)}, u32[]{:S(2)}, u32[]{:S(2)}) %collective-permute-start.27) | collective-permute-done | bytes 524320 | tf_op jit(solution)/shard_map/sums_1_2/ppermute | solution.py:100
  202.6 2.1 collective-permute-start.32
  207.6 9.4 %collective-permute-done.31 = bf16[2,128,1024]{2,1,0:T(8,128)(2,1)S(1)} collective-permute-done((bf16[2,128,1024]{2,1,0:T(8,128)(2,1)S(1)}, bf16[2,128,1024]{2,1,0:T(8,128)(2,1)S(1)}, u32[]{:S(2)}, u32[]{:S(2)}) %collective-permute-start.31) | collective-permute-done | bytes 524320 | tf_op jit(solution)/shard_map/sums_2/ppermute | solution.py:100
  217.0 11.5 %collective-permute-done.30 = bf16[2,128,1024]{2,1,0:T(8,128)(2,1)S(1)} collective-permute-done((bf16[2,128,1024]{2,1,0:T(8,128)(2,1)S(1)}, bf16[2,128,1024]{2,1,0:T(8,128)(2,1)S(1)}, u32[]{:S(2)}, u32[]{:S(2)}) %collective-permute-start.30) | collective-permute-done | bytes 524320 | tf_op jit(solution)/shard_map/sums_1/ppermute | solution.py:100
  228.8 17.7 %collective-permute-done.32 = bf16[512,512]{1,0:T(8,128)(2,1)S(1)} collective-permute-done((bf16[512,512]{1,0:T(8,128)(2,1)S(1)}, bf16[512,512]{1,0:T(8,128)(2,1)S(1)}, u32[]{:S(2)}, u32[]{:S(2)}) %collective-permute-start.32) | collective-permute-done | bytes 524320 | tf_op jit(solution)/shard_map/grads_1/ppermute | solution.py:100
  (136 shorter events, 26.2 us)
Async XLA Ops:
  1.7 15.0 %collective-permute-start.2 = (bf16[2,128,1024]{2,1,0:T(8,128)(2,1)S(1)}, bf16[2,128,1024]{2,1,0:T(8,128)(2,1)S(1)}, u32[]{:S(2)}, u32[]{:S(2)}) collective-permute-start(bf16[2,128,1024]{2,1,0:T(8,128)(2,1)S(1)} %pad_maximum_fusion.refs_12_), channel_id=1, source_target_pairs={{0,8},{4,12},{8,0},{12,4},{1,9},{5,13},{9,1},{13,5},{2,10},{6,14},... | collective-permute-start | bytes 1572872 | tf_op jit(solution)/shard_map/tokens_0_2/ppermute | solution.py:100
  4.8 22.0 %collective-permute-start.1 = (bf16[2,128,1024]{2,1,0:T(8,128)(2,1)S(1)}, bf16[2,128,1024]{2,1,0:T(8,128)(2,1)S(1)}, u32[]{:S(2)}, u32[]{:S(2)}) collective-permute-start(bf16[2,128,1024]{2,1,0:T(8,128)(2,1)S(1)} %pad_maximum_fusion.refs_12_), channel_id=1, source_target_pairs={{0,1},{1,0},{2,3},{3,2},{4,5},{5,4},{6,7},{7,6},{8,9},{9,8},{10,11... | collective-permute-start | bytes 1572872 | tf_op jit(solution)/shard_map/tokens_1/ppermute | solution.py:100
  8.8 25.5 %collective-permute-start = (bf16[2,128,1024]{2,1,0:T(8,128)(2,1)S(1)}, bf16[2,128,1024]{2,1,0:T(8,128)(2,1)}, u32[]{:S(2)}, u32[]{:S(2)}) collective-permute-start(bf16[2,128,1024]{2,1,0:T(8,128)(2,1)S(1)} %pad_maximum_fusion.refs_12_), channel_id=1, source_target_pairs={{0,2},{1,3},{2,0},{3,1},{4,6},{5,7},{6,4},{7,5},{8,10},{9,11},{10,... | collective-permute-start | bytes 1572872 | tf_op jit(solution)/shard_map/tokens_2/ppermute | solution.py:100
  11.4 22.9 %collective-permute-start.6 = (bf16[2,128,1024]{2,1,0:T(8,128)(2,1)S(1)}, bf16[2,128,1024]{2,1,0:T(8,128)(2,1)S(1)}, u32[]{:S(2)}, u32[]{:S(2)}) collective-permute-start(bf16[2,128,1024]{2,1,0:T(8,128)(2,1)S(1)} %pad_maximum_fusion.refs_12_), channel_id=1, source_target_pairs={{0,4},{4,0},{8,12},{12,8},{1,5},{5,1},{9,13},{13,9},{2,6},{6,2},{1... | collective-permute-start | bytes 1572872 | tf_op jit(solution)/shard_map/tokens_0_1/ppermute | solution.py:100
  26.8 20.7 %collective-permute-start.3 = (bf16[2,128,1024]{2,1,0:T(8,128)(2,1)S(1)}, bf16[2,128,1024]{2,1,0:T(8,128)(2,1)S(1)}, u32[]{:S(2)}, u32[]{:S(2)}) collective-permute-start(bf16[2,128,1024]{2,1,0:T(8,128)(2,1)S(1)} %collective-permute-done.1.refs_8_), channel_id=1, source_target_pairs={{0,8},{4,12},{8,0},{12,4},{1,9},{5,13},{9,1},{13,5},{2,10},{6,14},... | collective-permute-start | bytes 1572872 | tf_op jit(solution)/shard_map/tokens_1_2/ppermute | solution.py:100
  27.2 20.4 %collective-permute-start.7 = (bf16[2,128,1024]{2,1,0:T(8,128)(2,1)S(1)}, bf16[2,128,1024]{2,1,0:T(8,128)(2,1)S(1)}, u32[]{:S(2)}, u32[]{:S(2)}) collective-permute-start(bf16[2,128,1024]{2,1,0:T(8,128)(2,1)S(1)} %collective-permute-done.2.refs_14_), channel_id=1, source_target_pairs={{0,4},{4,0},{8,12},{12,8},{1,5},{5,1},{9,13},{13,9},{2,6},{6,2},{1... | collective-permute-start | bytes 1572872 | tf_op jit(solution)/shard_map/tokens_0_3/ppermute | solution.py:100
  27.2 12.4 %collective-permute-start.4 = (bf16[256,512]{1,0:T(8,128)(2,1)}, bf16[256,512]{1,0:T(8,128)(2,1)S(1)}, u32[]{:S(2)}, u32[]{:S(2)}) collective-permute-start(bf16[256,512]{1,0:T(8,128)(2,1)} %get-tuple-element.45), channel_id=1, source_target_pairs={{0,1},{1,0},{2,3},{3,2},{4,5},{5,4},{6,7},{7,6},{8,9},{9,8},{10,11... | collective-permute-start | bytes 786440 | tf_op jit(solution)/shard_map/weights_1/ppermute | solution.py:100
  34.3 13.2 %collective-permute-start.5 = (bf16[256,512]{1,0:T(8,128)(2,1)}, bf16[256,512]{1,0:T(8,128)(2,1)S(1)}, u32[]{:S(2)}, u32[]{:S(2)}) collective-permute-start(bf16[256,512]{1,0:T(8,128)(2,1)} %get-tuple-element.47), channel_id=1, source_target_pairs={{0,2},{1,3},{2,0},{3,1},{4,6},{5,7},{6,4},{7,5},{8,10},{9,11},{10,... | collective-permute-start | bytes 786440 | tf_op jit(solution)/shard_map/weights_2/ppermute | solution.py:100
  47.6 20.2 %collective-permute-start.11 = (bf16[2,128,1024]{2,1,0:T(8,128)(2,1)}, bf16[2,128,1024]{2,1,0:T(8,128)(2,1)}, u32[]{:S(2)}, u32[]{:S(2)}) collective-permute-start(bf16[2,128,1024]{2,1,0:T(8,128)(2,1)} %collective-permute-done.refs_4_), channel_id=1, source_target_pairs={{0,8},{4,12},{8,0},{12,4},{1,9},{5,13},{9,1},{13,5},{2,10},{6,14},... | collective-permute-start | bytes 1572872 | tf_op jit(solution)/shard_map/tokens_2_2/ppermute | solution.py:100
  48.2 19.6 %collective-permute-start.8 = (bf16[2,128,1024]{2,1,0:T(8,128)(2,1)}, bf16[2,128,1024]{2,1,0:T(8,128)(2,1)}, u32[]{:S(2)}, u32[]{:S(2)}) collective-permute-start(bf16[2,128,1024]{2,1,0:T(8,128)(2,1)} %collective-permute-done.refs_4_), channel_id=1, source_target_pairs={{0,1},{1,0},{2,3},{3,2},{4,5},{5,4},{6,7},{7,6},{8,9},{9,8},{10,11... | collective-permute-start | bytes 1572872 | tf_op jit(solution)/shard_map/tokens_3/ppermute | solution.py:100
  48.2 19.6 %collective-permute-start.10 = (bf16[256,512]{1,0:T(8,128)(2,1)}, bf16[256,512]{1,0:T(8,128)(2,1)S(1)}, u32[]{:S(2)}, u32[]{:S(2)}) collective-permute-start(bf16[256,512]{1,0:T(8,128)(2,1)} %get-tuple-element.50), channel_id=1, source_target_pairs={{0,3},{1,2},{2,1},{3,0},{4,7},{5,6},{6,5},{7,4},{8,11},{9,10},{10,... | collective-permute-start | bytes 786440 | tf_op jit(solution)/shard_map/weights_3/ppermute | solution.py:100
  50.6 20.9 %collective-permute-start.16 = (bf16[2,128,1024]{2,1,0:T(8,128)(2,1)S(1)}, bf16[2,128,1024]{2,1,0:T(8,128)(2,1)S(1)}, u32[]{:S(2)}, u32[]{:S(2)}) collective-permute-start(bf16[2,128,1024]{2,1,0:T(8,128)(2,1)S(1)} %collective-permute-done.1.refs_8_), channel_id=1, source_target_pairs={{0,4},{4,0},{8,12},{12,8},{1,5},{5,1},{9,13},{13,9},{2,6},{6,2},{1... | collective-permute-start | bytes 1572872 | tf_op jit(solution)/shard_map/tokens_1_1/ppermute | solution.py:100
  50.6 28.2 %collective-permute-start.17 = (bf16[2,128,1024]{2,1,0:T(8,128)(2,1)S(1)}, bf16[2,128,1024]{2,1,0:T(8,128)(2,1)S(1)}, u32[]{:S(2)}, u32[]{:S(2)}) collective-permute-start(bf16[2,128,1024]{2,1,0:T(8,128)(2,1)S(1)} %collective-permute-done.3.refs_10_), channel_id=1, source_target_pairs={{0,4},{4,0},{8,12},{12,8},{1,5},{5,1},{9,13},{13,9},{2,6},{6,2},{1... | collective-permute-start | bytes 1572872 | tf_op jit(solution)/shard_map/tokens_1_3/ppermute | solution.py:100
  67.8 13.3 %collective-permute-start.12 = (bf16[2,128,1024]{2,1,0:T(8,128)(2,1)}, bf16[2,128,1024]{2,1,0:T(8,128)(2,1)}, u32[]{:S(2)}, u32[]{:S(2)}) collective-permute-start(bf16[2,128,1024]{2,1,0:T(8,128)(2,1)} %collective-permute-done.8.refs_0_), channel_id=1, source_target_pairs={{0,8},{4,12},{8,0},{12,4},{1,9},{5,13},{9,1},{13,5},{2,10},{6,14},... | collective-permute-start | bytes 1572872 | tf_op jit(solution)/shard_map/tokens_3_2/ppermute | solution.py:100
  69.5 9.2 %collective-permute-start.19 = (bf16[256,512]{1,0:T(8,128)(2,1)S(1)}, bf16[256,512]{1,0:T(8,128)(2,1)S(1)}, u32[]{:S(2)}, u32[]{:S(2)}) collective-permute-start(bf16[256,512]{1,0:T(8,128)(2,1)S(1)} %collective-permute-done.5.rest_1_), channel_id=1, source_target_pairs={{0,16},{16,0},{1,17},{17,1},{2,18},{18,2},{3,19},{19,3},{4,20},{20... | collective-permute-start | bytes 786440 | tf_op jit(solution)/shard_map/weights_2/ppermute | solution.py:100
  71.0 11.2 %collective-permute-start.18 = (bf16[256,512]{1,0:T(8,128)(2,1)S(1)}, bf16[256,512]{1,0:T(8,128)(2,1)S(1)}, u32[]{:S(2)}, u32[]{:S(2)}) collective-permute-start(bf16[256,512]{1,0:T(8,128)(2,1)S(1)} %collective-permute-done.4.rest_0_), channel_id=1, source_target_pairs={{0,16},{16,0},{1,17},{17,1},{2,18},{18,2},{3,19},{19,3},{4,20},{20... | collective-permute-start | bytes 786440 | tf_op jit(solution)/shard_map/weights_1/ppermute | solution.py:100
  71.6 22.0 %collective-permute-start.14 = (bf16[2,128,1024]{2,1,0:T(8,128)(2,1)}, bf16[2,128,1024]{2,1,0:T(8,128)(2,1)}, u32[]{:S(2)}, u32[]{:S(2)}) collective-permute-start(bf16[2,128,1024]{2,1,0:T(8,128)(2,1)} %collective-permute-done.refs_4_), channel_id=1, source_target_pairs={{0,4},{4,0},{8,12},{12,8},{1,5},{5,1},{9,13},{13,9},{2,6},{6,2},{1... | collective-permute-start | bytes 1572872 | tf_op jit(solution)/shard_map/tokens_2_1/ppermute | solution.py:100
  78.8 14.8 %collective-permute-start.15 = (bf16[2,128,1024]{2,1,0:T(8,128)(2,1)}, bf16[2,128,1024]{2,1,0:T(8,128)(2,1)}, u32[]{:S(2)}, u32[]{:S(2)}) collective-permute-start(bf16[2,128,1024]{2,1,0:T(8,128)(2,1)} %collective-permute-done.11.refs_6_), channel_id=1, source_target_pairs={{0,4},{4,0},{8,12},{12,8},{1,5},{5,1},{9,13},{13,9},{2,6},{6,2},{1... | collective-permute-start | bytes 1572872 | tf_op jit(solution)/shard_map/tokens_2_3/ppermute | solution.py:100
  78.8 14.8 %collective-permute-start.9 = (bf16[2,128,1024]{2,1,0:T(8,128)(2,1)}, bf16[2,128,1024]{2,1,0:T(8,128)(2,1)}, u32[]{:S(2)}, u32[]{:S(2)}) collective-permute-start(bf16[2,128,1024]{2,1,0:T(8,128)(2,1)} %collective-permute-done.8.refs_0_), channel_id=1, source_target_pairs={{0,4},{4,0},{8,12},{12,8},{1,5},{5,1},{9,13},{13,9},{2,6},{6,2},{1... | collective-permute-start | bytes 1572872 | tf_op jit(solution)/shard_map/tokens_3_1/ppermute | solution.py:100
  81.1 12.5 %collective-permute-start.13 = (bf16[2,128,1024]{2,1,0:T(8,128)(2,1)}, bf16[2,128,1024]{2,1,0:T(8,128)(2,1)}, u32[]{:S(2)}, u32[]{:S(2)}) collective-permute-start(bf16[2,128,1024]{2,1,0:T(8,128)(2,1)} %collective-permute-done.12.refs_2_), channel_id=1, source_target_pairs={{0,4},{4,0},{8,12},{12,8},{1,5},{5,1},{9,13},{13,9},{2,6},{6,2},{1... | collective-permute-start | bytes 1572872 | tf_op jit(solution)/shard_map/tokens_3_3/ppermute | solution.py:100
  123.3 14.3 %collective-permute-start.25 = (bf16[1,2,128,1024]{3,2,1,0:T(8,128)(2,1)}, bf16[1,2,128,1024]{3,2,1,0:T(8,128)(2,1)}, u32[]{:S(2)}, u32[]{:S(2)}) collective-permute-start(bf16[1,2,128,1024]{3,2,1,0:T(8,128)(2,1)} %slice.100), channel_id=1, source_target_pairs={{0,8},{4,12},{8,0},{12,4},{1,9},{5,13},{9,1},{13,5},{2,10},{6,14},... | collective-permute-start | bytes 1572872 | tf_op jit(solution)/shard_map/sums_3_2/ppermute | solution.py:100
  125.3 62.0 %collective-permute-start.22 = (bf16[2,2,128,1024]{3,2,1,0:T(8,128)(2,1)}, bf16[2,2,128,1024]{3,2,1,0:T(8,128)(2,1)}, u32[]{:S(2)}, u32[]{:S(2)}) collective-permute-start(bf16[2,2,128,1024]{3,2,1,0:T(8,128)(2,1)} %get-tuple-element.60), channel_id=1, source_target_pairs={{0,4},{4,0},{8,12},{12,8},{1,5},{5,1},{9,13},{13,9},{2,6},{6,2},{1... | collective-permute-start | bytes 3145736 | tf_op jit(solution)/shard_map/sums_1_1/ppermute | solution.py:100
  125.4 66.6 %collective-permute-start.21 = (bf16[2,2,128,1024]{3,2,1,0:T(8,128)(2,1)}, bf16[2,2,128,1024]{3,2,1,0:T(8,128)(2,1)}, u32[]{:S(2)}, u32[]{:S(2)}) collective-permute-start(bf16[2,2,128,1024]{3,2,1,0:T(8,128)(2,1)} %get-tuple-element.58), channel_id=1, source_target_pairs={{0,4},{4,0},{8,12},{12,8},{1,5},{5,1},{9,13},{13,9},{2,6},{6,2},{1... | collective-permute-start | bytes 3145736 | tf_op jit(solution)/shard_map/sums_0_1/ppermute | solution.py:100
  127.1 77.6 %collective-permute-start.33 = (bf16[512,512]{1,0:T(8,128)(2,1)}, bf16[512,512]{1,0:T(8,128)(2,1)}, u32[]{:S(2)}, u32[]{:S(2)}) collective-permute-start(bf16[512,512]{1,0:T(8,128)(2,1)} %get-tuple-element.73), channel_id=1, source_target_pairs={{0,2},{1,3},{2,0},{3,1},{4,6},{5,7},{6,4},{7,5},{8,10},{9,11},{10,... | collective-permute-start | bytes 1572872 | tf_op jit(solution)/shard_map/grads_2/ppermute | solution.py:100
  137.6 51.7 %collective-permute-start.26 = (bf16[1,2,128,1024]{3,2,1,0:T(8,128)(2,1)}, bf16[1,2,128,1024]{3,2,1,0:T(8,128)(2,1)}, u32[]{:S(2)}, u32[]{:S(2)}) collective-permute-start(bf16[1,2,128,1024]{3,2,1,0:T(8,128)(2,1)} %slice.99), channel_id=1, source_target_pairs={{0,8},{4,12},{8,0},{12,4},{1,9},{5,13},{9,1},{13,5},{2,10},{6,14},... | collective-permute-start | bytes 1572872 | tf_op jit(solution)/shard_map/sums_2_2/ppermute | solution.py:100
  141.9 51.8 %collective-permute-start.29 = (bf16[2,128,1024]{2,1,0:T(8,128)(2,1)}, bf16[2,128,1024]{2,1,0:T(8,128)(2,1)S(1)}, u32[]{:S(2)}, u32[]{:S(2)}) collective-permute-start(bf16[2,128,1024]{2,1,0:T(8,128)(2,1)} %fusion.14), channel_id=1, source_target_pairs={{0,1},{1,0},{2,3},{3,2},{4,5},{5,4},{6,7},{7,6},{8,9},{9,8},{10,11... | collective-permute-start | bytes 1572872 | tf_op jit(solution)/shard_map/sums_3/ppermute | solution.py:100
  189.4 12.2 %collective-permute-start.27 = (bf16[1,2,128,1024]{3,2,1,0:T(8,128)(2,1)S(1)}, bf16[1,2,128,1024]{3,2,1,0:T(8,128)(2,1)S(1)}, u32[]{:S(2)}, u32[]{:S(2)}) collective-permute-start(bf16[1,2,128,1024]{3,2,1,0:T(8,128)(2,1)S(1)} %slice.98), channel_id=1, source_target_pairs={{0,8},{4,12},{8,0},{12,4},{1,9},{5,13},{9,1},{13,5},{2,10},{6,14},... | collective-permute-start | bytes 1572872 | tf_op jit(solution)/shard_map/sums_1_2/ppermute | solution.py:100
  195.1 21.9 %collective-permute-start.31 = (bf16[2,128,1024]{2,1,0:T(8,128)(2,1)S(1)}, bf16[2,128,1024]{2,1,0:T(8,128)(2,1)S(1)}, u32[]{:S(2)}, u32[]{:S(2)}) collective-permute-start(bf16[2,128,1024]{2,1,0:T(8,128)(2,1)S(1)} %fusion), channel_id=1, source_target_pairs={{0,2},{1,3},{2,0},{3,1},{4,6},{5,7},{6,4},{7,5},{8,10},{9,11},{10,... | collective-permute-start | bytes 1572872 | tf_op jit(solution)/shard_map/sums_2/ppermute | solution.py:100
  201.6 15.4 %collective-permute-start.28 = (bf16[1,2,128,1024]{3,2,1,0:T(8,128)(2,1)S(1)}, bf16[1,2,128,1024]{3,2,1,0:T(8,128)(2,1)S(1)}, u32[]{:S(2)}, u32[]{:S(2)}) collective-permute-start(bf16[1,2,128,1024]{3,2,1,0:T(8,128)(2,1)S(1)} %slice.97), channel_id=1, source_target_pairs={{0,8},{4,12},{8,0},{12,4},{1,9},{5,13},{9,1},{13,5},{2,10},{6,14},... | collective-permute-start | bytes 1572872 | tf_op jit(solution)/shard_map/sums_0_2/ppermute | solution.py:100
  202.4 26.1 %collective-permute-start.30 = (bf16[2,128,1024]{2,1,0:T(8,128)(2,1)S(1)}, bf16[2,128,1024]{2,1,0:T(8,128)(2,1)S(1)}, u32[]{:S(2)}, u32[]{:S(2)}) collective-permute-start(bf16[2,128,1024]{2,1,0:T(8,128)(2,1)S(1)} %fusion.16), channel_id=1, source_target_pairs={{0,1},{1,0},{2,3},{3,2},{4,5},{5,4},{6,7},{7,6},{8,9},{9,8},{10,11... | collective-permute-start | bytes 1572872 | tf_op jit(solution)/shard_map/sums_1/ppermute | solution.py:100
  202.6 43.9 %collective-permute-start.32 = (bf16[512,512]{1,0:T(8,128)(2,1)S(1)}, bf16[512,512]{1,0:T(8,128)(2,1)S(1)}, u32[]{:S(2)}, u32[]{:S(2)}) collective-permute-start(bf16[512,512]{1,0:T(8,128)(2,1)S(1)} %copy-done.19), channel_id=1, source_target_pairs={{0,1},{1,0},{2,3},{3,2},{4,5},{5,4},{6,7},{7,6},{8,9},{9,8},{10,11... | collective-permute-start | bytes 1572872 | tf_op jit(solution)/shard_map/grads_1/ppermute | solution.py:100
  204.7 42.0 %collective-permute-start.34 = (bf16[512,512]{1,0:T(8,128)(2,1)S(1)}, bf16[512,512]{1,0:T(8,128)(2,1)S(1)}, u32[]{:S(2)}, u32[]{:S(2)}) collective-permute-start(bf16[512,512]{1,0:T(8,128)(2,1)S(1)} %copy-done.18), channel_id=1, source_target_pairs={{0,3},{1,2},{2,1},{3,0},{4,7},{5,6},{6,5},{7,4},{8,11},{9,10},{10,... | collective-permute-start | bytes 1572872 | tf_op jit(solution)/shard_map/grads_3/ppermute | solution.py:100
  (30 other events, 547.5 us)

commit v6 on v5

--- a/solution.py
+++ b/solution.py
@@ -104,26 +104,34 @@
     return [1 << b for b in reversed(range(size.bit_length() - 1))]
 
 
+def share(k, n_dp, mates):
+    return mates if k >= bits_of(n_dp)[0] else 1
+
+
 def pack_weights(w_up, w_down, mates):
     n_dp = lax.axis_size("dp")
     depth, units = w_up.shape[0], w_up.shape[1] // n_dp
-    up_rows, down_rows, strips = depth // mates, units // mates, units // depth
-    strip_rows = down_rows // strips
+    strips = units // depth
 
     def kernel(up_ref, down_ref, *sends):
         place, mate = lax.axis_index("dp"), lax.rem(lax.axis_index("groups"), mates)
         for k in range(1, n_dp):
+            n = share(k, n_dp, mates)
+            part = mate if n > 1 else 0
+            rows = depth // n
             first = pl.multiple_of((place ^ k) * units, units)
             send = sends[k - 1]
-            row = pl.multiple_of(mate * up_rows, up_rows)
-            send[:up_rows, :] = up_ref[pl.ds(row, up_rows), pl.ds(first, units)]
+            send[:rows, :] = up_ref[pl.ds(pl.multiple_of(part * rows, rows), rows), pl.ds(first, units)]
             for c in range(strips):
-                row = pl.multiple_of(first + mate * down_rows + c * strip_rows, strip_rows)
-                send[up_rows:, c * depth : (c + 1) * depth] = down_ref[pl.ds(row, strip_rows), :]
+                row = pl.multiple_of(first + part * (units // n) + c * rows, rows)
+                send[rows:, c * depth : (c + 1) * depth] = down_ref[pl.ds(row, rows), :]
 
     return pl.pallas_call(
         kernel,
-        out_shape=[jax.ShapeDtypeStruct((2 * up_rows, units), w_up.dtype)] * (n_dp - 1),
+        out_shape=[
+            jax.ShapeDtypeStruct((2 * depth // share(k, n_dp, mates), units), w_up.dtype)
+            for k in range(1, n_dp)
+        ],
         in_specs=[pl.BlockSpec(memory_space=pltpu.VMEM)] * 2,
         out_specs=[pl.BlockSpec(memory_space=pltpu.VMEM)] * (n_dp - 1),
         cost_estimate=pl.CostEstimate(flops=0, bytes_accessed=8 * w_up.size, transcendentals=0),
@@ -134,11 +142,11 @@
 def unpack_weights(w_up, w_down, got, mates):
     n_dp = lax.axis_size("dp")
     depth, units = w_up.shape[0], w_up.shape[1] // n_dp
-    up_rows, down_rows, strips = depth // mates, units // mates, units // depth
-    strip_rows = down_rows // strips
+    strips = units // depth
+    n_copies = 2 + sum(len(got[k]) * (1 + strips) for k in got)
 
     def kernel(up_ref, down_ref, *rest):
-        pieces, (up_out, down_out, sem) = rest[:-3], rest[-3:]
+        pieces, (up_out, down_out, sem) = list(rest[:-3]), rest[-3:]
         place, mate = lax.axis_index("dp"), lax.rem(lax.axis_index("groups"), mates)
         copies = []
 
@@ -157,16 +165,18 @@
         )
         for k in range(1, n_dp):
             first = pl.multiple_of((place ^ k) * depth, depth)
-            for j in range(mates):
-                piece = pieces[j * (n_dp - 1) + k - 1]
-                part = mate ^ j
-                row = pl.multiple_of(first + part * up_rows, up_rows)
-                copy(piece.at[pl.ds(0, up_rows), :], up_out.at[pl.ds(row, up_rows), :])
+            n = len(got[k])
+            rows = depth // n
+            for j in range(n):
+                piece = pieces.pop(0)
+                part = mate ^ j if n > 1 else 0
+                row = pl.multiple_of(first + part * rows, rows)
+                copy(piece.at[pl.ds(0, rows), :], up_out.at[pl.ds(row, rows), :])
                 for c in range(strips):
-                    row = pl.multiple_of(part * down_rows + c * strip_rows, strip_rows)
+                    row = pl.multiple_of(part * (units // n) + c * rows, rows)
                     copy(
-                        piece.at[pl.ds(up_rows, strip_rows), pl.ds(c * depth, depth)],
-                        down_out.at[pl.ds(row, strip_rows), pl.ds(first, depth)],
+                        piece.at[pl.ds(rows, rows), pl.ds(c * depth, depth)],
+                        down_out.at[pl.ds(row, rows), pl.ds(first, depth)],
                     )
         for one in copies:
             one.wait()
@@ -177,12 +187,12 @@
             jax.ShapeDtypeStruct((depth * n_dp, units), w_up.dtype),
             jax.ShapeDtypeStruct((units, depth * n_dp), w_down.dtype),
         ],
-        in_specs=[pl.BlockSpec(memory_space=pl.ANY)] * (2 + mates * (n_dp - 1)),
+        in_specs=[pl.BlockSpec(memory_space=pl.ANY)] * (2 + sum(len(got[k]) for k in got)),
         out_specs=[pl.BlockSpec(memory_space=pltpu.VMEM)] * 2,
-        scratch_shapes=[pltpu.SemaphoreType.DMA((2 + mates * (n_dp - 1) * (1 + strips),))],
+        scratch_shapes=[pltpu.SemaphoreType.DMA((n_copies,))],
         cost_estimate=pl.CostEstimate(flops=0, bytes_accessed=16 * w_up.size, transcendentals=0),
         name="unpack_weights",
-    )(w_up, w_down, *[piece for pieces in got for piece in pieces])
+    )(w_up, w_down, *[piece for k in range(1, n_dp) for piece in got[k]])
 
 
 def core(chunks, up, down, gain, bias, n_dp):
@@ -338,26 +348,23 @@
     for bit in bits_of(n_dp)[:0:-1]:
         tokens_dp(bit)
     sends = pack_weights(w_up, w_down, mates)
-    tokens_dp(top, sends[0])
-    stage = [tokens[1], chunks[0][high]]
-    tokens_tensor(1, *stage)
-    for bit in reversed(bits_of(n_dp)):
-        weights_dp(bit, *stage)
-    stage = [tokens[top], chunks[1][high], *got.values(), *chunks[0].values()]
+    tokens_dp(top)
+    stage = [tokens[1], *chunks[0].values()]
+    tokens_tensor(1, tokens[1], chunks[0][high])
+    weights_dp(top, *stage)
+    stage = [tokens[top], got[top], chunks[1][high], *chunks[0].values()]
     for k in range(2, n_dp):
         if k & (k - 1):
             tokens_dp(k, *stage)
             weights_dp(k, *stage)
-            stage = [tokens[k], got[k], chunks[k - 1][high]]
-        if mates == 2:
-            for other in (k - 1, k):
-                if other & (other - 1) == 0 and other not in crossed:
-                    weights_groups(other, *stage)
+            stage = [tokens[k], got[k], *chunks[k - 2].values(), chunks[k - 1][high]]
         tokens_tensor(k, *stage)
     for k in range(1, n_dp):
-        if mates == 2 and k not in crossed:
-            weights_groups(k, *stage, *chunks[1].values())
-    got = [[pieces[k] for k in range(1, n_dp)] for pieces in (got, crossed)[:mates]]
+        if k < top:
+            weights_dp(k, *stage)
+        elif mates == 2:
+            weights_groups(k, *stage)
+    got = {k: [got[k]] + ([crossed[k]] if k in crossed else []) for k in got}
     up, down = unpack_weights(w_up, w_down, got, mates)
 
     order = sorted(chunks, reverse=True)
@@ -366,37 +373,47 @@
     )
     blocks = dict(enumerate(blocks))
     blocks[top] = swap(blocks[top], "dp", top, f"grads_{top}")
-    stats = jnp.sum(lax.all_gather(stats, ("tensor", "dp")), axis=0)
 
     sums, behind = {}, ()
     for k, (even, odd) in zip(order, halves, strict=True):
-        part = even + swap(odd, "tensor", 1, f"sums_{k}_1")
+        came = swap(odd, "tensor", 1, f"sums_{k}_1")
+        parts = {2 * j: (even[j], came[j]) for j in range(n_tensor // 2)}
         for bit in reversed(bits_of(n_tensor)[:-1]):
-            send = after(part[1::2], *behind)
-            came = swap(send, "tensor", bit, f"sums_{k}_{bit}")
-            part = part[0::2] + came
-            behind = (came,)
-        sums[k] = part[0]
+            for j in [j for j in parts if j & bit]:
+                send = after(sum(parts.pop(j)), *behind)
+                parts[j ^ bit] += (swap(send, "tensor", bit, f"sums_{k}_{j}"),)
+                behind = parts[j ^ bit][-1:]
+        sums[k] = parts[0]
+
+    def add(terms, dtype=jnp.bfloat16):
+        return sum(term.astype(jnp.float32) for term in terms).astype(dtype)
+
     came = {}
     for bit in bits_of(n_dp)[::-1]:
         for k in [k for k in order if k & bit and k in sums and k != bit]:
-            came[k] = swap(sums.pop(k), "dp", bit, f"sums_{k}")
-            sums[k ^ bit] = (sums[k ^ bit].astype(jnp.float32) + came[k]).astype(jnp.bfloat16)
-    last = sums[top]
+            came[k] = swap(add(sums.pop(k)), "dp", bit, f"sums_{k}")
+            sums[k ^ bit] += (came[k],)
+    last = add(sums[top])
     came[top] = swap(last, "dp", top, f"sums_{top}")
+    stats = after(stats, came[order[0]])
+    for bit in bits_of(n_tensor):
+        stats = stats + swap(stats, "tensor", bit, "stats")
+    stats = after(stats, last)
+    for bit in bits_of(n_dp):
+        stats = stats + swap(stats, "dp", bit, "stats")
+        if bit == top:
+            first = stats
     for bit in bits_of(n_dp)[:0:-1]:
-        came[bit] = swap(after(sums[bit], last), "dp", bit, f"sums_{bit}")
-    total = sums[0].astype(jnp.float32)
-    for bit in bits_of(n_dp)[::-1]:
-        total = total + came[bit].astype(jnp.float32)
+        came[bit] = swap(after(add(sums[bit]), last, first), "dp", bit, f"sums_{bit}")
+    total = add((*sums[0], *(came[bit] for bit in bits_of(n_dp)[::-1])), jnp.float32)
     sums = {0: total}
     for k in range(1, n_dp):
         if k < top:
-            blocks[k] = swap(after(blocks[k], last), "dp", k, f"grads_{k}")
+            blocks[k] = swap(after(blocks[k], last, first), "dp", k, f"grads_{k}")
         elif k > top:
             blocks[k] = swap(after(blocks[k], blocks[top], last), "dp", k, f"grads_{k}")
-    for k in range(1, n_dp):
-        blocks[k] = after(blocks[k], last if k == top else total)
+    for k in range(n_dp):
+        blocks[k] = after(blocks[k], last if k in (0, top) else total)
     branch, grad_normed = sums[0][0], sums[0][1]
     second_in, grad_first_in = finish_rows(
         branch, grad_normed, second_out, grad_first, first_out, norm_gain, norm_bias

time: 251 us -> 251 us (level)
  waiting for transfers between devices: 123 us -> 172 us
  blocking collectives: 45.3 us -> 0 us
  other arithmetic: 17.5 us -> 13.2 us
    ppermute x35 -> x38, waiting for transfers between devices: 123 us -> 172 us  [swap(): lax.ppermute(values, axis, [(i, i ^ mask) for i in range(lax.axis_size(ax...]
    all_gather x1 -> x0, blocking collectives: 45.3 us -> none  [gather_tokens_body(): stats = jnp.sum(lax.all_gather(stats, ('tensor', 'dp')), axis=0)]
    convert_element_type x1 -> x3, other arithmetic: 1.31 us -> 4.34 us  [add(): return sum((term.astype(jnp.float32) for term in terms)).astype(dtype)]
    add x5 -> x8, other arithmetic: 7.56 us -> 4.73 us  [the longest x4 4.27 us: gather_tokens_body(): send = after(sum(parts.pop(j)), *behind)]
    ppermute x35 -> x38, starting transfers between devices: 28.1 us -> 29.7 us  [swap(): lax.ppermute(values, axis, [(i, i ^ mask) for i in range(lax.axis_size(ax...]
  transfers between devices with their start and end apart: 35 -> 38, of which waited for: 16 -> 17; matrix products, arithmetic and copies ran while one was open for 7% -> 4% of each run, Pallas kernels for 2% -> 2%
where the time goes in v6:
time: 251 us; the launch traced here: 250 us
  waiting for transfers between devices  172 us (69%)
  Pallas kernels  29.9 us (12%)
  starting transfers between devices  29.7 us (12%)
  other arithmetic  13.2 us (5%)
  local copies, waits for them, and re-layouts  3.95 us (2%)
    ppermute x38, waiting for transfers between devices, swap(): lax.ppermute(values, axis, [(i, i ^ mask) for i in range(lax.axis_size(ax...  172 us
    ppermute x38, starting transfers between devices, swap(): lax.ppermute(values, axis, [(i, i ^ mask) for i in range(lax.axis_size(ax...  29.7 us
    pallas_call x1, Pallas kernels, core(): pl.pallas_call(kernel, out_shape=[half] * (2 * n_chunks) + [jax.ShapeDtyp...  24.4 us
  transfers between devices with their start and end apart: 38, of which 17 were waited for; matrix products, arithmetic and copies ran while one was open for 4% of the time, Pallas kernels for 2%

profile of v6, /device:TPU:0, one launch (start us, length us, event | category | flops | bytes accessed | tf_op | source)
XLA Modules:
  0.0 250.0 jit_solution(17857124412496898272)
XLA Ops:
  1.7 3.0 %collective-permute-start.2 = (bf16[2,128,1024]{2,1,0:T(8,128)(2,1)S(1)}, bf16[2,128,1024]{2,1,0:T(8,128)(2,1)S(1)}, u32[]{:S(2)}, u32[]{:S(2)}) collective-permute-start(bf16[2,128,1024]{2,1,0:T(8,128)(2,1)S(1)} %pad_maximum_fusion.refs_12_), channel_id=1, source_target_pairs={{0,8},{4,12},{8,0},{12,4},{1,9},{5,13},{9,1},{13,5},{2,10},{6,14},... | collective-permute-start | bytes 1572872 | tf_op jit(solution)/shard_map/tokens_0_2/ppermute | solution.py:100
  4.8 1.6 collective-permute-start.1
  6.3 10.3 %collective-permute-done.2.refs_14_ = bf16[2,128,1024]{2,1,0:T(8,128)(2,1)S(1)} collective-permute-done((bf16[2,128,1024]{2,1,0:T(8,128)(2,1)S(1)}, bf16[2,128,1024]{2,1,0:T(8,128)(2,1)S(1)}, u32[]{:S(2)}, u32[]{:S(2)}) %collective-permute-start.2) | collective-permute-done | bytes 524320 | tf_op jit(solution)/shard_map/tokens_0_2/ppermute | solution.py:100
  16.7 1.5 collective-permute-done.1.refs_8_
  18.5 2.7 %collective-permute-start = (bf16[2,128,1024]{2,1,0:T(8,128)(2,1)S(1)}, bf16[2,128,1024]{2,1,0:T(8,128)(2,1)}, u32[]{:S(2)}, u32[]{:S(2)}) collective-permute-start(bf16[2,128,1024]{2,1,0:T(8,128)(2,1)S(1)} %pad_maximum_fusion.refs_12_), channel_id=1, source_target_pairs={{0,2},{1,3},{2,0},{3,1},{4,6},{5,7},{6,4},{7,5},{8,10},{9,11},{10,... | collective-permute-start | bytes 1572872 | tf_op jit(solution)/shard_map/tokens_2/ppermute | solution.py:100
  21.2 2.6 %pack_weights.1 = (bf16[512,512]{1,0:T(8,128)(2,1)}, bf16[256,512]{1,0:T(8,128)(2,1)}, bf16[256,512]{1,0:T(8,128)(2,1)}) custom-call(bf16[256,2048]{1,0:T(8,128)(2,1)} %up_ref.3, bf16[2048,256]{1,0:T(8,128)(2,1)} %down_ref.3), custom_call_target="tpu_custom_call" | custom-call | bytes 4194304 | tf_op jit(solution)/shard_map/pack_weights/pallas_call | solution.py:129
  24.1 6.9 %collective-permute-done.6.refs_10_ = bf16[2,128,1024]{2,1,0:T(8,128)(2,1)S(1)} collective-permute-done((bf16[2,128,1024]{2,1,0:T(8,128)(2,1)S(1)}, bf16[2,128,1024]{2,1,0:T(8,128)(2,1)S(1)}, u32[]{:S(2)}, u32[]{:S(2)}) %collective-permute-start.6) | collective-permute-done | bytes 524320 | tf_op jit(solution)/shard_map/tokens_1_2/ppermute | solution.py:100
  31.0 20.1 %collective-permute-done.refs_4_ = bf16[2,128,1024]{2,1,0:T(8,128)(2,1)} collective-permute-done((bf16[2,128,1024]{2,1,0:T(8,128)(2,1)S(1)}, bf16[2,128,1024]{2,1,0:T(8,128)(2,1)}, u32[]{:S(2)}, u32[]{:S(2)}) %collective-permute-start) | collective-permute-done | bytes 524320 | tf_op jit(solution)/shard_map/tokens_2/ppermute | solution.py:100
  51.1 4.7 %collective-permute-done.5.rest_1_ = bf16[256,512]{1,0:T(8,128)(2,1)S(1)} collective-permute-done((bf16[256,512]{1,0:T(8,128)(2,1)}, bf16[256,512]{1,0:T(8,128)(2,1)S(1)}, u32[]{:S(2)}, u32[]{:S(2)}) %collective-permute-start.5) | collective-permute-done | bytes 262176 | tf_op jit(solution)/shard_map/weights_2/ppermute | solution.py:100
  57.1 2.7 %collective-permute-start.9 = (bf16[256,512]{1,0:T(8,128)(2,1)}, bf16[256,512]{1,0:T(8,128)(2,1)S(1)}, u32[]{:S(2)}, u32[]{:S(2)}) collective-permute-start(bf16[256,512]{1,0:T(8,128)(2,1)} %get-tuple-element.48), channel_id=1, source_target_pairs={{0,3},{1,2},{2,1},{3,0},{4,7},{5,6},{6,5},{7,4},{8,11},{9,10},{10,... | collective-permute-start | bytes 786440 | tf_op jit(solution)/shard_map/weights_3/ppermute | solution.py:100
  59.9 17.7 %collective-permute-done.9.rest_3_ = bf16[256,512]{1,0:T(8,128)(2,1)S(1)} collective-permute-done((bf16[256,512]{1,0:T(8,128)(2,1)}, bf16[256,512]{1,0:T(8,128)(2,1)S(1)}, u32[]{:S(2)}, u32[]{:S(2)}) %collective-permute-start.9) | collective-permute-done | bytes 262176 | tf_op jit(solution)/shard_map/weights_3/ppermute | solution.py:100
  77.5 1.6 collective-permute-start.13
  79.1 1.5 collective-permute-start.19
  81.2 7.2 %collective-permute-done.19.rest_4_ = bf16[256,512]{1,0:T(8,128)(2,1)S(1)} collective-permute-done((bf16[256,512]{1,0:T(8,128)(2,1)S(1)}, bf16[256,512]{1,0:T(8,128)(2,1)S(1)}, u32[]{:S(2)}, u32[]{:S(2)}) %collective-permute-start.19) | collective-permute-done | bytes 262176 | tf_op jit(solution)/shard_map/weights_3/ppermute | solution.py:100
  88.4 3.5 %collective-permute-done.18.rest_2_ = bf16[256,512]{1,0:T(8,128)(2,1)S(1)} collective-permute-done((bf16[256,512]{1,0:T(8,128)(2,1)S(1)}, bf16[256,512]{1,0:T(8,128)(2,1)S(1)}, u32[]{:S(2)}, u32[]{:S(2)}) %collective-permute-start.18) | collective-permute-done | bytes 262176 | tf_op jit(solution)/shard_map/weights_2/ppermute | solution.py:100
  92.4 3.3 %collective-permute-done.17.rest_0_ = bf16[512,512]{1,0:T(8,128)(2,1)S(1)} collective-permute-done((bf16[512,512]{1,0:T(8,128)(2,1)}, bf16[512,512]{1,0:T(8,128)(2,1)S(1)}, u32[]{:S(2)}, u32[]{:S(2)}) %collective-permute-start.17) | collective-permute-done | bytes 524320 | tf_op jit(solution)/shard_map/weights_1/ppermute | solution.py:100
  96.5 2.9 %unpack_weights.1 = (bf16[1024,512]{1,0:T(8,128)(2,1)}, bf16[512,1024]{1,0:T(8,128)(2,1)}) custom-call(bf16[256,2048]{1,0:T(8,128)(2,1)} %up_ref.3, bf16[2048,256]{1,0:T(8,128)(2,1)} %down_ref.3, bf16[512,512]{1,0:T(8,128)(2,1)} %copy-done.8, bf16[256,512]{1,0:T(8,128)(2,1)} %copy-done.10, bf16[256,512]{1,0:T(8,128)(2,1)} %copy-done.13, ...), custom_call_target="tpu_custom_call" | custom-call | bytes 8388608 | tf_op jit(solution)/shard_map/unpack_weights/pallas_call | solution.py:184
  99.6 24.4 %core.1 = (bf16[2,2,128,1024]{3,2,1,0:T(8,128)(2,1)}, bf16[2,2,128,1024]{3,2,1,0:T(8,128)(2,1)}, bf16[2,2,128,1024]{3,2,1,0:T(8,128)(2,1)}, bf16[2,2,128,1024]{3...) custom-call(bf16[2,128,1024]{2,1,0:T(8,128)(2,1)} %collective-permut, ...), custom_call_target="tpu_custom_call" | custom-call | flops 10737418240 | bytes 20971520 | tf_op jit(solution)/shard_map/core/pallas_call | solution.py:274
  125.2 2.4 collective-permute-done.23
  128.6 1.9 fusion.18
  133.0 11.8 %collective-permute-done.24 = bf16[2,128,1024]{2,1,0:T(8,128)(2,1)} collective-permute-done((bf16[2,128,1024]{2,1,0:T(8,128)(2,1)}, bf16[2,128,1024]{2,1,0:T(8,128)(2,1)}, u32[]{:S(2)}, u32[]{:S(2)}) %collective-permute-start.24) | collective-permute-done | bytes 524320 | tf_op jit(solution)/shard_map/sums_3_2/ppermute | solution.py:100
  145.3 1.6 fusion
  148.6 9.3 %collective-permute-done.25 = bf16[2,128,1024]{2,1,0:T(8,128)(2,1)S(1)} collective-permute-done((bf16[2,128,1024]{2,1,0:T(8,128)(2,1)S(1)}, bf16[2,128,1024]{2,1,0:T(8,128)(2,1)S(1)}, u32[]{:S(2)}, u32[]{:S(2)}) %collective-permute-start.25) | collective-permute-done | bytes 524320 | tf_op jit(solution)/shard_map/sums_2_2/ppermute | solution.py:100
  157.9 10.4 %collective-permute-done.28 = bf16[2,128,1024]{2,1,0:T(8,128)(2,1)S(1)} collective-permute-done((bf16[2,128,1024]{2,1,0:T(8,128)(2,1)S(1)}, bf16[2,128,1024]{2,1,0:T(8,128)(2,1)S(1)}, u32[]{:S(2)}, u32[]{:S(2)}) %collective-permute-start.28) | collective-permute-done | bytes 524320 | tf_op jit(solution)/shard_map/sums_3/ppermute | solution.py:100
  169.9 1.6 collective-permute-start.29
  172.3 1.9 collective-permute-start.36
  175.4 2.3 collective-permute-start.31
  177.7 39.9 %collective-permute-done.31 = f32[2,1024]{1,0:T(2,128)S(1)} collective-permute-done((f32[2,1024]{1,0:T(2,128)S(1)}, f32[2,1024]{1,0:T(2,128)S(1)}, u32[]{:S(2)}, u32[]{:S(2)}) %collective-permute-start.31) | collective-permute-done | bytes 8224 | tf_op jit(solution)/shard_map/stats/ppermute | solution.py:100
  217.7 1.6 collective-permute-start.27
  220.7 2.1 collective-permute-start.37
  223.0 11.1 %collective-permute-done.37 = f32[2,1024]{1,0:T(2,128)S(1)} collective-permute-done((f32[2,1024]{1,0:T(2,128)S(1)}, f32[2,1024]{1,0:T(2,128)S(1)}, u32[]{:S(2)}, u32[]{:S(2)}) %collective-permute-start.37) | collective-permute-done | bytes 8224 | tf_op jit(solution)/shard_map/stats/ppermute | solution.py:100
  235.5 11.0 %collective-permute-done.34 = bf16[512,512]{1,0:T(8,128)(2,1)S(1)} collective-permute-done((bf16[512,512]{1,0:T(8,128)(2,1)S(1)}, bf16[512,512]{1,0:T(8,128)(2,1)S(1)}, u32[]{:S(2)}, u32[]{:S(2)}) %collective-permute-start.34) | collective-permute-done | bytes 524320 | tf_op jit(solution)/shard_map/grads_1/ppermute | solution.py:100
  (139 shorter events, 21.7 us)
Async XLA Ops:
  1.7 15.0 %collective-permute-start.2 = (bf16[2,128,1024]{2,1,0:T(8,128)(2,1)S(1)}, bf16[2,128,1024]{2,1,0:T(8,128)(2,1)S(1)}, u32[]{:S(2)}, u32[]{:S(2)}) collective-permute-start(bf16[2,128,1024]{2,1,0:T(8,128)(2,1)S(1)} %pad_maximum_fusion.refs_12_), channel_id=1, source_target_pairs={{0,8},{4,12},{8,0},{12,4},{1,9},{5,13},{9,1},{13,5},{2,10},{6,14},... | collective-permute-start | bytes 1572872 | tf_op jit(solution)/shard_map/tokens_0_2/ppermute | solution.py:100
  4.8 13.4 %collective-permute-start.1 = (bf16[2,128,1024]{2,1,0:T(8,128)(2,1)S(1)}, bf16[2,128,1024]{2,1,0:T(8,128)(2,1)S(1)}, u32[]{:S(2)}, u32[]{:S(2)}) collective-permute-start(bf16[2,128,1024]{2,1,0:T(8,128)(2,1)S(1)} %pad_maximum_fusion.refs_12_), channel_id=1, source_target_pairs={{0,1},{1,0},{2,3},{3,2},{4,5},{5,4},{6,7},{7,6},{8,9},{9,8},{10,11... | collective-permute-start | bytes 1572872 | tf_op jit(solution)/shard_map/tokens_1/ppermute | solution.py:100
  6.3 17.5 %collective-permute-start.3 = (bf16[2,128,1024]{2,1,0:T(8,128)(2,1)S(1)}, bf16[2,128,1024]{2,1,0:T(8,128)(2,1)S(1)}, u32[]{:S(2)}, u32[]{:S(2)}) collective-permute-start(bf16[2,128,1024]{2,1,0:T(8,128)(2,1)S(1)} %pad_maximum_fusion.refs_12_), channel_id=1, source_target_pairs={{0,4},{4,0},{8,12},{12,8},{1,5},{5,1},{9,13},{13,9},{2,6},{6,2},{1... | collective-permute-start | bytes 1572872 | tf_op jit(solution)/shard_map/tokens_0_1/ppermute | solution.py:100
  18.1 12.9 %collective-permute-start.6 = (bf16[2,128,1024]{2,1,0:T(8,128)(2,1)S(1)}, bf16[2,128,1024]{2,1,0:T(8,128)(2,1)S(1)}, u32[]{:S(2)}, u32[]{:S(2)}) collective-permute-start(bf16[2,128,1024]{2,1,0:T(8,128)(2,1)S(1)} %collective-permute-done.1.refs_8_), channel_id=1, source_target_pairs={{0,8},{4,12},{8,0},{12,4},{1,9},{5,13},{9,1},{13,5},{2,10},{6,14},... | collective-permute-start | bytes 1572872 | tf_op jit(solution)/shard_map/tokens_1_2/ppermute | solution.py:100
  18.5 32.6 %collective-permute-start = (bf16[2,128,1024]{2,1,0:T(8,128)(2,1)S(1)}, bf16[2,128,1024]{2,1,0:T(8,128)(2,1)}, u32[]{:S(2)}, u32[]{:S(2)}) collective-permute-start(bf16[2,128,1024]{2,1,0:T(8,128)(2,1)S(1)} %pad_maximum_fusion.refs_12_), channel_id=1, source_target_pairs={{0,2},{1,3},{2,0},{3,1},{4,6},{5,7},{6,4},{7,5},{8,10},{9,11},{10,... | collective-permute-start | bytes 1572872 | tf_op jit(solution)/shard_map/tokens_2/ppermute | solution.py:100
  23.8 32.0 %collective-permute-start.5 = (bf16[256,512]{1,0:T(8,128)(2,1)}, bf16[256,512]{1,0:T(8,128)(2,1)S(1)}, u32[]{:S(2)}, u32[]{:S(2)}) collective-permute-start(bf16[256,512]{1,0:T(8,128)(2,1)} %get-tuple-element.44), channel_id=1, source_target_pairs={{0,2},{1,3},{2,0},{3,1},{4,6},{5,7},{6,4},{7,5},{8,10},{9,11},{10,... | collective-permute-start | bytes 786440 | tf_op jit(solution)/shard_map/weights_2/ppermute | solution.py:100
  24.1 35.8 %collective-permute-start.10 = (bf16[2,128,1024]{2,1,0:T(8,128)(2,1)S(1)}, bf16[2,128,1024]{2,1,0:T(8,128)(2,1)S(1)}, u32[]{:S(2)}, u32[]{:S(2)}) collective-permute-start(bf16[2,128,1024]{2,1,0:T(8,128)(2,1)S(1)} %collective-permute-done.1.refs_8_), channel_id=1, source_target_pairs={{0,4},{4,0},{8,12},{12,8},{1,5},{5,1},{9,13},{13,9},{2,6},{6,2},{1... | collective-permute-start | bytes 1572872 | tf_op jit(solution)/shard_map/tokens_1_1/ppermute | solution.py:100
  31.0 28.8 %collective-permute-start.11 = (bf16[2,128,1024]{2,1,0:T(8,128)(2,1)S(1)}, bf16[2,128,1024]{2,1,0:T(8,128)(2,1)S(1)}, u32[]{:S(2)}, u32[]{:S(2)}) collective-permute-start(bf16[2,128,1024]{2,1,0:T(8,128)(2,1)S(1)} %collective-permute-done.6.refs_10_), channel_id=1, source_target_pairs={{0,4},{4,0},{8,12},{12,8},{1,5},{5,1},{9,13},{13,9},{2,6},{6,2},{1... | collective-permute-start | bytes 1572872 | tf_op jit(solution)/shard_map/tokens_1_3/ppermute | solution.py:100
  55.9 21.7 %collective-permute-start.12 = (bf16[2,128,1024]{2,1,0:T(8,128)(2,1)}, bf16[2,128,1024]{2,1,0:T(8,128)(2,1)}, u32[]{:S(2)}, u32[]{:S(2)}) collective-permute-start(bf16[2,128,1024]{2,1,0:T(8,128)(2,1)} %collective-permute-done.refs_4_), channel_id=1, source_target_pairs={{0,8},{4,12},{8,0},{12,4},{1,9},{5,13},{9,1},{13,5},{2,10},{6,14},... | collective-permute-start | bytes 1572872 | tf_op jit(solution)/shard_map/tokens_2_2/ppermute | solution.py:100
  56.3 21.2 %collective-permute-start.7 = (bf16[2,128,1024]{2,1,0:T(8,128)(2,1)}, bf16[2,128,1024]{2,1,0:T(8,128)(2,1)}, u32[]{:S(2)}, u32[]{:S(2)}) collective-permute-start(bf16[2,128,1024]{2,1,0:T(8,128)(2,1)} %collective-permute-done.refs_4_), channel_id=1, source_target_pairs={{0,1},{1,0},{2,3},{3,2},{4,5},{5,4},{6,7},{7,6},{8,9},{9,8},{10,11... | collective-permute-start | bytes 1572872 | tf_op jit(solution)/shard_map/tokens_3/ppermute | solution.py:100
  57.1 20.4 %collective-permute-start.9 = (bf16[256,512]{1,0:T(8,128)(2,1)}, bf16[256,512]{1,0:T(8,128)(2,1)S(1)}, u32[]{:S(2)}, u32[]{:S(2)}) collective-permute-start(bf16[256,512]{1,0:T(8,128)(2,1)} %get-tuple-element.48), channel_id=1, source_target_pairs={{0,3},{1,2},{2,1},{3,0},{4,7},{5,6},{6,5},{7,4},{8,11},{9,10},{10,... | collective-permute-start | bytes 786440 | tf_op jit(solution)/shard_map/weights_3/ppermute | solution.py:100
  77.5 14.3 %collective-permute-start.13 = (bf16[2,128,1024]{2,1,0:T(8,128)(2,1)}, bf16[2,128,1024]{2,1,0:T(8,128)(2,1)}, u32[]{:S(2)}, u32[]{:S(2)}) collective-permute-start(bf16[2,128,1024]{2,1,0:T(8,128)(2,1)} %collective-permute-done.7.refs_0_), channel_id=1, source_target_pairs={{0,8},{4,12},{8,0},{12,4},{1,9},{5,13},{9,1},{13,5},{2,10},{6,14},... | collective-permute-start | bytes 1572872 | tf_op jit(solution)/shard_map/tokens_3_2/ppermute | solution.py:100
  79.1 9.2 %collective-permute-start.19 = (bf16[256,512]{1,0:T(8,128)(2,1)S(1)}, bf16[256,512]{1,0:T(8,128)(2,1)S(1)}, u32[]{:S(2)}, u32[]{:S(2)}) collective-permute-start(bf16[256,512]{1,0:T(8,128)(2,1)S(1)} %collective-permute-done.9.rest_3_), channel_id=1, source_target_pairs={{0,16},{16,0},{1,17},{17,1},{2,18},{18,2},{3,19},{19,3},{4,20},{20... | collective-permute-start | bytes 786440 | tf_op jit(solution)/shard_map/weights_3/ppermute | solution.py:100
  80.6 11.2 %collective-permute-start.18 = (bf16[256,512]{1,0:T(8,128)(2,1)S(1)}, bf16[256,512]{1,0:T(8,128)(2,1)S(1)}, u32[]{:S(2)}, u32[]{:S(2)}) collective-permute-start(bf16[256,512]{1,0:T(8,128)(2,1)S(1)} %collective-permute-done.5.rest_1_), channel_id=1, source_target_pairs={{0,16},{16,0},{1,17},{17,1},{2,18},{18,2},{3,19},{19,3},{4,20},{20... | collective-permute-start | bytes 786440 | tf_op jit(solution)/shard_map/weights_2/ppermute | solution.py:100
  81.2 18.3 %collective-permute-start.15 = (bf16[2,128,1024]{2,1,0:T(8,128)(2,1)}, bf16[2,128,1024]{2,1,0:T(8,128)(2,1)}, u32[]{:S(2)}, u32[]{:S(2)}) collective-permute-start(bf16[2,128,1024]{2,1,0:T(8,128)(2,1)} %collective-permute-done.refs_4_), channel_id=1, source_target_pairs={{0,4},{4,0},{8,12},{12,8},{1,5},{5,1},{9,13},{13,9},{2,6},{6,2},{1... | collective-permute-start | bytes 1572872 | tf_op jit(solution)/shard_map/tokens_2_1/ppermute | solution.py:100
  81.2 14.5 %collective-permute-start.17 = (bf16[512,512]{1,0:T(8,128)(2,1)}, bf16[512,512]{1,0:T(8,128)(2,1)S(1)}, u32[]{:S(2)}, u32[]{:S(2)}) collective-permute-start(bf16[512,512]{1,0:T(8,128)(2,1)} %get-tuple-element.51), channel_id=1, source_target_pairs={{0,1},{1,0},{2,3},{3,2},{4,5},{5,4},{6,7},{7,6},{8,9},{9,8},{10,11... | collective-permute-start | bytes 1572872 | tf_op jit(solution)/shard_map/weights_1/ppermute | solution.py:100
  88.4 11.1 %collective-permute-start.16 = (bf16[2,128,1024]{2,1,0:T(8,128)(2,1)}, bf16[2,128,1024]{2,1,0:T(8,128)(2,1)}, u32[]{:S(2)}, u32[]{:S(2)}) collective-permute-start(bf16[2,128,1024]{2,1,0:T(8,128)(2,1)} %collective-permute-done.12.refs_6_), channel_id=1, source_target_pairs={{0,4},{4,0},{8,12},{12,8},{1,5},{5,1},{9,13},{13,9},{2,6},{6,2},{1... | collective-permute-start | bytes 1572872 | tf_op jit(solution)/shard_map/tokens_2_3/ppermute | solution.py:100
  124.0 7.8 %collective-permute-start.22 = (bf16[2,2,128,1024]{3,2,1,0:T(8,128)(2,1)}, bf16[2,2,128,1024]{3,2,1,0:T(8,128)(2,1)}, u32[]{:S(2)}, u32[]{:S(2)}) collective-permute-start(bf16[2,2,128,1024]{3,2,1,0:T(8,128)(2,1)} %get-tuple-element.61), channel_id=1, source_target_pairs={{0,4},{4,0},{8,12},{12,8},{1,5},{5,1},{9,13},{13,9},{2,6},{6,2},{1... | collective-permute-start | bytes 3145736 | tf_op jit(solution)/shard_map/sums_2_1/ppermute | solution.py:100
  124.6 22.7 %collective-permute-start.20 = (bf16[2,2,128,1024]{3,2,1,0:T(8,128)(2,1)}, bf16[2,2,128,1024]{3,2,1,0:T(8,128)(2,1)S(1)}, u32[]{:S(2)}, u32[]{:S(2)}) collective-permute-start(bf16[2,2,128,1024]{3,2,1,0:T(8,128)(2,1)} %get-tuple-element.57), channel_id=1, source_target_pairs={{0,4},{4,0},{8,12},{12,8},{1,5},{5,1},{9,13},{13,9},{2,6},{6,2},{1... | collective-permute-start | bytes 3145736 | tf_op jit(solution)/shard_map/sums_0_1/ppermute | solution.py:100
  124.8 22.6 %collective-permute-start.21 = (bf16[2,2,128,1024]{3,2,1,0:T(8,128)(2,1)}, bf16[2,2,128,1024]{3,2,1,0:T(8,128)(2,1)}, u32[]{:S(2)}, u32[]{:S(2)}) collective-permute-start(bf16[2,2,128,1024]{3,2,1,0:T(8,128)(2,1)} %get-tuple-element.59), channel_id=1, source_target_pairs={{0,4},{4,0},{8,12},{12,8},{1,5},{5,1},{9,13},{13,9},{2,6},{6,2},{1... | collective-permute-start | bytes 3145736 | tf_op jit(solution)/shard_map/sums_1_1/ppermute | solution.py:100
  130.5 14.3 %collective-permute-start.24 = (bf16[2,128,1024]{2,1,0:T(8,128)(2,1)}, bf16[2,128,1024]{2,1,0:T(8,128)(2,1)}, u32[]{:S(2)}, u32[]{:S(2)}) collective-permute-start(bf16[2,128,1024]{2,1,0:T(8,128)(2,1)} %fusion.18), channel_id=1, source_target_pairs={{0,8},{4,12},{8,0},{12,4},{1,9},{5,13},{9,1},{13,5},{2,10},{6,14},... | collective-permute-start | bytes 1572872 | tf_op jit(solution)/shard_map/sums_3_2/ppermute | solution.py:100
  131.2 40.9 %collective-permute-start.35 = (bf16[512,512]{1,0:T(8,128)(2,1)}, bf16[512,512]{1,0:T(8,128)(2,1)S(1)}, u32[]{:S(2)}, u32[]{:S(2)}) collective-permute-start(bf16[512,512]{1,0:T(8,128)(2,1)} %get-tuple-element.76), channel_id=1, source_target_pairs={{0,2},{1,3},{2,0},{3,1},{4,6},{5,7},{6,4},{7,5},{8,10},{9,11},{10,... | collective-permute-start | bytes 1572872 | tf_op jit(solution)/shard_map/grads_2/ppermute | solution.py:100
  144.8 13.1 %collective-permute-start.25 = (bf16[2,128,1024]{2,1,0:T(8,128)(2,1)S(1)}, bf16[2,128,1024]{2,1,0:T(8,128)(2,1)S(1)}, u32[]{:S(2)}, u32[]{:S(2)}) collective-permute-start(bf16[2,128,1024]{2,1,0:T(8,128)(2,1)S(1)} %fusion.19), channel_id=1, source_target_pairs={{0,8},{4,12},{8,0},{12,4},{1,9},{5,13},{9,1},{13,5},{2,10},{6,14},... | collective-permute-start | bytes 1572872 | tf_op jit(solution)/shard_map/sums_2_2/ppermute | solution.py:100
  146.9 21.4 %collective-permute-start.28 = (bf16[2,128,1024]{2,1,0:T(8,128)(2,1)S(1)}, bf16[2,128,1024]{2,1,0:T(8,128)(2,1)S(1)}, u32[]{:S(2)}, u32[]{:S(2)}) collective-permute-start(bf16[2,128,1024]{2,1,0:T(8,128)(2,1)S(1)} %fusion), channel_id=1, source_target_pairs={{0,1},{1,0},{2,3},{3,2},{4,5},{5,4},{6,7},{7,6},{8,9},{9,8},{10,11... | collective-permute-start | bytes 1572872 | tf_op jit(solution)/shard_map/sums_3/ppermute | solution.py:100
  169.8 65.3 %collective-permute-start.33 = (bf16[2,128,1024]{2,1,0:T(8,128)(2,1)S(1)}, bf16[2,128,1024]{2,1,0:T(8,128)(2,1)S(1)}, u32[]{:S(2)}, u32[]{:S(2)}) collective-permute-start(bf16[2,128,1024]{2,1,0:T(8,128)(2,1)S(1)} %fusion.2), channel_id=1, source_target_pairs={{0,2},{1,3},{2,0},{3,1},{4,6},{5,7},{6,4},{7,5},{8,10},{9,11},{10,... | collective-permute-start | bytes 1572872 | tf_op jit(solution)/shard_map/sums_2/ppermute | solution.py:100
  171.4 46.3 %collective-permute-start.26 = (bf16[2,128,1024]{2,1,0:T(8,128)(2,1)S(1)}, bf16[2,128,1024]{2,1,0:T(8,128)(2,1)S(1)}, u32[]{:S(2)}, u32[]{:S(2)}) collective-permute-start(bf16[2,128,1024]{2,1,0:T(8,128)(2,1)S(1)} %fusion.20), channel_id=1, source_target_pairs={{0,8},{4,12},{8,0},{12,4},{1,9},{5,13},{9,1},{13,5},{2,10},{6,14},... | collective-permute-start | bytes 1572872 | tf_op jit(solution)/shard_map/sums_1_2/ppermute | solution.py:100
  172.3 74.4 %collective-permute-start.36 = (bf16[512,512]{1,0:T(8,128)(2,1)S(1)}, bf16[512,512]{1,0:T(8,128)(2,1)S(1)}, u32[]{:S(2)}, u32[]{:S(2)}) collective-permute-start(bf16[512,512]{1,0:T(8,128)(2,1)S(1)} %copy-done.18), channel_id=1, source_target_pairs={{0,3},{1,2},{2,1},{3,0},{4,7},{5,6},{6,5},{7,4},{8,11},{9,10},{10,... | collective-permute-start | bytes 1572872 | tf_op jit(solution)/shard_map/grads_3/ppermute | solution.py:100
  175.4 42.3 %collective-permute-start.31 = (f32[2,1024]{1,0:T(2,128)S(1)}, f32[2,1024]{1,0:T(2,128)S(1)}, u32[]{:S(2)}, u32[]{:S(2)}) collective-permute-start(f32[2,1024]{1,0:T(2,128)S(1)} %add.133), channel_id=1, source_target_pairs={{0,2},{1,3},{2,0},{3,1},{4,6},{5,7},{6,4},{7,5},{8,10},{9,11},{10,... | collective-permute-start | bytes 24584 | tf_op jit(solution)/shard_map/stats/ppermute | solution.py:100
  217.7 17.3 %collective-permute-start.27 = (bf16[2,128,1024]{2,1,0:T(8,128)(2,1)S(1)}, bf16[2,128,1024]{2,1,0:T(8,128)(2,1)S(1)}, u32[]{:S(2)}, u32[]{:S(2)}) collective-permute-start(bf16[2,128,1024]{2,1,0:T(8,128)(2,1)S(1)} %fusion.21), channel_id=1, source_target_pairs={{0,8},{4,12},{8,0},{12,4},{1,9},{5,13},{9,1},{13,5},{2,10},{6,14},... | collective-permute-start | bytes 1572872 | tf_op jit(solution)/shard_map/sums_0_2/ppermute | solution.py:100
  220.6 14.4 %collective-permute-start.32 = (bf16[2,128,1024]{2,1,0:T(8,128)(2,1)S(1)}, bf16[2,128,1024]{2,1,0:T(8,128)(2,1)S(1)}, u32[]{:S(2)}, u32[]{:S(2)}) collective-permute-start(bf16[2,128,1024]{2,1,0:T(8,128)(2,1)S(1)} %fusion.3), channel_id=1, source_target_pairs={{0,1},{1,0},{2,3},{3,2},{4,5},{5,4},{6,7},{7,6},{8,9},{9,8},{10,11... | collective-permute-start | bytes 1572872 | tf_op jit(solution)/shard_map/sums_1/ppermute | solution.py:100
  220.7 13.4 %collective-permute-start.37 = (f32[2,1024]{1,0:T(2,128)S(1)}, f32[2,1024]{1,0:T(2,128)S(1)}, u32[]{:S(2)}, u32[]{:S(2)}) collective-permute-start(f32[2,1024]{1,0:T(2,128)S(1)} %add.134), channel_id=1, source_target_pairs={{0,1},{1,0},{2,3},{3,2},{4,5},{5,4},{6,7},{7,6},{8,9},{9,8},{10,11... | collective-permute-start | bytes 24584 | tf_op jit(solution)/shard_map/stats/ppermute | solution.py:100
  234.1 12.4 %collective-permute-start.34 = (bf16[512,512]{1,0:T(8,128)(2,1)S(1)}, bf16[512,512]{1,0:T(8,128)(2,1)S(1)}, u32[]{:S(2)}, u32[]{:S(2)}) collective-permute-start(bf16[512,512]{1,0:T(8,128)(2,1)S(1)} %copy-done.19), channel_id=1, source_target_pairs={{0,1},{1,0},{2,3},{3,2},{4,5},{5,4},{6,7},{7,6},{8,9},{9,8},{10,11... | collective-permute-start | bytes 1572872 | tf_op jit(solution)/shard_map/grads_1/ppermute | solution.py:100
  (33 other events, 702.3 us)

commit v7 on v6

--- a/solution.py
+++ b/solution.py
@@ -334,36 +334,39 @@
     def tokens_tensor(k, *first):
         start = after(tokens[k], *first)
         chunks[k] = {0: tokens[k], high: swap(start, "tensor", high, f"tokens_{k}_{high}")}
+
+    def weights_dp(k, *first):
+        got[k] = swap(after(sends[k - 1], *first), "dp", k, f"weights_{k}")
+
+    def weights_groups(k, *first):
+        crossed[k] = swap(after(got[k], *first), "groups", 1, f"weights_{k}")
+
+    def tokens_rest(k, *first):
         for bit in others:
             for j in list(chunks[k]):
-                chunks[k][j | bit] = swap(chunks[k][j], "tensor", bit, f"tokens_{k}_{j | bit}")
-
-    def weights_dp(k, *first):
-        got[k] = swap(after(sends[k - 1], *first), "dp", k, f"weights_{k}")
-
-    def weights_groups(k, *first):
-        crossed[k] = swap(after(got[k], *first), "groups", 1, f"weights_{k}")
+                piece = after(chunks[k][j], *first)
+                chunks[k][j | bit] = swap(piece, "tensor", bit, f"tokens_{k}_{j | bit}")
 
     tokens_tensor(0)
-    for bit in bits_of(n_dp)[:0:-1]:
+    for bit in reversed(bits_of(n_dp)):
         tokens_dp(bit)
     sends = pack_weights(w_up, w_down, mates)
-    tokens_dp(top)
-    stage = [tokens[1], *chunks[0].values()]
+    for bit in bits_of(n_dp):
+        weights_dp(bit)
     tokens_tensor(1, tokens[1], chunks[0][high])
-    weights_dp(top, *stage)
-    stage = [tokens[top], got[top], chunks[1][high], *chunks[0].values()]
+    stage = [*tokens.values(), *got.values(), chunks[0][high]]
+    tokens_rest(0, *stage)
     for k in range(2, n_dp):
         if k & (k - 1):
             tokens_dp(k, *stage)
             weights_dp(k, *stage)
-            stage = [tokens[k], got[k], *chunks[k - 2].values(), chunks[k - 1][high]]
-        tokens_tensor(k, *stage)
-    for k in range(1, n_dp):
-        if k < top:
-            weights_dp(k, *stage)
-        elif mates == 2:
-            weights_groups(k, *stage)
+            stage = [tokens[k], got[k], chunks[k - 1][high], *chunks[0].values()]
+        tokens_tensor(k, *stage, chunks[k - 1][high])
+        tokens_rest(k - 1, *stage)
+    tokens_rest(n_dp - 1)
+    if mates == 2:
+        for k in range(top, n_dp):
+            weights_groups(k, *(stage if k == top else []))
     got = {k: [got[k]] + ([crossed[k]] if k in crossed else []) for k in got}
     up, down = unpack_weights(w_up, w_down, got, mates)
 
@@ -374,7 +377,7 @@
     blocks = dict(enumerate(blocks))
     blocks[top] = swap(blocks[top], "dp", top, f"grads_{top}")
 
-    sums, behind = {}, ()
+    sums, behind, hops = {}, (), []
     for k, (even, odd) in zip(order, halves, strict=True):
         came = swap(odd, "tensor", 1, f"sums_{k}_1")
         parts = {2 * j: (even[j], came[j]) for j in range(n_tensor // 2)}
@@ -383,10 +386,16 @@
                 send = after(sum(parts.pop(j)), *behind)
                 parts[j ^ bit] += (swap(send, "tensor", bit, f"sums_{k}_{j}"),)
                 behind = parts[j ^ bit][-1:]
+                hops += behind
         sums[k] = parts[0]
 
     def add(terms, dtype=jnp.bfloat16):
         return sum(term.astype(jnp.float32) for term in terms).astype(dtype)
+
+    for bit in bits_of(n_tensor):
+        stats = stats + swap(stats, "tensor", bit, "stats")
+    stats = {0: stats.astype(jnp.bfloat16)}
+    extra = 16
 
     came = {}
     for bit in bits_of(n_dp)[::-1]:
@@ -394,26 +403,29 @@
             came[k] = swap(add(sums.pop(k)), "dp", bit, f"sums_{k}")
             sums[k ^ bit] += (came[k],)
     last = add(sums[top])
+    rows = jnp.pad(stats[0][:, None], ((0, 0), (0, extra - 1), (0, 0)))
+    last = jnp.concatenate([last, rows], axis=1)
     came[top] = swap(last, "dp", top, f"sums_{top}")
-    stats = after(stats, came[order[0]])
-    for bit in bits_of(n_tensor):
-        stats = stats + swap(stats, "tensor", bit, "stats")
-    stats = after(stats, last)
-    for bit in bits_of(n_dp):
-        stats = stats + swap(stats, "dp", bit, "stats")
-        if bit == top:
-            first = stats
+    came[top], stats[top] = came[top][:, :own_rows], came[top][:, own_rows]
+    rows = stats[0].reshape(-1, units)
+    rows = jnp.pad(rows, ((0, extra - rows.shape[0]), (0, 0)))
+    for k in range(1, n_dp):
+        if k != top:
+            block = jnp.concatenate([blocks[k], rows])
+            first = [last] if k < top else [blocks[top], *hops[1:2]]
+            block = swap(after(block, *first), "dp", k, f"grads_{k}")
+            blocks[k], rest = block[: 2 * depth], block[2 * depth :]
+            stats[k] = rest[: stats[0].size // units].reshape(stats[0].shape)
     for bit in bits_of(n_dp)[:0:-1]:
-        came[bit] = swap(after(add(sums[bit]), last, first), "dp", bit, f"sums_{bit}")
+        came[bit] = swap(after(add(sums[bit]), last), "dp", bit, f"sums_{bit}")
     total = add((*sums[0], *(came[bit] for bit in bits_of(n_dp)[::-1])), jnp.float32)
     sums = {0: total}
-    for k in range(1, n_dp):
-        if k < top:
-            blocks[k] = swap(after(blocks[k], last, first), "dp", k, f"grads_{k}")
-        elif k > top:
-            blocks[k] = swap(after(blocks[k], blocks[top], last), "dp", k, f"grads_{k}")
     for k in range(n_dp):
-        blocks[k] = after(blocks[k], last if k in (0, top) else total)
+        blocks[k] = after(blocks[k], last if k in (0, top) else hops[-1])
+    stats = [stats[k].astype(jnp.float32) for k in range(n_dp)]
+    while len(stats) > 1:
+        stats = [one + two for one, two in zip(stats[0::2], stats[1::2], strict=True)]
+    stats = stats[0]
     branch, grad_normed = sums[0][0], sums[0][1]
     second_in, grad_first_in = finish_rows(
         branch, grad_normed, second_out, grad_first, first_out, norm_gain, norm_bias
@@ -440,6 +452,7 @@
     few_tokens = first_out.shape[0] * n_tensor < w_up.shape[1]
     units, depth = w_up.shape[1] // n_dp, w_up.shape[0]
     fits = w_up.shape[1] % n_dp == 0 and units % depth == 0 and depth % 128 == 0
+    fits = fits and first_out.shape[1] % units == 0 and first_out.shape[1] <= 8 * units
     pick = gather_tokens_body if powers and few_tokens and fits else gather_weights_body
     return pick(first_out, second_out, grad_first, grad_second, w_up, *rest)
 

time: 251 us -> 220 us (0.88)
  waiting for transfers between devices: 172 us -> 102 us
  other arithmetic: 13.2 us -> 31.1 us
  local copies, waits for them, and re-layouts: 3.95 us -> 20.9 us
  starting transfers between devices: 29.7 us -> 34.7 us
    ppermute x38 -> x36, waiting for transfers between devices: 172 us -> 102 us  [swap(): lax.ppermute(values, axis, [(i, i ^ mask) for i in range(lax.axis_size(ax...]
    pallas_call x0 -> x8, local copies, waits for them, and re-layouts: none -> 14.1 us  [core(): pl.pallas_call(kernel, out_shape=[half] * (2 * n_chunks) + [jax.ShapeDtyp...]
    ppermute x38 -> x36, starting transfers between devices: 29.7 us -> 34.7 us  [swap(): lax.ppermute(values, axis, [(i, i ^ mask) for i in range(lax.axis_size(ax...]
    add x4, other arithmetic: 4.27 us -> 7.95 us  [gather_tokens_body(): send = after(sum(parts.pop(j)), *behind)]
    concatenate x0 -> x2, other arithmetic: none -> 3.49 us  [the longest x1 2.18 us: gather_tokens_body(): block = jnp.concatenate([blocks[k], rows])]
    dynamic_update_slice x4, other arithmetic: 0.17 us -> 3.31 us  [gather_tokens_body(): lax.dynamic_update_slice_in_dim(grad_down, jnp.concatenate(strips, axis=0...]
    convert_element_type x3, other arithmetic: 4.34 us -> 7.18 us  [add(): return sum((term.astype(jnp.float32) for term in terms)).astype(dtype)]
  transfers between devices with their start and end apart: 38 -> 36, of which waited for: 17 -> 13; matrix products, arithmetic and copies ran while one was open for 4% -> 17% of each run, Pallas kernels for 2% -> 3%
where the time goes in v7:
time: 220 us
  waiting for transfers between devices  102 us (46%)
  starting transfers between devices  34.7 us (16%)
  other arithmetic  31.1 us (14%)
  Pallas kernels  29.8 us (14%)
  local copies, waits for them, and re-layouts  20.9 us (10%)
    ppermute x36, waiting for transfers between devices, swap(): lax.ppermute(values, axis, [(i, i ^ mask) for i in range(lax.axis_size(ax...  102 us
    ppermute x36, starting transfers between devices, swap(): lax.ppermute(values, axis, [(i, i ^ mask) for i in range(lax.axis_size(ax...  34.7 us
    pallas_call x1, Pallas kernels, core(): pl.pallas_call(kernel, out_shape=[half] * (2 * n_chunks) + [jax.ShapeDtyp...  24.3 us
    pallas_call x8, local copies, waits for them, and re-layouts, core(): pl.pallas_call(kernel, out_shape=[half] * (2 * n_chunks) + [jax.ShapeDtyp...  14.1 us
    add x4, other arithmetic, gather_tokens_body(): send = after(sum(parts.pop(j)), *behind)  7.95 us
    convert_element_type x3, other arithmetic, add(): return sum((term.astype(jnp.float32) for term in terms)).astype(dtype)  7.18 us
  transfers between devices with their start and end apart: 36, of which 13 were waited for; matrix products, arithmetic and copies ran while one was open for 17% of the time, Pallas kernels for 3%

profile of v7, /device:TPU:0, one launch (start us, length us, event | category | flops | bytes accessed | tf_op | source)
XLA Modules:
  0.0 219.6 jit_solution(453912745343641447)
XLA Ops:
  1.7 3.0 %collective-permute-start.4 = (bf16[2,128,1024]{2,1,0:T(8,128)(2,1)S(1)}, bf16[2,128,1024]{2,1,0:T(8,128)(2,1)S(1)}, u32[]{:S(2)}, u32[]{:S(2)}) collective-permute-start(bf16[2,128,1024]{2,1,0:T(8,128)(2,1)S(1)} %pad_maximum_fusion.refs_12_), channel_id=1, source_target_pairs={{0,8},{4,12},{8,0},{12,4},{1,9},{5,13},{9,1},{13,5},{2,10},{6,14},... | collective-permute-start | bytes 1572872 | tf_op jit(solution)/shard_map/tokens_0_2/ppermute | solution.py:100
  6.3 2.6 %collective-permute-start = (bf16[2,128,1024]{2,1,0:T(8,128)(2,1)S(1)}, bf16[2,128,1024]{2,1,0:T(8,128)(2,1)S(1)}, u32[]{:S(2)}, u32[]{:S(2)}) collective-permute-start(bf16[2,128,1024]{2,1,0:T(8,128)(2,1)S(1)} %pad_maximum_fusion.refs_12_), channel_id=1, source_target_pairs={{0,2},{1,3},{2,0},{3,1},{4,6},{5,7},{6,4},{7,5},{8,10},{9,11},{10,... | collective-permute-start | bytes 1572872 | tf_op jit(solution)/shard_map/tokens_2/ppermute | solution.py:100
  8.9 2.6 %pack_weights.1 = (bf16[512,512]{1,0:T(8,128)(2,1)}, bf16[256,512]{1,0:T(8,128)(2,1)}, bf16[256,512]{1,0:T(8,128)(2,1)}) custom-call(bf16[256,2048]{1,0:T(8,128)(2,1)} %up_ref.3, bf16[2048,256]{1,0:T(8,128)(2,1)} %down_ref.3), custom_call_target="tpu_custom_call" | custom-call | bytes 4194304 | tf_op jit(solution)/shard_map/pack_weights/pallas_call | solution.py:129
  11.9 4.7 %collective-permute-done.4.refs_14_ = bf16[2,128,1024]{2,1,0:T(8,128)(2,1)S(1)} collective-permute-done((bf16[2,128,1024]{2,1,0:T(8,128)(2,1)S(1)}, bf16[2,128,1024]{2,1,0:T(8,128)(2,1)S(1)}, u32[]{:S(2)}, u32[]{:S(2)}) %collective-permute-start.4) | collective-permute-done | bytes 524320 | tf_op jit(solution)/shard_map/tokens_0_2/ppermute | solution.py:100
  16.7 14.2 %collective-permute-done.1.refs_8_ = bf16[2,128,1024]{2,1,0:T(8,128)(2,1)S(1)} collective-permute-done((bf16[2,128,1024]{2,1,0:T(8,128)(2,1)S(1)}, bf16[2,128,1024]{2,1,0:T(8,128)(2,1)S(1)}, u32[]{:S(2)}, u32[]{:S(2)}) %collective-permute-start.1) | collective-permute-done | bytes 524320 | tf_op jit(solution)/shard_map/tokens_1/ppermute | solution.py:100
  32.6 12.9 %collective-permute-done.2.rest_1_ = bf16[256,512]{1,0:T(8,128)(2,1)S(1)} collective-permute-done((bf16[256,512]{1,0:T(8,128)(2,1)}, bf16[256,512]{1,0:T(8,128)(2,1)S(1)}, u32[]{:S(2)}, u32[]{:S(2)}) %collective-permute-start.2) | collective-permute-done | bytes 262176 | tf_op jit(solution)/shard_map/weights_2/ppermute | solution.py:100
  46.2 2.7 %collective-permute-start.5 = (bf16[2,128,1024]{2,1,0:T(8,128)(2,1)S(1)}, bf16[2,128,1024]{2,1,0:T(8,128)(2,1)}, u32[]{:S(2)}, u32[]{:S(2)}) collective-permute-start(bf16[2,128,1024]{2,1,0:T(8,128)(2,1)S(1)} %collective-permute-done.refs_4_), channel_id=1, source_target_pairs={{0,1},{1,0},{2,3},{3,2},{4,5},{5,4},{6,7},{7,6},{8,9},{9,8},{10,11... | collective-permute-start | bytes 1572872 | tf_op jit(solution)/shard_map/tokens_3/ppermute | solution.py:100
  51.3 15.1 %collective-permute-done.7.rest_3_ = bf16[256,512]{1,0:T(8,128)(2,1)S(1)} collective-permute-done((bf16[256,512]{1,0:T(8,128)(2,1)}, bf16[256,512]{1,0:T(8,128)(2,1)S(1)}, u32[]{:S(2)}, u32[]{:S(2)}) %collective-permute-start.7) | collective-permute-done | bytes 262176 | tf_op jit(solution)/shard_map/weights_3/ppermute | solution.py:100
  69.1 9.4 %collective-permute-done.12.refs_2_ = bf16[2,128,1024]{2,1,0:T(8,128)(2,1)} collective-permute-done((bf16[2,128,1024]{2,1,0:T(8,128)(2,1)}, bf16[2,128,1024]{2,1,0:T(8,128)(2,1)}, u32[]{:S(2)}, u32[]{:S(2)}) %collective-permute-start.12) | collective-permute-done | bytes 524320 | tf_op jit(solution)/shard_map/tokens_3_2/ppermute | solution.py:100
  79.1 2.3 %collective-permute-done.18.rest_2_ = bf16[256,512]{1,0:T(8,128)(2,1)S(1)} collective-permute-done((bf16[256,512]{1,0:T(8,128)(2,1)S(1)}, bf16[256,512]{1,0:T(8,128)(2,1)S(1)}, u32[]{:S(2)}, u32[]{:S(2)}) %collective-permute-start.18) | collective-permute-done | bytes 262176 | tf_op jit(solution)/shard_map/weights_2/ppermute | solution.py:100
  82.1 2.9 %unpack_weights.1 = (bf16[1024,512]{1,0:T(8,128)(2,1)}, bf16[512,1024]{1,0:T(8,128)(2,1)}) custom-call(bf16[256,2048]{1,0:T(8,128)(2,1)} %up_ref.3, bf16[2048,256]{1,0:T(8,128)(2,1)} %down_ref.3, bf16[512,512]{1,0:T(8,128)(2,1)} %copy-done.17, bf16[256,512]{1,0:T(8,128)(2,1)} %copy-done.19, bf16[256,512]{1,0:T(8,128)(2,1)} %copy-done.22, ...), custom_call_target="tpu_custom_call" | custom-call | bytes 8388608 | tf_op jit(solution)/shard_map/unpack_weights/pallas_call | solution.py:184
  85.1 24.3 %core.1 = (bf16[2,2,128,1024]{3,2,1,0:T(8,128)(2,1)}, bf16[2,2,128,1024]{3,2,1,0:T(8,128)(2,1)}, bf16[2,2,128,1024]{3,2,1,0:T(8,128)(2,1)}, bf16[2,2,128,1024]{3...) custom-call(bf16[2,128,1024]{2,1,0:T(8,128)(2,1)} %collective-permut, ...), custom_call_target="tpu_custom_call" | custom-call | flops 10737418240 | bytes 20971520 | tf_op jit(solution)/shard_map/core/pallas_call | solution.py:274
  109.5 3.4 %copy.21 = bf16[2,2,128,1024]{3,1,2,0:T(2,128)(2,1)} copy(bf16[2,2,128,1024]{3,2,1,0:T(8,128)(2,1)} %get-tuple-element.69) | data formatting | bytes 2097152 | tf_op jit(solution)/shard_map/core/pallas_call | solution.py:274
  113.0 2.0 copy.19
  119.7 2.0 copy.14
  122.8 2.3 %copy.17 = bf16[2,2,128,1024]{3,1,2,0:T(2,128)(2,1)} copy(bf16[2,2,128,1024]{3,2,1,0:T(8,128)(2,1)S(1)} %copy-done.8) | data formatting | bytes 2097152 | tf_op jit(solution)/shard_map/core/pallas_call | solution.py:274
  126.9 2.4 %fusion.19 = bf16[2,128,1024]{2,0,1:T(2,128)(2,1)} fusion(bf16[2,2,128,1024]{3,1,2,0:T(2,128)(2,1)} %collective-permute-done.23, bf16[2,2,128,1024]{3,1,2,0:T(2,128)(2,1)S(1)} %copy.20), kind=kLoop, calls=%fused_computation.36 | loop fusion | flops 262144 | bytes 1572864 | tf_op jit(solution)/shard_map/add | solution.py:386
  129.8 2.2 fusion.13
  133.6 10.3 %collective-permute-done.24 = bf16[2,128,1024]{2,0,1:T(2,128)(2,1)} collective-permute-done((bf16[2,128,1024]{2,0,1:T(2,128)(2,1)}, bf16[2,128,1024]{2,0,1:T(2,128)(2,1)}, u32[]{:S(2)}, u32[]{:S(2)}) %collective-permute-start.24) | collective-permute-done | bytes 524320 | tf_op jit(solution)/shard_map/sums_3_2/ppermute | solution.py:100
  144.4 2.4 %fusion.1 = bf16[2,128,1024]{2,0,1:T(2,128)(2,1)S(1)} fusion(bf16[2,128,1024]{2,0,1:T(2,128)(2,1)} %collective-permute-done.24, bf16[2,2,128,1024]{3,1,2,0:T(2,128)(2,1)} %collective-permute-done.23, bf16[2,2,128,1024]{3,1,2,0:T(2,128)(2,1)S(1)} %copy-done.2), kind=kLoop, calls=%fused_computation.4 | loop fusion | flops 1572864 | bytes 2097152 | tf_op jit(solution)/shard_map/convert_element_type | solution.py:393
  146.8 3.0 %collective-permute-start.28 = (bf16[2,128,1024]{2,0,1:T(2,128)(2,1)S(1)}, bf16[2,128,1024]{2,0,1:T(2,128)(2,1)S(1)}, u32[]{:S(2)}, u32[]{:S(2)}) collective-permute-start(bf16[2,128,1024]{2,0,1:T(2,128)(2,1)S(1)} %fusion.1), channel_id=1, source_target_pairs={{0,1},{1,0},{2,3},{3,2},{4,5},{5,4},{6,7},{7,6},{8,9},{9,8},{10,11... | collective-permute-start | bytes 1572872 | tf_op jit(solution)/shard_map/sums_3/ppermute | solution.py:100
  149.9 2.4 %fusion.22 = bf16[2,128,1024]{2,0,1:T(2,128)(2,1)} fusion(bf16[2,2,128,1024]{3,1,2,0:T(2,128)(2,1)} %collective-permute-done.20, bf16[2,2,128,1024]{3,1,2,0:T(2,128)(2,1)S(1)} %copy.13), kind=kLoop, calls=%fused_computation.42 | loop fusion | flops 262144 | bytes 1572864 | tf_op jit(solution)/shard_map/add | solution.py:386
  153.9 3.5 %collective-permute-done.25 = bf16[2,128,1024]{2,0,1:T(2,128)(2,1)S(1)} collective-permute-done((bf16[2,128,1024]{2,0,1:T(2,128)(2,1)S(1)}, bf16[2,128,1024]{2,0,1:T(2,128)(2,1)S(1)}, u32[]{:S(2)}, u32[]{:S(2)}) %collective-permute-start.25) | collective-permute-done | bytes 524320 | tf_op jit(solution)/shard_map/sums_2_2/ppermute | solution.py:100
  157.4 2.4 %collective-permute-start.35 = (bf16[528,512]{1,0:T(8,128)(2,1)S(1)}, bf16[528,512]{1,0:T(8,128)(2,1)S(1)}, u32[]{:S(2)}, u32[]{:S(2)}) collective-permute-start(bf16[528,512]{1,0:T(8,128)(2,1)S(1)} %get-tuple-element.83), channel_id=1, source_target_pairs={{0,3},{1,2},{2,1},{3,0},{4,7},{5,6},{6,5},{7,4},{8,11},{9,10},{10,... | collective-permute-start | bytes 1622024 | tf_op jit(solution)/shard_map/grads_3/ppermute | solution.py:100
  159.9 2.4 %collective-permute-done.28 = bf16[2,128,1024]{2,0,1:T(2,128)(2,1)S(1)} collective-permute-done((bf16[2,128,1024]{2,0,1:T(2,128)(2,1)S(1)}, bf16[2,128,1024]{2,0,1:T(2,128)(2,1)S(1)}, u32[]{:S(2)}, u32[]{:S(2)}) %collective-permute-start.28) | collective-permute-done | bytes 524320 | tf_op jit(solution)/shard_map/sums_3/ppermute | solution.py:100
  162.2 2.1 fusion.3
  165.7 2.4 %collective-permute-start.32 = (bf16[2,144,1024]{2,0,1:T(2,128)(2,1)}, bf16[2,144,1024]{2,0,1:T(2,128)(2,1)}, u32[]{:S(2)}, u32[]{:S(2)}) collective-permute-start(bf16[2,144,1024]{2,0,1:T(2,128)(2,1)} %fusion.11), channel_id=1, source_target_pairs={{0,2},{1,3},{2,0},{3,1},{4,6},{5,7},{6,4},{7,5},{8,10},{9,11},{10,... | collective-permute-start | bytes 1769480 | tf_op jit(solution)/shard_map/sums_2/ppermute | solution.py:100
  174.6 5.5 %collective-permute-done.26 = bf16[2,128,1024]{2,0,1:T(2,128)(2,1)S(1)} collective-permute-done((bf16[2,128,1024]{2,0,1:T(2,128)(2,1)S(1)}, bf16[2,128,1024]{2,0,1:T(2,128)(2,1)S(1)}, u32[]{:S(2)}, u32[]{:S(2)}) %collective-permute-start.26) | collective-permute-done | bytes 524320 | tf_op jit(solution)/shard_map/sums_1_2/ppermute | solution.py:100
  181.7 2.6 %fusion.4 = bf16[2,128,1024]{2,0,1:T(2,128)(2,1)} fusion(bf16[2,128,1024]{2,0,1:T(2,128)(2,1)S(1)} %collective-permute-done.26, bf16[2,2,128,1024]{3,1,2,0:T(2,128)(2,1)} %collective-permute-done.21, bf16[2,2,128,1024]{3,1,2,0:T(2,128)(2,1)S(1)} %copy.16), kind=kLoop, calls=%fused_computation.9 | loop fusion | flops 1572864 | bytes 2097152 | tf_op jit(solution)/shard_map/convert_element_type | solution.py:393
  187.2 11.0 %collective-permute-done.33 = bf16[528,512]{1,0:T(8,128)(2,1)} collective-permute-done((bf16[528,512]{1,0:T(8,128)(2,1)}, bf16[528,512]{1,0:T(8,128)(2,1)}, u32[]{:S(2)}, u32[]{:S(2)}) %collective-permute-start.33) | collective-permute-done | bytes 540704 | tf_op jit(solution)/shard_map/grads_1/ppermute | solution.py:100
  200.1 9.6 %collective-permute-done.32 = bf16[2,144,1024]{2,0,1:T(2,128)(2,1)} collective-permute-done((bf16[2,144,1024]{2,0,1:T(2,128)(2,1)}, bf16[2,144,1024]{2,0,1:T(2,128)(2,1)}, u32[]{:S(2)}, u32[]{:S(2)}) %collective-permute-start.32) | collective-permute-done | bytes 589856 | tf_op jit(solution)/shard_map/sums_2/ppermute | solution.py:100
  211.4 2.7 %fusion.6 = f32[2,128,1024]{2,0,1:T(2,128)S(1)} fusion(bf16[2,128,1024]{2,0,1:T(2,128)(2,1)} %collective-permute-done.31, bf16[2,128,1024]{2,0,1:T(2,128)(2,1)} %collective-permute-done.27, bf16[2,144,1024]{2,0,1:T(2,128)(2,1)} %collective-permute-done.32, bf16[2,2,128,1024]{3,1,2,0:T(2,128)(2,1)} %collective-permute-done.20, ...), kind=kLoop, calls=%fused_computation.12 | loop fusion | flops 2359296 | bytes 3670016 | tf_op jit(solution)/shard_map/add | solution.py:393
  (166 shorter events, 44.7 us)
Async XLA Ops:
  1.7 15.0 %collective-permute-start.4 = (bf16[2,128,1024]{2,1,0:T(8,128)(2,1)S(1)}, bf16[2,128,1024]{2,1,0:T(8,128)(2,1)S(1)}, u32[]{:S(2)}, u32[]{:S(2)}) collective-permute-start(bf16[2,128,1024]{2,1,0:T(8,128)(2,1)S(1)} %pad_maximum_fusion.refs_12_), channel_id=1, source_target_pairs={{0,8},{4,12},{8,0},{12,4},{1,9},{5,13},{9,1},{13,5},{2,10},{6,14},... | collective-permute-start | bytes 1572872 | tf_op jit(solution)/shard_map/tokens_0_2/ppermute | solution.py:100
  4.8 26.1 %collective-permute-start.1 = (bf16[2,128,1024]{2,1,0:T(8,128)(2,1)S(1)}, bf16[2,128,1024]{2,1,0:T(8,128)(2,1)S(1)}, u32[]{:S(2)}, u32[]{:S(2)}) collective-permute-start(bf16[2,128,1024]{2,1,0:T(8,128)(2,1)S(1)} %pad_maximum_fusion.refs_12_), channel_id=1, source_target_pairs={{0,1},{1,0},{2,3},{3,2},{4,5},{5,4},{6,7},{7,6},{8,9},{9,8},{10,11... | collective-permute-start | bytes 1572872 | tf_op jit(solution)/shard_map/tokens_1/ppermute | solution.py:100
  6.3 39.1 %collective-permute-start = (bf16[2,128,1024]{2,1,0:T(8,128)(2,1)S(1)}, bf16[2,128,1024]{2,1,0:T(8,128)(2,1)S(1)}, u32[]{:S(2)}, u32[]{:S(2)}) collective-permute-start(bf16[2,128,1024]{2,1,0:T(8,128)(2,1)S(1)} %pad_maximum_fusion.refs_12_), channel_id=1, source_target_pairs={{0,2},{1,3},{2,0},{3,1},{4,6},{5,7},{6,4},{7,5},{8,10},{9,11},{10,... | collective-permute-start | bytes 1572872 | tf_op jit(solution)/shard_map/tokens_2/ppermute | solution.py:100
  11.5 34.7 %collective-permute-start.3 = (bf16[512,512]{1,0:T(8,128)(2,1)}, bf16[512,512]{1,0:T(8,128)(2,1)S(1)}, u32[]{:S(2)}, u32[]{:S(2)}) collective-permute-start(bf16[512,512]{1,0:T(8,128)(2,1)} %get-tuple-element.46), channel_id=1, source_target_pairs={{0,1},{1,0},{2,3},{3,2},{4,5},{5,4},{6,7},{7,6},{8,9},{9,8},{10,11... | collective-permute-start | bytes 1572872 | tf_op jit(solution)/shard_map/weights_1/ppermute | solution.py:100
  30.8 18.6 %collective-permute-start.8 = (bf16[2,128,1024]{2,1,0:T(8,128)(2,1)S(1)}, bf16[2,128,1024]{2,1,0:T(8,128)(2,1)}, u32[]{:S(2)}, u32[]{:S(2)}) collective-permute-start(bf16[2,128,1024]{2,1,0:T(8,128)(2,1)S(1)} %collective-permute-done.1.refs_8_), channel_id=1, source_target_pairs={{0,8},{4,12},{8,0},{12,4},{1,9},{5,13},{9,1},{13,5},{2,10},{6,14},... | collective-permute-start | bytes 1572872 | tf_op jit(solution)/shard_map/tokens_1_2/ppermute | solution.py:100
  30.9 14.6 %collective-permute-start.2 = (bf16[256,512]{1,0:T(8,128)(2,1)}, bf16[256,512]{1,0:T(8,128)(2,1)S(1)}, u32[]{:S(2)}, u32[]{:S(2)}) collective-permute-start(bf16[256,512]{1,0:T(8,128)(2,1)} %get-tuple-element.45), channel_id=1, source_target_pairs={{0,2},{1,3},{2,0},{3,1},{4,6},{5,7},{6,4},{7,5},{8,10},{9,11},{10,... | collective-permute-start | bytes 786440 | tf_op jit(solution)/shard_map/weights_2/ppermute | solution.py:100
  46.2 20.2 %collective-permute-start.5 = (bf16[2,128,1024]{2,1,0:T(8,128)(2,1)S(1)}, bf16[2,128,1024]{2,1,0:T(8,128)(2,1)}, u32[]{:S(2)}, u32[]{:S(2)}) collective-permute-start(bf16[2,128,1024]{2,1,0:T(8,128)(2,1)S(1)} %collective-permute-done.refs_4_), channel_id=1, source_target_pairs={{0,1},{1,0},{2,3},{3,2},{4,5},{5,4},{6,7},{7,6},{8,9},{9,8},{10,11... | collective-permute-start | bytes 1572872 | tf_op jit(solution)/shard_map/tokens_3/ppermute | solution.py:100
  49.0 17.5 %collective-permute-start.11 = (bf16[2,128,1024]{2,1,0:T(8,128)(2,1)S(1)}, bf16[2,128,1024]{2,1,0:T(8,128)(2,1)S(1)}, u32[]{:S(2)}, u32[]{:S(2)}) collective-permute-start(bf16[2,128,1024]{2,1,0:T(8,128)(2,1)S(1)} %collective-permute-done.4.refs_14_), channel_id=1, source_target_pairs={{0,4},{4,0},{8,12},{12,8},{1,5},{5,1},{9,13},{13,9},{2,6},{6,2},{1... | collective-permute-start | bytes 1572872 | tf_op jit(solution)/shard_map/tokens_0_3/ppermute | solution.py:100
  49.0 17.5 %collective-permute-start.10 = (bf16[2,128,1024]{2,1,0:T(8,128)(2,1)S(1)}, bf16[2,128,1024]{2,1,0:T(8,128)(2,1)S(1)}, u32[]{:S(2)}, u32[]{:S(2)}) collective-permute-start(bf16[2,128,1024]{2,1,0:T(8,128)(2,1)S(1)} %pad_maximum_fusion.refs_12_), channel_id=1, source_target_pairs={{0,4},{4,0},{8,12},{12,8},{1,5},{5,1},{9,13},{13,9},{2,6},{6,2},{1... | collective-permute-start | bytes 1572872 | tf_op jit(solution)/shard_map/tokens_0_1/ppermute | solution.py:100
  49.5 17.0 %collective-permute-start.9 = (bf16[2,128,1024]{2,1,0:T(8,128)(2,1)S(1)}, bf16[2,128,1024]{2,1,0:T(8,128)(2,1)}, u32[]{:S(2)}, u32[]{:S(2)}) collective-permute-start(bf16[2,128,1024]{2,1,0:T(8,128)(2,1)S(1)} %collective-permute-done.refs_4_), channel_id=1, source_target_pairs={{0,8},{4,12},{8,0},{12,4},{1,9},{5,13},{9,1},{13,5},{2,10},{6,14},... | collective-permute-start | bytes 1572872 | tf_op jit(solution)/shard_map/tokens_2_2/ppermute | solution.py:100
  50.0 16.5 %collective-permute-start.7 = (bf16[256,512]{1,0:T(8,128)(2,1)}, bf16[256,512]{1,0:T(8,128)(2,1)S(1)}, u32[]{:S(2)}, u32[]{:S(2)}) collective-permute-start(bf16[256,512]{1,0:T(8,128)(2,1)} %get-tuple-element.49), channel_id=1, source_target_pairs={{0,3},{1,2},{2,1},{3,0},{4,7},{5,6},{6,5},{7,4},{8,11},{9,10},{10,... | collective-permute-start | bytes 786440 | tf_op jit(solution)/shard_map/weights_3/ppermute | solution.py:100
  66.5 12.0 %collective-permute-start.12 = (bf16[2,128,1024]{2,1,0:T(8,128)(2,1)}, bf16[2,128,1024]{2,1,0:T(8,128)(2,1)}, u32[]{:S(2)}, u32[]{:S(2)}) collective-permute-start(bf16[2,128,1024]{2,1,0:T(8,128)(2,1)} %collective-permute-done.5.refs_0_), channel_id=1, source_target_pairs={{0,8},{4,12},{8,0},{12,4},{1,9},{5,13},{9,1},{13,5},{2,10},{6,14},... | collective-permute-start | bytes 1572872 | tf_op jit(solution)/shard_map/tokens_3_2/ppermute | solution.py:100
  67.1 11.9 %collective-permute-start.16 = (bf16[2,128,1024]{2,1,0:T(8,128)(2,1)S(1)}, bf16[2,128,1024]{2,1,0:T(8,128)(2,1)S(1)}, u32[]{:S(2)}, u32[]{:S(2)}) collective-permute-start(bf16[2,128,1024]{2,1,0:T(8,128)(2,1)S(1)} %collective-permute-done.1.refs_8_), channel_id=1, source_target_pairs={{0,4},{4,0},{8,12},{12,8},{1,5},{5,1},{9,13},{13,9},{2,6},{6,2},{1... | collective-permute-start | bytes 1572872 | tf_op jit(solution)/shard_map/tokens_1_1/ppermute | solution.py:100
  67.1 11.4 %collective-permute-start.19 = (bf16[256,512]{1,0:T(8,128)(2,1)S(1)}, bf16[256,512]{1,0:T(8,128)(2,1)S(1)}, u32[]{:S(2)}, u32[]{:S(2)}) collective-permute-start(bf16[256,512]{1,0:T(8,128)(2,1)S(1)} %collective-permute-done.7.rest_3_), channel_id=1, source_target_pairs={{0,16},{16,0},{1,17},{17,1},{2,18},{18,2},{3,19},{19,3},{4,20},{20... | collective-permute-start | bytes 786440 | tf_op jit(solution)/shard_map/weights_3/ppermute | solution.py:100
  68.5 12.8 %collective-permute-start.18 = (bf16[256,512]{1,0:T(8,128)(2,1)S(1)}, bf16[256,512]{1,0:T(8,128)(2,1)S(1)}, u32[]{:S(2)}, u32[]{:S(2)}) collective-permute-start(bf16[256,512]{1,0:T(8,128)(2,1)S(1)} %collective-permute-done.2.rest_1_), channel_id=1, source_target_pairs={{0,16},{16,0},{1,17},{17,1},{2,18},{18,2},{3,19},{19,3},{4,20},{20... | collective-permute-start | bytes 786440 | tf_op jit(solution)/shard_map/weights_2/ppermute | solution.py:100
  69.1 16.0 %collective-permute-start.17 = (bf16[2,128,1024]{2,1,0:T(8,128)(2,1)}, bf16[2,128,1024]{2,1,0:T(8,128)(2,1)}, u32[]{:S(2)}, u32[]{:S(2)}) collective-permute-start(bf16[2,128,1024]{2,1,0:T(8,128)(2,1)} %collective-permute-done.8.refs_10_), channel_id=1, source_target_pairs={{0,4},{4,0},{8,12},{12,8},{1,5},{5,1},{9,13},{13,9},{2,6},{6,2},{1... | collective-permute-start | bytes 1572872 | tf_op jit(solution)/shard_map/tokens_1_3/ppermute | solution.py:100
  78.5 6.6 %collective-permute-start.6 = (bf16[2,128,1024]{2,1,0:T(8,128)(2,1)}, bf16[2,128,1024]{2,1,0:T(8,128)(2,1)}, u32[]{:S(2)}, u32[]{:S(2)}) collective-permute-start(bf16[2,128,1024]{2,1,0:T(8,128)(2,1)} %collective-permute-done.5.refs_0_), channel_id=1, source_target_pairs={{0,4},{4,0},{8,12},{12,8},{1,5},{5,1},{9,13},{13,9},{2,6},{6,2},{1... | collective-permute-start | bytes 1572872 | tf_op jit(solution)/shard_map/tokens_3_1/ppermute | solution.py:100
  112.9 13.9 %collective-permute-start.23 = (bf16[2,2,128,1024]{3,1,2,0:T(2,128)(2,1)}, bf16[2,2,128,1024]{3,1,2,0:T(2,128)(2,1)}, u32[]{:S(2)}, u32[]{:S(2)}) collective-permute-start(bf16[2,2,128,1024]{3,1,2,0:T(2,128)(2,1)} %copy.21), channel_id=1, source_target_pairs={{0,4},{4,0},{8,12},{12,8},{1,5},{5,1},{9,13},{13,9},{2,6},{6,2},{1... | collective-permute-start | bytes 3145736 | tf_op jit(solution)/shard_map/sums_3_1/ppermute | solution.py:100
  115.1 16.9 %collective-permute-start.22 = (bf16[2,2,128,1024]{3,1,2,0:T(2,128)(2,1)}, bf16[2,2,128,1024]{3,1,2,0:T(2,128)(2,1)}, u32[]{:S(2)}, u32[]{:S(2)}) collective-permute-start(bf16[2,2,128,1024]{3,1,2,0:T(2,128)(2,1)} %copy.19), channel_id=1, source_target_pairs={{0,4},{4,0},{8,12},{12,8},{1,5},{5,1},{9,13},{13,9},{2,6},{6,2},{1... | collective-permute-start | bytes 3145736 | tf_op jit(solution)/shard_map/sums_2_1/ppermute | solution.py:100
  115.8 10.4 %collective-permute-start.29 = (f32[2,1024]{1,0:T(2,128)S(1)}, f32[2,1024]{1,0:T(2,128)S(1)}, u32[]{:S(2)}, u32[]{:S(2)}) collective-permute-start(f32[2,1024]{1,0:T(2,128)S(1)} %copy-done.26), channel_id=1, source_target_pairs={{0,8},{4,12},{8,0},{12,4},{1,9},{5,13},{9,1},{13,5},{2,10},{6,14},... | collective-permute-start | bytes 24584 | tf_op jit(solution)/shard_map/stats/ppermute | solution.py:100
  119.6 34.3 %collective-permute-start.34 = (bf16[512,512]{1,0:T(8,128)(2,1)}, bf16[512,512]{1,0:T(8,128)(2,1)}, u32[]{:S(2)}, u32[]{:S(2)}) collective-permute-start(bf16[512,512]{1,0:T(8,128)(2,1)} %get-tuple-element.80), channel_id=1, source_target_pairs={{0,2},{1,3},{2,0},{3,1},{4,6},{5,7},{6,4},{7,5},{8,10},{9,11},{10,... | collective-permute-start | bytes 1572872 | tf_op jit(solution)/shard_map/grads_2/ppermute | solution.py:100
  121.7 28.1 %collective-permute-start.20 = (bf16[2,2,128,1024]{3,1,2,0:T(2,128)(2,1)}, bf16[2,2,128,1024]{3,1,2,0:T(2,128)(2,1)}, u32[]{:S(2)}, u32[]{:S(2)}) collective-permute-start(bf16[2,2,128,1024]{3,1,2,0:T(2,128)(2,1)} %copy.14), channel_id=1, source_target_pairs={{0,4},{4,0},{8,12},{12,8},{1,5},{5,1},{9,13},{13,9},{2,6},{6,2},{1... | collective-permute-start | bytes 3145736 | tf_op jit(solution)/shard_map/sums_0_1/ppermute | solution.py:100
  126.2 26.1 %collective-permute-start.21 = (bf16[2,2,128,1024]{3,1,2,0:T(2,128)(2,1)}, bf16[2,2,128,1024]{3,1,2,0:T(2,128)(2,1)}, u32[]{:S(2)}, u32[]{:S(2)}) collective-permute-start(bf16[2,2,128,1024]{3,1,2,0:T(2,128)(2,1)} %copy.17), channel_id=1, source_target_pairs={{0,4},{4,0},{8,12},{12,8},{1,5},{5,1},{9,13},{13,9},{2,6},{6,2},{1... | collective-permute-start | bytes 3145736 | tf_op jit(solution)/shard_map/sums_1_1/ppermute | solution.py:100
  129.3 14.6 %collective-permute-start.24 = (bf16[2,128,1024]{2,0,1:T(2,128)(2,1)}, bf16[2,128,1024]{2,0,1:T(2,128)(2,1)}, u32[]{:S(2)}, u32[]{:S(2)}) collective-permute-start(bf16[2,128,1024]{2,0,1:T(2,128)(2,1)} %fusion.19), channel_id=1, source_target_pairs={{0,8},{4,12},{8,0},{12,4},{1,9},{5,13},{9,1},{13,5},{2,10},{6,14},... | collective-permute-start | bytes 1572872 | tf_op jit(solution)/shard_map/sums_3_2/ppermute | solution.py:100
  143.9 13.5 %collective-permute-start.25 = (bf16[2,128,1024]{2,0,1:T(2,128)(2,1)S(1)}, bf16[2,128,1024]{2,0,1:T(2,128)(2,1)S(1)}, u32[]{:S(2)}, u32[]{:S(2)}) collective-permute-start(bf16[2,128,1024]{2,0,1:T(2,128)(2,1)S(1)} %fusion.20), channel_id=1, source_target_pairs={{0,8},{4,12},{8,0},{12,4},{1,9},{5,13},{9,1},{13,5},{2,10},{6,14},... | collective-permute-start | bytes 1572872 | tf_op jit(solution)/shard_map/sums_2_2/ppermute | solution.py:100
  146.8 15.4 %collective-permute-start.28 = (bf16[2,128,1024]{2,0,1:T(2,128)(2,1)S(1)}, bf16[2,128,1024]{2,0,1:T(2,128)(2,1)S(1)}, u32[]{:S(2)}, u32[]{:S(2)}) collective-permute-start(bf16[2,128,1024]{2,0,1:T(2,128)(2,1)S(1)} %fusion.1), channel_id=1, source_target_pairs={{0,1},{1,0},{2,3},{3,2},{4,5},{5,4},{6,7},{7,6},{8,9},{9,8},{10,11... | collective-permute-start | bytes 1572872 | tf_op jit(solution)/shard_map/sums_3/ppermute | solution.py:100
  157.4 29.0 %collective-permute-start.35 = (bf16[528,512]{1,0:T(8,128)(2,1)S(1)}, bf16[528,512]{1,0:T(8,128)(2,1)S(1)}, u32[]{:S(2)}, u32[]{:S(2)}) collective-permute-start(bf16[528,512]{1,0:T(8,128)(2,1)S(1)} %get-tuple-element.83), channel_id=1, source_target_pairs={{0,3},{1,2},{2,1},{3,0},{4,7},{5,6},{6,5},{7,4},{8,11},{9,10},{10,... | collective-permute-start | bytes 1622024 | tf_op jit(solution)/shard_map/grads_3/ppermute | solution.py:100
  165.7 44.0 %collective-permute-start.32 = (bf16[2,144,1024]{2,0,1:T(2,128)(2,1)}, bf16[2,144,1024]{2,0,1:T(2,128)(2,1)}, u32[]{:S(2)}, u32[]{:S(2)}) collective-permute-start(bf16[2,144,1024]{2,0,1:T(2,128)(2,1)} %fusion.11), channel_id=1, source_target_pairs={{0,2},{1,3},{2,0},{3,1},{4,6},{5,7},{6,4},{7,5},{8,10},{9,11},{10,... | collective-permute-start | bytes 1769480 | tf_op jit(solution)/shard_map/sums_2/ppermute | solution.py:100
  168.1 30.2 %collective-permute-start.33 = (bf16[528,512]{1,0:T(8,128)(2,1)}, bf16[528,512]{1,0:T(8,128)(2,1)}, u32[]{:S(2)}, u32[]{:S(2)}) collective-permute-start(bf16[528,512]{1,0:T(8,128)(2,1)} %get-tuple-element.78), channel_id=1, source_target_pairs={{0,1},{1,0},{2,3},{3,2},{4,5},{5,4},{6,7},{7,6},{8,9},{9,8},{10,11... | collective-permute-start | bytes 1622024 | tf_op jit(solution)/shard_map/grads_1/ppermute | solution.py:100
  168.4 11.8 %collective-permute-start.26 = (bf16[2,128,1024]{2,0,1:T(2,128)(2,1)S(1)}, bf16[2,128,1024]{2,0,1:T(2,128)(2,1)S(1)}, u32[]{:S(2)}, u32[]{:S(2)}) collective-permute-start(bf16[2,128,1024]{2,0,1:T(2,128)(2,1)S(1)} %fusion.21), channel_id=1, source_target_pairs={{0,8},{4,12},{8,0},{12,4},{1,9},{5,13},{9,1},{13,5},{2,10},{6,14},... | collective-permute-start | bytes 1572872 | tf_op jit(solution)/shard_map/sums_1_2/ppermute | solution.py:100
  180.2 30.8 %collective-permute-start.27 = (bf16[2,128,1024]{2,0,1:T(2,128)(2,1)}, bf16[2,128,1024]{2,0,1:T(2,128)(2,1)}, u32[]{:S(2)}, u32[]{:S(2)}) collective-permute-start(bf16[2,128,1024]{2,0,1:T(2,128)(2,1)} %fusion.22), channel_id=1, source_target_pairs={{0,8},{4,12},{8,0},{12,4},{1,9},{5,13},{9,1},{13,5},{2,10},{6,14},... | collective-permute-start | bytes 1572872 | tf_op jit(solution)/shard_map/sums_0_2/ppermute | solution.py:100
  184.4 27.0 %collective-permute-start.31 = (bf16[2,128,1024]{2,0,1:T(2,128)(2,1)}, bf16[2,128,1024]{2,0,1:T(2,128)(2,1)}, u32[]{:S(2)}, u32[]{:S(2)}) collective-permute-start(bf16[2,128,1024]{2,0,1:T(2,128)(2,1)} %fusion.4), channel_id=1, source_target_pairs={{0,1},{1,0},{2,3},{3,2},{4,5},{5,4},{6,7},{7,6},{8,9},{9,8},{10,11... | collective-permute-start | bytes 1572872 | tf_op jit(solution)/shard_map/sums_1/ppermute | solution.py:100
  (38 other events, 476.8 us)

commit v8 on v7

v8 whole, which is shorter than its diff:
```python
import math

import jax
import jax.numpy as jnp
from jax import lax
from jax.experimental import pallas as pl
from jax.experimental.pallas import tpu as pltpu
from jax.sharding import PartitionSpec as P

epsilon = 1e-06


def normalize(row_data, norm_gain, norm_bias):
    values = row_data.astype(jnp.float32)
    row_mean = jnp.mean(values, axis=-1, keepdims=True)
    centred = values - row_mean
    inv_std = lax.rsqrt(jnp.mean(centred * centred, axis=-1, keepdims=True) + epsilon)
    standard = centred * inv_std
    normed = (standard * norm_gain + norm_bias).astype(jnp.bfloat16)
    return (standard, inv_std, normed)


def contract_tokens(left_rows, right_rows):
    return lax.dot_general(
        left_rows, right_rows, (((0,), (0,)), ((), ())), preferred_element_type=jnp.float32
    )


def contract_last(left_rows, right_rows):
    return lax.dot_general(
        left_rows, right_rows, (((1,), (1,)), ((), ())), preferred_element_type=jnp.float32
    )


def finish_rows(branch, grad_normed, second_out, grad_first, first_out, norm_gain, norm_bias):
    standard, inv_std, _ = normalize(first_out, norm_gain, norm_bias)
    second_in = (second_out.astype(jnp.float32) - branch).astype(jnp.bfloat16)
    grad_std = grad_normed * norm_gain
    grad_rows = inv_std * (
        grad_std
        - jnp.mean(grad_std, axis=-1, keepdims=True)
        - standard * jnp.mean(grad_std * standard, axis=-1, keepdims=True)
    )
    return second_in, grad_first.astype(jnp.float32) + grad_rows


def gather_weights_body(
    first_out, second_out, grad_first, grad_second, w_up, w_down, norm_gain, norm_bias
):
    own_rows = first_out.shape[0]
    up_full = lax.all_gather(w_up, "dp", axis=0, tiled=True)
    down_full = lax.all_gather(w_down, "dp", axis=1, tiled=True)
    first_all = lax.all_gather(first_out, "tensor", axis=0, tiled=True)
    grad_all = lax.all_gather(grad_second, "tensor", axis=0, tiled=True)
    standard_all, _, normed = normalize(first_all, norm_gain, norm_bias)
    offset = lax.axis_index("tensor") * own_rows
    standard = lax.dynamic_slice_in_dim(standard_all, offset, own_rows, 0)
    preact = jnp.dot(normed, up_full, preferred_element_type=jnp.float32)
    hidden = jax.nn.gelu(preact).astype(jnp.bfloat16)
    branch = lax.psum_scatter(
        jnp.dot(hidden, down_full, preferred_element_type=jnp.float32).astype(jnp.bfloat16),
        "tensor",
        scatter_dimension=0,
        tiled=True,
    ).astype(jnp.float32)
    tokens = own_rows * lax.axis_size("tensor") * lax.axis_size("dp")
    grad_scale = tokens ** (-0.5)
    grad_down_part = contract_tokens(hidden, grad_all)
    grad_down = (
        lax.psum_scatter(
            grad_down_part.astype(jnp.bfloat16), "dp", scatter_dimension=1, tiled=True
        ).astype(jnp.float32)
        * grad_scale
    )
    grad_hidden = contract_last(grad_all, down_full)
    grad_pre = jax.vjp(jax.nn.gelu, preact)[1](grad_hidden)[0].astype(jnp.bfloat16)
    grad_up_part = contract_tokens(normed, grad_pre)
    grad_up = (
        lax.psum_scatter(
            grad_up_part.astype(jnp.bfloat16), "dp", scatter_dimension=0, tiled=True
        ).astype(jnp.float32)
        * grad_scale
    )
    grad_normed = lax.psum_scatter(
        contract_last(grad_pre, up_full).astype(jnp.bfloat16),
        "tensor",
        scatter_dimension=0,
        tiled=True,
    ).astype(jnp.float32)
    second_in, grad_first_in = finish_rows(
        branch, grad_normed, second_out, grad_first, first_out, norm_gain, norm_bias
    )
    local_stats = jnp.stack([jnp.sum(grad_normed * standard, axis=0), jnp.sum(grad_normed, axis=0)])
    grad_norm = lax.psum(local_stats, ("tensor", "dp")) * grad_scale
    return (second_in, grad_first_in, grad_up, grad_down, grad_norm)


def swap(values, axis, mask, scope):
    with jax.named_scope(scope):
        return lax.ppermute(values, axis, [(i, i ^ mask) for i in range(lax.axis_size(axis))])


def bits_of(size):
    return [1 << b for b in reversed(range(size.bit_length() - 1))]


def share(k, n_dp, mates):
    return mates if k >= bits_of(n_dp)[0] else 1


def pack_weights(w_up, w_down, mates):
    n_dp = lax.axis_size("dp")
    depth, units = w_up.shape[0], w_up.shape[1] // n_dp
    strips = units // depth

    def kernel(up_ref, down_ref, *sends):
        place, mate = lax.axis_index("dp"), lax.rem(lax.axis_index("groups"), mates)
        for k in range(1, n_dp):
            n = share(k, n_dp, mates)
            part = mate if n > 1 else 0
            rows = depth // n
            first = pl.multiple_of((place ^ k) * units, units)
            send = sends[k - 1]
            send[:, :units] = up_ref[pl.ds(pl.multiple_of(part * rows, rows), rows), pl.ds(first, units)]
            for c in range(strips):
                row = pl.multiple_of(first + part * (units // n) + c * rows, rows)
                send[:, units + c * depth : units + (c + 1) * depth] = down_ref[pl.ds(row, rows), :]

    return pl.pallas_call(
        kernel,
        out_shape=[
            jax.ShapeDtypeStruct((depth // share(k, n_dp, mates), 2 * units), w_up.dtype)
            for k in range(1, n_dp)
        ],
        in_specs=[pl.BlockSpec(memory_space=pltpu.VMEM)] * 2,
        out_specs=[pl.BlockSpec(memory_space=pltpu.VMEM)] * (n_dp - 1),
        cost_estimate=pl.CostEstimate(flops=0, bytes_accessed=8 * w_up.size, transcendentals=0),
        name="pack_weights",
    )(w_up, w_down)


def core(chunks, w_up, w_down, got, mates, gain, bias):
    n_chunks, n, n_dp = len(chunks), len(chunks[0]), lax.axis_size("dp")
    (piece_rows, width), units = chunks[0][0].shape, w_up.shape[1] // n_dp
    piece_rows //= 2
    depth = width // n_dp
    strips, pair = units // depth, 2 * piece_rows
    slope = (2.0 / math.pi) ** 0.5
    dtype = w_up.dtype
    pieces_of_weights = [piece for k in range(1, n_dp) for piece in got[k]]
    n_got = len(pieces_of_weights)

    def kernel(*refs):
        toks, refs = refs[: n_chunks * n], refs[n_chunks * n :]
        (own_up, own_down), weights, (gain_ref, bias_ref), refs = (
            refs[:2],
            list(refs[2 : 2 + n_got]),
            refs[2 + n_got : 4 + n_got],
            refs[4 + n_got :],
        )
        outs, blocks, stat_ref = refs[: 2 * n_chunks], refs[2 * n_chunks : 2 * n_chunks + n_dp], refs[2 * n_chunks + n_dp]
        tok, norm, hid, pre, part, block, up_ref, down_ref, in_sem, w_sem, out_sem, b_sem = refs[2 * n_chunks + n_dp + 1 :]
        place, mate = lax.axis_index("dp"), lax.rem(lax.axis_index("groups"), mates)
        reads, loads, writes = [], [], []

        def load(src, dst):
            loads.append(pltpu.make_async_copy(src, dst, w_sem.at[len(loads)]))
            loads[-1].start()

        for i, ref in enumerate(toks):
            reads.append(pltpu.make_async_copy(ref, tok.at[i], in_sem.at[i]))
            if i < n:
                reads[-1].start()
        mine = pl.ds(pl.multiple_of(place * units, units), units)
        rows = pl.ds(pl.multiple_of(place * depth, depth), depth)
        load(own_up.at[:, mine], up_ref.at[rows, :])
        load(own_down.at[mine, :], down_ref.at[:, rows])
        for k in range(1, n_dp):
            first = pl.multiple_of((place ^ k) * depth, depth)
            many = len(got[k])
            rows = depth // many
            for j in range(many):
                piece = weights.pop(0)
                which = mate ^ j if many > 1 else 0
                row = pl.multiple_of(first + which * rows, rows)
                load(piece.at[:, pl.ds(0, units)], up_ref.at[pl.ds(row, rows), :])
                for c in range(strips):
                    row = pl.multiple_of(which * (units // many) + c * rows, rows)
                    load(
                        piece.at[:, pl.ds(units + c * depth, depth)],
                        down_ref.at[pl.ds(row, rows), pl.ds(first, depth)],
                    )
        for one in reads[n:]:
            one.start()
        stat_ref[...] = jnp.zeros_like(stat_ref)
        for i in range(n_chunks):
            for one in reads[i * n : (i + 1) * n] + (loads if i == 0 else []):
                one.wait()

            @pl.loop(0, n // 2)
            def _(t):
                at = i * n + 2 * t
                span = pl.ds(pl.multiple_of(at * piece_rows, pair), pair)
                values = tok[pl.ds(at, 2), :piece_rows].reshape(pair, width).astype(jnp.float32)
                centred = values - jnp.mean(values, axis=-1, keepdims=True)
                inv_std = lax.rsqrt(jnp.mean(centred * centred, axis=-1, keepdims=True) + epsilon)
                standard = centred * inv_std
                normed = (standard * gain_ref[...] + bias_ref[...]).astype(dtype)
                norm[span, :] = normed
                x = jnp.dot(normed, up_ref[...], preferred_element_type=jnp.float32)
                gate = jnp.tanh(slope * (x + 0.044715 * (x * x * x)))
                half = 0.5 + 0.5 * gate
                hidden = (x * half).astype(dtype)
                hid[span, :] = hidden
                rise = half + (0.5 * slope) * x * (1.0 - gate * gate) * (1.0 + (3 * 0.044715) * (x * x))
                grads = tok[pl.ds(at, 2), piece_rows:].reshape(pair, width)
                grad_pre = (contract_last(grads, down_ref[...]) * rise).astype(dtype)
                pre[span, :] = grad_pre
                branch = jnp.dot(hidden, down_ref[...], preferred_element_type=jnp.float32)
                grad_normed = contract_last(grad_pre, up_ref[...])
                stat_ref[0:1, :] += jnp.sum(grad_normed * standard, axis=0, keepdims=True)
                stat_ref[1:2, :] += jnp.sum(grad_normed, axis=0, keepdims=True)
                row = pl.multiple_of(t * pair, pair)
                for odd in range(2):
                    own = slice(odd * piece_rows, (odd + 1) * piece_rows)
                    part[2 * i + odd, pl.ds(row, piece_rows), :] = branch[own].astype(dtype)
                    part[2 * i + odd, pl.ds(row + piece_rows, piece_rows), :] = grad_normed[own].astype(dtype)

            for odd in (1, 0):
                at = 2 * i + odd
                writes.append(pltpu.make_async_copy(part.at[at], outs[at], out_sem.at[at]))
                writes[-1].start()
        top = bits_of(n_dp)[0]
        for k in sorted(range(n_dp), key=lambda k: (k < top, k)):
            columns = pl.ds(pl.multiple_of((place ^ k) * depth, depth), depth)
            block[k, :depth, :] = contract_tokens(norm[:, columns], pre[...]).astype(dtype)
            grads = tok[:, piece_rows:, columns].reshape(n_chunks * n * piece_rows, depth)
            down_block = contract_tokens(hid[...], grads).astype(dtype)
            for c in range(strips):
                block[k, depth:, c * depth : (c + 1) * depth] = down_block[c * depth : (c + 1) * depth]
            writes.append(pltpu.make_async_copy(block.at[k], blocks[k], b_sem.at[k]))
            writes[-1].start()
        for one in writes:
            one.wait()

    rows = n_chunks * n * piece_rows
    half = (n // 2 * pair, width)
    far = pl.BlockSpec(memory_space=pl.ANY)
    near = pl.BlockSpec(memory_space=pltpu.VMEM)
    out = pl.pallas_call(
        kernel,
        out_shape=[jax.ShapeDtypeStruct(half, dtype)] * (2 * n_chunks)
        + [jax.ShapeDtypeStruct((2 * depth, units), dtype)] * n_dp
        + [jax.ShapeDtypeStruct((2, width), jnp.float32)],
        in_specs=[far] * (n_chunks * n + 2 + n_got) + [near] * 2,
        out_specs=[far] * (2 * n_chunks + n_dp) + [near],
        scratch_shapes=[
            pltpu.VMEM((n_chunks * n, pair, width), dtype),
            pltpu.VMEM((rows, width), dtype),
            pltpu.VMEM((rows, units), dtype),
            pltpu.VMEM((rows, units), dtype),
            pltpu.VMEM((2 * n_chunks, *half), dtype),
            pltpu.VMEM((n_dp, 2 * depth, units), dtype),
            pltpu.VMEM((width, units), dtype),
            pltpu.VMEM((units, width), dtype),
            pltpu.SemaphoreType.DMA((n_chunks * n,)),
            pltpu.SemaphoreType.DMA((2 + n_got * (1 + strips),)),
            pltpu.SemaphoreType.DMA((2 * n_chunks,)),
            pltpu.SemaphoreType.DMA((n_dp,)),
        ],
        compiler_params=pltpu.CompilerParams(vmem_limit_bytes=56 * 1024 * 1024),
        cost_estimate=pl.CostEstimate(
            flops=10 * rows * width * units,
            bytes_accessed=8 * rows * width + 8 * width * units,
            transcendentals=rows * units,
        ),
        name="core",
    )(
        *[piece for chunk in chunks for piece in chunk],
        w_up,
        w_down,
        *pieces_of_weights,
        gain.reshape(1, width),
        bias.reshape(1, width),
    )
    halves = [out[2 * i : 2 * i + 2] for i in range(n_chunks)]
    return halves, list(out[2 * n_chunks : -1]), out[-1]


def finish(blocks, terms, own_stats, first_out, second_out, grad_first, gain, bias, w_shapes, scale):
    (rows, width), n_dp = first_out.shape, len(blocks)
    depth, units = w_shapes[0][0], w_shapes[0][1] // n_dp
    strips, top, n_terms = units // depth, bits_of(n_dp)[0], len(terms)

    def kernel(*refs):
        parts, adds, (stat_ref, first_ref, second_ref, grad_ref, gain_ref, bias_ref), outs = (
            refs[:n_dp],
            refs[n_dp : n_dp + n_terms],
            refs[n_dp + n_terms : n_dp + n_terms + 6],
            refs[n_dp + n_terms + 6 :],
        )
        second_in, grad_in, up_out, down_out, norm_out = outs
        place = lax.axis_index("dp")
        for k in range(n_dp):
            first = pl.multiple_of((place ^ k) * units, units)
            up_out[:, pl.ds(first, units)] = parts[k][:depth, :].astype(jnp.float32) * scale
            for c in range(strips):
                block = parts[k][depth : 2 * depth, c * depth : (c + 1) * depth]
                row = pl.multiple_of(first + c * depth, depth)
                down_out[pl.ds(row, depth), :] = block.astype(jnp.float32) * scale
        total = sum(ref[: 2 * rows, :].astype(jnp.float32) for ref in adds)
        second_in[...] = (second_ref[...].astype(jnp.float32) - total[:rows]).astype(second_in.dtype)
        values = first_ref[...].astype(jnp.float32)
        centred = values - jnp.mean(values, axis=-1, keepdims=True)
        inv_std = lax.rsqrt(jnp.mean(centred * centred, axis=-1, keepdims=True) + epsilon)
        standard = centred * inv_std
        grad_std = total[rows:] * gain_ref[...]
        grad_rows = inv_std * (
            grad_std
            - jnp.mean(grad_std, axis=-1, keepdims=True)
            - standard * jnp.mean(grad_std * standard, axis=-1, keepdims=True)
        )
        grad_in[...] = grad_ref[...].astype(jnp.float32) + grad_rows
        stats = []
        for k in range(n_dp):
            if k == 0:
                one = stat_ref[...].astype(jnp.float32)
            elif k == top:
                one = adds[-1][2 * rows :, :].astype(jnp.float32)[:2]
            else:
                tail = parts[k][2 * depth :, :].astype(jnp.float32)
                per = width // units
                one = jnp.concatenate(
                    [
                        jnp.concatenate([tail[i * per + j : i * per + j + 1] for j in range(per)], axis=1)
                        for i in range(2)
                    ],
                    axis=0,
                )
            stats.append(one)
        while len(stats) > 1:
            stats = [one + two for one, two in zip(stats[0::2], stats[1::2], strict=True)]
        norm_out[...] = stats[0] * scale

    def whole(x):
        return pl.BlockSpec(x.shape, lambda i: (0, 0))

    arrays = [*blocks, *terms, own_stats, first_out, second_out, grad_first, gain.reshape(1, width), bias.reshape(1, width)]
    in_specs = [whole(x) for x in arrays]
    for i in range(n_terms - 1):
        in_specs[n_dp + i] = pl.BlockSpec((2 * rows, width), lambda i: (0, 0))
    out_shape = [
        jax.ShapeDtypeStruct((rows, width), second_out.dtype),
        jax.ShapeDtypeStruct((rows, width), jnp.float32),
        jax.ShapeDtypeStruct(w_shapes[0], jnp.float32),
        jax.ShapeDtypeStruct(w_shapes[1], jnp.float32),
        jax.ShapeDtypeStruct((2, width), jnp.float32),
    ]
    return pl.pallas_call(
        kernel,
        out_shape=out_shape,
        grid=(1,),
        in_specs=in_specs,
        out_specs=[whole(x) for x in out_shape],
        compiler_params=pltpu.CompilerParams(vmem_limit_bytes=48 * 1024 * 1024),
        cost_estimate=pl.CostEstimate(
            flops=0, bytes_accessed=12 * w_shapes[0][0] * w_shapes[0][1], transcendentals=0
        ),
        name="finish",
    )(*arrays)


def after(values, *others):
    return lax.optimization_barrier((values, *others))[0]


def gather_tokens_body(
    first_out, second_out, grad_first, grad_second, w_up, w_down, norm_gain, norm_bias
):
    n_dp, n_tensor, n_groups = (lax.axis_size(axis) for axis in ("dp", "tensor", "groups"))
    own_rows, depth = first_out.shape[0], w_up.shape[0]
    units = w_up.shape[1] // n_dp
    mates = 2 if n_groups % 2 == 0 else 1
    place = lax.axis_index("dp")
    top = bits_of(n_dp)[0]

    high, others = bits_of(n_tensor)[0], bits_of(n_tensor)[1:]
    own = jnp.concatenate([first_out, grad_second])
    tokens, chunks, got, crossed = {0: own}, {}, {}, {}

    def tokens_dp(k, *first):
        tokens[k] = swap(after(tokens[k & (k - 1)], *first), "dp", k & -k, f"tokens_{k}")

    def tokens_tensor(k, *first):
        start = after(tokens[k], *first)
        chunks[k] = {0: tokens[k], high: swap(start, "tensor", high, f"tokens_{k}_{high}")}

    def tokens_rest(k, *first):
        for bit in others:
            for j in list(chunks[k]):
                piece = after(chunks[k][j], *first)
                chunks[k][j | bit] = swap(piece, "tensor", bit, f"tokens_{k}_{j | bit}")

    def weights_dp(k, *first):
        got[k] = swap(after(sends[k - 1], *first), "dp", k, f"weights_{k}")

    def weights_groups(k, *first):
        crossed[k] = swap(after(got[k], *first), "groups", 1, f"weights_{k}")

    tokens_tensor(0)
    for bit in bits_of(n_dp)[:0:-1]:
        tokens_dp(bit)
    sends = pack_weights(w_up, w_down, mates)
    both = swap(jnp.concatenate([own, sends[top - 1]]), "dp", top, f"tokens_weights_{top}")
    tokens[top], got[top] = both[: 2 * own_rows], both[2 * own_rows :]
    for bit in bits_of(n_dp)[1:]:
        weights_dp(bit)
    tokens_tensor(1, tokens[1], chunks[0][high])
    stage = [*tokens.values(), *got.values(), chunks[0][high]]
    tokens_rest(0, *stage)
    for k in range(2, n_dp):
        if k & (k - 1):
            tokens_dp(k, *stage)
            weights_dp(k, *stage)
            if mates == 2 and top not in crossed:
                weights_groups(top, *stage)
            stage = [tokens[k], got[k], *crossed.values(), chunks[k - 1][high], *chunks[0].values()]
        tokens_tensor(k, *stage, chunks[k - 1][high])
        tokens_rest(k - 1, *stage)
    tokens_rest(n_dp - 1)
    if mates == 2:
        for k in range(top, n_dp):
            if k not in crossed:
                weights_groups(k)
    got = {k: [got[k]] + ([crossed[k]] if k in crossed else []) for k in got}

    order = sorted(chunks, reverse=True)
    halves, blocks, stats = core(
        [[chunks[k][j] for j in range(n_tensor)] for k in order], w_up, w_down, got, mates, norm_gain, norm_bias
    )
    blocks = dict(enumerate(blocks))
    blocks[top] = swap(blocks[top], "dp", top, f"grads_{top}")

    sums, behind, hops = {}, (), []
    for k, (even, odd) in zip(order, halves, strict=True):
        came = swap(odd, "tensor", 1, f"sums_{k}_1")
        spans = [slice(j * 2 * own_rows, (j + 1) * 2 * own_rows) for j in range(n_tensor // 2)]
        parts = {2 * j: (even[span], came[span]) for j, span in enumerate(spans)}
        parts[0] = (even, came)
        for bit in reversed(bits_of(n_tensor)[:-1]):
            for j in [j for j in parts if j & bit]:
                send = after(sum(parts.pop(j)), *behind)
                if not hops:
                    stats = after(stats, send)
                parts[j ^ bit] += (swap(send, "tensor", bit, f"sums_{k}_{j}"),)
                behind = parts[j ^ bit][-1:]
                hops += behind
        sums[k] = parts[0]

    def add(terms):
        return sum(term[: 2 * own_rows].astype(jnp.float32) for term in terms).astype(jnp.bfloat16)

    for bit in bits_of(n_tensor):
        stats = stats + swap(stats, "tensor", bit, "stats")
    stats = stats.astype(jnp.bfloat16)
    extra = 16

    came = {}
    for bit in bits_of(n_dp)[::-1]:
        for k in [k for k in order if k & bit and k in sums and k != bit]:
            came[k] = swap(add(sums.pop(k)), "dp", bit, f"sums_{k}")
            sums[k ^ bit] += (came[k],)
    last = jnp.concatenate([add(sums[top]), jnp.pad(stats, ((0, extra - 2), (0, 0)))])
    came[top] = swap(last, "dp", top, f"sums_{top}")
    rows = stats.reshape(-1, units)
    rows = jnp.pad(rows, ((0, extra - rows.shape[0]), (0, 0)))
    for k in range(1, n_dp):
        if k != top:
            block = jnp.concatenate([blocks[k], rows])
            first = [last] if k < top else [blocks[top], *hops[:1]]
            blocks[k] = swap(after(block, *first), "dp", k, f"grads_{k}")
    for bit in bits_of(n_dp)[:0:-1]:
        came[bit] = swap(after(add(sums[bit]), last), "dp", bit, f"sums_{bit}")

    scale = (own_rows * n_tensor * n_dp) ** (-0.5)
    terms = [*sums[0], *(came[bit] for bit in bits_of(n_dp)[::-1])]
    return tuple(
        finish(
            [blocks[k] for k in range(n_dp)],
            terms,
            stats,
            first_out,
            second_out,
            grad_first,
            norm_gain,
            norm_bias,
            (w_up.shape, w_down.shape),
            scale,
        )
    )


def body(first_out, second_out, grad_first, grad_second, w_up, *rest):
    n_dp, n_tensor = lax.axis_size("dp"), lax.axis_size("tensor")
    powers = all(size > 1 and size & (size - 1) == 0 for size in (n_dp, n_tensor))
    few_tokens = first_out.shape[0] * n_tensor < w_up.shape[1]
    units, depth = w_up.shape[1] // n_dp, w_up.shape[0]
    fits = w_up.shape[1] % n_dp == 0 and units % depth == 0 and depth % 128 == 0
    fits = fits and first_out.shape[1] == 2 * units and n_dp > 2 and n_tensor > 2
    pick = gather_tokens_body if powers and few_tokens and fits else gather_weights_body
    return pick(first_out, second_out, grad_first, grad_second, w_up, *rest)


def solution(mesh):
    in_specs = (
        P(("groups", "tensor", "dp"), None),
        P(("groups", "tensor", "dp"), None),
        P(("groups", "tensor", "dp"), None),
        P(("groups", "tensor", "dp"), None),
        P("dp", "tensor"),
        P("tensor", "dp"),
        P(),
        P(),
    )
    out_specs = (
        P(("groups", "tensor", "dp"), None),
        P(("groups", "tensor", "dp"), None),
        P(("groups", "dp"), "tensor"),
        P(("groups", "tensor"), "dp"),
        P("groups", None),
    )
    return jax.shard_map(body, mesh=mesh, in_specs=in_specs, out_specs=out_specs, check_vma=False)
```

time: 220 us -> 199 us (0.905)
  waiting for transfers between devices: 102 us -> 130 us
  other arithmetic: 31.1 us -> 8.37 us
  local copies, waits for them, and re-layouts: 20.9 us -> 3.18 us
  starting transfers between devices: 34.7 us -> 25.3 us
    ppermute x36 -> x35, waiting for transfers between devices: 102 us -> 130 us  [swap(): lax.ppermute(values, axis, [(i, i ^ mask) for i in range(lax.axis_size(ax...]
    pallas_call x8 -> x0, local copies, waits for them, and re-layouts: 14.1 us -> none  [core(): pl.pallas_call(kernel, out_shape=[half] * (2 * n_chunks) + [jax.ShapeDtyp...]
    ppermute x36 -> x35, starting transfers between devices: 34.7 us -> 25.3 us  [swap(): lax.ppermute(values, axis, [(i, i ^ mask) for i in range(lax.axis_size(ax...]
    add x4, other arithmetic: 7.95 us -> 2.99 us  [gather_tokens_body(): send = after(sum(parts.pop(j)), *behind)]
    convert_element_type x6 -> x4, other arithmetic: 7.89 us -> 3 us  [the longest x3 3 us: add(): sum((term[:2 * own_rows].astype(jnp.float32) for term in terms))]
    add x2 -> x0, other arithmetic: 3.92 us -> none  [the longest x1 2.74 us: add(): return sum((term.astype(jnp.float32) for term in terms)).astype(dtype)]
    dynamic_update_slice x4 -> x0, other arithmetic: 3.31 us -> none  [gather_tokens_body(): lax.dynamic_update_slice_in_dim(grad_down, jnp.concatenate(strips, axis=0...]
    mul x5 -> x0, other arithmetic: 2.86 us -> none  [the longest x4 1.57 us: gather_tokens_body(): block = blocks[k].astype(jnp.float32) * grad_scale]
  transfers between devices with their start and end apart: 36 -> 35, of which waited for: 13 -> 19; matrix products, arithmetic and copies ran while one was open for 17% -> 4% of each run, Pallas kernels for 3% -> 1%
where the time goes in v8:
time: 199 us
  waiting for transfers between devices  130 us (65%)
  Pallas kernels  31 us (16%)
  starting transfers between devices  25.3 us (13%)
  other arithmetic  8.37 us (4%)
  local copies, waits for them, and re-layouts  3.18 us (2%)
    ppermute x35, waiting for transfers between devices, swap(): lax.ppermute(values, axis, [(i, i ^ mask) for i in range(lax.axis_size(ax...  130 us
    ppermute x35, starting transfers between devices, swap(): lax.ppermute(values, axis, [(i, i ^ mask) for i in range(lax.axis_size(ax...  25.3 us
    pallas_call x1, Pallas kernels, core(): pl.pallas_call(kernel, out_shape=[jax.ShapeDtypeStruct(half, dtype)] * (2...  24.6 us
  transfers between devices with their start and end apart: 35, of which 19 were waited for; matrix products, arithmetic and copies ran while one was open for 4% of the time, Pallas kernels for 1%

profile of v8, /device:TPU:0, one launch (start us, length us, event | category | flops | bytes accessed | tf_op | source)
XLA Modules:
  0.0 199.1 jit_solution(12969755007871524374)
XLA Ops:
  2.6 3.0 %collective-permute-start.3 = (bf16[256,1024]{1,0:T(8,128)(2,1)S(1)}, bf16[256,1024]{1,0:T(8,128)(2,1)S(1)}, u32[]{:S(2)}, u32[]{:S(2)}) collective-permute-start(bf16[256,1024]{1,0:T(8,128)(2,1)S(1)} %constant_dynamic-update-slice_fusion.refs_12_), channel_id=1, source_target_pairs={{0,8},{4,12},{8,0},{12,4},{1,9},{5,13},{9,1},{13,5},{2,10},{6,14},... | collective-permute-start | bytes 1572872 | tf_op jit(solution)/shard_map/tokens_0_2/ppermute | solution.py:100
  5.6 1.6 collective-permute-start.1
  7.2 2.6 %pack_weights.1 = (bf16[256,1024]{1,0:T(8,128)(2,1)}, bf16[128,1024]{1,0:T(8,128)(2,1)}, bf16[128,1024]{1,0:T(8,128)(2,1)}) custom-call(bf16[256,2048]{1,0:T(8,128)(2,1)} %refs_16_.1, bf16[2048,256]{1,0:T(8,128)(2,1)} %refs_17_.1), custom_call_target="tpu_custom_call" | custom-call | bytes 4194304 | tf_op jit(solution)/shard_map/pack_weights/pallas_call | solution.py:129
  10.9 2.7 %collective-permute-start = (bf16[384,1024]{1,0:T(8,128)(2,1)S(1)}, bf16[384,1024]{1,0:T(8,128)(2,1)S(1)}, u32[]{:S(2)}, u32[]{:S(2)}) collective-permute-start(bf16[384,1024]{1,0:T(8,128)(2,1)S(1)} %pad_maximum_fusion), channel_id=1, source_target_pairs={{0,2},{1,3},{2,0},{3,1},{4,6},{5,7},{6,4},{7,5},{8,10},{9,11},{10,... | collective-permute-start | bytes 2359304 | tf_op jit(solution)/shard_map/tokens_weights_2/ppermute | solution.py:100
  14.0 3.6 %collective-permute-done.3.refs_14_ = bf16[256,1024]{1,0:T(8,128)(2,1)S(1)} collective-permute-done((bf16[256,1024]{1,0:T(8,128)(2,1)S(1)}, bf16[256,1024]{1,0:T(8,128)(2,1)S(1)}, u32[]{:S(2)}, u32[]{:S(2)}) %collective-permute-start.3) | collective-permute-done | bytes 524320 | tf_op jit(solution)/shard_map/tokens_0_2/ppermute | solution.py:100
  17.6 10.3 %collective-permute-done.1.refs_8_ = bf16[256,1024]{1,0:T(8,128)(2,1)S(1)} collective-permute-done((bf16[256,1024]{1,0:T(8,128)(2,1)S(1)}, bf16[256,1024]{1,0:T(8,128)(2,1)S(1)}, u32[]{:S(2)}, u32[]{:S(2)}) %collective-permute-start.1) | collective-permute-done | bytes 524320 | tf_op jit(solution)/shard_map/tokens_1/ppermute | solution.py:100
  27.9 19.6 %collective-permute-done = bf16[384,1024]{1,0:T(8,128)(2,1)S(1)} collective-permute-done((bf16[384,1024]{1,0:T(8,128)(2,1)S(1)}, bf16[384,1024]{1,0:T(8,128)(2,1)S(1)}, u32[]{:S(2)}, u32[]{:S(2)}) %collective-permute-start) | collective-permute-done | bytes 786464 | tf_op jit(solution)/shard_map/tokens_weights_2/ppermute | solution.py:100
  47.6 3.1 %collective-permute-start.6 = (bf16[128,1024]{1,0:T(8,128)(2,1)S(1)}, bf16[128,1024]{1,0:T(8,128)(2,1)S(1)}, u32[]{:S(2)}, u32[]{:S(2)}) collective-permute-start(bf16[128,1024]{1,0:T(8,128)(2,1)S(1)} %copy-done.40), channel_id=1, source_target_pairs={{0,3},{1,2},{2,1},{3,0},{4,7},{5,6},{6,5},{7,4},{8,11},{9,10},{10,... | collective-permute-start | bytes 786440 | tf_op jit(solution)/shard_map/weights_3/ppermute | solution.py:100
  51.8 7.0 %collective-permute-done.6.refs_21_ = bf16[128,1024]{1,0:T(8,128)(2,1)S(1)} collective-permute-done((bf16[128,1024]{1,0:T(8,128)(2,1)S(1)}, bf16[128,1024]{1,0:T(8,128)(2,1)S(1)}, u32[]{:S(2)}, u32[]{:S(2)}) %collective-permute-start.6) | collective-permute-done | bytes 262176 | tf_op jit(solution)/shard_map/weights_3/ppermute | solution.py:100
  58.8 1.5 collective-permute-start.7
  60.2 4.9 %collective-permute-done.7.refs_20_ = bf16[128,1024]{1,0:T(8,128)(2,1)S(1)} collective-permute-done((bf16[128,1024]{1,0:T(8,128)(2,1)S(1)}, bf16[128,1024]{1,0:T(8,128)(2,1)S(1)}, u32[]{:S(2)}, u32[]{:S(2)}) %collective-permute-start.7) | collective-permute-done | bytes 262176 | tf_op jit(solution)/shard_map/weights_2/ppermute | solution.py:100
  65.1 2.3 %collective-permute-done.4.refs_0_ = bf16[256,1024]{1,0:T(8,128)(2,1)S(1)} collective-permute-done((bf16[256,1024]{1,0:T(8,128)(2,1)S(1)}, bf16[256,1024]{1,0:T(8,128)(2,1)S(1)}, u32[]{:S(2)}, u32[]{:S(2)}) %collective-permute-start.4) | collective-permute-done | bytes 524320 | tf_op jit(solution)/shard_map/tokens_3/ppermute | solution.py:100
  68.0 1.5 collective-permute-start.18
  70.0 11.1 %collective-permute-done.12.refs_2_ = bf16[256,1024]{1,0:T(8,128)(2,1)S(1)} collective-permute-done((bf16[256,1024]{1,0:T(8,128)(2,1)S(1)}, bf16[256,1024]{1,0:T(8,128)(2,1)S(1)}, u32[]{:S(2)}, u32[]{:S(2)}) %collective-permute-start.12) | collective-permute-done | bytes 524320 | tf_op jit(solution)/shard_map/tokens_3_2/ppermute | solution.py:100
  81.8 1.3 collective-permute-done.14.refs_5_
  85.6 24.6 %core.1 = (bf16[512,1024]{1,0:T(8,128)(2,1)}, bf16[512,1024]{1,0:T(8,128)(2,1)}, bf16[512,1024]{1,0:T(8,128)(2,1)}, bf16[512,1024]{1,0:T(8,128)(2,1)}, bf16[512,...) custom-call(bf16[256,1024]{1,0:T(8,128)(2,1)} %copy-done.26, ...), custom_call_target="tpu_custom_call" | custom-call | flops 10737418240 | bytes 20971520 | tf_op jit(solution)/shard_map/core/pallas_call | solution.py:250
  111.2 1.8 collective-permute-done.19
  113.1 1.1 slice_add_fusion.3
  114.8 1.6 collective-permute-start.20
  117.3 11.1 %collective-permute-done.20 = f32[2,1024]{1,0:T(2,128)S(1)} collective-permute-done((f32[2,1024]{1,0:T(2,128)S(1)}, f32[2,1024]{1,0:T(2,128)S(1)}, u32[]{:S(2)}, u32[]{:S(2)}) %collective-permute-start.20) | collective-permute-done | bytes 8224 | tf_op jit(solution)/shard_map/stats/ppermute | solution.py:100
  131.3 11.8 %collective-permute-done.24 = bf16[256,1024]{1,0:T(8,128)(2,1)} collective-permute-done((bf16[256,1024]{1,0:T(8,128)(2,1)}, bf16[256,1024]{1,0:T(8,128)(2,1)}, u32[]{:S(2)}, u32[]{:S(2)}) %collective-permute-start.24) | collective-permute-done | bytes 524320 | tf_op jit(solution)/shard_map/sums_2_2/ppermute | solution.py:100
  143.6 1.3 fusion.4
  144.9 1.1 collective-permute-start.28
  146.0 1.7 collective-permute-done.25
  147.7 1.7 add_convert_fusion.1
  149.8 2.5 %collective-permute-start.26 = (bf16[528,512]{1,0:T(8,128)(2,1)S(1)}, bf16[528,512]{1,0:T(8,128)(2,1)S(1)}, u32[]{:S(2)}, u32[]{:S(2)}) collective-permute-start(bf16[528,512]{1,0:T(8,128)(2,1)S(1)} %get-tuple-element.64), channel_id=1, source_target_pairs={{0,1},{1,0},{2,3},{3,2},{4,5},{5,4},{6,7},{7,6},{8,9},{9,8},{10,11... | collective-permute-start | bytes 1622024 | tf_op jit(solution)/shard_map/grads_1/ppermute | solution.py:100
  152.2 4.5 %collective-permute-done.31 = bf16[256,1024]{1,0:T(8,128)(2,1)S(1)} collective-permute-done((bf16[256,1024]{1,0:T(8,128)(2,1)}, bf16[256,1024]{1,0:T(8,128)(2,1)S(1)}, u32[]{:S(2)}, u32[]{:S(2)}) %collective-permute-start.31) | collective-permute-done | bytes 524320 | tf_op jit(solution)/shard_map/sums_1_2/ppermute | solution.py:100
  157.7 4.4 %collective-permute-done.28.refs_3_ = bf16[528,512]{1,0:T(8,128)(2,1)S(1)} collective-permute-done((bf16[528,512]{1,0:T(8,128)(2,1)S(1)}, bf16[528,512]{1,0:T(8,128)(2,1)S(1)}, u32[]{:S(2)}, u32[]{:S(2)}) %collective-permute-start.28) | collective-permute-done | bytes 540704 | tf_op jit(solution)/shard_map/grads_3/ppermute | solution.py:100
  162.1 20.2 %collective-permute-done.26.refs_1_ = bf16[528,512]{1,0:T(8,128)(2,1)S(1)} collective-permute-done((bf16[528,512]{1,0:T(8,128)(2,1)S(1)}, bf16[528,512]{1,0:T(8,128)(2,1)S(1)}, u32[]{:S(2)}, u32[]{:S(2)}) %collective-permute-start.26) | collective-permute-done | bytes 540704 | tf_op jit(solution)/shard_map/grads_1/ppermute | solution.py:100
  182.3 11.1 %collective-permute-done.34.refs_8_ = bf16[272,1024]{1,0:T(8,128)(2,1)S(1)} collective-permute-done((bf16[272,1024]{1,0:T(8,128)(2,1)S(1)}, bf16[272,1024]{1,0:T(8,128)(2,1)S(1)}, u32[]{:S(2)}, u32[]{:S(2)}) %collective-permute-start.34) | collective-permute-done | bytes 557088 | tf_op jit(solution)/shard_map/sums_2/ppermute | solution.py:100
  193.4 1.8 collective-permute-done.33.refs_7_
  195.2 3.9 %finish.1 = (bf16[128,1024]{1,0:T(8,128)(2,1)}, f32[128,1024]{1,0:T(8,128)}, f32[256,2048]{1,0:T(8,128)}, f32[2048,256]{1,0:T(8,128)}, f32[2,1024]{1,0:T(2,128)}) custom-call(bf16[512,512]{1,0:T(8,128)(2,1)S(1)} %copy-done.2, bf16[528,512]{1,0:T(8,128)(2,1)S(1)} %collective-permute-done.26.refs_1_, bf16[512,512]{1,0:T(8,128)(2,1)S(1)} %collective-permute-done.27.refs_2_, ...), custom_call_target="tpu_custom_call" | custom-call | bytes 6291456 | tf_op jit(solution)/shard_map/finish/pallas_call | solution.py:359
  (140 shorter events, 15.9 us)
Async XLA Ops:
  2.6 15.0 %collective-permute-start.3 = (bf16[256,1024]{1,0:T(8,128)(2,1)S(1)}, bf16[256,1024]{1,0:T(8,128)(2,1)S(1)}, u32[]{:S(2)}, u32[]{:S(2)}) collective-permute-start(bf16[256,1024]{1,0:T(8,128)(2,1)S(1)} %constant_dynamic-update-slice_fusion.refs_12_), channel_id=1, source_target_pairs={{0,8},{4,12},{8,0},{12,4},{1,9},{5,13},{9,1},{13,5},{2,10},{6,14},... | collective-permute-start | bytes 1572872 | tf_op jit(solution)/shard_map/tokens_0_2/ppermute | solution.py:100
  5.6 22.2 %collective-permute-start.1 = (bf16[256,1024]{1,0:T(8,128)(2,1)S(1)}, bf16[256,1024]{1,0:T(8,128)(2,1)S(1)}, u32[]{:S(2)}, u32[]{:S(2)}) collective-permute-start(bf16[256,1024]{1,0:T(8,128)(2,1)S(1)} %constant_dynamic-update-slice_fusion.refs_12_), channel_id=1, source_target_pairs={{0,1},{1,0},{2,3},{3,2},{4,5},{5,4},{6,7},{7,6},{8,9},{9,8},{10,11... | collective-permute-start | bytes 1572872 | tf_op jit(solution)/shard_map/tokens_1/ppermute | solution.py:100
  10.9 36.6 %collective-permute-start = (bf16[384,1024]{1,0:T(8,128)(2,1)S(1)}, bf16[384,1024]{1,0:T(8,128)(2,1)S(1)}, u32[]{:S(2)}, u32[]{:S(2)}) collective-permute-start(bf16[384,1024]{1,0:T(8,128)(2,1)S(1)} %pad_maximum_fusion), channel_id=1, source_target_pairs={{0,2},{1,3},{2,0},{3,1},{4,6},{5,7},{6,4},{7,5},{8,10},{9,11},{10,... | collective-permute-start | bytes 2359304 | tf_op jit(solution)/shard_map/tokens_weights_2/ppermute | solution.py:100
  13.6 34.0 %collective-permute-start.2 = (bf16[256,1024]{1,0:T(8,128)(2,1)S(1)}, bf16[256,1024]{1,0:T(8,128)(2,1)S(1)}, u32[]{:S(2)}, u32[]{:S(2)}) collective-permute-start(bf16[256,1024]{1,0:T(8,128)(2,1)S(1)} %copy-done.37), channel_id=1, source_target_pairs={{0,1},{1,0},{2,3},{3,2},{4,5},{5,4},{6,7},{7,6},{8,9},{9,8},{10,11... | collective-permute-start | bytes 1572872 | tf_op jit(solution)/shard_map/weights_1/ppermute | solution.py:100
  27.9 23.4 %collective-permute-start.8 = (bf16[256,1024]{1,0:T(8,128)(2,1)S(1)}, bf16[256,1024]{1,0:T(8,128)(2,1)S(1)}, u32[]{:S(2)}, u32[]{:S(2)}) collective-permute-start(bf16[256,1024]{1,0:T(8,128)(2,1)S(1)} %collective-permute-done.1.refs_8_), channel_id=1, source_target_pairs={{0,8},{4,12},{8,0},{12,4},{1,9},{5,13},{9,1},{13,5},{2,10},{6,14},... | collective-permute-start | bytes 1572872 | tf_op jit(solution)/shard_map/tokens_1_2/ppermute | solution.py:100
  47.6 11.1 %collective-permute-start.6 = (bf16[128,1024]{1,0:T(8,128)(2,1)S(1)}, bf16[128,1024]{1,0:T(8,128)(2,1)S(1)}, u32[]{:S(2)}, u32[]{:S(2)}) collective-permute-start(bf16[128,1024]{1,0:T(8,128)(2,1)S(1)} %copy-done.40), channel_id=1, source_target_pairs={{0,3},{1,2},{2,1},{3,0},{4,7},{5,6},{6,5},{7,4},{8,11},{9,10},{10,... | collective-permute-start | bytes 786440 | tf_op jit(solution)/shard_map/weights_3/ppermute | solution.py:100
  50.7 16.7 %collective-permute-start.4 = (bf16[256,1024]{1,0:T(8,128)(2,1)S(1)}, bf16[256,1024]{1,0:T(8,128)(2,1)S(1)}, u32[]{:S(2)}, u32[]{:S(2)}) collective-permute-start(bf16[256,1024]{1,0:T(8,128)(2,1)S(1)} %slice.64.refs_4_), channel_id=1, source_target_pairs={{0,1},{1,0},{2,3},{3,2},{4,5},{5,4},{6,7},{7,6},{8,9},{9,8},{10,11... | collective-permute-start | bytes 1572872 | tf_op jit(solution)/shard_map/tokens_3/ppermute | solution.py:100
  50.7 16.7 %collective-permute-start.10 = (bf16[256,1024]{1,0:T(8,128)(2,1)S(1)}, bf16[256,1024]{1,0:T(8,128)(2,1)S(1)}, u32[]{:S(2)}, u32[]{:S(2)}) collective-permute-start(bf16[256,1024]{1,0:T(8,128)(2,1)S(1)} %constant_dynamic-update-slice_fusion.refs_12_), channel_id=1, source_target_pairs={{0,4},{4,0},{8,12},{12,8},{1,5},{5,1},{9,13},{13,9},{2,6},{6,2},{1... | collective-permute-start | bytes 1572872 | tf_op jit(solution)/shard_map/tokens_0_1/ppermute | solution.py:100
  50.7 16.7 %collective-permute-start.11 = (bf16[256,1024]{1,0:T(8,128)(2,1)S(1)}, bf16[256,1024]{1,0:T(8,128)(2,1)S(1)}, u32[]{:S(2)}, u32[]{:S(2)}) collective-permute-start(bf16[256,1024]{1,0:T(8,128)(2,1)S(1)} %collective-permute-done.3.refs_14_), channel_id=1, source_target_pairs={{0,4},{4,0},{8,12},{12,8},{1,5},{5,1},{9,13},{13,9},{2,6},{6,2},{1... | collective-permute-start | bytes 1572872 | tf_op jit(solution)/shard_map/tokens_0_3/ppermute | solution.py:100
  51.2 16.2 %collective-permute-start.9 = (bf16[256,1024]{1,0:T(8,128)(2,1)S(1)}, bf16[256,1024]{1,0:T(8,128)(2,1)S(1)}, u32[]{:S(2)}, u32[]{:S(2)}) collective-permute-start(bf16[256,1024]{1,0:T(8,128)(2,1)S(1)} %slice.64.refs_4_), channel_id=1, source_target_pairs={{0,8},{4,12},{8,0},{12,4},{1,9},{5,13},{9,1},{13,5},{2,10},{6,14},... | collective-permute-start | bytes 1572872 | tf_op jit(solution)/shard_map/tokens_2_2/ppermute | solution.py:100
  58.8 6.4 %collective-permute-start.7 = (bf16[128,1024]{1,0:T(8,128)(2,1)S(1)}, bf16[128,1024]{1,0:T(8,128)(2,1)S(1)}, u32[]{:S(2)}, u32[]{:S(2)}) collective-permute-start(bf16[128,1024]{1,0:T(8,128)(2,1)S(1)} %slice.65.refs_19_), channel_id=1, source_target_pairs={{0,16},{16,0},{1,17},{17,1},{2,18},{18,2},{3,19},{19,3},{4,20},{20... | collective-permute-start | bytes 786440 | tf_op jit(solution)/shard_map/weights_2/ppermute | solution.py:100
  67.5 13.7 %collective-permute-start.12 = (bf16[256,1024]{1,0:T(8,128)(2,1)S(1)}, bf16[256,1024]{1,0:T(8,128)(2,1)S(1)}, u32[]{:S(2)}, u32[]{:S(2)}) collective-permute-start(bf16[256,1024]{1,0:T(8,128)(2,1)S(1)} %collective-permute-done.4.refs_0_), channel_id=1, source_target_pairs={{0,8},{4,12},{8,0},{12,4},{1,9},{5,13},{9,1},{13,5},{2,10},{6,14},... | collective-permute-start | bytes 1572872 | tf_op jit(solution)/shard_map/tokens_3_2/ppermute | solution.py:100
  68.0 13.6 %collective-permute-start.16 = (bf16[256,1024]{1,0:T(8,128)(2,1)S(1)}, bf16[256,1024]{1,0:T(8,128)(2,1)S(1)}, u32[]{:S(2)}, u32[]{:S(2)}) collective-permute-start(bf16[256,1024]{1,0:T(8,128)(2,1)S(1)} %collective-permute-done.1.refs_8_), channel_id=1, source_target_pairs={{0,4},{4,0},{8,12},{12,8},{1,5},{5,1},{9,13},{13,9},{2,6},{6,2},{1... | collective-permute-start | bytes 1572872 | tf_op jit(solution)/shard_map/tokens_1_1/ppermute | solution.py:100
  68.0 13.1 %collective-permute-start.18 = (bf16[128,1024]{1,0:T(8,128)(2,1)S(1)}, bf16[128,1024]{1,0:T(8,128)(2,1)}, u32[]{:S(2)}, u32[]{:S(2)}) collective-permute-start(bf16[128,1024]{1,0:T(8,128)(2,1)S(1)} %collective-permute-done.6.refs_21_), channel_id=1, source_target_pairs={{0,16},{16,0},{1,17},{17,1},{2,18},{18,2},{3,19},{19,3},{4,20},{20... | collective-permute-start | bytes 786440 | tf_op jit(solution)/shard_map/weights_3/ppermute | solution.py:100
  69.5 12.2 %collective-permute-start.17 = (bf16[256,1024]{1,0:T(8,128)(2,1)S(1)}, bf16[256,1024]{1,0:T(8,128)(2,1)S(1)}, u32[]{:S(2)}, u32[]{:S(2)}) collective-permute-start(bf16[256,1024]{1,0:T(8,128)(2,1)S(1)} %collective-permute-done.8.refs_10_), channel_id=1, source_target_pairs={{0,4},{4,0},{8,12},{12,8},{1,5},{5,1},{9,13},{13,9},{2,6},{6,2},{1... | collective-permute-start | bytes 1572872 | tf_op jit(solution)/shard_map/tokens_1_3/ppermute | solution.py:100
  69.8 12.0 %collective-permute-start.5 = (bf16[256,1024]{1,0:T(8,128)(2,1)S(1)}, bf16[256,1024]{1,0:T(8,128)(2,1)S(1)}, u32[]{:S(2)}, u32[]{:S(2)}) collective-permute-start(bf16[256,1024]{1,0:T(8,128)(2,1)S(1)} %collective-permute-done.4.refs_0_), channel_id=1, source_target_pairs={{0,4},{4,0},{8,12},{12,8},{1,5},{5,1},{9,13},{13,9},{2,6},{6,2},{1... | collective-permute-start | bytes 1572872 | tf_op jit(solution)/shard_map/tokens_3_1/ppermute | solution.py:100
  81.7 2.9 %collective-permute-start.13 = (bf16[256,1024]{1,0:T(8,128)(2,1)S(1)}, bf16[256,1024]{1,0:T(8,128)(2,1)S(1)}, u32[]{:S(2)}, u32[]{:S(2)}) collective-permute-start(bf16[256,1024]{1,0:T(8,128)(2,1)S(1)} %collective-permute-done.12.refs_2_), channel_id=1, source_target_pairs={{0,4},{4,0},{8,12},{12,8},{1,5},{5,1},{9,13},{13,9},{2,6},{6,2},{1... | collective-permute-start | bytes 1572872 | tf_op jit(solution)/shard_map/tokens_3_3/ppermute | solution.py:100
  110.2 2.9 %collective-permute-start.19 = (bf16[512,1024]{1,0:T(8,128)(2,1)}, bf16[512,1024]{1,0:T(8,128)(2,1)S(1)}, u32[]{:S(2)}, u32[]{:S(2)}) collective-permute-start(bf16[512,1024]{1,0:T(8,128)(2,1)} %get-tuple-element.59), channel_id=1, source_target_pairs={{0,4},{4,0},{8,12},{12,8},{1,5},{5,1},{9,13},{13,9},{2,6},{6,2},{1... | collective-permute-start | bytes 3145736 | tf_op jit(solution)/shard_map/sums_3_1/ppermute | solution.py:100
  110.4 4.4 %collective-permute-start.22 = (bf16[512,1024]{1,0:T(8,128)(2,1)}, bf16[512,1024]{1,0:T(8,128)(2,1)S(1)}, u32[]{:S(2)}, u32[]{:S(2)}) collective-permute-start(bf16[512,1024]{1,0:T(8,128)(2,1)} %get-tuple-element.62), channel_id=1, source_target_pairs={{0,4},{4,0},{8,12},{12,8},{1,5},{5,1},{9,13},{13,9},{2,6},{6,2},{1... | collective-permute-start | bytes 3145736 | tf_op jit(solution)/shard_map/sums_2_1/ppermute | solution.py:100
  110.7 6.5 %collective-permute-start.29 = (bf16[512,1024]{1,0:T(8,128)(2,1)}, bf16[512,1024]{1,0:T(8,128)(2,1)S(1)}, u32[]{:S(2)}, u32[]{:S(2)}) collective-permute-start(bf16[512,1024]{1,0:T(8,128)(2,1)} %get-tuple-element.69), channel_id=1, source_target_pairs={{0,4},{4,0},{8,12},{12,8},{1,5},{5,1},{9,13},{13,9},{2,6},{6,2},{1... | collective-permute-start | bytes 3145736 | tf_op jit(solution)/shard_map/sums_0_1/ppermute | solution.py:100
  110.9 34.0 %collective-permute-start.27 = (bf16[512,512]{1,0:T(8,128)(2,1)}, bf16[512,512]{1,0:T(8,128)(2,1)S(1)}, u32[]{:S(2)}, u32[]{:S(2)}) collective-permute-start(bf16[512,512]{1,0:T(8,128)(2,1)} %get-tuple-element.65), channel_id=1, source_target_pairs={{0,2},{1,3},{2,0},{3,1},{4,6},{5,7},{6,4},{7,5},{8,10},{9,11},{10,... | collective-permute-start | bytes 1572872 | tf_op jit(solution)/shard_map/grads_2/ppermute | solution.py:100
  110.9 19.2 %collective-permute-start.30 = (bf16[512,1024]{1,0:T(8,128)(2,1)}, bf16[512,1024]{1,0:T(8,128)(2,1)S(1)}, u32[]{:S(2)}, u32[]{:S(2)}) collective-permute-start(bf16[512,1024]{1,0:T(8,128)(2,1)} %get-tuple-element.71), channel_id=1, source_target_pairs={{0,4},{4,0},{8,12},{12,8},{1,5},{5,1},{9,13},{13,9},{2,6},{6,2},{1... | collective-permute-start | bytes 3145736 | tf_op jit(solution)/shard_map/sums_1_1/ppermute | solution.py:100
  114.2 14.2 %collective-permute-start.23 = (bf16[256,1024]{1,0:T(8,128)(2,1)S(1)}, bf16[256,1024]{1,0:T(8,128)(2,1)S(1)}, u32[]{:S(2)}, u32[]{:S(2)}) collective-permute-start(bf16[256,1024]{1,0:T(8,128)(2,1)S(1)} %slice_add_fusion.3), channel_id=1, source_target_pairs={{0,8},{4,12},{8,0},{12,4},{1,9},{5,13},{9,1},{13,5},{2,10},{6,14},... | collective-permute-start | bytes 1572872 | tf_op jit(solution)/shard_map/sums_3_2/ppermute | solution.py:100
  114.8 13.6 %collective-permute-start.20 = (f32[2,1024]{1,0:T(2,128)S(1)}, f32[2,1024]{1,0:T(2,128)S(1)}, u32[]{:S(2)}, u32[]{:S(2)}) collective-permute-start(f32[2,1024]{1,0:T(2,128)S(1)} %copy-done.21), channel_id=1, source_target_pairs={{0,8},{4,12},{8,0},{12,4},{1,9},{5,13},{9,1},{13,5},{2,10},{6,14},... | collective-permute-start | bytes 24584 | tf_op jit(solution)/shard_map/stats/ppermute | solution.py:100
  128.4 14.7 %collective-permute-start.24 = (bf16[256,1024]{1,0:T(8,128)(2,1)}, bf16[256,1024]{1,0:T(8,128)(2,1)}, u32[]{:S(2)}, u32[]{:S(2)}) collective-permute-start(bf16[256,1024]{1,0:T(8,128)(2,1)} %slice_add_fusion.2), channel_id=1, source_target_pairs={{0,8},{4,12},{8,0},{12,4},{1,9},{5,13},{9,1},{13,5},{2,10},{6,14},... | collective-permute-start | bytes 1572872 | tf_op jit(solution)/shard_map/sums_2_2/ppermute | solution.py:100
  130.1 17.6 %collective-permute-start.25 = (bf16[256,1024]{1,0:T(8,128)(2,1)}, bf16[256,1024]{1,0:T(8,128)(2,1)}, u32[]{:S(2)}, u32[]{:S(2)}) collective-permute-start(bf16[256,1024]{1,0:T(8,128)(2,1)} %add_convert_fusion.2), channel_id=1, source_target_pairs={{0,1},{1,0},{2,3},{3,2},{4,5},{5,4},{6,7},{7,6},{8,9},{9,8},{10,11... | collective-permute-start | bytes 1572872 | tf_op jit(solution)/shard_map/sums_3/ppermute | solution.py:100
  143.1 13.7 %collective-permute-start.31 = (bf16[256,1024]{1,0:T(8,128)(2,1)}, bf16[256,1024]{1,0:T(8,128)(2,1)S(1)}, u32[]{:S(2)}, u32[]{:S(2)}) collective-permute-start(bf16[256,1024]{1,0:T(8,128)(2,1)} %slice_add_fusion), channel_id=1, source_target_pairs={{0,8},{4,12},{8,0},{12,4},{1,9},{5,13},{9,1},{13,5},{2,10},{6,14},... | collective-permute-start | bytes 1572872 | tf_op jit(solution)/shard_map/sums_1_2/ppermute | solution.py:100
  144.9 17.2 %collective-permute-start.28 = (bf16[528,512]{1,0:T(8,128)(2,1)S(1)}, bf16[528,512]{1,0:T(8,128)(2,1)S(1)}, u32[]{:S(2)}, u32[]{:S(2)}) collective-permute-start(bf16[528,512]{1,0:T(8,128)(2,1)S(1)} %get-tuple-element.67), channel_id=1, source_target_pairs={{0,3},{1,2},{2,1},{3,0},{4,7},{5,6},{6,5},{7,4},{8,11},{9,10},{10,... | collective-permute-start | bytes 1622024 | tf_op jit(solution)/shard_map/grads_3/ppermute | solution.py:100
  149.5 44.0 %collective-permute-start.34 = (bf16[272,1024]{1,0:T(8,128)(2,1)S(1)}, bf16[272,1024]{1,0:T(8,128)(2,1)S(1)}, u32[]{:S(2)}, u32[]{:S(2)}) collective-permute-start(bf16[272,1024]{1,0:T(8,128)(2,1)S(1)} %fusion.2), channel_id=1, source_target_pairs={{0,2},{1,3},{2,0},{3,1},{4,6},{5,7},{6,4},{7,5},{8,10},{9,11},{10,... | collective-permute-start | bytes 1671176 | tf_op jit(solution)/shard_map/sums_2/ppermute | solution.py:100
  149.8 32.5 %collective-permute-start.26 = (bf16[528,512]{1,0:T(8,128)(2,1)S(1)}, bf16[528,512]{1,0:T(8,128)(2,1)S(1)}, u32[]{:S(2)}, u32[]{:S(2)}) collective-permute-start(bf16[528,512]{1,0:T(8,128)(2,1)S(1)} %get-tuple-element.64), channel_id=1, source_target_pairs={{0,1},{1,0},{2,3},{3,2},{4,5},{5,4},{6,7},{7,6},{8,9},{9,8},{10,11... | collective-permute-start | bytes 1622024 | tf_op jit(solution)/shard_map/grads_1/ppermute | solution.py:100
  157.1 36.3 %collective-permute-start.32 = (bf16[256,1024]{1,0:T(8,128)(2,1)S(1)}, bf16[256,1024]{1,0:T(8,128)(2,1)S(1)}, u32[]{:S(2)}, u32[]{:S(2)}) collective-permute-start(bf16[256,1024]{1,0:T(8,128)(2,1)S(1)} %slice_add_fusion.1), channel_id=1, source_target_pairs={{0,8},{4,12},{8,0},{12,4},{1,9},{5,13},{9,1},{13,5},{2,10},{6,14},... | collective-permute-start | bytes 1572872 | tf_op jit(solution)/shard_map/sums_0_2/ppermute | solution.py:100
  157.7 37.5 %collective-permute-start.33 = (bf16[256,1024]{1,0:T(8,128)(2,1)S(1)}, bf16[256,1024]{1,0:T(8,128)(2,1)S(1)}, u32[]{:S(2)}, u32[]{:S(2)}) collective-permute-start(bf16[256,1024]{1,0:T(8,128)(2,1)S(1)} %add_convert_fusion), channel_id=1, source_target_pairs={{0,1},{1,0},{2,3},{3,2},{4,5},{5,4},{6,7},{7,6},{8,9},{9,8},{10,11... | collective-permute-start | bytes 1572872 | tf_op jit(solution)/shard_map/sums_1/ppermute | solution.py:100
  (44 other events, 840.2 us)

commit v9 on v8

--- a/solution.py
+++ b/solution.py
@@ -8,6 +8,7 @@
 from jax.sharding import PartitionSpec as P
 
 epsilon = 1e-06
+EXTRA = 16
 
 
 def normalize(row_data, norm_gain, norm_bias):
@@ -104,39 +105,37 @@
     return [1 << b for b in reversed(range(size.bit_length() - 1))]
 
 
-def share(k, n_dp, mates):
-    return mates if k >= bits_of(n_dp)[0] else 1
-
-
-def pack_weights(w_up, w_down, mates):
-    n_dp = lax.axis_size("dp")
+def pack(first_out, grad_second, w_up, w_down, mates):
+    n_dp, (own_rows, width) = lax.axis_size("dp"), first_out.shape
     depth, units = w_up.shape[0], w_up.shape[1] // n_dp
-    strips = units // depth
-
-    def kernel(up_ref, down_ref, *sends):
+    strips, rows = units // depth, depth // mates
+
+    def kernel(first_ref, grad_ref, up_ref, down_ref, own, *sends):
         place, mate = lax.axis_index("dp"), lax.rem(lax.axis_index("groups"), mates)
+        for ref in [own] + [sends[bit - 1] for bit in bits_of(n_dp)]:
+            ref[:own_rows, :] = first_ref[...]
+            ref[own_rows : 2 * own_rows, :] = grad_ref[...]
         for k in range(1, n_dp):
-            n = share(k, n_dp, mates)
-            part = mate if n > 1 else 0
-            rows = depth // n
             first = pl.multiple_of((place ^ k) * units, units)
-            send = sends[k - 1]
-            send[:, :units] = up_ref[pl.ds(pl.multiple_of(part * rows, rows), rows), pl.ds(first, units)]
+            send, skip = sends[k - 1], 0 if k & (k - 1) else 2 * own_rows
+            span = slice(skip, skip + rows)
+            send[span, :units] = up_ref[pl.ds(pl.multiple_of(mate * rows, rows), rows), pl.ds(first, units)]
             for c in range(strips):
-                row = pl.multiple_of(first + part * (units // n) + c * rows, rows)
-                send[:, units + c * depth : units + (c + 1) * depth] = down_ref[pl.ds(row, rows), :]
+                row = pl.multiple_of(first + mate * (units // mates) + c * rows, rows)
+                send[span, units + c * depth : units + (c + 1) * depth] = down_ref[pl.ds(row, rows), :]
 
     return pl.pallas_call(
         kernel,
-        out_shape=[
-            jax.ShapeDtypeStruct((depth // share(k, n_dp, mates), 2 * units), w_up.dtype)
+        out_shape=[jax.ShapeDtypeStruct((2 * own_rows, width), w_up.dtype)]
+        + [
+            jax.ShapeDtypeStruct((rows + (0 if k & (k - 1) else 2 * own_rows), width), w_up.dtype)
             for k in range(1, n_dp)
         ],
-        in_specs=[pl.BlockSpec(memory_space=pltpu.VMEM)] * 2,
-        out_specs=[pl.BlockSpec(memory_space=pltpu.VMEM)] * (n_dp - 1),
+        in_specs=[pl.BlockSpec(memory_space=pltpu.VMEM)] * 4,
+        out_specs=[pl.BlockSpec(memory_space=pltpu.VMEM)] * n_dp,
         cost_estimate=pl.CostEstimate(flops=0, bytes_accessed=8 * w_up.size, transcendentals=0),
-        name="pack_weights",
-    )(w_up, w_down)
+        name="pack",
+    )(first_out, grad_second, w_up, w_down)
 
 
 def core(chunks, w_up, w_down, got, mates, gain, bias):
@@ -159,7 +158,8 @@
             refs[4 + n_got :],
         )
         outs, blocks, stat_ref = refs[: 2 * n_chunks], refs[2 * n_chunks : 2 * n_chunks + n_dp], refs[2 * n_chunks + n_dp]
-        tok, norm, hid, pre, part, block, up_ref, down_ref, in_sem, w_sem, out_sem, b_sem = refs[2 * n_chunks + n_dp + 1 :]
+        scratch = refs[2 * n_chunks + n_dp + 1 :]
+        tok, norm, hid, pre, part, block, up_ref, down_ref, total, in_sem, w_sem, out_sem, b_sem = scratch
         place, mate = lax.axis_index("dp"), lax.rem(lax.axis_index("groups"), mates)
         reads, loads, writes = [], [], []
 
@@ -192,7 +192,7 @@
                     )
         for one in reads[n:]:
             one.start()
-        stat_ref[...] = jnp.zeros_like(stat_ref)
+        total[...] = jnp.zeros_like(total)
         for i in range(n_chunks):
             for one in reads[i * n : (i + 1) * n] + (loads if i == 0 else []):
                 one.wait()
@@ -218,8 +218,8 @@
                 pre[span, :] = grad_pre
                 branch = jnp.dot(hidden, down_ref[...], preferred_element_type=jnp.float32)
                 grad_normed = contract_last(grad_pre, up_ref[...])
-                stat_ref[0:1, :] += jnp.sum(grad_normed * standard, axis=0, keepdims=True)
-                stat_ref[1:2, :] += jnp.sum(grad_normed, axis=0, keepdims=True)
+                total[0:1, :] += jnp.sum(grad_normed * standard, axis=0, keepdims=True)
+                total[1:2, :] += jnp.sum(grad_normed, axis=0, keepdims=True)
                 row = pl.multiple_of(t * pair, pair)
                 for odd in range(2):
                     own = slice(odd * piece_rows, (odd + 1) * piece_rows)
@@ -228,8 +228,15 @@
 
             for odd in (1, 0):
                 at = 2 * i + odd
-                writes.append(pltpu.make_async_copy(part.at[at], outs[at], out_sem.at[at]))
+                out = outs[at].at[pl.ds(0, half[0]), :]
+                writes.append(pltpu.make_async_copy(part.at[at], out, out_sem.at[at]))
                 writes[-1].start()
+        stat_ref[...] = jnp.zeros_like(stat_ref)
+        stat_ref[0:2, :] = total[0:2, :].astype(dtype)
+        stat_ref[2:4, :] = (total[0:2, :] - stat_ref[0:2, :].astype(jnp.float32)).astype(dtype)
+        tail = outs[1].at[pl.ds(half[0], EXTRA), :]
+        writes.append(pltpu.make_async_copy(stat_ref, tail, out_sem.at[2 * n_chunks]))
+        writes[-1].start()
         top = bits_of(n_dp)[0]
         for k in sorted(range(n_dp), key=lambda k: (k < top, k)):
             columns = pl.ds(pl.multiple_of((place ^ k) * depth, depth), depth)
@@ -249,9 +256,11 @@
     near = pl.BlockSpec(memory_space=pltpu.VMEM)
     out = pl.pallas_call(
         kernel,
-        out_shape=[jax.ShapeDtypeStruct(half, dtype)] * (2 * n_chunks)
+        out_shape=[
+            jax.ShapeDtypeStruct((half[0] + (EXTRA if at == 1 else 0), width), dtype) for at in range(2 * n_chunks)
+        ]
         + [jax.ShapeDtypeStruct((2 * depth, units), dtype)] * n_dp
-        + [jax.ShapeDtypeStruct((2, width), jnp.float32)],
+        + [jax.ShapeDtypeStruct((EXTRA, width), dtype)],
         in_specs=[far] * (n_chunks * n + 2 + n_got) + [near] * 2,
         out_specs=[far] * (2 * n_chunks + n_dp) + [near],
         scratch_shapes=[
@@ -263,9 +272,10 @@
             pltpu.VMEM((n_dp, 2 * depth, units), dtype),
             pltpu.VMEM((width, units), dtype),
             pltpu.VMEM((units, width), dtype),
+            pltpu.VMEM((EXTRA, width), jnp.float32),
             pltpu.SemaphoreType.DMA((n_chunks * n,)),
             pltpu.SemaphoreType.DMA((2 + n_got * (1 + strips),)),
-            pltpu.SemaphoreType.DMA((2 * n_chunks,)),
+            pltpu.SemaphoreType.DMA((2 * n_chunks + 1,)),
             pltpu.SemaphoreType.DMA((n_dp,)),
         ],
         compiler_params=pltpu.CompilerParams(vmem_limit_bytes=56 * 1024 * 1024),
@@ -287,10 +297,10 @@
     return halves, list(out[2 * n_chunks : -1]), out[-1]
 
 
-def finish(blocks, terms, own_stats, first_out, second_out, grad_first, gain, bias, w_shapes, scale):
+def finish(blocks, terms, stats, first_out, second_out, grad_first, gain, bias, w_shapes, scale):
     (rows, width), n_dp = first_out.shape, len(blocks)
     depth, units = w_shapes[0][0], w_shapes[0][1] // n_dp
-    strips, top, n_terms = units // depth, bits_of(n_dp)[0], len(terms)
+    strips, n_terms = units // depth, len(terms)
 
     def kernel(*refs):
         parts, adds, (stat_ref, first_ref, second_ref, grad_ref, gain_ref, bias_ref), outs = (
@@ -321,31 +331,13 @@
             - standard * jnp.mean(grad_std * standard, axis=-1, keepdims=True)
         )
         grad_in[...] = grad_ref[...].astype(jnp.float32) + grad_rows
-        stats = []
-        for k in range(n_dp):
-            if k == 0:
-                one = stat_ref[...].astype(jnp.float32)
-            elif k == top:
-                one = adds[-1][2 * rows :, :].astype(jnp.float32)[:2]
-            else:
-                tail = parts[k][2 * depth :, :].astype(jnp.float32)
-                per = width // units
-                one = jnp.concatenate(
-                    [
-                        jnp.concatenate([tail[i * per + j : i * per + j + 1] for j in range(per)], axis=1)
-                        for i in range(2)
-                    ],
-                    axis=0,
-                )
-            stats.append(one)
-        while len(stats) > 1:
-            stats = [one + two for one, two in zip(stats[0::2], stats[1::2], strict=True)]
-        norm_out[...] = stats[0] * scale
+        one, two = stat_ref[...].astype(jnp.float32), adds[-1][2 * rows :, :].astype(jnp.float32)
+        norm_out[...] = ((one[0:2] + one[2:4]) + (two[0:2] + two[2:4])) * scale
 
     def whole(x):
         return pl.BlockSpec(x.shape, lambda i: (0, 0))
 
-    arrays = [*blocks, *terms, own_stats, first_out, second_out, grad_first, gain.reshape(1, width), bias.reshape(1, width)]
+    arrays = [*blocks, *terms, stats, first_out, second_out, grad_first, gain.reshape(1, width), bias.reshape(1, width)]
     in_specs = [whole(x) for x in arrays]
     for i in range(n_terms - 1):
         in_specs[n_dp + i] = pl.BlockSpec((2 * rows, width), lambda i: (0, 0))
@@ -370,6 +362,46 @@
     )(*arrays)
 
 
+def join(rows, terms, stats=()):
+    width = terms[0][0].shape[1]
+    arrays = [*terms, *stats]
+    n_terms = len(terms)
+
+    def kernel(*refs):
+        out = refs[len(arrays)]
+        total = sum(ref[...].astype(jnp.float32) for ref in refs[:n_terms])
+        out[:rows, :] = total.astype(out.dtype)
+        if stats:
+            one, two = (ref[...].astype(jnp.float32) for ref in refs[n_terms : n_terms + 2])
+            both = (one[0:2] + one[2:4]) + (two[0:2] + two[2:4])
+            tail = refs[-1]
+            tail[...] = jnp.zeros_like(tail)
+            tail[0:2, :] = both.astype(tail.dtype)
+            tail[2:4, :] = (both - tail[0:2, :].astype(jnp.float32)).astype(tail.dtype)
+            out[rows:, :] = tail[...]
+
+    def spec(height, place):
+        return pl.BlockSpec((height, width), lambda i: (place, 0))
+
+    out_shape = [jax.ShapeDtypeStruct((rows + (EXTRA if stats else 0), width), jnp.bfloat16)]
+    out_specs = [spec(out_shape[0].shape[0], 0)]
+    if stats:
+        out_shape.append(jax.ShapeDtypeStruct((EXTRA, width), jnp.bfloat16))
+        out_specs.append(spec(EXTRA, 0))
+    out = pl.pallas_call(
+        kernel,
+        out_shape=out_shape,
+        grid=(1,),
+        in_specs=[spec(rows, place) for _, place in terms] + [spec(EXTRA, place) for _, place in stats],
+        out_specs=out_specs,
+        cost_estimate=pl.CostEstimate(
+            flops=0, bytes_accessed=2 * (len(terms) + 1) * rows * width, transcendentals=0
+        ),
+        name="join",
+    )(*(x for x, _ in arrays))
+    return out if stats else out[0]
+
+
 def after(values, *others):
     return lax.optimization_barrier((values, *others))[0]
 
@@ -385,7 +417,7 @@
     top = bits_of(n_dp)[0]
 
     high, others = bits_of(n_tensor)[0], bits_of(n_tensor)[1:]
-    own = jnp.concatenate([first_out, grad_second])
+    own, *sends = pack(first_out, grad_second, w_up, w_down, mates)
     tokens, chunks, got, crossed = {0: own}, {}, {}, {}
 
     def tokens_dp(k, *first):
@@ -401,37 +433,29 @@
                 piece = after(chunks[k][j], *first)
                 chunks[k][j | bit] = swap(piece, "tensor", bit, f"tokens_{k}_{j | bit}")
 
-    def weights_dp(k, *first):
-        got[k] = swap(after(sends[k - 1], *first), "dp", k, f"weights_{k}")
-
     def weights_groups(k, *first):
-        crossed[k] = swap(after(got[k], *first), "groups", 1, f"weights_{k}")
+        if mates == 2:
+            crossed[k] = swap(after(got[k], *first), "groups", 1, f"weights_{k}")
 
     tokens_tensor(0)
-    for bit in bits_of(n_dp)[:0:-1]:
-        tokens_dp(bit)
-    sends = pack_weights(w_up, w_down, mates)
-    both = swap(jnp.concatenate([own, sends[top - 1]]), "dp", top, f"tokens_weights_{top}")
-    tokens[top], got[top] = both[: 2 * own_rows], both[2 * own_rows :]
-    for bit in bits_of(n_dp)[1:]:
-        weights_dp(bit)
+    tokens_rest(0)
+    for bit in reversed(bits_of(n_dp)):
+        both = swap(sends[bit - 1], "dp", bit, f"tokens_weights_{bit}")
+        tokens[bit], got[bit] = both[: 2 * own_rows], both[2 * own_rows :]
     tokens_tensor(1, tokens[1], chunks[0][high])
-    stage = [*tokens.values(), *got.values(), chunks[0][high]]
-    tokens_rest(0, *stage)
+    stage = [*tokens.values(), *got.values(), *chunks[0].values()]
+    for bit in reversed(bits_of(n_dp)):
+        weights_groups(bit, *stage)
     for k in range(2, n_dp):
         if k & (k - 1):
             tokens_dp(k, *stage)
-            weights_dp(k, *stage)
-            if mates == 2 and top not in crossed:
-                weights_groups(top, *stage)
-            stage = [tokens[k], got[k], *crossed.values(), chunks[k - 1][high], *chunks[0].values()]
-        tokens_tensor(k, *stage, chunks[k - 1][high])
-        tokens_rest(k - 1, *stage)
-    tokens_rest(n_dp - 1)
-    if mates == 2:
-        for k in range(top, n_dp):
-            if k not in crossed:
-                weights_groups(k)
+            got[k] = swap(after(sends[k - 1], *stage, chunks[1][high]), "dp", k, f"weights_{k}")
+            stage = [tokens[k], got[k], *crossed.values()]
+        tokens_rest(k - 1)
+        tokens_tensor(k, *stage, *(chunks[k - 2].values() if k > top else ()), chunks[k - 1][high])
+        if k & (k - 1):
+            weights_groups(k)
+    tokens_rest(n_dp - 1, *crossed.values())
     got = {k: [got[k]] + ([crossed[k]] if k in crossed else []) for k in got}
 
     order = sorted(chunks, reverse=True)
@@ -441,49 +465,49 @@
     blocks = dict(enumerate(blocks))
     blocks[top] = swap(blocks[top], "dp", top, f"grads_{top}")
 
-    sums, behind, hops = {}, (), []
+    for k in range(top + 1, n_dp):
+        blocks[k] = swap(blocks[k], "dp", k, f"grads_{k}")
+
+    sums, behind, span, waiting = {}, (), 2 * own_rows, None
     for k, (even, odd) in zip(order, halves, strict=True):
         came = swap(odd, "tensor", 1, f"sums_{k}_1")
-        spans = [slice(j * 2 * own_rows, (j + 1) * 2 * own_rows) for j in range(n_tensor // 2)]
-        parts = {2 * j: (even[span], came[span]) for j, span in enumerate(spans)}
-        parts[0] = (even, came)
+        if k == order[0]:
+            waiting = (came, even.shape[0] // EXTRA)
+        parts = {2 * j: [(x, j) for x in (even, came)] for j in range(n_tensor // 2)}
         for bit in reversed(bits_of(n_tensor)[:-1]):
             for j in [j for j in parts if j & bit]:
-                send = after(sum(parts.pop(j)), *behind)
-                if not hops:
-                    stats = after(stats, send)
-                parts[j ^ bit] += (swap(send, "tensor", bit, f"sums_{k}_{j}"),)
-                behind = parts[j ^ bit][-1:]
-                hops += behind
+                if k == order[0] and j == bit:
+                    send, stats = join(span, parts.pop(j), [(stats, 0), waiting])
+                else:
+                    send = join(span, parts.pop(j))
+                if k < 2:
+                    behind += (blocks[n_dp - 1 if k == 0 else top],)
+                came = swap(after(send, *behind), "tensor", bit, f"sums_{k}_{j}")
+                if k == order[0] and j == bit:
+                    waiting = (came, span // EXTRA)
+                parts[j ^ bit].append((came, 0))
+                behind = (came,)
         sums[k] = parts[0]
-
-    def add(terms):
-        return sum(term[: 2 * own_rows].astype(jnp.float32) for term in terms).astype(jnp.bfloat16)
-
-    for bit in bits_of(n_tensor):
-        stats = stats + swap(stats, "tensor", bit, "stats")
-    stats = stats.astype(jnp.bfloat16)
-    extra = 16
-
     came = {}
     for bit in bits_of(n_dp)[::-1]:
         for k in [k for k in order if k & bit and k in sums and k != bit]:
-            came[k] = swap(add(sums.pop(k)), "dp", bit, f"sums_{k}")
-            sums[k ^ bit] += (came[k],)
-    last = jnp.concatenate([add(sums[top]), jnp.pad(stats, ((0, extra - 2), (0, 0)))])
+            if k == (n_dp - 1) & -bit:
+                send, stats = join(span, sums.pop(k), [(stats, 0), waiting])
+            else:
+                send = join(span, sums.pop(k))
+            came[k] = swap(send, "dp", bit, f"sums_{k}")
+            if k == (n_dp - 1) & -bit:
+                waiting = (came[k], span // EXTRA)
+            sums[k ^ bit].append((came[k], 0))
+    last, stats = join(span, sums[top], [(stats, 0), waiting])
     came[top] = swap(last, "dp", top, f"sums_{top}")
-    rows = stats.reshape(-1, units)
-    rows = jnp.pad(rows, ((0, extra - rows.shape[0]), (0, 0)))
-    for k in range(1, n_dp):
-        if k != top:
-            block = jnp.concatenate([blocks[k], rows])
-            first = [last] if k < top else [blocks[top], *hops[:1]]
-            blocks[k] = swap(after(block, *first), "dp", k, f"grads_{k}")
     for bit in bits_of(n_dp)[:0:-1]:
-        came[bit] = swap(after(add(sums[bit]), last), "dp", bit, f"sums_{bit}")
+        came[bit] = swap(after(join(span, sums[bit]), last), "dp", bit, f"sums_{bit}")
+    for k in range(1, top):
+        blocks[k] = swap(after(blocks[k], last), "dp", k, f"grads_{k}")
 
     scale = (own_rows * n_tensor * n_dp) ** (-0.5)
-    terms = [*sums[0], *(came[bit] for bit in bits_of(n_dp)[::-1])]
+    terms = [*(x for x, _ in sums[0]), *(came[bit] for bit in bits_of(n_dp)[::-1])]
     return tuple(
         finish(
             [blocks[k] for k in range(n_dp)],

time: 199 us -> 215 us (1.080)
  Pallas kernels: 31 us -> 48.4 us
  other arithmetic: 8.37 us -> 0 us
  starting transfers between devices: 25.3 us -> 30.9 us
  local copies, waits for them, and re-layouts: 3.18 us -> 5.42 us
    pallas_call x2 -> x9, Pallas kernels: 27.2 us -> 44.2 us  [the longest x1 24.6 us: core(): pl.pallas_call(kernel, out_shape=[jax.ShapeDtypeStruct((half[0] + (EXTRA...]
    ppermute x35 -> x33, starting transfers between devices: 25.3 us -> 30.9 us  [swap(): lax.ppermute(values, axis, [(i, i ^ mask) for i in range(lax.axis_size(ax...]
    unnamed x83 -> x66, local copies, waits for them, and re-layouts: 2.15 us -> 5.32 us
    convert_element_type x4 -> x0, other arithmetic: 3 us -> none  [the longest x3 3 us: add(): sum((term[:2 * own_rows].astype(jnp.float32) for term in terms))]
    add x5 -> x0, other arithmetic: 3 us -> none  [the longest x4 2.99 us: gather_tokens_body(): send = after(sum(parts.pop(j)), *behind)]
    concatenate x3 -> x0, other arithmetic: 2.37 us -> none  [the longest x1 1.27 us: gather_tokens_body(): block = jnp.concatenate([blocks[k], rows])]
    ppermute x35 -> x33, waiting for transfers between devices: 130 us -> 129 us  [swap(): lax.ppermute(values, axis, [(i, i ^ mask) for i in range(lax.axis_size(ax...]
  transfers between devices with their start and end apart: 35 -> 33, of which waited for: 19 -> 17; matrix products, arithmetic and copies ran while one was open for 4% -> 0% of each run, Pallas kernels for 1% -> 8%
where the time goes in v9:
time: 215 us; the launch traced here: 214 us
  waiting for transfers between devices  129 us (60%)
  Pallas kernels  48.4 us (23%)
  starting transfers between devices  30.9 us (14%)
  local copies, waits for them, and re-layouts  5.42 us (3%)
    ppermute x33, waiting for transfers between devices, swap(): lax.ppermute(values, axis, [(i, i ^ mask) for i in range(lax.axis_size(ax...  129 us
    ppermute x33, starting transfers between devices, swap(): lax.ppermute(values, axis, [(i, i ^ mask) for i in range(lax.axis_size(ax...  30.9 us
    pallas_call x1, Pallas kernels, core(): pl.pallas_call(kernel, out_shape=[jax.ShapeDtypeStruct((half[0] + (EXTRA...  24.6 us
    pallas_call x7, Pallas kernels, join(): pl.pallas_call(kernel, out_shape=out_shape, grid=(1,), in_specs=[spec(row...  16.4 us
    unnamed x66, local copies, waits for them, and re-layouts  5.32 us
  transfers between devices with their start and end apart: 33, of which 17 were waited for; matrix products, arithmetic and copies ran while one was open for 0% of the time, Pallas kernels for 8%

profile of v9, /device:TPU:0, one launch (start us, length us, event | category | flops | bytes accessed | tf_op | source)
XLA Modules:
  0.0 214.5 jit_solution(5267044642773310334)
XLA Ops:
  0.6 3.2 %pack.1 = (bf16[256,1024]{1,0:T(8,128)(2,1)}, bf16[384,1024]{1,0:T(8,128)(2,1)}, bf16[384,1024]{1,0:T(8,128)(2,1)}, bf16[128,1024]{1,0:T(8,128)(2,1)}) custom-call(bf16[128,1024]{1,0:T(8,128)(2,1)} %refs_10_.1, bf16[128,1024]{1,0:T(8,128)(2,1)} %grad_ref.1, bf16[256,2048]{1,0:T(8,128)(2,1)} %refs_16_.1, bf16[2048,256]{1,0:T(8,128)(2,1)} %refs_17_.1), custom_call_target="tpu_custom_call" | custom-call | bytes 4194304 | tf_op jit(solution)/shard_map/pack/pallas_call | solution.py:127
  3.8 3.0 %collective-permute-start.1 = (bf16[384,1024]{1,0:T(8,128)(2,1)}, bf16[384,1024]{1,0:T(8,128)(2,1)S(1)}, u32[]{:S(2)}, u32[]{:S(2)}) collective-permute-start(bf16[384,1024]{1,0:T(8,128)(2,1)} %get-tuple-element.44), channel_id=1, source_target_pairs={{0,1},{1,0},{2,3},{3,2},{4,5},{5,4},{6,7},{7,6},{8,9},{9,8},{10,11... | collective-permute-start | bytes 2359304 | tf_op jit(solution)/shard_map/tokens_weights_1/ppermute | solution.py:101
  8.3 2.6 %collective-permute-start = (bf16[384,1024]{1,0:T(8,128)(2,1)}, bf16[384,1024]{1,0:T(8,128)(2,1)S(1)}, u32[]{:S(2)}, u32[]{:S(2)}) collective-permute-start(bf16[384,1024]{1,0:T(8,128)(2,1)} %get-tuple-element.42), channel_id=1, source_target_pairs={{0,2},{1,3},{2,0},{3,1},{4,6},{5,7},{6,4},{7,5},{8,10},{9,11},{10,... | collective-permute-start | bytes 2359304 | tf_op jit(solution)/shard_map/tokens_weights_2/ppermute | solution.py:101
  10.9 9.5 %collective-permute-done.2.refs_14_ = bf16[256,1024]{1,0:T(8,128)(2,1)S(1)} collective-permute-done((bf16[256,1024]{1,0:T(8,128)(2,1)}, bf16[256,1024]{1,0:T(8,128)(2,1)S(1)}, u32[]{:S(2)}, u32[]{:S(2)}) %collective-permute-start.2) | collective-permute-done | bytes 524320 | tf_op jit(solution)/shard_map/tokens_0_2/ppermute | solution.py:101
  20.4 19.6 %collective-permute-done.1 = bf16[384,1024]{1,0:T(8,128)(2,1)S(1)} collective-permute-done((bf16[384,1024]{1,0:T(8,128)(2,1)}, bf16[384,1024]{1,0:T(8,128)(2,1)S(1)}, u32[]{:S(2)}, u32[]{:S(2)}) %collective-permute-start.1) | collective-permute-done | bytes 786464 | tf_op jit(solution)/shard_map/tokens_weights_1/ppermute | solution.py:101
  40.1 2.8 %collective-permute-start.8 = (bf16[256,1024]{1,0:T(8,128)(2,1)S(1)}, bf16[256,1024]{1,0:T(8,128)(2,1)S(1)}, u32[]{:S(2)}, u32[]{:S(2)}) collective-permute-start(bf16[256,1024]{1,0:T(8,128)(2,1)S(1)} %slice.17.refs_8_), channel_id=1, source_target_pairs={{0,8},{4,12},{8,0},{12,4},{1,9},{5,13},{9,1},{13,5},{2,10},{6,14},... | collective-permute-start | bytes 1572872 | tf_op jit(solution)/shard_map/tokens_1_2/ppermute | solution.py:101
  42.9 2.2 %collective-permute-done = bf16[384,1024]{1,0:T(8,128)(2,1)S(1)} collective-permute-done((bf16[384,1024]{1,0:T(8,128)(2,1)}, bf16[384,1024]{1,0:T(8,128)(2,1)S(1)}, u32[]{:S(2)}, u32[]{:S(2)}) %collective-permute-start) | collective-permute-done | bytes 786464 | tf_op jit(solution)/shard_map/tokens_weights_2/ppermute | solution.py:101
  47.3 6.6 %collective-permute-done.8.refs_10_ = bf16[256,1024]{1,0:T(8,128)(2,1)S(1)} collective-permute-done((bf16[256,1024]{1,0:T(8,128)(2,1)S(1)}, bf16[256,1024]{1,0:T(8,128)(2,1)S(1)}, u32[]{:S(2)}, u32[]{:S(2)}) %collective-permute-start.8) | collective-permute-done | bytes 524320 | tf_op jit(solution)/shard_map/tokens_1_2/ppermute | solution.py:101
  53.9 1.7 collective-permute-start.14
  57.3 2.7 %collective-permute-start.9 = (bf16[128,1024]{1,0:T(8,128)(2,1)S(1)}, bf16[128,1024]{1,0:T(8,128)(2,1)S(1)}, u32[]{:S(2)}, u32[]{:S(2)}) collective-permute-start(bf16[128,1024]{1,0:T(8,128)(2,1)S(1)} %copy-done.31), channel_id=1, source_target_pairs={{0,3},{1,2},{2,1},{3,0},{4,7},{5,6},{6,5},{7,4},{8,11},{9,10},{10,... | collective-permute-start | bytes 786440 | tf_op jit(solution)/shard_map/weights_3/ppermute | solution.py:101
  61.4 6.5 %collective-permute-done.9.refs_22_ = bf16[128,1024]{1,0:T(8,128)(2,1)S(1)} collective-permute-done((bf16[128,1024]{1,0:T(8,128)(2,1)S(1)}, bf16[128,1024]{1,0:T(8,128)(2,1)S(1)}, u32[]{:S(2)}, u32[]{:S(2)}) %collective-permute-start.9) | collective-permute-done | bytes 262176 | tf_op jit(solution)/shard_map/weights_3/ppermute | solution.py:101
  70.0 6.0 %collective-permute-done.10.refs_23_ = bf16[128,1024]{1,0:T(8,128)(2,1)} collective-permute-done((bf16[128,1024]{1,0:T(8,128)(2,1)S(1)}, bf16[128,1024]{1,0:T(8,128)(2,1)}, u32[]{:S(2)}, u32[]{:S(2)}) %collective-permute-start.10) | collective-permute-done | bytes 262176 | tf_op jit(solution)/shard_map/weights_3/ppermute | solution.py:101
  76.5 4.8 %collective-permute-done.15.refs_2_ = bf16[256,1024]{1,0:T(8,128)(2,1)S(1)} collective-permute-done((bf16[256,1024]{1,0:T(8,128)(2,1)S(1)}, bf16[256,1024]{1,0:T(8,128)(2,1)S(1)}, u32[]{:S(2)}, u32[]{:S(2)}) %collective-permute-start.15) | collective-permute-done | bytes 524320 | tf_op jit(solution)/shard_map/tokens_3_2/ppermute | solution.py:101
  81.3 1.9 collective-permute-done.16.refs_3_
  84.1 24.6 %core.1 = (bf16[512,1024]{1,0:T(8,128)(2,1)}, bf16[528,1024]{1,0:T(8,128)(2,1)}, bf16[512,1024]{1,0:T(8,128)(2,1)}, bf16[512,1024]{1,0:T(8,128)(2,1)}, bf16[512,...) custom-call(bf16[256,1024]{1,0:T(8,128)(2,1)} %copy-done.21, ...), custom_call_target="tpu_custom_call" | custom-call | flops 10737418240 | bytes 20971520 | tf_op jit(solution)/shard_map/core/pallas_call | solution.py:257
  109.2 2.8 %collective-permute-done.20.refs_1_.refs_3_ = bf16[528,1024]{1,0:T(8,128)(2,1)S(1)} collective-permute-done((bf16[528,1024]{1,0:T(8,128)(2,1)}, bf16[528,1024]{1,0:T(8,128)(2,1)S(1)}, u32[]{:S(2)}, u32[]{:S(2)}) %collective-permute-start.20) | collective-permute-done | bytes 1081376 | tf_op jit(solution)/shard_map/sums_3_1/ppermute | solution.py:101
  113.0 2.3 %join.8 = (bf16[272,1024]{1,0:T(8,128)(2,1)}, bf16[16,1024]{1,0:T(8,128)(2,1)}) custom-call(bf16[512,1024]{1,0:T(8,128)(2,1)} %get-tuple-element.59.refs_0_, bf16[528,1024]{1,0:T(8,128)(2,1)} %copy-done.8, bf16[16,1024]{1,0:T(8,128)(2,1)} %get-tuple-element.61.refs_2_, bf16[528,1024]{1,0:T(8,128)(2,1)} %copy-done.8), custom_call_target="tpu_custom_call" | custom-call | bytes 1572864 | tf_op jit(solution)/shard_map/join/pallas_call | solution.py:391
  115.5 2.6 %collective-permute-start.25 = (bf16[512,512]{1,0:T(8,128)(2,1)}, bf16[512,512]{1,0:T(8,128)(2,1)S(1)}, u32[]{:S(2)}, u32[]{:S(2)}) collective-permute-start(bf16[512,512]{1,0:T(8,128)(2,1)} %get-tuple-element.69), channel_id=1, source_target_pairs={{0,2},{1,3},{2,0},{3,1},{4,6},{5,7},{6,4},{7,5},{8,10},{9,11},{10,... | collective-permute-start | bytes 1572872 | tf_op jit(solution)/shard_map/grads_2/ppermute | solution.py:101
  118.3 2.1 join.7
  120.4 9.8 %collective-permute-done.21.refs_2_.refs_4_ = bf16[272,1024]{1,0:T(8,128)(2,1)S(1)} collective-permute-done((bf16[272,1024]{1,0:T(8,128)(2,1)}, bf16[272,1024]{1,0:T(8,128)(2,1)S(1)}, u32[]{:S(2)}, u32[]{:S(2)}) %collective-permute-start.21) | collective-permute-done | bytes 557088 | tf_op jit(solution)/shard_map/sums_3_2/ppermute | solution.py:101
  131.0 2.6 %join.9 = (bf16[272,1024]{1,0:T(8,128)(2,1)}, bf16[16,1024]{1,0:T(8,128)(2,1)}) custom-call(bf16[512,1024]{1,0:T(8,128)(2,1)} %get-tuple-element.59.refs_0_, bf16[528,1024]{1,0:T(8,128)(2,1)} %copy-done.8, bf16[272,1024]{1,0:T(8,128)(2,1)} %copy-done.11, bf16[16,1024]{1,0:T(8,128)(2,1)} %get-tuple-element.64.refs_3_, bf16[272,1024]{1,0:T(8,128)(2,1)} %copy-done.11), custom_call_target="tpu_custom_call" | custom-call | bytes 2097152 | tf_op jit(solution)/shard_map/join/pallas_call | solution.py:391
  134.0 3.1 %collective-permute-start.26 = (bf16[512,512]{1,0:T(8,128)(2,1)}, bf16[512,512]{1,0:T(8,128)(2,1)S(1)}, u32[]{:S(2)}, u32[]{:S(2)}) collective-permute-start(bf16[512,512]{1,0:T(8,128)(2,1)} %get-tuple-element.70), channel_id=1, source_target_pairs={{0,3},{1,2},{2,1},{3,0},{4,7},{5,6},{6,5},{7,4},{8,11},{9,10},{10,... | collective-permute-start | bytes 1572872 | tf_op jit(solution)/shard_map/grads_3/ppermute | solution.py:101
  137.1 2.1 join.12
  139.2 2.8 %collective-permute-done.25.refs_2_ = bf16[512,512]{1,0:T(8,128)(2,1)S(1)} collective-permute-done((bf16[512,512]{1,0:T(8,128)(2,1)}, bf16[512,512]{1,0:T(8,128)(2,1)S(1)}, u32[]{:S(2)}, u32[]{:S(2)}) %collective-permute-start.25) | collective-permute-done | bytes 524320 | tf_op jit(solution)/shard_map/grads_2/ppermute | solution.py:101
  142.0 1.7 collective-permute-done.22.refs_2_
  144.0 21.1 %collective-permute-done.23.refs_3_.refs_5_ = bf16[272,1024]{1,0:T(8,128)(2,1)} collective-permute-done((bf16[272,1024]{1,0:T(8,128)(2,1)}, bf16[272,1024]{1,0:T(8,128)(2,1)}, u32[]{:S(2)}, u32[]{:S(2)}) %collective-permute-start.23) | collective-permute-done | bytes 557088 | tf_op jit(solution)/shard_map/sums_3/ppermute | solution.py:101
  165.1 2.8 %join.10 = (bf16[272,1024]{1,0:T(8,128)(2,1)}, bf16[16,1024]{1,0:T(8,128)(2,1)}) custom-call(bf16[512,1024]{1,0:T(8,128)(2,1)} %get-tuple-element.57.refs_0_, bf16[512,1024]{1,0:T(8,128)(2,1)} %collective-permute-done.19.refs_1_, bf16[256,1024]{1,0:T(8,128)(2,1)} %collective-permute-done.22.refs_2_, ...), custom_call_target="tpu_custom_call" | custom-call | bytes 2621440 | tf_op jit(solution)/shard_map/join/pallas_call | solution.py:391
  169.0 2.1 join.11
  174.1 2.4 %join.13 = bf16[256,1024]{1,0:T(8,128)(2,1)} custom-call(bf16[512,1024]{1,0:T(8,128)(2,1)} %get-tuple-element.73.refs_0_, bf16[512,1024]{1,0:T(8,128)(2,1)} %copy-done.10, bf16[256,1024]{1,0:T(8,128)(2,1)} %collective-permute-done.29.refs_2_), custom_call_target="tpu_custom_call" | custom-call | bytes 2097152 | tf_op jit(solution)/shard_map/join/pallas_call | solution.py:391
  177.6 20.5 %collective-permute-done.24.refs_1_ = bf16[512,512]{1,0:T(8,128)(2,1)} collective-permute-done((bf16[512,512]{1,0:T(8,128)(2,1)}, bf16[512,512]{1,0:T(8,128)(2,1)}, u32[]{:S(2)}, u32[]{:S(2)}) %collective-permute-start.24) | collective-permute-done | bytes 524320 | tf_op jit(solution)/shard_map/grads_1/ppermute | solution.py:101
  198.2 10.2 %collective-permute-done.31.refs_7_ = bf16[256,1024]{1,0:T(8,128)(2,1)S(1)} collective-permute-done((bf16[256,1024]{1,0:T(8,128)(2,1)}, bf16[256,1024]{1,0:T(8,128)(2,1)S(1)}, u32[]{:S(2)}, u32[]{:S(2)}) %collective-permute-start.31) | collective-permute-done | bytes 524320 | tf_op jit(solution)/shard_map/sums_1/ppermute | solution.py:101
  210.3 4.2 %finish.1 = (bf16[128,1024]{1,0:T(8,128)(2,1)}, f32[128,1024]{1,0:T(8,128)}, f32[256,2048]{1,0:T(8,128)}, f32[2048,256]{1,0:T(8,128)}, f32[2,1024]{1,0:T(2,128)}) custom-call(bf16[512,512]{1,0:T(8,128)(2,1)S(1)} %copy-done.2, bf16[512,512]{1,0:T(8,128)(2,1)} %collective-permute-done.24.refs_1_, bf16[512,512]{1,0:T(8,128)(2,1)S(1)} %collective-permute-done.25.refs_2_, ...), custom_call_target="tpu_custom_call" | custom-call | bytes 6291456 | tf_op jit(solution)/shard_map/finish/pallas_call | solution.py:351
  (114 shorter events, 20.8 us)
Async XLA Ops:
  3.8 36.3 %collective-permute-start.1 = (bf16[384,1024]{1,0:T(8,128)(2,1)}, bf16[384,1024]{1,0:T(8,128)(2,1)S(1)}, u32[]{:S(2)}, u32[]{:S(2)}) collective-permute-start(bf16[384,1024]{1,0:T(8,128)(2,1)} %get-tuple-element.44), channel_id=1, source_target_pairs={{0,1},{1,0},{2,3},{3,2},{4,5},{5,4},{6,7},{7,6},{8,9},{9,8},{10,11... | collective-permute-start | bytes 2359304 | tf_op jit(solution)/shard_map/tokens_weights_1/ppermute | solution.py:101
  6.8 13.6 %collective-permute-start.2 = (bf16[256,1024]{1,0:T(8,128)(2,1)}, bf16[256,1024]{1,0:T(8,128)(2,1)S(1)}, u32[]{:S(2)}, u32[]{:S(2)}) collective-permute-start(bf16[256,1024]{1,0:T(8,128)(2,1)} %get-tuple-element.43.refs_12_), channel_id=1, source_target_pairs={{0,8},{4,12},{8,0},{12,4},{1,9},{5,13},{9,1},{13,5},{2,10},{6,14},... | collective-permute-start | bytes 1572872 | tf_op jit(solution)/shard_map/tokens_0_2/ppermute | solution.py:101
  8.3 36.7 %collective-permute-start = (bf16[384,1024]{1,0:T(8,128)(2,1)}, bf16[384,1024]{1,0:T(8,128)(2,1)S(1)}, u32[]{:S(2)}, u32[]{:S(2)}) collective-permute-start(bf16[384,1024]{1,0:T(8,128)(2,1)} %get-tuple-element.42), channel_id=1, source_target_pairs={{0,2},{1,3},{2,0},{3,1},{4,6},{5,7},{6,4},{7,5},{8,10},{9,11},{10,... | collective-permute-start | bytes 2359304 | tf_op jit(solution)/shard_map/tokens_weights_2/ppermute | solution.py:101
  10.9 34.3 %collective-permute-start.3 = (bf16[256,1024]{1,0:T(8,128)(2,1)}, bf16[256,1024]{1,0:T(8,128)(2,1)S(1)}, u32[]{:S(2)}, u32[]{:S(2)}) collective-permute-start(bf16[256,1024]{1,0:T(8,128)(2,1)} %get-tuple-element.43.refs_12_), channel_id=1, source_target_pairs={{0,4},{4,0},{8,12},{12,8},{1,5},{5,1},{9,13},{13,9},{2,6},{6,2},{1... | collective-permute-start | bytes 1572872 | tf_op jit(solution)/shard_map/tokens_0_1/ppermute | solution.py:101
  20.4 24.8 %collective-permute-start.4 = (bf16[256,1024]{1,0:T(8,128)(2,1)S(1)}, bf16[256,1024]{1,0:T(8,128)(2,1)S(1)}, u32[]{:S(2)}, u32[]{:S(2)}) collective-permute-start(bf16[256,1024]{1,0:T(8,128)(2,1)S(1)} %collective-permute-done.2.refs_14_), channel_id=1, source_target_pairs={{0,4},{4,0},{8,12},{12,8},{1,5},{5,1},{9,13},{13,9},{2,6},{6,2},{1... | collective-permute-start | bytes 1572872 | tf_op jit(solution)/shard_map/tokens_0_3/ppermute | solution.py:101
  40.1 13.8 %collective-permute-start.8 = (bf16[256,1024]{1,0:T(8,128)(2,1)S(1)}, bf16[256,1024]{1,0:T(8,128)(2,1)S(1)}, u32[]{:S(2)}, u32[]{:S(2)}) collective-permute-start(bf16[256,1024]{1,0:T(8,128)(2,1)S(1)} %slice.17.refs_8_), channel_id=1, source_target_pairs={{0,8},{4,12},{8,0},{12,4},{1,9},{5,13},{9,1},{13,5},{2,10},{6,14},... | collective-permute-start | bytes 1572872 | tf_op jit(solution)/shard_map/tokens_1_2/ppermute | solution.py:101
  45.2 10.4 %collective-permute-start.6 = (bf16[128,1024]{1,0:T(8,128)(2,1)S(1)}, bf16[128,1024]{1,0:T(8,128)(2,1)S(1)}, u32[]{:S(2)}, u32[]{:S(2)}) collective-permute-start(bf16[128,1024]{1,0:T(8,128)(2,1)S(1)} %slice.18.refs_18_), channel_id=1, source_target_pairs={{0,16},{16,0},{1,17},{17,1},{2,18},{18,2},{3,19},{19,3},{4,20},{20... | collective-permute-start | bytes 786440 | tf_op jit(solution)/shard_map/weights_1/ppermute | solution.py:101
  46.8 13.2 %collective-permute-start.12 = (bf16[256,1024]{1,0:T(8,128)(2,1)S(1)}, bf16[256,1024]{1,0:T(8,128)(2,1)S(1)}, u32[]{:S(2)}, u32[]{:S(2)}) collective-permute-start(bf16[256,1024]{1,0:T(8,128)(2,1)S(1)} %slice.17.refs_8_), channel_id=1, source_target_pairs={{0,4},{4,0},{8,12},{12,8},{1,5},{5,1},{9,13},{13,9},{2,6},{6,2},{1... | collective-permute-start | bytes 1572872 | tf_op jit(solution)/shard_map/tokens_1_1/ppermute | solution.py:101
  46.8 10.5 %collective-permute-start.7 = (bf16[128,1024]{1,0:T(8,128)(2,1)S(1)}, bf16[128,1024]{1,0:T(8,128)(2,1)S(1)}, u32[]{:S(2)}, u32[]{:S(2)}) collective-permute-start(bf16[128,1024]{1,0:T(8,128)(2,1)S(1)} %slice.19.refs_20_), channel_id=1, source_target_pairs={{0,16},{16,0},{1,17},{17,1},{2,18},{18,2},{3,19},{19,3},{4,20},{20... | collective-permute-start | bytes 786440 | tf_op jit(solution)/shard_map/weights_2/ppermute | solution.py:101
  47.3 14.1 %collective-permute-start.5 = (bf16[256,1024]{1,0:T(8,128)(2,1)S(1)}, bf16[256,1024]{1,0:T(8,128)(2,1)S(1)}, u32[]{:S(2)}, u32[]{:S(2)}) collective-permute-start(bf16[256,1024]{1,0:T(8,128)(2,1)S(1)} %slice.16.refs_4_), channel_id=1, source_target_pairs={{0,1},{1,0},{2,3},{3,2},{4,5},{5,4},{6,7},{7,6},{8,9},{9,8},{10,11... | collective-permute-start | bytes 1572872 | tf_op jit(solution)/shard_map/tokens_3/ppermute | solution.py:101
  53.9 13.9 %collective-permute-start.14 = (bf16[256,1024]{1,0:T(8,128)(2,1)S(1)}, bf16[256,1024]{1,0:T(8,128)(2,1)S(1)}, u32[]{:S(2)}, u32[]{:S(2)}) collective-permute-start(bf16[256,1024]{1,0:T(8,128)(2,1)S(1)} %slice.16.refs_4_), channel_id=1, source_target_pairs={{0,8},{4,12},{8,0},{12,4},{1,9},{5,13},{9,1},{13,5},{2,10},{6,14},... | collective-permute-start | bytes 1572872 | tf_op jit(solution)/shard_map/tokens_2_2/ppermute | solution.py:101
  55.7 12.2 %collective-permute-start.13 = (bf16[256,1024]{1,0:T(8,128)(2,1)S(1)}, bf16[256,1024]{1,0:T(8,128)(2,1)S(1)}, u32[]{:S(2)}, u32[]{:S(2)}) collective-permute-start(bf16[256,1024]{1,0:T(8,128)(2,1)S(1)} %collective-permute-done.8.refs_10_), channel_id=1, source_target_pairs={{0,4},{4,0},{8,12},{12,8},{1,5},{5,1},{9,13},{13,9},{2,6},{6,2},{1... | collective-permute-start | bytes 1572872 | tf_op jit(solution)/shard_map/tokens_1_3/ppermute | solution.py:101
  57.3 10.5 %collective-permute-start.9 = (bf16[128,1024]{1,0:T(8,128)(2,1)S(1)}, bf16[128,1024]{1,0:T(8,128)(2,1)S(1)}, u32[]{:S(2)}, u32[]{:S(2)}) collective-permute-start(bf16[128,1024]{1,0:T(8,128)(2,1)S(1)} %copy-done.31), channel_id=1, source_target_pairs={{0,3},{1,2},{2,1},{3,0},{4,7},{5,6},{6,5},{7,4},{8,11},{9,10},{10,... | collective-permute-start | bytes 786440 | tf_op jit(solution)/shard_map/weights_3/ppermute | solution.py:101
  67.9 13.3 %collective-permute-start.15 = (bf16[256,1024]{1,0:T(8,128)(2,1)S(1)}, bf16[256,1024]{1,0:T(8,128)(2,1)S(1)}, u32[]{:S(2)}, u32[]{:S(2)}) collective-permute-start(bf16[256,1024]{1,0:T(8,128)(2,1)S(1)} %collective-permute-done.5.refs_0_), channel_id=1, source_target_pairs={{0,8},{4,12},{8,0},{12,4},{1,9},{5,13},{9,1},{13,5},{2,10},{6,14},... | collective-permute-start | bytes 1572872 | tf_op jit(solution)/shard_map/tokens_3_2/ppermute | solution.py:101
  68.5 7.5 %collective-permute-start.10 = (bf16[128,1024]{1,0:T(8,128)(2,1)S(1)}, bf16[128,1024]{1,0:T(8,128)(2,1)}, u32[]{:S(2)}, u32[]{:S(2)}) collective-permute-start(bf16[128,1024]{1,0:T(8,128)(2,1)S(1)} %collective-permute-done.9.refs_22_), channel_id=1, source_target_pairs={{0,16},{16,0},{1,17},{17,1},{2,18},{18,2},{3,19},{19,3},{4,20},{20... | collective-permute-start | bytes 786440 | tf_op jit(solution)/shard_map/weights_3/ppermute | solution.py:101
  70.0 11.3 %collective-permute-start.17 = (bf16[256,1024]{1,0:T(8,128)(2,1)S(1)}, bf16[256,1024]{1,0:T(8,128)(2,1)S(1)}, u32[]{:S(2)}, u32[]{:S(2)}) collective-permute-start(bf16[256,1024]{1,0:T(8,128)(2,1)S(1)} %slice.16.refs_4_), channel_id=1, source_target_pairs={{0,4},{4,0},{8,12},{12,8},{1,5},{5,1},{9,13},{13,9},{2,6},{6,2},{1... | collective-permute-start | bytes 1572872 | tf_op jit(solution)/shard_map/tokens_2_1/ppermute | solution.py:101
  76.0 5.3 %collective-permute-start.11 = (bf16[256,1024]{1,0:T(8,128)(2,1)S(1)}, bf16[256,1024]{1,0:T(8,128)(2,1)S(1)}, u32[]{:S(2)}, u32[]{:S(2)}) collective-permute-start(bf16[256,1024]{1,0:T(8,128)(2,1)S(1)} %collective-permute-done.5.refs_0_), channel_id=1, source_target_pairs={{0,4},{4,0},{8,12},{12,8},{1,5},{5,1},{9,13},{13,9},{2,6},{6,2},{1... | collective-permute-start | bytes 1572872 | tf_op jit(solution)/shard_map/tokens_3_1/ppermute | solution.py:101
  76.0 5.3 %collective-permute-start.18 = (bf16[256,1024]{1,0:T(8,128)(2,1)S(1)}, bf16[256,1024]{1,0:T(8,128)(2,1)S(1)}, u32[]{:S(2)}, u32[]{:S(2)}) collective-permute-start(bf16[256,1024]{1,0:T(8,128)(2,1)S(1)} %collective-permute-done.14.refs_6_), channel_id=1, source_target_pairs={{0,4},{4,0},{8,12},{12,8},{1,5},{5,1},{9,13},{13,9},{2,6},{6,2},{1... | collective-permute-start | bytes 1572872 | tf_op jit(solution)/shard_map/tokens_2_3/ppermute | solution.py:101
  108.7 3.3 %collective-permute-start.20 = (bf16[528,1024]{1,0:T(8,128)(2,1)}, bf16[528,1024]{1,0:T(8,128)(2,1)S(1)}, u32[]{:S(2)}, u32[]{:S(2)}) collective-permute-start(bf16[528,1024]{1,0:T(8,128)(2,1)} %get-tuple-element.60), channel_id=1, source_target_pairs={{0,4},{4,0},{8,12},{12,8},{1,5},{5,1},{9,13},{13,9},{2,6},{6,2},{1... | collective-permute-start | bytes 3244040 | tf_op jit(solution)/shard_map/sums_3_1/ppermute | solution.py:101
  108.9 9.5 %collective-permute-start.19 = (bf16[512,1024]{1,0:T(8,128)(2,1)}, bf16[512,1024]{1,0:T(8,128)(2,1)}, u32[]{:S(2)}, u32[]{:S(2)}) collective-permute-start(bf16[512,1024]{1,0:T(8,128)(2,1)} %get-tuple-element.58), channel_id=1, source_target_pairs={{0,4},{4,0},{8,12},{12,8},{1,5},{5,1},{9,13},{13,9},{2,6},{6,2},{1... | collective-permute-start | bytes 3145736 | tf_op jit(solution)/shard_map/sums_2_1/ppermute | solution.py:101
  115.3 14.9 %collective-permute-start.21 = (bf16[272,1024]{1,0:T(8,128)(2,1)}, bf16[272,1024]{1,0:T(8,128)(2,1)S(1)}, u32[]{:S(2)}, u32[]{:S(2)}) collective-permute-start(bf16[272,1024]{1,0:T(8,128)(2,1)} %get-tuple-element.62), channel_id=1, source_target_pairs={{0,8},{4,12},{8,0},{12,4},{1,9},{5,13},{9,1},{13,5},{2,10},{6,14},... | collective-permute-start | bytes 1671176 | tf_op jit(solution)/shard_map/sums_3_2/ppermute | solution.py:101
  115.5 18.5 %collective-permute-start.28 = (bf16[512,1024]{1,0:T(8,128)(2,1)}, bf16[512,1024]{1,0:T(8,128)(2,1)S(1)}, u32[]{:S(2)}, u32[]{:S(2)}) collective-permute-start(bf16[512,1024]{1,0:T(8,128)(2,1)} %get-tuple-element.74), channel_id=1, source_target_pairs={{0,4},{4,0},{8,12},{12,8},{1,5},{5,1},{9,13},{13,9},{2,6},{6,2},{1... | collective-permute-start | bytes 3145736 | tf_op jit(solution)/shard_map/sums_1_1/ppermute | solution.py:101
  115.5 26.5 %collective-permute-start.25 = (bf16[512,512]{1,0:T(8,128)(2,1)}, bf16[512,512]{1,0:T(8,128)(2,1)S(1)}, u32[]{:S(2)}, u32[]{:S(2)}) collective-permute-start(bf16[512,512]{1,0:T(8,128)(2,1)} %get-tuple-element.69), channel_id=1, source_target_pairs={{0,2},{1,3},{2,0},{3,1},{4,6},{5,7},{6,4},{7,5},{8,10},{9,11},{10,... | collective-permute-start | bytes 1572872 | tf_op jit(solution)/shard_map/grads_2/ppermute | solution.py:101
  118.1 49.9 %collective-permute-start.27 = (bf16[512,1024]{1,0:T(8,128)(2,1)}, bf16[512,1024]{1,0:T(8,128)(2,1)S(1)}, u32[]{:S(2)}, u32[]{:S(2)}) collective-permute-start(bf16[512,1024]{1,0:T(8,128)(2,1)} %get-tuple-element.72), channel_id=1, source_target_pairs={{0,4},{4,0},{8,12},{12,8},{1,5},{5,1},{9,13},{13,9},{2,6},{6,2},{1... | collective-permute-start | bytes 3145736 | tf_op jit(solution)/shard_map/sums_0_1/ppermute | solution.py:101
  130.2 13.5 %collective-permute-start.22 = (bf16[256,1024]{1,0:T(8,128)(2,1)}, bf16[256,1024]{1,0:T(8,128)(2,1)}, u32[]{:S(2)}, u32[]{:S(2)}) collective-permute-start(bf16[256,1024]{1,0:T(8,128)(2,1)} %join.7), channel_id=1, source_target_pairs={{0,8},{4,12},{8,0},{12,4},{1,9},{5,13},{9,1},{13,5},{2,10},{6,14},... | collective-permute-start | bytes 1572872 | tf_op jit(solution)/shard_map/sums_2_2/ppermute | solution.py:101
  133.6 31.6 %collective-permute-start.23 = (bf16[272,1024]{1,0:T(8,128)(2,1)}, bf16[272,1024]{1,0:T(8,128)(2,1)}, u32[]{:S(2)}, u32[]{:S(2)}) collective-permute-start(bf16[272,1024]{1,0:T(8,128)(2,1)} %get-tuple-element.65), channel_id=1, source_target_pairs={{0,1},{1,0},{2,3},{3,2},{4,5},{5,4},{6,7},{7,6},{8,9},{9,8},{10,11... | collective-permute-start | bytes 1671176 | tf_op jit(solution)/shard_map/sums_3/ppermute | solution.py:101
  134.0 38.8 %collective-permute-start.26 = (bf16[512,512]{1,0:T(8,128)(2,1)}, bf16[512,512]{1,0:T(8,128)(2,1)S(1)}, u32[]{:S(2)}, u32[]{:S(2)}) collective-permute-start(bf16[512,512]{1,0:T(8,128)(2,1)} %get-tuple-element.70), channel_id=1, source_target_pairs={{0,3},{1,2},{2,1},{3,0},{4,7},{5,6},{6,5},{7,4},{8,11},{9,10},{10,... | collective-permute-start | bytes 1572872 | tf_op jit(solution)/shard_map/grads_3/ppermute | solution.py:101
  143.6 29.1 %collective-permute-start.29 = (bf16[256,1024]{1,0:T(8,128)(2,1)}, bf16[256,1024]{1,0:T(8,128)(2,1)}, u32[]{:S(2)}, u32[]{:S(2)}) collective-permute-start(bf16[256,1024]{1,0:T(8,128)(2,1)} %join.12), channel_id=1, source_target_pairs={{0,8},{4,12},{8,0},{12,4},{1,9},{5,13},{9,1},{13,5},{2,10},{6,14},... | collective-permute-start | bytes 1572872 | tf_op jit(solution)/shard_map/sums_1_2/ppermute | solution.py:101
  168.0 30.2 %collective-permute-start.32 = (bf16[272,1024]{1,0:T(8,128)(2,1)}, bf16[272,1024]{1,0:T(8,128)(2,1)S(1)}, u32[]{:S(2)}, u32[]{:S(2)}) collective-permute-start(bf16[272,1024]{1,0:T(8,128)(2,1)} %get-tuple-element.67), channel_id=1, source_target_pairs={{0,2},{1,3},{2,0},{3,1},{4,6},{5,7},{6,4},{7,5},{8,10},{9,11},{10,... | collective-permute-start | bytes 1671176 | tf_op jit(solution)/shard_map/sums_2/ppermute | solution.py:101
  171.2 27.0 %collective-permute-start.24 = (bf16[512,512]{1,0:T(8,128)(2,1)}, bf16[512,512]{1,0:T(8,128)(2,1)}, u32[]{:S(2)}, u32[]{:S(2)}) collective-permute-start(bf16[512,512]{1,0:T(8,128)(2,1)} %get-tuple-element.68), channel_id=1, source_target_pairs={{0,1},{1,0},{2,3},{3,2},{4,5},{5,4},{6,7},{7,6},{8,9},{9,8},{10,11... | collective-permute-start | bytes 1572872 | tf_op jit(solution)/shard_map/grads_1/ppermute | solution.py:101
  172.8 25.4 %collective-permute-start.30 = (bf16[256,1024]{1,0:T(8,128)(2,1)}, bf16[256,1024]{1,0:T(8,128)(2,1)}, u32[]{:S(2)}, u32[]{:S(2)}) collective-permute-start(bf16[256,1024]{1,0:T(8,128)(2,1)} %join.11), channel_id=1, source_target_pairs={{0,8},{4,12},{8,0},{12,4},{1,9},{5,13},{9,1},{13,5},{2,10},{6,14},... | collective-permute-start | bytes 1572872 | tf_op jit(solution)/shard_map/sums_0_2/ppermute | solution.py:101
  176.4 31.9 %collective-permute-start.31 = (bf16[256,1024]{1,0:T(8,128)(2,1)}, bf16[256,1024]{1,0:T(8,128)(2,1)S(1)}, u32[]{:S(2)}, u32[]{:S(2)}) collective-permute-start(bf16[256,1024]{1,0:T(8,128)(2,1)} %join.13), channel_id=1, source_target_pairs={{0,1},{1,0},{2,3},{3,2},{4,5},{5,4},{6,7},{7,6},{8,9},{9,8},{10,11... | collective-permute-start | bytes 1572872 | tf_op jit(solution)/shard_map/sums_1/ppermute | solution.py:101
  (34 other events, 749.7 us)

commit v10 on v9

--- a/solution.py
+++ b/solution.py
@@ -112,25 +112,20 @@
 
     def kernel(first_ref, grad_ref, up_ref, down_ref, own, *sends):
         place, mate = lax.axis_index("dp"), lax.rem(lax.axis_index("groups"), mates)
-        for ref in [own] + [sends[bit - 1] for bit in bits_of(n_dp)]:
-            ref[:own_rows, :] = first_ref[...]
-            ref[own_rows : 2 * own_rows, :] = grad_ref[...]
+        own[:own_rows, :] = first_ref[...]
+        own[own_rows:, :] = grad_ref[...]
         for k in range(1, n_dp):
             first = pl.multiple_of((place ^ k) * units, units)
-            send, skip = sends[k - 1], 0 if k & (k - 1) else 2 * own_rows
-            span = slice(skip, skip + rows)
-            send[span, :units] = up_ref[pl.ds(pl.multiple_of(mate * rows, rows), rows), pl.ds(first, units)]
+            send = sends[k - 1]
+            send[:, :units] = up_ref[pl.ds(pl.multiple_of(mate * rows, rows), rows), pl.ds(first, units)]
             for c in range(strips):
                 row = pl.multiple_of(first + mate * (units // mates) + c * rows, rows)
-                send[span, units + c * depth : units + (c + 1) * depth] = down_ref[pl.ds(row, rows), :]
+                send[:, units + c * depth : units + (c + 1) * depth] = down_ref[pl.ds(row, rows), :]
 
     return pl.pallas_call(
         kernel,
         out_shape=[jax.ShapeDtypeStruct((2 * own_rows, width), w_up.dtype)]
-        + [
-            jax.ShapeDtypeStruct((rows + (0 if k & (k - 1) else 2 * own_rows), width), w_up.dtype)
-            for k in range(1, n_dp)
-        ],
+        + [jax.ShapeDtypeStruct((rows, width), w_up.dtype)] * (n_dp - 1),
         in_specs=[pl.BlockSpec(memory_space=pltpu.VMEM)] * 4,
         out_specs=[pl.BlockSpec(memory_space=pltpu.VMEM)] * n_dp,
         cost_estimate=pl.CostEstimate(flops=0, bytes_accessed=8 * w_up.size, transcendentals=0),
@@ -437,24 +432,28 @@
         if mates == 2:
             crossed[k] = swap(after(got[k], *first), "groups", 1, f"weights_{k}")
 
+    def weights_dp(k, *first):
+        got[k] = swap(after(sends[k - 1], *first), "dp", k, f"weights_{k}")
+
+    for bit in reversed(bits_of(n_dp)):
+        tokens_dp(bit)
     tokens_tensor(0)
     tokens_rest(0)
-    for bit in reversed(bits_of(n_dp)):
-        both = swap(sends[bit - 1], "dp", bit, f"tokens_weights_{bit}")
-        tokens[bit], got[bit] = both[: 2 * own_rows], both[2 * own_rows :]
-    tokens_tensor(1, tokens[1], chunks[0][high])
-    stage = [*tokens.values(), *got.values(), *chunks[0].values()]
-    for bit in reversed(bits_of(n_dp)):
-        weights_groups(bit, *stage)
+    tokens_tensor(1, tokens[top], chunks[0][high])
+    stage = [*tokens.values(), *chunks[0].values()]
     for k in range(2, n_dp):
         if k & (k - 1):
             tokens_dp(k, *stage)
-            got[k] = swap(after(sends[k - 1], *stage, chunks[1][high]), "dp", k, f"weights_{k}")
-            stage = [tokens[k], got[k], *crossed.values()]
+        weights_dp(k, *stage, *([got[top]] if top in got else []))
+    for k in range(2, n_dp):
         tokens_rest(k - 1)
-        tokens_tensor(k, *stage, *(chunks[k - 2].values() if k > top else ()), chunks[k - 1][high])
+        stage = [got[top]]
         if k & (k - 1):
-            weights_groups(k)
+            stage = [tokens[k], *got.values(), *chunks[k - 2].values()]
+        tokens_tensor(k, *stage, chunks[k - 1][high])
+    weights_dp(1, *stage)
+    for k in [*range(2, n_dp), 1]:
+        weights_groups(k)
     tokens_rest(n_dp - 1, *crossed.values())
     got = {k: [got[k]] + ([crossed[k]] if k in crossed else []) for k in got}
 
@@ -465,8 +464,14 @@
     blocks = dict(enumerate(blocks))
     blocks[top] = swap(blocks[top], "dp", top, f"grads_{top}")
 
+    for k in range(1, top):
+        blocks[k] = swap(blocks[k], "dp", k, f"grads_{k}")
     for k in range(top + 1, n_dp):
-        blocks[k] = swap(blocks[k], "dp", k, f"grads_{k}")
+        blocks[k] = swap(after(blocks[k], *(blocks[j] for j in range(1, k))), "dp", k, f"grads_{k}")
+
+    def add(terms):
+        spans = (x[place * span : (place + 1) * span].astype(jnp.float32) for x, place in terms)
+        return sum(spans).astype(jnp.bfloat16)
 
     sums, behind, span, waiting = {}, (), 2 * own_rows, None
     for k, (even, odd) in zip(order, halves, strict=True):
@@ -479,7 +484,7 @@
                 if k == order[0] and j == bit:
                     send, stats = join(span, parts.pop(j), [(stats, 0), waiting])
                 else:
-                    send = join(span, parts.pop(j))
+                    send = add(parts.pop(j))
                 if k < 2:
                     behind += (blocks[n_dp - 1 if k == 0 else top],)
                 came = swap(after(send, *behind), "tensor", bit, f"sums_{k}_{j}")
@@ -494,7 +499,7 @@
             if k == (n_dp - 1) & -bit:
                 send, stats = join(span, sums.pop(k), [(stats, 0), waiting])
             else:
-                send = join(span, sums.pop(k))
+                send = add(sums.pop(k))
             came[k] = swap(send, "dp", bit, f"sums_{k}")
             if k == (n_dp - 1) & -bit:
                 waiting = (came[k], span // EXTRA)
@@ -502,9 +507,7 @@
     last, stats = join(span, sums[top], [(stats, 0), waiting])
     came[top] = swap(last, "dp", top, f"sums_{top}")
     for bit in bits_of(n_dp)[:0:-1]:
-        came[bit] = swap(after(join(span, sums[bit]), last), "dp", bit, f"sums_{bit}")
-    for k in range(1, top):
-        blocks[k] = swap(after(blocks[k], last), "dp", k, f"grads_{k}")
+        came[bit] = swap(after(add(sums[bit]), last), "dp", bit, f"sums_{bit}")
 
     scale = (own_rows * n_tensor * n_dp) ** (-0.5)
     terms = [*(x for x, _ in sums[0]), *(came[bit] for bit in bits_of(n_dp)[::-1])]

time: 215 us -> 205 us (0.953)
  Pallas kernels: 48.4 us -> 39 us
  waiting for transfers between devices: 129 us -> 122 us
  other arithmetic: 0 us -> 6.98 us
  local copies, waits for them, and re-layouts: 5.42 us -> 3.24 us
    pallas_call x7 -> x3, Pallas kernels: 16.4 us -> 7.9 us  [join(): pl.pallas_call(kernel, out_shape=out_shape, grid=(1,), in_specs=[spec(row...]
    ppermute x33 -> x35, waiting for transfers between devices: 129 us -> 122 us  [swap(): lax.ppermute(values, axis, [(i, i ^ mask) for i in range(lax.axis_size(ax...]
    convert_element_type x0 -> x4, other arithmetic: none -> 6.98 us  [add(): return sum(spans).astype(jnp.bfloat16)]
    ppermute x33 -> x35, starting transfers between devices: 30.9 us -> 32.5 us  [swap(): lax.ppermute(values, axis, [(i, i ^ mask) for i in range(lax.axis_size(ax...]
  transfers between devices with their start and end apart: 33 -> 35, of which waited for: 17 -> 19; matrix products, arithmetic and copies ran while one was open for 0% -> 3% of each run, Pallas kernels for 8% -> 4%
where the time goes in v10:
time: 205 us; the launch traced here: 204 us
  waiting for transfers between devices  122 us (60%)
  Pallas kernels  39 us (19%)
  starting transfers between devices  32.5 us (16%)
  other arithmetic  6.98 us (3%)
  local copies, waits for them, and re-layouts  3.24 us (2%)
    ppermute x35, waiting for transfers between devices, swap(): lax.ppermute(values, axis, [(i, i ^ mask) for i in range(lax.axis_size(ax...  122 us
    ppermute x35, starting transfers between devices, swap(): lax.ppermute(values, axis, [(i, i ^ mask) for i in range(lax.axis_size(ax...  32.5 us
    pallas_call x1, Pallas kernels, core(): pl.pallas_call(kernel, out_shape=[jax.ShapeDtypeStruct((half[0] + (EXTRA...  24.5 us
    pallas_call x3, Pallas kernels, join(): pl.pallas_call(kernel, out_shape=out_shape, grid=(1,), in_specs=[spec(row...  7.9 us
    convert_element_type x4, other arithmetic, add(): return sum(spans).astype(jnp.bfloat16)  6.98 us
  transfers between devices with their start and end apart: 35, of which 19 were waited for; matrix products, arithmetic and copies ran while one was open for 3% of the time, Pallas kernels for 4%

profile of v10, /device:TPU:0, one launch (start us, length us, event | category | flops | bytes accessed | tf_op | source)
XLA Modules:
  0.0 204.2 jit_solution(13809202613559851777)
XLA Ops:
  0.6 2.8 %pack.1 = (bf16[256,1024]{1,0:T(8,128)(2,1)}, bf16[128,1024]{1,0:T(8,128)(2,1)}, bf16[128,1024]{1,0:T(8,128)(2,1)}, bf16[128,1024]{1,0:T(8,128)(2,1)}) custom-call(bf16[128,1024]{1,0:T(8,128)(2,1)} %refs_10_.1, bf16[128,1024]{1,0:T(8,128)(2,1)} %grad_ref.1, bf16[256,2048]{1,0:T(8,128)(2,1)} %refs_16_.1, bf16[2048,256]{1,0:T(8,128)(2,1)} %refs_17_.1), custom_call_target="tpu_custom_call" | custom-call | bytes 4194304 | tf_op jit(solution)/shard_map/pack/pallas_call | solution.py:125
  3.4 3.0 %collective-permute-start.2 = (bf16[256,1024]{1,0:T(8,128)(2,1)}, bf16[256,1024]{1,0:T(8,128)(2,1)S(1)}, u32[]{:S(2)}, u32[]{:S(2)}) collective-permute-start(bf16[256,1024]{1,0:T(8,128)(2,1)} %get-tuple-element.42.refs_12_), channel_id=1, source_target_pairs={{0,8},{4,12},{8,0},{12,4},{1,9},{5,13},{9,1},{13,5},{2,10},{6,14},... | collective-permute-start | bytes 1572872 | tf_op jit(solution)/shard_map/tokens_0_2/ppermute | solution.py:101
  8.0 2.6 %collective-permute-start = (bf16[256,1024]{1,0:T(8,128)(2,1)}, bf16[256,1024]{1,0:T(8,128)(2,1)S(1)}, u32[]{:S(2)}, u32[]{:S(2)}) collective-permute-start(bf16[256,1024]{1,0:T(8,128)(2,1)} %get-tuple-element.42.refs_12_), channel_id=1, source_target_pairs={{0,2},{1,3},{2,0},{3,1},{4,6},{5,7},{6,4},{7,5},{8,10},{9,11},{10,... | collective-permute-start | bytes 1572872 | tf_op jit(solution)/shard_map/tokens_2/ppermute | solution.py:101
  10.6 8.0 %collective-permute-done.2.refs_14_ = bf16[256,1024]{1,0:T(8,128)(2,1)S(1)} collective-permute-done((bf16[256,1024]{1,0:T(8,128)(2,1)}, bf16[256,1024]{1,0:T(8,128)(2,1)S(1)}, u32[]{:S(2)}, u32[]{:S(2)}) %collective-permute-start.2) | collective-permute-done | bytes 524320 | tf_op jit(solution)/shard_map/tokens_0_2/ppermute | solution.py:101
  18.5 12.6 %collective-permute-done.1.refs_8_ = bf16[256,1024]{1,0:T(8,128)(2,1)S(1)} collective-permute-done((bf16[256,1024]{1,0:T(8,128)(2,1)}, bf16[256,1024]{1,0:T(8,128)(2,1)S(1)}, u32[]{:S(2)}, u32[]{:S(2)}) %collective-permute-start.1) | collective-permute-done | bytes 524320 | tf_op jit(solution)/shard_map/tokens_1/ppermute | solution.py:101
  31.1 2.4 %collective-permute-done.refs_4_ = bf16[256,1024]{1,0:T(8,128)(2,1)S(1)} collective-permute-done((bf16[256,1024]{1,0:T(8,128)(2,1)}, bf16[256,1024]{1,0:T(8,128)(2,1)S(1)}, u32[]{:S(2)}, u32[]{:S(2)}) %collective-permute-start) | collective-permute-done | bytes 524320 | tf_op jit(solution)/shard_map/tokens_2/ppermute | solution.py:101
  34.4 2.7 %collective-permute-start.5 = (bf16[256,1024]{1,0:T(8,128)(2,1)S(1)}, bf16[256,1024]{1,0:T(8,128)(2,1)S(1)}, u32[]{:S(2)}, u32[]{:S(2)}) collective-permute-start(bf16[256,1024]{1,0:T(8,128)(2,1)S(1)} %collective-permute-done.refs_4_), channel_id=1, source_target_pairs={{0,1},{1,0},{2,3},{3,2},{4,5},{5,4},{6,7},{7,6},{8,9},{9,8},{10,11... | collective-permute-start | bytes 1572872 | tf_op jit(solution)/shard_map/tokens_3/ppermute | solution.py:101
  37.1 6.5 %collective-permute-done.10.refs_10_ = bf16[256,1024]{1,0:T(8,128)(2,1)S(1)} collective-permute-done((bf16[256,1024]{1,0:T(8,128)(2,1)S(1)}, bf16[256,1024]{1,0:T(8,128)(2,1)S(1)}, u32[]{:S(2)}, u32[]{:S(2)}) %collective-permute-start.10) | collective-permute-done | bytes 524320 | tf_op jit(solution)/shard_map/tokens_1_2/ppermute | solution.py:101
  43.6 1.7 collective-permute-done.6.refs_20_
  46.7 2.7 %collective-permute-start.8 = (bf16[128,1024]{1,0:T(8,128)(2,1)}, bf16[128,1024]{1,0:T(8,128)(2,1)S(1)}, u32[]{:S(2)}, u32[]{:S(2)}) collective-permute-start(bf16[128,1024]{1,0:T(8,128)(2,1)} %get-tuple-element.47), channel_id=1, source_target_pairs={{0,3},{1,2},{2,1},{3,0},{4,7},{5,6},{6,5},{7,4},{8,11},{9,10},{10,... | collective-permute-start | bytes 786440 | tf_op jit(solution)/shard_map/weights_3/ppermute | solution.py:101
  49.4 9.4 %collective-permute-done.5.refs_0_ = bf16[256,1024]{1,0:T(8,128)(2,1)S(1)} collective-permute-done((bf16[256,1024]{1,0:T(8,128)(2,1)S(1)}, bf16[256,1024]{1,0:T(8,128)(2,1)S(1)}, u32[]{:S(2)}, u32[]{:S(2)}) %collective-permute-start.5) | collective-permute-done | bytes 524320 | tf_op jit(solution)/shard_map/tokens_3/ppermute | solution.py:101
  58.9 2.2 %collective-permute-start.13 = (bf16[128,1024]{1,0:T(8,128)(2,1)}, bf16[128,1024]{1,0:T(8,128)(2,1)S(1)}, u32[]{:S(2)}, u32[]{:S(2)}) collective-permute-start(bf16[128,1024]{1,0:T(8,128)(2,1)} %get-tuple-element.50), channel_id=1, source_target_pairs={{0,1},{1,0},{2,3},{3,2},{4,5},{5,4},{6,7},{7,6},{8,9},{9,8},{10,11... | collective-permute-start | bytes 786440 | tf_op jit(solution)/shard_map/weights_1/ppermute | solution.py:101
  64.7 2.6 %collective-permute-done.13.refs_18_ = bf16[128,1024]{1,0:T(8,128)(2,1)S(1)} collective-permute-done((bf16[128,1024]{1,0:T(8,128)(2,1)}, bf16[128,1024]{1,0:T(8,128)(2,1)S(1)}, u32[]{:S(2)}, u32[]{:S(2)}) %collective-permute-start.13) | collective-permute-done | bytes 262176 | tf_op jit(solution)/shard_map/weights_1/ppermute | solution.py:101
  68.7 3.4 %collective-permute-done.7.refs_21_ = bf16[128,1024]{1,0:T(8,128)(2,1)} collective-permute-done((bf16[128,1024]{1,0:T(8,128)(2,1)S(1)}, bf16[128,1024]{1,0:T(8,128)(2,1)}, u32[]{:S(2)}, u32[]{:S(2)}) %collective-permute-start.7) | collective-permute-done | bytes 262176 | tf_op jit(solution)/shard_map/weights_2/ppermute | solution.py:101
  72.0 5.5 %collective-permute-done.9.refs_23_ = bf16[128,1024]{1,0:T(8,128)(2,1)S(1)} collective-permute-done((bf16[128,1024]{1,0:T(8,128)(2,1)S(1)}, bf16[128,1024]{1,0:T(8,128)(2,1)S(1)}, u32[]{:S(2)}, u32[]{:S(2)}) %collective-permute-start.9) | collective-permute-done | bytes 262176 | tf_op jit(solution)/shard_map/weights_3/ppermute | solution.py:101
  77.5 3.4 %collective-permute-done.14.refs_19_ = bf16[128,1024]{1,0:T(8,128)(2,1)S(1)} collective-permute-done((bf16[128,1024]{1,0:T(8,128)(2,1)S(1)}, bf16[128,1024]{1,0:T(8,128)(2,1)S(1)}, u32[]{:S(2)}, u32[]{:S(2)}) %collective-permute-start.14) | collective-permute-done | bytes 262176 | tf_op jit(solution)/shard_map/weights_1/ppermute | solution.py:101
  84.4 24.5 %core.1 = (bf16[512,1024]{1,0:T(8,128)(2,1)}, bf16[528,1024]{1,0:T(8,128)(2,1)}, bf16[512,1024]{1,0:T(8,128)(2,1)}, bf16[512,1024]{1,0:T(8,128)(2,1)}, bf16[512,...) custom-call(bf16[256,1024]{1,0:T(8,128)(2,1)} %copy-done.20, ...), custom_call_target="tpu_custom_call" | custom-call | flops 10737418240 | bytes 20971520 | tf_op jit(solution)/shard_map/core/pallas_call | solution.py:252
  109.6 2.3 %collective-permute-done.27.refs_1_.refs_3_ = bf16[528,1024]{1,0:T(8,128)(2,1)S(1)} collective-permute-done((bf16[528,1024]{1,0:T(8,128)(2,1)}, bf16[528,1024]{1,0:T(8,128)(2,1)S(1)}, u32[]{:S(2)}, u32[]{:S(2)}) %collective-permute-start.27) | collective-permute-done | bytes 1081376 | tf_op jit(solution)/shard_map/sums_3_1/ppermute | solution.py:101
  112.8 2.3 %join.3 = (bf16[272,1024]{1,0:T(8,128)(2,1)}, bf16[16,1024]{1,0:T(8,128)(2,1)}) custom-call(bf16[512,1024]{1,0:T(8,128)(2,1)} %get-tuple-element.66.refs_0_, bf16[528,1024]{1,0:T(8,128)(2,1)} %copy-done.8, bf16[16,1024]{1,0:T(8,128)(2,1)} %get-tuple-element.68.refs_2_, bf16[528,1024]{1,0:T(8,128)(2,1)} %copy-done.8), custom_call_target="tpu_custom_call" | custom-call | bytes 1572864 | tf_op jit(solution)/shard_map/join/pallas_call | solution.py:386
  118.7 11.3 %collective-permute-done.28.refs_2_.refs_4_ = bf16[272,1024]{1,0:T(8,128)(2,1)S(1)} collective-permute-done((bf16[272,1024]{1,0:T(8,128)(2,1)}, bf16[272,1024]{1,0:T(8,128)(2,1)S(1)}, u32[]{:S(2)}, u32[]{:S(2)}) %collective-permute-start.28) | collective-permute-done | bytes 557088 | tf_op jit(solution)/shard_map/sums_3_2/ppermute | solution.py:101
  130.5 10.2 %collective-permute-done.21.refs_1_ = bf16[512,512]{1,0:T(8,128)(2,1)S(1)} collective-permute-done((bf16[512,512]{1,0:T(8,128)(2,1)}, bf16[512,512]{1,0:T(8,128)(2,1)S(1)}, u32[]{:S(2)}, u32[]{:S(2)}) %collective-permute-start.21) | collective-permute-done | bytes 524320 | tf_op jit(solution)/shard_map/grads_1/ppermute | solution.py:101
  141.9 2.5 %collective-permute-start.23 = (bf16[512,512]{1,0:T(8,128)(2,1)}, bf16[512,512]{1,0:T(8,128)(2,1)S(1)}, u32[]{:S(2)}, u32[]{:S(2)}) collective-permute-start(bf16[512,512]{1,0:T(8,128)(2,1)} %get-tuple-element.59), channel_id=1, source_target_pairs={{0,3},{1,2},{2,1},{3,0},{4,7},{5,6},{6,5},{7,4},{8,11},{9,10},{10,... | collective-permute-start | bytes 1572872 | tf_op jit(solution)/shard_map/grads_3/ppermute | solution.py:101
  144.4 2.7 %join.4 = (bf16[272,1024]{1,0:T(8,128)(2,1)}, bf16[16,1024]{1,0:T(8,128)(2,1)}) custom-call(bf16[512,1024]{1,0:T(8,128)(2,1)} %get-tuple-element.66.refs_0_, bf16[528,1024]{1,0:T(8,128)(2,1)} %copy-done.8, bf16[272,1024]{1,0:T(8,128)(2,1)} %copy-done.11, bf16[16,1024]{1,0:T(8,128)(2,1)} %get-tuple-element.73.refs_3_, bf16[272,1024]{1,0:T(8,128)(2,1)} %copy-done.11), custom_call_target="tpu_custom_call" | custom-call | bytes 2097152 | tf_op jit(solution)/shard_map/join/pallas_call | solution.py:386
  147.1 2.2 %add_convert_fusion.2 = bf16[256,1024]{1,0:T(8,128)(2,1)} fusion(bf16[512,1024]{1,0:T(8,128)(2,1)} %collective-permute-done.25, bf16[512,1024]{1,0:T(8,128)(2,1)} %get-tuple-element.62), kind=kLoop, calls=%fused_computation.2 | loop fusion | flops 1048576 | bytes 1572864 | tf_op jit(solution)/shard_map/convert_element_type | solution.py:474
  150.9 2.0 add_convert_fusion.3
  152.9 14.8 %collective-permute-done.32.refs_3_.refs_5_ = bf16[272,1024]{1,0:T(8,128)(2,1)S(1)} collective-permute-done((bf16[272,1024]{1,0:T(8,128)(2,1)}, bf16[272,1024]{1,0:T(8,128)(2,1)S(1)}, u32[]{:S(2)}, u32[]{:S(2)}) %collective-permute-start.32) | collective-permute-done | bytes 557088 | tf_op jit(solution)/shard_map/sums_3/ppermute | solution.py:101
  168.5 2.9 %join.5 = (bf16[272,1024]{1,0:T(8,128)(2,1)}, bf16[16,1024]{1,0:T(8,128)(2,1)}) custom-call(bf16[512,1024]{1,0:T(8,128)(2,1)} %get-tuple-element.64.refs_0_, bf16[512,1024]{1,0:T(8,128)(2,1)} %copy-done.10, bf16[256,1024]{1,0:T(8,128)(2,1)} %collective-permute-done.29.refs_2_, bf16[272,1024]{1,0:T(8,128)(2,1)} %copy-done.12, ...), custom_call_target="tpu_custom_call" | custom-call | bytes 2621440 | tf_op jit(solution)/shard_map/join/pallas_call | solution.py:386
  172.1 1.6 collective-permute-start.31
  173.7 1.6 add_convert_fusion
  175.9 22.4 %collective-permute-done.34.refs_8_ = bf16[272,1024]{1,0:T(8,128)(2,1)S(1)} collective-permute-done((bf16[272,1024]{1,0:T(8,128)(2,1)}, bf16[272,1024]{1,0:T(8,128)(2,1)S(1)}, u32[]{:S(2)}, u32[]{:S(2)}) %collective-permute-start.34) | collective-permute-done | bytes 557088 | tf_op jit(solution)/shard_map/sums_2/ppermute | solution.py:101
  198.3 2.0 collective-permute-done.33.refs_7_
  200.4 3.9 %finish.1 = (bf16[128,1024]{1,0:T(8,128)(2,1)}, f32[128,1024]{1,0:T(8,128)}, f32[256,2048]{1,0:T(8,128)}, f32[2048,256]{1,0:T(8,128)}, f32[2,1024]{1,0:T(2,128)}) custom-call(bf16[512,512]{1,0:T(8,128)(2,1)S(1)} %copy-done.2, bf16[512,512]{1,0:T(8,128)(2,1)S(1)} %collective-permute-done.21.refs_1_, bf16[512,512]{1,0:T(8,128)(2,1)S(1)} %collective-permute-done.22.refs_2_, ...), custom_call_target="tpu_custom_call" | custom-call | bytes 6291456 | tf_op jit(solution)/shard_map/finish/pallas_call | solution.py:346
  (114 shorter events, 22.6 us)
Async XLA Ops:
  3.4 15.1 %collective-permute-start.2 = (bf16[256,1024]{1,0:T(8,128)(2,1)}, bf16[256,1024]{1,0:T(8,128)(2,1)S(1)}, u32[]{:S(2)}, u32[]{:S(2)}) collective-permute-start(bf16[256,1024]{1,0:T(8,128)(2,1)} %get-tuple-element.42.refs_12_), channel_id=1, source_target_pairs={{0,8},{4,12},{8,0},{12,4},{1,9},{5,13},{9,1},{13,5},{2,10},{6,14},... | collective-permute-start | bytes 1572872 | tf_op jit(solution)/shard_map/tokens_0_2/ppermute | solution.py:101
  6.4 24.7 %collective-permute-start.1 = (bf16[256,1024]{1,0:T(8,128)(2,1)}, bf16[256,1024]{1,0:T(8,128)(2,1)S(1)}, u32[]{:S(2)}, u32[]{:S(2)}) collective-permute-start(bf16[256,1024]{1,0:T(8,128)(2,1)} %get-tuple-element.42.refs_12_), channel_id=1, source_target_pairs={{0,1},{1,0},{2,3},{3,2},{4,5},{5,4},{6,7},{7,6},{8,9},{9,8},{10,11... | collective-permute-start | bytes 1572872 | tf_op jit(solution)/shard_map/tokens_1/ppermute | solution.py:101
  8.0 25.5 %collective-permute-start = (bf16[256,1024]{1,0:T(8,128)(2,1)}, bf16[256,1024]{1,0:T(8,128)(2,1)S(1)}, u32[]{:S(2)}, u32[]{:S(2)}) collective-permute-start(bf16[256,1024]{1,0:T(8,128)(2,1)} %get-tuple-element.42.refs_12_), channel_id=1, source_target_pairs={{0,2},{1,3},{2,0},{3,1},{4,6},{5,7},{6,4},{7,5},{8,10},{9,11},{10,... | collective-permute-start | bytes 1572872 | tf_op jit(solution)/shard_map/tokens_2/ppermute | solution.py:101
  10.6 23.4 %collective-permute-start.3 = (bf16[256,1024]{1,0:T(8,128)(2,1)}, bf16[256,1024]{1,0:T(8,128)(2,1)S(1)}, u32[]{:S(2)}, u32[]{:S(2)}) collective-permute-start(bf16[256,1024]{1,0:T(8,128)(2,1)} %get-tuple-element.42.refs_12_), channel_id=1, source_target_pairs={{0,4},{4,0},{8,12},{12,8},{1,5},{5,1},{9,13},{13,9},{2,6},{6,2},{1... | collective-permute-start | bytes 1572872 | tf_op jit(solution)/shard_map/tokens_0_1/ppermute | solution.py:101
  18.5 15.5 %collective-permute-start.4 = (bf16[256,1024]{1,0:T(8,128)(2,1)S(1)}, bf16[256,1024]{1,0:T(8,128)(2,1)S(1)}, u32[]{:S(2)}, u32[]{:S(2)}) collective-permute-start(bf16[256,1024]{1,0:T(8,128)(2,1)S(1)} %collective-permute-done.2.refs_14_), channel_id=1, source_target_pairs={{0,4},{4,0},{8,12},{12,8},{1,5},{5,1},{9,13},{13,9},{2,6},{6,2},{1... | collective-permute-start | bytes 1572872 | tf_op jit(solution)/shard_map/tokens_0_3/ppermute | solution.py:101
  33.5 10.1 %collective-permute-start.10 = (bf16[256,1024]{1,0:T(8,128)(2,1)S(1)}, bf16[256,1024]{1,0:T(8,128)(2,1)S(1)}, u32[]{:S(2)}, u32[]{:S(2)}) collective-permute-start(bf16[256,1024]{1,0:T(8,128)(2,1)S(1)} %collective-permute-done.1.refs_8_), channel_id=1, source_target_pairs={{0,8},{4,12},{8,0},{12,4},{1,9},{5,13},{9,1},{13,5},{2,10},{6,14},... | collective-permute-start | bytes 1572872 | tf_op jit(solution)/shard_map/tokens_1_2/ppermute | solution.py:101
  34.0 11.3 %collective-permute-start.6 = (bf16[128,1024]{1,0:T(8,128)(2,1)}, bf16[128,1024]{1,0:T(8,128)(2,1)S(1)}, u32[]{:S(2)}, u32[]{:S(2)}) collective-permute-start(bf16[128,1024]{1,0:T(8,128)(2,1)} %get-tuple-element.45), channel_id=1, source_target_pairs={{0,2},{1,3},{2,0},{3,1},{4,6},{5,7},{6,4},{7,5},{8,10},{9,11},{10,... | collective-permute-start | bytes 786440 | tf_op jit(solution)/shard_map/weights_2/ppermute | solution.py:101
  34.4 15.0 %collective-permute-start.11 = (bf16[256,1024]{1,0:T(8,128)(2,1)S(1)}, bf16[256,1024]{1,0:T(8,128)(2,1)S(1)}, u32[]{:S(2)}, u32[]{:S(2)}) collective-permute-start(bf16[256,1024]{1,0:T(8,128)(2,1)S(1)} %collective-permute-done.1.refs_8_), channel_id=1, source_target_pairs={{0,4},{4,0},{8,12},{12,8},{1,5},{5,1},{9,13},{13,9},{2,6},{6,2},{1... | collective-permute-start | bytes 1572872 | tf_op jit(solution)/shard_map/tokens_1_1/ppermute | solution.py:101
  34.4 24.5 %collective-permute-start.5 = (bf16[256,1024]{1,0:T(8,128)(2,1)S(1)}, bf16[256,1024]{1,0:T(8,128)(2,1)S(1)}, u32[]{:S(2)}, u32[]{:S(2)}) collective-permute-start(bf16[256,1024]{1,0:T(8,128)(2,1)S(1)} %collective-permute-done.refs_4_), channel_id=1, source_target_pairs={{0,1},{1,0},{2,3},{3,2},{4,5},{5,4},{6,7},{7,6},{8,9},{9,8},{10,11... | collective-permute-start | bytes 1572872 | tf_op jit(solution)/shard_map/tokens_3/ppermute | solution.py:101
  43.6 15.2 %collective-permute-start.12 = (bf16[256,1024]{1,0:T(8,128)(2,1)S(1)}, bf16[256,1024]{1,0:T(8,128)(2,1)S(1)}, u32[]{:S(2)}, u32[]{:S(2)}) collective-permute-start(bf16[256,1024]{1,0:T(8,128)(2,1)S(1)} %collective-permute-done.10.refs_10_), channel_id=1, source_target_pairs={{0,4},{4,0},{8,12},{12,8},{1,5},{5,1},{9,13},{13,9},{2,6},{6,2},{1... | collective-permute-start | bytes 1572872 | tf_op jit(solution)/shard_map/tokens_1_3/ppermute | solution.py:101
  45.4 15.8 %collective-permute-start.16 = (bf16[256,1024]{1,0:T(8,128)(2,1)S(1)}, bf16[256,1024]{1,0:T(8,128)(2,1)S(1)}, u32[]{:S(2)}, u32[]{:S(2)}) collective-permute-start(bf16[256,1024]{1,0:T(8,128)(2,1)S(1)} %collective-permute-done.refs_4_), channel_id=1, source_target_pairs={{0,8},{4,12},{8,0},{12,4},{1,9},{5,13},{9,1},{13,5},{2,10},{6,14},... | collective-permute-start | bytes 1572872 | tf_op jit(solution)/shard_map/tokens_2_2/ppermute | solution.py:101
  46.7 12.2 %collective-permute-start.8 = (bf16[128,1024]{1,0:T(8,128)(2,1)}, bf16[128,1024]{1,0:T(8,128)(2,1)S(1)}, u32[]{:S(2)}, u32[]{:S(2)}) collective-permute-start(bf16[128,1024]{1,0:T(8,128)(2,1)} %get-tuple-element.47), channel_id=1, source_target_pairs={{0,3},{1,2},{2,1},{3,0},{4,7},{5,6},{6,5},{7,4},{8,11},{9,10},{10,... | collective-permute-start | bytes 786440 | tf_op jit(solution)/shard_map/weights_3/ppermute | solution.py:101
  58.9 8.4 %collective-permute-start.13 = (bf16[128,1024]{1,0:T(8,128)(2,1)}, bf16[128,1024]{1,0:T(8,128)(2,1)S(1)}, u32[]{:S(2)}, u32[]{:S(2)}) collective-permute-start(bf16[128,1024]{1,0:T(8,128)(2,1)} %get-tuple-element.50), channel_id=1, source_target_pairs={{0,1},{1,0},{2,3},{3,2},{4,5},{5,4},{6,7},{7,6},{8,9},{9,8},{10,11... | collective-permute-start | bytes 786440 | tf_op jit(solution)/shard_map/weights_1/ppermute | solution.py:101
  61.2 20.4 %collective-permute-start.17 = (bf16[256,1024]{1,0:T(8,128)(2,1)S(1)}, bf16[256,1024]{1,0:T(8,128)(2,1)S(1)}, u32[]{:S(2)}, u32[]{:S(2)}) collective-permute-start(bf16[256,1024]{1,0:T(8,128)(2,1)S(1)} %collective-permute-done.5.refs_0_), channel_id=1, source_target_pairs={{0,8},{4,12},{8,0},{12,4},{1,9},{5,13},{9,1},{13,5},{2,10},{6,14},... | collective-permute-start | bytes 1572872 | tf_op jit(solution)/shard_map/tokens_3_2/ppermute | solution.py:101
  62.7 9.3 %collective-permute-start.7 = (bf16[128,1024]{1,0:T(8,128)(2,1)S(1)}, bf16[128,1024]{1,0:T(8,128)(2,1)}, u32[]{:S(2)}, u32[]{:S(2)}) collective-permute-start(bf16[128,1024]{1,0:T(8,128)(2,1)S(1)} %collective-permute-done.6.refs_20_), channel_id=1, source_target_pairs={{0,16},{16,0},{1,17},{17,1},{2,18},{18,2},{3,19},{19,3},{4,20},{20... | collective-permute-start | bytes 786440 | tf_op jit(solution)/shard_map/weights_2/ppermute | solution.py:101
  64.2 13.4 %collective-permute-start.9 = (bf16[128,1024]{1,0:T(8,128)(2,1)S(1)}, bf16[128,1024]{1,0:T(8,128)(2,1)S(1)}, u32[]{:S(2)}, u32[]{:S(2)}) collective-permute-start(bf16[128,1024]{1,0:T(8,128)(2,1)S(1)} %collective-permute-done.8.refs_22_), channel_id=1, source_target_pairs={{0,16},{16,0},{1,17},{17,1},{2,18},{18,2},{3,19},{19,3},{4,20},{20... | collective-permute-start | bytes 786440 | tf_op jit(solution)/shard_map/weights_3/ppermute | solution.py:101
  67.3 13.6 %collective-permute-start.14 = (bf16[128,1024]{1,0:T(8,128)(2,1)S(1)}, bf16[128,1024]{1,0:T(8,128)(2,1)S(1)}, u32[]{:S(2)}, u32[]{:S(2)}) collective-permute-start(bf16[128,1024]{1,0:T(8,128)(2,1)S(1)} %collective-permute-done.13.refs_18_), channel_id=1, source_target_pairs={{0,16},{16,0},{1,17},{17,1},{2,18},{18,2},{3,19},{19,3},{4,20},{20... | collective-permute-start | bytes 786440 | tf_op jit(solution)/shard_map/weights_1/ppermute | solution.py:101
  68.7 12.9 %collective-permute-start.19 = (bf16[256,1024]{1,0:T(8,128)(2,1)S(1)}, bf16[256,1024]{1,0:T(8,128)(2,1)S(1)}, u32[]{:S(2)}, u32[]{:S(2)}) collective-permute-start(bf16[256,1024]{1,0:T(8,128)(2,1)S(1)} %collective-permute-done.refs_4_), channel_id=1, source_target_pairs={{0,4},{4,0},{8,12},{12,8},{1,5},{5,1},{9,13},{13,9},{2,6},{6,2},{1... | collective-permute-start | bytes 1572872 | tf_op jit(solution)/shard_map/tokens_2_1/ppermute | solution.py:101
  72.0 9.6 %collective-permute-start.20 = (bf16[256,1024]{1,0:T(8,128)(2,1)S(1)}, bf16[256,1024]{1,0:T(8,128)(2,1)S(1)}, u32[]{:S(2)}, u32[]{:S(2)}) collective-permute-start(bf16[256,1024]{1,0:T(8,128)(2,1)S(1)} %collective-permute-done.16.refs_6_), channel_id=1, source_target_pairs={{0,4},{4,0},{8,12},{12,8},{1,5},{5,1},{9,13},{13,9},{2,6},{6,2},{1... | collective-permute-start | bytes 1572872 | tf_op jit(solution)/shard_map/tokens_2_3/ppermute | solution.py:101
  109.1 8.5 %collective-permute-start.26 = (bf16[512,1024]{1,0:T(8,128)(2,1)}, bf16[512,1024]{1,0:T(8,128)(2,1)S(1)}, u32[]{:S(2)}, u32[]{:S(2)}) collective-permute-start(bf16[512,1024]{1,0:T(8,128)(2,1)} %get-tuple-element.65), channel_id=1, source_target_pairs={{0,4},{4,0},{8,12},{12,8},{1,5},{5,1},{9,13},{13,9},{2,6},{6,2},{1... | collective-permute-start | bytes 3145736 | tf_op jit(solution)/shard_map/sums_2_1/ppermute | solution.py:101
  109.4 37.7 %collective-permute-start.25 = (bf16[512,1024]{1,0:T(8,128)(2,1)}, bf16[512,1024]{1,0:T(8,128)(2,1)}, u32[]{:S(2)}, u32[]{:S(2)}) collective-permute-start(bf16[512,1024]{1,0:T(8,128)(2,1)} %get-tuple-element.63), channel_id=1, source_target_pairs={{0,4},{4,0},{8,12},{12,8},{1,5},{5,1},{9,13},{13,9},{2,6},{6,2},{1... | collective-permute-start | bytes 3145736 | tf_op jit(solution)/shard_map/sums_1_1/ppermute | solution.py:101
  115.1 14.9 %collective-permute-start.28 = (bf16[272,1024]{1,0:T(8,128)(2,1)}, bf16[272,1024]{1,0:T(8,128)(2,1)S(1)}, u32[]{:S(2)}, u32[]{:S(2)}) collective-permute-start(bf16[272,1024]{1,0:T(8,128)(2,1)} %get-tuple-element.69), channel_id=1, source_target_pairs={{0,8},{4,12},{8,0},{12,4},{1,9},{5,13},{9,1},{13,5},{2,10},{6,14},... | collective-permute-start | bytes 1671176 | tf_op jit(solution)/shard_map/sums_3_2/ppermute | solution.py:101
  115.6 25.1 %collective-permute-start.21 = (bf16[512,512]{1,0:T(8,128)(2,1)}, bf16[512,512]{1,0:T(8,128)(2,1)S(1)}, u32[]{:S(2)}, u32[]{:S(2)}) collective-permute-start(bf16[512,512]{1,0:T(8,128)(2,1)} %get-tuple-element.56), channel_id=1, source_target_pairs={{0,1},{1,0},{2,3},{3,2},{4,5},{5,4},{6,7},{7,6},{8,9},{9,8},{10,11... | collective-permute-start | bytes 1572872 | tf_op jit(solution)/shard_map/grads_1/ppermute | solution.py:101
  116.1 25.8 %collective-permute-start.22 = (bf16[512,512]{1,0:T(8,128)(2,1)}, bf16[512,512]{1,0:T(8,128)(2,1)S(1)}, u32[]{:S(2)}, u32[]{:S(2)}) collective-permute-start(bf16[512,512]{1,0:T(8,128)(2,1)} %get-tuple-element.57), channel_id=1, source_target_pairs={{0,2},{1,3},{2,0},{3,1},{4,6},{5,7},{6,4},{7,5},{8,10},{9,11},{10,... | collective-permute-start | bytes 1572872 | tf_op jit(solution)/shard_map/grads_2/ppermute | solution.py:101
  117.6 33.3 %collective-permute-start.24 = (bf16[512,1024]{1,0:T(8,128)(2,1)}, bf16[512,1024]{1,0:T(8,128)(2,1)}, u32[]{:S(2)}, u32[]{:S(2)}) collective-permute-start(bf16[512,1024]{1,0:T(8,128)(2,1)} %get-tuple-element.61), channel_id=1, source_target_pairs={{0,4},{4,0},{8,12},{12,8},{1,5},{5,1},{9,13},{13,9},{2,6},{6,2},{1... | collective-permute-start | bytes 3145736 | tf_op jit(solution)/shard_map/sums_0_1/ppermute | solution.py:101
  130.0 19.3 %collective-permute-start.29 = (bf16[256,1024]{1,0:T(8,128)(2,1)}, bf16[256,1024]{1,0:T(8,128)(2,1)}, u32[]{:S(2)}, u32[]{:S(2)}) collective-permute-start(bf16[256,1024]{1,0:T(8,128)(2,1)} %add_convert_fusion.1), channel_id=1, source_target_pairs={{0,8},{4,12},{8,0},{12,4},{1,9},{5,13},{9,1},{13,5},{2,10},{6,14},... | collective-permute-start | bytes 1572872 | tf_op jit(solution)/shard_map/sums_2_2/ppermute | solution.py:101
  141.9 30.2 %collective-permute-start.23 = (bf16[512,512]{1,0:T(8,128)(2,1)}, bf16[512,512]{1,0:T(8,128)(2,1)S(1)}, u32[]{:S(2)}, u32[]{:S(2)}) collective-permute-start(bf16[512,512]{1,0:T(8,128)(2,1)} %get-tuple-element.59), channel_id=1, source_target_pairs={{0,3},{1,2},{2,1},{3,0},{4,7},{5,6},{6,5},{7,4},{8,11},{9,10},{10,... | collective-permute-start | bytes 1572872 | tf_op jit(solution)/shard_map/grads_3/ppermute | solution.py:101
  147.1 20.6 %collective-permute-start.32 = (bf16[272,1024]{1,0:T(8,128)(2,1)}, bf16[272,1024]{1,0:T(8,128)(2,1)S(1)}, u32[]{:S(2)}, u32[]{:S(2)}) collective-permute-start(bf16[272,1024]{1,0:T(8,128)(2,1)} %get-tuple-element.74), channel_id=1, source_target_pairs={{0,1},{1,0},{2,3},{3,2},{4,5},{5,4},{6,7},{7,6},{8,9},{9,8},{10,11... | collective-permute-start | bytes 1671176 | tf_op jit(solution)/shard_map/sums_3/ppermute | solution.py:101
  149.3 22.7 %collective-permute-start.30 = (bf16[256,1024]{1,0:T(8,128)(2,1)}, bf16[256,1024]{1,0:T(8,128)(2,1)}, u32[]{:S(2)}, u32[]{:S(2)}) collective-permute-start(bf16[256,1024]{1,0:T(8,128)(2,1)} %add_convert_fusion.2), channel_id=1, source_target_pairs={{0,8},{4,12},{8,0},{12,4},{1,9},{5,13},{9,1},{13,5},{2,10},{6,14},... | collective-permute-start | bytes 1572872 | tf_op jit(solution)/shard_map/sums_1_2/ppermute | solution.py:101
  171.4 26.9 %collective-permute-start.34 = (bf16[272,1024]{1,0:T(8,128)(2,1)}, bf16[272,1024]{1,0:T(8,128)(2,1)S(1)}, u32[]{:S(2)}, u32[]{:S(2)}) collective-permute-start(bf16[272,1024]{1,0:T(8,128)(2,1)} %get-tuple-element.76), channel_id=1, source_target_pairs={{0,2},{1,3},{2,0},{3,1},{4,6},{5,7},{6,4},{7,5},{8,10},{9,11},{10,... | collective-permute-start | bytes 1671176 | tf_op jit(solution)/shard_map/sums_2/ppermute | solution.py:101
  172.1 26.2 %collective-permute-start.31 = (bf16[256,1024]{1,0:T(8,128)(2,1)}, bf16[256,1024]{1,0:T(8,128)(2,1)S(1)}, u32[]{:S(2)}, u32[]{:S(2)}) collective-permute-start(bf16[256,1024]{1,0:T(8,128)(2,1)} %add_convert_fusion.3), channel_id=1, source_target_pairs={{0,8},{4,12},{8,0},{12,4},{1,9},{5,13},{9,1},{13,5},{2,10},{6,14},... | collective-permute-start | bytes 1572872 | tf_op jit(solution)/shard_map/sums_0_2/ppermute | solution.py:101
  175.3 25.0 %collective-permute-start.33 = (bf16[256,1024]{1,0:T(8,128)(2,1)S(1)}, bf16[256,1024]{1,0:T(8,128)(2,1)S(1)}, u32[]{:S(2)}, u32[]{:S(2)}) collective-permute-start(bf16[256,1024]{1,0:T(8,128)(2,1)S(1)} %add_convert_fusion), channel_id=1, source_target_pairs={{0,1},{1,0},{2,3},{3,2},{4,5},{5,4},{6,7},{7,6},{8,9},{9,8},{10,11... | collective-permute-start | bytes 1572872 | tf_op jit(solution)/shard_map/sums_1/ppermute | solution.py:101
  (36 other events, 771.0 us)

commit v11 on v10

--- a/solution.py
+++ b/solution.py
@@ -449,11 +449,13 @@
         tokens_rest(k - 1)
         stage = [got[top]]
         if k & (k - 1):
-            stage = [tokens[k], *got.values(), *chunks[k - 2].values()]
+            weights_groups(top)
+            stage = [tokens[k], *got.values(), *crossed.values(), *chunks[k - 2].values()]
         tokens_tensor(k, *stage, chunks[k - 1][high])
     weights_dp(1, *stage)
     for k in [*range(2, n_dp), 1]:
-        weights_groups(k)
+        if k not in crossed:
+            weights_groups(k)
     tokens_rest(n_dp - 1, *crossed.values())
     got = {k: [got[k]] + ([crossed[k]] if k in crossed else []) for k in got}
 
@@ -466,8 +468,9 @@
 
     for k in range(1, top):
         blocks[k] = swap(blocks[k], "dp", k, f"grads_{k}")
+    third = {}
     for k in range(top + 1, n_dp):
-        blocks[k] = swap(after(blocks[k], *(blocks[j] for j in range(1, k))), "dp", k, f"grads_{k}")
+        third[k] = blocks[k]
 
     def add(terms):
         spans = (x[place * span : (place + 1) * span].astype(jnp.float32) for x, place in terms)
@@ -485,8 +488,8 @@
                     send, stats = join(span, parts.pop(j), [(stats, 0), waiting])
                 else:
                     send = add(parts.pop(j))
-                if k < 2:
-                    behind += (blocks[n_dp - 1 if k == 0 else top],)
+                if behind and k:
+                    behind += (blocks[1 if k == top else top],)
                 came = swap(after(send, *behind), "tensor", bit, f"sums_{k}_{j}")
                 if k == order[0] and j == bit:
                     waiting = (came, span // EXTRA)
@@ -501,6 +504,9 @@
             else:
                 send = add(sums.pop(k))
             came[k] = swap(send, "dp", bit, f"sums_{k}")
+            for j in third:
+                blocks[j] = swap(after(third[j], blocks[top], send), "dp", j, f"grads_{j}")
+            third = {}
             if k == (n_dp - 1) & -bit:
                 waiting = (came[k], span // EXTRA)
             sums[k ^ bit].append((came[k], 0))

time: 205 us -> 202 us (0.985)
  no operation moved by 1% of the time
where the time goes in v11:
time: 202 us
  waiting for transfers between devices  120 us (59%)
  Pallas kernels  39.1 us (19%)
  starting transfers between devices  32.3 us (16%)
  other arithmetic  6.99 us (3%)
  local copies, waits for them, and re-layouts  2.54 us (1%)
    ppermute x35, waiting for transfers between devices, swap(): lax.ppermute(values, axis, [(i, i ^ mask) for i in range(lax.axis_size(ax...  120 us
    ppermute x35, starting transfers between devices, swap(): lax.ppermute(values, axis, [(i, i ^ mask) for i in range(lax.axis_size(ax...  32.3 us
    pallas_call x1, Pallas kernels, core(): pl.pallas_call(kernel, out_shape=[jax.ShapeDtypeStruct((half[0] + (EXTRA...  24.5 us
    pallas_call x3, Pallas kernels, join(): pl.pallas_call(kernel, out_shape=out_shape, grid=(1,), in_specs=[spec(row...  7.91 us
    convert_element_type x4, other arithmetic, add(): return sum(spans).astype(jnp.bfloat16)  6.99 us
  transfers between devices with their start and end apart: 35, of which 19 were waited for; matrix products, arithmetic and copies ran while one was open for 3% of the time, Pallas kernels for 4%

profile of v11, /device:TPU:0, one launch (start us, length us, event | category | flops | bytes accessed | tf_op | source)
XLA Modules:
  0.0 202.1 jit_solution(11930304435177223210)
XLA Ops:
  0.6 2.8 %pack.1 = (bf16[256,1024]{1,0:T(8,128)(2,1)}, bf16[128,1024]{1,0:T(8,128)(2,1)}, bf16[128,1024]{1,0:T(8,128)(2,1)}, bf16[128,1024]{1,0:T(8,128)(2,1)}) custom-call(bf16[128,1024]{1,0:T(8,128)(2,1)} %refs_10_.1, bf16[128,1024]{1,0:T(8,128)(2,1)} %grad_ref.1, bf16[256,2048]{1,0:T(8,128)(2,1)} %refs_16_.1, bf16[2048,256]{1,0:T(8,128)(2,1)} %refs_17_.1), custom_call_target="tpu_custom_call" | custom-call | bytes 4194304 | tf_op jit(solution)/shard_map/pack/pallas_call | solution.py:125
  3.4 3.0 %collective-permute-start.2 = (bf16[256,1024]{1,0:T(8,128)(2,1)}, bf16[256,1024]{1,0:T(8,128)(2,1)S(1)}, u32[]{:S(2)}, u32[]{:S(2)}) collective-permute-start(bf16[256,1024]{1,0:T(8,128)(2,1)} %get-tuple-element.42.refs_12_), channel_id=1, source_target_pairs={{0,8},{4,12},{8,0},{12,4},{1,9},{5,13},{9,1},{13,5},{2,10},{6,14},... | collective-permute-start | bytes 1572872 | tf_op jit(solution)/shard_map/tokens_0_2/ppermute | solution.py:101
  6.4 1.6 collective-permute-start.1
  8.0 2.6 %collective-permute-start = (bf16[256,1024]{1,0:T(8,128)(2,1)}, bf16[256,1024]{1,0:T(8,128)(2,1)S(1)}, u32[]{:S(2)}, u32[]{:S(2)}) collective-permute-start(bf16[256,1024]{1,0:T(8,128)(2,1)} %get-tuple-element.42.refs_12_), channel_id=1, source_target_pairs={{0,2},{1,3},{2,0},{3,1},{4,6},{5,7},{6,4},{7,5},{8,10},{9,11},{10,... | collective-permute-start | bytes 1572872 | tf_op jit(solution)/shard_map/tokens_2/ppermute | solution.py:101
  10.6 8.0 %collective-permute-done.2.refs_14_ = bf16[256,1024]{1,0:T(8,128)(2,1)S(1)} collective-permute-done((bf16[256,1024]{1,0:T(8,128)(2,1)}, bf16[256,1024]{1,0:T(8,128)(2,1)S(1)}, u32[]{:S(2)}, u32[]{:S(2)}) %collective-permute-start.2) | collective-permute-done | bytes 524320 | tf_op jit(solution)/shard_map/tokens_0_2/ppermute | solution.py:101
  18.5 12.6 %collective-permute-done.1.refs_8_ = bf16[256,1024]{1,0:T(8,128)(2,1)S(1)} collective-permute-done((bf16[256,1024]{1,0:T(8,128)(2,1)}, bf16[256,1024]{1,0:T(8,128)(2,1)S(1)}, u32[]{:S(2)}, u32[]{:S(2)}) %collective-permute-start.1) | collective-permute-done | bytes 524320 | tf_op jit(solution)/shard_map/tokens_1/ppermute | solution.py:101
  31.1 2.4 %collective-permute-done.refs_4_ = bf16[256,1024]{1,0:T(8,128)(2,1)S(1)} collective-permute-done((bf16[256,1024]{1,0:T(8,128)(2,1)}, bf16[256,1024]{1,0:T(8,128)(2,1)S(1)}, u32[]{:S(2)}, u32[]{:S(2)}) %collective-permute-start) | collective-permute-done | bytes 524320 | tf_op jit(solution)/shard_map/tokens_2/ppermute | solution.py:101
  34.4 2.7 %collective-permute-start.5 = (bf16[256,1024]{1,0:T(8,128)(2,1)S(1)}, bf16[256,1024]{1,0:T(8,128)(2,1)S(1)}, u32[]{:S(2)}, u32[]{:S(2)}) collective-permute-start(bf16[256,1024]{1,0:T(8,128)(2,1)S(1)} %collective-permute-done.refs_4_), channel_id=1, source_target_pairs={{0,1},{1,0},{2,3},{3,2},{4,5},{5,4},{6,7},{7,6},{8,9},{9,8},{10,11... | collective-permute-start | bytes 1572872 | tf_op jit(solution)/shard_map/tokens_3/ppermute | solution.py:101
  37.1 6.5 %collective-permute-done.10.refs_10_ = bf16[256,1024]{1,0:T(8,128)(2,1)S(1)} collective-permute-done((bf16[256,1024]{1,0:T(8,128)(2,1)S(1)}, bf16[256,1024]{1,0:T(8,128)(2,1)S(1)}, u32[]{:S(2)}, u32[]{:S(2)}) %collective-permute-start.10) | collective-permute-done | bytes 524320 | tf_op jit(solution)/shard_map/tokens_1_2/ppermute | solution.py:101
  43.6 5.9 %collective-permute-done.6.refs_20_ = bf16[128,1024]{1,0:T(8,128)(2,1)S(1)} collective-permute-done((bf16[128,1024]{1,0:T(8,128)(2,1)}, bf16[128,1024]{1,0:T(8,128)(2,1)S(1)}, u32[]{:S(2)}, u32[]{:S(2)}) %collective-permute-start.6) | collective-permute-done | bytes 262176 | tf_op jit(solution)/shard_map/weights_2/ppermute | solution.py:101
  49.5 1.5 collective-permute-start.16
  52.4 1.5 collective-permute-start.7
  55.0 6.0 %collective-permute-done.8.refs_22_ = bf16[128,1024]{1,0:T(8,128)(2,1)S(1)} collective-permute-done((bf16[128,1024]{1,0:T(8,128)(2,1)}, bf16[128,1024]{1,0:T(8,128)(2,1)S(1)}, u32[]{:S(2)}, u32[]{:S(2)}) %collective-permute-start.8) | collective-permute-done | bytes 262176 | tf_op jit(solution)/shard_map/weights_3/ppermute | solution.py:101
  61.1 2.4 %collective-permute-start.13 = (bf16[128,1024]{1,0:T(8,128)(2,1)}, bf16[128,1024]{1,0:T(8,128)(2,1)S(1)}, u32[]{:S(2)}, u32[]{:S(2)}) collective-permute-start(bf16[128,1024]{1,0:T(8,128)(2,1)} %get-tuple-element.50), channel_id=1, source_target_pairs={{0,1},{1,0},{2,3},{3,2},{4,5},{5,4},{6,7},{7,6},{8,9},{9,8},{10,11... | collective-permute-start | bytes 786440 | tf_op jit(solution)/shard_map/weights_1/ppermute | solution.py:101
  66.4 2.7 %collective-permute-done.13.refs_18_ = bf16[128,1024]{1,0:T(8,128)(2,1)S(1)} collective-permute-done((bf16[128,1024]{1,0:T(8,128)(2,1)}, bf16[128,1024]{1,0:T(8,128)(2,1)S(1)}, u32[]{:S(2)}, u32[]{:S(2)}) %collective-permute-start.13) | collective-permute-done | bytes 262176 | tf_op jit(solution)/shard_map/weights_1/ppermute | solution.py:101
  71.1 2.8 %collective-permute-done.9.refs_23_ = bf16[128,1024]{1,0:T(8,128)(2,1)S(1)} collective-permute-done((bf16[128,1024]{1,0:T(8,128)(2,1)S(1)}, bf16[128,1024]{1,0:T(8,128)(2,1)S(1)}, u32[]{:S(2)}, u32[]{:S(2)}) %collective-permute-start.9) | collective-permute-done | bytes 262176 | tf_op jit(solution)/shard_map/weights_3/ppermute | solution.py:101
  73.9 3.7 %collective-permute-done.14.refs_19_ = bf16[128,1024]{1,0:T(8,128)(2,1)S(1)} collective-permute-done((bf16[128,1024]{1,0:T(8,128)(2,1)S(1)}, bf16[128,1024]{1,0:T(8,128)(2,1)S(1)}, u32[]{:S(2)}, u32[]{:S(2)}) %collective-permute-start.14) | collective-permute-done | bytes 262176 | tf_op jit(solution)/shard_map/weights_1/ppermute | solution.py:101
  81.0 24.5 %core.1 = (bf16[512,1024]{1,0:T(8,128)(2,1)}, bf16[528,1024]{1,0:T(8,128)(2,1)}, bf16[512,1024]{1,0:T(8,128)(2,1)}, bf16[512,1024]{1,0:T(8,128)(2,1)}, bf16[512,...) custom-call(bf16[256,1024]{1,0:T(8,128)(2,1)} %copy-done.20, ...), custom_call_target="tpu_custom_call" | custom-call | flops 10737418240 | bytes 20971520 | tf_op jit(solution)/shard_map/core/pallas_call | solution.py:252
  106.3 2.4 %collective-permute-done.23.refs_1_.refs_3_ = bf16[528,1024]{1,0:T(8,128)(2,1)S(1)} collective-permute-done((bf16[528,1024]{1,0:T(8,128)(2,1)}, bf16[528,1024]{1,0:T(8,128)(2,1)S(1)}, u32[]{:S(2)}, u32[]{:S(2)}) %collective-permute-start.23) | collective-permute-done | bytes 1081376 | tf_op jit(solution)/shard_map/sums_3_1/ppermute | solution.py:101
  109.7 2.3 %join.3 = (bf16[272,1024]{1,0:T(8,128)(2,1)}, bf16[16,1024]{1,0:T(8,128)(2,1)}) custom-call(bf16[512,1024]{1,0:T(8,128)(2,1)} %get-tuple-element.59.refs_0_, bf16[528,1024]{1,0:T(8,128)(2,1)} %copy-done.8, bf16[16,1024]{1,0:T(8,128)(2,1)} %get-tuple-element.61.refs_2_, bf16[528,1024]{1,0:T(8,128)(2,1)} %copy-done.8), custom_call_target="tpu_custom_call" | custom-call | bytes 1572864 | tf_op jit(solution)/shard_map/join/pallas_call | solution.py:386
  112.7 2.7 %collective-permute-start.22 = (bf16[512,512]{1,0:T(8,128)(2,1)}, bf16[512,512]{1,0:T(8,128)(2,1)S(1)}, u32[]{:S(2)}, u32[]{:S(2)}) collective-permute-start(bf16[512,512]{1,0:T(8,128)(2,1)} %get-tuple-element.57), channel_id=1, source_target_pairs={{0,2},{1,3},{2,0},{3,1},{4,6},{5,7},{6,4},{7,5},{8,10},{9,11},{10,... | collective-permute-start | bytes 1572872 | tf_op jit(solution)/shard_map/grads_2/ppermute | solution.py:101
  115.4 2.0 %add_convert_fusion.1 = bf16[256,1024]{1,0:T(8,128)(2,1)} fusion(bf16[512,1024]{1,0:T(8,128)(2,1)} %collective-permute-done.28.refs_1_, bf16[512,1024]{1,0:T(8,128)(2,1)S(1)} %copy-done.9), kind=kLoop, calls=%fused_computation.1 | loop fusion | flops 1048576 | bytes 1572864 | tf_op jit(solution)/shard_map/convert_element_type | solution.py:477
  117.4 19.2 %collective-permute-done.21.refs_1_ = bf16[512,512]{1,0:T(8,128)(2,1)S(1)} collective-permute-done((bf16[512,512]{1,0:T(8,128)(2,1)}, bf16[512,512]{1,0:T(8,128)(2,1)S(1)}, u32[]{:S(2)}, u32[]{:S(2)}) %collective-permute-start.21) | collective-permute-done | bytes 524320 | tf_op jit(solution)/shard_map/grads_1/ppermute | solution.py:101
  137.9 2.7 %join.4 = (bf16[272,1024]{1,0:T(8,128)(2,1)}, bf16[16,1024]{1,0:T(8,128)(2,1)}) custom-call(bf16[512,1024]{1,0:T(8,128)(2,1)} %get-tuple-element.59.refs_0_, bf16[528,1024]{1,0:T(8,128)(2,1)} %copy-done.8, bf16[272,1024]{1,0:T(8,128)(2,1)} %copy-done.12, bf16[16,1024]{1,0:T(8,128)(2,1)} %get-tuple-element.63.refs_3_, bf16[272,1024]{1,0:T(8,128)(2,1)} %copy-done.12), custom_call_target="tpu_custom_call" | custom-call | bytes 2097152 | tf_op jit(solution)/shard_map/join/pallas_call | solution.py:386
  140.5 2.2 %add_convert_fusion.2 = bf16[256,1024]{1,0:T(8,128)(2,1)} fusion(bf16[512,1024]{1,0:T(8,128)(2,1)} %collective-permute-done.27, bf16[512,1024]{1,0:T(8,128)(2,1)} %get-tuple-element.68), kind=kLoop, calls=%fused_computation.2 | loop fusion | flops 1048576 | bytes 1572864 | tf_op jit(solution)/shard_map/convert_element_type | solution.py:477
  142.7 7.0 %collective-permute-done.29.refs_2_ = bf16[256,1024]{1,0:T(8,128)(2,1)} collective-permute-done((bf16[256,1024]{1,0:T(8,128)(2,1)}, bf16[256,1024]{1,0:T(8,128)(2,1)}, u32[]{:S(2)}, u32[]{:S(2)}) %collective-permute-start.29) | collective-permute-done | bytes 524320 | tf_op jit(solution)/shard_map/sums_2_2/ppermute | solution.py:101
  154.8 2.9 %join.5 = (bf16[272,1024]{1,0:T(8,128)(2,1)}, bf16[16,1024]{1,0:T(8,128)(2,1)}) custom-call(bf16[512,1024]{1,0:T(8,128)(2,1)} %get-tuple-element.70.refs_0_, bf16[512,1024]{1,0:T(8,128)(2,1)} %collective-permute-done.28.refs_1_, bf16[256,1024]{1,0:T(8,128)(2,1)} %collective-permute-done.29.refs_2_, bf16[272,1024]{1,0:T(8,128)(2,1)} %copy-done.11, ...), custom_call_target="tpu_custom_call" | custom-call | bytes 2621440 | tf_op jit(solution)/shard_map/join/pallas_call | solution.py:386
  157.9 4.0 %collective-permute-done.30 = bf16[256,1024]{1,0:T(8,128)(2,1)} collective-permute-done((bf16[256,1024]{1,0:T(8,128)(2,1)}, bf16[256,1024]{1,0:T(8,128)(2,1)}, u32[]{:S(2)}, u32[]{:S(2)}) %collective-permute-start.30) | collective-permute-done | bytes 524320 | tf_op jit(solution)/shard_map/sums_1_2/ppermute | solution.py:101
  163.2 1.6 add_convert_fusion
  164.9 4.2 %collective-permute-done.25.refs_3_ = bf16[512,512]{1,0:T(8,128)(2,1)S(1)} collective-permute-done((bf16[512,512]{1,0:T(8,128)(2,1)}, bf16[512,512]{1,0:T(8,128)(2,1)S(1)}, u32[]{:S(2)}, u32[]{:S(2)}) %collective-permute-start.25) | collective-permute-done | bytes 524320 | tf_op jit(solution)/shard_map/grads_3/ppermute | solution.py:101
  169.1 29.1 %collective-permute-done.34.refs_8_ = bf16[272,1024]{1,0:T(8,128)(2,1)S(1)} collective-permute-done((bf16[272,1024]{1,0:T(8,128)(2,1)}, bf16[272,1024]{1,0:T(8,128)(2,1)S(1)}, u32[]{:S(2)}, u32[]{:S(2)}) %collective-permute-start.34) | collective-permute-done | bytes 557088 | tf_op jit(solution)/shard_map/sums_2/ppermute | solution.py:101
  198.2 3.9 %finish.1 = (bf16[128,1024]{1,0:T(8,128)(2,1)}, f32[128,1024]{1,0:T(8,128)}, f32[256,2048]{1,0:T(8,128)}, f32[2048,256]{1,0:T(8,128)}, f32[2,1024]{1,0:T(2,128)}) custom-call(bf16[512,512]{1,0:T(8,128)(2,1)S(1)} %copy-done.2, bf16[512,512]{1,0:T(8,128)(2,1)S(1)} %collective-permute-done.21.refs_1_, bf16[512,512]{1,0:T(8,128)(2,1)S(1)} %collective-permute-done.22.refs_2_, ...), custom_call_target="tpu_custom_call" | custom-call | bytes 6291456 | tf_op jit(solution)/shard_map/finish/pallas_call | solution.py:346
  (116 shorter events, 21.8 us)
Async XLA Ops:
  3.4 15.1 %collective-permute-start.2 = (bf16[256,1024]{1,0:T(8,128)(2,1)}, bf16[256,1024]{1,0:T(8,128)(2,1)S(1)}, u32[]{:S(2)}, u32[]{:S(2)}) collective-permute-start(bf16[256,1024]{1,0:T(8,128)(2,1)} %get-tuple-element.42.refs_12_), channel_id=1, source_target_pairs={{0,8},{4,12},{8,0},{12,4},{1,9},{5,13},{9,1},{13,5},{2,10},{6,14},... | collective-permute-start | bytes 1572872 | tf_op jit(solution)/shard_map/tokens_0_2/ppermute | solution.py:101
  6.4 24.7 %collective-permute-start.1 = (bf16[256,1024]{1,0:T(8,128)(2,1)}, bf16[256,1024]{1,0:T(8,128)(2,1)S(1)}, u32[]{:S(2)}, u32[]{:S(2)}) collective-permute-start(bf16[256,1024]{1,0:T(8,128)(2,1)} %get-tuple-element.42.refs_12_), channel_id=1, source_target_pairs={{0,1},{1,0},{2,3},{3,2},{4,5},{5,4},{6,7},{7,6},{8,9},{9,8},{10,11... | collective-permute-start | bytes 1572872 | tf_op jit(solution)/shard_map/tokens_1/ppermute | solution.py:101
  8.0 25.5 %collective-permute-start = (bf16[256,1024]{1,0:T(8,128)(2,1)}, bf16[256,1024]{1,0:T(8,128)(2,1)S(1)}, u32[]{:S(2)}, u32[]{:S(2)}) collective-permute-start(bf16[256,1024]{1,0:T(8,128)(2,1)} %get-tuple-element.42.refs_12_), channel_id=1, source_target_pairs={{0,2},{1,3},{2,0},{3,1},{4,6},{5,7},{6,4},{7,5},{8,10},{9,11},{10,... | collective-permute-start | bytes 1572872 | tf_op jit(solution)/shard_map/tokens_2/ppermute | solution.py:101
  10.6 23.4 %collective-permute-start.3 = (bf16[256,1024]{1,0:T(8,128)(2,1)}, bf16[256,1024]{1,0:T(8,128)(2,1)S(1)}, u32[]{:S(2)}, u32[]{:S(2)}) collective-permute-start(bf16[256,1024]{1,0:T(8,128)(2,1)} %get-tuple-element.42.refs_12_), channel_id=1, source_target_pairs={{0,4},{4,0},{8,12},{12,8},{1,5},{5,1},{9,13},{13,9},{2,6},{6,2},{1... | collective-permute-start | bytes 1572872 | tf_op jit(solution)/shard_map/tokens_0_1/ppermute | solution.py:101
  18.5 15.5 %collective-permute-start.4 = (bf16[256,1024]{1,0:T(8,128)(2,1)S(1)}, bf16[256,1024]{1,0:T(8,128)(2,1)S(1)}, u32[]{:S(2)}, u32[]{:S(2)}) collective-permute-start(bf16[256,1024]{1,0:T(8,128)(2,1)S(1)} %collective-permute-done.2.refs_14_), channel_id=1, source_target_pairs={{0,4},{4,0},{8,12},{12,8},{1,5},{5,1},{9,13},{13,9},{2,6},{6,2},{1... | collective-permute-start | bytes 1572872 | tf_op jit(solution)/shard_map/tokens_0_3/ppermute | solution.py:101
  33.5 10.1 %collective-permute-start.10 = (bf16[256,1024]{1,0:T(8,128)(2,1)S(1)}, bf16[256,1024]{1,0:T(8,128)(2,1)S(1)}, u32[]{:S(2)}, u32[]{:S(2)}) collective-permute-start(bf16[256,1024]{1,0:T(8,128)(2,1)S(1)} %collective-permute-done.1.refs_8_), channel_id=1, source_target_pairs={{0,8},{4,12},{8,0},{12,4},{1,9},{5,13},{9,1},{13,5},{2,10},{6,14},... | collective-permute-start | bytes 1572872 | tf_op jit(solution)/shard_map/tokens_1_2/ppermute | solution.py:101
  34.0 18.4 %collective-permute-start.11 = (bf16[256,1024]{1,0:T(8,128)(2,1)S(1)}, bf16[256,1024]{1,0:T(8,128)(2,1)S(1)}, u32[]{:S(2)}, u32[]{:S(2)}) collective-permute-start(bf16[256,1024]{1,0:T(8,128)(2,1)S(1)} %collective-permute-done.1.refs_8_), channel_id=1, source_target_pairs={{0,4},{4,0},{8,12},{12,8},{1,5},{5,1},{9,13},{13,9},{2,6},{6,2},{1... | collective-permute-start | bytes 1572872 | tf_op jit(solution)/shard_map/tokens_1_1/ppermute | solution.py:101
  34.0 15.5 %collective-permute-start.6 = (bf16[128,1024]{1,0:T(8,128)(2,1)}, bf16[128,1024]{1,0:T(8,128)(2,1)S(1)}, u32[]{:S(2)}, u32[]{:S(2)}) collective-permute-start(bf16[128,1024]{1,0:T(8,128)(2,1)} %get-tuple-element.45), channel_id=1, source_target_pairs={{0,2},{1,3},{2,0},{3,1},{4,6},{5,7},{6,4},{7,5},{8,10},{9,11},{10,... | collective-permute-start | bytes 786440 | tf_op jit(solution)/shard_map/weights_2/ppermute | solution.py:101
  34.4 20.6 %collective-permute-start.5 = (bf16[256,1024]{1,0:T(8,128)(2,1)S(1)}, bf16[256,1024]{1,0:T(8,128)(2,1)S(1)}, u32[]{:S(2)}, u32[]{:S(2)}) collective-permute-start(bf16[256,1024]{1,0:T(8,128)(2,1)S(1)} %collective-permute-done.refs_4_), channel_id=1, source_target_pairs={{0,1},{1,0},{2,3},{3,2},{4,5},{5,4},{6,7},{7,6},{8,9},{9,8},{10,11... | collective-permute-start | bytes 1572872 | tf_op jit(solution)/shard_map/tokens_3/ppermute | solution.py:101
  43.6 11.4 %collective-permute-start.12 = (bf16[256,1024]{1,0:T(8,128)(2,1)S(1)}, bf16[256,1024]{1,0:T(8,128)(2,1)S(1)}, u32[]{:S(2)}, u32[]{:S(2)}) collective-permute-start(bf16[256,1024]{1,0:T(8,128)(2,1)S(1)} %collective-permute-done.10.refs_10_), channel_id=1, source_target_pairs={{0,4},{4,0},{8,12},{12,8},{1,5},{5,1},{9,13},{13,9},{2,6},{6,2},{1... | collective-permute-start | bytes 1572872 | tf_op jit(solution)/shard_map/tokens_1_3/ppermute | solution.py:101
  49.5 14.0 %collective-permute-start.16 = (bf16[256,1024]{1,0:T(8,128)(2,1)S(1)}, bf16[256,1024]{1,0:T(8,128)(2,1)S(1)}, u32[]{:S(2)}, u32[]{:S(2)}) collective-permute-start(bf16[256,1024]{1,0:T(8,128)(2,1)S(1)} %collective-permute-done.refs_4_), channel_id=1, source_target_pairs={{0,8},{4,12},{8,0},{12,4},{1,9},{5,13},{9,1},{13,5},{2,10},{6,14},... | collective-permute-start | bytes 1572872 | tf_op jit(solution)/shard_map/tokens_2_2/ppermute | solution.py:101
  51.0 10.1 %collective-permute-start.8 = (bf16[128,1024]{1,0:T(8,128)(2,1)}, bf16[128,1024]{1,0:T(8,128)(2,1)S(1)}, u32[]{:S(2)}, u32[]{:S(2)}) collective-permute-start(bf16[128,1024]{1,0:T(8,128)(2,1)} %get-tuple-element.47), channel_id=1, source_target_pairs={{0,3},{1,2},{2,1},{3,0},{4,7},{5,6},{6,5},{7,4},{8,11},{9,10},{10,... | collective-permute-start | bytes 786440 | tf_op jit(solution)/shard_map/weights_3/ppermute | solution.py:101
  52.4 8.7 %collective-permute-start.7 = (bf16[128,1024]{1,0:T(8,128)(2,1)S(1)}, bf16[128,1024]{1,0:T(8,128)(2,1)S(1)}, u32[]{:S(2)}, u32[]{:S(2)}) collective-permute-start(bf16[128,1024]{1,0:T(8,128)(2,1)S(1)} %collective-permute-done.6.refs_20_), channel_id=1, source_target_pairs={{0,16},{16,0},{1,17},{17,1},{2,18},{18,2},{3,19},{19,3},{4,20},{20... | collective-permute-start | bytes 786440 | tf_op jit(solution)/shard_map/weights_2/ppermute | solution.py:101
  61.1 8.0 %collective-permute-start.13 = (bf16[128,1024]{1,0:T(8,128)(2,1)}, bf16[128,1024]{1,0:T(8,128)(2,1)S(1)}, u32[]{:S(2)}, u32[]{:S(2)}) collective-permute-start(bf16[128,1024]{1,0:T(8,128)(2,1)} %get-tuple-element.50), channel_id=1, source_target_pairs={{0,1},{1,0},{2,3},{3,2},{4,5},{5,4},{6,7},{7,6},{8,9},{9,8},{10,11... | collective-permute-start | bytes 786440 | tf_op jit(solution)/shard_map/weights_1/ppermute | solution.py:101
  63.5 14.1 %collective-permute-start.17 = (bf16[256,1024]{1,0:T(8,128)(2,1)S(1)}, bf16[256,1024]{1,0:T(8,128)(2,1)S(1)}, u32[]{:S(2)}, u32[]{:S(2)}) collective-permute-start(bf16[256,1024]{1,0:T(8,128)(2,1)S(1)} %collective-permute-done.5.refs_0_), channel_id=1, source_target_pairs={{0,8},{4,12},{8,0},{12,4},{1,9},{5,13},{9,1},{13,5},{2,10},{6,14},... | collective-permute-start | bytes 1572872 | tf_op jit(solution)/shard_map/tokens_3_2/ppermute | solution.py:101
  64.9 9.0 %collective-permute-start.9 = (bf16[128,1024]{1,0:T(8,128)(2,1)S(1)}, bf16[128,1024]{1,0:T(8,128)(2,1)S(1)}, u32[]{:S(2)}, u32[]{:S(2)}) collective-permute-start(bf16[128,1024]{1,0:T(8,128)(2,1)S(1)} %collective-permute-done.8.refs_22_), channel_id=1, source_target_pairs={{0,16},{16,0},{1,17},{17,1},{2,18},{18,2},{3,19},{19,3},{4,20},{20... | collective-permute-start | bytes 786440 | tf_op jit(solution)/shard_map/weights_3/ppermute | solution.py:101
  69.1 8.5 %collective-permute-start.14 = (bf16[128,1024]{1,0:T(8,128)(2,1)S(1)}, bf16[128,1024]{1,0:T(8,128)(2,1)S(1)}, u32[]{:S(2)}, u32[]{:S(2)}) collective-permute-start(bf16[128,1024]{1,0:T(8,128)(2,1)S(1)} %collective-permute-done.13.refs_18_), channel_id=1, source_target_pairs={{0,16},{16,0},{1,17},{17,1},{2,18},{18,2},{3,19},{19,3},{4,20},{20... | collective-permute-start | bytes 786440 | tf_op jit(solution)/shard_map/weights_1/ppermute | solution.py:101
  70.6 7.6 %collective-permute-start.19 = (bf16[256,1024]{1,0:T(8,128)(2,1)S(1)}, bf16[256,1024]{1,0:T(8,128)(2,1)S(1)}, u32[]{:S(2)}, u32[]{:S(2)}) collective-permute-start(bf16[256,1024]{1,0:T(8,128)(2,1)S(1)} %collective-permute-done.refs_4_), channel_id=1, source_target_pairs={{0,4},{4,0},{8,12},{12,8},{1,5},{5,1},{9,13},{13,9},{2,6},{6,2},{1... | collective-permute-start | bytes 1572872 | tf_op jit(solution)/shard_map/tokens_2_1/ppermute | solution.py:101
  70.6 7.6 %collective-permute-start.20 = (bf16[256,1024]{1,0:T(8,128)(2,1)S(1)}, bf16[256,1024]{1,0:T(8,128)(2,1)S(1)}, u32[]{:S(2)}, u32[]{:S(2)}) collective-permute-start(bf16[256,1024]{1,0:T(8,128)(2,1)S(1)} %collective-permute-done.16.refs_6_), channel_id=1, source_target_pairs={{0,4},{4,0},{8,12},{12,8},{1,5},{5,1},{9,13},{13,9},{2,6},{6,2},{1... | collective-permute-start | bytes 1572872 | tf_op jit(solution)/shard_map/tokens_2_3/ppermute | solution.py:101
  105.8 6.9 %collective-permute-start.28 = (bf16[512,1024]{1,0:T(8,128)(2,1)}, bf16[512,1024]{1,0:T(8,128)(2,1)}, u32[]{:S(2)}, u32[]{:S(2)}) collective-permute-start(bf16[512,1024]{1,0:T(8,128)(2,1)} %get-tuple-element.71), channel_id=1, source_target_pairs={{0,4},{4,0},{8,12},{12,8},{1,5},{5,1},{9,13},{13,9},{2,6},{6,2},{1... | collective-permute-start | bytes 3145736 | tf_op jit(solution)/shard_map/sums_2_1/ppermute | solution.py:101
  106.2 34.4 %collective-permute-start.27 = (bf16[512,1024]{1,0:T(8,128)(2,1)}, bf16[512,1024]{1,0:T(8,128)(2,1)}, u32[]{:S(2)}, u32[]{:S(2)}) collective-permute-start(bf16[512,1024]{1,0:T(8,128)(2,1)} %get-tuple-element.69), channel_id=1, source_target_pairs={{0,4},{4,0},{8,12},{12,8},{1,5},{5,1},{9,13},{13,9},{2,6},{6,2},{1... | collective-permute-start | bytes 3145736 | tf_op jit(solution)/shard_map/sums_1_1/ppermute | solution.py:101
  112.0 24.6 %collective-permute-start.24 = (bf16[272,1024]{1,0:T(8,128)(2,1)}, bf16[272,1024]{1,0:T(8,128)(2,1)S(1)}, u32[]{:S(2)}, u32[]{:S(2)}) collective-permute-start(bf16[272,1024]{1,0:T(8,128)(2,1)} %get-tuple-element.62), channel_id=1, source_target_pairs={{0,8},{4,12},{8,0},{12,4},{1,9},{5,13},{9,1},{13,5},{2,10},{6,14},... | collective-permute-start | bytes 1671176 | tf_op jit(solution)/shard_map/sums_3_2/ppermute | solution.py:101
  112.5 24.1 %collective-permute-start.21 = (bf16[512,512]{1,0:T(8,128)(2,1)}, bf16[512,512]{1,0:T(8,128)(2,1)S(1)}, u32[]{:S(2)}, u32[]{:S(2)}) collective-permute-start(bf16[512,512]{1,0:T(8,128)(2,1)} %get-tuple-element.56), channel_id=1, source_target_pairs={{0,1},{1,0},{2,3},{3,2},{4,5},{5,4},{6,7},{7,6},{8,9},{9,8},{10,11... | collective-permute-start | bytes 1572872 | tf_op jit(solution)/shard_map/grads_1/ppermute | solution.py:101
  112.7 38.3 %collective-permute-start.26 = (bf16[512,1024]{1,0:T(8,128)(2,1)}, bf16[512,1024]{1,0:T(8,128)(2,1)S(1)}, u32[]{:S(2)}, u32[]{:S(2)}) collective-permute-start(bf16[512,1024]{1,0:T(8,128)(2,1)} %get-tuple-element.67), channel_id=1, source_target_pairs={{0,4},{4,0},{8,12},{12,8},{1,5},{5,1},{9,13},{13,9},{2,6},{6,2},{1... | collective-permute-start | bytes 3145736 | tf_op jit(solution)/shard_map/sums_0_1/ppermute | solution.py:101
  112.7 30.0 %collective-permute-start.22 = (bf16[512,512]{1,0:T(8,128)(2,1)}, bf16[512,512]{1,0:T(8,128)(2,1)S(1)}, u32[]{:S(2)}, u32[]{:S(2)}) collective-permute-start(bf16[512,512]{1,0:T(8,128)(2,1)} %get-tuple-element.57), channel_id=1, source_target_pairs={{0,2},{1,3},{2,0},{3,1},{4,6},{5,7},{6,4},{7,5},{8,10},{9,11},{10,... | collective-permute-start | bytes 1572872 | tf_op jit(solution)/shard_map/grads_2/ppermute | solution.py:101
  136.6 13.1 %collective-permute-start.29 = (bf16[256,1024]{1,0:T(8,128)(2,1)}, bf16[256,1024]{1,0:T(8,128)(2,1)}, u32[]{:S(2)}, u32[]{:S(2)}) collective-permute-start(bf16[256,1024]{1,0:T(8,128)(2,1)} %add_convert_fusion.1), channel_id=1, source_target_pairs={{0,8},{4,12},{8,0},{12,4},{1,9},{5,13},{9,1},{13,5},{2,10},{6,14},... | collective-permute-start | bytes 1572872 | tf_op jit(solution)/shard_map/sums_2_2/ppermute | solution.py:101
  140.5 13.4 %collective-permute-start.32 = (bf16[272,1024]{1,0:T(8,128)(2,1)}, bf16[272,1024]{1,0:T(8,128)(2,1)S(1)}, u32[]{:S(2)}, u32[]{:S(2)}) collective-permute-start(bf16[272,1024]{1,0:T(8,128)(2,1)} %get-tuple-element.64), channel_id=1, source_target_pairs={{0,1},{1,0},{2,3},{3,2},{4,5},{5,4},{6,7},{7,6},{8,9},{9,8},{10,11... | collective-permute-start | bytes 1671176 | tf_op jit(solution)/shard_map/sums_3/ppermute | solution.py:101
  149.7 12.2 %collective-permute-start.30 = (bf16[256,1024]{1,0:T(8,128)(2,1)}, bf16[256,1024]{1,0:T(8,128)(2,1)}, u32[]{:S(2)}, u32[]{:S(2)}) collective-permute-start(bf16[256,1024]{1,0:T(8,128)(2,1)} %add_convert_fusion.2), channel_id=1, source_target_pairs={{0,8},{4,12},{8,0},{12,4},{1,9},{5,13},{9,1},{13,5},{2,10},{6,14},... | collective-permute-start | bytes 1572872 | tf_op jit(solution)/shard_map/sums_1_2/ppermute | solution.py:101
  152.1 16.9 %collective-permute-start.25 = (bf16[512,512]{1,0:T(8,128)(2,1)}, bf16[512,512]{1,0:T(8,128)(2,1)S(1)}, u32[]{:S(2)}, u32[]{:S(2)}) collective-permute-start(bf16[512,512]{1,0:T(8,128)(2,1)} %get-tuple-element.65), channel_id=1, source_target_pairs={{0,3},{1,2},{2,1},{3,0},{4,7},{5,6},{6,5},{7,4},{8,11},{9,10},{10,... | collective-permute-start | bytes 1572872 | tf_op jit(solution)/shard_map/grads_3/ppermute | solution.py:101
  157.7 40.4 %collective-permute-start.34 = (bf16[272,1024]{1,0:T(8,128)(2,1)}, bf16[272,1024]{1,0:T(8,128)(2,1)S(1)}, u32[]{:S(2)}, u32[]{:S(2)}) collective-permute-start(bf16[272,1024]{1,0:T(8,128)(2,1)} %get-tuple-element.76), channel_id=1, source_target_pairs={{0,2},{1,3},{2,0},{3,1},{4,6},{5,7},{6,4},{7,5},{8,10},{9,11},{10,... | collective-permute-start | bytes 1671176 | tf_op jit(solution)/shard_map/sums_2/ppermute | solution.py:101
  161.9 36.2 %collective-permute-start.31 = (bf16[256,1024]{1,0:T(8,128)(2,1)}, bf16[256,1024]{1,0:T(8,128)(2,1)S(1)}, u32[]{:S(2)}, u32[]{:S(2)}) collective-permute-start(bf16[256,1024]{1,0:T(8,128)(2,1)} %add_convert_fusion.3), channel_id=1, source_target_pairs={{0,8},{4,12},{8,0},{12,4},{1,9},{5,13},{9,1},{13,5},{2,10},{6,14},... | collective-permute-start | bytes 1572872 | tf_op jit(solution)/shard_map/sums_0_2/ppermute | solution.py:101
  164.8 33.3 %collective-permute-start.33 = (bf16[256,1024]{1,0:T(8,128)(2,1)S(1)}, bf16[256,1024]{1,0:T(8,128)(2,1)S(1)}, u32[]{:S(2)}, u32[]{:S(2)}) collective-permute-start(bf16[256,1024]{1,0:T(8,128)(2,1)S(1)} %add_convert_fusion), channel_id=1, source_target_pairs={{0,1},{1,0},{2,3},{3,2},{4,5},{5,4},{6,7},{7,6},{8,9},{9,8},{10,11... | collective-permute-start | bytes 1572872 | tf_op jit(solution)/shard_map/sums_1/ppermute | solution.py:101
  (37 other events, 791.9 us)

commit v12 on v11

--- a/solution.py
+++ b/solution.py
@@ -466,11 +466,8 @@
     blocks = dict(enumerate(blocks))
     blocks[top] = swap(blocks[top], "dp", top, f"grads_{top}")
 
-    for k in range(1, top):
-        blocks[k] = swap(blocks[k], "dp", k, f"grads_{k}")
-    third = {}
     for k in range(top + 1, n_dp):
-        third[k] = blocks[k]
+        blocks[k] = swap(after(blocks[k], blocks[top]), "dp", k, f"grads_{k}")
 
     def add(terms):
         spans = (x[place * span : (place + 1) * span].astype(jnp.float32) for x, place in terms)
@@ -488,13 +485,16 @@
                     send, stats = join(span, parts.pop(j), [(stats, 0), waiting])
                 else:
                     send = add(parts.pop(j))
-                if behind and k:
-                    behind += (blocks[1 if k == top else top],)
+                if k < top:
+                    behind += (blocks[n_dp - 1 if k == 0 else top],)
                 came = swap(after(send, *behind), "tensor", bit, f"sums_{k}_{j}")
                 if k == order[0] and j == bit:
                     waiting = (came, span // EXTRA)
                 parts[j ^ bit].append((came, 0))
                 behind = (came,)
+                if k == top:
+                    for i in range(1, top):
+                        blocks[i] = swap(after(blocks[i], came), "dp", i, f"grads_{i}")
         sums[k] = parts[0]
     came = {}
     for bit in bits_of(n_dp)[::-1]:
@@ -504,9 +504,6 @@
             else:
                 send = add(sums.pop(k))
             came[k] = swap(send, "dp", bit, f"sums_{k}")
-            for j in third:
-                blocks[j] = swap(after(third[j], blocks[top], send), "dp", j, f"grads_{j}")
-            third = {}
             if k == (n_dp - 1) & -bit:
                 waiting = (came[k], span // EXTRA)
             sums[k ^ bit].append((came[k], 0))

time: 202 us -> 205 us (1.015)
  starting transfers between devices: 32.3 us -> 35.6 us
    ppermute x35, starting transfers between devices: 32.3 us -> 35.6 us  [swap(): lax.ppermute(values, axis, [(i, i ^ mask) for i in range(lax.axis_size(ax...]
  transfers between devices with their start and end apart: 35 -> 35, of which waited for: 19 -> 19; matrix products, arithmetic and copies ran while one was open for 3% -> 4% of each run, Pallas kernels for 4% -> 4%
where the time goes in v12:
time: 205 us; the launch traced here: 204 us
  waiting for transfers between devices  118 us (58%)
  Pallas kernels  39.1 us (19%)
  starting transfers between devices  35.6 us (17%)
  other arithmetic  7.87 us (4%)
  local copies, waits for them, and re-layouts  2.54 us (1%)
    ppermute x35, waiting for transfers between devices, swap(): lax.ppermute(values, axis, [(i, i ^ mask) for i in range(lax.axis_size(ax...  118 us
    ppermute x35, starting transfers between devices, swap(): lax.ppermute(values, axis, [(i, i ^ mask) for i in range(lax.axis_size(ax...  35.6 us
    pallas_call x1, Pallas kernels, core(): pl.pallas_call(kernel, out_shape=[jax.ShapeDtypeStruct((half[0] + (EXTRA...  24.5 us
    pallas_call x3, Pallas kernels, join(): pl.pallas_call(kernel, out_shape=out_shape, grid=(1,), in_specs=[spec(row...  7.95 us
    convert_element_type x4, other arithmetic, add(): return sum(spans).astype(jnp.bfloat16)  7.87 us
  transfers between devices with their start and end apart: 35, of which 19 were waited for; matrix products, arithmetic and copies ran while one was open for 4% of the time, Pallas kernels for 4%

profile of v12, /device:TPU:0, one launch (start us, length us, event | category | flops | bytes accessed | tf_op | source)
XLA Modules:
  0.0 204.4 jit_solution(9260370589063105556)
XLA Ops:
  0.6 2.8 %pack.1 = (bf16[256,1024]{1,0:T(8,128)(2,1)}, bf16[128,1024]{1,0:T(8,128)(2,1)}, bf16[128,1024]{1,0:T(8,128)(2,1)}, bf16[128,1024]{1,0:T(8,128)(2,1)}) custom-call(bf16[128,1024]{1,0:T(8,128)(2,1)} %refs_10_.1, bf16[128,1024]{1,0:T(8,128)(2,1)} %grad_ref.1, bf16[256,2048]{1,0:T(8,128)(2,1)} %refs_16_.1, bf16[2048,256]{1,0:T(8,128)(2,1)} %refs_17_.1), custom_call_target="tpu_custom_call" | custom-call | bytes 4194304 | tf_op jit(solution)/shard_map/pack/pallas_call | solution.py:125
  3.4 3.0 %collective-permute-start.2 = (bf16[256,1024]{1,0:T(8,128)(2,1)}, bf16[256,1024]{1,0:T(8,128)(2,1)S(1)}, u32[]{:S(2)}, u32[]{:S(2)}) collective-permute-start(bf16[256,1024]{1,0:T(8,128)(2,1)} %get-tuple-element.43.refs_12_), channel_id=1, source_target_pairs={{0,8},{4,12},{8,0},{12,4},{1,9},{5,13},{9,1},{13,5},{2,10},{6,14},... | collective-permute-start | bytes 1572872 | tf_op jit(solution)/shard_map/tokens_0_2/ppermute | solution.py:101
  8.0 2.6 %collective-permute-start = (bf16[256,1024]{1,0:T(8,128)(2,1)}, bf16[256,1024]{1,0:T(8,128)(2,1)S(1)}, u32[]{:S(2)}, u32[]{:S(2)}) collective-permute-start(bf16[256,1024]{1,0:T(8,128)(2,1)} %get-tuple-element.43.refs_12_), channel_id=1, source_target_pairs={{0,2},{1,3},{2,0},{3,1},{4,6},{5,7},{6,4},{7,5},{8,10},{9,11},{10,... | collective-permute-start | bytes 1572872 | tf_op jit(solution)/shard_map/tokens_2/ppermute | solution.py:101
  10.6 8.0 %collective-permute-done.2.refs_14_ = bf16[256,1024]{1,0:T(8,128)(2,1)S(1)} collective-permute-done((bf16[256,1024]{1,0:T(8,128)(2,1)}, bf16[256,1024]{1,0:T(8,128)(2,1)S(1)}, u32[]{:S(2)}, u32[]{:S(2)}) %collective-permute-start.2) | collective-permute-done | bytes 524320 | tf_op jit(solution)/shard_map/tokens_0_2/ppermute | solution.py:101
  18.5 12.6 %collective-permute-done.1.refs_8_ = bf16[256,1024]{1,0:T(8,128)(2,1)S(1)} collective-permute-done((bf16[256,1024]{1,0:T(8,128)(2,1)}, bf16[256,1024]{1,0:T(8,128)(2,1)S(1)}, u32[]{:S(2)}, u32[]{:S(2)}) %collective-permute-start.1) | collective-permute-done | bytes 524320 | tf_op jit(solution)/shard_map/tokens_1/ppermute | solution.py:101
  31.1 2.4 %collective-permute-done.refs_4_ = bf16[256,1024]{1,0:T(8,128)(2,1)S(1)} collective-permute-done((bf16[256,1024]{1,0:T(8,128)(2,1)}, bf16[256,1024]{1,0:T(8,128)(2,1)S(1)}, u32[]{:S(2)}, u32[]{:S(2)}) %collective-permute-start) | collective-permute-done | bytes 524320 | tf_op jit(solution)/shard_map/tokens_2/ppermute | solution.py:101
  34.4 2.7 %collective-permute-start.5 = (bf16[256,1024]{1,0:T(8,128)(2,1)S(1)}, bf16[256,1024]{1,0:T(8,128)(2,1)S(1)}, u32[]{:S(2)}, u32[]{:S(2)}) collective-permute-start(bf16[256,1024]{1,0:T(8,128)(2,1)S(1)} %collective-permute-done.refs_4_), channel_id=1, source_target_pairs={{0,1},{1,0},{2,3},{3,2},{4,5},{5,4},{6,7},{7,6},{8,9},{9,8},{10,11... | collective-permute-start | bytes 1572872 | tf_op jit(solution)/shard_map/tokens_3/ppermute | solution.py:101
  37.1 6.5 %collective-permute-done.10.refs_10_ = bf16[256,1024]{1,0:T(8,128)(2,1)S(1)} collective-permute-done((bf16[256,1024]{1,0:T(8,128)(2,1)S(1)}, bf16[256,1024]{1,0:T(8,128)(2,1)S(1)}, u32[]{:S(2)}, u32[]{:S(2)}) %collective-permute-start.10) | collective-permute-done | bytes 524320 | tf_op jit(solution)/shard_map/tokens_1_2/ppermute | solution.py:101
  43.6 5.9 %collective-permute-done.6.refs_20_ = bf16[128,1024]{1,0:T(8,128)(2,1)S(1)} collective-permute-done((bf16[128,1024]{1,0:T(8,128)(2,1)}, bf16[128,1024]{1,0:T(8,128)(2,1)S(1)}, u32[]{:S(2)}, u32[]{:S(2)}) %collective-permute-start.6) | collective-permute-done | bytes 262176 | tf_op jit(solution)/shard_map/weights_2/ppermute | solution.py:101
  55.0 6.0 %collective-permute-done.8.refs_22_ = bf16[128,1024]{1,0:T(8,128)(2,1)S(1)} collective-permute-done((bf16[128,1024]{1,0:T(8,128)(2,1)}, bf16[128,1024]{1,0:T(8,128)(2,1)S(1)}, u32[]{:S(2)}, u32[]{:S(2)}) %collective-permute-start.8) | collective-permute-done | bytes 262176 | tf_op jit(solution)/shard_map/weights_3/ppermute | solution.py:101
  61.1 2.4 %collective-permute-start.13 = (bf16[128,1024]{1,0:T(8,128)(2,1)}, bf16[128,1024]{1,0:T(8,128)(2,1)S(1)}, u32[]{:S(2)}, u32[]{:S(2)}) collective-permute-start(bf16[128,1024]{1,0:T(8,128)(2,1)} %get-tuple-element.51), channel_id=1, source_target_pairs={{0,1},{1,0},{2,3},{3,2},{4,5},{5,4},{6,7},{7,6},{8,9},{9,8},{10,11... | collective-permute-start | bytes 786440 | tf_op jit(solution)/shard_map/weights_1/ppermute | solution.py:101
  66.4 2.7 %collective-permute-done.13.refs_18_ = bf16[128,1024]{1,0:T(8,128)(2,1)S(1)} collective-permute-done((bf16[128,1024]{1,0:T(8,128)(2,1)}, bf16[128,1024]{1,0:T(8,128)(2,1)S(1)}, u32[]{:S(2)}, u32[]{:S(2)}) %collective-permute-start.13) | collective-permute-done | bytes 262176 | tf_op jit(solution)/shard_map/weights_1/ppermute | solution.py:101
  71.1 2.8 %collective-permute-done.9.refs_23_ = bf16[128,1024]{1,0:T(8,128)(2,1)S(1)} collective-permute-done((bf16[128,1024]{1,0:T(8,128)(2,1)S(1)}, bf16[128,1024]{1,0:T(8,128)(2,1)S(1)}, u32[]{:S(2)}, u32[]{:S(2)}) %collective-permute-start.9) | collective-permute-done | bytes 262176 | tf_op jit(solution)/shard_map/weights_3/ppermute | solution.py:101
  73.9 3.7 %collective-permute-done.14.refs_19_ = bf16[128,1024]{1,0:T(8,128)(2,1)S(1)} collective-permute-done((bf16[128,1024]{1,0:T(8,128)(2,1)S(1)}, bf16[128,1024]{1,0:T(8,128)(2,1)S(1)}, u32[]{:S(2)}, u32[]{:S(2)}) %collective-permute-start.14) | collective-permute-done | bytes 262176 | tf_op jit(solution)/shard_map/weights_1/ppermute | solution.py:101
  81.0 24.5 %core.1 = (bf16[512,1024]{1,0:T(8,128)(2,1)}, bf16[528,1024]{1,0:T(8,128)(2,1)}, bf16[512,1024]{1,0:T(8,128)(2,1)}, bf16[512,1024]{1,0:T(8,128)(2,1)}, bf16[512,...) custom-call(bf16[256,1024]{1,0:T(8,128)(2,1)} %copy-done.20, ...), custom_call_target="tpu_custom_call" | custom-call | flops 10737418240 | bytes 20971520 | tf_op jit(solution)/shard_map/core/pallas_call | solution.py:252
  106.2 2.4 %collective-permute-done.22.refs_1_.refs_3_ = bf16[528,1024]{1,0:T(8,128)(2,1)S(1)} collective-permute-done((bf16[528,1024]{1,0:T(8,128)(2,1)}, bf16[528,1024]{1,0:T(8,128)(2,1)S(1)}, u32[]{:S(2)}, u32[]{:S(2)}) %collective-permute-start.22) | collective-permute-done | bytes 1081376 | tf_op jit(solution)/shard_map/sums_3_1/ppermute | solution.py:101
  109.6 2.3 %join.3 = (bf16[272,1024]{1,0:T(8,128)(2,1)}, bf16[16,1024]{1,0:T(8,128)(2,1)}) custom-call(bf16[512,1024]{1,0:T(8,128)(2,1)} %get-tuple-element.60.refs_0_, bf16[528,1024]{1,0:T(8,128)(2,1)} %copy-done.8, bf16[16,1024]{1,0:T(8,128)(2,1)} %get-tuple-element.62.refs_2_, bf16[528,1024]{1,0:T(8,128)(2,1)} %copy-done.8), custom_call_target="tpu_custom_call" | custom-call | bytes 1572864 | tf_op jit(solution)/shard_map/join/pallas_call | solution.py:386
  113.7 2.0 add_convert_fusion.3
  115.8 11.1 %collective-permute-done.23.refs_2_.refs_4_ = bf16[272,1024]{1,0:T(8,128)(2,1)S(1)} collective-permute-done((bf16[272,1024]{1,0:T(8,128)(2,1)}, bf16[272,1024]{1,0:T(8,128)(2,1)S(1)}, u32[]{:S(2)}, u32[]{:S(2)}) %collective-permute-start.23) | collective-permute-done | bytes 557088 | tf_op jit(solution)/shard_map/sums_3_2/ppermute | solution.py:101
  127.3 10.8 %collective-permute-done.26.refs_2_ = bf16[512,512]{1,0:T(8,128)(2,1)S(1)} collective-permute-done((bf16[512,512]{1,0:T(8,128)(2,1)}, bf16[512,512]{1,0:T(8,128)(2,1)S(1)}, u32[]{:S(2)}, u32[]{:S(2)}) %collective-permute-start.26) | collective-permute-done | bytes 524320 | tf_op jit(solution)/shard_map/grads_2/ppermute | solution.py:101
  138.2 2.5 %collective-permute-start.27 = (bf16[512,512]{1,0:T(8,128)(2,1)}, bf16[512,512]{1,0:T(8,128)(2,1)S(1)}, u32[]{:S(2)}, u32[]{:S(2)}) collective-permute-start(bf16[512,512]{1,0:T(8,128)(2,1)} %get-tuple-element.68), channel_id=1, source_target_pairs={{0,3},{1,2},{2,1},{3,0},{4,7},{5,6},{6,5},{7,4},{8,11},{9,10},{10,... | collective-permute-start | bytes 1572872 | tf_op jit(solution)/shard_map/grads_3/ppermute | solution.py:101
  140.7 2.7 %join.4 = (bf16[272,1024]{1,0:T(8,128)(2,1)}, bf16[16,1024]{1,0:T(8,128)(2,1)}) custom-call(bf16[512,1024]{1,0:T(8,128)(2,1)} %get-tuple-element.60.refs_0_, bf16[528,1024]{1,0:T(8,128)(2,1)} %copy-done.8, bf16[272,1024]{1,0:T(8,128)(2,1)} %copy-done.10, bf16[16,1024]{1,0:T(8,128)(2,1)} %get-tuple-element.75.refs_3_, bf16[272,1024]{1,0:T(8,128)(2,1)} %copy-done.10), custom_call_target="tpu_custom_call" | custom-call | bytes 2097152 | tf_op jit(solution)/shard_map/join/pallas_call | solution.py:386
  143.4 2.2 %add_convert_fusion.1 = bf16[256,1024]{1,0:T(8,128)(2,1)} fusion(bf16[512,1024]{1,0:T(8,128)(2,1)} %collective-permute-done.29, bf16[512,1024]{1,0:T(8,128)(2,1)} %get-tuple-element.71), kind=kLoop, calls=%fused_computation.1 | loop fusion | flops 1048576 | bytes 1572864 | tf_op jit(solution)/shard_map/convert_element_type | solution.py:474
  146.6 2.0 add_convert_fusion.2
  148.6 2.0 collective-permute-start.25
  150.6 15.5 %collective-permute-done.32.refs_3_.refs_5_ = bf16[272,1024]{1,0:T(8,128)(2,1)S(1)} collective-permute-done((bf16[272,1024]{1,0:T(8,128)(2,1)}, bf16[272,1024]{1,0:T(8,128)(2,1)S(1)}, u32[]{:S(2)}, u32[]{:S(2)}) %collective-permute-start.32) | collective-permute-done | bytes 557088 | tf_op jit(solution)/shard_map/sums_3/ppermute | solution.py:101
  167.0 2.9 %join.5 = (bf16[272,1024]{1,0:T(8,128)(2,1)}, bf16[16,1024]{1,0:T(8,128)(2,1)}) custom-call(bf16[512,1024]{1,0:T(8,128)(2,1)} %get-tuple-element.58.refs_0_, bf16[512,1024]{1,0:T(8,128)(2,1)} %collective-permute-done.21.refs_1_, bf16[256,1024]{1,0:T(8,128)(2,1)} %copy-done.12, bf16[272,1024]{1,0:T(8,128)(2,1)} %copy-done.11, ...), custom_call_target="tpu_custom_call" | custom-call | bytes 2621440 | tf_op jit(solution)/shard_map/join/pallas_call | solution.py:386
  173.9 1.8 collective-permute-start.33
  175.7 5.4 %collective-permute-done.25.refs_1_ = bf16[512,512]{1,0:T(8,128)(2,1)S(1)} collective-permute-done((bf16[512,512]{1,0:T(8,128)(2,1)}, bf16[512,512]{1,0:T(8,128)(2,1)S(1)}, u32[]{:S(2)}, u32[]{:S(2)}) %collective-permute-start.25) | collective-permute-done | bytes 524320 | tf_op jit(solution)/shard_map/grads_1/ppermute | solution.py:101
  181.1 16.5 %collective-permute-done.34.refs_8_ = bf16[272,1024]{1,0:T(8,128)(2,1)S(1)} collective-permute-done((bf16[272,1024]{1,0:T(8,128)(2,1)}, bf16[272,1024]{1,0:T(8,128)(2,1)S(1)}, u32[]{:S(2)}, u32[]{:S(2)}) %collective-permute-start.34) | collective-permute-done | bytes 557088 | tf_op jit(solution)/shard_map/sums_2/ppermute | solution.py:101
  197.6 2.8 %collective-permute-done.33.refs_7_ = bf16[256,1024]{1,0:T(8,128)(2,1)S(1)} collective-permute-done((bf16[256,1024]{1,0:T(8,128)(2,1)S(1)}, bf16[256,1024]{1,0:T(8,128)(2,1)S(1)}, u32[]{:S(2)}, u32[]{:S(2)}) %collective-permute-start.33) | collective-permute-done | bytes 524320 | tf_op jit(solution)/shard_map/sums_1/ppermute | solution.py:101
  200.5 3.9 %finish.1 = (bf16[128,1024]{1,0:T(8,128)(2,1)}, f32[128,1024]{1,0:T(8,128)}, f32[256,2048]{1,0:T(8,128)}, f32[2048,256]{1,0:T(8,128)}, f32[2,1024]{1,0:T(2,128)}) custom-call(bf16[512,512]{1,0:T(8,128)(2,1)S(1)} %copy-done.2, bf16[512,512]{1,0:T(8,128)(2,1)S(1)} %collective-permute-done.25.refs_1_, bf16[512,512]{1,0:T(8,128)(2,1)S(1)} %collective-permute-done.26.refs_2_, ...), custom_call_target="tpu_custom_call" | custom-call | bytes 6291456 | tf_op jit(solution)/shard_map/finish/pallas_call | solution.py:346
  (116 shorter events, 26.1 us)
Async XLA Ops:
  3.4 15.1 %collective-permute-start.2 = (bf16[256,1024]{1,0:T(8,128)(2,1)}, bf16[256,1024]{1,0:T(8,128)(2,1)S(1)}, u32[]{:S(2)}, u32[]{:S(2)}) collective-permute-start(bf16[256,1024]{1,0:T(8,128)(2,1)} %get-tuple-element.43.refs_12_), channel_id=1, source_target_pairs={{0,8},{4,12},{8,0},{12,4},{1,9},{5,13},{9,1},{13,5},{2,10},{6,14},... | collective-permute-start | bytes 1572872 | tf_op jit(solution)/shard_map/tokens_0_2/ppermute | solution.py:101
  6.4 24.7 %collective-permute-start.1 = (bf16[256,1024]{1,0:T(8,128)(2,1)}, bf16[256,1024]{1,0:T(8,128)(2,1)S(1)}, u32[]{:S(2)}, u32[]{:S(2)}) collective-permute-start(bf16[256,1024]{1,0:T(8,128)(2,1)} %get-tuple-element.43.refs_12_), channel_id=1, source_target_pairs={{0,1},{1,0},{2,3},{3,2},{4,5},{5,4},{6,7},{7,6},{8,9},{9,8},{10,11... | collective-permute-start | bytes 1572872 | tf_op jit(solution)/shard_map/tokens_1/ppermute | solution.py:101
  8.0 25.5 %collective-permute-start = (bf16[256,1024]{1,0:T(8,128)(2,1)}, bf16[256,1024]{1,0:T(8,128)(2,1)S(1)}, u32[]{:S(2)}, u32[]{:S(2)}) collective-permute-start(bf16[256,1024]{1,0:T(8,128)(2,1)} %get-tuple-element.43.refs_12_), channel_id=1, source_target_pairs={{0,2},{1,3},{2,0},{3,1},{4,6},{5,7},{6,4},{7,5},{8,10},{9,11},{10,... | collective-permute-start | bytes 1572872 | tf_op jit(solution)/shard_map/tokens_2/ppermute | solution.py:101
  10.6 23.4 %collective-permute-start.3 = (bf16[256,1024]{1,0:T(8,128)(2,1)}, bf16[256,1024]{1,0:T(8,128)(2,1)S(1)}, u32[]{:S(2)}, u32[]{:S(2)}) collective-permute-start(bf16[256,1024]{1,0:T(8,128)(2,1)} %get-tuple-element.43.refs_12_), channel_id=1, source_target_pairs={{0,4},{4,0},{8,12},{12,8},{1,5},{5,1},{9,13},{13,9},{2,6},{6,2},{1... | collective-permute-start | bytes 1572872 | tf_op jit(solution)/shard_map/tokens_0_1/ppermute | solution.py:101
  18.5 15.5 %collective-permute-start.4 = (bf16[256,1024]{1,0:T(8,128)(2,1)S(1)}, bf16[256,1024]{1,0:T(8,128)(2,1)S(1)}, u32[]{:S(2)}, u32[]{:S(2)}) collective-permute-start(bf16[256,1024]{1,0:T(8,128)(2,1)S(1)} %collective-permute-done.2.refs_14_), channel_id=1, source_target_pairs={{0,4},{4,0},{8,12},{12,8},{1,5},{5,1},{9,13},{13,9},{2,6},{6,2},{1... | collective-permute-start | bytes 1572872 | tf_op jit(solution)/shard_map/tokens_0_3/ppermute | solution.py:101
  33.5 10.1 %collective-permute-start.10 = (bf16[256,1024]{1,0:T(8,128)(2,1)S(1)}, bf16[256,1024]{1,0:T(8,128)(2,1)S(1)}, u32[]{:S(2)}, u32[]{:S(2)}) collective-permute-start(bf16[256,1024]{1,0:T(8,128)(2,1)S(1)} %collective-permute-done.1.refs_8_), channel_id=1, source_target_pairs={{0,8},{4,12},{8,0},{12,4},{1,9},{5,13},{9,1},{13,5},{2,10},{6,14},... | collective-permute-start | bytes 1572872 | tf_op jit(solution)/shard_map/tokens_1_2/ppermute | solution.py:101
  34.0 18.4 %collective-permute-start.11 = (bf16[256,1024]{1,0:T(8,128)(2,1)S(1)}, bf16[256,1024]{1,0:T(8,128)(2,1)S(1)}, u32[]{:S(2)}, u32[]{:S(2)}) collective-permute-start(bf16[256,1024]{1,0:T(8,128)(2,1)S(1)} %collective-permute-done.1.refs_8_), channel_id=1, source_target_pairs={{0,4},{4,0},{8,12},{12,8},{1,5},{5,1},{9,13},{13,9},{2,6},{6,2},{1... | collective-permute-start | bytes 1572872 | tf_op jit(solution)/shard_map/tokens_1_1/ppermute | solution.py:101
  34.0 15.5 %collective-permute-start.6 = (bf16[128,1024]{1,0:T(8,128)(2,1)}, bf16[128,1024]{1,0:T(8,128)(2,1)S(1)}, u32[]{:S(2)}, u32[]{:S(2)}) collective-permute-start(bf16[128,1024]{1,0:T(8,128)(2,1)} %get-tuple-element.46), channel_id=1, source_target_pairs={{0,2},{1,3},{2,0},{3,1},{4,6},{5,7},{6,4},{7,5},{8,10},{9,11},{10,... | collective-permute-start | bytes 786440 | tf_op jit(solution)/shard_map/weights_2/ppermute | solution.py:101
  34.4 20.6 %collective-permute-start.5 = (bf16[256,1024]{1,0:T(8,128)(2,1)S(1)}, bf16[256,1024]{1,0:T(8,128)(2,1)S(1)}, u32[]{:S(2)}, u32[]{:S(2)}) collective-permute-start(bf16[256,1024]{1,0:T(8,128)(2,1)S(1)} %collective-permute-done.refs_4_), channel_id=1, source_target_pairs={{0,1},{1,0},{2,3},{3,2},{4,5},{5,4},{6,7},{7,6},{8,9},{9,8},{10,11... | collective-permute-start | bytes 1572872 | tf_op jit(solution)/shard_map/tokens_3/ppermute | solution.py:101
  43.6 11.4 %collective-permute-start.12 = (bf16[256,1024]{1,0:T(8,128)(2,1)S(1)}, bf16[256,1024]{1,0:T(8,128)(2,1)S(1)}, u32[]{:S(2)}, u32[]{:S(2)}) collective-permute-start(bf16[256,1024]{1,0:T(8,128)(2,1)S(1)} %collective-permute-done.10.refs_10_), channel_id=1, source_target_pairs={{0,4},{4,0},{8,12},{12,8},{1,5},{5,1},{9,13},{13,9},{2,6},{6,2},{1... | collective-permute-start | bytes 1572872 | tf_op jit(solution)/shard_map/tokens_1_3/ppermute | solution.py:101
  49.5 14.0 %collective-permute-start.16 = (bf16[256,1024]{1,0:T(8,128)(2,1)S(1)}, bf16[256,1024]{1,0:T(8,128)(2,1)S(1)}, u32[]{:S(2)}, u32[]{:S(2)}) collective-permute-start(bf16[256,1024]{1,0:T(8,128)(2,1)S(1)} %collective-permute-done.refs_4_), channel_id=1, source_target_pairs={{0,8},{4,12},{8,0},{12,4},{1,9},{5,13},{9,1},{13,5},{2,10},{6,14},... | collective-permute-start | bytes 1572872 | tf_op jit(solution)/shard_map/tokens_2_2/ppermute | solution.py:101
  51.0 10.1 %collective-permute-start.8 = (bf16[128,1024]{1,0:T(8,128)(2,1)}, bf16[128,1024]{1,0:T(8,128)(2,1)S(1)}, u32[]{:S(2)}, u32[]{:S(2)}) collective-permute-start(bf16[128,1024]{1,0:T(8,128)(2,1)} %get-tuple-element.48), channel_id=1, source_target_pairs={{0,3},{1,2},{2,1},{3,0},{4,7},{5,6},{6,5},{7,4},{8,11},{9,10},{10,... | collective-permute-start | bytes 786440 | tf_op jit(solution)/shard_map/weights_3/ppermute | solution.py:101
  52.4 8.7 %collective-permute-start.7 = (bf16[128,1024]{1,0:T(8,128)(2,1)S(1)}, bf16[128,1024]{1,0:T(8,128)(2,1)S(1)}, u32[]{:S(2)}, u32[]{:S(2)}) collective-permute-start(bf16[128,1024]{1,0:T(8,128)(2,1)S(1)} %collective-permute-done.6.refs_20_), channel_id=1, source_target_pairs={{0,16},{16,0},{1,17},{17,1},{2,18},{18,2},{3,19},{19,3},{4,20},{20... | collective-permute-start | bytes 786440 | tf_op jit(solution)/shard_map/weights_2/ppermute | solution.py:101
  61.1 8.0 %collective-permute-start.13 = (bf16[128,1024]{1,0:T(8,128)(2,1)}, bf16[128,1024]{1,0:T(8,128)(2,1)S(1)}, u32[]{:S(2)}, u32[]{:S(2)}) collective-permute-start(bf16[128,1024]{1,0:T(8,128)(2,1)} %get-tuple-element.51), channel_id=1, source_target_pairs={{0,1},{1,0},{2,3},{3,2},{4,5},{5,4},{6,7},{7,6},{8,9},{9,8},{10,11... | collective-permute-start | bytes 786440 | tf_op jit(solution)/shard_map/weights_1/ppermute | solution.py:101
  63.5 14.1 %collective-permute-start.17 = (bf16[256,1024]{1,0:T(8,128)(2,1)S(1)}, bf16[256,1024]{1,0:T(8,128)(2,1)S(1)}, u32[]{:S(2)}, u32[]{:S(2)}) collective-permute-start(bf16[256,1024]{1,0:T(8,128)(2,1)S(1)} %collective-permute-done.5.refs_0_), channel_id=1, source_target_pairs={{0,8},{4,12},{8,0},{12,4},{1,9},{5,13},{9,1},{13,5},{2,10},{6,14},... | collective-permute-start | bytes 1572872 | tf_op jit(solution)/shard_map/tokens_3_2/ppermute | solution.py:101
  64.9 9.0 %collective-permute-start.9 = (bf16[128,1024]{1,0:T(8,128)(2,1)S(1)}, bf16[128,1024]{1,0:T(8,128)(2,1)S(1)}, u32[]{:S(2)}, u32[]{:S(2)}) collective-permute-start(bf16[128,1024]{1,0:T(8,128)(2,1)S(1)} %collective-permute-done.8.refs_22_), channel_id=1, source_target_pairs={{0,16},{16,0},{1,17},{17,1},{2,18},{18,2},{3,19},{19,3},{4,20},{20... | collective-permute-start | bytes 786440 | tf_op jit(solution)/shard_map/weights_3/ppermute | solution.py:101
  69.1 8.5 %collective-permute-start.14 = (bf16[128,1024]{1,0:T(8,128)(2,1)S(1)}, bf16[128,1024]{1,0:T(8,128)(2,1)S(1)}, u32[]{:S(2)}, u32[]{:S(2)}) collective-permute-start(bf16[128,1024]{1,0:T(8,128)(2,1)S(1)} %collective-permute-done.13.refs_18_), channel_id=1, source_target_pairs={{0,16},{16,0},{1,17},{17,1},{2,18},{18,2},{3,19},{19,3},{4,20},{20... | collective-permute-start | bytes 786440 | tf_op jit(solution)/shard_map/weights_1/ppermute | solution.py:101
  70.6 7.6 %collective-permute-start.19 = (bf16[256,1024]{1,0:T(8,128)(2,1)S(1)}, bf16[256,1024]{1,0:T(8,128)(2,1)S(1)}, u32[]{:S(2)}, u32[]{:S(2)}) collective-permute-start(bf16[256,1024]{1,0:T(8,128)(2,1)S(1)} %collective-permute-done.refs_4_), channel_id=1, source_target_pairs={{0,4},{4,0},{8,12},{12,8},{1,5},{5,1},{9,13},{13,9},{2,6},{6,2},{1... | collective-permute-start | bytes 1572872 | tf_op jit(solution)/shard_map/tokens_2_1/ppermute | solution.py:101
  70.6 7.6 %collective-permute-start.20 = (bf16[256,1024]{1,0:T(8,128)(2,1)S(1)}, bf16[256,1024]{1,0:T(8,128)(2,1)S(1)}, u32[]{:S(2)}, u32[]{:S(2)}) collective-permute-start(bf16[256,1024]{1,0:T(8,128)(2,1)S(1)} %collective-permute-done.16.refs_6_), channel_id=1, source_target_pairs={{0,4},{4,0},{8,12},{12,8},{1,5},{5,1},{9,13},{13,9},{2,6},{6,2},{1... | collective-permute-start | bytes 1572872 | tf_op jit(solution)/shard_map/tokens_2_3/ppermute | solution.py:101
  105.7 8.0 %collective-permute-start.21 = (bf16[512,1024]{1,0:T(8,128)(2,1)}, bf16[512,1024]{1,0:T(8,128)(2,1)}, u32[]{:S(2)}, u32[]{:S(2)}) collective-permute-start(bf16[512,1024]{1,0:T(8,128)(2,1)} %get-tuple-element.59), channel_id=1, source_target_pairs={{0,4},{4,0},{8,12},{12,8},{1,5},{5,1},{9,13},{13,9},{2,6},{6,2},{1... | collective-permute-start | bytes 3145736 | tf_op jit(solution)/shard_map/sums_2_1/ppermute | solution.py:101
  106.1 37.3 %collective-permute-start.29 = (bf16[512,1024]{1,0:T(8,128)(2,1)}, bf16[512,1024]{1,0:T(8,128)(2,1)}, u32[]{:S(2)}, u32[]{:S(2)}) collective-permute-start(bf16[512,1024]{1,0:T(8,128)(2,1)} %get-tuple-element.72), channel_id=1, source_target_pairs={{0,4},{4,0},{8,12},{12,8},{1,5},{5,1},{9,13},{13,9},{2,6},{6,2},{1... | collective-permute-start | bytes 3145736 | tf_op jit(solution)/shard_map/sums_1_1/ppermute | solution.py:101
  112.0 14.9 %collective-permute-start.23 = (bf16[272,1024]{1,0:T(8,128)(2,1)}, bf16[272,1024]{1,0:T(8,128)(2,1)S(1)}, u32[]{:S(2)}, u32[]{:S(2)}) collective-permute-start(bf16[272,1024]{1,0:T(8,128)(2,1)} %get-tuple-element.63), channel_id=1, source_target_pairs={{0,8},{4,12},{8,0},{12,4},{1,9},{5,13},{9,1},{13,5},{2,10},{6,14},... | collective-permute-start | bytes 1671176 | tf_op jit(solution)/shard_map/sums_3_2/ppermute | solution.py:101
  112.5 25.7 %collective-permute-start.26 = (bf16[512,512]{1,0:T(8,128)(2,1)}, bf16[512,512]{1,0:T(8,128)(2,1)S(1)}, u32[]{:S(2)}, u32[]{:S(2)}) collective-permute-start(bf16[512,512]{1,0:T(8,128)(2,1)} %get-tuple-element.66), channel_id=1, source_target_pairs={{0,2},{1,3},{2,0},{3,1},{4,6},{5,7},{6,4},{7,5},{8,10},{9,11},{10,... | collective-permute-start | bytes 1572872 | tf_op jit(solution)/shard_map/grads_2/ppermute | solution.py:101
  113.7 32.8 %collective-permute-start.28 = (bf16[512,1024]{1,0:T(8,128)(2,1)}, bf16[512,1024]{1,0:T(8,128)(2,1)}, u32[]{:S(2)}, u32[]{:S(2)}) collective-permute-start(bf16[512,1024]{1,0:T(8,128)(2,1)} %get-tuple-element.70), channel_id=1, source_target_pairs={{0,4},{4,0},{8,12},{12,8},{1,5},{5,1},{9,13},{13,9},{2,6},{6,2},{1... | collective-permute-start | bytes 3145736 | tf_op jit(solution)/shard_map/sums_0_1/ppermute | solution.py:101
  126.8 18.7 %collective-permute-start.24 = (bf16[256,1024]{1,0:T(8,128)(2,1)}, bf16[256,1024]{1,0:T(8,128)(2,1)S(1)}, u32[]{:S(2)}, u32[]{:S(2)}) collective-permute-start(bf16[256,1024]{1,0:T(8,128)(2,1)} %add_convert_fusion.3), channel_id=1, source_target_pairs={{0,8},{4,12},{8,0},{12,4},{1,9},{5,13},{9,1},{13,5},{2,10},{6,14},... | collective-permute-start | bytes 1572872 | tf_op jit(solution)/shard_map/sums_2_2/ppermute | solution.py:101
  138.2 33.2 %collective-permute-start.27 = (bf16[512,512]{1,0:T(8,128)(2,1)}, bf16[512,512]{1,0:T(8,128)(2,1)S(1)}, u32[]{:S(2)}, u32[]{:S(2)}) collective-permute-start(bf16[512,512]{1,0:T(8,128)(2,1)} %get-tuple-element.68), channel_id=1, source_target_pairs={{0,3},{1,2},{2,1},{3,0},{4,7},{5,6},{6,5},{7,4},{8,11},{9,10},{10,... | collective-permute-start | bytes 1572872 | tf_op jit(solution)/shard_map/grads_3/ppermute | solution.py:101
  143.4 22.8 %collective-permute-start.32 = (bf16[272,1024]{1,0:T(8,128)(2,1)}, bf16[272,1024]{1,0:T(8,128)(2,1)S(1)}, u32[]{:S(2)}, u32[]{:S(2)}) collective-permute-start(bf16[272,1024]{1,0:T(8,128)(2,1)} %get-tuple-element.76), channel_id=1, source_target_pairs={{0,1},{1,0},{2,3},{3,2},{4,5},{5,4},{6,7},{7,6},{8,9},{9,8},{10,11... | collective-permute-start | bytes 1671176 | tf_op jit(solution)/shard_map/sums_3/ppermute | solution.py:101
  145.6 25.8 %collective-permute-start.30 = (bf16[256,1024]{1,0:T(8,128)(2,1)}, bf16[256,1024]{1,0:T(8,128)(2,1)}, u32[]{:S(2)}, u32[]{:S(2)}) collective-permute-start(bf16[256,1024]{1,0:T(8,128)(2,1)} %add_convert_fusion.1), channel_id=1, source_target_pairs={{0,8},{4,12},{8,0},{12,4},{1,9},{5,13},{9,1},{13,5},{2,10},{6,14},... | collective-permute-start | bytes 1572872 | tf_op jit(solution)/shard_map/sums_1_2/ppermute | solution.py:101
  148.6 32.5 %collective-permute-start.25 = (bf16[512,512]{1,0:T(8,128)(2,1)}, bf16[512,512]{1,0:T(8,128)(2,1)S(1)}, u32[]{:S(2)}, u32[]{:S(2)}) collective-permute-start(bf16[512,512]{1,0:T(8,128)(2,1)} %get-tuple-element.65), channel_id=1, source_target_pairs={{0,1},{1,0},{2,3},{3,2},{4,5},{5,4},{6,7},{7,6},{8,9},{9,8},{10,11... | collective-permute-start | bytes 1572872 | tf_op jit(solution)/shard_map/grads_1/ppermute | solution.py:101
  169.9 27.7 %collective-permute-start.34 = (bf16[272,1024]{1,0:T(8,128)(2,1)}, bf16[272,1024]{1,0:T(8,128)(2,1)S(1)}, u32[]{:S(2)}, u32[]{:S(2)}) collective-permute-start(bf16[272,1024]{1,0:T(8,128)(2,1)} %get-tuple-element.78), channel_id=1, source_target_pairs={{0,2},{1,3},{2,0},{3,1},{4,6},{5,7},{6,4},{7,5},{8,10},{9,11},{10,... | collective-permute-start | bytes 1671176 | tf_op jit(solution)/shard_map/sums_2/ppermute | solution.py:101
  171.4 26.3 %collective-permute-start.31 = (bf16[256,1024]{1,0:T(8,128)(2,1)}, bf16[256,1024]{1,0:T(8,128)(2,1)S(1)}, u32[]{:S(2)}, u32[]{:S(2)}) collective-permute-start(bf16[256,1024]{1,0:T(8,128)(2,1)} %add_convert_fusion.2), channel_id=1, source_target_pairs={{0,8},{4,12},{8,0},{12,4},{1,9},{5,13},{9,1},{13,5},{2,10},{6,14},... | collective-permute-start | bytes 1572872 | tf_op jit(solution)/shard_map/sums_0_2/ppermute | solution.py:101
  173.9 26.5 %collective-permute-start.33 = (bf16[256,1024]{1,0:T(8,128)(2,1)S(1)}, bf16[256,1024]{1,0:T(8,128)(2,1)S(1)}, u32[]{:S(2)}, u32[]{:S(2)}) collective-permute-start(bf16[256,1024]{1,0:T(8,128)(2,1)S(1)} %add_convert_fusion), channel_id=1, source_target_pairs={{0,1},{1,0},{2,3},{3,2},{4,5},{5,4},{6,7},{7,6},{8,9},{9,8},{10,11... | collective-permute-start | bytes 1572872 | tf_op jit(solution)/shard_map/sums_1/ppermute | solution.py:101
  (37 other events, 746.0 us)

commit v13 on v12

--- a/solution.py
+++ b/solution.py
@@ -133,39 +133,21 @@
     )(first_out, grad_second, w_up, w_down)
 
 
-def core(chunks, w_up, w_down, got, mates, gain, bias):
-    n_chunks, n, n_dp = len(chunks), len(chunks[0]), lax.axis_size("dp")
-    (piece_rows, width), units = chunks[0][0].shape, w_up.shape[1] // n_dp
-    piece_rows //= 2
-    depth = width // n_dp
-    strips, pair = units // depth, 2 * piece_rows
-    slope = (2.0 / math.pi) ** 0.5
-    dtype = w_up.dtype
-    pieces_of_weights = [piece for k in range(1, n_dp) for piece in got[k]]
-    n_got = len(pieces_of_weights)
-
-    def kernel(*refs):
-        toks, refs = refs[: n_chunks * n], refs[n_chunks * n :]
-        (own_up, own_down), weights, (gain_ref, bias_ref), refs = (
-            refs[:2],
-            list(refs[2 : 2 + n_got]),
-            refs[2 + n_got : 4 + n_got],
-            refs[4 + n_got :],
-        )
-        outs, blocks, stat_ref = refs[: 2 * n_chunks], refs[2 * n_chunks : 2 * n_chunks + n_dp], refs[2 * n_chunks + n_dp]
-        scratch = refs[2 * n_chunks + n_dp + 1 :]
-        tok, norm, hid, pre, part, block, up_ref, down_ref, total, in_sem, w_sem, out_sem, b_sem = scratch
+def unpack(w_up, w_down, got, mates):
+    n_dp = lax.axis_size("dp")
+    depth, units = w_up.shape[0], w_up.shape[1] // n_dp
+    strips = units // depth
+    pieces = [piece for k in range(1, n_dp) for piece in got[k]]
+
+    def kernel(own_up, own_down, *rest):
+        left, (up_ref, down_ref, sem) = list(rest[:-3]), rest[-3:]
         place, mate = lax.axis_index("dp"), lax.rem(lax.axis_index("groups"), mates)
-        reads, loads, writes = [], [], []
+        loads = []
 
         def load(src, dst):
-            loads.append(pltpu.make_async_copy(src, dst, w_sem.at[len(loads)]))
+            loads.append(pltpu.make_async_copy(src, dst, sem.at[len(loads)]))
             loads[-1].start()
 
-        for i, ref in enumerate(toks):
-            reads.append(pltpu.make_async_copy(ref, tok.at[i], in_sem.at[i]))
-            if i < n:
-                reads[-1].start()
         mine = pl.ds(pl.multiple_of(place * units, units), units)
         rows = pl.ds(pl.multiple_of(place * depth, depth), depth)
         load(own_up.at[:, mine], up_ref.at[rows, :])
@@ -175,7 +157,7 @@
             many = len(got[k])
             rows = depth // many
             for j in range(many):
-                piece = weights.pop(0)
+                piece = left.pop(0)
                 which = mate ^ j if many > 1 else 0
                 row = pl.multiple_of(first + which * rows, rows)
                 load(piece.at[:, pl.ds(0, units)], up_ref.at[pl.ds(row, rows), :])
@@ -185,6 +167,48 @@
                         piece.at[:, pl.ds(units + c * depth, depth)],
                         down_ref.at[pl.ds(row, rows), pl.ds(first, depth)],
                     )
+        for one in loads:
+            one.wait()
+
+    return pl.pallas_call(
+        kernel,
+        out_shape=[
+            jax.ShapeDtypeStruct((depth * n_dp, units), w_up.dtype),
+            jax.ShapeDtypeStruct((units, depth * n_dp), w_down.dtype),
+        ],
+        in_specs=[pl.BlockSpec(memory_space=pl.ANY)] * (2 + len(pieces)),
+        out_specs=[pl.BlockSpec(memory_space=pltpu.VMEM)] * 2,
+        scratch_shapes=[pltpu.SemaphoreType.DMA((2 + len(pieces) * (1 + strips),))],
+        cost_estimate=pl.CostEstimate(flops=0, bytes_accessed=8 * w_up.size, transcendentals=0),
+        name="unpack",
+    )(w_up, w_down, *pieces)
+
+
+def core(chunks, up, down, gain, bias):
+    n_chunks, n, n_dp = len(chunks), len(chunks[0]), lax.axis_size("dp")
+    (piece_rows, width), units = chunks[0][0].shape, up.shape[1]
+    piece_rows //= 2
+    depth = width // n_dp
+    strips, pair = units // depth, 2 * piece_rows
+    slope = (2.0 / math.pi) ** 0.5
+    dtype = up.dtype
+
+    def kernel(*refs):
+        toks, refs = refs[: n_chunks * n], refs[n_chunks * n :]
+        (up_hbm, down_hbm, gain_ref, bias_ref), refs = refs[:4], refs[4:]
+        outs, blocks, stat_ref = refs[: 2 * n_chunks], refs[2 * n_chunks : 2 * n_chunks + n_dp], refs[2 * n_chunks + n_dp]
+        scratch = refs[2 * n_chunks + n_dp + 1 :]
+        tok, norm, hid, pre, part, block, up_ref, down_ref, total, in_sem, w_sem, out_sem, b_sem = scratch
+        place = lax.axis_index("dp")
+        reads, writes = [], []
+        for i, ref in enumerate(toks):
+            reads.append(pltpu.make_async_copy(ref, tok.at[i], in_sem.at[i]))
+        loads = [
+            pltpu.make_async_copy(up_hbm, up_ref, w_sem.at[0]),
+            pltpu.make_async_copy(down_hbm, down_ref, w_sem.at[1]),
+        ]
+        for one in reads[:n] + loads:
+            one.start()
         for one in reads[n:]:
             one.start()
         total[...] = jnp.zeros_like(total)
@@ -256,7 +280,7 @@
         ]
         + [jax.ShapeDtypeStruct((2 * depth, units), dtype)] * n_dp
         + [jax.ShapeDtypeStruct((EXTRA, width), dtype)],
-        in_specs=[far] * (n_chunks * n + 2 + n_got) + [near] * 2,
+        in_specs=[far] * (n_chunks * n + 2) + [near] * 2,
         out_specs=[far] * (2 * n_chunks + n_dp) + [near],
         scratch_shapes=[
             pltpu.VMEM((n_chunks * n, pair, width), dtype),
@@ -269,7 +293,7 @@
             pltpu.VMEM((units, width), dtype),
             pltpu.VMEM((EXTRA, width), jnp.float32),
             pltpu.SemaphoreType.DMA((n_chunks * n,)),
-            pltpu.SemaphoreType.DMA((2 + n_got * (1 + strips),)),
+            pltpu.SemaphoreType.DMA((2,)),
             pltpu.SemaphoreType.DMA((2 * n_chunks + 1,)),
             pltpu.SemaphoreType.DMA((n_dp,)),
         ],
@@ -282,9 +306,8 @@
         name="core",
     )(
         *[piece for chunk in chunks for piece in chunk],
-        w_up,
-        w_down,
-        *pieces_of_weights,
+        up,
+        down,
         gain.reshape(1, width),
         bias.reshape(1, width),
     )
@@ -425,7 +448,7 @@
     def tokens_rest(k, *first):
         for bit in others:
             for j in list(chunks[k]):
-                piece = after(chunks[k][j], *first)
+                piece = chunks[k][j] if j else after(chunks[k][j], *first)
                 chunks[k][j | bit] = swap(piece, "tensor", bit, f"tokens_{k}_{j | bit}")
 
     def weights_groups(k, *first):
@@ -444,71 +467,82 @@
     for k in range(2, n_dp):
         if k & (k - 1):
             tokens_dp(k, *stage)
+        if k == top:
+            weights_dp(1, *stage)
         weights_dp(k, *stage, *([got[top]] if top in got else []))
     for k in range(2, n_dp):
         tokens_rest(k - 1)
         stage = [got[top]]
         if k & (k - 1):
-            weights_groups(top)
+            for bit in reversed(bits_of(n_dp)):
+                if bit not in crossed:
+                    weights_groups(bit)
             stage = [tokens[k], *got.values(), *crossed.values(), *chunks[k - 2].values()]
         tokens_tensor(k, *stage, chunks[k - 1][high])
-    weights_dp(1, *stage)
-    for k in [*range(2, n_dp), 1]:
+    for k in range(1, n_dp):
         if k not in crossed:
             weights_groups(k)
-    tokens_rest(n_dp - 1, *crossed.values())
     got = {k: [got[k]] + ([crossed[k]] if k in crossed else []) for k in got}
+    up, down = unpack(w_up, w_down, got, mates)
+    tokens_rest(n_dp - 1, up)
+
 
     order = sorted(chunks, reverse=True)
     halves, blocks, stats = core(
-        [[chunks[k][j] for j in range(n_tensor)] for k in order], w_up, w_down, got, mates, norm_gain, norm_bias
+        [[chunks[k][j] for j in range(n_tensor)] for k in order], up, down, norm_gain, norm_bias
     )
     blocks = dict(enumerate(blocks))
     blocks[top] = swap(blocks[top], "dp", top, f"grads_{top}")
 
-    for k in range(top + 1, n_dp):
-        blocks[k] = swap(after(blocks[k], blocks[top]), "dp", k, f"grads_{k}")
 
     def add(terms):
         spans = (x[place * span : (place + 1) * span].astype(jnp.float32) for x, place in terms)
         return sum(spans).astype(jnp.bfloat16)
 
-    sums, behind, span, waiting = {}, (), 2 * own_rows, None
+    span, first = 2 * own_rows, order[0]
+    sums, came, behind = {}, {}, ()
     for k, (even, odd) in zip(order, halves, strict=True):
-        came = swap(odd, "tensor", 1, f"sums_{k}_1")
-        if k == order[0]:
-            waiting = (came, even.shape[0] // EXTRA)
-        parts = {2 * j: [(x, j) for x in (even, came)] for j in range(n_tensor // 2)}
+        other = swap(odd, "tensor", 1, f"sums_{k}_1")
+        if k == first:
+            waiting = (other, even.shape[0] // EXTRA)
+        parts = {2 * j: [(x, j) for x in (even, other)] for j in range(n_tensor // 2)}
         for bit in reversed(bits_of(n_tensor)[:-1]):
             for j in [j for j in parts if j & bit]:
-                if k == order[0] and j == bit:
+                carries = k == first and j == bit
+                if carries:
                     send, stats = join(span, parts.pop(j), [(stats, 0), waiting])
                 else:
                     send = add(parts.pop(j))
-                if k < top:
-                    behind += (blocks[n_dp - 1 if k == 0 else top],)
-                came = swap(after(send, *behind), "tensor", bit, f"sums_{k}_{j}")
-                if k == order[0] and j == bit:
-                    waiting = (came, span // EXTRA)
-                parts[j ^ bit].append((came, 0))
-                behind = (came,)
-                if k == top:
-                    for i in range(1, top):
-                        blocks[i] = swap(after(blocks[i], came), "dp", i, f"grads_{i}")
+                if k in (0, top):
+                    behind += (blocks[top if k else n_dp - 1],)
+                other = swap(after(send, *behind), "tensor", bit, f"sums_{k}_{j}")
+                if carries:
+                    waiting = (other, span // EXTRA)
+                parts[j ^ bit].append((other, 0))
+                behind = (other,)
         sums[k] = parts[0]
-    came = {}
+        if k == first:
+            send, stats = join(span, sums.pop(k), [(stats, 0), waiting])
+            came[k] = swap(send, "dp", k & -k, f"sums_{k}")
+            waiting = (came[k], span // EXTRA)
+            for i in range(top + 1, n_dp):
+                blocks[i] = swap(after(blocks[i], blocks[top], send), "dp", i, f"grads_{i}")
+    sums[first & (first - 1)].append((came[first], 0))
     for bit in bits_of(n_dp)[::-1]:
         for k in [k for k in order if k & bit and k in sums and k != bit]:
-            if k == (n_dp - 1) & -bit:
+            carries = k == (n_dp - 1) & -bit
+            if carries:
                 send, stats = join(span, sums.pop(k), [(stats, 0), waiting])
             else:
                 send = add(sums.pop(k))
             came[k] = swap(send, "dp", bit, f"sums_{k}")
-            if k == (n_dp - 1) & -bit:
+            if carries:
                 waiting = (came[k], span // EXTRA)
             sums[k ^ bit].append((came[k], 0))
     last, stats = join(span, sums[top], [(stats, 0), waiting])
     came[top] = swap(last, "dp", top, f"sums_{top}")
+    for k in range(1, top):
+        blocks[k] = swap(after(blocks[k], last), "dp", k, f"grads_{k}")
     for bit in bits_of(n_dp)[:0:-1]:
         came[bit] = swap(after(add(sums[bit]), last), "dp", bit, f"sums_{bit}")
 

time: 205 us -> 219 us (1.068)
  waiting for transfers between devices: 118 us -> 129 us
  Pallas kernels: 39.1 us -> 42.1 us
    ppermute x35, waiting for transfers between devices: 118 us -> 129 us  [swap(): lax.ppermute(values, axis, [(i, i ^ mask) for i in range(lax.axis_size(ax...]
    pallas_call x0 -> x1, Pallas kernels: none -> 3.01 us  [unpack(): pl.pallas_call(kernel, out_shape=[jax.ShapeDtypeStruct((depth * n_dp, uni...]
  transfers between devices with their start and end apart: 35 -> 35, of which waited for: 19 -> 19; matrix products, arithmetic and copies ran while one was open for 4% -> 4% of each run, Pallas kernels for 4% -> 5%
where the time goes in v13:
time: 219 us
  waiting for transfers between devices  129 us (59%)
  Pallas kernels  42.1 us (19%)
  starting transfers between devices  35 us (16%)
  other arithmetic  7.81 us (4%)
  local copies, waits for them, and re-layouts  3.39 us (2%)
    ppermute x35, waiting for transfers between devices, swap(): lax.ppermute(values, axis, [(i, i ^ mask) for i in range(lax.axis_size(ax...  129 us
    ppermute x35, starting transfers between devices, swap(): lax.ppermute(values, axis, [(i, i ^ mask) for i in range(lax.axis_size(ax...  35 us
    pallas_call x1, Pallas kernels, core(): pl.pallas_call(kernel, out_shape=[jax.ShapeDtypeStruct((half[0] + (EXTRA...  24.4 us
    pallas_call x3, Pallas kernels, join(): pl.pallas_call(kernel, out_shape=out_shape, grid=(1,), in_specs=[spec(row...  7.96 us
    convert_element_type x4, other arithmetic, add(): return sum(spans).astype(jnp.bfloat16)  7.81 us
  transfers between devices with their start and end apart: 35, of which 19 were waited for; matrix products, arithmetic and copies ran while one was open for 4% of the time, Pallas kernels for 5%

profile of v13, /device:TPU:0, one launch (start us, length us, event | category | flops | bytes accessed | tf_op | source)
XLA Modules:
  0.0 218.6 jit_solution(15930720777156160209)
XLA Ops:
  0.6 2.8 %pack.1 = (bf16[256,1024]{1,0:T(8,128)(2,1)}, bf16[128,1024]{1,0:T(8,128)(2,1)}, bf16[128,1024]{1,0:T(8,128)(2,1)}, bf16[128,1024]{1,0:T(8,128)(2,1)}) custom-call(bf16[128,1024]{1,0:T(8,128)(2,1)} %refs_10_.1, bf16[128,1024]{1,0:T(8,128)(2,1)} %grad_ref.1, bf16[256,2048]{1,0:T(8,128)(2,1)} %own_up.1, bf16[2048,256]{1,0:T(8,128)(2,1)} %own_down.1), custom_call_target="tpu_custom_call" | custom-call | bytes 4194304 | tf_op jit(solution)/shard_map/pack/pallas_call | solution.py:125
  3.4 3.0 %collective-permute-start.2 = (bf16[256,1024]{1,0:T(8,128)(2,1)}, bf16[256,1024]{1,0:T(8,128)(2,1)S(1)}, u32[]{:S(2)}, u32[]{:S(2)}) collective-permute-start(bf16[256,1024]{1,0:T(8,128)(2,1)} %get-tuple-element.44.refs_12_), channel_id=1, source_target_pairs={{0,8},{4,12},{8,0},{12,4},{1,9},{5,13},{9,1},{13,5},{2,10},{6,14},... | collective-permute-start | bytes 1572872 | tf_op jit(solution)/shard_map/tokens_0_2/ppermute | solution.py:101
  8.0 2.6 %collective-permute-start = (bf16[256,1024]{1,0:T(8,128)(2,1)}, bf16[256,1024]{1,0:T(8,128)(2,1)S(1)}, u32[]{:S(2)}, u32[]{:S(2)}) collective-permute-start(bf16[256,1024]{1,0:T(8,128)(2,1)} %get-tuple-element.44.refs_12_), channel_id=1, source_target_pairs={{0,2},{1,3},{2,0},{3,1},{4,6},{5,7},{6,4},{7,5},{8,10},{9,11},{10,... | collective-permute-start | bytes 1572872 | tf_op jit(solution)/shard_map/tokens_2/ppermute | solution.py:101
  10.6 8.0 %collective-permute-done.2.refs_14_ = bf16[256,1024]{1,0:T(8,128)(2,1)S(1)} collective-permute-done((bf16[256,1024]{1,0:T(8,128)(2,1)}, bf16[256,1024]{1,0:T(8,128)(2,1)S(1)}, u32[]{:S(2)}, u32[]{:S(2)}) %collective-permute-start.2) | collective-permute-done | bytes 524320 | tf_op jit(solution)/shard_map/tokens_0_2/ppermute | solution.py:101
  18.5 12.6 %collective-permute-done.1.refs_8_ = bf16[256,1024]{1,0:T(8,128)(2,1)S(1)} collective-permute-done((bf16[256,1024]{1,0:T(8,128)(2,1)}, bf16[256,1024]{1,0:T(8,128)(2,1)S(1)}, u32[]{:S(2)}, u32[]{:S(2)}) %collective-permute-start.1) | collective-permute-done | bytes 524320 | tf_op jit(solution)/shard_map/tokens_1/ppermute | solution.py:101
  31.1 2.4 %collective-permute-done.refs_4_ = bf16[256,1024]{1,0:T(8,128)(2,1)S(1)} collective-permute-done((bf16[256,1024]{1,0:T(8,128)(2,1)}, bf16[256,1024]{1,0:T(8,128)(2,1)S(1)}, u32[]{:S(2)}, u32[]{:S(2)}) %collective-permute-start) | collective-permute-done | bytes 524320 | tf_op jit(solution)/shard_map/tokens_2/ppermute | solution.py:101
  34.4 2.7 %collective-permute-start.5 = (bf16[256,1024]{1,0:T(8,128)(2,1)S(1)}, bf16[256,1024]{1,0:T(8,128)(2,1)}, u32[]{:S(2)}, u32[]{:S(2)}) collective-permute-start(bf16[256,1024]{1,0:T(8,128)(2,1)S(1)} %collective-permute-done.refs_4_), channel_id=1, source_target_pairs={{0,1},{1,0},{2,3},{3,2},{4,5},{5,4},{6,7},{7,6},{8,9},{9,8},{10,11... | collective-permute-start | bytes 1572872 | tf_op jit(solution)/shard_map/tokens_3/ppermute | solution.py:101
  37.2 6.5 %collective-permute-done.13.refs_10_ = bf16[256,1024]{1,0:T(8,128)(2,1)S(1)} collective-permute-done((bf16[256,1024]{1,0:T(8,128)(2,1)S(1)}, bf16[256,1024]{1,0:T(8,128)(2,1)S(1)}, u32[]{:S(2)}, u32[]{:S(2)}) %collective-permute-start.13) | collective-permute-done | bytes 524320 | tf_op jit(solution)/shard_map/tokens_1_2/ppermute | solution.py:101
  43.6 5.9 %collective-permute-done.8.rest_2_ = bf16[128,1024]{1,0:T(8,128)(2,1)S(1)} collective-permute-done((bf16[128,1024]{1,0:T(8,128)(2,1)}, bf16[128,1024]{1,0:T(8,128)(2,1)S(1)}, u32[]{:S(2)}, u32[]{:S(2)}) %collective-permute-start.8) | collective-permute-done | bytes 262176 | tf_op jit(solution)/shard_map/weights_2/ppermute | solution.py:101
  51.0 9.6 %collective-permute-done.6.rest_0_ = bf16[128,1024]{1,0:T(8,128)(2,1)S(1)} collective-permute-done((bf16[128,1024]{1,0:T(8,128)(2,1)}, bf16[128,1024]{1,0:T(8,128)(2,1)S(1)}, u32[]{:S(2)}, u32[]{:S(2)}) %collective-permute-start.6) | collective-permute-done | bytes 262176 | tf_op jit(solution)/shard_map/weights_1/ppermute | solution.py:101
  64.2 5.6 %collective-permute-done.7.rest_1_ = bf16[128,1024]{1,0:T(8,128)(2,1)S(1)} collective-permute-done((bf16[128,1024]{1,0:T(8,128)(2,1)S(1)}, bf16[128,1024]{1,0:T(8,128)(2,1)S(1)}, u32[]{:S(2)}, u32[]{:S(2)}) %collective-permute-start.7) | collective-permute-done | bytes 262176 | tf_op jit(solution)/shard_map/weights_1/ppermute | solution.py:101
  69.9 2.1 collective-permute-done.10.rest_4_
  72.0 2.3 %collective-permute-done.9.rest_3_ = bf16[128,1024]{1,0:T(8,128)(2,1)S(1)} collective-permute-done((bf16[128,1024]{1,0:T(8,128)(2,1)S(1)}, bf16[128,1024]{1,0:T(8,128)(2,1)S(1)}, u32[]{:S(2)}, u32[]{:S(2)}) %collective-permute-start.9) | collective-permute-done | bytes 262176 | tf_op jit(solution)/shard_map/weights_2/ppermute | solution.py:101
  77.4 5.3 %collective-permute-done.11.rest_5_ = bf16[128,1024]{1,0:T(8,128)(2,1)S(1)} collective-permute-done((bf16[128,1024]{1,0:T(8,128)(2,1)S(1)}, bf16[128,1024]{1,0:T(8,128)(2,1)S(1)}, u32[]{:S(2)}, u32[]{:S(2)}) %collective-permute-start.11) | collective-permute-done | bytes 262176 | tf_op jit(solution)/shard_map/weights_3/ppermute | solution.py:101
  83.4 3.0 %unpack.1 = (bf16[1024,512]{1,0:T(8,128)(2,1)}, bf16[512,1024]{1,0:T(8,128)(2,1)}) custom-call(bf16[256,2048]{1,0:T(8,128)(2,1)} %own_up.1, bf16[2048,256]{1,0:T(8,128)(2,1)} %own_down.1, bf16[128,1024]{1,0:T(8,128)(2,1)} %copy-done.14, bf16[128,1024]{1,0:T(8,128)(2,1)} %copy-done.15, bf16[128,1024]{1,0:T(8,128)(2,1)} %copy-done.13, ...), custom_call_target="tpu_custom_call" | custom-call | bytes 4194304 | tf_op jit(solution)/shard_map/unpack/pallas_call | solution.py:173
  87.3 2.0 collective-permute-done.20.refs_7_
  90.9 24.4 %core.1 = (bf16[512,1024]{1,0:T(8,128)(2,1)}, bf16[528,1024]{1,0:T(8,128)(2,1)}, bf16[512,1024]{1,0:T(8,128)(2,1)}, bf16[512,1024]{1,0:T(8,128)(2,1)}, bf16[512,...) custom-call(bf16[256,1024]{1,0:T(8,128)(2,1)} %collective-permute-do, ...), custom_call_target="tpu_custom_call" | custom-call | flops 10737418240 | bytes 20971520 | tf_op jit(solution)/shard_map/core/pallas_call | solution.py:276
  116.0 2.6 %collective-permute-done.22.refs_1_.refs_3_ = bf16[528,1024]{1,0:T(8,128)(2,1)S(1)} collective-permute-done((bf16[528,1024]{1,0:T(8,128)(2,1)}, bf16[528,1024]{1,0:T(8,128)(2,1)S(1)}, u32[]{:S(2)}, u32[]{:S(2)}) %collective-permute-start.22) | collective-permute-done | bytes 1081376 | tf_op jit(solution)/shard_map/sums_3_1/ppermute | solution.py:101
  119.6 2.3 %join.3 = (bf16[272,1024]{1,0:T(8,128)(2,1)}, bf16[16,1024]{1,0:T(8,128)(2,1)}) custom-call(bf16[512,1024]{1,0:T(8,128)(2,1)} %get-tuple-element.62.refs_0_, bf16[528,1024]{1,0:T(8,128)(2,1)} %copy-done.8, bf16[16,1024]{1,0:T(8,128)(2,1)} %get-tuple-element.64.refs_2_, bf16[528,1024]{1,0:T(8,128)(2,1)} %copy-done.8), custom_call_target="tpu_custom_call" | custom-call | bytes 1572864 | tf_op jit(solution)/shard_map/join/pallas_call | solution.py:409
  124.3 2.1 add_convert_fusion.3
  126.4 22.3 %collective-permute-done.24.refs_2_ = bf16[512,512]{1,0:T(8,128)(2,1)S(1)} collective-permute-done((bf16[512,512]{1,0:T(8,128)(2,1)}, bf16[512,512]{1,0:T(8,128)(2,1)S(1)}, u32[]{:S(2)}, u32[]{:S(2)}) %collective-permute-start.24) | collective-permute-done | bytes 524320 | tf_op jit(solution)/shard_map/grads_2/ppermute | solution.py:101
  150.0 2.7 %join.4 = (bf16[272,1024]{1,0:T(8,128)(2,1)}, bf16[16,1024]{1,0:T(8,128)(2,1)}) custom-call(bf16[512,1024]{1,0:T(8,128)(2,1)} %get-tuple-element.62.refs_0_, bf16[528,1024]{1,0:T(8,128)(2,1)} %copy-done.8, bf16[272,1024]{1,0:T(8,128)(2,1)} %copy-done.11, bf16[16,1024]{1,0:T(8,128)(2,1)} %get-tuple-element.68.refs_3_, bf16[272,1024]{1,0:T(8,128)(2,1)} %copy-done.11), custom_call_target="tpu_custom_call" | custom-call | bytes 2097152 | tf_op jit(solution)/shard_map/join/pallas_call | solution.py:409
  152.7 2.0 add_convert_fusion.1
  155.9 6.9 %collective-permute-done.25.refs_2_ = bf16[256,1024]{1,0:T(8,128)(2,1)} collective-permute-done((bf16[256,1024]{1,0:T(8,128)(2,1)}, bf16[256,1024]{1,0:T(8,128)(2,1)}, u32[]{:S(2)}, u32[]{:S(2)}) %collective-permute-start.25) | collective-permute-done | bytes 524320 | tf_op jit(solution)/shard_map/sums_2_2/ppermute | solution.py:101
  164.0 2.0 add_convert_fusion.2
  166.0 12.9 %collective-permute-done.26.refs_3_.refs_5_ = bf16[272,1024]{1,0:T(8,128)(2,1)S(1)} collective-permute-done((bf16[272,1024]{1,0:T(8,128)(2,1)}, bf16[272,1024]{1,0:T(8,128)(2,1)S(1)}, u32[]{:S(2)}, u32[]{:S(2)}) %collective-permute-start.26) | collective-permute-done | bytes 557088 | tf_op jit(solution)/shard_map/sums_3/ppermute | solution.py:101
  179.8 2.9 %join.5 = (bf16[272,1024]{1,0:T(8,128)(2,1)}, bf16[16,1024]{1,0:T(8,128)(2,1)}) custom-call(bf16[512,1024]{1,0:T(8,128)(2,1)} %get-tuple-element.60.refs_0_, bf16[512,1024]{1,0:T(8,128)(2,1)} %collective-permute-done.21.refs_1_, bf16[256,1024]{1,0:T(8,128)(2,1)} %collective-permute-done.25.refs_2_, bf16[272,1024]{1,0:T(8,128)(2,1)} %copy-done.10, ...), custom_call_target="tpu_custom_call" | custom-call | bytes 2621440 | tf_op jit(solution)/shard_map/join/pallas_call | solution.py:409
  184.0 1.6 add_convert_fusion
  185.6 7.6 %collective-permute-start.33 = (bf16[256,1024]{1,0:T(8,128)(2,1)S(1)}, bf16[256,1024]{1,0:T(8,128)(2,1)S(1)}, u32[]{:S(2)}, u32[]{:S(2)}) collective-permute-start(bf16[256,1024]{1,0:T(8,128)(2,1)S(1)} %add_convert_fusion), channel_id=1, source_target_pairs={{0,1},{1,0},{2,3},{3,2},{4,5},{5,4},{6,7},{7,6},{8,9},{9,8},{10,11... | collective-permute-start | bytes 1572872 | tf_op jit(solution)/shard_map/sums_1/ppermute | solution.py:101
  193.3 13.7 %collective-permute-done.27.refs_1_ = bf16[512,512]{1,0:T(8,128)(2,1)S(1)} collective-permute-done((bf16[512,512]{1,0:T(8,128)(2,1)}, bf16[512,512]{1,0:T(8,128)(2,1)S(1)}, u32[]{:S(2)}, u32[]{:S(2)}) %collective-permute-start.27) | collective-permute-done | bytes 524320 | tf_op jit(solution)/shard_map/grads_1/ppermute | solution.py:101
  207.0 7.8 %collective-permute-done.33.refs_7_ = bf16[256,1024]{1,0:T(8,128)(2,1)S(1)} collective-permute-done((bf16[256,1024]{1,0:T(8,128)(2,1)S(1)}, bf16[256,1024]{1,0:T(8,128)(2,1)S(1)}, u32[]{:S(2)}, u32[]{:S(2)}) %collective-permute-start.33) | collective-permute-done | bytes 524320 | tf_op jit(solution)/shard_map/sums_1/ppermute | solution.py:101
  214.8 3.9 %finish.1 = (bf16[128,1024]{1,0:T(8,128)(2,1)}, f32[128,1024]{1,0:T(8,128)}, f32[256,2048]{1,0:T(8,128)}, f32[2048,256]{1,0:T(8,128)}, f32[2,1024]{1,0:T(2,128)}) custom-call(bf16[512,512]{1,0:T(8,128)(2,1)S(1)} %copy-done.2, bf16[512,512]{1,0:T(8,128)(2,1)S(1)} %collective-permute-done.27.refs_1_, bf16[512,512]{1,0:T(8,128)(2,1)S(1)} %collective-permute-done.24.refs_2_, ...), custom_call_target="tpu_custom_call" | custom-call | bytes 6291456 | tf_op jit(solution)/shard_map/finish/pallas_call | solution.py:369
  (109 shorter events, 23.6 us)
Async XLA Ops:
  3.4 15.1 %collective-permute-start.2 = (bf16[256,1024]{1,0:T(8,128)(2,1)}, bf16[256,1024]{1,0:T(8,128)(2,1)S(1)}, u32[]{:S(2)}, u32[]{:S(2)}) collective-permute-start(bf16[256,1024]{1,0:T(8,128)(2,1)} %get-tuple-element.44.refs_12_), channel_id=1, source_target_pairs={{0,8},{4,12},{8,0},{12,4},{1,9},{5,13},{9,1},{13,5},{2,10},{6,14},... | collective-permute-start | bytes 1572872 | tf_op jit(solution)/shard_map/tokens_0_2/ppermute | solution.py:101
  6.4 24.7 %collective-permute-start.1 = (bf16[256,1024]{1,0:T(8,128)(2,1)}, bf16[256,1024]{1,0:T(8,128)(2,1)S(1)}, u32[]{:S(2)}, u32[]{:S(2)}) collective-permute-start(bf16[256,1024]{1,0:T(8,128)(2,1)} %get-tuple-element.44.refs_12_), channel_id=1, source_target_pairs={{0,1},{1,0},{2,3},{3,2},{4,5},{5,4},{6,7},{7,6},{8,9},{9,8},{10,11... | collective-permute-start | bytes 1572872 | tf_op jit(solution)/shard_map/tokens_1/ppermute | solution.py:101
  8.0 25.5 %collective-permute-start = (bf16[256,1024]{1,0:T(8,128)(2,1)}, bf16[256,1024]{1,0:T(8,128)(2,1)S(1)}, u32[]{:S(2)}, u32[]{:S(2)}) collective-permute-start(bf16[256,1024]{1,0:T(8,128)(2,1)} %get-tuple-element.44.refs_12_), channel_id=1, source_target_pairs={{0,2},{1,3},{2,0},{3,1},{4,6},{5,7},{6,4},{7,5},{8,10},{9,11},{10,... | collective-permute-start | bytes 1572872 | tf_op jit(solution)/shard_map/tokens_2/ppermute | solution.py:101
  10.6 23.4 %collective-permute-start.3 = (bf16[256,1024]{1,0:T(8,128)(2,1)}, bf16[256,1024]{1,0:T(8,128)(2,1)S(1)}, u32[]{:S(2)}, u32[]{:S(2)}) collective-permute-start(bf16[256,1024]{1,0:T(8,128)(2,1)} %get-tuple-element.44.refs_12_), channel_id=1, source_target_pairs={{0,4},{4,0},{8,12},{12,8},{1,5},{5,1},{9,13},{13,9},{2,6},{6,2},{1... | collective-permute-start | bytes 1572872 | tf_op jit(solution)/shard_map/tokens_0_1/ppermute | solution.py:101
  18.5 15.5 %collective-permute-start.4 = (bf16[256,1024]{1,0:T(8,128)(2,1)S(1)}, bf16[256,1024]{1,0:T(8,128)(2,1)S(1)}, u32[]{:S(2)}, u32[]{:S(2)}) collective-permute-start(bf16[256,1024]{1,0:T(8,128)(2,1)S(1)} %collective-permute-done.2.refs_14_), channel_id=1, source_target_pairs={{0,4},{4,0},{8,12},{12,8},{1,5},{5,1},{9,13},{13,9},{2,6},{6,2},{1... | collective-permute-start | bytes 1572872 | tf_op jit(solution)/shard_map/tokens_0_3/ppermute | solution.py:101
  33.5 10.1 %collective-permute-start.13 = (bf16[256,1024]{1,0:T(8,128)(2,1)S(1)}, bf16[256,1024]{1,0:T(8,128)(2,1)S(1)}, u32[]{:S(2)}, u32[]{:S(2)}) collective-permute-start(bf16[256,1024]{1,0:T(8,128)(2,1)S(1)} %collective-permute-done.1.refs_8_), channel_id=1, source_target_pairs={{0,8},{4,12},{8,0},{12,4},{1,9},{5,13},{9,1},{13,5},{2,10},{6,14},... | collective-permute-start | bytes 1572872 | tf_op jit(solution)/shard_map/tokens_1_2/ppermute | solution.py:101
  34.0 28.2 %collective-permute-start.14 = (bf16[256,1024]{1,0:T(8,128)(2,1)S(1)}, bf16[256,1024]{1,0:T(8,128)(2,1)}, u32[]{:S(2)}, u32[]{:S(2)}) collective-permute-start(bf16[256,1024]{1,0:T(8,128)(2,1)S(1)} %collective-permute-done.1.refs_8_), channel_id=1, source_target_pairs={{0,4},{4,0},{8,12},{12,8},{1,5},{5,1},{9,13},{13,9},{2,6},{6,2},{1... | collective-permute-start | bytes 1572872 | tf_op jit(solution)/shard_map/tokens_1_1/ppermute | solution.py:101
  34.0 15.5 %collective-permute-start.8 = (bf16[128,1024]{1,0:T(8,128)(2,1)}, bf16[128,1024]{1,0:T(8,128)(2,1)S(1)}, u32[]{:S(2)}, u32[]{:S(2)}) collective-permute-start(bf16[128,1024]{1,0:T(8,128)(2,1)} %get-tuple-element.49), channel_id=1, source_target_pairs={{0,2},{1,3},{2,0},{3,1},{4,6},{5,7},{6,4},{7,5},{8,10},{9,11},{10,... | collective-permute-start | bytes 786440 | tf_op jit(solution)/shard_map/weights_2/ppermute | solution.py:101
  34.4 29.3 %collective-permute-start.5 = (bf16[256,1024]{1,0:T(8,128)(2,1)S(1)}, bf16[256,1024]{1,0:T(8,128)(2,1)}, u32[]{:S(2)}, u32[]{:S(2)}) collective-permute-start(bf16[256,1024]{1,0:T(8,128)(2,1)S(1)} %collective-permute-done.refs_4_), channel_id=1, source_target_pairs={{0,1},{1,0},{2,3},{3,2},{4,5},{5,4},{6,7},{7,6},{8,9},{9,8},{10,11... | collective-permute-start | bytes 1572872 | tf_op jit(solution)/shard_map/tokens_3/ppermute | solution.py:101
  37.1 23.5 %collective-permute-start.6 = (bf16[128,1024]{1,0:T(8,128)(2,1)}, bf16[128,1024]{1,0:T(8,128)(2,1)S(1)}, u32[]{:S(2)}, u32[]{:S(2)}) collective-permute-start(bf16[128,1024]{1,0:T(8,128)(2,1)} %get-tuple-element.47), channel_id=1, source_target_pairs={{0,1},{1,0},{2,3},{3,2},{4,5},{5,4},{6,7},{7,6},{8,9},{9,8},{10,11... | collective-permute-start | bytes 786440 | tf_op jit(solution)/shard_map/weights_1/ppermute | solution.py:101
  43.6 20.6 %collective-permute-start.15 = (bf16[256,1024]{1,0:T(8,128)(2,1)S(1)}, bf16[256,1024]{1,0:T(8,128)(2,1)S(1)}, u32[]{:S(2)}, u32[]{:S(2)}) collective-permute-start(bf16[256,1024]{1,0:T(8,128)(2,1)S(1)} %collective-permute-done.13.refs_10_), channel_id=1, source_target_pairs={{0,4},{4,0},{8,12},{12,8},{1,5},{5,1},{9,13},{13,9},{2,6},{6,2},{1... | collective-permute-start | bytes 1572872 | tf_op jit(solution)/shard_map/tokens_1_3/ppermute | solution.py:101
  49.5 24.7 %collective-permute-start.16 = (bf16[256,1024]{1,0:T(8,128)(2,1)S(1)}, bf16[256,1024]{1,0:T(8,128)(2,1)S(1)}, u32[]{:S(2)}, u32[]{:S(2)}) collective-permute-start(bf16[256,1024]{1,0:T(8,128)(2,1)S(1)} %collective-permute-done.refs_4_), channel_id=1, source_target_pairs={{0,8},{4,12},{8,0},{12,4},{1,9},{5,13},{9,1},{13,5},{2,10},{6,14},... | collective-permute-start | bytes 1572872 | tf_op jit(solution)/shard_map/tokens_2_2/ppermute | solution.py:101
  60.7 9.2 %collective-permute-start.7 = (bf16[128,1024]{1,0:T(8,128)(2,1)S(1)}, bf16[128,1024]{1,0:T(8,128)(2,1)S(1)}, u32[]{:S(2)}, u32[]{:S(2)}) collective-permute-start(bf16[128,1024]{1,0:T(8,128)(2,1)S(1)} %collective-permute-done.6.rest_0_), channel_id=1, source_target_pairs={{0,16},{16,0},{1,17},{17,1},{2,18},{18,2},{3,19},{19,3},{4,20},{20... | collective-permute-start | bytes 786440 | tf_op jit(solution)/shard_map/weights_1/ppermute | solution.py:101
  62.2 9.8 %collective-permute-start.10 = (bf16[128,1024]{1,0:T(8,128)(2,1)}, bf16[128,1024]{1,0:T(8,128)(2,1)S(1)}, u32[]{:S(2)}, u32[]{:S(2)}) collective-permute-start(bf16[128,1024]{1,0:T(8,128)(2,1)} %get-tuple-element.51), channel_id=1, source_target_pairs={{0,3},{1,2},{2,1},{3,0},{4,7},{5,6},{6,5},{7,4},{8,11},{9,10},{10,... | collective-permute-start | bytes 786440 | tf_op jit(solution)/shard_map/weights_3/ppermute | solution.py:101
  63.7 10.5 %collective-permute-start.9 = (bf16[128,1024]{1,0:T(8,128)(2,1)S(1)}, bf16[128,1024]{1,0:T(8,128)(2,1)S(1)}, u32[]{:S(2)}, u32[]{:S(2)}) collective-permute-start(bf16[128,1024]{1,0:T(8,128)(2,1)S(1)} %collective-permute-done.8.rest_2_), channel_id=1, source_target_pairs={{0,16},{16,0},{1,17},{17,1},{2,18},{18,2},{3,19},{19,3},{4,20},{20... | collective-permute-start | bytes 786440 | tf_op jit(solution)/shard_map/weights_2/ppermute | solution.py:101
  74.3 13.1 %collective-permute-start.17 = (bf16[256,1024]{1,0:T(8,128)(2,1)}, bf16[256,1024]{1,0:T(8,128)(2,1)}, u32[]{:S(2)}, u32[]{:S(2)}) collective-permute-start(bf16[256,1024]{1,0:T(8,128)(2,1)} %collective-permute-done.5.refs_0_), channel_id=1, source_target_pairs={{0,8},{4,12},{8,0},{12,4},{1,9},{5,13},{9,1},{13,5},{2,10},{6,14},... | collective-permute-start | bytes 1572872 | tf_op jit(solution)/shard_map/tokens_3_2/ppermute | solution.py:101
  75.8 6.8 %collective-permute-start.11 = (bf16[128,1024]{1,0:T(8,128)(2,1)S(1)}, bf16[128,1024]{1,0:T(8,128)(2,1)S(1)}, u32[]{:S(2)}, u32[]{:S(2)}) collective-permute-start(bf16[128,1024]{1,0:T(8,128)(2,1)S(1)} %collective-permute-done.10.rest_4_), channel_id=1, source_target_pairs={{0,16},{16,0},{1,17},{17,1},{2,18},{18,2},{3,19},{19,3},{4,20},{20... | collective-permute-start | bytes 786440 | tf_op jit(solution)/shard_map/weights_3/ppermute | solution.py:101
  77.3 10.0 %collective-permute-start.19 = (bf16[256,1024]{1,0:T(8,128)(2,1)S(1)}, bf16[256,1024]{1,0:T(8,128)(2,1)}, u32[]{:S(2)}, u32[]{:S(2)}) collective-permute-start(bf16[256,1024]{1,0:T(8,128)(2,1)S(1)} %collective-permute-done.refs_4_), channel_id=1, source_target_pairs={{0,4},{4,0},{8,12},{12,8},{1,5},{5,1},{9,13},{13,9},{2,6},{6,2},{1... | collective-permute-start | bytes 1572872 | tf_op jit(solution)/shard_map/tokens_2_1/ppermute | solution.py:101
  115.3 3.3 %collective-permute-start.22 = (bf16[528,1024]{1,0:T(8,128)(2,1)}, bf16[528,1024]{1,0:T(8,128)(2,1)S(1)}, u32[]{:S(2)}, u32[]{:S(2)}) collective-permute-start(bf16[528,1024]{1,0:T(8,128)(2,1)} %get-tuple-element.63), channel_id=1, source_target_pairs={{0,4},{4,0},{8,12},{12,8},{1,5},{5,1},{9,13},{13,9},{2,6},{6,2},{1... | collective-permute-start | bytes 3244040 | tf_op jit(solution)/shard_map/sums_3_1/ppermute | solution.py:101
  115.5 8.7 %collective-permute-start.21 = (bf16[512,1024]{1,0:T(8,128)(2,1)}, bf16[512,1024]{1,0:T(8,128)(2,1)}, u32[]{:S(2)}, u32[]{:S(2)}) collective-permute-start(bf16[512,1024]{1,0:T(8,128)(2,1)} %get-tuple-element.61), channel_id=1, source_target_pairs={{0,4},{4,0},{8,12},{12,8},{1,5},{5,1},{9,13},{13,9},{2,6},{6,2},{1... | collective-permute-start | bytes 3145736 | tf_op jit(solution)/shard_map/sums_2_1/ppermute | solution.py:101
  115.9 36.8 %collective-permute-start.30 = (bf16[512,1024]{1,0:T(8,128)(2,1)}, bf16[512,1024]{1,0:T(8,128)(2,1)}, u32[]{:S(2)}, u32[]{:S(2)}) collective-permute-start(bf16[512,1024]{1,0:T(8,128)(2,1)} %get-tuple-element.78), channel_id=1, source_target_pairs={{0,4},{4,0},{8,12},{12,8},{1,5},{5,1},{9,13},{13,9},{2,6},{6,2},{1... | collective-permute-start | bytes 3145736 | tf_op jit(solution)/shard_map/sums_1_1/ppermute | solution.py:101
  121.9 26.8 %collective-permute-start.23 = (bf16[272,1024]{1,0:T(8,128)(2,1)}, bf16[272,1024]{1,0:T(8,128)(2,1)S(1)}, u32[]{:S(2)}, u32[]{:S(2)}) collective-permute-start(bf16[272,1024]{1,0:T(8,128)(2,1)} %get-tuple-element.65), channel_id=1, source_target_pairs={{0,8},{4,12},{8,0},{12,4},{1,9},{5,13},{9,1},{13,5},{2,10},{6,14},... | collective-permute-start | bytes 1671176 | tf_op jit(solution)/shard_map/sums_3_2/ppermute | solution.py:101
  122.7 26.0 %collective-permute-start.24 = (bf16[512,512]{1,0:T(8,128)(2,1)}, bf16[512,512]{1,0:T(8,128)(2,1)S(1)}, u32[]{:S(2)}, u32[]{:S(2)}) collective-permute-start(bf16[512,512]{1,0:T(8,128)(2,1)} %get-tuple-element.66), channel_id=1, source_target_pairs={{0,2},{1,3},{2,0},{3,1},{4,6},{5,7},{6,4},{7,5},{8,10},{9,11},{10,... | collective-permute-start | bytes 1572872 | tf_op jit(solution)/shard_map/grads_2/ppermute | solution.py:101
  124.3 39.7 %collective-permute-start.29 = (bf16[512,1024]{1,0:T(8,128)(2,1)}, bf16[512,1024]{1,0:T(8,128)(2,1)}, u32[]{:S(2)}, u32[]{:S(2)}) collective-permute-start(bf16[512,1024]{1,0:T(8,128)(2,1)} %get-tuple-element.76), channel_id=1, source_target_pairs={{0,4},{4,0},{8,12},{12,8},{1,5},{5,1},{9,13},{13,9},{2,6},{6,2},{1... | collective-permute-start | bytes 3145736 | tf_op jit(solution)/shard_map/sums_0_1/ppermute | solution.py:101
  148.7 14.0 %collective-permute-start.25 = (bf16[256,1024]{1,0:T(8,128)(2,1)}, bf16[256,1024]{1,0:T(8,128)(2,1)}, u32[]{:S(2)}, u32[]{:S(2)}) collective-permute-start(bf16[256,1024]{1,0:T(8,128)(2,1)} %add_convert_fusion.3), channel_id=1, source_target_pairs={{0,8},{4,12},{8,0},{12,4},{1,9},{5,13},{9,1},{13,5},{2,10},{6,14},... | collective-permute-start | bytes 1572872 | tf_op jit(solution)/shard_map/sums_2_2/ppermute | solution.py:101
  152.7 26.3 %collective-permute-start.26 = (bf16[272,1024]{1,0:T(8,128)(2,1)}, bf16[272,1024]{1,0:T(8,128)(2,1)S(1)}, u32[]{:S(2)}, u32[]{:S(2)}) collective-permute-start(bf16[272,1024]{1,0:T(8,128)(2,1)} %get-tuple-element.69), channel_id=1, source_target_pairs={{0,1},{1,0},{2,3},{3,2},{4,5},{5,4},{6,7},{7,6},{8,9},{9,8},{10,11... | collective-permute-start | bytes 1671176 | tf_op jit(solution)/shard_map/sums_3/ppermute | solution.py:101
  154.8 28.1 %collective-permute-start.28 = (bf16[512,512]{1,0:T(8,128)(2,1)}, bf16[512,512]{1,0:T(8,128)(2,1)S(1)}, u32[]{:S(2)}, u32[]{:S(2)}) collective-permute-start(bf16[512,512]{1,0:T(8,128)(2,1)} %get-tuple-element.74), channel_id=1, source_target_pairs={{0,3},{1,2},{2,1},{3,0},{4,7},{5,6},{6,5},{7,4},{8,11},{9,10},{10,... | collective-permute-start | bytes 1572872 | tf_op jit(solution)/shard_map/grads_3/ppermute | solution.py:101
  162.8 20.1 %collective-permute-start.31 = (bf16[256,1024]{1,0:T(8,128)(2,1)}, bf16[256,1024]{1,0:T(8,128)(2,1)}, u32[]{:S(2)}, u32[]{:S(2)}) collective-permute-start(bf16[256,1024]{1,0:T(8,128)(2,1)} %add_convert_fusion.1), channel_id=1, source_target_pairs={{0,8},{4,12},{8,0},{12,4},{1,9},{5,13},{9,1},{13,5},{2,10},{6,14},... | collective-permute-start | bytes 1572872 | tf_op jit(solution)/shard_map/sums_1_2/ppermute | solution.py:101
  182.8 24.2 %collective-permute-start.34 = (bf16[272,1024]{1,0:T(8,128)(2,1)}, bf16[272,1024]{1,0:T(8,128)(2,1)S(1)}, u32[]{:S(2)}, u32[]{:S(2)}) collective-permute-start(bf16[272,1024]{1,0:T(8,128)(2,1)} %get-tuple-element.71), channel_id=1, source_target_pairs={{0,2},{1,3},{2,0},{3,1},{4,6},{5,7},{6,4},{7,5},{8,10},{9,11},{10,... | collective-permute-start | bytes 1671176 | tf_op jit(solution)/shard_map/sums_2/ppermute | solution.py:101
  182.8 24.2 %collective-permute-start.27 = (bf16[512,512]{1,0:T(8,128)(2,1)}, bf16[512,512]{1,0:T(8,128)(2,1)S(1)}, u32[]{:S(2)}, u32[]{:S(2)}) collective-permute-start(bf16[512,512]{1,0:T(8,128)(2,1)} %get-tuple-element.72), channel_id=1, source_target_pairs={{0,1},{1,0},{2,3},{3,2},{4,5},{5,4},{6,7},{7,6},{8,9},{9,8},{10,11... | collective-permute-start | bytes 1572872 | tf_op jit(solution)/shard_map/grads_1/ppermute | solution.py:101
  182.9 24.1 %collective-permute-start.32 = (bf16[256,1024]{1,0:T(8,128)(2,1)}, bf16[256,1024]{1,0:T(8,128)(2,1)S(1)}, u32[]{:S(2)}, u32[]{:S(2)}) collective-permute-start(bf16[256,1024]{1,0:T(8,128)(2,1)} %add_convert_fusion.2), channel_id=1, source_target_pairs={{0,8},{4,12},{8,0},{12,4},{1,9},{5,13},{9,1},{13,5},{2,10},{6,14},... | collective-permute-start | bytes 1572872 | tf_op jit(solution)/shard_map/sums_0_2/ppermute | solution.py:101
  185.6 29.1 %collective-permute-start.33 = (bf16[256,1024]{1,0:T(8,128)(2,1)S(1)}, bf16[256,1024]{1,0:T(8,128)(2,1)S(1)}, u32[]{:S(2)}, u32[]{:S(2)}) collective-permute-start(bf16[256,1024]{1,0:T(8,128)(2,1)S(1)} %add_convert_fusion), channel_id=1, source_target_pairs={{0,1},{1,0},{2,3},{3,2},{4,5},{5,4},{6,7},{7,6},{8,9},{9,8},{10,11... | collective-permute-start | bytes 1572872 | tf_op jit(solution)/shard_map/sums_1/ppermute | solution.py:101
  (33 other events, 718.8 us)

commit v14 on v8

--- a/solution.py
+++ b/solution.py
@@ -104,39 +104,32 @@
     return [1 << b for b in reversed(range(size.bit_length() - 1))]
 
 
-def share(k, n_dp, mates):
-    return mates if k >= bits_of(n_dp)[0] else 1
-
-
-def pack_weights(w_up, w_down, mates):
-    n_dp = lax.axis_size("dp")
+def pack(first_out, grad_second, w_up, w_down, mates):
+    n_dp, (own_rows, width) = lax.axis_size("dp"), first_out.shape
     depth, units = w_up.shape[0], w_up.shape[1] // n_dp
-    strips = units // depth
-
-    def kernel(up_ref, down_ref, *sends):
+    strips, rows = units // depth, depth // mates
+
+    def kernel(first_ref, grad_ref, up_ref, down_ref, own, *sends):
         place, mate = lax.axis_index("dp"), lax.rem(lax.axis_index("groups"), mates)
+        own[:own_rows, :] = first_ref[...]
+        own[own_rows:, :] = grad_ref[...]
         for k in range(1, n_dp):
-            n = share(k, n_dp, mates)
-            part = mate if n > 1 else 0
-            rows = depth // n
             first = pl.multiple_of((place ^ k) * units, units)
             send = sends[k - 1]
-            send[:, :units] = up_ref[pl.ds(pl.multiple_of(part * rows, rows), rows), pl.ds(first, units)]
+            send[:, :units] = up_ref[pl.ds(pl.multiple_of(mate * rows, rows), rows), pl.ds(first, units)]
             for c in range(strips):
-                row = pl.multiple_of(first + part * (units // n) + c * rows, rows)
+                row = pl.multiple_of(first + mate * (units // mates) + c * rows, rows)
                 send[:, units + c * depth : units + (c + 1) * depth] = down_ref[pl.ds(row, rows), :]
 
     return pl.pallas_call(
         kernel,
-        out_shape=[
-            jax.ShapeDtypeStruct((depth // share(k, n_dp, mates), 2 * units), w_up.dtype)
-            for k in range(1, n_dp)
-        ],
-        in_specs=[pl.BlockSpec(memory_space=pltpu.VMEM)] * 2,
-        out_specs=[pl.BlockSpec(memory_space=pltpu.VMEM)] * (n_dp - 1),
+        out_shape=[jax.ShapeDtypeStruct((2 * own_rows, width), w_up.dtype)]
+        + [jax.ShapeDtypeStruct((rows, width), w_up.dtype)] * (n_dp - 1),
+        in_specs=[pl.BlockSpec(memory_space=pltpu.VMEM)] * 4,
+        out_specs=[pl.BlockSpec(memory_space=pltpu.VMEM)] * n_dp,
         cost_estimate=pl.CostEstimate(flops=0, bytes_accessed=8 * w_up.size, transcendentals=0),
-        name="pack_weights",
-    )(w_up, w_down)
+        name="pack",
+    )(first_out, grad_second, w_up, w_down)
 
 
 def core(chunks, w_up, w_down, got, mates, gain, bias):
@@ -385,7 +378,7 @@
     top = bits_of(n_dp)[0]
 
     high, others = bits_of(n_tensor)[0], bits_of(n_tensor)[1:]
-    own = jnp.concatenate([first_out, grad_second])
+    own, *sends = pack(first_out, grad_second, w_up, w_down, mates)
     tokens, chunks, got, crossed = {0: own}, {}, {}, {}
 
     def tokens_dp(k, *first):
@@ -401,37 +394,35 @@
                 piece = after(chunks[k][j], *first)
                 chunks[k][j | bit] = swap(piece, "tensor", bit, f"tokens_{k}_{j | bit}")
 
+    def weights_groups(k, *first):
+        if mates == 2:
+            crossed[k] = swap(after(got[k], *first), "groups", 1, f"weights_{k}")
+
     def weights_dp(k, *first):
         got[k] = swap(after(sends[k - 1], *first), "dp", k, f"weights_{k}")
 
-    def weights_groups(k, *first):
-        crossed[k] = swap(after(got[k], *first), "groups", 1, f"weights_{k}")
-
+    for bit in reversed(bits_of(n_dp)):
+        tokens_dp(bit)
     tokens_tensor(0)
-    for bit in bits_of(n_dp)[:0:-1]:
-        tokens_dp(bit)
-    sends = pack_weights(w_up, w_down, mates)
-    both = swap(jnp.concatenate([own, sends[top - 1]]), "dp", top, f"tokens_weights_{top}")
-    tokens[top], got[top] = both[: 2 * own_rows], both[2 * own_rows :]
-    for bit in bits_of(n_dp)[1:]:
-        weights_dp(bit)
-    tokens_tensor(1, tokens[1], chunks[0][high])
-    stage = [*tokens.values(), *got.values(), chunks[0][high]]
-    tokens_rest(0, *stage)
+    tokens_rest(0)
+    tokens_tensor(1, tokens[top], chunks[0][high])
+    stage = [*tokens.values(), *chunks[0].values()]
     for k in range(2, n_dp):
         if k & (k - 1):
             tokens_dp(k, *stage)
-            weights_dp(k, *stage)
-            if mates == 2 and top not in crossed:
-                weights_groups(top, *stage)
-            stage = [tokens[k], got[k], *crossed.values(), chunks[k - 1][high], *chunks[0].values()]
+        weights_dp(k, *stage, *([got[top]] if top in got else []))
+    for k in range(2, n_dp):
+        tokens_rest(k - 1)
+        stage = [got[top]]
+        if k & (k - 1):
+            weights_groups(top)
+            stage = [tokens[k], *got.values(), *crossed.values(), *chunks[k - 2].values()]
         tokens_tensor(k, *stage, chunks[k - 1][high])
-        tokens_rest(k - 1, *stage)
-    tokens_rest(n_dp - 1)
-    if mates == 2:
-        for k in range(top, n_dp):
-            if k not in crossed:
-                weights_groups(k)
+    weights_dp(1, *stage)
+    for k in [*range(2, n_dp), 1]:
+        if k not in crossed:
+            weights_groups(k)
+    tokens_rest(n_dp - 1, *crossed.values())
     got = {k: [got[k]] + ([crossed[k]] if k in crossed else []) for k in got}
 
     order = sorted(chunks, reverse=True)

time: 199 us -> 195 us (0.980)
  waiting for transfers between devices: 130 us -> 119 us
  starting transfers between devices: 25.3 us -> 35.2 us
  local copies, waits for them, and re-layouts: 3.18 us -> 1.01 us
    ppermute x35 -> x37, waiting for transfers between devices: 130 us -> 119 us  [swap(): lax.ppermute(values, axis, [(i, i ^ mask) for i in range(lax.axis_size(ax...]
    ppermute x35 -> x37, starting transfers between devices: 25.3 us -> 35.2 us  [swap(): lax.ppermute(values, axis, [(i, i ^ mask) for i in range(lax.axis_size(ax...]
  transfers between devices with their start and end apart: 35 -> 37, of which waited for: 19 -> 21; matrix products, arithmetic and copies ran while one was open for 4% -> 4% of each run, Pallas kernels for 1% -> 0%
where the time goes in v14:
time: 195 us
  waiting for transfers between devices  119 us (61%)
  starting transfers between devices  35.2 us (18%)
  Pallas kernels  31.2 us (16%)
  other arithmetic  7.27 us (4%)
    ppermute x37, waiting for transfers between devices, swap(): lax.ppermute(values, axis, [(i, i ^ mask) for i in range(lax.axis_size(ax...  119 us
    ppermute x37, starting transfers between devices, swap(): lax.ppermute(values, axis, [(i, i ^ mask) for i in range(lax.axis_size(ax...  35.2 us
    pallas_call x1, Pallas kernels, core(): pl.pallas_call(kernel, out_shape=[jax.ShapeDtypeStruct(half, dtype)] * (2...  24.5 us
  transfers between devices with their start and end apart: 37, of which 21 were waited for; matrix products, arithmetic and copies ran while one was open for 4% of the time, Pallas kernels for 0%

profile of v14, /device:TPU:0, one launch (start us, length us, event | category | flops | bytes accessed | tf_op | source)
XLA Modules:
  0.0 194.5 jit_solution(9892998406126358425)
XLA Ops:
  0.6 2.8 %pack.1 = (bf16[256,1024]{1,0:T(8,128)(2,1)}, bf16[128,1024]{1,0:T(8,128)(2,1)}, bf16[128,1024]{1,0:T(8,128)(2,1)}, bf16[128,1024]{1,0:T(8,128)(2,1)}) custom-call(bf16[128,1024]{1,0:T(8,128)(2,1)} %refs_10_.1, bf16[128,1024]{1,0:T(8,128)(2,1)} %grad_ref.1, bf16[256,2048]{1,0:T(8,128)(2,1)} %refs_16_.1, bf16[2048,256]{1,0:T(8,128)(2,1)} %refs_17_.1), custom_call_target="tpu_custom_call" | custom-call | bytes 4194304 | tf_op jit(solution)/shard_map/pack/pallas_call | solution.py:124
  3.4 3.0 %collective-permute-start.2 = (bf16[256,1024]{1,0:T(8,128)(2,1)}, bf16[256,1024]{1,0:T(8,128)(2,1)S(1)}, u32[]{:S(2)}, u32[]{:S(2)}) collective-permute-start(bf16[256,1024]{1,0:T(8,128)(2,1)} %get-tuple-element.38.refs_12_), channel_id=1, source_target_pairs={{0,8},{4,12},{8,0},{12,4},{1,9},{5,13},{9,1},{13,5},{2,10},{6,14},... | collective-permute-start | bytes 1572872 | tf_op jit(solution)/shard_map/tokens_0_2/ppermute | solution.py:100
  6.4 1.6 collective-permute-start.1
  8.0 2.6 %collective-permute-start = (bf16[256,1024]{1,0:T(8,128)(2,1)}, bf16[256,1024]{1,0:T(8,128)(2,1)S(1)}, u32[]{:S(2)}, u32[]{:S(2)}) collective-permute-start(bf16[256,1024]{1,0:T(8,128)(2,1)} %get-tuple-element.38.refs_12_), channel_id=1, source_target_pairs={{0,2},{1,3},{2,0},{3,1},{4,6},{5,7},{6,4},{7,5},{8,10},{9,11},{10,... | collective-permute-start | bytes 1572872 | tf_op jit(solution)/shard_map/tokens_2/ppermute | solution.py:100
  10.6 8.0 %collective-permute-done.2.refs_14_ = bf16[256,1024]{1,0:T(8,128)(2,1)S(1)} collective-permute-done((bf16[256,1024]{1,0:T(8,128)(2,1)}, bf16[256,1024]{1,0:T(8,128)(2,1)S(1)}, u32[]{:S(2)}, u32[]{:S(2)}) %collective-permute-start.2) | collective-permute-done | bytes 524320 | tf_op jit(solution)/shard_map/tokens_0_2/ppermute | solution.py:100
  18.5 12.6 %collective-permute-done.1.refs_8_ = bf16[256,1024]{1,0:T(8,128)(2,1)S(1)} collective-permute-done((bf16[256,1024]{1,0:T(8,128)(2,1)}, bf16[256,1024]{1,0:T(8,128)(2,1)S(1)}, u32[]{:S(2)}, u32[]{:S(2)}) %collective-permute-start.1) | collective-permute-done | bytes 524320 | tf_op jit(solution)/shard_map/tokens_1/ppermute | solution.py:100
  31.1 2.4 %collective-permute-done.refs_4_ = bf16[256,1024]{1,0:T(8,128)(2,1)S(1)} collective-permute-done((bf16[256,1024]{1,0:T(8,128)(2,1)}, bf16[256,1024]{1,0:T(8,128)(2,1)S(1)}, u32[]{:S(2)}, u32[]{:S(2)}) %collective-permute-start) | collective-permute-done | bytes 524320 | tf_op jit(solution)/shard_map/tokens_2/ppermute | solution.py:100
  34.4 2.7 %collective-permute-start.5 = (bf16[256,1024]{1,0:T(8,128)(2,1)S(1)}, bf16[256,1024]{1,0:T(8,128)(2,1)S(1)}, u32[]{:S(2)}, u32[]{:S(2)}) collective-permute-start(bf16[256,1024]{1,0:T(8,128)(2,1)S(1)} %collective-permute-done.refs_4_), channel_id=1, source_target_pairs={{0,1},{1,0},{2,3},{3,2},{4,5},{5,4},{6,7},{7,6},{8,9},{9,8},{10,11... | collective-permute-start | bytes 1572872 | tf_op jit(solution)/shard_map/tokens_3/ppermute | solution.py:100
  37.1 6.5 %collective-permute-done.10.refs_10_ = bf16[256,1024]{1,0:T(8,128)(2,1)S(1)} collective-permute-done((bf16[256,1024]{1,0:T(8,128)(2,1)S(1)}, bf16[256,1024]{1,0:T(8,128)(2,1)S(1)}, u32[]{:S(2)}, u32[]{:S(2)}) %collective-permute-start.10) | collective-permute-done | bytes 524320 | tf_op jit(solution)/shard_map/tokens_1_2/ppermute | solution.py:100
  43.6 5.9 %collective-permute-done.6.refs_20_ = bf16[128,1024]{1,0:T(8,128)(2,1)S(1)} collective-permute-done((bf16[128,1024]{1,0:T(8,128)(2,1)}, bf16[128,1024]{1,0:T(8,128)(2,1)S(1)}, u32[]{:S(2)}, u32[]{:S(2)}) %collective-permute-start.6) | collective-permute-done | bytes 262176 | tf_op jit(solution)/shard_map/weights_2/ppermute | solution.py:100
  49.5 1.5 collective-permute-start.16
  52.4 1.5 collective-permute-start.7
  55.0 6.0 %collective-permute-done.8.refs_22_ = bf16[128,1024]{1,0:T(8,128)(2,1)S(1)} collective-permute-done((bf16[128,1024]{1,0:T(8,128)(2,1)}, bf16[128,1024]{1,0:T(8,128)(2,1)S(1)}, u32[]{:S(2)}, u32[]{:S(2)}) %collective-permute-start.8) | collective-permute-done | bytes 262176 | tf_op jit(solution)/shard_map/weights_3/ppermute | solution.py:100
  61.1 2.4 %collective-permute-start.13 = (bf16[128,1024]{1,0:T(8,128)(2,1)}, bf16[128,1024]{1,0:T(8,128)(2,1)S(1)}, u32[]{:S(2)}, u32[]{:S(2)}) collective-permute-start(bf16[128,1024]{1,0:T(8,128)(2,1)} %get-tuple-element.46), channel_id=1, source_target_pairs={{0,1},{1,0},{2,3},{3,2},{4,5},{5,4},{6,7},{7,6},{8,9},{9,8},{10,11... | collective-permute-start | bytes 786440 | tf_op jit(solution)/shard_map/weights_1/ppermute | solution.py:100
  64.9 1.5 collective-permute-start.9
  66.4 2.7 %collective-permute-done.13.refs_18_ = bf16[128,1024]{1,0:T(8,128)(2,1)S(1)} collective-permute-done((bf16[128,1024]{1,0:T(8,128)(2,1)}, bf16[128,1024]{1,0:T(8,128)(2,1)S(1)}, u32[]{:S(2)}, u32[]{:S(2)}) %collective-permute-start.13) | collective-permute-done | bytes 262176 | tf_op jit(solution)/shard_map/weights_1/ppermute | solution.py:100
  69.1 1.5 collective-permute-start.14
  71.1 2.8 %collective-permute-done.9.refs_23_ = bf16[128,1024]{1,0:T(8,128)(2,1)S(1)} collective-permute-done((bf16[128,1024]{1,0:T(8,128)(2,1)S(1)}, bf16[128,1024]{1,0:T(8,128)(2,1)S(1)}, u32[]{:S(2)}, u32[]{:S(2)}) %collective-permute-start.9) | collective-permute-done | bytes 262176 | tf_op jit(solution)/shard_map/weights_3/ppermute | solution.py:100
  73.9 3.7 %collective-permute-done.14.refs_19_ = bf16[128,1024]{1,0:T(8,128)(2,1)S(1)} collective-permute-done((bf16[128,1024]{1,0:T(8,128)(2,1)S(1)}, bf16[128,1024]{1,0:T(8,128)(2,1)S(1)}, u32[]{:S(2)}, u32[]{:S(2)}) %collective-permute-start.14) | collective-permute-done | bytes 262176 | tf_op jit(solution)/shard_map/weights_1/ppermute | solution.py:100
  81.0 24.5 %core.1 = (bf16[512,1024]{1,0:T(8,128)(2,1)}, bf16[512,1024]{1,0:T(8,128)(2,1)}, bf16[512,1024]{1,0:T(8,128)(2,1)}, bf16[512,1024]{1,0:T(8,128)(2,1)}, bf16[512,...) custom-call(bf16[256,1024]{1,0:T(8,128)(2,1)} %copy-done.25, ...), custom_call_target="tpu_custom_call" | custom-call | flops 10737418240 | bytes 20971520 | tf_op jit(solution)/shard_map/core/pallas_call | solution.py:243
  107.1 1.5 collective-permute-done.21
  110.2 1.6 collective-permute-start.22
  112.8 11.1 %collective-permute-done.22 = f32[2,1024]{1,0:T(2,128)S(1)} collective-permute-done((f32[2,1024]{1,0:T(2,128)S(1)}, f32[2,1024]{1,0:T(2,128)S(1)}, u32[]{:S(2)}, u32[]{:S(2)}) %collective-permute-start.22) | collective-permute-done | bytes 8224 | tf_op jit(solution)/shard_map/stats/ppermute | solution.py:100
  127.6 10.9 %collective-permute-done.26 = bf16[256,1024]{1,0:T(8,128)(2,1)} collective-permute-done((bf16[256,1024]{1,0:T(8,128)(2,1)}, bf16[256,1024]{1,0:T(8,128)(2,1)}, u32[]{:S(2)}, u32[]{:S(2)}) %collective-permute-start.26) | collective-permute-done | bytes 524320 | tf_op jit(solution)/shard_map/sums_2_2/ppermute | solution.py:100
  140.3 2.2 %collective-permute-start.30 = (bf16[528,512]{1,0:T(8,128)(2,1)S(1)}, bf16[528,512]{1,0:T(8,128)(2,1)S(1)}, u32[]{:S(2)}, u32[]{:S(2)}) collective-permute-start(bf16[528,512]{1,0:T(8,128)(2,1)S(1)} %get-tuple-element.63), channel_id=1, source_target_pairs={{0,3},{1,2},{2,1},{3,0},{4,7},{5,6},{6,5},{7,4},{8,11},{9,10},{10,... | collective-permute-start | bytes 1622024 | tf_op jit(solution)/shard_map/grads_3/ppermute | solution.py:100
  143.2 1.7 add_convert_fusion.1
  145.5 2.5 %collective-permute-start.28 = (bf16[528,512]{1,0:T(8,128)(2,1)S(1)}, bf16[528,512]{1,0:T(8,128)(2,1)S(1)}, u32[]{:S(2)}, u32[]{:S(2)}) collective-permute-start(bf16[528,512]{1,0:T(8,128)(2,1)S(1)} %get-tuple-element.60), channel_id=1, source_target_pairs={{0,1},{1,0},{2,3},{3,2},{4,5},{5,4},{6,7},{7,6},{8,9},{9,8},{10,11... | collective-permute-start | bytes 1622024 | tf_op jit(solution)/shard_map/grads_1/ppermute | solution.py:100
  148.0 4.2 %collective-permute-done.33 = bf16[256,1024]{1,0:T(8,128)(2,1)S(1)} collective-permute-done((bf16[256,1024]{1,0:T(8,128)(2,1)}, bf16[256,1024]{1,0:T(8,128)(2,1)S(1)}, u32[]{:S(2)}, u32[]{:S(2)}) %collective-permute-start.33) | collective-permute-done | bytes 524320 | tf_op jit(solution)/shard_map/sums_1_2/ppermute | solution.py:100
  154.0 3.5 %collective-permute-done.30.refs_3_ = bf16[528,512]{1,0:T(8,128)(2,1)S(1)} collective-permute-done((bf16[528,512]{1,0:T(8,128)(2,1)S(1)}, bf16[528,512]{1,0:T(8,128)(2,1)S(1)}, u32[]{:S(2)}, u32[]{:S(2)}) %collective-permute-start.30) | collective-permute-done | bytes 540704 | tf_op jit(solution)/shard_map/grads_3/ppermute | solution.py:100
  157.5 21.4 %collective-permute-done.28.refs_1_ = bf16[528,512]{1,0:T(8,128)(2,1)S(1)} collective-permute-done((bf16[528,512]{1,0:T(8,128)(2,1)S(1)}, bf16[528,512]{1,0:T(8,128)(2,1)S(1)}, u32[]{:S(2)}, u32[]{:S(2)}) %collective-permute-start.28) | collective-permute-done | bytes 540704 | tf_op jit(solution)/shard_map/grads_1/ppermute | solution.py:100
  178.9 11.0 %collective-permute-done.36.refs_8_ = bf16[272,1024]{1,0:T(8,128)(2,1)S(1)} collective-permute-done((bf16[272,1024]{1,0:T(8,128)(2,1)S(1)}, bf16[272,1024]{1,0:T(8,128)(2,1)S(1)}, u32[]{:S(2)}, u32[]{:S(2)}) %collective-permute-start.36) | collective-permute-done | bytes 557088 | tf_op jit(solution)/shard_map/sums_2/ppermute | solution.py:100
  190.7 3.9 %finish.1 = (bf16[128,1024]{1,0:T(8,128)(2,1)}, f32[128,1024]{1,0:T(8,128)}, f32[256,2048]{1,0:T(8,128)}, f32[2048,256]{1,0:T(8,128)}, f32[2,1024]{1,0:T(2,128)}) custom-call(bf16[512,512]{1,0:T(8,128)(2,1)S(1)} %copy-done.2, bf16[528,512]{1,0:T(8,128)(2,1)S(1)} %collective-permute-done.28.refs_1_, bf16[512,512]{1,0:T(8,128)(2,1)S(1)} %collective-permute-done.29.refs_2_, ...), custom_call_target="tpu_custom_call" | custom-call | bytes 6291456 | tf_op jit(solution)/shard_map/finish/pallas_call | solution.py:352
  (135 shorter events, 21.9 us)
Async XLA Ops:
  3.4 15.1 %collective-permute-start.2 = (bf16[256,1024]{1,0:T(8,128)(2,1)}, bf16[256,1024]{1,0:T(8,128)(2,1)S(1)}, u32[]{:S(2)}, u32[]{:S(2)}) collective-permute-start(bf16[256,1024]{1,0:T(8,128)(2,1)} %get-tuple-element.38.refs_12_), channel_id=1, source_target_pairs={{0,8},{4,12},{8,0},{12,4},{1,9},{5,13},{9,1},{13,5},{2,10},{6,14},... | collective-permute-start | bytes 1572872 | tf_op jit(solution)/shard_map/tokens_0_2/ppermute | solution.py:100
  6.4 24.7 %collective-permute-start.1 = (bf16[256,1024]{1,0:T(8,128)(2,1)}, bf16[256,1024]{1,0:T(8,128)(2,1)S(1)}, u32[]{:S(2)}, u32[]{:S(2)}) collective-permute-start(bf16[256,1024]{1,0:T(8,128)(2,1)} %get-tuple-element.38.refs_12_), channel_id=1, source_target_pairs={{0,1},{1,0},{2,3},{3,2},{4,5},{5,4},{6,7},{7,6},{8,9},{9,8},{10,11... | collective-permute-start | bytes 1572872 | tf_op jit(solution)/shard_map/tokens_1/ppermute | solution.py:100
  8.0 25.5 %collective-permute-start = (bf16[256,1024]{1,0:T(8,128)(2,1)}, bf16[256,1024]{1,0:T(8,128)(2,1)S(1)}, u32[]{:S(2)}, u32[]{:S(2)}) collective-permute-start(bf16[256,1024]{1,0:T(8,128)(2,1)} %get-tuple-element.38.refs_12_), channel_id=1, source_target_pairs={{0,2},{1,3},{2,0},{3,1},{4,6},{5,7},{6,4},{7,5},{8,10},{9,11},{10,... | collective-permute-start | bytes 1572872 | tf_op jit(solution)/shard_map/tokens_2/ppermute | solution.py:100
  10.6 23.4 %collective-permute-start.3 = (bf16[256,1024]{1,0:T(8,128)(2,1)}, bf16[256,1024]{1,0:T(8,128)(2,1)S(1)}, u32[]{:S(2)}, u32[]{:S(2)}) collective-permute-start(bf16[256,1024]{1,0:T(8,128)(2,1)} %get-tuple-element.38.refs_12_), channel_id=1, source_target_pairs={{0,4},{4,0},{8,12},{12,8},{1,5},{5,1},{9,13},{13,9},{2,6},{6,2},{1... | collective-permute-start | bytes 1572872 | tf_op jit(solution)/shard_map/tokens_0_1/ppermute | solution.py:100
  18.5 15.5 %collective-permute-start.4 = (bf16[256,1024]{1,0:T(8,128)(2,1)S(1)}, bf16[256,1024]{1,0:T(8,128)(2,1)S(1)}, u32[]{:S(2)}, u32[]{:S(2)}) collective-permute-start(bf16[256,1024]{1,0:T(8,128)(2,1)S(1)} %collective-permute-done.2.refs_14_), channel_id=1, source_target_pairs={{0,4},{4,0},{8,12},{12,8},{1,5},{5,1},{9,13},{13,9},{2,6},{6,2},{1... | collective-permute-start | bytes 1572872 | tf_op jit(solution)/shard_map/tokens_0_3/ppermute | solution.py:100
  33.5 10.1 %collective-permute-start.10 = (bf16[256,1024]{1,0:T(8,128)(2,1)S(1)}, bf16[256,1024]{1,0:T(8,128)(2,1)S(1)}, u32[]{:S(2)}, u32[]{:S(2)}) collective-permute-start(bf16[256,1024]{1,0:T(8,128)(2,1)S(1)} %collective-permute-done.1.refs_8_), channel_id=1, source_target_pairs={{0,8},{4,12},{8,0},{12,4},{1,9},{5,13},{9,1},{13,5},{2,10},{6,14},... | collective-permute-start | bytes 1572872 | tf_op jit(solution)/shard_map/tokens_1_2/ppermute | solution.py:100
  34.0 18.4 %collective-permute-start.11 = (bf16[256,1024]{1,0:T(8,128)(2,1)S(1)}, bf16[256,1024]{1,0:T(8,128)(2,1)S(1)}, u32[]{:S(2)}, u32[]{:S(2)}) collective-permute-start(bf16[256,1024]{1,0:T(8,128)(2,1)S(1)} %collective-permute-done.1.refs_8_), channel_id=1, source_target_pairs={{0,4},{4,0},{8,12},{12,8},{1,5},{5,1},{9,13},{13,9},{2,6},{6,2},{1... | collective-permute-start | bytes 1572872 | tf_op jit(solution)/shard_map/tokens_1_1/ppermute | solution.py:100
  34.0 15.5 %collective-permute-start.6 = (bf16[128,1024]{1,0:T(8,128)(2,1)}, bf16[128,1024]{1,0:T(8,128)(2,1)S(1)}, u32[]{:S(2)}, u32[]{:S(2)}) collective-permute-start(bf16[128,1024]{1,0:T(8,128)(2,1)} %get-tuple-element.41), channel_id=1, source_target_pairs={{0,2},{1,3},{2,0},{3,1},{4,6},{5,7},{6,4},{7,5},{8,10},{9,11},{10,... | collective-permute-start | bytes 786440 | tf_op jit(solution)/shard_map/weights_2/ppermute | solution.py:100
  34.4 20.6 %collective-permute-start.5 = (bf16[256,1024]{1,0:T(8,128)(2,1)S(1)}, bf16[256,1024]{1,0:T(8,128)(2,1)S(1)}, u32[]{:S(2)}, u32[]{:S(2)}) collective-permute-start(bf16[256,1024]{1,0:T(8,128)(2,1)S(1)} %collective-permute-done.refs_4_), channel_id=1, source_target_pairs={{0,1},{1,0},{2,3},{3,2},{4,5},{5,4},{6,7},{7,6},{8,9},{9,8},{10,11... | collective-permute-start | bytes 1572872 | tf_op jit(solution)/shard_map/tokens_3/ppermute | solution.py:100
  43.6 11.4 %collective-permute-start.12 = (bf16[256,1024]{1,0:T(8,128)(2,1)S(1)}, bf16[256,1024]{1,0:T(8,128)(2,1)S(1)}, u32[]{:S(2)}, u32[]{:S(2)}) collective-permute-start(bf16[256,1024]{1,0:T(8,128)(2,1)S(1)} %collective-permute-done.10.refs_10_), channel_id=1, source_target_pairs={{0,4},{4,0},{8,12},{12,8},{1,5},{5,1},{9,13},{13,9},{2,6},{6,2},{1... | collective-permute-start | bytes 1572872 | tf_op jit(solution)/shard_map/tokens_1_3/ppermute | solution.py:100
  49.5 14.0 %collective-permute-start.16 = (bf16[256,1024]{1,0:T(8,128)(2,1)S(1)}, bf16[256,1024]{1,0:T(8,128)(2,1)S(1)}, u32[]{:S(2)}, u32[]{:S(2)}) collective-permute-start(bf16[256,1024]{1,0:T(8,128)(2,1)S(1)} %collective-permute-done.refs_4_), channel_id=1, source_target_pairs={{0,8},{4,12},{8,0},{12,4},{1,9},{5,13},{9,1},{13,5},{2,10},{6,14},... | collective-permute-start | bytes 1572872 | tf_op jit(solution)/shard_map/tokens_2_2/ppermute | solution.py:100
  51.0 10.1 %collective-permute-start.8 = (bf16[128,1024]{1,0:T(8,128)(2,1)}, bf16[128,1024]{1,0:T(8,128)(2,1)S(1)}, u32[]{:S(2)}, u32[]{:S(2)}) collective-permute-start(bf16[128,1024]{1,0:T(8,128)(2,1)} %get-tuple-element.43), channel_id=1, source_target_pairs={{0,3},{1,2},{2,1},{3,0},{4,7},{5,6},{6,5},{7,4},{8,11},{9,10},{10,... | collective-permute-start | bytes 786440 | tf_op jit(solution)/shard_map/weights_3/ppermute | solution.py:100
  52.4 8.7 %collective-permute-start.7 = (bf16[128,1024]{1,0:T(8,128)(2,1)S(1)}, bf16[128,1024]{1,0:T(8,128)(2,1)S(1)}, u32[]{:S(2)}, u32[]{:S(2)}) collective-permute-start(bf16[128,1024]{1,0:T(8,128)(2,1)S(1)} %collective-permute-done.6.refs_20_), channel_id=1, source_target_pairs={{0,16},{16,0},{1,17},{17,1},{2,18},{18,2},{3,19},{19,3},{4,20},{20... | collective-permute-start | bytes 786440 | tf_op jit(solution)/shard_map/weights_2/ppermute | solution.py:100
  61.1 8.0 %collective-permute-start.13 = (bf16[128,1024]{1,0:T(8,128)(2,1)}, bf16[128,1024]{1,0:T(8,128)(2,1)S(1)}, u32[]{:S(2)}, u32[]{:S(2)}) collective-permute-start(bf16[128,1024]{1,0:T(8,128)(2,1)} %get-tuple-element.46), channel_id=1, source_target_pairs={{0,1},{1,0},{2,3},{3,2},{4,5},{5,4},{6,7},{7,6},{8,9},{9,8},{10,11... | collective-permute-start | bytes 786440 | tf_op jit(solution)/shard_map/weights_1/ppermute | solution.py:100
  63.5 14.1 %collective-permute-start.17 = (bf16[256,1024]{1,0:T(8,128)(2,1)S(1)}, bf16[256,1024]{1,0:T(8,128)(2,1)S(1)}, u32[]{:S(2)}, u32[]{:S(2)}) collective-permute-start(bf16[256,1024]{1,0:T(8,128)(2,1)S(1)} %collective-permute-done.5.refs_0_), channel_id=1, source_target_pairs={{0,8},{4,12},{8,0},{12,4},{1,9},{5,13},{9,1},{13,5},{2,10},{6,14},... | collective-permute-start | bytes 1572872 | tf_op jit(solution)/shard_map/tokens_3_2/ppermute | solution.py:100
  64.9 9.0 %collective-permute-start.9 = (bf16[128,1024]{1,0:T(8,128)(2,1)S(1)}, bf16[128,1024]{1,0:T(8,128)(2,1)S(1)}, u32[]{:S(2)}, u32[]{:S(2)}) collective-permute-start(bf16[128,1024]{1,0:T(8,128)(2,1)S(1)} %collective-permute-done.8.refs_22_), channel_id=1, source_target_pairs={{0,16},{16,0},{1,17},{17,1},{2,18},{18,2},{3,19},{19,3},{4,20},{20... | collective-permute-start | bytes 786440 | tf_op jit(solution)/shard_map/weights_3/ppermute | solution.py:100
  69.1 8.5 %collective-permute-start.14 = (bf16[128,1024]{1,0:T(8,128)(2,1)S(1)}, bf16[128,1024]{1,0:T(8,128)(2,1)S(1)}, u32[]{:S(2)}, u32[]{:S(2)}) collective-permute-start(bf16[128,1024]{1,0:T(8,128)(2,1)S(1)} %collective-permute-done.13.refs_18_), channel_id=1, source_target_pairs={{0,16},{16,0},{1,17},{17,1},{2,18},{18,2},{3,19},{19,3},{4,20},{20... | collective-permute-start | bytes 786440 | tf_op jit(solution)/shard_map/weights_1/ppermute | solution.py:100
  70.6 7.6 %collective-permute-start.19 = (bf16[256,1024]{1,0:T(8,128)(2,1)S(1)}, bf16[256,1024]{1,0:T(8,128)(2,1)S(1)}, u32[]{:S(2)}, u32[]{:S(2)}) collective-permute-start(bf16[256,1024]{1,0:T(8,128)(2,1)S(1)} %collective-permute-done.refs_4_), channel_id=1, source_target_pairs={{0,4},{4,0},{8,12},{12,8},{1,5},{5,1},{9,13},{13,9},{2,6},{6,2},{1... | collective-permute-start | bytes 1572872 | tf_op jit(solution)/shard_map/tokens_2_1/ppermute | solution.py:100
  70.6 7.6 %collective-permute-start.20 = (bf16[256,1024]{1,0:T(8,128)(2,1)S(1)}, bf16[256,1024]{1,0:T(8,128)(2,1)S(1)}, u32[]{:S(2)}, u32[]{:S(2)}) collective-permute-start(bf16[256,1024]{1,0:T(8,128)(2,1)S(1)} %collective-permute-done.16.refs_6_), channel_id=1, source_target_pairs={{0,4},{4,0},{8,12},{12,8},{1,5},{5,1},{9,13},{13,9},{2,6},{6,2},{1... | collective-permute-start | bytes 1572872 | tf_op jit(solution)/shard_map/tokens_2_3/ppermute | solution.py:100
  106.2 6.5 %collective-permute-start.31 = (bf16[512,1024]{1,0:T(8,128)(2,1)}, bf16[512,1024]{1,0:T(8,128)(2,1)S(1)}, u32[]{:S(2)}, u32[]{:S(2)}) collective-permute-start(bf16[512,1024]{1,0:T(8,128)(2,1)} %get-tuple-element.65), channel_id=1, source_target_pairs={{0,4},{4,0},{8,12},{12,8},{1,5},{5,1},{9,13},{13,9},{2,6},{6,2},{1... | collective-permute-start | bytes 3145736 | tf_op jit(solution)/shard_map/sums_0_1/ppermute | solution.py:100
  106.3 34.0 %collective-permute-start.29 = (bf16[512,512]{1,0:T(8,128)(2,1)}, bf16[512,512]{1,0:T(8,128)(2,1)S(1)}, u32[]{:S(2)}, u32[]{:S(2)}) collective-permute-start(bf16[512,512]{1,0:T(8,128)(2,1)} %get-tuple-element.61), channel_id=1, source_target_pairs={{0,2},{1,3},{2,0},{3,1},{4,6},{5,7},{6,4},{7,5},{8,10},{9,11},{10,... | collective-permute-start | bytes 1572872 | tf_op jit(solution)/shard_map/grads_2/ppermute | solution.py:100
  107.0 19.5 %collective-permute-start.32 = (bf16[512,1024]{1,0:T(8,128)(2,1)}, bf16[512,1024]{1,0:T(8,128)(2,1)S(1)}, u32[]{:S(2)}, u32[]{:S(2)}) collective-permute-start(bf16[512,1024]{1,0:T(8,128)(2,1)} %get-tuple-element.67), channel_id=1, source_target_pairs={{0,4},{4,0},{8,12},{12,8},{1,5},{5,1},{9,13},{13,9},{2,6},{6,2},{1... | collective-permute-start | bytes 3145736 | tf_op jit(solution)/shard_map/sums_1_1/ppermute | solution.py:100
  109.7 14.2 %collective-permute-start.25 = (bf16[256,1024]{1,0:T(8,128)(2,1)S(1)}, bf16[256,1024]{1,0:T(8,128)(2,1)S(1)}, u32[]{:S(2)}, u32[]{:S(2)}) collective-permute-start(bf16[256,1024]{1,0:T(8,128)(2,1)S(1)} %slice_add_fusion.3), channel_id=1, source_target_pairs={{0,8},{4,12},{8,0},{12,4},{1,9},{5,13},{9,1},{13,5},{2,10},{6,14},... | collective-permute-start | bytes 1572872 | tf_op jit(solution)/shard_map/sums_3_2/ppermute | solution.py:100
  110.2 13.6 %collective-permute-start.22 = (f32[2,1024]{1,0:T(2,128)S(1)}, f32[2,1024]{1,0:T(2,128)S(1)}, u32[]{:S(2)}, u32[]{:S(2)}) collective-permute-start(f32[2,1024]{1,0:T(2,128)S(1)} %copy-done.17), channel_id=1, source_target_pairs={{0,8},{4,12},{8,0},{12,4},{1,9},{5,13},{9,1},{13,5},{2,10},{6,14},... | collective-permute-start | bytes 24584 | tf_op jit(solution)/shard_map/stats/ppermute | solution.py:100
  123.9 14.7 %collective-permute-start.26 = (bf16[256,1024]{1,0:T(8,128)(2,1)}, bf16[256,1024]{1,0:T(8,128)(2,1)}, u32[]{:S(2)}, u32[]{:S(2)}) collective-permute-start(bf16[256,1024]{1,0:T(8,128)(2,1)} %slice_add_fusion.2), channel_id=1, source_target_pairs={{0,8},{4,12},{8,0},{12,4},{1,9},{5,13},{9,1},{13,5},{2,10},{6,14},... | collective-permute-start | bytes 1572872 | tf_op jit(solution)/shard_map/sums_2_2/ppermute | solution.py:100
  125.5 17.7 %collective-permute-start.27 = (bf16[256,1024]{1,0:T(8,128)(2,1)}, bf16[256,1024]{1,0:T(8,128)(2,1)}, u32[]{:S(2)}, u32[]{:S(2)}) collective-permute-start(bf16[256,1024]{1,0:T(8,128)(2,1)} %add_convert_fusion.2), channel_id=1, source_target_pairs={{0,1},{1,0},{2,3},{3,2},{4,5},{5,4},{6,7},{7,6},{8,9},{9,8},{10,11... | collective-permute-start | bytes 1572872 | tf_op jit(solution)/shard_map/sums_3/ppermute | solution.py:100
  138.5 13.7 %collective-permute-start.33 = (bf16[256,1024]{1,0:T(8,128)(2,1)}, bf16[256,1024]{1,0:T(8,128)(2,1)S(1)}, u32[]{:S(2)}, u32[]{:S(2)}) collective-permute-start(bf16[256,1024]{1,0:T(8,128)(2,1)} %slice_add_fusion), channel_id=1, source_target_pairs={{0,8},{4,12},{8,0},{12,4},{1,9},{5,13},{9,1},{13,5},{2,10},{6,14},... | collective-permute-start | bytes 1572872 | tf_op jit(solution)/shard_map/sums_1_2/ppermute | solution.py:100
  140.3 17.2 %collective-permute-start.30 = (bf16[528,512]{1,0:T(8,128)(2,1)S(1)}, bf16[528,512]{1,0:T(8,128)(2,1)S(1)}, u32[]{:S(2)}, u32[]{:S(2)}) collective-permute-start(bf16[528,512]{1,0:T(8,128)(2,1)S(1)} %get-tuple-element.63), channel_id=1, source_target_pairs={{0,3},{1,2},{2,1},{3,0},{4,7},{5,6},{6,5},{7,4},{8,11},{9,10},{10,... | collective-permute-start | bytes 1622024 | tf_op jit(solution)/shard_map/grads_3/ppermute | solution.py:100
  145.0 44.9 %collective-permute-start.36 = (bf16[272,1024]{1,0:T(8,128)(2,1)S(1)}, bf16[272,1024]{1,0:T(8,128)(2,1)S(1)}, u32[]{:S(2)}, u32[]{:S(2)}) collective-permute-start(bf16[272,1024]{1,0:T(8,128)(2,1)S(1)} %fusion.2), channel_id=1, source_target_pairs={{0,2},{1,3},{2,0},{3,1},{4,6},{5,7},{6,4},{7,5},{8,10},{9,11},{10,... | collective-permute-start | bytes 1671176 | tf_op jit(solution)/shard_map/sums_2/ppermute | solution.py:100
  145.5 33.3 %collective-permute-start.28 = (bf16[528,512]{1,0:T(8,128)(2,1)S(1)}, bf16[528,512]{1,0:T(8,128)(2,1)S(1)}, u32[]{:S(2)}, u32[]{:S(2)}) collective-permute-start(bf16[528,512]{1,0:T(8,128)(2,1)S(1)} %get-tuple-element.60), channel_id=1, source_target_pairs={{0,1},{1,0},{2,3},{3,2},{4,5},{5,4},{6,7},{7,6},{8,9},{9,8},{10,11... | collective-permute-start | bytes 1622024 | tf_op jit(solution)/shard_map/grads_1/ppermute | solution.py:100
  152.5 37.4 %collective-permute-start.34 = (bf16[256,1024]{1,0:T(8,128)(2,1)S(1)}, bf16[256,1024]{1,0:T(8,128)(2,1)S(1)}, u32[]{:S(2)}, u32[]{:S(2)}) collective-permute-start(bf16[256,1024]{1,0:T(8,128)(2,1)S(1)} %slice_add_fusion.1), channel_id=1, source_target_pairs={{0,8},{4,12},{8,0},{12,4},{1,9},{5,13},{9,1},{13,5},{2,10},{6,14},... | collective-permute-start | bytes 1572872 | tf_op jit(solution)/shard_map/sums_0_2/ppermute | solution.py:100
  153.1 37.5 %collective-permute-start.35 = (bf16[256,1024]{1,0:T(8,128)(2,1)S(1)}, bf16[256,1024]{1,0:T(8,128)(2,1)S(1)}, u32[]{:S(2)}, u32[]{:S(2)}) collective-permute-start(bf16[256,1024]{1,0:T(8,128)(2,1)S(1)} %add_convert_fusion), channel_id=1, source_target_pairs={{0,1},{1,0},{2,3},{3,2},{4,5},{5,4},{6,7},{7,6},{8,9},{9,8},{10,11... | collective-permute-start | bytes 1572872 | tf_op jit(solution)/shard_map/sums_1/ppermute | solution.py:100
  (44 other events, 855.3 us)

commit v15 on v14

--- a/solution.py
+++ b/solution.py
@@ -283,7 +283,7 @@
 def finish(blocks, terms, own_stats, first_out, second_out, grad_first, gain, bias, w_shapes, scale):
     (rows, width), n_dp = first_out.shape, len(blocks)
     depth, units = w_shapes[0][0], w_shapes[0][1] // n_dp
-    strips, top, n_terms = units // depth, bits_of(n_dp)[0], len(terms)
+    strips, n_bits, n_terms = units // depth, len(bits_of(n_dp)), len(terms)
 
     def kernel(*refs):
         parts, adds, (stat_ref, first_ref, second_ref, grad_ref, gain_ref, bias_ref), outs = (
@@ -318,8 +318,8 @@
         for k in range(n_dp):
             if k == 0:
                 one = stat_ref[...].astype(jnp.float32)
-            elif k == top:
-                one = adds[-1][2 * rows :, :].astype(jnp.float32)[:2]
+            elif k & (k - 1) == 0:
+                one = adds[n_terms - n_bits + k.bit_length() - 1][2 * rows :, :].astype(jnp.float32)[:2]
             else:
                 tail = parts[k][2 * depth :, :].astype(jnp.float32)
                 per = width // units
@@ -340,7 +340,7 @@
 
     arrays = [*blocks, *terms, own_stats, first_out, second_out, grad_first, gain.reshape(1, width), bias.reshape(1, width)]
     in_specs = [whole(x) for x in arrays]
-    for i in range(n_terms - 1):
+    for i in range(n_terms - n_bits):
         in_specs[n_dp + i] = pl.BlockSpec((2 * rows, width), lambda i: (0, 0))
     out_shape = [
         jax.ShapeDtypeStruct((rows, width), second_out.dtype),
@@ -430,7 +430,8 @@
         [[chunks[k][j] for j in range(n_tensor)] for k in order], w_up, w_down, got, mates, norm_gain, norm_bias
     )
     blocks = dict(enumerate(blocks))
-    blocks[top] = swap(blocks[top], "dp", top, f"grads_{top}")
+    for bit in bits_of(n_dp):
+        blocks[bit] = swap(blocks[bit], "dp", bit, f"grads_{bit}")
 
     sums, behind, hops = {}, (), []
     for k, (even, odd) in zip(order, halves, strict=True):
@@ -443,7 +444,10 @@
                 send = after(sum(parts.pop(j)), *behind)
                 if not hops:
                     stats = after(stats, send)
-                parts[j ^ bit] += (swap(send, "tensor", bit, f"sums_{k}_{j}"),)
+                came = swap(send, "tensor", bit, f"sums_{k}_{j}")
+                if k == top:
+                    came = after(came, blocks[top])
+                parts[j ^ bit] += (came,)
                 behind = parts[j ^ bit][-1:]
                 hops += behind
         sums[k] = parts[0]
@@ -466,12 +470,13 @@
     rows = stats.reshape(-1, units)
     rows = jnp.pad(rows, ((0, extra - rows.shape[0]), (0, 0)))
     for k in range(1, n_dp):
-        if k != top:
+        if k & (k - 1):
             block = jnp.concatenate([blocks[k], rows])
-            first = [last] if k < top else [blocks[top], *hops[:1]]
-            blocks[k] = swap(after(block, *first), "dp", k, f"grads_{k}")
+            block = after(block, blocks[top], *hops[:1])
+            blocks[k] = swap(block, "dp", k, f"grads_{k}")
     for bit in bits_of(n_dp)[:0:-1]:
-        came[bit] = swap(after(add(sums[bit]), last), "dp", bit, f"sums_{bit}")
+        send = jnp.concatenate([add(sums[bit]), jnp.pad(after(stats, last), ((0, extra - 2), (0, 0)))])
+        came[bit] = swap(send, "dp", bit, f"sums_{bit}")
 
     scale = (own_rows * n_tensor * n_dp) ** (-0.5)
     terms = [*sums[0], *(came[bit] for bit in bits_of(n_dp)[::-1])]

time: 195 us -> 193 us (0.990)
  transfers between devices with their start and end apart: 37 -> 37, of which waited for: 21 -> 20; matrix products, arithmetic and copies ran while one was open for 4% -> 4% of each run, Pallas kernels for 0% -> 0%
where the time goes in v15:
time: 193 us
  waiting for transfers between devices  119 us (62%)
  starting transfers between devices  33.6 us (17%)
  Pallas kernels  31.2 us (16%)
  other arithmetic  7.21 us (4%)
    ppermute x37, waiting for transfers between devices, swap(): lax.ppermute(values, axis, [(i, i ^ mask) for i in range(lax.axis_size(ax...  119 us
    ppermute x37, starting transfers between devices, swap(): lax.ppermute(values, axis, [(i, i ^ mask) for i in range(lax.axis_size(ax...  33.6 us
    pallas_call x1, Pallas kernels, core(): pl.pallas_call(kernel, out_shape=[jax.ShapeDtypeStruct(half, dtype)] * (2...  24.5 us
    pallas_call x1, Pallas kernels, finish(): pl.pallas_call(kernel, out_shape=out_shape, grid=(1,), in_specs=in_specs,...  3.86 us
  transfers between devices with their start and end apart: 37, of which 20 were waited for; matrix products, arithmetic and copies ran while one was open for 4% of the time, Pallas kernels for 0%

profile of v15, /device:TPU:0, one launch (start us, length us, event | category | flops | bytes accessed | tf_op | source)
XLA Modules:
  0.0 192.6 jit_solution(18342392041334263783)
XLA Ops:
  0.6 2.8 %pack.1 = (bf16[256,1024]{1,0:T(8,128)(2,1)}, bf16[128,1024]{1,0:T(8,128)(2,1)}, bf16[128,1024]{1,0:T(8,128)(2,1)}, bf16[128,1024]{1,0:T(8,128)(2,1)}) custom-call(bf16[128,1024]{1,0:T(8,128)(2,1)} %refs_10_.1, bf16[128,1024]{1,0:T(8,128)(2,1)} %grad_ref.1, bf16[256,2048]{1,0:T(8,128)(2,1)} %refs_16_.1, bf16[2048,256]{1,0:T(8,128)(2,1)} %refs_17_.1), custom_call_target="tpu_custom_call" | custom-call | bytes 4194304 | tf_op jit(solution)/shard_map/pack/pallas_call | solution.py:124
  3.4 3.0 %collective-permute-start.2 = (bf16[256,1024]{1,0:T(8,128)(2,1)}, bf16[256,1024]{1,0:T(8,128)(2,1)S(1)}, u32[]{:S(2)}, u32[]{:S(2)}) collective-permute-start(bf16[256,1024]{1,0:T(8,128)(2,1)} %get-tuple-element.38.refs_12_), channel_id=1, source_target_pairs={{0,8},{4,12},{8,0},{12,4},{1,9},{5,13},{9,1},{13,5},{2,10},{6,14},... | collective-permute-start | bytes 1572872 | tf_op jit(solution)/shard_map/tokens_0_2/ppermute | solution.py:100
  6.4 1.6 collective-permute-start.1
  8.0 2.6 %collective-permute-start = (bf16[256,1024]{1,0:T(8,128)(2,1)}, bf16[256,1024]{1,0:T(8,128)(2,1)S(1)}, u32[]{:S(2)}, u32[]{:S(2)}) collective-permute-start(bf16[256,1024]{1,0:T(8,128)(2,1)} %get-tuple-element.38.refs_12_), channel_id=1, source_target_pairs={{0,2},{1,3},{2,0},{3,1},{4,6},{5,7},{6,4},{7,5},{8,10},{9,11},{10,... | collective-permute-start | bytes 1572872 | tf_op jit(solution)/shard_map/tokens_2/ppermute | solution.py:100
  10.6 8.0 %collective-permute-done.2.refs_14_ = bf16[256,1024]{1,0:T(8,128)(2,1)S(1)} collective-permute-done((bf16[256,1024]{1,0:T(8,128)(2,1)}, bf16[256,1024]{1,0:T(8,128)(2,1)S(1)}, u32[]{:S(2)}, u32[]{:S(2)}) %collective-permute-start.2) | collective-permute-done | bytes 524320 | tf_op jit(solution)/shard_map/tokens_0_2/ppermute | solution.py:100
  18.5 12.6 %collective-permute-done.1.refs_8_ = bf16[256,1024]{1,0:T(8,128)(2,1)S(1)} collective-permute-done((bf16[256,1024]{1,0:T(8,128)(2,1)}, bf16[256,1024]{1,0:T(8,128)(2,1)S(1)}, u32[]{:S(2)}, u32[]{:S(2)}) %collective-permute-start.1) | collective-permute-done | bytes 524320 | tf_op jit(solution)/shard_map/tokens_1/ppermute | solution.py:100
  31.1 2.4 %collective-permute-done.refs_4_ = bf16[256,1024]{1,0:T(8,128)(2,1)S(1)} collective-permute-done((bf16[256,1024]{1,0:T(8,128)(2,1)}, bf16[256,1024]{1,0:T(8,128)(2,1)S(1)}, u32[]{:S(2)}, u32[]{:S(2)}) %collective-permute-start) | collective-permute-done | bytes 524320 | tf_op jit(solution)/shard_map/tokens_2/ppermute | solution.py:100
  34.4 2.7 %collective-permute-start.5 = (bf16[256,1024]{1,0:T(8,128)(2,1)S(1)}, bf16[256,1024]{1,0:T(8,128)(2,1)S(1)}, u32[]{:S(2)}, u32[]{:S(2)}) collective-permute-start(bf16[256,1024]{1,0:T(8,128)(2,1)S(1)} %collective-permute-done.refs_4_), channel_id=1, source_target_pairs={{0,1},{1,0},{2,3},{3,2},{4,5},{5,4},{6,7},{7,6},{8,9},{9,8},{10,11... | collective-permute-start | bytes 1572872 | tf_op jit(solution)/shard_map/tokens_3/ppermute | solution.py:100
  37.1 6.5 %collective-permute-done.10.refs_10_ = bf16[256,1024]{1,0:T(8,128)(2,1)S(1)} collective-permute-done((bf16[256,1024]{1,0:T(8,128)(2,1)S(1)}, bf16[256,1024]{1,0:T(8,128)(2,1)S(1)}, u32[]{:S(2)}, u32[]{:S(2)}) %collective-permute-start.10) | collective-permute-done | bytes 524320 | tf_op jit(solution)/shard_map/tokens_1_2/ppermute | solution.py:100
  43.6 5.9 %collective-permute-done.6.refs_20_ = bf16[128,1024]{1,0:T(8,128)(2,1)S(1)} collective-permute-done((bf16[128,1024]{1,0:T(8,128)(2,1)}, bf16[128,1024]{1,0:T(8,128)(2,1)S(1)}, u32[]{:S(2)}, u32[]{:S(2)}) %collective-permute-start.6) | collective-permute-done | bytes 262176 | tf_op jit(solution)/shard_map/weights_2/ppermute | solution.py:100
  49.5 1.5 collective-permute-start.16
  52.4 1.5 collective-permute-start.7
  55.0 6.0 %collective-permute-done.8.refs_22_ = bf16[128,1024]{1,0:T(8,128)(2,1)S(1)} collective-permute-done((bf16[128,1024]{1,0:T(8,128)(2,1)}, bf16[128,1024]{1,0:T(8,128)(2,1)S(1)}, u32[]{:S(2)}, u32[]{:S(2)}) %collective-permute-start.8) | collective-permute-done | bytes 262176 | tf_op jit(solution)/shard_map/weights_3/ppermute | solution.py:100
  61.1 2.4 %collective-permute-start.13 = (bf16[128,1024]{1,0:T(8,128)(2,1)}, bf16[128,1024]{1,0:T(8,128)(2,1)S(1)}, u32[]{:S(2)}, u32[]{:S(2)}) collective-permute-start(bf16[128,1024]{1,0:T(8,128)(2,1)} %get-tuple-element.46), channel_id=1, source_target_pairs={{0,1},{1,0},{2,3},{3,2},{4,5},{5,4},{6,7},{7,6},{8,9},{9,8},{10,11... | collective-permute-start | bytes 786440 | tf_op jit(solution)/shard_map/weights_1/ppermute | solution.py:100
  64.9 1.5 collective-permute-start.9
  66.4 2.7 %collective-permute-done.13.refs_18_ = bf16[128,1024]{1,0:T(8,128)(2,1)S(1)} collective-permute-done((bf16[128,1024]{1,0:T(8,128)(2,1)}, bf16[128,1024]{1,0:T(8,128)(2,1)S(1)}, u32[]{:S(2)}, u32[]{:S(2)}) %collective-permute-start.13) | collective-permute-done | bytes 262176 | tf_op jit(solution)/shard_map/weights_1/ppermute | solution.py:100
  71.1 2.8 %collective-permute-done.9.refs_23_ = bf16[128,1024]{1,0:T(8,128)(2,1)S(1)} collective-permute-done((bf16[128,1024]{1,0:T(8,128)(2,1)S(1)}, bf16[128,1024]{1,0:T(8,128)(2,1)S(1)}, u32[]{:S(2)}, u32[]{:S(2)}) %collective-permute-start.9) | collective-permute-done | bytes 262176 | tf_op jit(solution)/shard_map/weights_3/ppermute | solution.py:100
  73.9 3.7 %collective-permute-done.14.refs_19_ = bf16[128,1024]{1,0:T(8,128)(2,1)S(1)} collective-permute-done((bf16[128,1024]{1,0:T(8,128)(2,1)S(1)}, bf16[128,1024]{1,0:T(8,128)(2,1)S(1)}, u32[]{:S(2)}, u32[]{:S(2)}) %collective-permute-start.14) | collective-permute-done | bytes 262176 | tf_op jit(solution)/shard_map/weights_1/ppermute | solution.py:100
  81.0 24.5 %core.1 = (bf16[512,1024]{1,0:T(8,128)(2,1)}, bf16[512,1024]{1,0:T(8,128)(2,1)}, bf16[512,1024]{1,0:T(8,128)(2,1)}, bf16[512,1024]{1,0:T(8,128)(2,1)}, bf16[512,...) custom-call(bf16[256,1024]{1,0:T(8,128)(2,1)} %copy-done.24, ...), custom_call_target="tpu_custom_call" | custom-call | flops 10737418240 | bytes 20971520 | tf_op jit(solution)/shard_map/core/pallas_call | solution.py:243
  106.3 2.2 %collective-permute-done.23 = bf16[512,1024]{1,0:T(8,128)(2,1)S(1)} collective-permute-done((bf16[512,1024]{1,0:T(8,128)(2,1)}, bf16[512,1024]{1,0:T(8,128)(2,1)S(1)}, u32[]{:S(2)}, u32[]{:S(2)}) %collective-permute-start.23) | collective-permute-done | bytes 1048608 | tf_op jit(solution)/shard_map/sums_3_1/ppermute | solution.py:100
  110.2 2.7 %collective-permute-start.22 = (bf16[512,512]{1,0:T(8,128)(2,1)}, bf16[512,512]{1,0:T(8,128)(2,1)S(1)}, u32[]{:S(2)}, u32[]{:S(2)}) collective-permute-start(bf16[512,512]{1,0:T(8,128)(2,1)} %get-tuple-element.53), channel_id=1, source_target_pairs={{0,2},{1,3},{2,0},{3,1},{4,6},{5,7},{6,4},{7,5},{8,10},{9,11},{10,... | collective-permute-start | bytes 1572872 | tf_op jit(solution)/shard_map/grads_2/ppermute | solution.py:100
  114.6 9.2 %collective-permute-done.24 = f32[2,1024]{1,0:T(2,128)S(1)} collective-permute-done((f32[2,1024]{1,0:T(2,128)S(1)}, f32[2,1024]{1,0:T(2,128)S(1)}, u32[]{:S(2)}, u32[]{:S(2)}) %collective-permute-start.24) | collective-permute-done | bytes 8224 | tf_op jit(solution)/shard_map/stats/ppermute | solution.py:100
  126.9 8.7 %collective-permute-done.22.refs_2_ = bf16[512,512]{1,0:T(8,128)(2,1)S(1)} collective-permute-done((bf16[512,512]{1,0:T(8,128)(2,1)}, bf16[512,512]{1,0:T(8,128)(2,1)S(1)}, u32[]{:S(2)}, u32[]{:S(2)}) %collective-permute-start.22) | collective-permute-done | bytes 524320 | tf_op jit(solution)/shard_map/grads_2/ppermute | solution.py:100
  135.6 2.9 %collective-permute-done.31 = bf16[256,1024]{1,0:T(8,128)(2,1)} collective-permute-done((bf16[256,1024]{1,0:T(8,128)(2,1)}, bf16[256,1024]{1,0:T(8,128)(2,1)}, u32[]{:S(2)}, u32[]{:S(2)}) %collective-permute-start.31) | collective-permute-done | bytes 524320 | tf_op jit(solution)/shard_map/sums_2_2/ppermute | solution.py:100
  140.1 2.2 %collective-permute-start.27 = (bf16[528,512]{1,0:T(8,128)(2,1)S(1)}, bf16[528,512]{1,0:T(8,128)(2,1)S(1)}, u32[]{:S(2)}, u32[]{:S(2)}) collective-permute-start(bf16[528,512]{1,0:T(8,128)(2,1)S(1)} %fusion.5), channel_id=1, source_target_pairs={{0,3},{1,2},{2,1},{3,0},{4,7},{5,6},{6,5},{7,4},{8,11},{9,10},{10,... | collective-permute-start | bytes 1622024 | tf_op jit(solution)/shard_map/grads_3/ppermute | solution.py:100
  142.4 4.9 %collective-permute-done.34 = bf16[256,1024]{1,0:T(8,128)(2,1)} collective-permute-done((bf16[256,1024]{1,0:T(8,128)(2,1)}, bf16[256,1024]{1,0:T(8,128)(2,1)}, u32[]{:S(2)}, u32[]{:S(2)}) %collective-permute-start.34) | collective-permute-done | bytes 524320 | tf_op jit(solution)/shard_map/sums_3/ppermute | solution.py:100
  147.3 1.6 add_convert_fusion
  149.0 1.7 collective-permute-start.36
  150.7 1.5 collective-permute-done.32
  153.4 6.6 %collective-permute-done.27.refs_3_ = bf16[528,512]{1,0:T(8,128)(2,1)S(1)} collective-permute-done((bf16[528,512]{1,0:T(8,128)(2,1)S(1)}, bf16[528,512]{1,0:T(8,128)(2,1)S(1)}, u32[]{:S(2)}, u32[]{:S(2)}) %collective-permute-start.27) | collective-permute-done | bytes 540704 | tf_op jit(solution)/shard_map/grads_3/ppermute | solution.py:100
  160.0 28.7 %collective-permute-done.36.refs_8_ = bf16[272,1024]{1,0:T(8,128)(2,1)S(1)} collective-permute-done((bf16[272,1024]{1,0:T(8,128)(2,1)S(1)}, bf16[272,1024]{1,0:T(8,128)(2,1)S(1)}, u32[]{:S(2)}, u32[]{:S(2)}) %collective-permute-start.36) | collective-permute-done | bytes 557088 | tf_op jit(solution)/shard_map/sums_2/ppermute | solution.py:100
  188.7 3.9 %finish.1 = (bf16[128,1024]{1,0:T(8,128)(2,1)}, f32[128,1024]{1,0:T(8,128)}, f32[256,2048]{1,0:T(8,128)}, f32[2048,256]{1,0:T(8,128)}, f32[2,1024]{1,0:T(2,128)}) custom-call(bf16[512,512]{1,0:T(8,128)(2,1)S(1)} %copy-done.2, bf16[512,512]{1,0:T(8,128)(2,1)S(1)} %collective-permute-done.21.refs_1_, bf16[512,512]{1,0:T(8,128)(2,1)S(1)} %collective-permute-done.22.refs_2_, ...), custom_call_target="tpu_custom_call" | custom-call | bytes 6291456 | tf_op jit(solution)/shard_map/finish/pallas_call | solution.py:352
  (134 shorter events, 19.8 us)
Async XLA Ops:
  3.4 15.1 %collective-permute-start.2 = (bf16[256,1024]{1,0:T(8,128)(2,1)}, bf16[256,1024]{1,0:T(8,128)(2,1)S(1)}, u32[]{:S(2)}, u32[]{:S(2)}) collective-permute-start(bf16[256,1024]{1,0:T(8,128)(2,1)} %get-tuple-element.38.refs_12_), channel_id=1, source_target_pairs={{0,8},{4,12},{8,0},{12,4},{1,9},{5,13},{9,1},{13,5},{2,10},{6,14},... | collective-permute-start | bytes 1572872 | tf_op jit(solution)/shard_map/tokens_0_2/ppermute | solution.py:100
  6.4 24.7 %collective-permute-start.1 = (bf16[256,1024]{1,0:T(8,128)(2,1)}, bf16[256,1024]{1,0:T(8,128)(2,1)S(1)}, u32[]{:S(2)}, u32[]{:S(2)}) collective-permute-start(bf16[256,1024]{1,0:T(8,128)(2,1)} %get-tuple-element.38.refs_12_), channel_id=1, source_target_pairs={{0,1},{1,0},{2,3},{3,2},{4,5},{5,4},{6,7},{7,6},{8,9},{9,8},{10,11... | collective-permute-start | bytes 1572872 | tf_op jit(solution)/shard_map/tokens_1/ppermute | solution.py:100
  8.0 25.5 %collective-permute-start = (bf16[256,1024]{1,0:T(8,128)(2,1)}, bf16[256,1024]{1,0:T(8,128)(2,1)S(1)}, u32[]{:S(2)}, u32[]{:S(2)}) collective-permute-start(bf16[256,1024]{1,0:T(8,128)(2,1)} %get-tuple-element.38.refs_12_), channel_id=1, source_target_pairs={{0,2},{1,3},{2,0},{3,1},{4,6},{5,7},{6,4},{7,5},{8,10},{9,11},{10,... | collective-permute-start | bytes 1572872 | tf_op jit(solution)/shard_map/tokens_2/ppermute | solution.py:100
  10.6 23.4 %collective-permute-start.3 = (bf16[256,1024]{1,0:T(8,128)(2,1)}, bf16[256,1024]{1,0:T(8,128)(2,1)S(1)}, u32[]{:S(2)}, u32[]{:S(2)}) collective-permute-start(bf16[256,1024]{1,0:T(8,128)(2,1)} %get-tuple-element.38.refs_12_), channel_id=1, source_target_pairs={{0,4},{4,0},{8,12},{12,8},{1,5},{5,1},{9,13},{13,9},{2,6},{6,2},{1... | collective-permute-start | bytes 1572872 | tf_op jit(solution)/shard_map/tokens_0_1/ppermute | solution.py:100
  18.5 15.5 %collective-permute-start.4 = (bf16[256,1024]{1,0:T(8,128)(2,1)S(1)}, bf16[256,1024]{1,0:T(8,128)(2,1)S(1)}, u32[]{:S(2)}, u32[]{:S(2)}) collective-permute-start(bf16[256,1024]{1,0:T(8,128)(2,1)S(1)} %collective-permute-done.2.refs_14_), channel_id=1, source_target_pairs={{0,4},{4,0},{8,12},{12,8},{1,5},{5,1},{9,13},{13,9},{2,6},{6,2},{1... | collective-permute-start | bytes 1572872 | tf_op jit(solution)/shard_map/tokens_0_3/ppermute | solution.py:100
  33.5 10.1 %collective-permute-start.10 = (bf16[256,1024]{1,0:T(8,128)(2,1)S(1)}, bf16[256,1024]{1,0:T(8,128)(2,1)S(1)}, u32[]{:S(2)}, u32[]{:S(2)}) collective-permute-start(bf16[256,1024]{1,0:T(8,128)(2,1)S(1)} %collective-permute-done.1.refs_8_), channel_id=1, source_target_pairs={{0,8},{4,12},{8,0},{12,4},{1,9},{5,13},{9,1},{13,5},{2,10},{6,14},... | collective-permute-start | bytes 1572872 | tf_op jit(solution)/shard_map/tokens_1_2/ppermute | solution.py:100
  34.0 18.4 %collective-permute-start.11 = (bf16[256,1024]{1,0:T(8,128)(2,1)S(1)}, bf16[256,1024]{1,0:T(8,128)(2,1)S(1)}, u32[]{:S(2)}, u32[]{:S(2)}) collective-permute-start(bf16[256,1024]{1,0:T(8,128)(2,1)S(1)} %collective-permute-done.1.refs_8_), channel_id=1, source_target_pairs={{0,4},{4,0},{8,12},{12,8},{1,5},{5,1},{9,13},{13,9},{2,6},{6,2},{1... | collective-permute-start | bytes 1572872 | tf_op jit(solution)/shard_map/tokens_1_1/ppermute | solution.py:100
  34.0 15.5 %collective-permute-start.6 = (bf16[128,1024]{1,0:T(8,128)(2,1)}, bf16[128,1024]{1,0:T(8,128)(2,1)S(1)}, u32[]{:S(2)}, u32[]{:S(2)}) collective-permute-start(bf16[128,1024]{1,0:T(8,128)(2,1)} %get-tuple-element.41), channel_id=1, source_target_pairs={{0,2},{1,3},{2,0},{3,1},{4,6},{5,7},{6,4},{7,5},{8,10},{9,11},{10,... | collective-permute-start | bytes 786440 | tf_op jit(solution)/shard_map/weights_2/ppermute | solution.py:100
  34.4 20.6 %collective-permute-start.5 = (bf16[256,1024]{1,0:T(8,128)(2,1)S(1)}, bf16[256,1024]{1,0:T(8,128)(2,1)S(1)}, u32[]{:S(2)}, u32[]{:S(2)}) collective-permute-start(bf16[256,1024]{1,0:T(8,128)(2,1)S(1)} %collective-permute-done.refs_4_), channel_id=1, source_target_pairs={{0,1},{1,0},{2,3},{3,2},{4,5},{5,4},{6,7},{7,6},{8,9},{9,8},{10,11... | collective-permute-start | bytes 1572872 | tf_op jit(solution)/shard_map/tokens_3/ppermute | solution.py:100
  43.6 11.4 %collective-permute-start.12 = (bf16[256,1024]{1,0:T(8,128)(2,1)S(1)}, bf16[256,1024]{1,0:T(8,128)(2,1)S(1)}, u32[]{:S(2)}, u32[]{:S(2)}) collective-permute-start(bf16[256,1024]{1,0:T(8,128)(2,1)S(1)} %collective-permute-done.10.refs_10_), channel_id=1, source_target_pairs={{0,4},{4,0},{8,12},{12,8},{1,5},{5,1},{9,13},{13,9},{2,6},{6,2},{1... | collective-permute-start | bytes 1572872 | tf_op jit(solution)/shard_map/tokens_1_3/ppermute | solution.py:100
  49.5 14.0 %collective-permute-start.16 = (bf16[256,1024]{1,0:T(8,128)(2,1)S(1)}, bf16[256,1024]{1,0:T(8,128)(2,1)S(1)}, u32[]{:S(2)}, u32[]{:S(2)}) collective-permute-start(bf16[256,1024]{1,0:T(8,128)(2,1)S(1)} %collective-permute-done.refs_4_), channel_id=1, source_target_pairs={{0,8},{4,12},{8,0},{12,4},{1,9},{5,13},{9,1},{13,5},{2,10},{6,14},... | collective-permute-start | bytes 1572872 | tf_op jit(solution)/shard_map/tokens_2_2/ppermute | solution.py:100
  51.0 10.1 %collective-permute-start.8 = (bf16[128,1024]{1,0:T(8,128)(2,1)}, bf16[128,1024]{1,0:T(8,128)(2,1)S(1)}, u32[]{:S(2)}, u32[]{:S(2)}) collective-permute-start(bf16[128,1024]{1,0:T(8,128)(2,1)} %get-tuple-element.43), channel_id=1, source_target_pairs={{0,3},{1,2},{2,1},{3,0},{4,7},{5,6},{6,5},{7,4},{8,11},{9,10},{10,... | collective-permute-start | bytes 786440 | tf_op jit(solution)/shard_map/weights_3/ppermute | solution.py:100
  52.4 8.7 %collective-permute-start.7 = (bf16[128,1024]{1,0:T(8,128)(2,1)S(1)}, bf16[128,1024]{1,0:T(8,128)(2,1)S(1)}, u32[]{:S(2)}, u32[]{:S(2)}) collective-permute-start(bf16[128,1024]{1,0:T(8,128)(2,1)S(1)} %collective-permute-done.6.refs_20_), channel_id=1, source_target_pairs={{0,16},{16,0},{1,17},{17,1},{2,18},{18,2},{3,19},{19,3},{4,20},{20... | collective-permute-start | bytes 786440 | tf_op jit(solution)/shard_map/weights_2/ppermute | solution.py:100
  61.1 8.0 %collective-permute-start.13 = (bf16[128,1024]{1,0:T(8,128)(2,1)}, bf16[128,1024]{1,0:T(8,128)(2,1)S(1)}, u32[]{:S(2)}, u32[]{:S(2)}) collective-permute-start(bf16[128,1024]{1,0:T(8,128)(2,1)} %get-tuple-element.46), channel_id=1, source_target_pairs={{0,1},{1,0},{2,3},{3,2},{4,5},{5,4},{6,7},{7,6},{8,9},{9,8},{10,11... | collective-permute-start | bytes 786440 | tf_op jit(solution)/shard_map/weights_1/ppermute | solution.py:100
  63.5 14.1 %collective-permute-start.17 = (bf16[256,1024]{1,0:T(8,128)(2,1)S(1)}, bf16[256,1024]{1,0:T(8,128)(2,1)S(1)}, u32[]{:S(2)}, u32[]{:S(2)}) collective-permute-start(bf16[256,1024]{1,0:T(8,128)(2,1)S(1)} %collective-permute-done.5.refs_0_), channel_id=1, source_target_pairs={{0,8},{4,12},{8,0},{12,4},{1,9},{5,13},{9,1},{13,5},{2,10},{6,14},... | collective-permute-start | bytes 1572872 | tf_op jit(solution)/shard_map/tokens_3_2/ppermute | solution.py:100
  64.9 9.0 %collective-permute-start.9 = (bf16[128,1024]{1,0:T(8,128)(2,1)S(1)}, bf16[128,1024]{1,0:T(8,128)(2,1)S(1)}, u32[]{:S(2)}, u32[]{:S(2)}) collective-permute-start(bf16[128,1024]{1,0:T(8,128)(2,1)S(1)} %collective-permute-done.8.refs_22_), channel_id=1, source_target_pairs={{0,16},{16,0},{1,17},{17,1},{2,18},{18,2},{3,19},{19,3},{4,20},{20... | collective-permute-start | bytes 786440 | tf_op jit(solution)/shard_map/weights_3/ppermute | solution.py:100
  69.1 8.5 %collective-permute-start.14 = (bf16[128,1024]{1,0:T(8,128)(2,1)S(1)}, bf16[128,1024]{1,0:T(8,128)(2,1)S(1)}, u32[]{:S(2)}, u32[]{:S(2)}) collective-permute-start(bf16[128,1024]{1,0:T(8,128)(2,1)S(1)} %collective-permute-done.13.refs_18_), channel_id=1, source_target_pairs={{0,16},{16,0},{1,17},{17,1},{2,18},{18,2},{3,19},{19,3},{4,20},{20... | collective-permute-start | bytes 786440 | tf_op jit(solution)/shard_map/weights_1/ppermute | solution.py:100
  70.6 7.6 %collective-permute-start.19 = (bf16[256,1024]{1,0:T(8,128)(2,1)S(1)}, bf16[256,1024]{1,0:T(8,128)(2,1)S(1)}, u32[]{:S(2)}, u32[]{:S(2)}) collective-permute-start(bf16[256,1024]{1,0:T(8,128)(2,1)S(1)} %collective-permute-done.refs_4_), channel_id=1, source_target_pairs={{0,4},{4,0},{8,12},{12,8},{1,5},{5,1},{9,13},{13,9},{2,6},{6,2},{1... | collective-permute-start | bytes 1572872 | tf_op jit(solution)/shard_map/tokens_2_1/ppermute | solution.py:100
  70.6 7.6 %collective-permute-start.20 = (bf16[256,1024]{1,0:T(8,128)(2,1)S(1)}, bf16[256,1024]{1,0:T(8,128)(2,1)S(1)}, u32[]{:S(2)}, u32[]{:S(2)}) collective-permute-start(bf16[256,1024]{1,0:T(8,128)(2,1)S(1)} %collective-permute-done.16.refs_6_), channel_id=1, source_target_pairs={{0,4},{4,0},{8,12},{12,8},{1,5},{5,1},{9,13},{13,9},{2,6},{6,2},{1... | collective-permute-start | bytes 1572872 | tf_op jit(solution)/shard_map/tokens_2_3/ppermute | solution.py:100
  106.2 19.4 %collective-permute-start.29 = (bf16[512,1024]{1,0:T(8,128)(2,1)}, bf16[512,1024]{1,0:T(8,128)(2,1)S(1)}, u32[]{:S(2)}, u32[]{:S(2)}) collective-permute-start(bf16[512,1024]{1,0:T(8,128)(2,1)} %get-tuple-element.63), channel_id=1, source_target_pairs={{0,4},{4,0},{8,12},{12,8},{1,5},{5,1},{9,13},{13,9},{2,6},{6,2},{1... | collective-permute-start | bytes 3145736 | tf_op jit(solution)/shard_map/sums_1_1/ppermute | solution.py:100
  109.7 14.2 %collective-permute-start.26 = (bf16[256,1024]{1,0:T(8,128)(2,1)S(1)}, bf16[256,1024]{1,0:T(8,128)(2,1)S(1)}, u32[]{:S(2)}, u32[]{:S(2)}) collective-permute-start(bf16[256,1024]{1,0:T(8,128)(2,1)S(1)} %slice_add_fusion.3), channel_id=1, source_target_pairs={{0,8},{4,12},{8,0},{12,4},{1,9},{5,13},{9,1},{13,5},{2,10},{6,14},... | collective-permute-start | bytes 1572872 | tf_op jit(solution)/shard_map/sums_3_2/ppermute | solution.py:100
  110.2 43.2 %collective-permute-start.21 = (bf16[512,512]{1,0:T(8,128)(2,1)}, bf16[512,512]{1,0:T(8,128)(2,1)S(1)}, u32[]{:S(2)}, u32[]{:S(2)}) collective-permute-start(bf16[512,512]{1,0:T(8,128)(2,1)} %get-tuple-element.52), channel_id=1, source_target_pairs={{0,1},{1,0},{2,3},{3,2},{4,5},{5,4},{6,7},{7,6},{8,9},{9,8},{10,11... | collective-permute-start | bytes 1572872 | tf_op jit(solution)/shard_map/grads_1/ppermute | solution.py:100
  110.2 25.4 %collective-permute-start.22 = (bf16[512,512]{1,0:T(8,128)(2,1)}, bf16[512,512]{1,0:T(8,128)(2,1)S(1)}, u32[]{:S(2)}, u32[]{:S(2)}) collective-permute-start(bf16[512,512]{1,0:T(8,128)(2,1)} %get-tuple-element.53), channel_id=1, source_target_pairs={{0,2},{1,3},{2,0},{3,1},{4,6},{5,7},{6,4},{7,5},{8,10},{9,11},{10,... | collective-permute-start | bytes 1572872 | tf_op jit(solution)/shard_map/grads_2/ppermute | solution.py:100
  113.0 10.9 %collective-permute-start.24 = (f32[2,1024]{1,0:T(2,128)S(1)}, f32[2,1024]{1,0:T(2,128)S(1)}, u32[]{:S(2)}, u32[]{:S(2)}) collective-permute-start(f32[2,1024]{1,0:T(2,128)S(1)} %copy-done.16), channel_id=1, source_target_pairs={{0,8},{4,12},{8,0},{12,4},{1,9},{5,13},{9,1},{13,5},{2,10},{6,14},... | collective-permute-start | bytes 24584 | tf_op jit(solution)/shard_map/stats/ppermute | solution.py:100
  123.9 14.7 %collective-permute-start.31 = (bf16[256,1024]{1,0:T(8,128)(2,1)}, bf16[256,1024]{1,0:T(8,128)(2,1)}, u32[]{:S(2)}, u32[]{:S(2)}) collective-permute-start(bf16[256,1024]{1,0:T(8,128)(2,1)} %slice_add_fusion), channel_id=1, source_target_pairs={{0,8},{4,12},{8,0},{12,4},{1,9},{5,13},{9,1},{13,5},{2,10},{6,14},... | collective-permute-start | bytes 1572872 | tf_op jit(solution)/shard_map/sums_2_2/ppermute | solution.py:100
  125.6 21.8 %collective-permute-start.34 = (bf16[256,1024]{1,0:T(8,128)(2,1)}, bf16[256,1024]{1,0:T(8,128)(2,1)}, u32[]{:S(2)}, u32[]{:S(2)}) collective-permute-start(bf16[256,1024]{1,0:T(8,128)(2,1)} %add_convert_fusion.1), channel_id=1, source_target_pairs={{0,1},{1,0},{2,3},{3,2},{4,5},{5,4},{6,7},{7,6},{8,9},{9,8},{10,11... | collective-permute-start | bytes 1572872 | tf_op jit(solution)/shard_map/sums_3/ppermute | solution.py:100
  126.7 26.0 %collective-permute-start.28 = (bf16[512,1024]{1,0:T(8,128)(2,1)}, bf16[512,1024]{1,0:T(8,128)(2,1)S(1)}, u32[]{:S(2)}, u32[]{:S(2)}) collective-permute-start(bf16[512,1024]{1,0:T(8,128)(2,1)} %get-tuple-element.61), channel_id=1, source_target_pairs={{0,4},{4,0},{8,12},{12,8},{1,5},{5,1},{9,13},{13,9},{2,6},{6,2},{1... | collective-permute-start | bytes 3145736 | tf_op jit(solution)/shard_map/sums_0_1/ppermute | solution.py:100
  138.6 13.7 %collective-permute-start.32 = (bf16[256,1024]{1,0:T(8,128)(2,1)}, bf16[256,1024]{1,0:T(8,128)(2,1)S(1)}, u32[]{:S(2)}, u32[]{:S(2)}) collective-permute-start(bf16[256,1024]{1,0:T(8,128)(2,1)} %slice_add_fusion.1), channel_id=1, source_target_pairs={{0,8},{4,12},{8,0},{12,4},{1,9},{5,13},{9,1},{13,5},{2,10},{6,14},... | collective-permute-start | bytes 1572872 | tf_op jit(solution)/shard_map/sums_1_2/ppermute | solution.py:100
  140.1 19.8 %collective-permute-start.27 = (bf16[528,512]{1,0:T(8,128)(2,1)S(1)}, bf16[528,512]{1,0:T(8,128)(2,1)S(1)}, u32[]{:S(2)}, u32[]{:S(2)}) collective-permute-start(bf16[528,512]{1,0:T(8,128)(2,1)S(1)} %fusion.5), channel_id=1, source_target_pairs={{0,3},{1,2},{2,1},{3,0},{4,7},{5,6},{6,5},{7,4},{8,11},{9,10},{10,... | collective-permute-start | bytes 1622024 | tf_op jit(solution)/shard_map/grads_3/ppermute | solution.py:100
  149.0 39.6 %collective-permute-start.36 = (bf16[272,1024]{1,0:T(8,128)(2,1)S(1)}, bf16[272,1024]{1,0:T(8,128)(2,1)S(1)}, u32[]{:S(2)}, u32[]{:S(2)}) collective-permute-start(bf16[272,1024]{1,0:T(8,128)(2,1)S(1)} %fusion.3), channel_id=1, source_target_pairs={{0,2},{1,3},{2,0},{3,1},{4,6},{5,7},{6,4},{7,5},{8,10},{9,11},{10,... | collective-permute-start | bytes 1671176 | tf_op jit(solution)/shard_map/sums_2/ppermute | solution.py:100
  152.6 36.0 %collective-permute-start.35 = (bf16[272,1024]{1,0:T(8,128)(2,1)S(1)}, bf16[272,1024]{1,0:T(8,128)(2,1)S(1)}, u32[]{:S(2)}, u32[]{:S(2)}) collective-permute-start(bf16[272,1024]{1,0:T(8,128)(2,1)S(1)} %fusion.4), channel_id=1, source_target_pairs={{0,1},{1,0},{2,3},{3,2},{4,5},{5,4},{6,7},{7,6},{8,9},{9,8},{10,11... | collective-permute-start | bytes 1671176 | tf_op jit(solution)/shard_map/sums_1/ppermute | solution.py:100
  152.8 35.8 %collective-permute-start.33 = (bf16[256,1024]{1,0:T(8,128)(2,1)S(1)}, bf16[256,1024]{1,0:T(8,128)(2,1)S(1)}, u32[]{:S(2)}, u32[]{:S(2)}) collective-permute-start(bf16[256,1024]{1,0:T(8,128)(2,1)S(1)} %slice_add_fusion.2), channel_id=1, source_target_pairs={{0,8},{4,12},{8,0},{12,4},{1,9},{5,13},{9,1},{13,5},{2,10},{6,14},... | collective-permute-start | bytes 1572872 | tf_op jit(solution)/shard_map/sums_0_2/ppermute | solution.py:100
  (43 other events, 819.9 us)

commit v16 on v15

--- a/solution.py
+++ b/solution.py
@@ -413,7 +413,7 @@
         weights_dp(k, *stage, *([got[top]] if top in got else []))
     for k in range(2, n_dp):
         tokens_rest(k - 1)
-        stage = [got[top]]
+        stage = [tokens[top]]
         if k & (k - 1):
             weights_groups(top)
             stage = [tokens[k], *got.values(), *crossed.values(), *chunks[k - 2].values()]

time: 193 us -> 193 us (level)
  waiting for transfers between devices: 119 us -> 114 us
  starting transfers between devices: 33.6 us -> 38 us
    ppermute x37, waiting for transfers between devices: 119 us -> 114 us  [swap(): lax.ppermute(values, axis, [(i, i ^ mask) for i in range(lax.axis_size(ax...]
    ppermute x37, starting transfers between devices: 33.6 us -> 38 us  [swap(): lax.ppermute(values, axis, [(i, i ^ mask) for i in range(lax.axis_size(ax...]
  transfers between devices with their start and end apart: 37 -> 37, of which waited for: 20 -> 19; matrix products, arithmetic and copies ran while one was open for 4% -> 4% of each run, Pallas kernels for 0% -> 0%
where the time goes in v16:
time: 193 us; the launch traced here: 192 us
  waiting for transfers between devices  114 us (59%)
  starting transfers between devices  38 us (20%)
  Pallas kernels  31.2 us (16%)
  other arithmetic  7.01 us (4%)
    ppermute x37, waiting for transfers between devices, swap(): lax.ppermute(values, axis, [(i, i ^ mask) for i in range(lax.axis_size(ax...  114 us
    ppermute x37, starting transfers between devices, swap(): lax.ppermute(values, axis, [(i, i ^ mask) for i in range(lax.axis_size(ax...  38 us
    pallas_call x1, Pallas kernels, core(): pl.pallas_call(kernel, out_shape=[jax.ShapeDtypeStruct(half, dtype)] * (2...  24.5 us
    pallas_call x1, Pallas kernels, finish(): pl.pallas_call(kernel, out_shape=out_shape, grid=(1,), in_specs=in_specs,...  3.86 us
  transfers between devices with their start and end apart: 37, of which 19 were waited for; matrix products, arithmetic and copies ran while one was open for 4% of the time, Pallas kernels for 0%

profile of v16, /device:TPU:0, one launch (start us, length us, event | category | flops | bytes accessed | tf_op | source)
XLA Modules:
  0.0 192.3 jit_solution(3846680269122652584)
XLA Ops:
  0.6 2.8 %pack.1 = (bf16[256,1024]{1,0:T(8,128)(2,1)}, bf16[128,1024]{1,0:T(8,128)(2,1)}, bf16[128,1024]{1,0:T(8,128)(2,1)}, bf16[128,1024]{1,0:T(8,128)(2,1)}) custom-call(bf16[128,1024]{1,0:T(8,128)(2,1)} %refs_10_.1, bf16[128,1024]{1,0:T(8,128)(2,1)} %grad_ref.1, bf16[256,2048]{1,0:T(8,128)(2,1)} %refs_16_.1, bf16[2048,256]{1,0:T(8,128)(2,1)} %refs_17_.1), custom_call_target="tpu_custom_call" | custom-call | bytes 4194304 | tf_op jit(solution)/shard_map/pack/pallas_call | solution.py:124
  3.4 3.0 %collective-permute-start.2 = (bf16[256,1024]{1,0:T(8,128)(2,1)}, bf16[256,1024]{1,0:T(8,128)(2,1)S(1)}, u32[]{:S(2)}, u32[]{:S(2)}) collective-permute-start(bf16[256,1024]{1,0:T(8,128)(2,1)} %get-tuple-element.38.refs_12_), channel_id=1, source_target_pairs={{0,8},{4,12},{8,0},{12,4},{1,9},{5,13},{9,1},{13,5},{2,10},{6,14},... | collective-permute-start | bytes 1572872 | tf_op jit(solution)/shard_map/tokens_0_2/ppermute | solution.py:100
  6.4 1.6 collective-permute-start.1
  8.0 2.6 %collective-permute-start = (bf16[256,1024]{1,0:T(8,128)(2,1)}, bf16[256,1024]{1,0:T(8,128)(2,1)S(1)}, u32[]{:S(2)}, u32[]{:S(2)}) collective-permute-start(bf16[256,1024]{1,0:T(8,128)(2,1)} %get-tuple-element.38.refs_12_), channel_id=1, source_target_pairs={{0,2},{1,3},{2,0},{3,1},{4,6},{5,7},{6,4},{7,5},{8,10},{9,11},{10,... | collective-permute-start | bytes 1572872 | tf_op jit(solution)/shard_map/tokens_2/ppermute | solution.py:100
  10.6 8.0 %collective-permute-done.2.refs_14_ = bf16[256,1024]{1,0:T(8,128)(2,1)S(1)} collective-permute-done((bf16[256,1024]{1,0:T(8,128)(2,1)}, bf16[256,1024]{1,0:T(8,128)(2,1)S(1)}, u32[]{:S(2)}, u32[]{:S(2)}) %collective-permute-start.2) | collective-permute-done | bytes 524320 | tf_op jit(solution)/shard_map/tokens_0_2/ppermute | solution.py:100
  18.5 12.6 %collective-permute-done.1.refs_8_ = bf16[256,1024]{1,0:T(8,128)(2,1)S(1)} collective-permute-done((bf16[256,1024]{1,0:T(8,128)(2,1)}, bf16[256,1024]{1,0:T(8,128)(2,1)S(1)}, u32[]{:S(2)}, u32[]{:S(2)}) %collective-permute-start.1) | collective-permute-done | bytes 524320 | tf_op jit(solution)/shard_map/tokens_1/ppermute | solution.py:100
  31.1 2.4 %collective-permute-done.refs_4_ = bf16[256,1024]{1,0:T(8,128)(2,1)S(1)} collective-permute-done((bf16[256,1024]{1,0:T(8,128)(2,1)}, bf16[256,1024]{1,0:T(8,128)(2,1)S(1)}, u32[]{:S(2)}, u32[]{:S(2)}) %collective-permute-start) | collective-permute-done | bytes 524320 | tf_op jit(solution)/shard_map/tokens_2/ppermute | solution.py:100
  34.4 2.7 %collective-permute-start.5 = (bf16[256,1024]{1,0:T(8,128)(2,1)S(1)}, bf16[256,1024]{1,0:T(8,128)(2,1)S(1)}, u32[]{:S(2)}, u32[]{:S(2)}) collective-permute-start(bf16[256,1024]{1,0:T(8,128)(2,1)S(1)} %collective-permute-done.refs_4_), channel_id=1, source_target_pairs={{0,1},{1,0},{2,3},{3,2},{4,5},{5,4},{6,7},{7,6},{8,9},{9,8},{10,11... | collective-permute-start | bytes 1572872 | tf_op jit(solution)/shard_map/tokens_3/ppermute | solution.py:100
  37.1 6.5 %collective-permute-done.10.refs_10_ = bf16[256,1024]{1,0:T(8,128)(2,1)S(1)} collective-permute-done((bf16[256,1024]{1,0:T(8,128)(2,1)S(1)}, bf16[256,1024]{1,0:T(8,128)(2,1)S(1)}, u32[]{:S(2)}, u32[]{:S(2)}) %collective-permute-start.10) | collective-permute-done | bytes 524320 | tf_op jit(solution)/shard_map/tokens_1_2/ppermute | solution.py:100
  44.3 5.2 %collective-permute-done.6.refs_20_ = bf16[128,1024]{1,0:T(8,128)(2,1)S(1)} collective-permute-done((bf16[128,1024]{1,0:T(8,128)(2,1)}, bf16[128,1024]{1,0:T(8,128)(2,1)S(1)}, u32[]{:S(2)}, u32[]{:S(2)}) %collective-permute-start.6) | collective-permute-done | bytes 262176 | tf_op jit(solution)/shard_map/weights_2/ppermute | solution.py:100
  52.4 3.0 %collective-permute-done.5.refs_0_ = bf16[256,1024]{1,0:T(8,128)(2,1)S(1)} collective-permute-done((bf16[256,1024]{1,0:T(8,128)(2,1)S(1)}, bf16[256,1024]{1,0:T(8,128)(2,1)S(1)}, u32[]{:S(2)}, u32[]{:S(2)}) %collective-permute-start.5) | collective-permute-done | bytes 524320 | tf_op jit(solution)/shard_map/tokens_3/ppermute | solution.py:100
  55.4 5.4 %collective-permute-done.8.refs_22_ = bf16[128,1024]{1,0:T(8,128)(2,1)S(1)} collective-permute-done((bf16[128,1024]{1,0:T(8,128)(2,1)}, bf16[128,1024]{1,0:T(8,128)(2,1)S(1)}, u32[]{:S(2)}, u32[]{:S(2)}) %collective-permute-start.8) | collective-permute-done | bytes 262176 | tf_op jit(solution)/shard_map/weights_3/ppermute | solution.py:100
  62.3 1.5 collective-permute-start.17
  65.3 3.6 %collective-permute-done.13.refs_18_ = bf16[128,1024]{1,0:T(8,128)(2,1)S(1)} collective-permute-done((bf16[128,1024]{1,0:T(8,128)(2,1)}, bf16[128,1024]{1,0:T(8,128)(2,1)S(1)}, u32[]{:S(2)}, u32[]{:S(2)}) %collective-permute-start.13) | collective-permute-done | bytes 262176 | tf_op jit(solution)/shard_map/weights_1/ppermute | solution.py:100
  71.0 4.9 %collective-permute-done.14.refs_19_ = bf16[128,1024]{1,0:T(8,128)(2,1)S(1)} collective-permute-done((bf16[128,1024]{1,0:T(8,128)(2,1)S(1)}, bf16[128,1024]{1,0:T(8,128)(2,1)S(1)}, u32[]{:S(2)}, u32[]{:S(2)}) %collective-permute-start.14) | collective-permute-done | bytes 262176 | tf_op jit(solution)/shard_map/weights_1/ppermute | solution.py:100
  79.4 24.5 %core.1 = (bf16[512,1024]{1,0:T(8,128)(2,1)}, bf16[512,1024]{1,0:T(8,128)(2,1)}, bf16[512,1024]{1,0:T(8,128)(2,1)}, bf16[512,1024]{1,0:T(8,128)(2,1)}, bf16[512,...) custom-call(bf16[256,1024]{1,0:T(8,128)(2,1)} %copy-done.24, ...), custom_call_target="tpu_custom_call" | custom-call | flops 10737418240 | bytes 20971520 | tf_op jit(solution)/shard_map/core/pallas_call | solution.py:243
  104.7 2.2 %collective-permute-done.23 = bf16[512,1024]{1,0:T(8,128)(2,1)S(1)} collective-permute-done((bf16[512,1024]{1,0:T(8,128)(2,1)}, bf16[512,1024]{1,0:T(8,128)(2,1)S(1)}, u32[]{:S(2)}, u32[]{:S(2)}) %collective-permute-start.23) | collective-permute-done | bytes 1048608 | tf_op jit(solution)/shard_map/sums_3_1/ppermute | solution.py:100
  108.0 1.6 collective-permute-start.26
  110.0 2.0 %collective-permute-start.22 = (bf16[512,512]{1,0:T(8,128)(2,1)}, bf16[512,512]{1,0:T(8,128)(2,1)S(1)}, u32[]{:S(2)}, u32[]{:S(2)}) collective-permute-start(bf16[512,512]{1,0:T(8,128)(2,1)} %get-tuple-element.53), channel_id=1, source_target_pairs={{0,2},{1,3},{2,0},{3,1},{4,6},{5,7},{6,4},{7,5},{8,10},{9,11},{10,... | collective-permute-start | bytes 1572872 | tf_op jit(solution)/shard_map/grads_2/ppermute | solution.py:100
  112.0 1.6 collective-permute-start.24
  114.5 7.7 %collective-permute-done.24 = f32[2,1024]{1,0:T(2,128)S(1)} collective-permute-done((f32[2,1024]{1,0:T(2,128)S(1)}, f32[2,1024]{1,0:T(2,128)S(1)}, u32[]{:S(2)}, u32[]{:S(2)}) %collective-permute-start.24) | collective-permute-done | bytes 8224 | tf_op jit(solution)/shard_map/stats/ppermute | solution.py:100
  122.2 1.6 collective-permute-start.31
  126.3 7.6 %collective-permute-done.22.refs_2_ = bf16[512,512]{1,0:T(8,128)(2,1)S(1)} collective-permute-done((bf16[512,512]{1,0:T(8,128)(2,1)}, bf16[512,512]{1,0:T(8,128)(2,1)S(1)}, u32[]{:S(2)}, u32[]{:S(2)}) %collective-permute-start.22) | collective-permute-done | bytes 524320 | tf_op jit(solution)/shard_map/grads_2/ppermute | solution.py:100
  133.9 3.0 %collective-permute-done.31 = bf16[256,1024]{1,0:T(8,128)(2,1)} collective-permute-done((bf16[256,1024]{1,0:T(8,128)(2,1)}, bf16[256,1024]{1,0:T(8,128)(2,1)}, u32[]{:S(2)}, u32[]{:S(2)}) %collective-permute-start.31) | collective-permute-done | bytes 524320 | tf_op jit(solution)/shard_map/sums_2_2/ppermute | solution.py:100
  136.9 1.5 collective-permute-start.32
  139.5 2.0 %collective-permute-start.27 = (bf16[528,512]{1,0:T(8,128)(2,1)S(1)}, bf16[528,512]{1,0:T(8,128)(2,1)S(1)}, u32[]{:S(2)}, u32[]{:S(2)}) collective-permute-start(bf16[528,512]{1,0:T(8,128)(2,1)S(1)} %fusion.5), channel_id=1, source_target_pairs={{0,3},{1,2},{2,1},{3,0},{4,7},{5,6},{6,5},{7,4},{8,11},{9,10},{10,... | collective-permute-start | bytes 1622024 | tf_op jit(solution)/shard_map/grads_3/ppermute | solution.py:100
  141.4 4.7 %collective-permute-done.34 = bf16[256,1024]{1,0:T(8,128)(2,1)} collective-permute-done((bf16[256,1024]{1,0:T(8,128)(2,1)}, bf16[256,1024]{1,0:T(8,128)(2,1)}, u32[]{:S(2)}, u32[]{:S(2)}) %collective-permute-start.34) | collective-permute-done | bytes 524320 | tf_op jit(solution)/shard_map/sums_3/ppermute | solution.py:100
  146.1 1.6 add_convert_fusion
  147.9 2.7 %collective-permute-start.36 = (bf16[272,1024]{1,0:T(8,128)(2,1)S(1)}, bf16[272,1024]{1,0:T(8,128)(2,1)S(1)}, u32[]{:S(2)}, u32[]{:S(2)}) collective-permute-start(bf16[272,1024]{1,0:T(8,128)(2,1)S(1)} %fusion.3), channel_id=1, source_target_pairs={{0,2},{1,3},{2,0},{3,1},{4,6},{5,7},{6,4},{7,5},{8,10},{9,11},{10,... | collective-permute-start | bytes 1671176 | tf_op jit(solution)/shard_map/sums_2/ppermute | solution.py:100
  153.2 6.6 %collective-permute-done.27.refs_3_ = bf16[528,512]{1,0:T(8,128)(2,1)S(1)} collective-permute-done((bf16[528,512]{1,0:T(8,128)(2,1)S(1)}, bf16[528,512]{1,0:T(8,128)(2,1)S(1)}, u32[]{:S(2)}, u32[]{:S(2)}) %collective-permute-start.27) | collective-permute-done | bytes 540704 | tf_op jit(solution)/shard_map/grads_3/ppermute | solution.py:100
  159.8 28.6 %collective-permute-done.36.refs_8_ = bf16[272,1024]{1,0:T(8,128)(2,1)S(1)} collective-permute-done((bf16[272,1024]{1,0:T(8,128)(2,1)S(1)}, bf16[272,1024]{1,0:T(8,128)(2,1)S(1)}, u32[]{:S(2)}, u32[]{:S(2)}) %collective-permute-start.36) | collective-permute-done | bytes 557088 | tf_op jit(solution)/shard_map/sums_2/ppermute | solution.py:100
  188.5 3.9 %finish.1 = (bf16[128,1024]{1,0:T(8,128)(2,1)}, f32[128,1024]{1,0:T(8,128)}, f32[256,2048]{1,0:T(8,128)}, f32[2048,256]{1,0:T(8,128)}, f32[2,1024]{1,0:T(2,128)}) custom-call(bf16[512,512]{1,0:T(8,128)(2,1)S(1)} %copy-done.2, bf16[512,512]{1,0:T(8,128)(2,1)S(1)} %collective-permute-done.21.refs_1_, bf16[512,512]{1,0:T(8,128)(2,1)S(1)} %collective-permute-done.22.refs_2_, ...), custom_call_target="tpu_custom_call" | custom-call | bytes 6291456 | tf_op jit(solution)/shard_map/finish/pallas_call | solution.py:352
  (134 shorter events, 22.1 us)
Async XLA Ops:
  3.4 15.1 %collective-permute-start.2 = (bf16[256,1024]{1,0:T(8,128)(2,1)}, bf16[256,1024]{1,0:T(8,128)(2,1)S(1)}, u32[]{:S(2)}, u32[]{:S(2)}) collective-permute-start(bf16[256,1024]{1,0:T(8,128)(2,1)} %get-tuple-element.38.refs_12_), channel_id=1, source_target_pairs={{0,8},{4,12},{8,0},{12,4},{1,9},{5,13},{9,1},{13,5},{2,10},{6,14},... | collective-permute-start | bytes 1572872 | tf_op jit(solution)/shard_map/tokens_0_2/ppermute | solution.py:100
  6.4 24.7 %collective-permute-start.1 = (bf16[256,1024]{1,0:T(8,128)(2,1)}, bf16[256,1024]{1,0:T(8,128)(2,1)S(1)}, u32[]{:S(2)}, u32[]{:S(2)}) collective-permute-start(bf16[256,1024]{1,0:T(8,128)(2,1)} %get-tuple-element.38.refs_12_), channel_id=1, source_target_pairs={{0,1},{1,0},{2,3},{3,2},{4,5},{5,4},{6,7},{7,6},{8,9},{9,8},{10,11... | collective-permute-start | bytes 1572872 | tf_op jit(solution)/shard_map/tokens_1/ppermute | solution.py:100
  8.0 25.5 %collective-permute-start = (bf16[256,1024]{1,0:T(8,128)(2,1)}, bf16[256,1024]{1,0:T(8,128)(2,1)S(1)}, u32[]{:S(2)}, u32[]{:S(2)}) collective-permute-start(bf16[256,1024]{1,0:T(8,128)(2,1)} %get-tuple-element.38.refs_12_), channel_id=1, source_target_pairs={{0,2},{1,3},{2,0},{3,1},{4,6},{5,7},{6,4},{7,5},{8,10},{9,11},{10,... | collective-permute-start | bytes 1572872 | tf_op jit(solution)/shard_map/tokens_2/ppermute | solution.py:100
  10.6 23.4 %collective-permute-start.3 = (bf16[256,1024]{1,0:T(8,128)(2,1)}, bf16[256,1024]{1,0:T(8,128)(2,1)S(1)}, u32[]{:S(2)}, u32[]{:S(2)}) collective-permute-start(bf16[256,1024]{1,0:T(8,128)(2,1)} %get-tuple-element.38.refs_12_), channel_id=1, source_target_pairs={{0,4},{4,0},{8,12},{12,8},{1,5},{5,1},{9,13},{13,9},{2,6},{6,2},{1... | collective-permute-start | bytes 1572872 | tf_op jit(solution)/shard_map/tokens_0_1/ppermute | solution.py:100
  18.5 15.5 %collective-permute-start.4 = (bf16[256,1024]{1,0:T(8,128)(2,1)S(1)}, bf16[256,1024]{1,0:T(8,128)(2,1)S(1)}, u32[]{:S(2)}, u32[]{:S(2)}) collective-permute-start(bf16[256,1024]{1,0:T(8,128)(2,1)S(1)} %collective-permute-done.2.refs_14_), channel_id=1, source_target_pairs={{0,4},{4,0},{8,12},{12,8},{1,5},{5,1},{9,13},{13,9},{2,6},{6,2},{1... | collective-permute-start | bytes 1572872 | tf_op jit(solution)/shard_map/tokens_0_3/ppermute | solution.py:100
  33.5 10.1 %collective-permute-start.10 = (bf16[256,1024]{1,0:T(8,128)(2,1)S(1)}, bf16[256,1024]{1,0:T(8,128)(2,1)S(1)}, u32[]{:S(2)}, u32[]{:S(2)}) collective-permute-start(bf16[256,1024]{1,0:T(8,128)(2,1)S(1)} %collective-permute-done.1.refs_8_), channel_id=1, source_target_pairs={{0,8},{4,12},{8,0},{12,4},{1,9},{5,13},{9,1},{13,5},{2,10},{6,14},... | collective-permute-start | bytes 1572872 | tf_op jit(solution)/shard_map/tokens_1_2/ppermute | solution.py:100
  34.0 16.9 %collective-permute-start.11 = (bf16[256,1024]{1,0:T(8,128)(2,1)S(1)}, bf16[256,1024]{1,0:T(8,128)(2,1)S(1)}, u32[]{:S(2)}, u32[]{:S(2)}) collective-permute-start(bf16[256,1024]{1,0:T(8,128)(2,1)S(1)} %collective-permute-done.1.refs_8_), channel_id=1, source_target_pairs={{0,4},{4,0},{8,12},{12,8},{1,5},{5,1},{9,13},{13,9},{2,6},{6,2},{1... | collective-permute-start | bytes 1572872 | tf_op jit(solution)/shard_map/tokens_1_1/ppermute | solution.py:100
  34.0 15.5 %collective-permute-start.6 = (bf16[128,1024]{1,0:T(8,128)(2,1)}, bf16[128,1024]{1,0:T(8,128)(2,1)S(1)}, u32[]{:S(2)}, u32[]{:S(2)}) collective-permute-start(bf16[128,1024]{1,0:T(8,128)(2,1)} %get-tuple-element.41), channel_id=1, source_target_pairs={{0,2},{1,3},{2,0},{3,1},{4,6},{5,7},{6,4},{7,5},{8,10},{9,11},{10,... | collective-permute-start | bytes 786440 | tf_op jit(solution)/shard_map/weights_2/ppermute | solution.py:100
  34.4 21.0 %collective-permute-start.5 = (bf16[256,1024]{1,0:T(8,128)(2,1)S(1)}, bf16[256,1024]{1,0:T(8,128)(2,1)S(1)}, u32[]{:S(2)}, u32[]{:S(2)}) collective-permute-start(bf16[256,1024]{1,0:T(8,128)(2,1)S(1)} %collective-permute-done.refs_4_), channel_id=1, source_target_pairs={{0,1},{1,0},{2,3},{3,2},{4,5},{5,4},{6,7},{7,6},{8,9},{9,8},{10,11... | collective-permute-start | bytes 1572872 | tf_op jit(solution)/shard_map/tokens_3/ppermute | solution.py:100
  43.6 11.8 %collective-permute-start.12 = (bf16[256,1024]{1,0:T(8,128)(2,1)S(1)}, bf16[256,1024]{1,0:T(8,128)(2,1)S(1)}, u32[]{:S(2)}, u32[]{:S(2)}) collective-permute-start(bf16[256,1024]{1,0:T(8,128)(2,1)S(1)} %collective-permute-done.10.refs_10_), channel_id=1, source_target_pairs={{0,4},{4,0},{8,12},{12,8},{1,5},{5,1},{9,13},{13,9},{2,6},{6,2},{1... | collective-permute-start | bytes 1572872 | tf_op jit(solution)/shard_map/tokens_1_3/ppermute | solution.py:100
  43.6 18.6 %collective-permute-start.16 = (bf16[256,1024]{1,0:T(8,128)(2,1)S(1)}, bf16[256,1024]{1,0:T(8,128)(2,1)S(1)}, u32[]{:S(2)}, u32[]{:S(2)}) collective-permute-start(bf16[256,1024]{1,0:T(8,128)(2,1)S(1)} %collective-permute-done.refs_4_), channel_id=1, source_target_pairs={{0,8},{4,12},{8,0},{12,4},{1,9},{5,13},{9,1},{13,5},{2,10},{6,14},... | collective-permute-start | bytes 1572872 | tf_op jit(solution)/shard_map/tokens_2_2/ppermute | solution.py:100
  49.5 11.3 %collective-permute-start.8 = (bf16[128,1024]{1,0:T(8,128)(2,1)}, bf16[128,1024]{1,0:T(8,128)(2,1)S(1)}, u32[]{:S(2)}, u32[]{:S(2)}) collective-permute-start(bf16[128,1024]{1,0:T(8,128)(2,1)} %get-tuple-element.43), channel_id=1, source_target_pairs={{0,3},{1,2},{2,1},{3,0},{4,7},{5,6},{6,5},{7,4},{8,11},{9,10},{10,... | collective-permute-start | bytes 786440 | tf_op jit(solution)/shard_map/weights_3/ppermute | solution.py:100
  50.9 9.9 %collective-permute-start.7 = (bf16[128,1024]{1,0:T(8,128)(2,1)S(1)}, bf16[128,1024]{1,0:T(8,128)(2,1)S(1)}, u32[]{:S(2)}, u32[]{:S(2)}) collective-permute-start(bf16[128,1024]{1,0:T(8,128)(2,1)S(1)} %collective-permute-done.6.refs_20_), channel_id=1, source_target_pairs={{0,16},{16,0},{1,17},{17,1},{2,18},{18,2},{3,19},{19,3},{4,20},{20... | collective-permute-start | bytes 786440 | tf_op jit(solution)/shard_map/weights_2/ppermute | solution.py:100
  60.8 8.1 %collective-permute-start.13 = (bf16[128,1024]{1,0:T(8,128)(2,1)}, bf16[128,1024]{1,0:T(8,128)(2,1)S(1)}, u32[]{:S(2)}, u32[]{:S(2)}) collective-permute-start(bf16[128,1024]{1,0:T(8,128)(2,1)} %get-tuple-element.46), channel_id=1, source_target_pairs={{0,1},{1,0},{2,3},{3,2},{4,5},{5,4},{6,7},{7,6},{8,9},{9,8},{10,11... | collective-permute-start | bytes 786440 | tf_op jit(solution)/shard_map/weights_1/ppermute | solution.py:100
  62.3 13.7 %collective-permute-start.17 = (bf16[256,1024]{1,0:T(8,128)(2,1)S(1)}, bf16[256,1024]{1,0:T(8,128)(2,1)S(1)}, u32[]{:S(2)}, u32[]{:S(2)}) collective-permute-start(bf16[256,1024]{1,0:T(8,128)(2,1)S(1)} %collective-permute-done.5.refs_0_), channel_id=1, source_target_pairs={{0,8},{4,12},{8,0},{12,4},{1,9},{5,13},{9,1},{13,5},{2,10},{6,14},... | collective-permute-start | bytes 1572872 | tf_op jit(solution)/shard_map/tokens_3_2/ppermute | solution.py:100
  63.8 7.1 %collective-permute-start.9 = (bf16[128,1024]{1,0:T(8,128)(2,1)S(1)}, bf16[128,1024]{1,0:T(8,128)(2,1)S(1)}, u32[]{:S(2)}, u32[]{:S(2)}) collective-permute-start(bf16[128,1024]{1,0:T(8,128)(2,1)S(1)} %collective-permute-done.8.refs_22_), channel_id=1, source_target_pairs={{0,16},{16,0},{1,17},{17,1},{2,18},{18,2},{3,19},{19,3},{4,20},{20... | collective-permute-start | bytes 786440 | tf_op jit(solution)/shard_map/weights_3/ppermute | solution.py:100
  68.9 7.0 %collective-permute-start.14 = (bf16[128,1024]{1,0:T(8,128)(2,1)S(1)}, bf16[128,1024]{1,0:T(8,128)(2,1)S(1)}, u32[]{:S(2)}, u32[]{:S(2)}) collective-permute-start(bf16[128,1024]{1,0:T(8,128)(2,1)S(1)} %collective-permute-done.13.refs_18_), channel_id=1, source_target_pairs={{0,16},{16,0},{1,17},{17,1},{2,18},{18,2},{3,19},{19,3},{4,20},{20... | collective-permute-start | bytes 786440 | tf_op jit(solution)/shard_map/weights_1/ppermute | solution.py:100
  70.4 6.1 %collective-permute-start.20 = (bf16[256,1024]{1,0:T(8,128)(2,1)S(1)}, bf16[256,1024]{1,0:T(8,128)(2,1)S(1)}, u32[]{:S(2)}, u32[]{:S(2)}) collective-permute-start(bf16[256,1024]{1,0:T(8,128)(2,1)S(1)} %collective-permute-done.16.refs_6_), channel_id=1, source_target_pairs={{0,4},{4,0},{8,12},{12,8},{1,5},{5,1},{9,13},{13,9},{2,6},{6,2},{1... | collective-permute-start | bytes 1572872 | tf_op jit(solution)/shard_map/tokens_2_3/ppermute | solution.py:100
  104.2 7.9 %collective-permute-start.30 = (bf16[512,1024]{1,0:T(8,128)(2,1)}, bf16[512,1024]{1,0:T(8,128)(2,1)S(1)}, u32[]{:S(2)}, u32[]{:S(2)}) collective-permute-start(bf16[512,1024]{1,0:T(8,128)(2,1)} %get-tuple-element.65), channel_id=1, source_target_pairs={{0,4},{4,0},{8,12},{12,8},{1,5},{5,1},{9,13},{13,9},{2,6},{6,2},{1... | collective-permute-start | bytes 3145736 | tf_op jit(solution)/shard_map/sums_2_1/ppermute | solution.py:100
  104.5 20.4 %collective-permute-start.29 = (bf16[512,1024]{1,0:T(8,128)(2,1)}, bf16[512,1024]{1,0:T(8,128)(2,1)S(1)}, u32[]{:S(2)}, u32[]{:S(2)}) collective-permute-start(bf16[512,1024]{1,0:T(8,128)(2,1)} %get-tuple-element.63), channel_id=1, source_target_pairs={{0,4},{4,0},{8,12},{12,8},{1,5},{5,1},{9,13},{13,9},{2,6},{6,2},{1... | collective-permute-start | bytes 3145736 | tf_op jit(solution)/shard_map/sums_1_1/ppermute | solution.py:100
  108.0 14.2 %collective-permute-start.26 = (bf16[256,1024]{1,0:T(8,128)(2,1)S(1)}, bf16[256,1024]{1,0:T(8,128)(2,1)S(1)}, u32[]{:S(2)}, u32[]{:S(2)}) collective-permute-start(bf16[256,1024]{1,0:T(8,128)(2,1)S(1)} %slice_add_fusion.3), channel_id=1, source_target_pairs={{0,8},{4,12},{8,0},{12,4},{1,9},{5,13},{9,1},{13,5},{2,10},{6,14},... | collective-permute-start | bytes 1572872 | tf_op jit(solution)/shard_map/sums_3_2/ppermute | solution.py:100
  109.6 43.6 %collective-permute-start.21 = (bf16[512,512]{1,0:T(8,128)(2,1)}, bf16[512,512]{1,0:T(8,128)(2,1)S(1)}, u32[]{:S(2)}, u32[]{:S(2)}) collective-permute-start(bf16[512,512]{1,0:T(8,128)(2,1)} %get-tuple-element.52), channel_id=1, source_target_pairs={{0,1},{1,0},{2,3},{3,2},{4,5},{5,4},{6,7},{7,6},{8,9},{9,8},{10,11... | collective-permute-start | bytes 1572872 | tf_op jit(solution)/shard_map/grads_1/ppermute | solution.py:100
  110.0 23.9 %collective-permute-start.22 = (bf16[512,512]{1,0:T(8,128)(2,1)}, bf16[512,512]{1,0:T(8,128)(2,1)S(1)}, u32[]{:S(2)}, u32[]{:S(2)}) collective-permute-start(bf16[512,512]{1,0:T(8,128)(2,1)} %get-tuple-element.53), channel_id=1, source_target_pairs={{0,2},{1,3},{2,0},{3,1},{4,6},{5,7},{6,4},{7,5},{8,10},{9,11},{10,... | collective-permute-start | bytes 1572872 | tf_op jit(solution)/shard_map/grads_2/ppermute | solution.py:100
  112.0 10.2 %collective-permute-start.24 = (f32[2,1024]{1,0:T(2,128)S(1)}, f32[2,1024]{1,0:T(2,128)S(1)}, u32[]{:S(2)}, u32[]{:S(2)}) collective-permute-start(f32[2,1024]{1,0:T(2,128)S(1)} %copy-done.16), channel_id=1, source_target_pairs={{0,8},{4,12},{8,0},{12,4},{1,9},{5,13},{9,1},{13,5},{2,10},{6,14},... | collective-permute-start | bytes 24584 | tf_op jit(solution)/shard_map/stats/ppermute | solution.py:100
  122.2 14.7 %collective-permute-start.31 = (bf16[256,1024]{1,0:T(8,128)(2,1)}, bf16[256,1024]{1,0:T(8,128)(2,1)}, u32[]{:S(2)}, u32[]{:S(2)}) collective-permute-start(bf16[256,1024]{1,0:T(8,128)(2,1)} %slice_add_fusion), channel_id=1, source_target_pairs={{0,8},{4,12},{8,0},{12,4},{1,9},{5,13},{9,1},{13,5},{2,10},{6,14},... | collective-permute-start | bytes 1572872 | tf_op jit(solution)/shard_map/sums_2_2/ppermute | solution.py:100
  124.9 21.2 %collective-permute-start.34 = (bf16[256,1024]{1,0:T(8,128)(2,1)}, bf16[256,1024]{1,0:T(8,128)(2,1)}, u32[]{:S(2)}, u32[]{:S(2)}) collective-permute-start(bf16[256,1024]{1,0:T(8,128)(2,1)} %add_convert_fusion.1), channel_id=1, source_target_pairs={{0,1},{1,0},{2,3},{3,2},{4,5},{5,4},{6,7},{7,6},{8,9},{9,8},{10,11... | collective-permute-start | bytes 1572872 | tf_op jit(solution)/shard_map/sums_3/ppermute | solution.py:100
  126.2 26.2 %collective-permute-start.28 = (bf16[512,1024]{1,0:T(8,128)(2,1)}, bf16[512,1024]{1,0:T(8,128)(2,1)S(1)}, u32[]{:S(2)}, u32[]{:S(2)}) collective-permute-start(bf16[512,1024]{1,0:T(8,128)(2,1)} %get-tuple-element.61), channel_id=1, source_target_pairs={{0,4},{4,0},{8,12},{12,8},{1,5},{5,1},{9,13},{13,9},{2,6},{6,2},{1... | collective-permute-start | bytes 3145736 | tf_op jit(solution)/shard_map/sums_0_1/ppermute | solution.py:100
  136.9 13.7 %collective-permute-start.32 = (bf16[256,1024]{1,0:T(8,128)(2,1)}, bf16[256,1024]{1,0:T(8,128)(2,1)S(1)}, u32[]{:S(2)}, u32[]{:S(2)}) collective-permute-start(bf16[256,1024]{1,0:T(8,128)(2,1)} %slice_add_fusion.1), channel_id=1, source_target_pairs={{0,8},{4,12},{8,0},{12,4},{1,9},{5,13},{9,1},{13,5},{2,10},{6,14},... | collective-permute-start | bytes 1572872 | tf_op jit(solution)/shard_map/sums_1_2/ppermute | solution.py:100
  139.5 20.3 %collective-permute-start.27 = (bf16[528,512]{1,0:T(8,128)(2,1)S(1)}, bf16[528,512]{1,0:T(8,128)(2,1)S(1)}, u32[]{:S(2)}, u32[]{:S(2)}) collective-permute-start(bf16[528,512]{1,0:T(8,128)(2,1)S(1)} %fusion.5), channel_id=1, source_target_pairs={{0,3},{1,2},{2,1},{3,0},{4,7},{5,6},{6,5},{7,4},{8,11},{9,10},{10,... | collective-permute-start | bytes 1622024 | tf_op jit(solution)/shard_map/grads_3/ppermute | solution.py:100
  147.9 40.5 %collective-permute-start.36 = (bf16[272,1024]{1,0:T(8,128)(2,1)S(1)}, bf16[272,1024]{1,0:T(8,128)(2,1)S(1)}, u32[]{:S(2)}, u32[]{:S(2)}) collective-permute-start(bf16[272,1024]{1,0:T(8,128)(2,1)S(1)} %fusion.3), channel_id=1, source_target_pairs={{0,2},{1,3},{2,0},{3,1},{4,6},{5,7},{6,4},{7,5},{8,10},{9,11},{10,... | collective-permute-start | bytes 1671176 | tf_op jit(solution)/shard_map/sums_2/ppermute | solution.py:100
  151.0 37.4 %collective-permute-start.35 = (bf16[272,1024]{1,0:T(8,128)(2,1)S(1)}, bf16[272,1024]{1,0:T(8,128)(2,1)S(1)}, u32[]{:S(2)}, u32[]{:S(2)}) collective-permute-start(bf16[272,1024]{1,0:T(8,128)(2,1)S(1)} %fusion.4), channel_id=1, source_target_pairs={{0,1},{1,0},{2,3},{3,2},{4,5},{5,4},{6,7},{7,6},{8,9},{9,8},{10,11... | collective-permute-start | bytes 1671176 | tf_op jit(solution)/shard_map/sums_1/ppermute | solution.py:100
  152.5 35.9 %collective-permute-start.33 = (bf16[256,1024]{1,0:T(8,128)(2,1)S(1)}, bf16[256,1024]{1,0:T(8,128)(2,1)S(1)}, u32[]{:S(2)}, u32[]{:S(2)}) collective-permute-start(bf16[256,1024]{1,0:T(8,128)(2,1)S(1)} %slice_add_fusion.2), channel_id=1, source_target_pairs={{0,8},{4,12},{8,0},{12,4},{1,9},{5,13},{9,1},{13,5},{2,10},{6,14},... | collective-permute-start | bytes 1572872 | tf_op jit(solution)/shard_map/sums_0_2/ppermute | solution.py:100
  (43 other events, 809.6 us)

commit v17 on v16

--- a/solution.py
+++ b/solution.py
@@ -418,7 +418,7 @@
             weights_groups(top)
             stage = [tokens[k], *got.values(), *crossed.values(), *chunks[k - 2].values()]
         tokens_tensor(k, *stage, chunks[k - 1][high])
-    weights_dp(1, *stage)
+    weights_dp(1, *stage, chunks[top][high])
     for k in [*range(2, n_dp), 1]:
         if k not in crossed:
             weights_groups(k)

time: 193 us -> 193 us (level)
  no operation moved by 1% of the time
where the time goes in v17:
time: 193 us; the launch traced here: 192 us
  waiting for transfers between devices  114 us (59%)
  starting transfers between devices  37.8 us (20%)
  Pallas kernels  31.2 us (16%)
  other arithmetic  7.01 us (4%)
    ppermute x37, waiting for transfers between devices, swap(): lax.ppermute(values, axis, [(i, i ^ mask) for i in range(lax.axis_size(ax...  114 us
    ppermute x37, starting transfers between devices, swap(): lax.ppermute(values, axis, [(i, i ^ mask) for i in range(lax.axis_size(ax...  37.8 us
    pallas_call x1, Pallas kernels, core(): pl.pallas_call(kernel, out_shape=[jax.ShapeDtypeStruct(half, dtype)] * (2...  24.5 us
    pallas_call x1, Pallas kernels, finish(): pl.pallas_call(kernel, out_shape=out_shape, grid=(1,), in_specs=in_specs,...  3.86 us
  transfers between devices with their start and end apart: 37, of which 19 were waited for; matrix products, arithmetic and copies ran while one was open for 4% of the time, Pallas kernels for 0%

profile of v17, /device:TPU:0, one launch (start us, length us, event | category | flops | bytes accessed | tf_op | source)
XLA Modules:
  0.0 192.3 jit_solution(16216880146053111809)
XLA Ops:
  0.6 2.8 %pack.1 = (bf16[256,1024]{1,0:T(8,128)(2,1)}, bf16[128,1024]{1,0:T(8,128)(2,1)}, bf16[128,1024]{1,0:T(8,128)(2,1)}, bf16[128,1024]{1,0:T(8,128)(2,1)}) custom-call(bf16[128,1024]{1,0:T(8,128)(2,1)} %refs_10_.1, bf16[128,1024]{1,0:T(8,128)(2,1)} %grad_ref.1, bf16[256,2048]{1,0:T(8,128)(2,1)} %refs_16_.1, bf16[2048,256]{1,0:T(8,128)(2,1)} %refs_17_.1), custom_call_target="tpu_custom_call" | custom-call | bytes 4194304 | tf_op jit(solution)/shard_map/pack/pallas_call | solution.py:124
  3.4 3.0 %collective-permute-start.2 = (bf16[256,1024]{1,0:T(8,128)(2,1)}, bf16[256,1024]{1,0:T(8,128)(2,1)S(1)}, u32[]{:S(2)}, u32[]{:S(2)}) collective-permute-start(bf16[256,1024]{1,0:T(8,128)(2,1)} %get-tuple-element.38.refs_12_), channel_id=1, source_target_pairs={{0,8},{4,12},{8,0},{12,4},{1,9},{5,13},{9,1},{13,5},{2,10},{6,14},... | collective-permute-start | bytes 1572872 | tf_op jit(solution)/shard_map/tokens_0_2/ppermute | solution.py:100
  6.4 1.6 collective-permute-start.1
  8.0 2.6 %collective-permute-start = (bf16[256,1024]{1,0:T(8,128)(2,1)}, bf16[256,1024]{1,0:T(8,128)(2,1)S(1)}, u32[]{:S(2)}, u32[]{:S(2)}) collective-permute-start(bf16[256,1024]{1,0:T(8,128)(2,1)} %get-tuple-element.38.refs_12_), channel_id=1, source_target_pairs={{0,2},{1,3},{2,0},{3,1},{4,6},{5,7},{6,4},{7,5},{8,10},{9,11},{10,... | collective-permute-start | bytes 1572872 | tf_op jit(solution)/shard_map/tokens_2/ppermute | solution.py:100
  10.6 8.0 %collective-permute-done.2.refs_14_ = bf16[256,1024]{1,0:T(8,128)(2,1)S(1)} collective-permute-done((bf16[256,1024]{1,0:T(8,128)(2,1)}, bf16[256,1024]{1,0:T(8,128)(2,1)S(1)}, u32[]{:S(2)}, u32[]{:S(2)}) %collective-permute-start.2) | collective-permute-done | bytes 524320 | tf_op jit(solution)/shard_map/tokens_0_2/ppermute | solution.py:100
  18.5 12.6 %collective-permute-done.1.refs_8_ = bf16[256,1024]{1,0:T(8,128)(2,1)S(1)} collective-permute-done((bf16[256,1024]{1,0:T(8,128)(2,1)}, bf16[256,1024]{1,0:T(8,128)(2,1)S(1)}, u32[]{:S(2)}, u32[]{:S(2)}) %collective-permute-start.1) | collective-permute-done | bytes 524320 | tf_op jit(solution)/shard_map/tokens_1/ppermute | solution.py:100
  31.1 2.4 %collective-permute-done.refs_4_ = bf16[256,1024]{1,0:T(8,128)(2,1)S(1)} collective-permute-done((bf16[256,1024]{1,0:T(8,128)(2,1)}, bf16[256,1024]{1,0:T(8,128)(2,1)S(1)}, u32[]{:S(2)}, u32[]{:S(2)}) %collective-permute-start) | collective-permute-done | bytes 524320 | tf_op jit(solution)/shard_map/tokens_2/ppermute | solution.py:100
  34.4 2.7 %collective-permute-start.5 = (bf16[256,1024]{1,0:T(8,128)(2,1)S(1)}, bf16[256,1024]{1,0:T(8,128)(2,1)S(1)}, u32[]{:S(2)}, u32[]{:S(2)}) collective-permute-start(bf16[256,1024]{1,0:T(8,128)(2,1)S(1)} %collective-permute-done.refs_4_), channel_id=1, source_target_pairs={{0,1},{1,0},{2,3},{3,2},{4,5},{5,4},{6,7},{7,6},{8,9},{9,8},{10,11... | collective-permute-start | bytes 1572872 | tf_op jit(solution)/shard_map/tokens_3/ppermute | solution.py:100
  37.1 8.5 %collective-permute-done.10.refs_10_ = bf16[256,1024]{1,0:T(8,128)(2,1)S(1)} collective-permute-done((bf16[256,1024]{1,0:T(8,128)(2,1)S(1)}, bf16[256,1024]{1,0:T(8,128)(2,1)S(1)}, u32[]{:S(2)}, u32[]{:S(2)}) %collective-permute-start.10) | collective-permute-done | bytes 524320 | tf_op jit(solution)/shard_map/tokens_1_2/ppermute | solution.py:100
  46.1 3.4 %collective-permute-done.6.refs_20_ = bf16[128,1024]{1,0:T(8,128)(2,1)S(1)} collective-permute-done((bf16[128,1024]{1,0:T(8,128)(2,1)}, bf16[128,1024]{1,0:T(8,128)(2,1)S(1)}, u32[]{:S(2)}, u32[]{:S(2)}) %collective-permute-start.6) | collective-permute-done | bytes 262176 | tf_op jit(solution)/shard_map/weights_2/ppermute | solution.py:100
  52.4 3.0 %collective-permute-done.5.refs_0_ = bf16[256,1024]{1,0:T(8,128)(2,1)S(1)} collective-permute-done((bf16[256,1024]{1,0:T(8,128)(2,1)S(1)}, bf16[256,1024]{1,0:T(8,128)(2,1)S(1)}, u32[]{:S(2)}, u32[]{:S(2)}) %collective-permute-start.5) | collective-permute-done | bytes 524320 | tf_op jit(solution)/shard_map/tokens_3/ppermute | solution.py:100
  55.4 5.4 %collective-permute-done.8.refs_22_ = bf16[128,1024]{1,0:T(8,128)(2,1)S(1)} collective-permute-done((bf16[128,1024]{1,0:T(8,128)(2,1)}, bf16[128,1024]{1,0:T(8,128)(2,1)S(1)}, u32[]{:S(2)}, u32[]{:S(2)}) %collective-permute-start.8) | collective-permute-done | bytes 262176 | tf_op jit(solution)/shard_map/weights_3/ppermute | solution.py:100
  62.3 1.5 collective-permute-start.17
  65.3 3.7 %collective-permute-done.14.refs_18_ = bf16[128,1024]{1,0:T(8,128)(2,1)S(1)} collective-permute-done((bf16[128,1024]{1,0:T(8,128)(2,1)}, bf16[128,1024]{1,0:T(8,128)(2,1)S(1)}, u32[]{:S(2)}, u32[]{:S(2)}) %collective-permute-start.14) | collective-permute-done | bytes 262176 | tf_op jit(solution)/shard_map/weights_1/ppermute | solution.py:100
  71.0 4.9 %collective-permute-done.15.refs_19_ = bf16[128,1024]{1,0:T(8,128)(2,1)S(1)} collective-permute-done((bf16[128,1024]{1,0:T(8,128)(2,1)S(1)}, bf16[128,1024]{1,0:T(8,128)(2,1)S(1)}, u32[]{:S(2)}, u32[]{:S(2)}) %collective-permute-start.15) | collective-permute-done | bytes 262176 | tf_op jit(solution)/shard_map/weights_1/ppermute | solution.py:100
  79.4 24.5 %core.1 = (bf16[512,1024]{1,0:T(8,128)(2,1)}, bf16[512,1024]{1,0:T(8,128)(2,1)}, bf16[512,1024]{1,0:T(8,128)(2,1)}, bf16[512,1024]{1,0:T(8,128)(2,1)}, bf16[512,...) custom-call(bf16[256,1024]{1,0:T(8,128)(2,1)} %copy-done.24, ...), custom_call_target="tpu_custom_call" | custom-call | flops 10737418240 | bytes 20971520 | tf_op jit(solution)/shard_map/core/pallas_call | solution.py:243
  104.7 2.2 %collective-permute-done.23 = bf16[512,1024]{1,0:T(8,128)(2,1)S(1)} collective-permute-done((bf16[512,1024]{1,0:T(8,128)(2,1)}, bf16[512,1024]{1,0:T(8,128)(2,1)S(1)}, u32[]{:S(2)}, u32[]{:S(2)}) %collective-permute-start.23) | collective-permute-done | bytes 1048608 | tf_op jit(solution)/shard_map/sums_3_1/ppermute | solution.py:100
  108.0 1.6 collective-permute-start.26
  110.0 2.1 %collective-permute-start.22 = (bf16[512,512]{1,0:T(8,128)(2,1)}, bf16[512,512]{1,0:T(8,128)(2,1)S(1)}, u32[]{:S(2)}, u32[]{:S(2)}) collective-permute-start(bf16[512,512]{1,0:T(8,128)(2,1)} %get-tuple-element.53), channel_id=1, source_target_pairs={{0,2},{1,3},{2,0},{3,1},{4,6},{5,7},{6,4},{7,5},{8,10},{9,11},{10,... | collective-permute-start | bytes 1572872 | tf_op jit(solution)/shard_map/grads_2/ppermute | solution.py:100
  112.0 1.6 collective-permute-start.24
  114.5 7.7 %collective-permute-done.24 = f32[2,1024]{1,0:T(2,128)S(1)} collective-permute-done((f32[2,1024]{1,0:T(2,128)S(1)}, f32[2,1024]{1,0:T(2,128)S(1)}, u32[]{:S(2)}, u32[]{:S(2)}) %collective-permute-start.24) | collective-permute-done | bytes 8224 | tf_op jit(solution)/shard_map/stats/ppermute | solution.py:100
  122.2 1.6 collective-permute-start.31
  126.3 7.6 %collective-permute-done.22.refs_2_ = bf16[512,512]{1,0:T(8,128)(2,1)S(1)} collective-permute-done((bf16[512,512]{1,0:T(8,128)(2,1)}, bf16[512,512]{1,0:T(8,128)(2,1)S(1)}, u32[]{:S(2)}, u32[]{:S(2)}) %collective-permute-start.22) | collective-permute-done | bytes 524320 | tf_op jit(solution)/shard_map/grads_2/ppermute | solution.py:100
  133.9 3.0 %collective-permute-done.31 = bf16[256,1024]{1,0:T(8,128)(2,1)} collective-permute-done((bf16[256,1024]{1,0:T(8,128)(2,1)}, bf16[256,1024]{1,0:T(8,128)(2,1)}, u32[]{:S(2)}, u32[]{:S(2)}) %collective-permute-start.31) | collective-permute-done | bytes 524320 | tf_op jit(solution)/shard_map/sums_2_2/ppermute | solution.py:100
  136.9 1.5 collective-permute-start.32
  139.5 2.0 %collective-permute-start.27 = (bf16[528,512]{1,0:T(8,128)(2,1)S(1)}, bf16[528,512]{1,0:T(8,128)(2,1)S(1)}, u32[]{:S(2)}, u32[]{:S(2)}) collective-permute-start(bf16[528,512]{1,0:T(8,128)(2,1)S(1)} %fusion.5), channel_id=1, source_target_pairs={{0,3},{1,2},{2,1},{3,0},{4,7},{5,6},{6,5},{7,4},{8,11},{9,10},{10,... | collective-permute-start | bytes 1622024 | tf_op jit(solution)/shard_map/grads_3/ppermute | solution.py:100
  141.4 4.7 %collective-permute-done.34 = bf16[256,1024]{1,0:T(8,128)(2,1)} collective-permute-done((bf16[256,1024]{1,0:T(8,128)(2,1)}, bf16[256,1024]{1,0:T(8,128)(2,1)}, u32[]{:S(2)}, u32[]{:S(2)}) %collective-permute-start.34) | collective-permute-done | bytes 524320 | tf_op jit(solution)/shard_map/sums_3/ppermute | solution.py:100
  146.1 1.6 add_convert_fusion
  147.9 2.6 %collective-permute-start.36 = (bf16[272,1024]{1,0:T(8,128)(2,1)S(1)}, bf16[272,1024]{1,0:T(8,128)(2,1)S(1)}, u32[]{:S(2)}, u32[]{:S(2)}) collective-permute-start(bf16[272,1024]{1,0:T(8,128)(2,1)S(1)} %fusion.3), channel_id=1, source_target_pairs={{0,2},{1,3},{2,0},{3,1},{4,6},{5,7},{6,4},{7,5},{8,10},{9,11},{10,... | collective-permute-start | bytes 1671176 | tf_op jit(solution)/shard_map/sums_2/ppermute | solution.py:100
  153.2 6.6 %collective-permute-done.27.refs_3_ = bf16[528,512]{1,0:T(8,128)(2,1)S(1)} collective-permute-done((bf16[528,512]{1,0:T(8,128)(2,1)S(1)}, bf16[528,512]{1,0:T(8,128)(2,1)S(1)}, u32[]{:S(2)}, u32[]{:S(2)}) %collective-permute-start.27) | collective-permute-done | bytes 540704 | tf_op jit(solution)/shard_map/grads_3/ppermute | solution.py:100
  159.8 28.6 %collective-permute-done.36.refs_8_ = bf16[272,1024]{1,0:T(8,128)(2,1)S(1)} collective-permute-done((bf16[272,1024]{1,0:T(8,128)(2,1)S(1)}, bf16[272,1024]{1,0:T(8,128)(2,1)S(1)}, u32[]{:S(2)}, u32[]{:S(2)}) %collective-permute-start.36) | collective-permute-done | bytes 557088 | tf_op jit(solution)/shard_map/sums_2/ppermute | solution.py:100
  188.5 3.9 %finish.1 = (bf16[128,1024]{1,0:T(8,128)(2,1)}, f32[128,1024]{1,0:T(8,128)}, f32[256,2048]{1,0:T(8,128)}, f32[2048,256]{1,0:T(8,128)}, f32[2,1024]{1,0:T(2,128)}) custom-call(bf16[512,512]{1,0:T(8,128)(2,1)S(1)} %copy-done.2, bf16[512,512]{1,0:T(8,128)(2,1)S(1)} %collective-permute-done.21.refs_1_, bf16[512,512]{1,0:T(8,128)(2,1)S(1)} %collective-permute-done.22.refs_2_, ...), custom_call_target="tpu_custom_call" | custom-call | bytes 6291456 | tf_op jit(solution)/shard_map/finish/pallas_call | solution.py:352
  (134 shorter events, 21.9 us)
Async XLA Ops:
  3.4 15.1 %collective-permute-start.2 = (bf16[256,1024]{1,0:T(8,128)(2,1)}, bf16[256,1024]{1,0:T(8,128)(2,1)S(1)}, u32[]{:S(2)}, u32[]{:S(2)}) collective-permute-start(bf16[256,1024]{1,0:T(8,128)(2,1)} %get-tuple-element.38.refs_12_), channel_id=1, source_target_pairs={{0,8},{4,12},{8,0},{12,4},{1,9},{5,13},{9,1},{13,5},{2,10},{6,14},... | collective-permute-start | bytes 1572872 | tf_op jit(solution)/shard_map/tokens_0_2/ppermute | solution.py:100
  6.4 24.7 %collective-permute-start.1 = (bf16[256,1024]{1,0:T(8,128)(2,1)}, bf16[256,1024]{1,0:T(8,128)(2,1)S(1)}, u32[]{:S(2)}, u32[]{:S(2)}) collective-permute-start(bf16[256,1024]{1,0:T(8,128)(2,1)} %get-tuple-element.38.refs_12_), channel_id=1, source_target_pairs={{0,1},{1,0},{2,3},{3,2},{4,5},{5,4},{6,7},{7,6},{8,9},{9,8},{10,11... | collective-permute-start | bytes 1572872 | tf_op jit(solution)/shard_map/tokens_1/ppermute | solution.py:100
  8.0 25.5 %collective-permute-start = (bf16[256,1024]{1,0:T(8,128)(2,1)}, bf16[256,1024]{1,0:T(8,128)(2,1)S(1)}, u32[]{:S(2)}, u32[]{:S(2)}) collective-permute-start(bf16[256,1024]{1,0:T(8,128)(2,1)} %get-tuple-element.38.refs_12_), channel_id=1, source_target_pairs={{0,2},{1,3},{2,0},{3,1},{4,6},{5,7},{6,4},{7,5},{8,10},{9,11},{10,... | collective-permute-start | bytes 1572872 | tf_op jit(solution)/shard_map/tokens_2/ppermute | solution.py:100
  10.6 23.4 %collective-permute-start.3 = (bf16[256,1024]{1,0:T(8,128)(2,1)}, bf16[256,1024]{1,0:T(8,128)(2,1)S(1)}, u32[]{:S(2)}, u32[]{:S(2)}) collective-permute-start(bf16[256,1024]{1,0:T(8,128)(2,1)} %get-tuple-element.38.refs_12_), channel_id=1, source_target_pairs={{0,4},{4,0},{8,12},{12,8},{1,5},{5,1},{9,13},{13,9},{2,6},{6,2},{1... | collective-permute-start | bytes 1572872 | tf_op jit(solution)/shard_map/tokens_0_1/ppermute | solution.py:100
  18.5 15.5 %collective-permute-start.4 = (bf16[256,1024]{1,0:T(8,128)(2,1)S(1)}, bf16[256,1024]{1,0:T(8,128)(2,1)S(1)}, u32[]{:S(2)}, u32[]{:S(2)}) collective-permute-start(bf16[256,1024]{1,0:T(8,128)(2,1)S(1)} %collective-permute-done.2.refs_14_), channel_id=1, source_target_pairs={{0,4},{4,0},{8,12},{12,8},{1,5},{5,1},{9,13},{13,9},{2,6},{6,2},{1... | collective-permute-start | bytes 1572872 | tf_op jit(solution)/shard_map/tokens_0_3/ppermute | solution.py:100
  33.5 12.1 %collective-permute-start.10 = (bf16[256,1024]{1,0:T(8,128)(2,1)S(1)}, bf16[256,1024]{1,0:T(8,128)(2,1)S(1)}, u32[]{:S(2)}, u32[]{:S(2)}) collective-permute-start(bf16[256,1024]{1,0:T(8,128)(2,1)S(1)} %collective-permute-done.1.refs_8_), channel_id=1, source_target_pairs={{0,8},{4,12},{8,0},{12,4},{1,9},{5,13},{9,1},{13,5},{2,10},{6,14},... | collective-permute-start | bytes 1572872 | tf_op jit(solution)/shard_map/tokens_1_2/ppermute | solution.py:100
  34.0 16.9 %collective-permute-start.11 = (bf16[256,1024]{1,0:T(8,128)(2,1)S(1)}, bf16[256,1024]{1,0:T(8,128)(2,1)S(1)}, u32[]{:S(2)}, u32[]{:S(2)}) collective-permute-start(bf16[256,1024]{1,0:T(8,128)(2,1)S(1)} %collective-permute-done.1.refs_8_), channel_id=1, source_target_pairs={{0,4},{4,0},{8,12},{12,8},{1,5},{5,1},{9,13},{13,9},{2,6},{6,2},{1... | collective-permute-start | bytes 1572872 | tf_op jit(solution)/shard_map/tokens_1_1/ppermute | solution.py:100
  34.0 15.5 %collective-permute-start.6 = (bf16[128,1024]{1,0:T(8,128)(2,1)}, bf16[128,1024]{1,0:T(8,128)(2,1)S(1)}, u32[]{:S(2)}, u32[]{:S(2)}) collective-permute-start(bf16[128,1024]{1,0:T(8,128)(2,1)} %get-tuple-element.41), channel_id=1, source_target_pairs={{0,2},{1,3},{2,0},{3,1},{4,6},{5,7},{6,4},{7,5},{8,10},{9,11},{10,... | collective-permute-start | bytes 786440 | tf_op jit(solution)/shard_map/weights_2/ppermute | solution.py:100
  34.4 21.0 %collective-permute-start.5 = (bf16[256,1024]{1,0:T(8,128)(2,1)S(1)}, bf16[256,1024]{1,0:T(8,128)(2,1)S(1)}, u32[]{:S(2)}, u32[]{:S(2)}) collective-permute-start(bf16[256,1024]{1,0:T(8,128)(2,1)S(1)} %collective-permute-done.refs_4_), channel_id=1, source_target_pairs={{0,1},{1,0},{2,3},{3,2},{4,5},{5,4},{6,7},{7,6},{8,9},{9,8},{10,11... | collective-permute-start | bytes 1572872 | tf_op jit(solution)/shard_map/tokens_3/ppermute | solution.py:100
  45.6 9.8 %collective-permute-start.13 = (bf16[256,1024]{1,0:T(8,128)(2,1)S(1)}, bf16[256,1024]{1,0:T(8,128)(2,1)S(1)}, u32[]{:S(2)}, u32[]{:S(2)}) collective-permute-start(bf16[256,1024]{1,0:T(8,128)(2,1)S(1)} %collective-permute-done.refs_4_), channel_id=1, source_target_pairs={{0,8},{4,12},{8,0},{12,4},{1,9},{5,13},{9,1},{13,5},{2,10},{6,14},... | collective-permute-start | bytes 1572872 | tf_op jit(solution)/shard_map/tokens_2_2/ppermute | solution.py:100
  46.1 9.3 %collective-permute-start.12 = (bf16[256,1024]{1,0:T(8,128)(2,1)S(1)}, bf16[256,1024]{1,0:T(8,128)(2,1)S(1)}, u32[]{:S(2)}, u32[]{:S(2)}) collective-permute-start(bf16[256,1024]{1,0:T(8,128)(2,1)S(1)} %collective-permute-done.10.refs_10_), channel_id=1, source_target_pairs={{0,4},{4,0},{8,12},{12,8},{1,5},{5,1},{9,13},{13,9},{2,6},{6,2},{1... | collective-permute-start | bytes 1572872 | tf_op jit(solution)/shard_map/tokens_1_3/ppermute | solution.py:100
  49.5 11.3 %collective-permute-start.8 = (bf16[128,1024]{1,0:T(8,128)(2,1)}, bf16[128,1024]{1,0:T(8,128)(2,1)S(1)}, u32[]{:S(2)}, u32[]{:S(2)}) collective-permute-start(bf16[128,1024]{1,0:T(8,128)(2,1)} %get-tuple-element.43), channel_id=1, source_target_pairs={{0,3},{1,2},{2,1},{3,0},{4,7},{5,6},{6,5},{7,4},{8,11},{9,10},{10,... | collective-permute-start | bytes 786440 | tf_op jit(solution)/shard_map/weights_3/ppermute | solution.py:100
  50.9 9.9 %collective-permute-start.7 = (bf16[128,1024]{1,0:T(8,128)(2,1)S(1)}, bf16[128,1024]{1,0:T(8,128)(2,1)S(1)}, u32[]{:S(2)}, u32[]{:S(2)}) collective-permute-start(bf16[128,1024]{1,0:T(8,128)(2,1)S(1)} %collective-permute-done.6.refs_20_), channel_id=1, source_target_pairs={{0,16},{16,0},{1,17},{17,1},{2,18},{18,2},{3,19},{19,3},{4,20},{20... | collective-permute-start | bytes 786440 | tf_op jit(solution)/shard_map/weights_2/ppermute | solution.py:100
  60.8 8.1 %collective-permute-start.14 = (bf16[128,1024]{1,0:T(8,128)(2,1)}, bf16[128,1024]{1,0:T(8,128)(2,1)S(1)}, u32[]{:S(2)}, u32[]{:S(2)}) collective-permute-start(bf16[128,1024]{1,0:T(8,128)(2,1)} %get-tuple-element.47), channel_id=1, source_target_pairs={{0,1},{1,0},{2,3},{3,2},{4,5},{5,4},{6,7},{7,6},{8,9},{9,8},{10,11... | collective-permute-start | bytes 786440 | tf_op jit(solution)/shard_map/weights_1/ppermute | solution.py:100
  62.3 13.7 %collective-permute-start.17 = (bf16[256,1024]{1,0:T(8,128)(2,1)S(1)}, bf16[256,1024]{1,0:T(8,128)(2,1)S(1)}, u32[]{:S(2)}, u32[]{:S(2)}) collective-permute-start(bf16[256,1024]{1,0:T(8,128)(2,1)S(1)} %collective-permute-done.5.refs_0_), channel_id=1, source_target_pairs={{0,8},{4,12},{8,0},{12,4},{1,9},{5,13},{9,1},{13,5},{2,10},{6,14},... | collective-permute-start | bytes 1572872 | tf_op jit(solution)/shard_map/tokens_3_2/ppermute | solution.py:100
  63.8 7.2 %collective-permute-start.9 = (bf16[128,1024]{1,0:T(8,128)(2,1)S(1)}, bf16[128,1024]{1,0:T(8,128)(2,1)S(1)}, u32[]{:S(2)}, u32[]{:S(2)}) collective-permute-start(bf16[128,1024]{1,0:T(8,128)(2,1)S(1)} %collective-permute-done.8.refs_22_), channel_id=1, source_target_pairs={{0,16},{16,0},{1,17},{17,1},{2,18},{18,2},{3,19},{19,3},{4,20},{20... | collective-permute-start | bytes 786440 | tf_op jit(solution)/shard_map/weights_3/ppermute | solution.py:100
  68.9 7.0 %collective-permute-start.15 = (bf16[128,1024]{1,0:T(8,128)(2,1)S(1)}, bf16[128,1024]{1,0:T(8,128)(2,1)S(1)}, u32[]{:S(2)}, u32[]{:S(2)}) collective-permute-start(bf16[128,1024]{1,0:T(8,128)(2,1)S(1)} %collective-permute-done.14.refs_18_), channel_id=1, source_target_pairs={{0,16},{16,0},{1,17},{17,1},{2,18},{18,2},{3,19},{19,3},{4,20},{20... | collective-permute-start | bytes 786440 | tf_op jit(solution)/shard_map/weights_1/ppermute | solution.py:100
  70.4 6.1 %collective-permute-start.20 = (bf16[256,1024]{1,0:T(8,128)(2,1)S(1)}, bf16[256,1024]{1,0:T(8,128)(2,1)S(1)}, u32[]{:S(2)}, u32[]{:S(2)}) collective-permute-start(bf16[256,1024]{1,0:T(8,128)(2,1)S(1)} %collective-permute-done.13.refs_6_), channel_id=1, source_target_pairs={{0,4},{4,0},{8,12},{12,8},{1,5},{5,1},{9,13},{13,9},{2,6},{6,2},{1... | collective-permute-start | bytes 1572872 | tf_op jit(solution)/shard_map/tokens_2_3/ppermute | solution.py:100
  104.2 7.9 %collective-permute-start.30 = (bf16[512,1024]{1,0:T(8,128)(2,1)}, bf16[512,1024]{1,0:T(8,128)(2,1)S(1)}, u32[]{:S(2)}, u32[]{:S(2)}) collective-permute-start(bf16[512,1024]{1,0:T(8,128)(2,1)} %get-tuple-element.65), channel_id=1, source_target_pairs={{0,4},{4,0},{8,12},{12,8},{1,5},{5,1},{9,13},{13,9},{2,6},{6,2},{1... | collective-permute-start | bytes 3145736 | tf_op jit(solution)/shard_map/sums_2_1/ppermute | solution.py:100
  104.5 20.4 %collective-permute-start.29 = (bf16[512,1024]{1,0:T(8,128)(2,1)}, bf16[512,1024]{1,0:T(8,128)(2,1)S(1)}, u32[]{:S(2)}, u32[]{:S(2)}) collective-permute-start(bf16[512,1024]{1,0:T(8,128)(2,1)} %get-tuple-element.63), channel_id=1, source_target_pairs={{0,4},{4,0},{8,12},{12,8},{1,5},{5,1},{9,13},{13,9},{2,6},{6,2},{1... | collective-permute-start | bytes 3145736 | tf_op jit(solution)/shard_map/sums_1_1/ppermute | solution.py:100
  108.0 14.2 %collective-permute-start.26 = (bf16[256,1024]{1,0:T(8,128)(2,1)S(1)}, bf16[256,1024]{1,0:T(8,128)(2,1)S(1)}, u32[]{:S(2)}, u32[]{:S(2)}) collective-permute-start(bf16[256,1024]{1,0:T(8,128)(2,1)S(1)} %slice_add_fusion.3), channel_id=1, source_target_pairs={{0,8},{4,12},{8,0},{12,4},{1,9},{5,13},{9,1},{13,5},{2,10},{6,14},... | collective-permute-start | bytes 1572872 | tf_op jit(solution)/shard_map/sums_3_2/ppermute | solution.py:100
  109.6 43.6 %collective-permute-start.21 = (bf16[512,512]{1,0:T(8,128)(2,1)}, bf16[512,512]{1,0:T(8,128)(2,1)S(1)}, u32[]{:S(2)}, u32[]{:S(2)}) collective-permute-start(bf16[512,512]{1,0:T(8,128)(2,1)} %get-tuple-element.52), channel_id=1, source_target_pairs={{0,1},{1,0},{2,3},{3,2},{4,5},{5,4},{6,7},{7,6},{8,9},{9,8},{10,11... | collective-permute-start | bytes 1572872 | tf_op jit(solution)/shard_map/grads_1/ppermute | solution.py:100
  110.0 23.9 %collective-permute-start.22 = (bf16[512,512]{1,0:T(8,128)(2,1)}, bf16[512,512]{1,0:T(8,128)(2,1)S(1)}, u32[]{:S(2)}, u32[]{:S(2)}) collective-permute-start(bf16[512,512]{1,0:T(8,128)(2,1)} %get-tuple-element.53), channel_id=1, source_target_pairs={{0,2},{1,3},{2,0},{3,1},{4,6},{5,7},{6,4},{7,5},{8,10},{9,11},{10,... | collective-permute-start | bytes 1572872 | tf_op jit(solution)/shard_map/grads_2/ppermute | solution.py:100
  112.0 10.2 %collective-permute-start.24 = (f32[2,1024]{1,0:T(2,128)S(1)}, f32[2,1024]{1,0:T(2,128)S(1)}, u32[]{:S(2)}, u32[]{:S(2)}) collective-permute-start(f32[2,1024]{1,0:T(2,128)S(1)} %copy-done.16), channel_id=1, source_target_pairs={{0,8},{4,12},{8,0},{12,4},{1,9},{5,13},{9,1},{13,5},{2,10},{6,14},... | collective-permute-start | bytes 24584 | tf_op jit(solution)/shard_map/stats/ppermute | solution.py:100
  122.2 14.7 %collective-permute-start.31 = (bf16[256,1024]{1,0:T(8,128)(2,1)}, bf16[256,1024]{1,0:T(8,128)(2,1)}, u32[]{:S(2)}, u32[]{:S(2)}) collective-permute-start(bf16[256,1024]{1,0:T(8,128)(2,1)} %slice_add_fusion), channel_id=1, source_target_pairs={{0,8},{4,12},{8,0},{12,4},{1,9},{5,13},{9,1},{13,5},{2,10},{6,14},... | collective-permute-start | bytes 1572872 | tf_op jit(solution)/shard_map/sums_2_2/ppermute | solution.py:100
  124.9 21.2 %collective-permute-start.34 = (bf16[256,1024]{1,0:T(8,128)(2,1)}, bf16[256,1024]{1,0:T(8,128)(2,1)}, u32[]{:S(2)}, u32[]{:S(2)}) collective-permute-start(bf16[256,1024]{1,0:T(8,128)(2,1)} %add_convert_fusion.1), channel_id=1, source_target_pairs={{0,1},{1,0},{2,3},{3,2},{4,5},{5,4},{6,7},{7,6},{8,9},{9,8},{10,11... | collective-permute-start | bytes 1572872 | tf_op jit(solution)/shard_map/sums_3/ppermute | solution.py:100
  126.2 26.2 %collective-permute-start.28 = (bf16[512,1024]{1,0:T(8,128)(2,1)}, bf16[512,1024]{1,0:T(8,128)(2,1)S(1)}, u32[]{:S(2)}, u32[]{:S(2)}) collective-permute-start(bf16[512,1024]{1,0:T(8,128)(2,1)} %get-tuple-element.61), channel_id=1, source_target_pairs={{0,4},{4,0},{8,12},{12,8},{1,5},{5,1},{9,13},{13,9},{2,6},{6,2},{1... | collective-permute-start | bytes 3145736 | tf_op jit(solution)/shard_map/sums_0_1/ppermute | solution.py:100
  136.9 13.7 %collective-permute-start.32 = (bf16[256,1024]{1,0:T(8,128)(2,1)}, bf16[256,1024]{1,0:T(8,128)(2,1)S(1)}, u32[]{:S(2)}, u32[]{:S(2)}) collective-permute-start(bf16[256,1024]{1,0:T(8,128)(2,1)} %slice_add_fusion.1), channel_id=1, source_target_pairs={{0,8},{4,12},{8,0},{12,4},{1,9},{5,13},{9,1},{13,5},{2,10},{6,14},... | collective-permute-start | bytes 1572872 | tf_op jit(solution)/shard_map/sums_1_2/ppermute | solution.py:100
  139.5 20.3 %collective-permute-start.27 = (bf16[528,512]{1,0:T(8,128)(2,1)S(1)}, bf16[528,512]{1,0:T(8,128)(2,1)S(1)}, u32[]{:S(2)}, u32[]{:S(2)}) collective-permute-start(bf16[528,512]{1,0:T(8,128)(2,1)S(1)} %fusion.5), channel_id=1, source_target_pairs={{0,3},{1,2},{2,1},{3,0},{4,7},{5,6},{6,5},{7,4},{8,11},{9,10},{10,... | collective-permute-start | bytes 1622024 | tf_op jit(solution)/shard_map/grads_3/ppermute | solution.py:100
  147.9 40.5 %collective-permute-start.36 = (bf16[272,1024]{1,0:T(8,128)(2,1)S(1)}, bf16[272,1024]{1,0:T(8,128)(2,1)S(1)}, u32[]{:S(2)}, u32[]{:S(2)}) collective-permute-start(bf16[272,1024]{1,0:T(8,128)(2,1)S(1)} %fusion.3), channel_id=1, source_target_pairs={{0,2},{1,3},{2,0},{3,1},{4,6},{5,7},{6,4},{7,5},{8,10},{9,11},{10,... | collective-permute-start | bytes 1671176 | tf_op jit(solution)/shard_map/sums_2/ppermute | solution.py:100
  151.0 37.4 %collective-permute-start.35 = (bf16[272,1024]{1,0:T(8,128)(2,1)S(1)}, bf16[272,1024]{1,0:T(8,128)(2,1)S(1)}, u32[]{:S(2)}, u32[]{:S(2)}) collective-permute-start(bf16[272,1024]{1,0:T(8,128)(2,1)S(1)} %fusion.4), channel_id=1, source_target_pairs={{0,1},{1,0},{2,3},{3,2},{4,5},{5,4},{6,7},{7,6},{8,9},{9,8},{10,11... | collective-permute-start | bytes 1671176 | tf_op jit(solution)/shard_map/sums_1/ppermute | solution.py:100
  152.5 35.9 %collective-permute-start.33 = (bf16[256,1024]{1,0:T(8,128)(2,1)S(1)}, bf16[256,1024]{1,0:T(8,128)(2,1)S(1)}, u32[]{:S(2)}, u32[]{:S(2)}) collective-permute-start(bf16[256,1024]{1,0:T(8,128)(2,1)S(1)} %slice_add_fusion.2), channel_id=1, source_target_pairs={{0,8},{4,12},{8,0},{12,4},{1,9},{5,13},{9,1},{13,5},{2,10},{6,14},... | collective-permute-start | bytes 1572872 | tf_op jit(solution)/shard_map/sums_0_2/ppermute | solution.py:100
  (43 other events, 814.5 us)
